TPU v7x, 32 devices: a whole 2x2x4 slice. The times are simulated.
32 devices in a mesh: groups: 2 (over x), latent: 16 (over z, y, core).
Axes of the slice: x: 2, y: 2, z: 4, core: 2. Of those that a mesh axis runs over, the one named last changes fastest.
Arguments:
- activations: bfloat16 [512, 2304], P(('groups', 'latent')), parts along dimension 0, may hold values from -6 to 6
- encoder: bfloat16 [4096, 2304], P(('groups', 'latent')), parts along dimension 0, may hold values from -0.125 to 0.125
- encoder_bias: float32 [4096], P(('groups', 'latent')), parts along dimension 0, may hold values from -3 to 3
- decoder: bfloat16 [4096, 2304], P(('groups', 'latent')), parts along dimension 0, may hold values from -0.125 to 0.125
- decoder_bias: float32 [4608], P('groups'), parts along dimension 0, may hold values from -3 to 3
- encoder_moment: float32 [4096, 2304], P(('groups', 'latent')), parts along dimension 0, may hold values from -0.375 to 0.375
- encoder_square: float32 [4096, 2304], P(('groups', 'latent')), parts along dimension 0, may hold values from 3.90625e-05 to 0.001171875
- decoder_moment: float32 [4096, 2304], P(('groups', 'latent')), parts along dimension 0, may hold values from -0.25 to 0.25
- decoder_square: float32 [4096, 2304], P(('groups', 'latent')), parts along dimension 0, may hold values from 3.90625e-05 to 0.001171875
Outputs:
- row_error: bfloat16 [512, 2304], P(('groups', 'latent')), parts along dimension 0
- encoder_next: bfloat16 [4096, 2304], P(('groups', 'latent')), parts along dimension 0
- decoder_next: bfloat16 [4096, 2304], P(('groups', 'latent')), parts along dimension 0
- encoder_moment_next: float32 [4096, 2304], P(('groups', 'latent')), parts along dimension 0
- encoder_square_next: float32 [4096, 2304], P(('groups', 'latent')), parts along dimension 0
- decoder_moment_next: float32 [4096, 2304], P(('groups', 'latent')), parts along dimension 0
- decoder_square_next: float32 [4096, 2304], P(('groups', 'latent')), parts along dimension 0
There are 2 independent parts, one for each index of `groups`. A program takes and returns all parts, laid end to end along the dimension named above; each array names one. Nothing has to cross between parts.
All inputs are finite; a program needn't handle non-finite values.
Results may differ from a plain program's by a relative error of at most 0.01.
Values may be sent and summed in bfloat16 or wider, within the bound.
No kernel may reach another device: no remote copies, remote signals or barrier semaphores. Data moves between devices by JAX's collectives and lax.ppermute only.
A program may use at most 128 MiB of HBM per device.

v0:
```python
import jax
import jax.numpy as jnp
from jax import lax
from jax.sharding import PartitionSpec as P

beta_first = 0.9
beta_second = 0.999
step_rate = 0.001
adam_epsilon = 1e-08


def inner_last(left, right):
    return lax.dot_general(
        left, right, (((1,), (1,)), ((), ())), preferred_element_type=jnp.float32
    )


def inner_first(left, right):
    return lax.dot_general(
        left, right, (((0,), (0,)), ((), ())), preferred_element_type=jnp.float32
    )


def adam_update(weight, grad, moment, square):
    moment_next = beta_first * moment + (1.0 - beta_first) * grad
    square_next = beta_second * square + (1.0 - beta_second) * grad * grad
    weight_next = (
        weight.astype(jnp.float32)
        - step_rate * moment_next / (jnp.sqrt(square_next) + adam_epsilon)
    ).astype(jnp.bfloat16)
    return (weight_next, moment_next, square_next)


def body(
    activations,
    encoder,
    encoder_bias,
    decoder,
    decoder_bias,
    encoder_moment,
    encoder_square,
    decoder_moment,
    decoder_square,
):
    rows_here = activations.shape[0]
    total_rows = rows_here * lax.axis_size("latent")
    centered = (activations.astype(jnp.float32) - decoder_bias).astype(jnp.bfloat16)
    gathered = lax.all_gather(centered, "latent", axis=0, tiled=True)
    codes = jnp.maximum(inner_last(gathered, encoder) + encoder_bias, 0.0).astype(jnp.bfloat16)
    partial_sums = jnp.dot(codes, decoder, preferred_element_type=jnp.float32)
    summed_all = lax.psum(partial_sums, "latent")
    error_all = (summed_all - gathered.astype(jnp.float32)).astype(jnp.bfloat16)
    own_start = lax.axis_index("latent") * rows_here
    row_error = lax.dynamic_slice_in_dim(error_all, own_start, rows_here, 0)
    decoder_total = inner_first(codes, error_all)
    signal = inner_last(error_all, decoder)
    delta = jnp.where(codes > 0, signal, 0.0).astype(jnp.bfloat16)
    encoder_total = inner_first(delta, gathered)
    encoder_grad = encoder_total / total_rows
    decoder_grad = decoder_total / total_rows
    encoder_next, encoder_moment_next, encoder_square_next = adam_update(
        encoder, encoder_grad, encoder_moment, encoder_square
    )
    decoder_next, decoder_moment_next, decoder_square_next = adam_update(
        decoder, decoder_grad, decoder_moment, decoder_square
    )
    return (
        row_error,
        encoder_next,
        decoder_next,
        encoder_moment_next,
        encoder_square_next,
        decoder_moment_next,
        decoder_square_next,
    )


def solution(mesh):
    return jax.shard_map(
        body,
        mesh=mesh,
        in_specs=(
            P(("groups", "latent"), None),
            P(("groups", "latent"), None),
            P(("groups", "latent")),
            P(("groups", "latent"), None),
            P("groups"),
            P(("groups", "latent"), None),
            P(("groups", "latent"), None),
            P(("groups", "latent"), None),
            P(("groups", "latent"), None),
        ),
        out_specs=(
            P(("groups", "latent"), None),
            P(("groups", "latent"), None),
            P(("groups", "latent"), None),
            P(("groups", "latent"), None),
            P(("groups", "latent"), None),
            P(("groups", "latent"), None),
            P(("groups", "latent"), None),
        ),
        check_vma=False,
    )
```

profile of v0, /device:TPU:0, one launch (start us, length us, event | category | flops | bytes accessed | tf_op | source)
XLA Modules:
  0.0 171.7 jit_solution(6220811448994482319)
XLA Ops:
  7.2 0.0 copy-start.2
  7.2 0.0 all-gather.2.cloned.1.call-start
  7.2 1.6 subtract_convert_fusion.3
  8.8 0.0 all-gather.2.cloned.1.call-update
  8.8 0.0 all-reduce.2.cloned.1.call-start
  8.9 43.0 %all-gather.2.cloned.1.call-done = bf16[256,2304]{1,0:T(8,128)(2,1)} async-done(((bf16[16,2304]{1,0:T(8,128)(2,1)}), bf16[256,2304]{1,0:T(8,128)(2,1)}) %all-gather.2.cloned.1.call-update) | async-done | bytes 1179664 | tf_op jit(solution)/shard_map/all_gather | solution.py:48
  51.9 1.9 %fusion.1 = bf16[256,128]{1,0:T(8,128)(2,1)S(1)} fusion(bf16[256,2304]{1,0:T(8,128)(2,1)} %all-gather.2.cloned.1.call-done, bf16[128,2304]{1,0:T(8,128)(2,1)} %param.10, f32[128]{0:T(128)} %param.11), kind=kOutput, calls=%fused_computation.10 | convolution fusion | flops 151093248 | bytes 1835520 | tf_op jit(solution)/shard_map/dot_general | solution.py:13
  53.9 0.0 copy-start.3
  53.9 0.6 copy-done.3
  54.5 0.0 copy-done.2
  54.5 1.9 %fusion.9 = f32[256,2304]{1,0:T(8,128)} fusion(bf16[256,128]{1,0:T(8,128)(2,1)S(1)} %fusion.1, bf16[128,2304]{1,0:T(8,128)(2,1)S(1)} %copy-done.2), kind=kOutput, calls=%fused_computation.20 | convolution fusion | flops 150994944 | bytes 3014656 | tf_op jit(solution)/shard_map/dot_general | solution.py:50
  56.4 0.0 copy-start
  56.4 0.0 all-reduce.2.cloned.1.call-update
  56.4 98.3 %all-reduce.2.cloned.1.call-done = f32[256,2304]{1,0:T(8,128)} async-done(((f32[256,2304]{1,0:T(8,128)}), f32[256,2304]{1,0:T(8,128)}) %all-reduce.2.cloned.1.call-update) | async-done | bytes 2359312 | tf_op jit(solution)/shard_map/psum | solution.py:51
  154.7 0.0 copy-done
  154.7 0.0 copy-start.4
  154.7 0.0 copy-start.5
  154.7 0.0 copy-start.6
  154.7 2.0 %subtract_convert_fusion = bf16[256,2304]{1,0:T(8,128)(2,1)S(1)} fusion(f32[256,2304]{1,0:T(8,128)} %all-reduce.2.cloned.1.call-done, bf16[256,2304]{1,0:T(8,128)(2,1)S(1)} %copy-done), kind=kLoop, calls=%fused_computation | loop fusion | flops 1769472 | bytes 4718592 | tf_op jit(solution)/shard_map/convert_element_type | solution.py:52
  156.7 0.6 constant_dynamic-slice_fusion
  157.4 0.0 copy-done.4
  157.4 0.0 copy-done.5
  157.4 0.0 copy-done.6
  157.4 0.0 copy-start.1
  157.4 2.6 %subtract_convert_fusion.1 = (bf16[128,2304]{1,0:T(8,128)(2,1)}, f32[128,2304]{1,0:T(8,128)}, f32[128,2304]{1,0:T(8,128)}) fusion(bf16[128,2304]{1,0:T(8,128)(2,1)S(1)} %copy-done.2, f32[128,2304]{1,0:T(8,128)S(1)} %copy-done.5, f32[128,2304]{1,0:T(8,128)S(1)} %copy-done.6, bf16[256,128]{1,0:T(8,128)(2,1)S(1)} %copy-done.4, ...), kind=kOutput, calls=%fused_computation.1 | convolution fusion | flops 155123712 | bytes 7143424 | tf_op jit(solution)/shard_map/dot_general | solution.py:19
  160.0 0.0 copy-done.1
  160.0 4.8 %subtract_convert_fusion.2 = (bf16[128,2304]{1,0:T(8,128)(2,1)}, f32[128,2304]{1,0:T(8,128)}, f32[128,2304]{1,0:T(8,128)}) fusion(bf16[128,2304]{1,0:T(8,128)(2,1)S(1)} %copy-done.1, f32[128,2304]{1,0:T(8,128)} %param.14, f32[128,2304]{1,0:T(8,128)} %param.15, bf16[256,2304]{1,0:T(8,128)(2,1)S(1)} %copy-done, ...), kind=kOutput, calls=%fused_computation.4 | convolution fusion | flops 306216960 | bytes 8912896 | tf_op jit(solution)/shard_map/dot_general | solution.py:19
Async XLA Ops:
  7.2 47.3 %copy-start.2 = (bf16[128,2304]{1,0:T(8,128)(2,1)S(1)}, bf16[128,2304]{1,0:T(8,128)(2,1)}, u32[]{:S(2)}) copy-start(bf16[128,2304]{1,0:T(8,128)(2,1)} %param.12) | copy-start | bytes 1769476
  7.2 44.8 %all-gather.2.cloned.1.call-start = ((), (), s32[]{:S(2)}) async-start(), calls=%async_computation | async-start | bytes 1253376 | tf_op jit(solution)/shard_map/all_gather | solution.py:48
  8.8 145.9 %all-reduce.2.cloned.1.call-start = ((), (), s32[]{:S(2)}) async-start(), calls=%async_computation.1 | async-start | bytes 4718592 | tf_op jit(solution)/shard_map/psum | solution.py:51
  53.9 0.6 copy-start.3
  56.4 98.4 %copy-start = (bf16[256,2304]{1,0:T(8,128)(2,1)S(1)}, bf16[256,2304]{1,0:T(8,128)(2,1)}, u32[]{:S(2)}) copy-start(bf16[256,2304]{1,0:T(8,128)(2,1)} %all-gather.2.cloned.1.call-done) | copy-start | bytes 3538948
  154.7 2.7 %copy-start.4 = (bf16[256,128]{1,0:T(8,128)(2,1)S(1)}, bf16[256,128]{1,0:T(8,128)(2,1)}, u32[]{:S(2)}) copy-start(bf16[256,128]{1,0:T(8,128)(2,1)} %copy-done.3) | copy-start | bytes 196612
  154.7 2.7 %copy-start.5 = (f32[128,2304]{1,0:T(8,128)S(1)}, f32[128,2304]{1,0:T(8,128)}, u32[]{:S(2)}) copy-start(f32[128,2304]{1,0:T(8,128)} %param.16) | copy-start | bytes 3538948
  154.7 2.7 %copy-start.6 = (f32[128,2304]{1,0:T(8,128)S(1)}, f32[128,2304]{1,0:T(8,128)}, u32[]{:S(2)}) copy-start(f32[128,2304]{1,0:T(8,128)} %param.17) | copy-start | bytes 3538948
  157.4 2.6 %copy-start.1 = (bf16[128,2304]{1,0:T(8,128)(2,1)S(1)}, bf16[128,2304]{1,0:T(8,128)(2,1)}, u32[]{:S(2)}) copy-start(bf16[128,2304]{1,0:T(8,128)(2,1)} %param.10) | copy-start | bytes 1769476
Sparse Core Ops, SparseCore 0:
  10.9 41.0 all-gather.1
  56.5 98.1 all-reduce.1
where the time goes:
time: 172 us
  waiting for transfers between devices  141 us (82%)
  between operations  14.1 us (8%)
  matrix products  11.2 us (7%)
  other arithmetic  3.6 us (2%)
    psum x1, waiting for transfers between devices, body(): summed_all = lax.psum(partial_sums, 'latent')  98.3 us
    all_gather x1, waiting for transfers between devices, body(): gathered = lax.all_gather(centered, 'latent', axis=0, tiled=True)  43 us
    dot_general x2, matrix products, inner_first(): lax.dot_general(left, right, (((0,), (0,)), ((), ())), preferred_element_...  7.46 us
  transfers between devices with their start and end apart: 2, of which 2 were waited for; matrix products, arithmetic and copies ran while one was open for 0% of the time, Pallas kernels for 0%

commit v1 on v0

v1 whole, which is shorter than its diff:
```python
import jax
import jax.numpy as jnp
from jax import lax
from jax.sharding import PartitionSpec as P

beta_first = 0.9
beta_second = 0.999
step_rate = 0.001
adam_epsilon = 1e-08


def inner_last(left, right):
    return lax.dot_general(
        left, right, (((1,), (1,)), ((), ())), preferred_element_type=jnp.float32
    )


def inner_first(left, right):
    return lax.dot_general(
        left, right, (((0,), (0,)), ((), ())), preferred_element_type=jnp.float32
    )


def adam_update(weight, grad, moment, square):
    moment_next = beta_first * moment + (1.0 - beta_first) * grad
    square_next = beta_second * square + (1.0 - beta_second) * grad * grad
    weight_next = (
        weight.astype(jnp.float32)
        - step_rate * moment_next / (jnp.sqrt(square_next) + adam_epsilon)
    ).astype(jnp.bfloat16)
    return (weight_next, moment_next, square_next)


def to_chip(block, distance):
    size = lax.axis_size("latent")
    return lax.ppermute(
        block, "latent", [(i, i ^ (2 * distance)) for i in range(size)]
    )


def to_other_core(block):
    size = lax.axis_size("latent")
    return lax.ppermute(block, "latent", [(i, i ^ 1) for i in range(size)])


def body(
    activations,
    encoder,
    encoder_bias,
    decoder,
    decoder_bias,
    encoder_moment,
    encoder_square,
    decoder_moment,
    decoder_square,
):
    rows_here, width = activations.shape
    latents_here = encoder.shape[0]
    size = lax.axis_size("latent")
    chips = size // 2
    total_rows = rows_here * size

    row_blocks = [activations] + [to_chip(activations, k) for k in range(1, chips)]
    encoder_both = jnp.concatenate([encoder, to_other_core(encoder)], 0)
    decoder_both = jnp.concatenate([decoder, to_other_core(decoder)], 0)
    bias_both = jnp.concatenate([encoder_bias, to_other_core(encoder_bias)], 0)

    rows_core = jnp.concatenate(row_blocks, 0)
    centered = (rows_core.astype(jnp.float32) - decoder_bias).astype(jnp.bfloat16)
    codes = jnp.maximum(inner_last(centered, encoder_both) + bias_both, 0.0).astype(
        jnp.bfloat16
    )
    partial_sums = jnp.dot(codes, decoder_both, preferred_element_type=jnp.float32).astype(
        jnp.bfloat16
    )
    summed = partial_sums[:rows_here].astype(jnp.float32)
    arrived = [
        to_chip(partial_sums[k * rows_here : (k + 1) * rows_here], k) for k in range(1, chips)
    ]
    for block in arrived:
        summed = summed + block.astype(jnp.float32)
    row_error = (summed - centered[:rows_here].astype(jnp.float32)).astype(jnp.bfloat16)

    other_codes = to_other_core(codes[:, latents_here:])
    other_centered = to_other_core(centered)
    codes_all = jnp.concatenate([codes[:, :latents_here], other_codes], 0)
    centered_all = jnp.concatenate([centered, other_centered], 0)

    error_core = jnp.concatenate([row_error] + [to_chip(row_error, k) for k in range(1, chips)], 0)
    error_all = jnp.concatenate([error_core, to_other_core(error_core)], 0)

    decoder_grad = inner_first(codes_all, error_all) / total_rows
    signal = inner_last(error_all, decoder)
    delta = jnp.where(codes_all > 0, signal, 0.0).astype(jnp.bfloat16)
    encoder_grad = inner_first(delta, centered_all) / total_rows
    encoder_next, encoder_moment_next, encoder_square_next = adam_update(
        encoder, encoder_grad, encoder_moment, encoder_square
    )
    decoder_next, decoder_moment_next, decoder_square_next = adam_update(
        decoder, decoder_grad, decoder_moment, decoder_square
    )
    return (
        row_error,
        encoder_next,
        decoder_next,
        encoder_moment_next,
        encoder_square_next,
        decoder_moment_next,
        decoder_square_next,
    )


def solution(mesh):
    sharded = P(("groups", "latent"), None)
    return jax.shard_map(
        body,
        mesh=mesh,
        in_specs=(
            sharded,
            sharded,
            P(("groups", "latent")),
            sharded,
            P("groups"),
            sharded,
            sharded,
            sharded,
            sharded,
        ),
        out_specs=(sharded,) * 7,
        check_vma=False,
    )
```

time: 172 us -> 79.1 us (0.46)
  waiting for transfers between devices: 141 us -> 32.7 us
  starting transfers between devices: 0.08 us -> 34.2 us
  between operations: 14.1 us -> 0.9 us
  other arithmetic: 3.6 us -> 0.85 us
  matrix products: 11.2 us -> 8.49 us
    psum x1 -> x0, waiting for transfers between devices: 98.3 us -> none  [body(): summed_all = lax.psum(partial_sums, 'latent')]
    all_gather x1 -> x0, waiting for transfers between devices: 43 us -> none  [body(): gathered = lax.all_gather(centered, 'latent', axis=0, tiled=True)]
    ppermute x0 -> x27, starting transfers between devices: none -> 34.2 us  [the longest x21 33 us: to_chip(): lax.ppermute(block, 'latent', [(i, i ^ 2 * distance) for i in range(size)])]
    ppermute x0 -> x27, waiting for transfers between devices: none -> 32.7 us  [the longest x21 30.9 us: to_chip(): lax.ppermute(block, 'latent', [(i, i ^ 2 * distance) for i in range(size)])]
    convert_element_type x2 -> x1, other arithmetic: 3.6 us -> 0.1 us  [body(): (rows_core.astype(jnp.float32) - decoder_bias).astype(jnp.bfloat16)]
  transfers between devices with their start and end apart: 2 -> 27, of which waited for: 2 -> 11; matrix products, arithmetic and copies ran while one was open for 0% -> 6% of each run, Pallas kernels for 0% -> 0%
where the time goes in v1:
time: 79.1 us; the launch traced here: 78.8 us
  starting transfers between devices  34.2 us (43%)
  waiting for transfers between devices  32.7 us (41%)
  matrix products  8.49 us (11%)
  local copies, waits for them, and re-layouts  1.68 us (2%)
  between operations  0.9 us (1%)
  other arithmetic  0.85 us (1%)
    ppermute x21, starting transfers between devices, to_chip(): lax.ppermute(block, 'latent', [(i, i ^ 2 * distance) for i in range(size)])  33 us
    ppermute x21, waiting for transfers between devices, to_chip(): lax.ppermute(block, 'latent', [(i, i ^ 2 * distance) for i in range(size)])  30.9 us
    dot_general x2, matrix products, inner_first(): lax.dot_general(left, right, (((0,), (0,)), ((), ())), preferred_element_...  7.62 us
    ppermute x6, waiting for transfers between devices, to_other_core(): return lax.ppermute(block, 'latent', [(i, i ^ 1) for i in range(size)])  1.8 us
  transfers between devices with their start and end apart: 27, of which 11 were waited for; matrix products, arithmetic and copies ran while one was open for 6% of the time, Pallas kernels for 0%

profile of v1, /device:TPU:0, one launch (start us, length us, event | category | flops | bytes accessed | tf_op | source)
XLA Modules:
  0.0 78.8 jit_solution(4796092676307830243)
XLA Ops:
  0.7 5.1 %collective-permute-start.5 = (bf16[16,2304]{1,0:T(8,128)(2,1)}, bf16[16,2304]{1,0:T(8,128)(2,1)S(1)}, u32[]{:S(2)}, u32[]{:S(2)}) collective-permute-start(bf16[16,2304]{1,0:T(8,128)(2,1)} %param.9), channel_id=1, source_target_pairs={{0,12},{1,13},{2,14},{3,15},{4,8},{5,9},{6,10},{7,11},{8,4},{9,5},... | collective-permute-start | bytes 221192 | tf_op jit(solution)/shard_map/ppermute | solution.py:36
  5.8 0.4 collective-permute-start.4
  6.2 3.5 %collective-permute-start.3 = (bf16[16,2304]{1,0:T(8,128)(2,1)}, bf16[16,2304]{1,0:T(8,128)(2,1)S(1)}, u32[]{:S(2)}, u32[]{:S(2)}) collective-permute-start(bf16[16,2304]{1,0:T(8,128)(2,1)} %param.9), channel_id=1, source_target_pairs={{0,8},{1,9},{2,10},{3,11},{4,12},{5,13},{6,14},{7,15},{8,0},{9,1},... | collective-permute-start | bytes 221192 | tf_op jit(solution)/shard_map/ppermute | solution.py:36
  9.7 1.0 %constant_dynamic-update-slice_fusion.7 = bf16[128,2304]{1,0:T(8,128)(2,1)S(1)} fusion(bf16[16,2304]{1,0:T(8,128)(2,1)} %param.9), kind=kLoop, calls=%fused_computation.33 | loop fusion | bytes 147456
  10.9 1.0 %collective-permute-start = (bf16[16,2304]{1,0:T(8,128)(2,1)}, bf16[16,2304]{1,0:T(8,128)(2,1)S(1)}, u32[]{:S(2)}, u32[]{:S(2)}) collective-permute-start(bf16[16,2304]{1,0:T(8,128)(2,1)} %param.9), channel_id=1, source_target_pairs={{0,2},{1,3},{2,0},{3,1},{4,6},{5,7},{6,4},{7,5},{8,10},{9,11},{10,... | collective-permute-start | bytes 221192 | tf_op jit(solution)/shard_map/ppermute | solution.py:36
  11.9 0.7 pad_maximum_fusion.3
  12.6 3.8 %collective-permute-done = bf16[16,2304]{1,0:T(8,128)(2,1)S(1)} collective-permute-done((bf16[16,2304]{1,0:T(8,128)(2,1)}, bf16[16,2304]{1,0:T(8,128)(2,1)S(1)}, u32[]{:S(2)}, u32[]{:S(2)}) %collective-permute-start) | collective-permute-done | bytes 73760 | tf_op jit(solution)/shard_map/ppermute | solution.py:36
  16.4 1.1 %collective-permute-start.1 = (bf16[16,2304]{1,0:T(8,128)(2,1)}, bf16[16,2304]{1,0:T(8,128)(2,1)S(1)}, u32[]{:S(2)}, u32[]{:S(2)}) collective-permute-start(bf16[16,2304]{1,0:T(8,128)(2,1)} %param.9), channel_id=1, source_target_pairs={{0,4},{1,5},{2,6},{3,7},{4,0},{5,1},{6,2},{7,3},{8,12},{9,13},{10,... | collective-permute-start | bytes 221192 | tf_op jit(solution)/shard_map/ppermute | solution.py:36
  17.5 3.5 %collective-permute-done.1 = bf16[16,2304]{1,0:T(8,128)(2,1)S(1)} collective-permute-done((bf16[16,2304]{1,0:T(8,128)(2,1)}, bf16[16,2304]{1,0:T(8,128)(2,1)S(1)}, u32[]{:S(2)}, u32[]{:S(2)}) %collective-permute-start.1) | collective-permute-done | bytes 73760 | tf_op jit(solution)/shard_map/ppermute | solution.py:36
  21.0 1.9 %collective-permute-start.6 = (bf16[16,2304]{1,0:T(8,128)(2,1)}, bf16[16,2304]{1,0:T(8,128)(2,1)S(1)}, u32[]{:S(2)}, u32[]{:S(2)}) collective-permute-start(bf16[16,2304]{1,0:T(8,128)(2,1)} %param.9), channel_id=1, source_target_pairs={{0,14},{1,15},{2,12},{3,13},{4,10},{5,11},{6,8},{7,9},{8,6},{9,7},... | collective-permute-start | bytes 221192 | tf_op jit(solution)/shard_map/ppermute | solution.py:36
  23.0 0.5 collective-permute-start.9
  23.6 4.7 %collective-permute-done.6 = bf16[16,2304]{1,0:T(8,128)(2,1)S(1)} collective-permute-done((bf16[16,2304]{1,0:T(8,128)(2,1)}, bf16[16,2304]{1,0:T(8,128)(2,1)S(1)}, u32[]{:S(2)}, u32[]{:S(2)}) %collective-permute-start.6) | collective-permute-done | bytes 73760 | tf_op jit(solution)/shard_map/ppermute | solution.py:36
  28.4 0.5 fusion.17
  28.9 0.5 copy-done.6
  29.8 0.8 %collective-permute-start.10 = (bf16[16,2304]{1,0:T(8,128)(2,1)S(1)}, bf16[16,2304]{1,0:T(8,128)(2,1)S(1)}, u32[]{:S(2)}, u32[]{:S(2)}) collective-permute-start(bf16[16,2304]{1,0:T(8,128)(2,1)S(1)} %get-tuple-element.15), channel_id=1, source_target_pairs={{0,2},{1,3},{2,0},{3,1},{4,6},{5,7},{6,4},{7,5},{8,10},{9,11},{10,... | collective-permute-start | bytes 221192 | tf_op jit(solution)/shard_map/ppermute | solution.py:36
  30.6 1.9 %collective-permute-start.16 = (bf16[16,2304]{1,0:T(8,128)(2,1)S(1)}, bf16[16,2304]{1,0:T(8,128)(2,1)S(1)}, u32[]{:S(2)}, u32[]{:S(2)}) collective-permute-start(bf16[16,2304]{1,0:T(8,128)(2,1)S(1)} %get-tuple-element.16), channel_id=1, source_target_pairs={{0,14},{1,15},{2,12},{3,13},{4,10},{5,11},{6,8},{7,9},{8,6},{9,7},... | collective-permute-start | bytes 221192 | tf_op jit(solution)/shard_map/ppermute | solution.py:36
  32.6 2.6 %collective-permute-start.15 = (bf16[16,2304]{1,0:T(8,128)(2,1)S(1)}, bf16[16,2304]{1,0:T(8,128)(2,1)S(1)}, u32[]{:S(2)}, u32[]{:S(2)}) collective-permute-start(bf16[16,2304]{1,0:T(8,128)(2,1)S(1)} %get-tuple-element.17), channel_id=1, source_target_pairs={{0,12},{1,13},{2,14},{3,15},{4,8},{5,9},{6,10},{7,11},{8,4},{9,5},... | collective-permute-start | bytes 221192 | tf_op jit(solution)/shard_map/ppermute | solution.py:36
  35.2 3.1 %collective-permute-start.13 = (bf16[16,2304]{1,0:T(8,128)(2,1)S(1)}, bf16[16,2304]{1,0:T(8,128)(2,1)S(1)}, u32[]{:S(2)}, u32[]{:S(2)}) collective-permute-start(bf16[16,2304]{1,0:T(8,128)(2,1)S(1)} %get-tuple-element.19), channel_id=1, source_target_pairs={{0,8},{1,9},{2,10},{3,11},{4,12},{5,13},{6,14},{7,15},{8,0},{9,1},... | collective-permute-start | bytes 221192 | tf_op jit(solution)/shard_map/ppermute | solution.py:36
  38.3 2.7 %collective-permute-start.11 = (bf16[16,2304]{1,0:T(8,128)(2,1)S(1)}, bf16[16,2304]{1,0:T(8,128)(2,1)S(1)}, u32[]{:S(2)}, u32[]{:S(2)}) collective-permute-start(bf16[16,2304]{1,0:T(8,128)(2,1)S(1)} %get-tuple-element.21), channel_id=1, source_target_pairs={{0,4},{1,5},{2,6},{3,7},{4,0},{5,1},{6,2},{7,3},{8,12},{9,13},{10,... | collective-permute-start | bytes 221192 | tf_op jit(solution)/shard_map/ppermute | solution.py:36
  41.0 3.3 %collective-permute-done.14 = bf16[16,2304]{1,0:T(8,128)(2,1)S(1)} collective-permute-done((bf16[16,2304]{1,0:T(8,128)(2,1)S(1)}, bf16[16,2304]{1,0:T(8,128)(2,1)S(1)}, u32[]{:S(2)}, u32[]{:S(2)}) %collective-permute-start.14) | collective-permute-done | bytes 73760 | tf_op jit(solution)/shard_map/ppermute | solution.py:36
  44.3 1.2 %collective-permute-done.12 = bf16[16,2304]{1,0:T(8,128)(2,1)S(1)} collective-permute-done((bf16[16,2304]{1,0:T(8,128)(2,1)S(1)}, bf16[16,2304]{1,0:T(8,128)(2,1)S(1)}, u32[]{:S(2)}, u32[]{:S(2)}) %collective-permute-start.12) | collective-permute-done | bytes 73760 | tf_op jit(solution)/shard_map/ppermute | solution.py:36
  45.9 1.3 %collective-permute-start.24 = (bf16[16,2304]{1,0:T(8,128)(2,1)S(1)}, bf16[16,2304]{1,0:T(8,128)(2,1)S(1)}, u32[]{:S(2)}, u32[]{:S(2)}) collective-permute-start(bf16[16,2304]{1,0:T(8,128)(2,1)S(1)} %get-tuple-element.14), channel_id=1, source_target_pairs={{0,14},{1,15},{2,12},{3,13},{4,10},{5,11},{6,8},{7,9},{8,6},{9,7},... | collective-permute-start | bytes 221192 | tf_op jit(solution)/shard_map/ppermute | solution.py:36
  47.1 3.1 %collective-permute-start.23 = (bf16[16,2304]{1,0:T(8,128)(2,1)S(1)}, bf16[16,2304]{1,0:T(8,128)(2,1)S(1)}, u32[]{:S(2)}, u32[]{:S(2)}) collective-permute-start(bf16[16,2304]{1,0:T(8,128)(2,1)S(1)} %get-tuple-element.14), channel_id=1, source_target_pairs={{0,12},{1,13},{2,14},{3,15},{4,8},{5,9},{6,10},{7,11},{8,4},{9,5},... | collective-permute-start | bytes 221192 | tf_op jit(solution)/shard_map/ppermute | solution.py:36
  50.3 3.3 %collective-permute-start.21 = (bf16[16,2304]{1,0:T(8,128)(2,1)S(1)}, bf16[16,2304]{1,0:T(8,128)(2,1)S(1)}, u32[]{:S(2)}, u32[]{:S(2)}) collective-permute-start(bf16[16,2304]{1,0:T(8,128)(2,1)S(1)} %get-tuple-element.14), channel_id=1, source_target_pairs={{0,8},{1,9},{2,10},{3,11},{4,12},{5,13},{6,14},{7,15},{8,0},{9,1},... | collective-permute-start | bytes 221192 | tf_op jit(solution)/shard_map/ppermute | solution.py:36
  53.6 1.1 %collective-permute-start.18 = (bf16[16,2304]{1,0:T(8,128)(2,1)S(1)}, bf16[16,2304]{1,0:T(8,128)(2,1)S(1)}, u32[]{:S(2)}, u32[]{:S(2)}) collective-permute-start(bf16[16,2304]{1,0:T(8,128)(2,1)S(1)} %get-tuple-element.14), channel_id=1, source_target_pairs={{0,2},{1,3},{2,0},{3,1},{4,6},{5,7},{6,4},{7,5},{8,10},{9,11},{10,... | collective-permute-start | bytes 221192 | tf_op jit(solution)/shard_map/ppermute | solution.py:36
  54.7 4.0 %collective-permute-done.18 = bf16[16,2304]{1,0:T(8,128)(2,1)S(1)} collective-permute-done((bf16[16,2304]{1,0:T(8,128)(2,1)S(1)}, bf16[16,2304]{1,0:T(8,128)(2,1)S(1)}, u32[]{:S(2)}, u32[]{:S(2)}) %collective-permute-start.18) | collective-permute-done | bytes 73760 | tf_op jit(solution)/shard_map/ppermute | solution.py:36
  58.7 4.9 %collective-permute-done.19 = bf16[16,2304]{1,0:T(8,128)(2,1)S(1)} collective-permute-done((bf16[16,2304]{1,0:T(8,128)(2,1)S(1)}, bf16[16,2304]{1,0:T(8,128)(2,1)S(1)}, u32[]{:S(2)}, u32[]{:S(2)}) %collective-permute-start.19) | collective-permute-done | bytes 73760 | tf_op jit(solution)/shard_map/ppermute | solution.py:36
  63.6 5.2 %collective-permute-done.20 = bf16[16,2304]{1,0:T(8,128)(2,1)S(1)} collective-permute-done((bf16[16,2304]{1,0:T(8,128)(2,1)S(1)}, bf16[16,2304]{1,0:T(8,128)(2,1)S(1)}, u32[]{:S(2)}, u32[]{:S(2)}) %collective-permute-start.20) | collective-permute-done | bytes 73760 | tf_op jit(solution)/shard_map/ppermute | solution.py:36
  69.1 0.5 collective-permute-start.26
  69.6 1.5 %collective-permute-done.25 = bf16[128,2304]{1,0:T(8,128)(2,1)S(1)} collective-permute-done((bf16[128,2304]{1,0:T(8,128)(2,1)S(1)}, bf16[128,2304]{1,0:T(8,128)(2,1)S(1)}, u32[]{:S(2)}, u32[]{:S(2)}) %collective-permute-start.25) | collective-permute-done | bytes 589856 | tf_op jit(solution)/shard_map/ppermute | solution.py:43
  71.2 2.6 %subtract_convert_fusion = (bf16[128,2304]{1,0:T(8,128)(2,1)}, f32[128,2304]{1,0:T(8,128)}, f32[128,2304]{1,0:T(8,128)}) fusion(bf16[128,2304]{1,0:T(8,128)(2,1)S(1)} %copy-done.6, f32[128,2304]{1,0:T(8,128)S(1)} %copy-done.2, f32[128,2304]{1,0:T(8,128)S(1)} %copy-done.3, bf16[256,2304]{1,0:T(8,128)(2,1)S(1)} %constant_dynamic-update-slice_fusion.16, ...), kind=kOutput, calls=%fused_computation.12 | convolution fusion | flops 155254784 | bytes 7143424 | tf_op jit(solution)/shard_map/dot_general | solution.py:19
  73.8 5.0 %subtract_convert_fusion.1 = (bf16[128,2304]{1,0:T(8,128)(2,1)}, f32[128,2304]{1,0:T(8,128)}, f32[128,2304]{1,0:T(8,128)}) fusion(bf16[128,2304]{1,0:T(8,128)(2,1)} %param.10, f32[128,2304]{1,0:T(8,128)S(1)} %copy-done.4, f32[128,2304]{1,0:T(8,128)} %param.15, bf16[128,2304]{1,0:T(8,128)(2,1)} %collective-permute-done.26, ...), kind=kOutput, calls=%fused_computation.15 | convolution fusion | flops 308674560 | bytes 8912896 | tf_op jit(solution)/shard_map/dot_general | solution.py:19
  (62 shorter events, 1.7 us)
Async XLA Ops:
  0.6 27.8 %copy-start.5 = (bf16[128,2304]{1,0:T(8,128)(2,1)S(1)}, bf16[128,2304]{1,0:T(8,128)(2,1)}, u32[]{:S(2)}) copy-start(bf16[128,2304]{1,0:T(8,128)(2,1)} %param.10) | copy-start | bytes 1769476
  0.6 27.6 %copy-start.1 = (f32[2304]{0:T(1024)S(1)}, f32[2304]{0:T(1024)}, u32[]{:S(2)}) copy-start(f32[2304]{0:T(1024)} %param.13) | copy-start | bytes 27652
  0.7 22.9 %collective-permute-start.5 = (bf16[16,2304]{1,0:T(8,128)(2,1)}, bf16[16,2304]{1,0:T(8,128)(2,1)S(1)}, u32[]{:S(2)}, u32[]{:S(2)}) collective-permute-start(bf16[16,2304]{1,0:T(8,128)(2,1)} %param.9), channel_id=1, source_target_pairs={{0,12},{1,13},{2,14},{3,15},{4,8},{5,9},{6,10},{7,11},{8,4},{9,5},... | collective-permute-start | bytes 221192 | tf_op jit(solution)/shard_map/ppermute | solution.py:36
  5.8 17.8 %collective-permute-start.4 = (bf16[16,2304]{1,0:T(8,128)(2,1)}, bf16[16,2304]{1,0:T(8,128)(2,1)S(1)}, u32[]{:S(2)}, u32[]{:S(2)}) collective-permute-start(bf16[16,2304]{1,0:T(8,128)(2,1)} %param.9), channel_id=1, source_target_pairs={{0,10},{1,11},{2,8},{3,9},{4,14},{5,15},{6,12},{7,13},{8,2},{9,3},... | collective-permute-start | bytes 221192 | tf_op jit(solution)/shard_map/ppermute | solution.py:36
  6.2 16.8 %collective-permute-start.3 = (bf16[16,2304]{1,0:T(8,128)(2,1)}, bf16[16,2304]{1,0:T(8,128)(2,1)S(1)}, u32[]{:S(2)}, u32[]{:S(2)}) collective-permute-start(bf16[16,2304]{1,0:T(8,128)(2,1)} %param.9), channel_id=1, source_target_pairs={{0,8},{1,9},{2,10},{3,11},{4,12},{5,13},{6,14},{7,15},{8,0},{9,1},... | collective-permute-start | bytes 221192 | tf_op jit(solution)/shard_map/ppermute | solution.py:36
  9.7 13.2 %collective-permute-start.2 = (bf16[16,2304]{1,0:T(8,128)(2,1)}, bf16[16,2304]{1,0:T(8,128)(2,1)S(1)}, u32[]{:S(2)}, u32[]{:S(2)}) collective-permute-start(bf16[16,2304]{1,0:T(8,128)(2,1)} %param.9), channel_id=1, source_target_pairs={{0,6},{1,7},{2,4},{3,5},{4,2},{5,3},{6,0},{7,1},{8,14},{9,15},{10,... | collective-permute-start | bytes 221192 | tf_op jit(solution)/shard_map/ppermute | solution.py:36
  9.7 1.3 %collective-permute-start.8 = (f32[128]{0:T(128)}, f32[128]{0:T(128)S(1)}, u32[]{:S(2)}, u32[]{:S(2)}) collective-permute-start(f32[128]{0:T(128)} %param.11), channel_id=1, source_target_pairs={{0,1},{1,0},{2,3},{3,2},{4,5},{5,4},{6,7},{7,6},{8,9},{9,8},{10,11... | collective-permute-start | bytes 1544 | tf_op jit(solution)/shard_map/ppermute | solution.py:43
  10.9 5.5 %collective-permute-start = (bf16[16,2304]{1,0:T(8,128)(2,1)}, bf16[16,2304]{1,0:T(8,128)(2,1)S(1)}, u32[]{:S(2)}, u32[]{:S(2)}) collective-permute-start(bf16[16,2304]{1,0:T(8,128)(2,1)} %param.9), channel_id=1, source_target_pairs={{0,2},{1,3},{2,0},{3,1},{4,6},{5,7},{6,4},{7,5},{8,10},{9,11},{10,... | collective-permute-start | bytes 221192 | tf_op jit(solution)/shard_map/ppermute | solution.py:36
  16.4 4.6 %collective-permute-start.1 = (bf16[16,2304]{1,0:T(8,128)(2,1)}, bf16[16,2304]{1,0:T(8,128)(2,1)S(1)}, u32[]{:S(2)}, u32[]{:S(2)}) collective-permute-start(bf16[16,2304]{1,0:T(8,128)(2,1)} %param.9), channel_id=1, source_target_pairs={{0,4},{1,5},{2,6},{3,7},{4,0},{5,1},{6,2},{7,3},{8,12},{9,13},{10,... | collective-permute-start | bytes 221192 | tf_op jit(solution)/shard_map/ppermute | solution.py:36
  21.0 7.3 %collective-permute-start.6 = (bf16[16,2304]{1,0:T(8,128)(2,1)}, bf16[16,2304]{1,0:T(8,128)(2,1)S(1)}, u32[]{:S(2)}, u32[]{:S(2)}) collective-permute-start(bf16[16,2304]{1,0:T(8,128)(2,1)} %param.9), channel_id=1, source_target_pairs={{0,14},{1,15},{2,12},{3,13},{4,10},{5,11},{6,8},{7,9},{8,6},{9,7},... | collective-permute-start | bytes 221192 | tf_op jit(solution)/shard_map/ppermute | solution.py:36
  22.9 5.5 %collective-permute-start.7 = (bf16[128,2304]{1,0:T(8,128)(2,1)}, bf16[128,2304]{1,0:T(8,128)(2,1)S(1)}, u32[]{:S(2)}, u32[]{:S(2)}) collective-permute-start(bf16[128,2304]{1,0:T(8,128)(2,1)} %param.10), channel_id=1, source_target_pairs={{0,1},{1,0},{2,3},{3,2},{4,5},{5,4},{6,7},{7,6},{8,9},{9,8},{10,11... | collective-permute-start | bytes 1769480 | tf_op jit(solution)/shard_map/ppermute | solution.py:43
  23.0 6.0 %collective-permute-start.9 = (bf16[128,2304]{1,0:T(8,128)(2,1)}, bf16[128,2304]{1,0:T(8,128)(2,1)S(1)}, u32[]{:S(2)}, u32[]{:S(2)}) collective-permute-start(bf16[128,2304]{1,0:T(8,128)(2,1)} %param.12), channel_id=1, source_target_pairs={{0,1},{1,0},{2,3},{3,2},{4,5},{5,4},{6,7},{7,6},{8,9},{9,8},{10,11... | collective-permute-start | bytes 1769480 | tf_op jit(solution)/shard_map/ppermute | solution.py:43
  29.8 8.5 %collective-permute-start.10 = (bf16[16,2304]{1,0:T(8,128)(2,1)S(1)}, bf16[16,2304]{1,0:T(8,128)(2,1)S(1)}, u32[]{:S(2)}, u32[]{:S(2)}) collective-permute-start(bf16[16,2304]{1,0:T(8,128)(2,1)S(1)} %get-tuple-element.15), channel_id=1, source_target_pairs={{0,2},{1,3},{2,0},{3,1},{4,6},{5,7},{6,4},{7,5},{8,10},{9,11},{10,... | collective-permute-start | bytes 221192 | tf_op jit(solution)/shard_map/ppermute | solution.py:36
  30.6 7.7 %collective-permute-start.16 = (bf16[16,2304]{1,0:T(8,128)(2,1)S(1)}, bf16[16,2304]{1,0:T(8,128)(2,1)S(1)}, u32[]{:S(2)}, u32[]{:S(2)}) collective-permute-start(bf16[16,2304]{1,0:T(8,128)(2,1)S(1)} %get-tuple-element.16), channel_id=1, source_target_pairs={{0,14},{1,15},{2,12},{3,13},{4,10},{5,11},{6,8},{7,9},{8,6},{9,7},... | collective-permute-start | bytes 221192 | tf_op jit(solution)/shard_map/ppermute | solution.py:36
  32.6 8.5 %collective-permute-start.15 = (bf16[16,2304]{1,0:T(8,128)(2,1)S(1)}, bf16[16,2304]{1,0:T(8,128)(2,1)S(1)}, u32[]{:S(2)}, u32[]{:S(2)}) collective-permute-start(bf16[16,2304]{1,0:T(8,128)(2,1)S(1)} %get-tuple-element.17), channel_id=1, source_target_pairs={{0,12},{1,13},{2,14},{3,15},{4,8},{5,9},{6,10},{7,11},{8,4},{9,5},... | collective-permute-start | bytes 221192 | tf_op jit(solution)/shard_map/ppermute | solution.py:36
  35.2 9.1 %collective-permute-start.14 = (bf16[16,2304]{1,0:T(8,128)(2,1)S(1)}, bf16[16,2304]{1,0:T(8,128)(2,1)S(1)}, u32[]{:S(2)}, u32[]{:S(2)}) collective-permute-start(bf16[16,2304]{1,0:T(8,128)(2,1)S(1)} %get-tuple-element.18), channel_id=1, source_target_pairs={{0,10},{1,11},{2,8},{3,9},{4,14},{5,15},{6,12},{7,13},{8,2},{9,3},... | collective-permute-start | bytes 221192 | tf_op jit(solution)/shard_map/ppermute | solution.py:36
  35.2 9.1 %collective-permute-start.13 = (bf16[16,2304]{1,0:T(8,128)(2,1)S(1)}, bf16[16,2304]{1,0:T(8,128)(2,1)S(1)}, u32[]{:S(2)}, u32[]{:S(2)}) collective-permute-start(bf16[16,2304]{1,0:T(8,128)(2,1)S(1)} %get-tuple-element.19), channel_id=1, source_target_pairs={{0,8},{1,9},{2,10},{3,11},{4,12},{5,13},{6,14},{7,15},{8,0},{9,1},... | collective-permute-start | bytes 221192 | tf_op jit(solution)/shard_map/ppermute | solution.py:36
  38.3 7.2 %collective-permute-start.12 = (bf16[16,2304]{1,0:T(8,128)(2,1)S(1)}, bf16[16,2304]{1,0:T(8,128)(2,1)S(1)}, u32[]{:S(2)}, u32[]{:S(2)}) collective-permute-start(bf16[16,2304]{1,0:T(8,128)(2,1)S(1)} %get-tuple-element.20), channel_id=1, source_target_pairs={{0,6},{1,7},{2,4},{3,5},{4,2},{5,3},{6,0},{7,1},{8,14},{9,15},{10,... | collective-permute-start | bytes 221192 | tf_op jit(solution)/shard_map/ppermute | solution.py:36
  38.3 7.5 %collective-permute-start.11 = (bf16[16,2304]{1,0:T(8,128)(2,1)S(1)}, bf16[16,2304]{1,0:T(8,128)(2,1)S(1)}, u32[]{:S(2)}, u32[]{:S(2)}) collective-permute-start(bf16[16,2304]{1,0:T(8,128)(2,1)S(1)} %get-tuple-element.21), channel_id=1, source_target_pairs={{0,4},{1,5},{2,6},{3,7},{4,0},{5,1},{6,2},{7,3},{8,12},{9,13},{10,... | collective-permute-start | bytes 221192 | tf_op jit(solution)/shard_map/ppermute | solution.py:36
  45.9 25.3 %copy-start = (bf16[16,2304]{1,0:T(8,128)(2,1)}, bf16[16,2304]{1,0:T(8,128)(2,1)S(1)}, u32[]{:S(2)}) copy-start(bf16[16,2304]{1,0:T(8,128)(2,1)S(1)} %get-tuple-element.14) | copy-start | bytes 221188
  45.9 23.1 %collective-permute-start.24 = (bf16[16,2304]{1,0:T(8,128)(2,1)S(1)}, bf16[16,2304]{1,0:T(8,128)(2,1)S(1)}, u32[]{:S(2)}, u32[]{:S(2)}) collective-permute-start(bf16[16,2304]{1,0:T(8,128)(2,1)S(1)} %get-tuple-element.14), channel_id=1, source_target_pairs={{0,14},{1,15},{2,12},{3,13},{4,10},{5,11},{6,8},{7,9},{8,6},{9,7},... | collective-permute-start | bytes 221192 | tf_op jit(solution)/shard_map/ppermute | solution.py:36
  47.1 21.8 %collective-permute-start.23 = (bf16[16,2304]{1,0:T(8,128)(2,1)S(1)}, bf16[16,2304]{1,0:T(8,128)(2,1)S(1)}, u32[]{:S(2)}, u32[]{:S(2)}) collective-permute-start(bf16[16,2304]{1,0:T(8,128)(2,1)S(1)} %get-tuple-element.14), channel_id=1, source_target_pairs={{0,12},{1,13},{2,14},{3,15},{4,8},{5,9},{6,10},{7,11},{8,4},{9,5},... | collective-permute-start | bytes 221192 | tf_op jit(solution)/shard_map/ppermute | solution.py:36
  50.3 18.6 %collective-permute-start.22 = (bf16[16,2304]{1,0:T(8,128)(2,1)S(1)}, bf16[16,2304]{1,0:T(8,128)(2,1)S(1)}, u32[]{:S(2)}, u32[]{:S(2)}) collective-permute-start(bf16[16,2304]{1,0:T(8,128)(2,1)S(1)} %get-tuple-element.14), channel_id=1, source_target_pairs={{0,10},{1,11},{2,8},{3,9},{4,14},{5,15},{6,12},{7,13},{8,2},{9,3},... | collective-permute-start | bytes 221192 | tf_op jit(solution)/shard_map/ppermute | solution.py:36
  50.3 18.6 %collective-permute-start.21 = (bf16[16,2304]{1,0:T(8,128)(2,1)S(1)}, bf16[16,2304]{1,0:T(8,128)(2,1)S(1)}, u32[]{:S(2)}, u32[]{:S(2)}) collective-permute-start(bf16[16,2304]{1,0:T(8,128)(2,1)S(1)} %get-tuple-element.14), channel_id=1, source_target_pairs={{0,8},{1,9},{2,10},{3,11},{4,12},{5,13},{6,14},{7,15},{8,0},{9,1},... | collective-permute-start | bytes 221192 | tf_op jit(solution)/shard_map/ppermute | solution.py:36
  53.6 5.1 %collective-permute-start.18 = (bf16[16,2304]{1,0:T(8,128)(2,1)S(1)}, bf16[16,2304]{1,0:T(8,128)(2,1)S(1)}, u32[]{:S(2)}, u32[]{:S(2)}) collective-permute-start(bf16[16,2304]{1,0:T(8,128)(2,1)S(1)} %get-tuple-element.14), channel_id=1, source_target_pairs={{0,2},{1,3},{2,0},{3,1},{4,6},{5,7},{6,4},{7,5},{8,10},{9,11},{10,... | collective-permute-start | bytes 221192 | tf_op jit(solution)/shard_map/ppermute | solution.py:36
  58.7 4.9 %collective-permute-start.19 = (bf16[16,2304]{1,0:T(8,128)(2,1)S(1)}, bf16[16,2304]{1,0:T(8,128)(2,1)S(1)}, u32[]{:S(2)}, u32[]{:S(2)}) collective-permute-start(bf16[16,2304]{1,0:T(8,128)(2,1)S(1)} %get-tuple-element.14), channel_id=1, source_target_pairs={{0,4},{1,5},{2,6},{3,7},{4,0},{5,1},{6,2},{7,3},{8,12},{9,13},{10,... | collective-permute-start | bytes 221192 | tf_op jit(solution)/shard_map/ppermute | solution.py:36
  63.6 5.3 %collective-permute-start.20 = (bf16[16,2304]{1,0:T(8,128)(2,1)S(1)}, bf16[16,2304]{1,0:T(8,128)(2,1)S(1)}, u32[]{:S(2)}, u32[]{:S(2)}) collective-permute-start(bf16[16,2304]{1,0:T(8,128)(2,1)S(1)} %get-tuple-element.14), channel_id=1, source_target_pairs={{0,6},{1,7},{2,4},{3,5},{4,2},{5,3},{6,0},{7,1},{8,14},{9,15},{10,... | collective-permute-start | bytes 221192 | tf_op jit(solution)/shard_map/ppermute | solution.py:36
  68.8 2.4 %copy-start.3 = (f32[128,2304]{1,0:T(8,128)S(1)}, f32[128,2304]{1,0:T(8,128)}, u32[]{:S(2)}) copy-start(f32[128,2304]{1,0:T(8,128)} %param.17) | copy-start | bytes 3538948
  69.0 2.1 %collective-permute-start.25 = (bf16[128,2304]{1,0:T(8,128)(2,1)S(1)}, bf16[128,2304]{1,0:T(8,128)(2,1)S(1)}, u32[]{:S(2)}, u32[]{:S(2)}) collective-permute-start(bf16[128,2304]{1,0:T(8,128)(2,1)S(1)} %get-tuple-element.22), channel_id=1, source_target_pairs={{0,1},{1,0},{2,3},{3,2},{4,5},{5,4},{6,7},{7,6},{8,9},{9,8},{10,11... | collective-permute-start | bytes 1769480 | tf_op jit(solution)/shard_map/ppermute | solution.py:43
  69.1 4.8 %collective-permute-start.26 = (bf16[128,2304]{1,0:T(8,128)(2,1)S(1)}, bf16[128,2304]{1,0:T(8,128)(2,1)}, u32[]{:S(2)}, u32[]{:S(2)}) collective-permute-start(bf16[128,2304]{1,0:T(8,128)(2,1)S(1)} %subtract_convert_fusion.2), channel_id=1, source_target_pairs={{0,1},{1,0},{2,3},{3,2},{4,5},{5,4},{6,7},{7,6},{8,9},{9,8},{10,11... | collective-permute-start | bytes 1769480 | tf_op jit(solution)/shard_map/ppermute | solution.py:43
  69.6 1.6 %collective-permute-start.17 = (bf16[128,128]{1,0:T(8,128)(2,1)S(1)}, bf16[128,128]{1,0:T(8,128)(2,1)S(1)}, u32[]{:S(2)}, u32[]{:S(2)}) collective-permute-start(bf16[128,128]{1,0:T(8,128)(2,1)S(1)} %get-tuple-element.37), channel_id=1, source_target_pairs={{0,1},{1,0},{2,3},{3,2},{4,5},{5,4},{6,7},{7,6},{8,9},{9,8},{10,11... | collective-permute-start | bytes 98312 | tf_op jit(solution)/shard_map/ppermute | solution.py:43
  71.2 2.6 %copy-start.4 = (f32[128,2304]{1,0:T(8,128)S(1)}, f32[128,2304]{1,0:T(8,128)}, u32[]{:S(2)}) copy-start(f32[128,2304]{1,0:T(8,128)} %param.14) | copy-start | bytes 3538948
  (2 other events, 3.4 us)

commit v2 on v1

--- a/solution.py
+++ b/solution.py
@@ -31,10 +31,11 @@
     return (weight_next, moment_next, square_next)
 
 
-def to_chip(block, distance):
+def swap_all(blocks):
     size = lax.axis_size("latent")
-    return lax.ppermute(
-        block, "latent", [(i, i ^ (2 * distance)) for i in range(size)]
+    groups = [list(range(core, size, 2)) for core in range(2)]
+    return lax.all_to_all(
+        blocks, "latent", split_axis=0, concat_axis=0, axis_index_groups=groups, tiled=False
     )
 
 
@@ -60,12 +61,13 @@
     chips = size // 2
     total_rows = rows_here * size
 
-    row_blocks = [activations] + [to_chip(activations, k) for k in range(1, chips)]
+    rows_core = swap_all(jnp.broadcast_to(activations, (chips, rows_here, width))).reshape(
+        chips * rows_here, width
+    )
     encoder_both = jnp.concatenate([encoder, to_other_core(encoder)], 0)
     decoder_both = jnp.concatenate([decoder, to_other_core(decoder)], 0)
     bias_both = jnp.concatenate([encoder_bias, to_other_core(encoder_bias)], 0)
 
-    rows_core = jnp.concatenate(row_blocks, 0)
     centered = (rows_core.astype(jnp.float32) - decoder_bias).astype(jnp.bfloat16)
     codes = jnp.maximum(inner_last(centered, encoder_both) + bias_both, 0.0).astype(
         jnp.bfloat16
@@ -73,20 +75,19 @@
     partial_sums = jnp.dot(codes, decoder_both, preferred_element_type=jnp.float32).astype(
         jnp.bfloat16
     )
-    summed = partial_sums[:rows_here].astype(jnp.float32)
-    arrived = [
-        to_chip(partial_sums[k * rows_here : (k + 1) * rows_here], k) for k in range(1, chips)
-    ]
-    for block in arrived:
-        summed = summed + block.astype(jnp.float32)
-    row_error = (summed - centered[:rows_here].astype(jnp.float32)).astype(jnp.bfloat16)
+    arrived = swap_all(partial_sums.reshape(chips, rows_here, width))
+    summed = jnp.sum(arrived.astype(jnp.float32), 0)
+    centered_own = (activations.astype(jnp.float32) - decoder_bias).astype(jnp.bfloat16)
+    row_error = (summed - centered_own.astype(jnp.float32)).astype(jnp.bfloat16)
 
     other_codes = to_other_core(codes[:, latents_here:])
     other_centered = to_other_core(centered)
     codes_all = jnp.concatenate([codes[:, :latents_here], other_codes], 0)
     centered_all = jnp.concatenate([centered, other_centered], 0)
 
-    error_core = jnp.concatenate([row_error] + [to_chip(row_error, k) for k in range(1, chips)], 0)
+    error_core = swap_all(jnp.broadcast_to(row_error, (chips, rows_here, width))).reshape(
+        chips * rows_here, width
+    )
     error_all = jnp.concatenate([error_core, to_other_core(error_core)], 0)
 
     decoder_grad = inner_first(codes_all, error_all) / total_rows

time: 79.1 us -> 77.6 us (0.981)
  blocking collectives: 0 us -> 39.7 us
  starting transfers between devices: 34.2 us -> 8.51 us
  waiting for transfers between devices: 32.7 us -> 17.5 us
    all_to_all x0 -> x2, blocking collectives: none -> 39.7 us  [swap_all(): lax.all_to_all(blocks, 'latent', split_axis=0, concat_axis=0, axis_index_...]
    ppermute x21 -> x0, starting transfers between devices: 33 us -> none  [to_chip(): lax.ppermute(block, 'latent', [(i, i ^ 2 * distance) for i in range(size)])]
    ppermute x21 -> x0, waiting for transfers between devices: 30.9 us -> none  [to_chip(): lax.ppermute(block, 'latent', [(i, i ^ 2 * distance) for i in range(size)])]
    all_to_all x0 -> x1, waiting for transfers between devices: none -> 14.7 us  [swap_all(): lax.all_to_all(blocks, 'latent', split_axis=0, concat_axis=0, axis_index_...]
    all_to_all x0 -> x1, starting transfers between devices: none -> 7.28 us  [swap_all(): lax.all_to_all(blocks, 'latent', split_axis=0, concat_axis=0, axis_index_...]
    broadcast_in_dim x0 -> x2, local copies, waits for them, and re-layouts: none -> 1.87 us  [the longest x1 1.83 us: body(): jnp.broadcast_to(activations, (chips, rows_here, width))]
    unnamed x28 -> x22, local copies, waits for them, and re-layouts: 1.58 us -> 0.06 us
    ppermute x6, waiting for transfers between devices: 1.8 us -> 2.84 us  [to_other_core(): return lax.ppermute(block, 'latent', [(i, i ^ 1) for i in range(size)])]
  transfers between devices with their start and end apart: 27 -> 7, of which waited for: 11 -> 3; matrix products, arithmetic and copies ran while one was open for 6% -> 4% of each run, Pallas kernels for 0% -> 0%
where the time goes in v2:
time: 77.6 us; the launch traced here: 77.2 us
  blocking collectives  39.7 us (51%)
  waiting for transfers between devices  17.5 us (23%)
  matrix products  8.52 us (11%)
  starting transfers between devices  8.51 us (11%)
  local copies, waits for them, and re-layouts  1.93 us (2%)
  between operations  0.81 us (1%)
    all_to_all x2, blocking collectives, swap_all(): lax.all_to_all(blocks, 'latent', split_axis=0, concat_axis=0, axis_index_...  39.7 us
    all_to_all x1, waiting for transfers between devices, swap_all(): lax.all_to_all(blocks, 'latent', split_axis=0, concat_axis=0, axis_index_...  14.7 us
    dot_general x2, matrix products, inner_first(): lax.dot_general(left, right, (((0,), (0,)), ((), ())), preferred_element_...  7.64 us
    all_to_all x1, starting transfers between devices, swap_all(): lax.all_to_all(blocks, 'latent', split_axis=0, concat_axis=0, axis_index_...  7.28 us
    ppermute x6, waiting for transfers between devices, to_other_core(): return lax.ppermute(block, 'latent', [(i, i ^ 1) for i in range(size)])  2.84 us
    broadcast_in_dim x1, local copies, waits for them, and re-layouts, body(): jnp.broadcast_to(activations, (chips, rows_here, width))  1.83 us
  transfers between devices with their start and end apart: 7, of which 3 were waited for; matrix products, arithmetic and copies ran while one was open for 4% of the time, Pallas kernels for 0%

profile of v2, /device:TPU:0, one launch (start us, length us, event | category | flops | bytes accessed | tf_op | source)
XLA Modules:
  0.0 77.2 jit_solution(15307427026633071601)
XLA Ops:
  0.7 0.0 copy-start.8
  0.7 1.8 %broadcast_in_dim.13 = bf16[8,16,2304]{2,1,0:T(8,128)(2,1)} broadcast(bf16[16,2304]{1,0:T(8,128)(2,1)} %param.9), dimensions={1,2} | broadcast | bytes 663552 | tf_op jit(solution)/shard_map/broadcast_in_dim | solution.py:64
  2.5 7.3 %all-to-all-start = ((bf16[8,16,2304]{2,1,0:T(8,128)(2,1)}), bf16[8,16,2304]{2,1,0:T(8,128)(2,1)S(1)}, u32[]{:S(2)}, u32[]{:S(2)}) async-start(bf16[8,16,2304]{2,1,0:T(8,128)(2,1)} %broadcast_in_dim.13), calls=%async_computation | async-start | bytes 1179648 | tf_op jit(solution)/shard_map/all_to_all | solution.py:37
  9.8 0.1 collective-permute-start.1
  9.9 0.0 copy-done.7
  9.9 0.5 collective-permute-start
  10.4 0.0 copy-done.8
  10.4 0.1 collective-permute-start.2
  10.5 0.5 collective-permute-done.1
  11.0 14.7 %all-to-all-done = bf16[8,16,2304]{2,1,0:T(8,128)(2,1)S(1)} async-done(((bf16[8,16,2304]{2,1,0:T(8,128)(2,1)}), bf16[8,16,2304]{2,1,0:T(8,128)(2,1)S(1)}, u32[]{:S(2)}, u32[]{:S(2)}) %all-to-all-start) | async-done | bytes 589856 | tf_op jit(solution)/shard_map/all_to_all | solution.py:37
  25.7 0.0 copy-done.2
  25.7 0.1 fusion.11
  25.8 0.0 collective-permute-done
  25.8 0.6 fusion.18
  26.4 0.0 collective-permute-done.2
  26.4 0.3 convolution_convert_fusion
  26.7 0.0 copy-start
  26.7 20.3 %all_to_all.15 = bf16[8,16,2304]{2,1,0:T(8,128)(2,1)S(1)} all-to-all(bf16[8,16,2304]{2,1,0:T(8,128)(2,1)S(1)} %bitcast.11), channel_id=1, replica_groups={{0,2,4,6,8,10,12,14},{1,3,5,7,9,11,13,15},{16,18,20,22,24,26,28,30},{17..., dimensions={0} | all-to-all | bytes 1179648 | tf_op jit(solution)/shard_map/all_to_all | solution.py:37
  47.0 0.1 convert_reduce_fusion
  47.1 0.0 copy-start.4
  47.1 0.0 copy-start.9
  47.2 0.0 copy-start.1
  47.2 19.4 %all_to_all.16 = bf16[8,16,2304]{2,1,0:T(8,128)(2,1)S(1)} all-to-all(bf16[8,16,2304]{2,1,0:T(8,128)(2,1)S(1)} %broadcast_in_dim.14), channel_id=1, replica_groups={{0,2,4,6,8,10,12,14},{1,3,5,7,9,11,13,15},{16,18,20,22,24,26,28,30},{17..., dimensions={0} | all-to-all | bytes 1179648 | tf_op jit(solution)/shard_map/all_to_all | solution.py:37
  66.6 0.0 collective-permute-start.4
  66.6 0.5 collective-permute-start.5
  67.1 0.1 collective-permute-start.3
  67.2 2.3 %collective-permute-done.3 = bf16[128,128]{1,0:T(8,128)(2,1)S(1)} collective-permute-done((bf16[128,128]{1,0:T(8,128)(2,1)S(1)}, bf16[128,128]{1,0:T(8,128)(2,1)S(1)}, u32[]{:S(2)}, u32[]{:S(2)}) %collective-permute-start.3) | collective-permute-done | bytes 32800 | tf_op jit(solution)/shard_map/ppermute | solution.py:44
  69.5 0.0 collective-permute-done.4
  69.5 0.0 copy-start.6
  69.5 2.6 %subtract_convert_fusion = (bf16[128,2304]{1,0:T(8,128)(2,1)}, f32[128,2304]{1,0:T(8,128)}, f32[128,2304]{1,0:T(8,128)}) fusion(bf16[128,2304]{1,0:T(8,128)(2,1)S(1)} %copy-done.9, f32[128,2304]{1,0:T(8,128)S(1)} %copy-done.4, f32[128,2304]{1,0:T(8,128)S(1)} %copy-done.5, bf16[128,2304]{1,0:T(8,128)(2,1)S(1)} %collective-permute-done.4, ...), kind=kOutput, calls=%fused_computation.15 | convolution fusion | flops 157614080 | bytes 7143424 | tf_op jit(solution)/shard_map/dot_general | solution.py:19
  72.2 0.0 collective-permute-done.5
  72.2 5.0 %subtract_convert_fusion.1 = (bf16[128,2304]{1,0:T(8,128)(2,1)}, f32[128,2304]{1,0:T(8,128)}, f32[128,2304]{1,0:T(8,128)}) fusion(bf16[128,2304]{1,0:T(8,128)(2,1)S(1)} %copy-done.7, f32[128,2304]{1,0:T(8,128)S(1)} %copy-done.6, f32[128,2304]{1,0:T(8,128)} %param.15, bf16[128,2304]{1,0:T(8,128)(2,1)} %collective-permute-done.5, ...), kind=kOutput, calls=%fused_computation.18 | convolution fusion | flops 311066624 | bytes 8912896 | tf_op jit(solution)/shard_map/dot_general | solution.py:19
  (17 shorter events, 0.1 us)
Async XLA Ops:
  0.6 9.2 %copy-start.3 = (f32[128]{0:T(128)S(1)}, f32[128]{0:T(128)}, u32[]{:S(2)}) copy-start(f32[128]{0:T(128)} %param.11) | copy-start | bytes 1540
  0.6 9.2 %copy-start.7 = (bf16[128,2304]{1,0:T(8,128)(2,1)S(1)}, bf16[128,2304]{1,0:T(8,128)(2,1)}, u32[]{:S(2)}) copy-start(bf16[128,2304]{1,0:T(8,128)(2,1)} %param.10) | copy-start | bytes 1769476
  0.7 9.7 %copy-start.8 = (bf16[128,2304]{1,0:T(8,128)(2,1)S(1)}, bf16[128,2304]{1,0:T(8,128)(2,1)}, u32[]{:S(2)}) copy-start(bf16[128,2304]{1,0:T(8,128)(2,1)} %param.12) | copy-start | bytes 1769476
  0.7 25.0 %copy-start.2 = (f32[2304]{0:T(1024)S(1)}, f32[2304]{0:T(1024)}, u32[]{:S(2)}) copy-start(f32[2304]{0:T(1024)} %param.13) | copy-start | bytes 27652
  2.5 23.2 %all-to-all-start = ((bf16[8,16,2304]{2,1,0:T(8,128)(2,1)}), bf16[8,16,2304]{2,1,0:T(8,128)(2,1)S(1)}, u32[]{:S(2)}, u32[]{:S(2)}) async-start(bf16[8,16,2304]{2,1,0:T(8,128)(2,1)} %broadcast_in_dim.13), calls=%async_computation | async-start | bytes 1179648 | tf_op jit(solution)/shard_map/all_to_all | solution.py:37
  9.8 1.2 %collective-permute-start.1 = (f32[128]{0:T(128)S(1)}, f32[128]{0:T(128)S(1)}, u32[]{:S(2)}, u32[]{:S(2)}) collective-permute-start(f32[128]{0:T(128)S(1)} %copy-done.3), channel_id=1, source_target_pairs={{0,1},{1,0},{2,3},{3,2},{4,5},{5,4},{6,7},{7,6},{8,9},{9,8},{10,11... | collective-permute-start | bytes 1544 | tf_op jit(solution)/shard_map/ppermute | solution.py:44
  9.9 15.9 %collective-permute-start = (bf16[128,2304]{1,0:T(8,128)(2,1)S(1)}, bf16[128,2304]{1,0:T(8,128)(2,1)S(1)}, u32[]{:S(2)}, u32[]{:S(2)}) collective-permute-start(bf16[128,2304]{1,0:T(8,128)(2,1)S(1)} %copy-done.7), channel_id=1, source_target_pairs={{0,1},{1,0},{2,3},{3,2},{4,5},{5,4},{6,7},{7,6},{8,9},{9,8},{10,11... | collective-permute-start | bytes 1769480 | tf_op jit(solution)/shard_map/ppermute | solution.py:44
  10.4 16.0 %collective-permute-start.2 = (bf16[128,2304]{1,0:T(8,128)(2,1)S(1)}, bf16[128,2304]{1,0:T(8,128)(2,1)S(1)}, u32[]{:S(2)}, u32[]{:S(2)}) collective-permute-start(bf16[128,2304]{1,0:T(8,128)(2,1)S(1)} %copy-done.8), channel_id=1, source_target_pairs={{0,1},{1,0},{2,3},{3,2},{4,5},{5,4},{6,7},{7,6},{8,9},{9,8},{10,11... | collective-permute-start | bytes 1769480 | tf_op jit(solution)/shard_map/ppermute | solution.py:44
  26.7 20.4 %copy-start = (bf16[16,2304]{1,0:T(8,128)(2,1)S(1)}, bf16[16,2304]{1,0:T(8,128)(2,1)}, u32[]{:S(2)}) copy-start(bf16[16,2304]{1,0:T(8,128)(2,1)} %param.9) | copy-start | bytes 221188
  47.0 22.5 %copy-start.5 = (f32[128,2304]{1,0:T(8,128)S(1)}, f32[128,2304]{1,0:T(8,128)}, u32[]{:S(2)}) copy-start(f32[128,2304]{1,0:T(8,128)} %param.17) | copy-start | bytes 3538948
  47.1 22.4 %copy-start.4 = (f32[128,2304]{1,0:T(8,128)S(1)}, f32[128,2304]{1,0:T(8,128)}, u32[]{:S(2)}) copy-start(f32[128,2304]{1,0:T(8,128)} %param.16) | copy-start | bytes 3538948
  47.1 22.4 %copy-start.9 = (bf16[128,2304]{1,0:T(8,128)(2,1)S(1)}, bf16[128,2304]{1,0:T(8,128)(2,1)}, u32[]{:S(2)}) copy-start(bf16[128,2304]{1,0:T(8,128)(2,1)} %param.12) | copy-start | bytes 1769476
  47.2 25.0 %copy-start.1 = (bf16[16,2304]{1,0:T(8,128)(2,1)}, bf16[16,2304]{1,0:T(8,128)(2,1)S(1)}, u32[]{:S(2)}) copy-start(bf16[16,2304]{1,0:T(8,128)(2,1)S(1)} %subtract_convert_fusion.2) | copy-start | bytes 221188
  66.6 2.9 %collective-permute-start.4 = (bf16[128,2304]{1,0:T(8,128)(2,1)S(1)}, bf16[128,2304]{1,0:T(8,128)(2,1)S(1)}, u32[]{:S(2)}, u32[]{:S(2)}) collective-permute-start(bf16[128,2304]{1,0:T(8,128)(2,1)S(1)} %bitcast.8), channel_id=1, source_target_pairs={{0,1},{1,0},{2,3},{3,2},{4,5},{5,4},{6,7},{7,6},{8,9},{9,8},{10,11... | collective-permute-start | bytes 1769480 | tf_op jit(solution)/shard_map/ppermute | solution.py:44
  66.6 5.6 %collective-permute-start.5 = (bf16[128,2304]{1,0:T(8,128)(2,1)S(1)}, bf16[128,2304]{1,0:T(8,128)(2,1)}, u32[]{:S(2)}, u32[]{:S(2)}) collective-permute-start(bf16[128,2304]{1,0:T(8,128)(2,1)S(1)} %fusion.11), channel_id=1, source_target_pairs={{0,1},{1,0},{2,3},{3,2},{4,5},{5,4},{6,7},{7,6},{8,9},{9,8},{10,11... | collective-permute-start | bytes 1769480 | tf_op jit(solution)/shard_map/ppermute | solution.py:44
  67.1 2.4 %collective-permute-start.3 = (bf16[128,128]{1,0:T(8,128)(2,1)S(1)}, bf16[128,128]{1,0:T(8,128)(2,1)S(1)}, u32[]{:S(2)}, u32[]{:S(2)}) collective-permute-start(bf16[128,128]{1,0:T(8,128)(2,1)S(1)} %get-tuple-element.14), channel_id=1, source_target_pairs={{0,1},{1,0},{2,3},{3,2},{4,5},{5,4},{6,7},{7,6},{8,9},{9,8},{10,11... | collective-permute-start | bytes 98312 | tf_op jit(solution)/shard_map/ppermute | solution.py:44
  69.5 2.7 %copy-start.10 = (bf16[128,2304]{1,0:T(8,128)(2,1)}, bf16[128,2304]{1,0:T(8,128)(2,1)S(1)}, u32[]{:S(2)}) copy-start(bf16[128,2304]{1,0:T(8,128)(2,1)S(1)} %collective-permute-done.4) | copy-start | bytes 1769476
  69.5 2.7 %copy-start.6 = (f32[128,2304]{1,0:T(8,128)S(1)}, f32[128,2304]{1,0:T(8,128)}, u32[]{:S(2)}) copy-start(f32[128,2304]{1,0:T(8,128)} %param.14) | copy-start | bytes 3538948

commit v3 on v1

--- a/solution.py
+++ b/solution.py
@@ -43,6 +43,27 @@
     return lax.ppermute(block, "latent", [(i, i ^ 1) for i in range(size)])
 
 
+def gather_chips(block, chips):
+    far = [to_chip(block, k) for k in range(2, chips, 2)]
+    blocks = [block, to_chip(block, 1)]
+    for one in far:
+        blocks += [one, to_chip(one, 1)]
+    return blocks
+
+
+def sum_chips(blocks):
+    pairs = []
+    for k in range(0, len(blocks), 2):
+        pairs.append(
+            blocks[k].astype(jnp.float32)
+            + to_chip(blocks[k + 1].astype(jnp.bfloat16), 1).astype(jnp.float32)
+        )
+    summed = pairs[0]
+    for k, pair in enumerate(pairs[1:], 1):
+        summed = summed + to_chip(pair.astype(jnp.bfloat16), 2 * k).astype(jnp.float32)
+    return summed
+
+
 def body(
     activations,
     encoder,
@@ -60,7 +81,7 @@
     chips = size // 2
     total_rows = rows_here * size
 
-    row_blocks = [activations] + [to_chip(activations, k) for k in range(1, chips)]
+    row_blocks = gather_chips(activations, chips)
     encoder_both = jnp.concatenate([encoder, to_other_core(encoder)], 0)
     decoder_both = jnp.concatenate([decoder, to_other_core(decoder)], 0)
     bias_both = jnp.concatenate([encoder_bias, to_other_core(encoder_bias)], 0)
@@ -70,15 +91,10 @@
     codes = jnp.maximum(inner_last(centered, encoder_both) + bias_both, 0.0).astype(
         jnp.bfloat16
     )
-    partial_sums = jnp.dot(codes, decoder_both, preferred_element_type=jnp.float32).astype(
-        jnp.bfloat16
+    partial_sums = jnp.dot(codes, decoder_both, preferred_element_type=jnp.float32)
+    summed = sum_chips(
+        [partial_sums[k * rows_here : (k + 1) * rows_here] for k in range(chips)]
     )
-    summed = partial_sums[:rows_here].astype(jnp.float32)
-    arrived = [
-        to_chip(partial_sums[k * rows_here : (k + 1) * rows_here], k) for k in range(1, chips)
-    ]
-    for block in arrived:
-        summed = summed + block.astype(jnp.float32)
     row_error = (summed - centered[:rows_here].astype(jnp.float32)).astype(jnp.bfloat16)
 
     other_codes = to_other_core(codes[:, latents_here:])
@@ -86,7 +102,7 @@
     codes_all = jnp.concatenate([codes[:, :latents_here], other_codes], 0)
     centered_all = jnp.concatenate([centered, other_centered], 0)
 
-    error_core = jnp.concatenate([row_error] + [to_chip(row_error, k) for k in range(1, chips)], 0)
+    error_core = jnp.concatenate(gather_chips(row_error, chips), 0)
     error_all = jnp.concatenate([error_core, to_other_core(error_core)], 0)
 
     decoder_grad = inner_first(codes_all, error_all) / total_rows

time: 79.1 us -> 61.4 us (0.78)
  waiting for transfers between devices: 32.7 us -> 21 us
  starting transfers between devices: 34.2 us -> 28.3 us
    ppermute x21, waiting for transfers between devices: 30.9 us -> 19.1 us  [to_chip(): lax.ppermute(block, 'latent', [(i, i ^ 2 * distance) for i in range(size)])]
    ppermute x21, starting transfers between devices: 33 us -> 27.1 us  [to_chip(): lax.ppermute(block, 'latent', [(i, i ^ 2 * distance) for i in range(size)])]
  transfers between devices with their start and end apart: 27 -> 27, of which waited for: 11 -> 14; matrix products, arithmetic and copies ran while one was open for 6% -> 8% of each run, Pallas kernels for 0% -> 0%
where the time goes in v3:
time: 61.4 us; the launch traced here: 61.1 us
  starting transfers between devices  28.3 us (46%)
  waiting for transfers between devices  21 us (34%)
  matrix products  8.5 us (14%)
  local copies, waits for them, and re-layouts  1.63 us (3%)
  other arithmetic  0.88 us (1%)
  between operations  0.86 us (1%)
    ppermute x21, starting transfers between devices, to_chip(): lax.ppermute(block, 'latent', [(i, i ^ 2 * distance) for i in range(size)])  27.1 us
    ppermute x21, waiting for transfers between devices, to_chip(): lax.ppermute(block, 'latent', [(i, i ^ 2 * distance) for i in range(size)])  19.1 us
    dot_general x2, matrix products, inner_first(): lax.dot_general(left, right, (((0,), (0,)), ((), ())), preferred_element_...  7.63 us
    ppermute x6, waiting for transfers between devices, to_other_core(): return lax.ppermute(block, 'latent', [(i, i ^ 1) for i in range(size)])  1.83 us
    unnamed x26, local copies, waits for them, and re-layouts  1.54 us
  transfers between devices with their start and end apart: 27, of which 14 were waited for; matrix products, arithmetic and copies ran while one was open for 8% of the time, Pallas kernels for 0%

profile of v3, /device:TPU:0, one launch (start us, length us, event | category | flops | bytes accessed | tf_op | source)
XLA Modules:
  0.0 61.1 jit_solution(3295590953069160304)
XLA Ops:
  0.7 4.1 %collective-permute-start.3 = (bf16[16,2304]{1,0:T(8,128)(2,1)}, bf16[16,2304]{1,0:T(8,128)(2,1)S(1)}, u32[]{:S(2)}, u32[]{:S(2)}) collective-permute-start(bf16[16,2304]{1,0:T(8,128)(2,1)} %param.9), channel_id=1, source_target_pairs={{0,8},{1,9},{2,10},{3,11},{4,12},{5,13},{6,14},{7,15},{8,0},{9,1},... | collective-permute-start | bytes 221192 | tf_op jit(solution)/shard_map/ppermute | solution.py:36
  4.8 1.6 %collective-permute-start.1 = (bf16[16,2304]{1,0:T(8,128)(2,1)}, bf16[16,2304]{1,0:T(8,128)(2,1)S(1)}, u32[]{:S(2)}, u32[]{:S(2)}) collective-permute-start(bf16[16,2304]{1,0:T(8,128)(2,1)} %param.9), channel_id=1, source_target_pairs={{0,4},{1,5},{2,6},{3,7},{4,0},{5,1},{6,2},{7,3},{8,12},{9,13},{10,... | collective-permute-start | bytes 221192 | tf_op jit(solution)/shard_map/ppermute | solution.py:36
  6.3 1.5 %collective-permute-start = (bf16[16,2304]{1,0:T(8,128)(2,1)}, bf16[16,2304]{1,0:T(8,128)(2,1)S(1)}, u32[]{:S(2)}, u32[]{:S(2)}) collective-permute-start(bf16[16,2304]{1,0:T(8,128)(2,1)} %param.9), channel_id=1, source_target_pairs={{0,2},{1,3},{2,0},{3,1},{4,6},{5,7},{6,4},{7,5},{8,10},{9,11},{10,... | collective-permute-start | bytes 221192 | tf_op jit(solution)/shard_map/ppermute | solution.py:36
  8.1 0.9 %constant_dynamic-update-slice_fusion.7 = bf16[128,2304]{1,0:T(8,128)(2,1)S(1)} fusion(bf16[16,2304]{1,0:T(8,128)(2,1)} %param.9), kind=kLoop, calls=%fused_computation.44 | loop fusion | bytes 147456
  9.5 0.7 %pad_maximum_fusion.3 = f32[256]{0:T(256)S(1)} fusion(f32[128]{0:T(128)S(1)} %collective-permute-done.8, f32[128]{0:T(128)} %param.11), kind=kLoop, calls=%fused_computation.64 | loop fusion | flops 256 | bytes 2048 | tf_op jit(solution)/shard_map/concatenate | solution.py:87
  11.0 1.6 %collective-permute-start.2 = (bf16[16,2304]{1,0:T(8,128)(2,1)S(1)}, bf16[16,2304]{1,0:T(8,128)(2,1)S(1)}, u32[]{:S(2)}, u32[]{:S(2)}) collective-permute-start(bf16[16,2304]{1,0:T(8,128)(2,1)S(1)} %collective-permute-done.1), channel_id=1, source_target_pairs={{0,2},{1,3},{2,0},{3,1},{4,6},{5,7},{6,4},{7,5},{8,10},{9,11},{10,... | collective-permute-start | bytes 221192 | tf_op jit(solution)/shard_map/ppermute | solution.py:36
  12.6 1.6 %collective-permute-done.5 = bf16[16,2304]{1,0:T(8,128)(2,1)S(1)} collective-permute-done((bf16[16,2304]{1,0:T(8,128)(2,1)}, bf16[16,2304]{1,0:T(8,128)(2,1)S(1)}, u32[]{:S(2)}, u32[]{:S(2)}) %collective-permute-start.5) | collective-permute-done | bytes 73760 | tf_op jit(solution)/shard_map/ppermute | solution.py:36
  14.2 0.5 collective-permute-start.6
  14.7 2.5 %collective-permute-done.2 = bf16[16,2304]{1,0:T(8,128)(2,1)S(1)} collective-permute-done((bf16[16,2304]{1,0:T(8,128)(2,1)S(1)}, bf16[16,2304]{1,0:T(8,128)(2,1)S(1)}, u32[]{:S(2)}, u32[]{:S(2)}) %collective-permute-start.2) | collective-permute-done | bytes 73760 | tf_op jit(solution)/shard_map/ppermute | solution.py:36
  17.3 1.3 %collective-permute-done.6 = bf16[16,2304]{1,0:T(8,128)(2,1)S(1)} collective-permute-done((bf16[16,2304]{1,0:T(8,128)(2,1)S(1)}, bf16[16,2304]{1,0:T(8,128)(2,1)S(1)}, u32[]{:S(2)}, u32[]{:S(2)}) %collective-permute-start.6) | collective-permute-done | bytes 73760 | tf_op jit(solution)/shard_map/ppermute | solution.py:36
  18.7 0.5 fusion.18
  20.1 0.6 collective-permute-start.15
  20.7 1.5 %collective-permute-start.13 = (bf16[16,2304]{1,0:T(8,128)(2,1)S(1)}, bf16[16,2304]{1,0:T(8,128)(2,1)S(1)}, u32[]{:S(2)}, u32[]{:S(2)}) collective-permute-start(bf16[16,2304]{1,0:T(8,128)(2,1)S(1)} %get-tuple-element.20), channel_id=1, source_target_pairs={{0,2},{1,3},{2,0},{3,1},{4,6},{5,7},{6,4},{7,5},{8,10},{9,11},{10,... | collective-permute-start | bytes 221192 | tf_op jit(solution)/shard_map/ppermute | solution.py:36
  22.7 1.5 %collective-permute-start.10 = (bf16[16,2304]{1,0:T(8,128)(2,1)S(1)}, bf16[16,2304]{1,0:T(8,128)(2,1)S(1)}, u32[]{:S(2)}, u32[]{:S(2)}) collective-permute-start(bf16[16,2304]{1,0:T(8,128)(2,1)S(1)} %get-tuple-element.18), channel_id=1, source_target_pairs={{0,2},{1,3},{2,0},{3,1},{4,6},{5,7},{6,4},{7,5},{8,10},{9,11},{10,... | collective-permute-start | bytes 221192 | tf_op jit(solution)/shard_map/ppermute | solution.py:36
  24.2 1.2 %collective-permute-done.15 = bf16[16,2304]{1,0:T(8,128)(2,1)S(1)} collective-permute-done((bf16[16,2304]{1,0:T(8,128)(2,1)S(1)}, bf16[16,2304]{1,0:T(8,128)(2,1)S(1)}, u32[]{:S(2)}, u32[]{:S(2)}) %collective-permute-start.15) | collective-permute-done | bytes 73760 | tf_op jit(solution)/shard_map/ppermute | solution.py:36
  25.4 0.9 %collective-permute-done.13 = bf16[16,2304]{1,0:T(8,128)(2,1)S(1)} collective-permute-done((bf16[16,2304]{1,0:T(8,128)(2,1)S(1)}, bf16[16,2304]{1,0:T(8,128)(2,1)S(1)}, u32[]{:S(2)}, u32[]{:S(2)}) %collective-permute-start.13) | collective-permute-done | bytes 73760 | tf_op jit(solution)/shard_map/ppermute | solution.py:36
  26.3 0.8 %collective-permute-done.11 = bf16[16,2304]{1,0:T(8,128)(2,1)S(1)} collective-permute-done((bf16[16,2304]{1,0:T(8,128)(2,1)S(1)}, bf16[16,2304]{1,0:T(8,128)(2,1)S(1)}, u32[]{:S(2)}, u32[]{:S(2)}) %collective-permute-start.11) | collective-permute-done | bytes 73760 | tf_op jit(solution)/shard_map/ppermute | solution.py:36
  27.5 3.9 %collective-permute-start.16 = (bf16[16,2304]{1,0:T(8,128)(2,1)S(1)}, bf16[16,2304]{1,0:T(8,128)(2,1)S(1)}, u32[]{:S(2)}, u32[]{:S(2)}) collective-permute-start(bf16[16,2304]{1,0:T(8,128)(2,1)S(1)} %get-tuple-element.16), channel_id=1, source_target_pairs={{0,12},{1,13},{2,14},{3,15},{4,8},{5,9},{6,10},{7,11},{8,4},{9,5},... | collective-permute-start | bytes 221192 | tf_op jit(solution)/shard_map/ppermute | solution.py:36
  32.4 3.0 %collective-permute-done.16 = bf16[16,2304]{1,0:T(8,128)(2,1)S(1)} collective-permute-done((bf16[16,2304]{1,0:T(8,128)(2,1)S(1)}, bf16[16,2304]{1,0:T(8,128)(2,1)S(1)}, u32[]{:S(2)}, u32[]{:S(2)}) %collective-permute-start.16) | collective-permute-done | bytes 73760 | tf_op jit(solution)/shard_map/ppermute | solution.py:36
  35.4 2.5 %collective-permute-done.14 = bf16[16,2304]{1,0:T(8,128)(2,1)S(1)} collective-permute-done((bf16[16,2304]{1,0:T(8,128)(2,1)S(1)}, bf16[16,2304]{1,0:T(8,128)(2,1)S(1)}, u32[]{:S(2)}, u32[]{:S(2)}) %collective-permute-start.14) | collective-permute-done | bytes 73760 | tf_op jit(solution)/shard_map/ppermute | solution.py:36
  37.9 2.7 %collective-permute-start.23 = (bf16[16,2304]{1,0:T(8,128)(2,1)S(1)}, bf16[16,2304]{1,0:T(8,128)(2,1)S(1)}, u32[]{:S(2)}, u32[]{:S(2)}) collective-permute-start(bf16[16,2304]{1,0:T(8,128)(2,1)S(1)} %get-tuple-element.14), channel_id=1, source_target_pairs={{0,12},{1,13},{2,14},{3,15},{4,8},{5,9},{6,10},{7,11},{8,4},{9,5},... | collective-permute-start | bytes 221192 | tf_op jit(solution)/shard_map/ppermute | solution.py:36
  40.6 1.8 %collective-permute-start.19 = (bf16[16,2304]{1,0:T(8,128)(2,1)S(1)}, bf16[16,2304]{1,0:T(8,128)(2,1)S(1)}, u32[]{:S(2)}, u32[]{:S(2)}) collective-permute-start(bf16[16,2304]{1,0:T(8,128)(2,1)S(1)} %get-tuple-element.14), channel_id=1, source_target_pairs={{0,4},{1,5},{2,6},{3,7},{4,0},{5,1},{6,2},{7,3},{8,12},{9,13},{10,... | collective-permute-start | bytes 221192 | tf_op jit(solution)/shard_map/ppermute | solution.py:36
  42.4 0.9 %collective-permute-start.18 = (bf16[16,2304]{1,0:T(8,128)(2,1)S(1)}, bf16[16,2304]{1,0:T(8,128)(2,1)S(1)}, u32[]{:S(2)}, u32[]{:S(2)}) collective-permute-start(bf16[16,2304]{1,0:T(8,128)(2,1)S(1)} %get-tuple-element.14), channel_id=1, source_target_pairs={{0,2},{1,3},{2,0},{3,1},{4,6},{5,7},{6,4},{7,5},{8,10},{9,11},{10,... | collective-permute-start | bytes 221192 | tf_op jit(solution)/shard_map/ppermute | solution.py:36
  43.3 0.9 %collective-permute-done.23 = bf16[16,2304]{1,0:T(8,128)(2,1)S(1)} collective-permute-done((bf16[16,2304]{1,0:T(8,128)(2,1)S(1)}, bf16[16,2304]{1,0:T(8,128)(2,1)S(1)}, u32[]{:S(2)}, u32[]{:S(2)}) %collective-permute-start.23) | collective-permute-done | bytes 73760 | tf_op jit(solution)/shard_map/ppermute | solution.py:36
  44.2 0.9 %collective-permute-start.24 = (bf16[16,2304]{1,0:T(8,128)(2,1)S(1)}, bf16[16,2304]{1,0:T(8,128)(2,1)S(1)}, u32[]{:S(2)}, u32[]{:S(2)}) collective-permute-start(bf16[16,2304]{1,0:T(8,128)(2,1)S(1)} %collective-permute-done.23), channel_id=1, source_target_pairs={{0,2},{1,3},{2,0},{3,1},{4,6},{5,7},{6,4},{7,5},{8,10},{9,11},{10,... | collective-permute-start | bytes 221192 | tf_op jit(solution)/shard_map/ppermute | solution.py:36
  45.0 0.8 %collective-permute-done.21 = bf16[16,2304]{1,0:T(8,128)(2,1)S(1)} collective-permute-done((bf16[16,2304]{1,0:T(8,128)(2,1)S(1)}, bf16[16,2304]{1,0:T(8,128)(2,1)S(1)}, u32[]{:S(2)}, u32[]{:S(2)}) %collective-permute-start.21) | collective-permute-done | bytes 73760 | tf_op jit(solution)/shard_map/ppermute | solution.py:36
  45.9 0.9 %collective-permute-start.22 = (bf16[16,2304]{1,0:T(8,128)(2,1)S(1)}, bf16[16,2304]{1,0:T(8,128)(2,1)S(1)}, u32[]{:S(2)}, u32[]{:S(2)}) collective-permute-start(bf16[16,2304]{1,0:T(8,128)(2,1)S(1)} %collective-permute-done.21), channel_id=1, source_target_pairs={{0,2},{1,3},{2,0},{3,1},{4,6},{5,7},{6,4},{7,5},{8,10},{9,11},{10,... | collective-permute-start | bytes 221192 | tf_op jit(solution)/shard_map/ppermute | solution.py:36
  46.8 1.1 %collective-permute-start.20 = (bf16[16,2304]{1,0:T(8,128)(2,1)S(1)}, bf16[16,2304]{1,0:T(8,128)(2,1)S(1)}, u32[]{:S(2)}, u32[]{:S(2)}) collective-permute-start(bf16[16,2304]{1,0:T(8,128)(2,1)S(1)} %collective-permute-done.19), channel_id=1, source_target_pairs={{0,2},{1,3},{2,0},{3,1},{4,6},{5,7},{6,4},{7,5},{8,10},{9,11},{10,... | collective-permute-start | bytes 221192 | tf_op jit(solution)/shard_map/ppermute | solution.py:36
  48.0 3.2 %collective-permute-done.20 = bf16[16,2304]{1,0:T(8,128)(2,1)S(1)} collective-permute-done((bf16[16,2304]{1,0:T(8,128)(2,1)S(1)}, bf16[16,2304]{1,0:T(8,128)(2,1)S(1)}, u32[]{:S(2)}, u32[]{:S(2)}) %collective-permute-start.20) | collective-permute-done | bytes 73760 | tf_op jit(solution)/shard_map/ppermute | solution.py:36
  52.0 1.5 %collective-permute-done.25 = bf16[128,2304]{1,0:T(8,128)(2,1)S(1)} collective-permute-done((bf16[128,2304]{1,0:T(8,128)(2,1)S(1)}, bf16[128,2304]{1,0:T(8,128)(2,1)S(1)}, u32[]{:S(2)}, u32[]{:S(2)}) %collective-permute-start.25) | collective-permute-done | bytes 589856 | tf_op jit(solution)/shard_map/ppermute | solution.py:43
  53.5 2.6 %subtract_convert_fusion = (bf16[128,2304]{1,0:T(8,128)(2,1)}, f32[128,2304]{1,0:T(8,128)}, f32[128,2304]{1,0:T(8,128)}) fusion(bf16[128,2304]{1,0:T(8,128)(2,1)S(1)} %copy-done, f32[128,2304]{1,0:T(8,128)S(1)} %copy-done.3, f32[128,2304]{1,0:T(8,128)S(1)} %copy-done.4, bf16[256,2304]{1,0:T(8,128)(2,1)S(1)} %constant_dynamic-update-slice_fusion.16, ...), kind=kOutput, calls=%fused_computation.12 | convolution fusion | flops 155254784 | bytes 7143424 | tf_op jit(solution)/shard_map/dot_general | solution.py:19
  56.2 5.0 %subtract_convert_fusion.1 = (bf16[128,2304]{1,0:T(8,128)(2,1)}, f32[128,2304]{1,0:T(8,128)}, f32[128,2304]{1,0:T(8,128)}) fusion(bf16[128,2304]{1,0:T(8,128)(2,1)S(1)} %copy-done.5, f32[128,2304]{1,0:T(8,128)} %param.14, f32[128,2304]{1,0:T(8,128)} %param.15, bf16[128,2304]{1,0:T(8,128)(2,1)} %collective-permute-done.26, ...), kind=kOutput, calls=%fused_computation.15 | convolution fusion | flops 308674560 | bytes 8912896 | tf_op jit(solution)/shard_map/dot_general | solution.py:19
  (61 shorter events, 5.3 us)
Async XLA Ops:
  0.6 18.1 %copy-start.5 = (bf16[128,2304]{1,0:T(8,128)(2,1)S(1)}, bf16[128,2304]{1,0:T(8,128)(2,1)}, u32[]{:S(2)}) copy-start(bf16[128,2304]{1,0:T(8,128)(2,1)} %param.10) | copy-start | bytes 1769476
  0.6 17.9 %copy-start.2 = (f32[2304]{0:T(1024)S(1)}, f32[2304]{0:T(1024)}, u32[]{:S(2)}) copy-start(f32[2304]{0:T(1024)} %param.13) | copy-start | bytes 27652
  0.7 9.6 %collective-permute-start.3 = (bf16[16,2304]{1,0:T(8,128)(2,1)}, bf16[16,2304]{1,0:T(8,128)(2,1)S(1)}, u32[]{:S(2)}, u32[]{:S(2)}) collective-permute-start(bf16[16,2304]{1,0:T(8,128)(2,1)} %param.9), channel_id=1, source_target_pairs={{0,8},{1,9},{2,10},{3,11},{4,12},{5,13},{6,14},{7,15},{8,0},{9,1},... | collective-permute-start | bytes 221192 | tf_op jit(solution)/shard_map/ppermute | solution.py:36
  4.8 5.8 %collective-permute-start.1 = (bf16[16,2304]{1,0:T(8,128)(2,1)}, bf16[16,2304]{1,0:T(8,128)(2,1)S(1)}, u32[]{:S(2)}, u32[]{:S(2)}) collective-permute-start(bf16[16,2304]{1,0:T(8,128)(2,1)} %param.9), channel_id=1, source_target_pairs={{0,4},{1,5},{2,6},{3,7},{4,0},{5,1},{6,2},{7,3},{8,12},{9,13},{10,... | collective-permute-start | bytes 221192 | tf_op jit(solution)/shard_map/ppermute | solution.py:36
  6.3 4.7 %collective-permute-start = (bf16[16,2304]{1,0:T(8,128)(2,1)}, bf16[16,2304]{1,0:T(8,128)(2,1)S(1)}, u32[]{:S(2)}, u32[]{:S(2)}) collective-permute-start(bf16[16,2304]{1,0:T(8,128)(2,1)} %param.9), channel_id=1, source_target_pairs={{0,2},{1,3},{2,0},{3,1},{4,6},{5,7},{6,4},{7,5},{8,10},{9,11},{10,... | collective-permute-start | bytes 221192 | tf_op jit(solution)/shard_map/ppermute | solution.py:36
  7.9 6.4 %collective-permute-start.5 = (bf16[16,2304]{1,0:T(8,128)(2,1)}, bf16[16,2304]{1,0:T(8,128)(2,1)S(1)}, u32[]{:S(2)}, u32[]{:S(2)}) collective-permute-start(bf16[16,2304]{1,0:T(8,128)(2,1)} %param.9), channel_id=1, source_target_pairs={{0,12},{1,13},{2,14},{3,15},{4,8},{5,9},{6,10},{7,11},{8,4},{9,5},... | collective-permute-start | bytes 221192 | tf_op jit(solution)/shard_map/ppermute | solution.py:36
  8.1 1.3 %collective-permute-start.8 = (f32[128]{0:T(128)}, f32[128]{0:T(128)S(1)}, u32[]{:S(2)}, u32[]{:S(2)}) collective-permute-start(f32[128]{0:T(128)} %param.11), channel_id=1, source_target_pairs={{0,1},{1,0},{2,3},{3,2},{4,5},{5,4},{6,7},{7,6},{8,9},{9,8},{10,11... | collective-permute-start | bytes 1544 | tf_op jit(solution)/shard_map/ppermute | solution.py:43
  9.3 9.4 %collective-permute-start.7 = (bf16[128,2304]{1,0:T(8,128)(2,1)}, bf16[128,2304]{1,0:T(8,128)(2,1)S(1)}, u32[]{:S(2)}, u32[]{:S(2)}) collective-permute-start(bf16[128,2304]{1,0:T(8,128)(2,1)} %param.10), channel_id=1, source_target_pairs={{0,1},{1,0},{2,3},{3,2},{4,5},{5,4},{6,7},{7,6},{8,9},{9,8},{10,11... | collective-permute-start | bytes 1769480 | tf_op jit(solution)/shard_map/ppermute | solution.py:43
  10.2 9.1 %collective-permute-start.9 = (bf16[128,2304]{1,0:T(8,128)(2,1)}, bf16[128,2304]{1,0:T(8,128)(2,1)S(1)}, u32[]{:S(2)}, u32[]{:S(2)}) collective-permute-start(bf16[128,2304]{1,0:T(8,128)(2,1)} %param.12), channel_id=1, source_target_pairs={{0,1},{1,0},{2,3},{3,2},{4,5},{5,4},{6,7},{7,6},{8,9},{9,8},{10,11... | collective-permute-start | bytes 1769480 | tf_op jit(solution)/shard_map/ppermute | solution.py:43
  10.6 6.7 %collective-permute-start.4 = (bf16[16,2304]{1,0:T(8,128)(2,1)S(1)}, bf16[16,2304]{1,0:T(8,128)(2,1)S(1)}, u32[]{:S(2)}, u32[]{:S(2)}) collective-permute-start(bf16[16,2304]{1,0:T(8,128)(2,1)S(1)} %collective-permute-done.3), channel_id=1, source_target_pairs={{0,2},{1,3},{2,0},{3,1},{4,6},{5,7},{6,4},{7,5},{8,10},{9,11},{10,... | collective-permute-start | bytes 221192 | tf_op jit(solution)/shard_map/ppermute | solution.py:36
  11.0 6.3 %collective-permute-start.2 = (bf16[16,2304]{1,0:T(8,128)(2,1)S(1)}, bf16[16,2304]{1,0:T(8,128)(2,1)S(1)}, u32[]{:S(2)}, u32[]{:S(2)}) collective-permute-start(bf16[16,2304]{1,0:T(8,128)(2,1)S(1)} %collective-permute-done.1), channel_id=1, source_target_pairs={{0,2},{1,3},{2,0},{3,1},{4,6},{5,7},{6,4},{7,5},{8,10},{9,11},{10,... | collective-permute-start | bytes 221192 | tf_op jit(solution)/shard_map/ppermute | solution.py:36
  14.2 4.4 %collective-permute-start.6 = (bf16[16,2304]{1,0:T(8,128)(2,1)S(1)}, bf16[16,2304]{1,0:T(8,128)(2,1)S(1)}, u32[]{:S(2)}, u32[]{:S(2)}) collective-permute-start(bf16[16,2304]{1,0:T(8,128)(2,1)S(1)} %collective-permute-done.5), channel_id=1, source_target_pairs={{0,2},{1,3},{2,0},{3,1},{4,6},{5,7},{6,4},{7,5},{8,10},{9,11},{10,... | collective-permute-start | bytes 221192 | tf_op jit(solution)/shard_map/ppermute | solution.py:36
  20.1 5.3 %collective-permute-start.15 = (bf16[16,2304]{1,0:T(8,128)(2,1)S(1)}, bf16[16,2304]{1,0:T(8,128)(2,1)S(1)}, u32[]{:S(2)}, u32[]{:S(2)}) collective-permute-start(bf16[16,2304]{1,0:T(8,128)(2,1)S(1)} %get-tuple-element.19), channel_id=1, source_target_pairs={{0,2},{1,3},{2,0},{3,1},{4,6},{5,7},{6,4},{7,5},{8,10},{9,11},{10,... | collective-permute-start | bytes 221192 | tf_op jit(solution)/shard_map/ppermute | solution.py:36
  20.7 5.6 %collective-permute-start.13 = (bf16[16,2304]{1,0:T(8,128)(2,1)S(1)}, bf16[16,2304]{1,0:T(8,128)(2,1)S(1)}, u32[]{:S(2)}, u32[]{:S(2)}) collective-permute-start(bf16[16,2304]{1,0:T(8,128)(2,1)S(1)} %get-tuple-element.20), channel_id=1, source_target_pairs={{0,2},{1,3},{2,0},{3,1},{4,6},{5,7},{6,4},{7,5},{8,10},{9,11},{10,... | collective-permute-start | bytes 221192 | tf_op jit(solution)/shard_map/ppermute | solution.py:36
  22.2 4.9 %collective-permute-start.11 = (bf16[16,2304]{1,0:T(8,128)(2,1)S(1)}, bf16[16,2304]{1,0:T(8,128)(2,1)S(1)}, u32[]{:S(2)}, u32[]{:S(2)}) collective-permute-start(bf16[16,2304]{1,0:T(8,128)(2,1)S(1)} %get-tuple-element.21), channel_id=1, source_target_pairs={{0,2},{1,3},{2,0},{3,1},{4,6},{5,7},{6,4},{7,5},{8,10},{9,11},{10,... | collective-permute-start | bytes 221192 | tf_op jit(solution)/shard_map/ppermute | solution.py:36
  22.7 9.2 %collective-permute-start.10 = (bf16[16,2304]{1,0:T(8,128)(2,1)S(1)}, bf16[16,2304]{1,0:T(8,128)(2,1)S(1)}, u32[]{:S(2)}, u32[]{:S(2)}) collective-permute-start(bf16[16,2304]{1,0:T(8,128)(2,1)S(1)} %get-tuple-element.18), channel_id=1, source_target_pairs={{0,2},{1,3},{2,0},{3,1},{4,6},{5,7},{6,4},{7,5},{8,10},{9,11},{10,... | collective-permute-start | bytes 221192 | tf_op jit(solution)/shard_map/ppermute | solution.py:36
  27.2 5.2 %collective-permute-start.12 = (bf16[16,2304]{1,0:T(8,128)(2,1)S(1)}, bf16[16,2304]{1,0:T(8,128)(2,1)S(1)}, u32[]{:S(2)}, u32[]{:S(2)}) collective-permute-start(bf16[16,2304]{1,0:T(8,128)(2,1)S(1)} %get-tuple-element.15), channel_id=1, source_target_pairs={{0,4},{1,5},{2,6},{3,7},{4,0},{5,1},{6,2},{7,3},{8,12},{9,13},{10,... | collective-permute-start | bytes 221192 | tf_op jit(solution)/shard_map/ppermute | solution.py:36
  27.5 7.9 %collective-permute-start.16 = (bf16[16,2304]{1,0:T(8,128)(2,1)S(1)}, bf16[16,2304]{1,0:T(8,128)(2,1)S(1)}, u32[]{:S(2)}, u32[]{:S(2)}) collective-permute-start(bf16[16,2304]{1,0:T(8,128)(2,1)S(1)} %get-tuple-element.16), channel_id=1, source_target_pairs={{0,12},{1,13},{2,14},{3,15},{4,8},{5,9},{6,10},{7,11},{8,4},{9,5},... | collective-permute-start | bytes 221192 | tf_op jit(solution)/shard_map/ppermute | solution.py:36
  31.4 6.4 %collective-permute-start.14 = (bf16[16,2304]{1,0:T(8,128)(2,1)S(1)}, bf16[16,2304]{1,0:T(8,128)(2,1)S(1)}, u32[]{:S(2)}, u32[]{:S(2)}) collective-permute-start(bf16[16,2304]{1,0:T(8,128)(2,1)S(1)} %get-tuple-element.17), channel_id=1, source_target_pairs={{0,8},{1,9},{2,10},{3,11},{4,12},{5,13},{6,14},{7,15},{8,0},{9,1},... | collective-permute-start | bytes 221192 | tf_op jit(solution)/shard_map/ppermute | solution.py:36
  37.9 15.5 %copy-start.1 = (bf16[16,2304]{1,0:T(8,128)(2,1)}, bf16[16,2304]{1,0:T(8,128)(2,1)S(1)}, u32[]{:S(2)}) copy-start(bf16[16,2304]{1,0:T(8,128)(2,1)S(1)} %get-tuple-element.14) | copy-start | bytes 221188
  37.9 6.2 %collective-permute-start.23 = (bf16[16,2304]{1,0:T(8,128)(2,1)S(1)}, bf16[16,2304]{1,0:T(8,128)(2,1)S(1)}, u32[]{:S(2)}, u32[]{:S(2)}) collective-permute-start(bf16[16,2304]{1,0:T(8,128)(2,1)S(1)} %get-tuple-element.14), channel_id=1, source_target_pairs={{0,12},{1,13},{2,14},{3,15},{4,8},{5,9},{6,10},{7,11},{8,4},{9,5},... | collective-permute-start | bytes 221192 | tf_op jit(solution)/shard_map/ppermute | solution.py:36
  40.6 5.3 %collective-permute-start.21 = (bf16[16,2304]{1,0:T(8,128)(2,1)S(1)}, bf16[16,2304]{1,0:T(8,128)(2,1)S(1)}, u32[]{:S(2)}, u32[]{:S(2)}) collective-permute-start(bf16[16,2304]{1,0:T(8,128)(2,1)S(1)} %get-tuple-element.14), channel_id=1, source_target_pairs={{0,8},{1,9},{2,10},{3,11},{4,12},{5,13},{6,14},{7,15},{8,0},{9,1},... | collective-permute-start | bytes 221192 | tf_op jit(solution)/shard_map/ppermute | solution.py:36
  40.6 6.2 %collective-permute-start.19 = (bf16[16,2304]{1,0:T(8,128)(2,1)S(1)}, bf16[16,2304]{1,0:T(8,128)(2,1)S(1)}, u32[]{:S(2)}, u32[]{:S(2)}) collective-permute-start(bf16[16,2304]{1,0:T(8,128)(2,1)S(1)} %get-tuple-element.14), channel_id=1, source_target_pairs={{0,4},{1,5},{2,6},{3,7},{4,0},{5,1},{6,2},{7,3},{8,12},{9,13},{10,... | collective-permute-start | bytes 221192 | tf_op jit(solution)/shard_map/ppermute | solution.py:36
  42.4 5.5 %collective-permute-start.18 = (bf16[16,2304]{1,0:T(8,128)(2,1)S(1)}, bf16[16,2304]{1,0:T(8,128)(2,1)S(1)}, u32[]{:S(2)}, u32[]{:S(2)}) collective-permute-start(bf16[16,2304]{1,0:T(8,128)(2,1)S(1)} %get-tuple-element.14), channel_id=1, source_target_pairs={{0,2},{1,3},{2,0},{3,1},{4,6},{5,7},{6,4},{7,5},{8,10},{9,11},{10,... | collective-permute-start | bytes 221192 | tf_op jit(solution)/shard_map/ppermute | solution.py:36
  44.2 7.1 %collective-permute-start.24 = (bf16[16,2304]{1,0:T(8,128)(2,1)S(1)}, bf16[16,2304]{1,0:T(8,128)(2,1)S(1)}, u32[]{:S(2)}, u32[]{:S(2)}) collective-permute-start(bf16[16,2304]{1,0:T(8,128)(2,1)S(1)} %collective-permute-done.23), channel_id=1, source_target_pairs={{0,2},{1,3},{2,0},{3,1},{4,6},{5,7},{6,4},{7,5},{8,10},{9,11},{10,... | collective-permute-start | bytes 221192 | tf_op jit(solution)/shard_map/ppermute | solution.py:36
  45.9 5.3 %collective-permute-start.22 = (bf16[16,2304]{1,0:T(8,128)(2,1)S(1)}, bf16[16,2304]{1,0:T(8,128)(2,1)S(1)}, u32[]{:S(2)}, u32[]{:S(2)}) collective-permute-start(bf16[16,2304]{1,0:T(8,128)(2,1)S(1)} %collective-permute-done.21), channel_id=1, source_target_pairs={{0,2},{1,3},{2,0},{3,1},{4,6},{5,7},{6,4},{7,5},{8,10},{9,11},{10,... | collective-permute-start | bytes 221192 | tf_op jit(solution)/shard_map/ppermute | solution.py:36
  46.8 4.4 %collective-permute-start.20 = (bf16[16,2304]{1,0:T(8,128)(2,1)S(1)}, bf16[16,2304]{1,0:T(8,128)(2,1)S(1)}, u32[]{:S(2)}, u32[]{:S(2)}) collective-permute-start(bf16[16,2304]{1,0:T(8,128)(2,1)S(1)} %collective-permute-done.19), channel_id=1, source_target_pairs={{0,2},{1,3},{2,0},{3,1},{4,6},{5,7},{6,4},{7,5},{8,10},{9,11},{10,... | collective-permute-start | bytes 221192 | tf_op jit(solution)/shard_map/ppermute | solution.py:36
  51.2 2.3 %copy-start.3 = (f32[128,2304]{1,0:T(8,128)S(1)}, f32[128,2304]{1,0:T(8,128)}, u32[]{:S(2)}) copy-start(f32[128,2304]{1,0:T(8,128)} %param.16) | copy-start | bytes 3538948
  51.2 2.3 %copy-start.4 = (f32[128,2304]{1,0:T(8,128)S(1)}, f32[128,2304]{1,0:T(8,128)}, u32[]{:S(2)}) copy-start(f32[128,2304]{1,0:T(8,128)} %param.17) | copy-start | bytes 3538948
  51.3 2.1 %collective-permute-start.25 = (bf16[128,2304]{1,0:T(8,128)(2,1)S(1)}, bf16[128,2304]{1,0:T(8,128)(2,1)S(1)}, u32[]{:S(2)}, u32[]{:S(2)}) collective-permute-start(bf16[128,2304]{1,0:T(8,128)(2,1)S(1)} %get-tuple-element.22), channel_id=1, source_target_pairs={{0,1},{1,0},{2,3},{3,2},{4,5},{5,4},{6,7},{7,6},{8,9},{9,8},{10,11... | collective-permute-start | bytes 1769480 | tf_op jit(solution)/shard_map/ppermute | solution.py:43
  51.4 4.8 %collective-permute-start.26 = (bf16[128,2304]{1,0:T(8,128)(2,1)S(1)}, bf16[128,2304]{1,0:T(8,128)(2,1)}, u32[]{:S(2)}, u32[]{:S(2)}) collective-permute-start(bf16[128,2304]{1,0:T(8,128)(2,1)S(1)} %subtract_convert_fusion.2), channel_id=1, source_target_pairs={{0,1},{1,0},{2,3},{3,2},{4,5},{5,4},{6,7},{7,6},{8,9},{9,8},{10,11... | collective-permute-start | bytes 1769480 | tf_op jit(solution)/shard_map/ppermute | solution.py:43
  51.9 1.6 %collective-permute-start.17 = (bf16[128,128]{1,0:T(8,128)(2,1)S(1)}, bf16[128,128]{1,0:T(8,128)(2,1)S(1)}, u32[]{:S(2)}, u32[]{:S(2)}) collective-permute-start(bf16[128,128]{1,0:T(8,128)(2,1)S(1)} %get-tuple-element.37), channel_id=1, source_target_pairs={{0,1},{1,0},{2,3},{3,2},{4,5},{5,4},{6,7},{7,6},{8,9},{9,8},{10,11... | collective-permute-start | bytes 98312 | tf_op jit(solution)/shard_map/ppermute | solution.py:43
  (1 other events, 1.1 us)

commit v4 on v1

v4 whole, which is shorter than its diff:
```python
import functools

import jax
import jax.numpy as jnp
from jax import lax
from jax.experimental import pallas as pl
from jax.experimental.pallas import tpu as pltpu
from jax.sharding import PartitionSpec as P

beta_first = 0.9
beta_second = 0.999
step_rate = 0.001
adam_epsilon = 1e-08


def inner_last(left, right):
    return lax.dot_general(
        left, right, (((1,), (1,)), ((), ())), preferred_element_type=jnp.float32
    )


def update_kernel(
    columns,
    scale,
    codes_across,
    centered,
    *refs,
):
    errors = refs[:4]
    encoder, decoder = refs[4:6]
    moments_in = refs[6:10]
    outs = refs[10:16]
    error_all = refs[16]
    held_in = refs[17:21]
    held_out = refs[21:27]
    sem_in, sem_out = refs[27:]
    width = encoder.shape[1]
    tiles = width // columns

    def span(t):
        return pl.ds(t * columns, columns)

    def fetch(t, i):
        return pltpu.make_async_copy(
            moments_in[i].at[:, span(t)], held_in[i].at[:, span(t)], sem_in.at[t, i]
        )

    def write(t, i):
        return pltpu.make_async_copy(
            held_out[i].at[:, span(t)], outs[i].at[:, span(t)], sem_out.at[t, i]
        )

    for t in range(tiles):
        for i in range(4):
            fetch(t, i).start()
    start = 0
    for one in errors:
        error_all[pl.ds(start, one.shape[0]), :] = one[...]
        start += one.shape[0]
    codes_t = codes_across[...]
    signal = inner_last(decoder[...], error_all[...])
    delta_t = jnp.where(codes_t.astype(jnp.float32) > 0, signal, 0.0).astype(jnp.bfloat16)
    for t in range(tiles):
        at = span(t)
        for i in range(4):
            fetch(t, i).wait()
        for which, (left, right, weight) in enumerate(
            ((delta_t, centered, encoder), (codes_t, error_all, decoder))
        ):
            grad = jnp.dot(left, right[:, at], preferred_element_type=jnp.float32) * scale
            moment = beta_first * held_in[2 * which][:, at] + (1.0 - beta_first) * grad
            square = (
                beta_second * held_in[2 * which + 1][:, at] + (1.0 - beta_second) * grad * grad
            )
            held_out[3 * which][:, at] = (
                weight[:, at].astype(jnp.float32)
                - step_rate * moment / (jnp.sqrt(square) + adam_epsilon)
            ).astype(jnp.bfloat16)
            held_out[3 * which + 1][:, at] = moment
            held_out[3 * which + 2][:, at] = square
            for i in range(3 * which, 3 * which + 3):
                write(t, i).start()
    for t in range(tiles):
        for i in range(6):
            write(t, i).wait()


def update(total_rows, codes_across, centered, errors, weights, moments):
    latents, width = weights[0].shape
    rows = centered.shape[0]
    columns = next(c for c in (384, 256, 128, width) if width % c == 0)
    tiles = width // columns
    full = jax.ShapeDtypeStruct((latents, width), jnp.float32)
    half = jax.ShapeDtypeStruct((latents, width), jnp.bfloat16)
    vmem = pl.BlockSpec(memory_space=pltpu.VMEM)
    anywhere = pl.BlockSpec(memory_space=pl.ANY)
    wide = pltpu.VMEM((latents, width), jnp.float32)
    narrow = pltpu.VMEM((latents, width), jnp.bfloat16)
    return pl.pallas_call(
        functools.partial(update_kernel, columns, 1.0 / total_rows),
        out_shape=(half, full, full, half, full, full),
        in_specs=[vmem] * 8 + [anywhere] * 4,
        out_specs=[anywhere] * 6,
        scratch_shapes=[
            pltpu.VMEM((rows, width), jnp.bfloat16),
            wide,
            wide,
            wide,
            wide,
            narrow,
            wide,
            wide,
            narrow,
            wide,
            wide,
            pltpu.SemaphoreType.DMA((tiles, 4)),
            pltpu.SemaphoreType.DMA((tiles, 6)),
        ],
        compiler_params=pltpu.CompilerParams(vmem_limit_bytes=40 * 1024 * 1024),
        cost_estimate=pl.CostEstimate(
            flops=6 * latents * width * rows,
            bytes_accessed=44 * latents * width,
            transcendentals=4 * latents * width,
        ),
        name="update",
    )(codes_across, centered, *errors, *weights, *moments)


def to_chip(block, distance):
    size = lax.axis_size("latent")
    return lax.ppermute(
        block, "latent", [(i, i ^ (2 * distance)) for i in range(size)]
    )


def to_other_core(block):
    size = lax.axis_size("latent")
    return lax.ppermute(block, "latent", [(i, i ^ 1) for i in range(size)])


def gather_chips(block, chips):
    far = [to_chip(block, k) for k in reversed(range(2, chips, 2))]
    far_next = [to_chip(one, 1) for one in far]
    return [block] + far[::-1] + [to_chip(block, 1)] + far_next[::-1]


def body(
    activations,
    encoder,
    encoder_bias,
    decoder,
    decoder_bias,
    encoder_moment,
    encoder_square,
    decoder_moment,
    decoder_square,
):
    rows_here, width = activations.shape
    latents_here = encoder.shape[0]
    size = lax.axis_size("latent")
    chips = size // 2
    pairs = chips // 2
    total_rows = rows_here * size

    rows_core = jnp.concatenate(gather_chips(activations, chips), 0)
    encoder_both = jnp.concatenate([encoder, to_other_core(encoder)], 0)
    decoder_both = jnp.concatenate([decoder, to_other_core(decoder)], 0)
    bias_both = jnp.concatenate([encoder_bias, to_other_core(encoder_bias)], 0)

    centered = (rows_core.astype(jnp.float32) - decoder_bias).astype(jnp.bfloat16)
    codes = jnp.maximum(inner_last(centered, encoder_both) + bias_both, 0.0).astype(
        jnp.bfloat16
    )
    other_codes = to_other_core(codes[:, latents_here:])
    other_centered = to_other_core(centered)

    given = jnp.dot(
        codes[pairs * rows_here :], decoder_both, preferred_element_type=jnp.float32
    ).astype(jnp.bfloat16)
    summed = None
    for k in range(pairs):
        rows = slice(k * rows_here, (k + 1) * rows_here)
        pair = jnp.dot(
            codes[rows], decoder_both, preferred_element_type=jnp.float32
        ) + to_chip(given[rows], 1).astype(jnp.float32)
        if k:
            pair = to_chip(pair.astype(jnp.bfloat16), 2 * k).astype(jnp.float32)
        summed = pair if summed is None else summed + pair
    row_error = (summed - centered[:rows_here].astype(jnp.float32)).astype(jnp.bfloat16)

    errors = gather_chips(row_error, chips)
    near = [0, 1, pairs, pairs + 1]
    rest = [k for k in range(chips) if k not in near]
    near_error = jnp.concatenate([errors[k] for k in near], 0)
    rest_error = jnp.concatenate([errors[k] for k in rest], 0)

    def arranged(whole):
        return [whole[k * rows_here : (k + 1) * rows_here] for k in near + rest]

    codes_across = jnp.concatenate(
        arranged(codes[:, :latents_here]) + arranged(other_codes), 0
    ).T
    centered_all = jnp.concatenate(arranged(centered) + arranged(other_centered), 0)
    (
        encoder_next,
        encoder_moment_next,
        encoder_square_next,
        decoder_next,
        decoder_moment_next,
        decoder_square_next,
    ) = update(
        total_rows,
        codes_across,
        centered_all,
        (near_error, rest_error, to_other_core(near_error), to_other_core(rest_error)),
        (encoder, decoder),
        (encoder_moment, encoder_square, decoder_moment, decoder_square),
    )
    return (
        row_error,
        encoder_next,
        decoder_next,
        encoder_moment_next,
        encoder_square_next,
        decoder_moment_next,
        decoder_square_next,
    )


def solution(mesh):
    sharded = P(("groups", "latent"), None)
    return jax.shard_map(
        body,
        mesh=mesh,
        in_specs=(
            sharded,
            sharded,
            P(("groups", "latent")),
            sharded,
            P("groups"),
            sharded,
            sharded,
            sharded,
            sharded,
        ),
        out_specs=(sharded,) * 7,
        check_vma=False,
    )
```

time: 79.1 us -> 69.9 us (0.88)
  waiting for transfers between devices: 32.7 us -> 14 us
  local copies, waits for them, and re-layouts: 1.68 us -> 12.4 us
  Pallas kernels: 0 us -> 5.19 us
  starting transfers between devices: 34.2 us -> 29.1 us
  matrix products: 8.49 us -> 6.77 us
    ppermute x21, waiting for transfers between devices: 30.9 us -> 13.3 us  [to_chip(): lax.ppermute(block, 'latent', [(i, i ^ 2 * distance) for i in range(size)])]
    unnamed x28 -> x44, local copies, waits for them, and re-layouts: 1.58 us -> 7.69 us
    pallas_call x0 -> x1, Pallas kernels: none -> 5.19 us  [update(): pl.pallas_call(functools.partial(update_kernel, columns, 1.0 / total_rows...]
    ppermute x21, starting transfers between devices: 33 us -> 28.2 us  [to_chip(): lax.ppermute(block, 'latent', [(i, i ^ 2 * distance) for i in range(size)])]
    dot_general x3 -> x5, matrix products: 7.95 us -> 5.23 us  [the longest x4 4.8 us: body(): jnp.dot(codes[rows], decoder_both, preferred_element_type=jnp.float32)]
    concatenate x3 -> x5, local copies, waits for them, and re-layouts: 0.06 us -> 2.6 us  [the longest x1 1.62 us: body(): jnp.concatenate(arranged(codes[:, :latents_here]) + arranged(other_codes)...]
    slice x2 -> x4, local copies, waits for them, and re-layouts: 0.04 us -> 2.14 us  [the longest x2 1.47 us: arranged(): return [whole[k * rows_here:(k + 1) * rows_here] for k in near + rest]]
    ppermute x6 -> x7, waiting for transfers between devices: 1.8 us -> 0.77 us  [to_other_core(): return lax.ppermute(block, 'latent', [(i, i ^ 1) for i in range(size)])]
  transfers between devices with their start and end apart: 27 -> 28, of which waited for: 11 -> 12; matrix products, arithmetic and copies ran while one was open for 6% -> 29% of each run, Pallas kernels for 0% -> 0%
where the time goes in v4:
time: 69.9 us; the launch traced here: 69.4 us
  starting transfers between devices  29.1 us (42%)
  waiting for transfers between devices  14 us (20%)
  local copies, waits for them, and re-layouts  12.4 us (18%)
  matrix products  6.77 us (10%)
  Pallas kernels  5.19 us (7%)
  between operations  0.98 us (1%)
  other arithmetic  0.94 us (1%)
    ppermute x21, starting transfers between devices, to_chip(): lax.ppermute(block, 'latent', [(i, i ^ 2 * distance) for i in range(size)])  28.2 us
    ppermute x21, waiting for transfers between devices, to_chip(): lax.ppermute(block, 'latent', [(i, i ^ 2 * distance) for i in range(size)])  13.3 us
    unnamed x44, local copies, waits for them, and re-layouts  7.69 us
    pallas_call x1, Pallas kernels, update(): pl.pallas_call(functools.partial(update_kernel, columns, 1.0 / total_rows...  5.19 us
    dot_general x4, matrix products, body(): jnp.dot(codes[rows], decoder_both, preferred_element_type=jnp.float32)  4.8 us
    concatenate x1, local copies, waits for them, and re-layouts, body(): jnp.concatenate(arranged(codes[:, :latents_here]) + arranged(other_codes)...  1.62 us
    dot_general x1, matrix products, inner_last(): lax.dot_general(left, right, (((1,), (1,)), ((), ())), preferred_element_...  1.54 us
    slice x2, local copies, waits for them, and re-layouts, arranged(): return [whole[k * rows_here:(k + 1) * rows_here] for k in near + rest]  1.47 us
  transfers between devices with their start and end apart: 28, of which 12 were waited for; matrix products, arithmetic and copies ran while one was open for 29% of the time, Pallas kernels for 0%

profile of v4, /device:TPU:0, one launch (start us, length us, event | category | flops | bytes accessed | tf_op | source)
XLA Modules:
  0.0 69.4 jit_solution(10288555085768056698)
XLA Ops:
  0.7 5.1 %collective-permute-start.2 = (bf16[16,2304]{1,0:T(8,128)(2,1)}, bf16[16,2304]{1,0:T(8,128)(2,1)S(1)}, u32[]{:S(2)}, u32[]{:S(2)}) collective-permute-start(bf16[16,2304]{1,0:T(8,128)(2,1)} %param.9), channel_id=1, source_target_pairs={{0,12},{1,13},{2,14},{3,15},{4,8},{5,9},{6,10},{7,11},{8,4},{9,5},... | collective-permute-start | bytes 221192 | tf_op jit(solution)/shard_map/ppermute | solution.py:131
  6.4 1.7 %collective-permute-start.3 = (bf16[16,2304]{1,0:T(8,128)(2,1)}, bf16[16,2304]{1,0:T(8,128)(2,1)S(1)}, u32[]{:S(2)}, u32[]{:S(2)}) collective-permute-start(bf16[16,2304]{1,0:T(8,128)(2,1)} %param.9), channel_id=1, source_target_pairs={{0,2},{1,3},{2,0},{3,1},{4,6},{5,7},{6,4},{7,5},{8,10},{9,11},{10,... | collective-permute-start | bytes 221192 | tf_op jit(solution)/shard_map/ppermute | solution.py:131
  8.1 1.1 %constant_dynamic-update-slice_fusion.9 = bf16[256,2304]{1,0:T(8,128)(2,1)S(1)} fusion(bf16[128,2304]{1,0:T(8,128)(2,1)} %refs_5_.1), kind=kLoop, calls=%fused_computation.44 | loop fusion | bytes 1179648
  10.0 2.3 %collective-permute-done.1 = bf16[16,2304]{1,0:T(8,128)(2,1)S(1)} collective-permute-done((bf16[16,2304]{1,0:T(8,128)(2,1)}, bf16[16,2304]{1,0:T(8,128)(2,1)S(1)}, u32[]{:S(2)}, u32[]{:S(2)}) %collective-permute-start.1) | collective-permute-done | bytes 73760 | tf_op jit(solution)/shard_map/ppermute | solution.py:131
  12.2 1.5 %collective-permute-start.6 = (bf16[16,2304]{1,0:T(8,128)(2,1)S(1)}, bf16[16,2304]{1,0:T(8,128)(2,1)S(1)}, u32[]{:S(2)}, u32[]{:S(2)}) collective-permute-start(bf16[16,2304]{1,0:T(8,128)(2,1)S(1)} %collective-permute-done.2), channel_id=1, source_target_pairs={{0,2},{1,3},{2,0},{3,1},{4,6},{5,7},{6,4},{7,5},{8,10},{9,11},{10,... | collective-permute-start | bytes 221192 | tf_op jit(solution)/shard_map/ppermute | solution.py:131
  14.3 1.6 %collective-permute-start.4 = (bf16[16,2304]{1,0:T(8,128)(2,1)S(1)}, bf16[16,2304]{1,0:T(8,128)(2,1)S(1)}, u32[]{:S(2)}, u32[]{:S(2)}) collective-permute-start(bf16[16,2304]{1,0:T(8,128)(2,1)S(1)} %collective-permute-done), channel_id=1, source_target_pairs={{0,2},{1,3},{2,0},{3,1},{4,6},{5,7},{6,4},{7,5},{8,10},{9,11},{10,... | collective-permute-start | bytes 221192 | tf_op jit(solution)/shard_map/ppermute | solution.py:131
  15.9 3.8 %collective-permute-done.4 = bf16[16,2304]{1,0:T(8,128)(2,1)S(1)} collective-permute-done((bf16[16,2304]{1,0:T(8,128)(2,1)S(1)}, bf16[16,2304]{1,0:T(8,128)(2,1)S(1)}, u32[]{:S(2)}, u32[]{:S(2)}) %collective-permute-start.4) | collective-permute-done | bytes 73760 | tf_op jit(solution)/shard_map/ppermute | solution.py:131
  21.6 0.9 %slice_dynamic-update-slice_fusion.6 = bf16[256,2304]{1,0:T(8,128)(2,1)S(1)} fusion(bf16[256,2304]{1,0:T(8,128)(2,1)S(1)} %slice_dynamic-update-slice_fusion.7, bf16[128,2304]{1,0:T(8,128)(2,1)} %subtract_convert_fusion), kind=kLoop, calls=%fused_computation.28 | loop fusion | bytes 294912
  22.5 0.9 %slice_dynamic-update-slice_fusion.5 = bf16[256,2304]{1,0:T(8,128)(2,1)S(1)} fusion(bf16[256,2304]{1,0:T(8,128)(2,1)S(1)} %slice_dynamic-update-slice_fusion.6, bf16[128,2304]{1,0:T(8,128)(2,1)} %subtract_convert_fusion), kind=kLoop, calls=%fused_computation.27 | loop fusion | bytes 294912
  23.4 0.9 %slice_dynamic-update-slice_fusion.4 = bf16[256,2304]{1,0:T(8,128)(2,1)S(1)} fusion(bf16[256,2304]{1,0:T(8,128)(2,1)S(1)} %slice_dynamic-update-slice_fusion.5, bf16[128,2304]{1,0:T(8,128)(2,1)} %subtract_convert_fusion), kind=kLoop, calls=%fused_computation.26 | loop fusion | bytes 294912
  24.4 1.5 %fusion.18 = bf16[128,256]{0,1:T(8,128)(2,1)S(1)} fusion(bf16[128,2304]{1,0:T(8,128)(2,1)} %subtract_convert_fusion, bf16[128,2304]{1,0:T(8,128)(2,1)S(1)} %collective-permute-done.7, bf16[128,2304]{1,0:T(8,128)(2,1)S(1)} %copy-done.5, f32[256]{0:T(256)S(1)} %pad_maximum_fusion.1), kind=kOutput, calls=%fused_computation.20 | convolution fusion | flops 153452544 | bytes 1836032 | tf_op jit(solution)/shard_map/dot_general | solution.py:17
  27.1 1.1 %collective-permute-start.15 = (bf16[16,2304]{1,0:T(8,128)(2,1)S(1)}, bf16[16,2304]{1,0:T(8,128)(2,1)S(1)}, u32[]{:S(2)}, u32[]{:S(2)}) collective-permute-start(bf16[16,2304]{1,0:T(8,128)(2,1)S(1)} %get-tuple-element.20), channel_id=1, source_target_pairs={{0,2},{1,3},{2,0},{3,1},{4,6},{5,7},{6,4},{7,5},{8,10},{9,11},{10,... | collective-permute-start | bytes 221192 | tf_op jit(solution)/shard_map/ppermute | solution.py:131
  29.1 1.0 %collective-permute-start.10 = (bf16[16,2304]{1,0:T(8,128)(2,1)}, bf16[16,2304]{1,0:T(8,128)(2,1)}, u32[]{:S(2)}, u32[]{:S(2)}) collective-permute-start(bf16[16,2304]{1,0:T(8,128)(2,1)} %get-tuple-element.19), channel_id=1, source_target_pairs={{0,2},{1,3},{2,0},{3,1},{4,6},{5,7},{6,4},{7,5},{8,10},{9,11},{10,... | collective-permute-start | bytes 221192 | tf_op jit(solution)/shard_map/ppermute | solution.py:131
  30.1 1.1 %collective-permute-start.13 = (bf16[16,2304]{1,0:T(8,128)(2,1)S(1)}, bf16[16,2304]{1,0:T(8,128)(2,1)S(1)}, u32[]{:S(2)}, u32[]{:S(2)}) collective-permute-start(bf16[16,2304]{1,0:T(8,128)(2,1)S(1)} %get-tuple-element.21), channel_id=1, source_target_pairs={{0,2},{1,3},{2,0},{3,1},{4,6},{5,7},{6,4},{7,5},{8,10},{9,11},{10,... | collective-permute-start | bytes 221192 | tf_op jit(solution)/shard_map/ppermute | solution.py:131
  31.8 1.1 %collective-permute-start.11 = (bf16[16,2304]{1,0:T(8,128)(2,1)S(1)}, bf16[16,2304]{1,0:T(8,128)(2,1)S(1)}, u32[]{:S(2)}, u32[]{:S(2)}) collective-permute-start(bf16[16,2304]{1,0:T(8,128)(2,1)S(1)} %get-tuple-element.22), channel_id=1, source_target_pairs={{0,2},{1,3},{2,0},{3,1},{4,6},{5,7},{6,4},{7,5},{8,10},{9,11},{10,... | collective-permute-start | bytes 221192 | tf_op jit(solution)/shard_map/ppermute | solution.py:131
  32.8 1.0 %fusion.7 = bf16[16,2304]{1,0:T(8,128)(2,1)} fusion(bf16[256,2304]{1,0:T(8,128)(2,1)S(1)} %constant_dynamic-update-slice_fusion.8, bf16[16,2304]{1,0:T(8,128)(2,1)S(1)} %collective-permute-done.15, bf16[128,256]{0,1:T(8,128)(2,1)S(1)} %fusion.18), kind=kOutput, calls=%fused_computation.12 | convolution fusion | flops 18984960 | bytes 1392640 | tf_op jit(solution)/shard_map/dot_general | solution.py:183
  33.8 2.2 %collective-permute-done.13 = bf16[16,2304]{1,0:T(8,128)(2,1)S(1)} collective-permute-done((bf16[16,2304]{1,0:T(8,128)(2,1)S(1)}, bf16[16,2304]{1,0:T(8,128)(2,1)S(1)}, u32[]{:S(2)}, u32[]{:S(2)}) %collective-permute-start.13) | collective-permute-done | bytes 73760 | tf_op jit(solution)/shard_map/ppermute | solution.py:131
  36.0 2.2 %collective-permute-start.16 = (bf16[16,2304]{1,0:T(8,128)(2,1)}, bf16[16,2304]{1,0:T(8,128)(2,1)}, u32[]{:S(2)}, u32[]{:S(2)}) collective-permute-start(bf16[16,2304]{1,0:T(8,128)(2,1)} %fusion.7), channel_id=1, source_target_pairs={{0,12},{1,13},{2,14},{3,15},{4,8},{5,9},{6,10},{7,11},{8,4},{9,5},... | collective-permute-start | bytes 221192 | tf_op jit(solution)/shard_map/ppermute | solution.py:131
  38.2 1.0 %fusion.6 = bf16[16,2304]{1,0:T(8,128)(2,1)} fusion(bf16[256,2304]{1,0:T(8,128)(2,1)S(1)} %constant_dynamic-update-slice_fusion.8, bf16[16,2304]{1,0:T(8,128)(2,1)S(1)} %collective-permute-done.13, bf16[128,256]{0,1:T(8,128)(2,1)S(1)} %fusion.18), kind=kOutput, calls=%fused_computation.11 | convolution fusion | flops 18984960 | bytes 1392640 | tf_op jit(solution)/shard_map/dot_general | solution.py:183
  39.3 1.0 %fusion.5 = bf16[16,2304]{1,0:T(8,128)(2,1)} fusion(bf16[256,2304]{1,0:T(8,128)(2,1)S(1)} %constant_dynamic-update-slice_fusion.8, bf16[16,2304]{1,0:T(8,128)(2,1)S(1)} %collective-permute-done.11, bf16[128,256]{0,1:T(8,128)(2,1)S(1)} %fusion.18), kind=kOutput, calls=%fused_computation.10 | convolution fusion | flops 18984960 | bytes 1392640 | tf_op jit(solution)/shard_map/dot_general | solution.py:183
  40.3 2.1 %collective-permute-start.12 = (bf16[16,2304]{1,0:T(8,128)(2,1)}, bf16[16,2304]{1,0:T(8,128)(2,1)}, u32[]{:S(2)}, u32[]{:S(2)}) collective-permute-start(bf16[16,2304]{1,0:T(8,128)(2,1)} %fusion.5), channel_id=1, source_target_pairs={{0,4},{1,5},{2,6},{3,7},{4,0},{5,1},{6,2},{7,3},{8,12},{9,13},{10,... | collective-permute-start | bytes 221192 | tf_op jit(solution)/shard_map/ppermute | solution.py:131
  43.2 1.6 %concatenate.29 = bf16[256,128]{0,1:T(8,128)(2,1)} concatenate(bf16[32,128]{0,1:T(8,128)(2,1)} %get-tuple-element.26, bf16[32,128]{0,1:T(8,128)(2,1)} %get-tuple-element.25, bf16[32,128]{0,1:T(8,128)(2,1)} %get-tuple-element.24, bf16[32,128]{0,1:T(8,128)(2,1)} %get-tuple-element.23, bf16[32,128]{0,1:T(8,128)(2,1)} %get-tuple-element.30, bf16[32,128]{0,1:T(8,128)(2,1)} %get-tuple-element.29, ...), dimensions={0} | concatenate | bytes 131072 | tf_op jit(solution)/shard_map/concatenate | solution.py:200
  45.8 1.8 %fusion.4 = bf16[16,2304]{1,0:T(8,128)(2,1)S(1)} fusion(bf16[256,2304]{1,0:T(8,128)(2,1)} %copy-done.7, bf16[16,2304]{1,0:T(8,128)(2,1)} %collective-permute-done.16, bf16[16,2304]{1,0:T(8,128)(2,1)} %collective-permute-done.14, bf16[16,2304]{1,0:T(8,128)(2,1)} %collective-permute-done.12, bf16[16,2304]{1,0:T(8,128)(2,1)} %collective-permute-done.10, ...), kind=kOutput, calls=%fused_computation.9 | convolution fusion | flops 19279872 | bytes 1687552 | tf_op jit(solution)/shard_map/dot_general | solution.py:183
  47.6 2.3 %collective-permute-start.23 = (bf16[16,2304]{1,0:T(8,128)(2,1)S(1)}, bf16[16,2304]{1,0:T(8,128)(2,1)S(1)}, u32[]{:S(2)}, u32[]{:S(2)}) collective-permute-start(bf16[16,2304]{1,0:T(8,128)(2,1)S(1)} %fusion.4), channel_id=1, source_target_pairs={{0,12},{1,13},{2,14},{3,15},{4,8},{5,9},{6,10},{7,11},{8,4},{9,5},... | collective-permute-start | bytes 221192 | tf_op jit(solution)/shard_map/ppermute | solution.py:131
  50.4 1.0 %collective-permute-start.20 = (bf16[16,2304]{1,0:T(8,128)(2,1)S(1)}, bf16[16,2304]{1,0:T(8,128)(2,1)S(1)}, u32[]{:S(2)}, u32[]{:S(2)}) collective-permute-start(bf16[16,2304]{1,0:T(8,128)(2,1)S(1)} %fusion.4), channel_id=1, source_target_pairs={{0,2},{1,3},{2,0},{3,1},{4,6},{5,7},{6,4},{7,5},{8,10},{9,11},{10,... | collective-permute-start | bytes 221192 | tf_op jit(solution)/shard_map/ppermute | solution.py:131
  51.4 1.5 %collective-permute-start.19 = (bf16[16,2304]{1,0:T(8,128)(2,1)S(1)}, bf16[16,2304]{1,0:T(8,128)(2,1)S(1)}, u32[]{:S(2)}, u32[]{:S(2)}) collective-permute-start(bf16[16,2304]{1,0:T(8,128)(2,1)S(1)} %fusion.4), channel_id=1, source_target_pairs={{0,4},{1,5},{2,6},{3,7},{4,0},{5,1},{6,2},{7,3},{8,12},{9,13},{10,... | collective-permute-start | bytes 221192 | tf_op jit(solution)/shard_map/ppermute | solution.py:131
  53.9 0.9 %slice_dynamic-update-slice_fusion.2 = bf16[256,2304]{1,0:T(8,128)(2,1)S(1)} fusion(bf16[256,2304]{1,0:T(8,128)(2,1)S(1)} %slice_dynamic-update-slice_fusion.3, bf16[128,2304]{1,0:T(8,128)(2,1)} %collective-permute-done.18), kind=kLoop, calls=%fused_computation.24 | loop fusion | bytes 294912
  54.8 0.9 %slice_dynamic-update-slice_fusion.1 = bf16[256,2304]{1,0:T(8,128)(2,1)S(1)} fusion(bf16[256,2304]{1,0:T(8,128)(2,1)S(1)} %slice_dynamic-update-slice_fusion.2, bf16[128,2304]{1,0:T(8,128)(2,1)} %collective-permute-done.18), kind=kLoop, calls=%fused_computation.23 | loop fusion | bytes 294912
  56.0 1.2 %collective-permute-start.24 = (bf16[16,2304]{1,0:T(8,128)(2,1)S(1)}, bf16[16,2304]{1,0:T(8,128)(2,1)S(1)}, u32[]{:S(2)}, u32[]{:S(2)}) collective-permute-start(bf16[16,2304]{1,0:T(8,128)(2,1)S(1)} %collective-permute-done.22), channel_id=1, source_target_pairs={{0,2},{1,3},{2,0},{3,1},{4,6},{5,7},{6,4},{7,5},{8,10},{9,11},{10,... | collective-permute-start | bytes 221192 | tf_op jit(solution)/shard_map/ppermute | solution.py:131
  58.1 1.2 %collective-permute-start.21 = (bf16[16,2304]{1,0:T(8,128)(2,1)S(1)}, bf16[16,2304]{1,0:T(8,128)(2,1)S(1)}, u32[]{:S(2)}, u32[]{:S(2)}) collective-permute-start(bf16[16,2304]{1,0:T(8,128)(2,1)S(1)} %collective-permute-done.19), channel_id=1, source_target_pairs={{0,2},{1,3},{2,0},{3,1},{4,6},{5,7},{6,4},{7,5},{8,10},{9,11},{10,... | collective-permute-start | bytes 221192 | tf_op jit(solution)/shard_map/ppermute | solution.py:131
  59.4 1.5 %collective-permute-done.24 = bf16[16,2304]{1,0:T(8,128)(2,1)S(1)} collective-permute-done((bf16[16,2304]{1,0:T(8,128)(2,1)S(1)}, bf16[16,2304]{1,0:T(8,128)(2,1)S(1)}, u32[]{:S(2)}, u32[]{:S(2)}) %collective-permute-start.24) | collective-permute-done | bytes 73760 | tf_op jit(solution)/shard_map/ppermute | solution.py:131
  64.2 5.2 %update.1 = (bf16[128,2304]{1,0:T(8,128)(2,1)}, f32[128,2304]{1,0:T(8,128)}, f32[128,2304]{1,0:T(8,128)}, bf16[128,2304]{1,0:T(8,128)(2,1)}, f32[128,2304]{1,0:T(8,128)}, /*index=5*/f32[128,2304]{1,0:T(8,128)}) custom-call(bf16[128,256]{1,0:T(8,128)(2,1)S(1)} %bitcast.7, bf16[256,2304]{1,0:T(8,128)(2,1)S(1)} %slice_dynamic-update-slice_fusion.centered, ...), custom_call_target="tpu_custom_call" | custom-call | flops 452984832 | bytes 12976128 | tf_op jit(solution)/shard_map/update/pallas_call | solution.py:99
  (87 shorter events, 14.2 us)
Async XLA Ops:
  0.7 19.1 %copy-start.11 = (f32[2304]{0:T(1024)S(1)}, f32[2304]{0:T(1024)}, u32[]{:S(2)}) copy-start(f32[2304]{0:T(1024)} %param.13) | copy-start | bytes 27652
  0.7 9.2 %collective-permute-start.2 = (bf16[16,2304]{1,0:T(8,128)(2,1)}, bf16[16,2304]{1,0:T(8,128)(2,1)S(1)}, u32[]{:S(2)}, u32[]{:S(2)}) collective-permute-start(bf16[16,2304]{1,0:T(8,128)(2,1)} %param.9), channel_id=1, source_target_pairs={{0,12},{1,13},{2,14},{3,15},{4,8},{5,9},{6,10},{7,11},{8,4},{9,5},... | collective-permute-start | bytes 221192 | tf_op jit(solution)/shard_map/ppermute | solution.py:131
  5.8 6.4 %collective-permute-start.1 = (bf16[16,2304]{1,0:T(8,128)(2,1)}, bf16[16,2304]{1,0:T(8,128)(2,1)S(1)}, u32[]{:S(2)}, u32[]{:S(2)}) collective-permute-start(bf16[16,2304]{1,0:T(8,128)(2,1)} %param.9), channel_id=1, source_target_pairs={{0,8},{1,9},{2,10},{3,11},{4,12},{5,13},{6,14},{7,15},{8,0},{9,1},... | collective-permute-start | bytes 221192 | tf_op jit(solution)/shard_map/ppermute | solution.py:131
  5.8 7.9 %collective-permute-start = (bf16[16,2304]{1,0:T(8,128)(2,1)}, bf16[16,2304]{1,0:T(8,128)(2,1)S(1)}, u32[]{:S(2)}, u32[]{:S(2)}) collective-permute-start(bf16[16,2304]{1,0:T(8,128)(2,1)} %param.9), channel_id=1, source_target_pairs={{0,4},{1,5},{2,6},{3,7},{4,0},{5,1},{6,2},{7,3},{8,12},{9,13},{10,... | collective-permute-start | bytes 221192 | tf_op jit(solution)/shard_map/ppermute | solution.py:131
  6.4 7.8 %collective-permute-start.3 = (bf16[16,2304]{1,0:T(8,128)(2,1)}, bf16[16,2304]{1,0:T(8,128)(2,1)S(1)}, u32[]{:S(2)}, u32[]{:S(2)}) collective-permute-start(bf16[16,2304]{1,0:T(8,128)(2,1)} %param.9), channel_id=1, source_target_pairs={{0,2},{1,3},{2,0},{3,1},{4,6},{5,7},{6,4},{7,5},{8,10},{9,11},{10,... | collective-permute-start | bytes 221192 | tf_op jit(solution)/shard_map/ppermute | solution.py:131
  8.1 1.3 %collective-permute-start.8 = (f32[128]{0:T(128)}, f32[128]{0:T(128)S(1)}, u32[]{:S(2)}, u32[]{:S(2)}) collective-permute-start(f32[128]{0:T(128)} %param.11), channel_id=1, source_target_pairs={{0,1},{1,0},{2,3},{3,2},{4,5},{5,4},{6,7},{7,6},{8,9},{9,8},{10,11... | collective-permute-start | bytes 1544 | tf_op jit(solution)/shard_map/ppermute | solution.py:138
  9.4 16.6 %collective-permute-start.9 = (bf16[128,2304]{1,0:T(8,128)(2,1)S(1)}, bf16[128,2304]{1,0:T(8,128)(2,1)S(1)}, u32[]{:S(2)}, u32[]{:S(2)}) collective-permute-start(bf16[128,2304]{1,0:T(8,128)(2,1)S(1)} %copy-done), channel_id=1, source_target_pairs={{0,1},{1,0},{2,3},{3,2},{4,5},{5,4},{6,7},{7,6},{8,9},{9,8},{10,11... | collective-permute-start | bytes 1769480 | tf_op jit(solution)/shard_map/ppermute | solution.py:138
  9.9 14.5 %collective-permute-start.7 = (bf16[128,2304]{1,0:T(8,128)(2,1)S(1)}, bf16[128,2304]{1,0:T(8,128)(2,1)S(1)}, u32[]{:S(2)}, u32[]{:S(2)}) collective-permute-start(bf16[128,2304]{1,0:T(8,128)(2,1)S(1)} %copy-done.5), channel_id=1, source_target_pairs={{0,1},{1,0},{2,3},{3,2},{4,5},{5,4},{6,7},{7,6},{8,9},{9,8},{10,11... | collective-permute-start | bytes 1769480 | tf_op jit(solution)/shard_map/ppermute | solution.py:138
  12.2 7.5 %collective-permute-start.6 = (bf16[16,2304]{1,0:T(8,128)(2,1)S(1)}, bf16[16,2304]{1,0:T(8,128)(2,1)S(1)}, u32[]{:S(2)}, u32[]{:S(2)}) collective-permute-start(bf16[16,2304]{1,0:T(8,128)(2,1)S(1)} %collective-permute-done.2), channel_id=1, source_target_pairs={{0,2},{1,3},{2,0},{3,1},{4,6},{5,7},{6,4},{7,5},{8,10},{9,11},{10,... | collective-permute-start | bytes 221192 | tf_op jit(solution)/shard_map/ppermute | solution.py:131
  13.7 5.9 %collective-permute-start.5 = (bf16[16,2304]{1,0:T(8,128)(2,1)S(1)}, bf16[16,2304]{1,0:T(8,128)(2,1)S(1)}, u32[]{:S(2)}, u32[]{:S(2)}) collective-permute-start(bf16[16,2304]{1,0:T(8,128)(2,1)S(1)} %collective-permute-done.1), channel_id=1, source_target_pairs={{0,2},{1,3},{2,0},{3,1},{4,6},{5,7},{6,4},{7,5},{8,10},{9,11},{10,... | collective-permute-start | bytes 221192 | tf_op jit(solution)/shard_map/ppermute | solution.py:131
  14.3 5.4 %collective-permute-start.4 = (bf16[16,2304]{1,0:T(8,128)(2,1)S(1)}, bf16[16,2304]{1,0:T(8,128)(2,1)S(1)}, u32[]{:S(2)}, u32[]{:S(2)}) collective-permute-start(bf16[16,2304]{1,0:T(8,128)(2,1)S(1)} %collective-permute-done), channel_id=1, source_target_pairs={{0,2},{1,3},{2,0},{3,1},{4,6},{5,7},{6,4},{7,5},{8,10},{9,11},{10,... | collective-permute-start | bytes 221192 | tf_op jit(solution)/shard_map/ppermute | solution.py:131
  20.6 32.3 %collective-permute-start.18 = (bf16[128,2304]{1,0:T(8,128)(2,1)}, bf16[128,2304]{1,0:T(8,128)(2,1)}, u32[]{:S(2)}, u32[]{:S(2)}) collective-permute-start(bf16[128,2304]{1,0:T(8,128)(2,1)} %subtract_convert_fusion), channel_id=1, source_target_pairs={{0,1},{1,0},{2,3},{3,2},{4,5},{5,4},{6,7},{7,6},{8,9},{9,8},{10,11... | collective-permute-start | bytes 1769480 | tf_op jit(solution)/shard_map/ppermute | solution.py:138
  27.1 4.7 %collective-permute-start.15 = (bf16[16,2304]{1,0:T(8,128)(2,1)S(1)}, bf16[16,2304]{1,0:T(8,128)(2,1)S(1)}, u32[]{:S(2)}, u32[]{:S(2)}) collective-permute-start(bf16[16,2304]{1,0:T(8,128)(2,1)S(1)} %get-tuple-element.20), channel_id=1, source_target_pairs={{0,2},{1,3},{2,0},{3,1},{4,6},{5,7},{6,4},{7,5},{8,10},{9,11},{10,... | collective-permute-start | bytes 221192 | tf_op jit(solution)/shard_map/ppermute | solution.py:131
  28.9 11.4 %collective-permute-start.17 = (bf16[128,128]{0,1:T(8,128)(2,1)S(1)}, bf16[128,128]{0,1:T(8,128)(2,1)S(1)}, u32[]{:S(2)}, u32[]{:S(2)}) collective-permute-start(bf16[128,128]{0,1:T(8,128)(2,1)S(1)} %slice.163), channel_id=1, source_target_pairs={{0,1},{1,0},{2,3},{3,2},{4,5},{5,4},{6,7},{7,6},{8,9},{9,8},{10,11... | collective-permute-start | bytes 98312 | tf_op jit(solution)/shard_map/ppermute | solution.py:138
  29.1 15.7 %collective-permute-start.10 = (bf16[16,2304]{1,0:T(8,128)(2,1)}, bf16[16,2304]{1,0:T(8,128)(2,1)}, u32[]{:S(2)}, u32[]{:S(2)}) collective-permute-start(bf16[16,2304]{1,0:T(8,128)(2,1)} %get-tuple-element.19), channel_id=1, source_target_pairs={{0,2},{1,3},{2,0},{3,1},{4,6},{5,7},{6,4},{7,5},{8,10},{9,11},{10,... | collective-permute-start | bytes 221192 | tf_op jit(solution)/shard_map/ppermute | solution.py:131
  30.1 5.9 %collective-permute-start.13 = (bf16[16,2304]{1,0:T(8,128)(2,1)S(1)}, bf16[16,2304]{1,0:T(8,128)(2,1)S(1)}, u32[]{:S(2)}, u32[]{:S(2)}) collective-permute-start(bf16[16,2304]{1,0:T(8,128)(2,1)S(1)} %get-tuple-element.21), channel_id=1, source_target_pairs={{0,2},{1,3},{2,0},{3,1},{4,6},{5,7},{6,4},{7,5},{8,10},{9,11},{10,... | collective-permute-start | bytes 221192 | tf_op jit(solution)/shard_map/ppermute | solution.py:131
  31.8 7.5 %collective-permute-start.11 = (bf16[16,2304]{1,0:T(8,128)(2,1)S(1)}, bf16[16,2304]{1,0:T(8,128)(2,1)S(1)}, u32[]{:S(2)}, u32[]{:S(2)}) collective-permute-start(bf16[16,2304]{1,0:T(8,128)(2,1)S(1)} %get-tuple-element.22), channel_id=1, source_target_pairs={{0,2},{1,3},{2,0},{3,1},{4,6},{5,7},{6,4},{7,5},{8,10},{9,11},{10,... | collective-permute-start | bytes 221192 | tf_op jit(solution)/shard_map/ppermute | solution.py:131
  36.0 8.8 %collective-permute-start.16 = (bf16[16,2304]{1,0:T(8,128)(2,1)}, bf16[16,2304]{1,0:T(8,128)(2,1)}, u32[]{:S(2)}, u32[]{:S(2)}) collective-permute-start(bf16[16,2304]{1,0:T(8,128)(2,1)} %fusion.7), channel_id=1, source_target_pairs={{0,12},{1,13},{2,14},{3,15},{4,8},{5,9},{6,10},{7,11},{8,4},{9,5},... | collective-permute-start | bytes 221192 | tf_op jit(solution)/shard_map/ppermute | solution.py:131
  39.3 5.9 %collective-permute-start.14 = (bf16[16,2304]{1,0:T(8,128)(2,1)}, bf16[16,2304]{1,0:T(8,128)(2,1)}, u32[]{:S(2)}, u32[]{:S(2)}) collective-permute-start(bf16[16,2304]{1,0:T(8,128)(2,1)} %fusion.6), channel_id=1, source_target_pairs={{0,8},{1,9},{2,10},{3,11},{4,12},{5,13},{6,14},{7,15},{8,0},{9,1},... | collective-permute-start | bytes 221192 | tf_op jit(solution)/shard_map/ppermute | solution.py:131
  39.3 24.9 %copy-start.4 = (f32[128,2304]{1,0:T(8,128)S(1)}, f32[128,2304]{1,0:T(8,128)}, u32[]{:S(2)}) copy-start(f32[128,2304]{1,0:T(8,128)} %refs_9_.1) | copy-start | bytes 3538948
  40.3 5.5 %collective-permute-start.12 = (bf16[16,2304]{1,0:T(8,128)(2,1)}, bf16[16,2304]{1,0:T(8,128)(2,1)}, u32[]{:S(2)}, u32[]{:S(2)}) collective-permute-start(bf16[16,2304]{1,0:T(8,128)(2,1)} %fusion.5), channel_id=1, source_target_pairs={{0,4},{1,5},{2,6},{3,7},{4,0},{5,1},{6,2},{7,3},{8,12},{9,13},{10,... | collective-permute-start | bytes 221192 | tf_op jit(solution)/shard_map/ppermute | solution.py:131
  45.8 18.4 %copy-start.3 = (f32[128,2304]{1,0:T(8,128)S(1)}, f32[128,2304]{1,0:T(8,128)}, u32[]{:S(2)}) copy-start(f32[128,2304]{1,0:T(8,128)} %refs_8_.1) | copy-start | bytes 3538948
  45.8 18.4 %copy-start.6 = (bf16[256,128]{0,1:T(8,128)(2,1)S(1)}, bf16[256,128]{0,1:T(8,128)(2,1)}, u32[]{:S(2)}) copy-start(bf16[256,128]{0,1:T(8,128)(2,1)} %concatenate.29) | copy-start | bytes 196612
  47.6 9.6 %collective-permute-start.23 = (bf16[16,2304]{1,0:T(8,128)(2,1)S(1)}, bf16[16,2304]{1,0:T(8,128)(2,1)S(1)}, u32[]{:S(2)}, u32[]{:S(2)}) collective-permute-start(bf16[16,2304]{1,0:T(8,128)(2,1)S(1)} %fusion.4), channel_id=1, source_target_pairs={{0,12},{1,13},{2,14},{3,15},{4,8},{5,9},{6,10},{7,11},{8,4},{9,5},... | collective-permute-start | bytes 221192 | tf_op jit(solution)/shard_map/ppermute | solution.py:131
  50.0 6.1 %collective-permute-start.22 = (bf16[16,2304]{1,0:T(8,128)(2,1)S(1)}, bf16[16,2304]{1,0:T(8,128)(2,1)S(1)}, u32[]{:S(2)}, u32[]{:S(2)}) collective-permute-start(bf16[16,2304]{1,0:T(8,128)(2,1)S(1)} %fusion.4), channel_id=1, source_target_pairs={{0,8},{1,9},{2,10},{3,11},{4,12},{5,13},{6,14},{7,15},{8,0},{9,1},... | collective-permute-start | bytes 221192 | tf_op jit(solution)/shard_map/ppermute | solution.py:131
  50.4 11.3 %collective-permute-start.20 = (bf16[16,2304]{1,0:T(8,128)(2,1)S(1)}, bf16[16,2304]{1,0:T(8,128)(2,1)S(1)}, u32[]{:S(2)}, u32[]{:S(2)}) collective-permute-start(bf16[16,2304]{1,0:T(8,128)(2,1)S(1)} %fusion.4), channel_id=1, source_target_pairs={{0,2},{1,3},{2,0},{3,1},{4,6},{5,7},{6,4},{7,5},{8,10},{9,11},{10,... | collective-permute-start | bytes 221192 | tf_op jit(solution)/shard_map/ppermute | solution.py:131
  51.4 6.7 %collective-permute-start.19 = (bf16[16,2304]{1,0:T(8,128)(2,1)S(1)}, bf16[16,2304]{1,0:T(8,128)(2,1)S(1)}, u32[]{:S(2)}, u32[]{:S(2)}) collective-permute-start(bf16[16,2304]{1,0:T(8,128)(2,1)S(1)} %fusion.4), channel_id=1, source_target_pairs={{0,4},{1,5},{2,6},{3,7},{4,0},{5,1},{6,2},{7,3},{8,12},{9,13},{10,... | collective-permute-start | bytes 221192 | tf_op jit(solution)/shard_map/ppermute | solution.py:131
  56.0 4.8 %collective-permute-start.24 = (bf16[16,2304]{1,0:T(8,128)(2,1)S(1)}, bf16[16,2304]{1,0:T(8,128)(2,1)S(1)}, u32[]{:S(2)}, u32[]{:S(2)}) collective-permute-start(bf16[16,2304]{1,0:T(8,128)(2,1)S(1)} %collective-permute-done.22), channel_id=1, source_target_pairs={{0,2},{1,3},{2,0},{3,1},{4,6},{5,7},{6,4},{7,5},{8,10},{9,11},{10,... | collective-permute-start | bytes 221192 | tf_op jit(solution)/shard_map/ppermute | solution.py:131
  57.3 4.4 %collective-permute-start.25 = (bf16[16,2304]{1,0:T(8,128)(2,1)S(1)}, bf16[16,2304]{1,0:T(8,128)(2,1)S(1)}, u32[]{:S(2)}, u32[]{:S(2)}) collective-permute-start(bf16[16,2304]{1,0:T(8,128)(2,1)S(1)} %collective-permute-done.23), channel_id=1, source_target_pairs={{0,2},{1,3},{2,0},{3,1},{4,6},{5,7},{6,4},{7,5},{8,10},{9,11},{10,... | collective-permute-start | bytes 221192 | tf_op jit(solution)/shard_map/ppermute | solution.py:131
  58.1 4.4 %collective-permute-start.21 = (bf16[16,2304]{1,0:T(8,128)(2,1)S(1)}, bf16[16,2304]{1,0:T(8,128)(2,1)S(1)}, u32[]{:S(2)}, u32[]{:S(2)}) collective-permute-start(bf16[16,2304]{1,0:T(8,128)(2,1)S(1)} %collective-permute-done.19), channel_id=1, source_target_pairs={{0,2},{1,3},{2,0},{3,1},{4,6},{5,7},{6,4},{7,5},{8,10},{9,11},{10,... | collective-permute-start | bytes 221192 | tf_op jit(solution)/shard_map/ppermute | solution.py:131
  61.7 1.8 %collective-permute-start.27 = (bf16[64,2304]{1,0:T(8,128)(2,1)S(1)}, bf16[64,2304]{1,0:T(8,128)(2,1)S(1)}, u32[]{:S(2)}, u32[]{:S(2)}) collective-permute-start(bf16[64,2304]{1,0:T(8,128)(2,1)S(1)} %constant_dynamic-update-slice_fusion.10.refs_1_), channel_id=1, source_target_pairs={{0,1},{1,0},{2,3},{3,2},{4,5},{5,4},{6,7},{7,6},{8,9},{9,8},{10,11... | collective-permute-start | bytes 884744 | tf_op jit(solution)/shard_map/ppermute | solution.py:138
  62.5 1.6 %collective-permute-start.26 = (bf16[64,2304]{1,0:T(8,128)(2,1)S(1)}, bf16[64,2304]{1,0:T(8,128)(2,1)S(1)}, u32[]{:S(2)}, u32[]{:S(2)}) collective-permute-start(bf16[64,2304]{1,0:T(8,128)(2,1)S(1)} %pad_maximum_fusion.refs_0_), channel_id=1, source_target_pairs={{0,1},{1,0},{2,3},{3,2},{4,5},{5,4},{6,7},{7,6},{8,9},{9,8},{10,11... | collective-permute-start | bytes 884744 | tf_op jit(solution)/shard_map/ppermute | solution.py:138
  (9 other events, 112.1 us)

commit v5 on v4

v5 whole, which is shorter than its diff:
```python
import functools

import jax
import jax.numpy as jnp
from jax import lax
from jax.experimental import pallas as pl
from jax.experimental.pallas import tpu as pltpu
from jax.sharding import PartitionSpec as P

beta_first = 0.9
beta_second = 0.999
step_rate = 0.001
adam_epsilon = 1e-08


def inner_last(left, right):
    return lax.dot_general(
        left, right, (((1,), (1,)), ((), ())), preferred_element_type=jnp.float32
    )


def update_kernel(columns, rows_total, codes_across, centered, *refs):
    blocks = len(refs) - 20
    errors, (encoder, decoder) = refs[:blocks], refs[blocks : blocks + 2]
    moments = refs[blocks + 2 : blocks + 6]
    outs = refs[blocks + 6 : blocks + 12]
    error_all, *held, sem = refs[blocks + 12 :]
    tiles = encoder.shape[1] // columns

    def write(t, i):
        at = pl.ds(t * columns, columns)
        return pltpu.make_async_copy(held[i].at[:, at], outs[i].at[:, at], sem.at[t, i])

    start = 0
    for one in errors:
        error_all[pl.ds(start, one.shape[0]), :] = one[...]
        start += one.shape[0]
    codes_t = codes_across[...]
    signal = inner_last(decoder[...], error_all[...])
    delta_t = jnp.where(codes_t.astype(jnp.float32) > 0, signal, 0.0).astype(jnp.bfloat16)
    first = (1.0 - beta_first) / rows_total
    second = (1.0 - beta_second) / (rows_total * rows_total)
    for t in range(tiles):
        at = pl.ds(t * columns, columns)
        for which, (left, right, weight) in enumerate(
            ((delta_t, centered, encoder), (codes_t, error_all, decoder))
        ):
            total = jnp.dot(left, right[:, at], preferred_element_type=jnp.float32)
            moment = beta_first * moments[2 * which][:, at] + first * total
            square = beta_second * moments[2 * which + 1][:, at] + second * (total * total)
            root = square * lax.rsqrt(square)
            held[3 * which][:, at] = (
                weight[:, at].astype(jnp.float32)
                - step_rate * moment * pl.reciprocal(root + adam_epsilon, approx=True)
            ).astype(jnp.bfloat16)
            held[3 * which + 1][:, at] = moment
            held[3 * which + 2][:, at] = square
            for i in range(3 * which, 3 * which + 3):
                write(t, i).start()
    for t in range(tiles):
        for i in range(6):
            write(t, i).wait()


def update(total_rows, codes_across, centered, errors, weights, moments):
    latents, width = weights[0].shape
    rows = centered.shape[0]
    columns = next(c for c in (256, 128, width) if width % c == 0)
    full = jax.ShapeDtypeStruct((latents, width), jnp.float32)
    half = jax.ShapeDtypeStruct((latents, width), jnp.bfloat16)
    vmem = pl.BlockSpec(memory_space=pltpu.VMEM)
    wide = pltpu.VMEM((latents, width), jnp.float32)
    narrow = pltpu.VMEM((latents, width), jnp.bfloat16)
    return pl.pallas_call(
        functools.partial(update_kernel, columns, float(total_rows)),
        out_shape=(half, full, full, half, full, full),
        in_specs=[vmem] * (len(errors) + 8),
        out_specs=[pl.BlockSpec(memory_space=pl.ANY)] * 6,
        scratch_shapes=[
            pltpu.VMEM((rows, width), jnp.bfloat16),
            narrow,
            wide,
            wide,
            narrow,
            wide,
            wide,
            pltpu.SemaphoreType.DMA((width // columns, 6)),
        ],
        compiler_params=pltpu.CompilerParams(vmem_limit_bytes=20 * 1024 * 1024 + 8 * rows * width),
        cost_estimate=pl.CostEstimate(
            flops=6 * latents * width * rows,
            bytes_accessed=44 * latents * width,
            transcendentals=4 * latents * width,
        ),
        name="update",
    )(codes_across, centered, *errors, *weights, *moments)


def to_chip(block, distance):
    size = lax.axis_size("latent")
    return lax.ppermute(
        block, "latent", [(i, i ^ (2 * distance)) for i in range(size)]
    )


def to_other_core(block):
    size = lax.axis_size("latent")
    return lax.ppermute(block, "latent", [(i, i ^ 1) for i in range(size)])


def gather_chips(block, chips):
    near = [block, to_chip(block, 2)]
    far = [to_chip(block, k) for k in range(4, chips, 2)]
    near = jnp.concatenate(near, 0)
    far = jnp.concatenate(far, 0)
    return [near, far, to_chip(near, 1), to_chip(far, 1)]


def body(
    activations,
    encoder,
    encoder_bias,
    decoder,
    decoder_bias,
    encoder_moment,
    encoder_square,
    decoder_moment,
    decoder_square,
):
    rows_here, width = activations.shape
    latents_here = encoder.shape[0]
    size = lax.axis_size("latent")
    chips = size // 2
    pairs = chips // 2
    total_rows = rows_here * size

    rows_core = jnp.concatenate(gather_chips(activations, chips), 0)
    encoder_both = jnp.concatenate([encoder, to_other_core(encoder)], 0)
    decoder_both = jnp.concatenate([decoder, to_other_core(decoder)], 0)
    bias_both = jnp.concatenate([encoder_bias, to_other_core(encoder_bias)], 0)

    centered = (rows_core.astype(jnp.float32) - decoder_bias).astype(jnp.bfloat16)
    codes = jnp.maximum(inner_last(centered, encoder_both) + bias_both, 0.0).astype(
        jnp.bfloat16
    )
    other_codes = to_other_core(codes[:, latents_here:])
    other_centered = to_other_core(centered)

    split = 2 * rows_here
    given = jnp.dot(
        codes[pairs * rows_here :], decoder_both, preferred_element_type=jnp.float32
    ).astype(jnp.bfloat16)

    def pair_sums(first, last):
        return jnp.dot(
            codes[first:last], decoder_both, preferred_element_type=jnp.float32
        ) + to_chip(given[first:last], 1).astype(jnp.float32)

    near = pair_sums(0, split)
    far = pair_sums(split, pairs * rows_here).astype(jnp.bfloat16)
    summed = near[:rows_here] + to_chip(near[rows_here:].astype(jnp.bfloat16), 2).astype(
        jnp.float32
    )
    for k in range(2, pairs):
        block = far[(k - 2) * rows_here : (k - 1) * rows_here]
        summed = summed + to_chip(block, 2 * k).astype(jnp.float32)
    row_error = (summed - centered[:rows_here].astype(jnp.float32)).astype(jnp.bfloat16)

    errors = gather_chips(row_error, chips)
    codes_across = jnp.concatenate([codes[:, :latents_here], other_codes], 0).T
    centered_all = jnp.concatenate([centered, other_centered], 0)
    (
        encoder_next,
        encoder_moment_next,
        encoder_square_next,
        decoder_next,
        decoder_moment_next,
        decoder_square_next,
    ) = update(
        total_rows,
        codes_across,
        centered_all,
        errors + [to_other_core(one) for one in errors],
        (encoder, decoder),
        (encoder_moment, encoder_square, decoder_moment, decoder_square),
    )
    return (
        row_error,
        encoder_next,
        decoder_next,
        encoder_moment_next,
        encoder_square_next,
        decoder_moment_next,
        decoder_square_next,
    )


def solution(mesh):
    sharded = P(("groups", "latent"), None)
    return jax.shard_map(
        body,
        mesh=mesh,
        in_specs=(
            sharded,
            sharded,
            P(("groups", "latent")),
            sharded,
            P("groups"),
            sharded,
            sharded,
            sharded,
            sharded,
        ),
        out_specs=(sharded,) * 7,
        check_vma=False,
    )
```

time: 69.9 us -> 58.3 us (0.83)
  waiting for transfers between devices: 14 us -> 28 us
  local copies, waits for them, and re-layouts: 12.4 us -> 1.31 us
  starting transfers between devices: 29.1 us -> 22 us
  matrix products: 6.77 us -> 1.67 us
  Pallas kernels: 5.19 us -> 3.92 us
    ppermute x21 -> x15, waiting for transfers between devices: 13.3 us -> 25.5 us  [to_chip(): lax.ppermute(block, 'latent', [(i, i ^ 2 * distance) for i in range(size)])]
    ppermute x21 -> x15, starting transfers between devices: 28.2 us -> 20.7 us  [to_chip(): lax.ppermute(block, 'latent', [(i, i ^ 2 * distance) for i in range(size)])]
    unnamed x44 -> x27, local copies, waits for them, and re-layouts: 7.69 us -> 1.19 us
    dot_general x4 -> x2, matrix products: 4.8 us -> 0.77 us  [pair_sums(): jnp.dot(codes[first:last], decoder_both, preferred_element_type=jnp.float32)]
    concatenate x3 -> x1, local copies, waits for them, and re-layouts: 2.55 us -> 0.01 us  [gather_chips(): far = jnp.concatenate(far, 0)]
    slice x4, local copies, waits for them, and re-layouts: 2.14 us -> 0.06 us  [the longest x1 0.02 us: pair_sums(): given[first:last]]
    ppermute x7 -> x9, waiting for transfers between devices: 0.77 us -> 2.46 us  [to_other_core(): return lax.ppermute(block, 'latent', [(i, i ^ 1) for i in range(size)])]
    pallas_call x1, Pallas kernels: 5.19 us -> 3.92 us  [update(): pl.pallas_call(functools.partial(update_kernel, columns, float(total_rows...]
  transfers between devices with their start and end apart: 28 -> 24, of which waited for: 12 -> 13; matrix products, arithmetic and copies ran while one was open for 29% -> 4% of each run, Pallas kernels for 0% -> 0%
where the time goes in v5:
time: 58.3 us; the launch traced here: 58.1 us
  waiting for transfers between devices  28 us (48%)
  starting transfers between devices  22 us (38%)
  Pallas kernels  3.92 us (7%)
  matrix products  1.67 us (3%)
  local copies, waits for them, and re-layouts  1.31 us (2%)
  between operations  0.97 us (2%)
    ppermute x15, waiting for transfers between devices, to_chip(): lax.ppermute(block, 'latent', [(i, i ^ 2 * distance) for i in range(size)])  25.5 us
    ppermute x15, starting transfers between devices, to_chip(): lax.ppermute(block, 'latent', [(i, i ^ 2 * distance) for i in range(size)])  20.7 us
    pallas_call x1, Pallas kernels, update(): pl.pallas_call(functools.partial(update_kernel, columns, float(total_rows...  3.92 us
    ppermute x9, waiting for transfers between devices, to_other_core(): return lax.ppermute(block, 'latent', [(i, i ^ 1) for i in range(size)])  2.46 us
    ppermute x9, starting transfers between devices, to_other_core(): return lax.ppermute(block, 'latent', [(i, i ^ 1) for i in range(size)])  1.33 us
    unnamed x27, local copies, waits for them, and re-layouts  1.19 us
  transfers between devices with their start and end apart: 24, of which 13 were waited for; matrix products, arithmetic and copies ran while one was open for 4% of the time, Pallas kernels for 0%

profile of v5, /device:TPU:0, one launch (start us, length us, event | category | flops | bytes accessed | tf_op | source)
XLA Modules:
  0.0 58.1 jit_solution(7689869725613675707)
XLA Ops:
  0.7 5.1 %collective-permute-start.2 = (bf16[16,2304]{1,0:T(8,128)(2,1)}, bf16[16,2304]{1,0:T(8,128)(2,1)S(1)}, u32[]{:S(2)}, u32[]{:S(2)}) collective-permute-start(bf16[16,2304]{1,0:T(8,128)(2,1)} %param.9), channel_id=1, source_target_pairs={{0,12},{1,13},{2,14},{3,15},{4,8},{5,9},{6,10},{7,11},{8,4},{9,5},... | collective-permute-start | bytes 221192 | tf_op jit(solution)/shard_map/ppermute | solution.py:101
  5.8 0.6 %collective-permute-start = (bf16[16,2304]{1,0:T(8,128)(2,1)}, bf16[16,2304]{1,0:T(8,128)(2,1)S(1)}, u32[]{:S(2)}, u32[]{:S(2)}) collective-permute-start(bf16[16,2304]{1,0:T(8,128)(2,1)} %param.9), channel_id=1, source_target_pairs={{0,4},{1,5},{2,6},{3,7},{4,0},{5,1},{6,2},{7,3},{8,12},{9,13},{10,... | collective-permute-start | bytes 221192 | tf_op jit(solution)/shard_map/ppermute | solution.py:101
  6.4 0.5 collective-permute-start.7
  6.9 1.1 %constant_dynamic-update-slice_fusion.7 = bf16[256,2304]{1,0:T(8,128)(2,1)S(1)} fusion(bf16[128,2304]{1,0:T(8,128)(2,1)} %refs_9_.1), kind=kLoop, calls=%fused_computation.33 | loop fusion | bytes 1179648
  8.2 0.6 collective-permute-done.2
  8.8 3.4 %collective-permute-done.1 = bf16[16,2304]{1,0:T(8,128)(2,1)S(1)} collective-permute-done((bf16[16,2304]{1,0:T(8,128)(2,1)}, bf16[16,2304]{1,0:T(8,128)(2,1)S(1)}, u32[]{:S(2)}, u32[]{:S(2)}) %collective-permute-start.1) | collective-permute-done | bytes 73760 | tf_op jit(solution)/shard_map/ppermute | solution.py:101
  12.2 1.6 %collective-permute-start.4 = (bf16[32,2304]{1,0:T(8,128)(2,1)S(1)}, bf16[32,2304]{1,0:T(8,128)(2,1)S(1)}, u32[]{:S(2)}, u32[]{:S(2)}) collective-permute-start(bf16[32,2304]{1,0:T(8,128)(2,1)S(1)} %pad_maximum_fusion.2), channel_id=1, source_target_pairs={{0,2},{1,3},{2,0},{3,1},{4,6},{5,7},{6,4},{7,5},{8,10},{9,11},{10,... | collective-permute-start | bytes 442376 | tf_op jit(solution)/shard_map/ppermute | solution.py:101
  13.8 0.6 collective-permute-start.3
  14.4 6.2 %collective-permute-done.3 = bf16[32,2304]{1,0:T(8,128)(2,1)S(1)} collective-permute-done((bf16[32,2304]{1,0:T(8,128)(2,1)S(1)}, bf16[32,2304]{1,0:T(8,128)(2,1)S(1)}, u32[]{:S(2)}, u32[]{:S(2)}) %collective-permute-start.3) | collective-permute-done | bytes 147488 | tf_op jit(solution)/shard_map/ppermute | solution.py:101
  20.9 0.5 fusion.11
  21.3 0.4 convolution_convert_fusion
  21.8 1.8 %collective-permute-start.10 = (bf16[32,2304]{1,0:T(8,128)(2,1)S(1)}, bf16[32,2304]{1,0:T(8,128)(2,1)S(1)}, u32[]{:S(2)}, u32[]{:S(2)}) collective-permute-start(bf16[32,2304]{1,0:T(8,128)(2,1)S(1)} %get-tuple-element.19), channel_id=1, source_target_pairs={{0,2},{1,3},{2,0},{3,1},{4,6},{5,7},{6,4},{7,5},{8,10},{9,11},{10,... | collective-permute-start | bytes 442376 | tf_op jit(solution)/shard_map/ppermute | solution.py:101
  23.9 4.1 %collective-permute-done.10 = bf16[32,2304]{1,0:T(8,128)(2,1)S(1)} collective-permute-done((bf16[32,2304]{1,0:T(8,128)(2,1)S(1)}, bf16[32,2304]{1,0:T(8,128)(2,1)S(1)}, u32[]{:S(2)}, u32[]{:S(2)}) %collective-permute-start.10) | collective-permute-done | bytes 147488 | tf_op jit(solution)/shard_map/ppermute | solution.py:101
  28.0 0.4 fusion
  28.5 0.9 %collective-permute-start.12 = (bf16[16,2304]{1,0:T(8,128)(2,1)S(1)}, bf16[16,2304]{1,0:T(8,128)(2,1)S(1)}, u32[]{:S(2)}, u32[]{:S(2)}) collective-permute-start(bf16[16,2304]{1,0:T(8,128)(2,1)S(1)} %get-tuple-element.22), channel_id=1, source_target_pairs={{0,12},{1,13},{2,14},{3,15},{4,8},{5,9},{6,10},{7,11},{8,4},{9,5},... | collective-permute-start | bytes 221192 | tf_op jit(solution)/shard_map/ppermute | solution.py:101
  29.5 0.3 convolution_add_fusion.1
  29.9 2.5 %collective-permute-start.9 = (bf16[16,2304]{1,0:T(8,128)(2,1)S(1)}, bf16[16,2304]{1,0:T(8,128)(2,1)S(1)}, u32[]{:S(2)}, u32[]{:S(2)}) collective-permute-start(bf16[16,2304]{1,0:T(8,128)(2,1)S(1)} %slice.78), channel_id=1, source_target_pairs={{0,4},{1,5},{2,6},{3,7},{4,0},{5,1},{6,2},{7,3},{8,12},{9,13},{10,... | collective-permute-start | bytes 221192 | tf_op jit(solution)/shard_map/ppermute | solution.py:101
  32.4 1.3 %collective-permute-done.11 = bf16[16,2304]{1,0:T(8,128)(2,1)S(1)} collective-permute-done((bf16[16,2304]{1,0:T(8,128)(2,1)S(1)}, bf16[16,2304]{1,0:T(8,128)(2,1)S(1)}, u32[]{:S(2)}, u32[]{:S(2)}) %collective-permute-start.11) | collective-permute-done | bytes 73760 | tf_op jit(solution)/shard_map/ppermute | solution.py:101
  33.7 1.7 %collective-permute-done.12 = bf16[16,2304]{1,0:T(8,128)(2,1)S(1)} collective-permute-done((bf16[16,2304]{1,0:T(8,128)(2,1)S(1)}, bf16[16,2304]{1,0:T(8,128)(2,1)S(1)}, u32[]{:S(2)}, u32[]{:S(2)}) %collective-permute-start.12) | collective-permute-done | bytes 73760 | tf_op jit(solution)/shard_map/ppermute | solution.py:101
  35.4 0.8 %collective-permute-done.9 = bf16[16,2304]{1,0:T(8,128)(2,1)S(1)} collective-permute-done((bf16[16,2304]{1,0:T(8,128)(2,1)S(1)}, bf16[16,2304]{1,0:T(8,128)(2,1)S(1)}, u32[]{:S(2)}, u32[]{:S(2)}) %collective-permute-start.9) | collective-permute-done | bytes 73760 | tf_op jit(solution)/shard_map/ppermute | solution.py:101
  36.3 0.6 %collective-permute-start.15 = (bf16[16,2304]{1,0:T(8,128)(2,1)S(1)}, bf16[16,2304]{1,0:T(8,128)(2,1)S(1)}, u32[]{:S(2)}, u32[]{:S(2)}) collective-permute-start(bf16[16,2304]{1,0:T(8,128)(2,1)S(1)} %fusion.17), channel_id=1, source_target_pairs={{0,4},{1,5},{2,6},{3,7},{4,0},{5,1},{6,2},{7,3},{8,12},{9,13},{10,... | collective-permute-start | bytes 221192 | tf_op jit(solution)/shard_map/ppermute | solution.py:101
  36.9 1.6 %collective-permute-start.17 = (bf16[16,2304]{1,0:T(8,128)(2,1)S(1)}, bf16[16,2304]{1,0:T(8,128)(2,1)S(1)}, u32[]{:S(2)}, u32[]{:S(2)}) collective-permute-start(bf16[16,2304]{1,0:T(8,128)(2,1)S(1)} %fusion.17), channel_id=1, source_target_pairs={{0,12},{1,13},{2,14},{3,15},{4,8},{5,9},{6,10},{7,11},{8,4},{9,5},... | collective-permute-start | bytes 221192 | tf_op jit(solution)/shard_map/ppermute | solution.py:101
  38.4 1.4 %collective-permute-start.16 = (bf16[16,2304]{1,0:T(8,128)(2,1)S(1)}, bf16[16,2304]{1,0:T(8,128)(2,1)S(1)}, u32[]{:S(2)}, u32[]{:S(2)}) collective-permute-start(bf16[16,2304]{1,0:T(8,128)(2,1)S(1)} %fusion.17), channel_id=1, source_target_pairs={{0,8},{1,9},{2,10},{3,11},{4,12},{5,13},{6,14},{7,15},{8,0},{9,1},... | collective-permute-start | bytes 221192 | tf_op jit(solution)/shard_map/ppermute | solution.py:101
  39.8 0.9 %collective-permute-done.15 = bf16[16,2304]{1,0:T(8,128)(2,1)S(1)} collective-permute-done((bf16[16,2304]{1,0:T(8,128)(2,1)S(1)}, bf16[16,2304]{1,0:T(8,128)(2,1)S(1)}, u32[]{:S(2)}, u32[]{:S(2)}) %collective-permute-start.15) | collective-permute-done | bytes 73760 | tf_op jit(solution)/shard_map/ppermute | solution.py:101
  40.7 1.8 %collective-permute-start.18 = (bf16[32,2304]{1,0:T(8,128)(2,1)S(1)}, bf16[32,2304]{1,0:T(8,128)(2,1)S(1)}, u32[]{:S(2)}, u32[]{:S(2)}) collective-permute-start(bf16[32,2304]{1,0:T(8,128)(2,1)S(1)} %pad_maximum_fusion.3.refs_0_), channel_id=1, source_target_pairs={{0,2},{1,3},{2,0},{3,1},{4,6},{5,7},{6,4},{7,5},{8,10},{9,11},{10,... | collective-permute-start | bytes 442376 | tf_op jit(solution)/shard_map/ppermute | solution.py:101
  42.5 4.7 %collective-permute-done.16 = bf16[16,2304]{1,0:T(8,128)(2,1)S(1)} collective-permute-done((bf16[16,2304]{1,0:T(8,128)(2,1)S(1)}, bf16[16,2304]{1,0:T(8,128)(2,1)S(1)}, u32[]{:S(2)}, u32[]{:S(2)}) %collective-permute-start.16) | collective-permute-done | bytes 73760 | tf_op jit(solution)/shard_map/ppermute | solution.py:101
  47.2 1.8 %collective-permute-start.19 = (bf16[32,2304]{1,0:T(8,128)(2,1)S(1)}, bf16[32,2304]{1,0:T(8,128)(2,1)S(1)}, u32[]{:S(2)}, u32[]{:S(2)}) collective-permute-start(bf16[32,2304]{1,0:T(8,128)(2,1)S(1)} %constant_dynamic-update-slice_fusion.8.refs_1_), channel_id=1, source_target_pairs={{0,2},{1,3},{2,0},{3,1},{4,6},{5,7},{6,4},{7,5},{8,10},{9,11},{10,... | collective-permute-start | bytes 442376 | tf_op jit(solution)/shard_map/ppermute | solution.py:101
  49.1 1.2 %collective-permute-done.13 = bf16[128,128]{0,1:T(8,128)(2,1)S(1)} collective-permute-done((bf16[128,128]{0,1:T(8,128)(2,1)S(1)}, bf16[128,128]{0,1:T(8,128)(2,1)S(1)}, u32[]{:S(2)}, u32[]{:S(2)}) %collective-permute-start.13) | collective-permute-done | bytes 32800 | tf_op jit(solution)/shard_map/ppermute | solution.py:108
  50.5 0.3 collective-permute-start.21
  51.0 1.7 %collective-permute-done.19.refs_3_ = bf16[32,2304]{1,0:T(8,128)(2,1)S(1)} collective-permute-done((bf16[32,2304]{1,0:T(8,128)(2,1)S(1)}, bf16[32,2304]{1,0:T(8,128)(2,1)S(1)}, u32[]{:S(2)}, u32[]{:S(2)}) %collective-permute-start.19) | collective-permute-done | bytes 147488 | tf_op jit(solution)/shard_map/ppermute | solution.py:101
  52.9 1.2 %collective-permute-done.23.refs_7_ = bf16[32,2304]{1,0:T(8,128)(2,1)S(1)} collective-permute-done((bf16[32,2304]{1,0:T(8,128)(2,1)S(1)}, bf16[32,2304]{1,0:T(8,128)(2,1)S(1)}, u32[]{:S(2)}, u32[]{:S(2)}) %collective-permute-start.23) | collective-permute-done | bytes 147488 | tf_op jit(solution)/shard_map/ppermute | solution.py:108
  54.2 3.9 %update.1 = (bf16[128,2304]{1,0:T(8,128)(2,1)}, f32[128,2304]{1,0:T(8,128)}, f32[128,2304]{1,0:T(8,128)}, bf16[128,2304]{1,0:T(8,128)(2,1)}, f32[128,2304]{1,0:T(8,128)}, /*index=5*/f32[128,2304]{1,0:T(8,128)}) custom-call(bf16[128,256]{1,0:T(8,128)(2,1)S(1)} %maximum_bitcast_fusion.codes_across, bf16[256,2304]{1,0:T(8,128)(2,1)S(1)} %pad_maximum_fusion.centered, ...), custom_call_target="tpu_custom_call" | custom-call | flops 452984832 | bytes 12976128 | tf_op jit(solution)/shard_map/update/pallas_call | solution.py:74
  (63 shorter events, 1.5 us)
Async XLA Ops:
  0.6 7.4 %copy-start.6 = (bf16[16,2304]{1,0:T(8,128)(2,1)S(1)}, bf16[16,2304]{1,0:T(8,128)(2,1)}, u32[]{:S(2)}) copy-start(bf16[16,2304]{1,0:T(8,128)(2,1)} %param.9) | copy-start | bytes 221188
  0.6 7.5 %copy-start.9 = (f32[128]{0:T(128)S(1)}, f32[128]{0:T(128)}, u32[]{:S(2)}) copy-start(f32[128]{0:T(128)} %param.11) | copy-start | bytes 1540
  0.7 7.4 %copy-start.5 = (bf16[128,2304]{1,0:T(8,128)(2,1)S(1)}, bf16[128,2304]{1,0:T(8,128)(2,1)}, u32[]{:S(2)}) copy-start(bf16[128,2304]{1,0:T(8,128)(2,1)} %refs_8_.1) | copy-start | bytes 1769476
  0.7 8.1 %collective-permute-start.2 = (bf16[16,2304]{1,0:T(8,128)(2,1)}, bf16[16,2304]{1,0:T(8,128)(2,1)S(1)}, u32[]{:S(2)}, u32[]{:S(2)}) collective-permute-start(bf16[16,2304]{1,0:T(8,128)(2,1)} %param.9), channel_id=1, source_target_pairs={{0,12},{1,13},{2,14},{3,15},{4,8},{5,9},{6,10},{7,11},{8,4},{9,5},... | collective-permute-start | bytes 221192 | tf_op jit(solution)/shard_map/ppermute | solution.py:101
  5.8 6.4 %collective-permute-start.1 = (bf16[16,2304]{1,0:T(8,128)(2,1)}, bf16[16,2304]{1,0:T(8,128)(2,1)S(1)}, u32[]{:S(2)}, u32[]{:S(2)}) collective-permute-start(bf16[16,2304]{1,0:T(8,128)(2,1)} %param.9), channel_id=1, source_target_pairs={{0,8},{1,9},{2,10},{3,11},{4,12},{5,13},{6,14},{7,15},{8,0},{9,1},... | collective-permute-start | bytes 221192 | tf_op jit(solution)/shard_map/ppermute | solution.py:101
  5.8 8.0 %collective-permute-start = (bf16[16,2304]{1,0:T(8,128)(2,1)}, bf16[16,2304]{1,0:T(8,128)(2,1)S(1)}, u32[]{:S(2)}, u32[]{:S(2)}) collective-permute-start(bf16[16,2304]{1,0:T(8,128)(2,1)} %param.9), channel_id=1, source_target_pairs={{0,4},{1,5},{2,6},{3,7},{4,0},{5,1},{6,2},{7,3},{8,12},{9,13},{10,... | collective-permute-start | bytes 221192 | tf_op jit(solution)/shard_map/ppermute | solution.py:101
  6.4 1.7 %collective-permute-start.6 = (f32[128]{0:T(128)}, f32[128]{0:T(128)S(1)}, u32[]{:S(2)}, u32[]{:S(2)}) collective-permute-start(f32[128]{0:T(128)} %param.11), channel_id=1, source_target_pairs={{0,1},{1,0},{2,3},{3,2},{4,5},{5,4},{6,7},{7,6},{8,9},{9,8},{10,11... | collective-permute-start | bytes 1544 | tf_op jit(solution)/shard_map/ppermute | solution.py:108
  6.4 14.4 %collective-permute-start.7 = (bf16[128,2304]{1,0:T(8,128)(2,1)}, bf16[128,2304]{1,0:T(8,128)(2,1)S(1)}, u32[]{:S(2)}, u32[]{:S(2)}) collective-permute-start(bf16[128,2304]{1,0:T(8,128)(2,1)} %refs_9_.1), channel_id=1, source_target_pairs={{0,1},{1,0},{2,3},{3,2},{4,5},{5,4},{6,7},{7,6},{8,9},{9,8},{10,11... | collective-permute-start | bytes 1769480 | tf_op jit(solution)/shard_map/ppermute | solution.py:108
  8.0 12.6 %copy-start.8 = (f32[2304]{0:T(1024)S(1)}, f32[2304]{0:T(1024)}, u32[]{:S(2)}) copy-start(f32[2304]{0:T(1024)} %param.13) | copy-start | bytes 27652
  8.1 12.8 %collective-permute-start.5 = (bf16[128,2304]{1,0:T(8,128)(2,1)S(1)}, bf16[128,2304]{1,0:T(8,128)(2,1)S(1)}, u32[]{:S(2)}, u32[]{:S(2)}) collective-permute-start(bf16[128,2304]{1,0:T(8,128)(2,1)S(1)} %copy-done.5), channel_id=1, source_target_pairs={{0,1},{1,0},{2,3},{3,2},{4,5},{5,4},{6,7},{7,6},{8,9},{9,8},{10,11... | collective-permute-start | bytes 1769480 | tf_op jit(solution)/shard_map/ppermute | solution.py:108
  12.2 8.4 %collective-permute-start.4 = (bf16[32,2304]{1,0:T(8,128)(2,1)S(1)}, bf16[32,2304]{1,0:T(8,128)(2,1)S(1)}, u32[]{:S(2)}, u32[]{:S(2)}) collective-permute-start(bf16[32,2304]{1,0:T(8,128)(2,1)S(1)} %pad_maximum_fusion.2), channel_id=1, source_target_pairs={{0,2},{1,3},{2,0},{3,1},{4,6},{5,7},{6,4},{7,5},{8,10},{9,11},{10,... | collective-permute-start | bytes 442376 | tf_op jit(solution)/shard_map/ppermute | solution.py:101
  13.8 6.8 %collective-permute-start.3 = (bf16[32,2304]{1,0:T(8,128)(2,1)S(1)}, bf16[32,2304]{1,0:T(8,128)(2,1)S(1)}, u32[]{:S(2)}, u32[]{:S(2)}) collective-permute-start(bf16[32,2304]{1,0:T(8,128)(2,1)S(1)} %pad_maximum_fusion.1), channel_id=1, source_target_pairs={{0,2},{1,3},{2,0},{3,1},{4,6},{5,7},{6,4},{7,5},{8,10},{9,11},{10,... | collective-permute-start | bytes 442376 | tf_op jit(solution)/shard_map/ppermute | solution.py:101
  21.8 6.2 %collective-permute-start.10 = (bf16[32,2304]{1,0:T(8,128)(2,1)S(1)}, bf16[32,2304]{1,0:T(8,128)(2,1)S(1)}, u32[]{:S(2)}, u32[]{:S(2)}) collective-permute-start(bf16[32,2304]{1,0:T(8,128)(2,1)S(1)} %get-tuple-element.19), channel_id=1, source_target_pairs={{0,2},{1,3},{2,0},{3,1},{4,6},{5,7},{6,4},{7,5},{8,10},{9,11},{10,... | collective-permute-start | bytes 442376 | tf_op jit(solution)/shard_map/ppermute | solution.py:101
  23.6 5.9 %collective-permute-start.8 = (bf16[32,2304]{1,0:T(8,128)(2,1)S(1)}, bf16[32,2304]{1,0:T(8,128)(2,1)S(1)}, u32[]{:S(2)}, u32[]{:S(2)}) collective-permute-start(bf16[32,2304]{1,0:T(8,128)(2,1)S(1)} %get-tuple-element.20), channel_id=1, source_target_pairs={{0,2},{1,3},{2,0},{3,1},{4,6},{5,7},{6,4},{7,5},{8,10},{9,11},{10,... | collective-permute-start | bytes 442376 | tf_op jit(solution)/shard_map/ppermute | solution.py:101
  28.4 5.3 %collective-permute-start.11 = (bf16[16,2304]{1,0:T(8,128)(2,1)S(1)}, bf16[16,2304]{1,0:T(8,128)(2,1)S(1)}, u32[]{:S(2)}, u32[]{:S(2)}) collective-permute-start(bf16[16,2304]{1,0:T(8,128)(2,1)S(1)} %get-tuple-element.21), channel_id=1, source_target_pairs={{0,8},{1,9},{2,10},{3,11},{4,12},{5,13},{6,14},{7,15},{8,0},{9,1},... | collective-permute-start | bytes 221192 | tf_op jit(solution)/shard_map/ppermute | solution.py:101
  28.5 6.9 %collective-permute-start.12 = (bf16[16,2304]{1,0:T(8,128)(2,1)S(1)}, bf16[16,2304]{1,0:T(8,128)(2,1)S(1)}, u32[]{:S(2)}, u32[]{:S(2)}) collective-permute-start(bf16[16,2304]{1,0:T(8,128)(2,1)S(1)} %get-tuple-element.22), channel_id=1, source_target_pairs={{0,12},{1,13},{2,14},{3,15},{4,8},{5,9},{6,10},{7,11},{8,4},{9,5},... | collective-permute-start | bytes 221192 | tf_op jit(solution)/shard_map/ppermute | solution.py:101
  29.5 24.6 %copy-start.3 = (f32[128,2304]{1,0:T(8,128)S(1)}, f32[128,2304]{1,0:T(8,128)}, u32[]{:S(2)}) copy-start(f32[128,2304]{1,0:T(8,128)} %refs_12_.1) | copy-start | bytes 3538948
  29.5 24.6 %copy-start.4 = (f32[128,2304]{1,0:T(8,128)S(1)}, f32[128,2304]{1,0:T(8,128)}, u32[]{:S(2)}) copy-start(f32[128,2304]{1,0:T(8,128)} %refs_13_.1) | copy-start | bytes 3538948
  29.9 6.3 %collective-permute-start.9 = (bf16[16,2304]{1,0:T(8,128)(2,1)S(1)}, bf16[16,2304]{1,0:T(8,128)(2,1)S(1)}, u32[]{:S(2)}, u32[]{:S(2)}) collective-permute-start(bf16[16,2304]{1,0:T(8,128)(2,1)S(1)} %slice.78), channel_id=1, source_target_pairs={{0,4},{1,5},{2,6},{3,7},{4,0},{5,1},{6,2},{7,3},{8,12},{9,13},{10,... | collective-permute-start | bytes 221192 | tf_op jit(solution)/shard_map/ppermute | solution.py:101
  36.3 16.6 %copy-start.7 = (bf16[16,2304]{1,0:T(8,128)(2,1)}, bf16[16,2304]{1,0:T(8,128)(2,1)S(1)}, u32[]{:S(2)}) copy-start(bf16[16,2304]{1,0:T(8,128)(2,1)S(1)} %fusion.17) | copy-start | bytes 221188
  36.3 4.4 %collective-permute-start.15 = (bf16[16,2304]{1,0:T(8,128)(2,1)S(1)}, bf16[16,2304]{1,0:T(8,128)(2,1)S(1)}, u32[]{:S(2)}, u32[]{:S(2)}) collective-permute-start(bf16[16,2304]{1,0:T(8,128)(2,1)S(1)} %fusion.17), channel_id=1, source_target_pairs={{0,4},{1,5},{2,6},{3,7},{4,0},{5,1},{6,2},{7,3},{8,12},{9,13},{10,... | collective-permute-start | bytes 221192 | tf_op jit(solution)/shard_map/ppermute | solution.py:101
  36.9 15.9 %collective-permute-start.14 = (bf16[128,2304]{1,0:T(8,128)(2,1)S(1)}, bf16[128,2304]{1,0:T(8,128)(2,1)S(1)}, u32[]{:S(2)}, u32[]{:S(2)}) collective-permute-start(bf16[128,2304]{1,0:T(8,128)(2,1)S(1)} %subtract_convert_fusion), channel_id=1, source_target_pairs={{0,1},{1,0},{2,3},{3,2},{4,5},{5,4},{6,7},{7,6},{8,9},{9,8},{10,11... | collective-permute-start | bytes 1769480 | tf_op jit(solution)/shard_map/ppermute | solution.py:108
  36.9 10.3 %collective-permute-start.17 = (bf16[16,2304]{1,0:T(8,128)(2,1)S(1)}, bf16[16,2304]{1,0:T(8,128)(2,1)S(1)}, u32[]{:S(2)}, u32[]{:S(2)}) collective-permute-start(bf16[16,2304]{1,0:T(8,128)(2,1)S(1)} %fusion.17), channel_id=1, source_target_pairs={{0,12},{1,13},{2,14},{3,15},{4,8},{5,9},{6,10},{7,11},{8,4},{9,5},... | collective-permute-start | bytes 221192 | tf_op jit(solution)/shard_map/ppermute | solution.py:101
  38.4 8.8 %collective-permute-start.16 = (bf16[16,2304]{1,0:T(8,128)(2,1)S(1)}, bf16[16,2304]{1,0:T(8,128)(2,1)S(1)}, u32[]{:S(2)}, u32[]{:S(2)}) collective-permute-start(bf16[16,2304]{1,0:T(8,128)(2,1)S(1)} %fusion.17), channel_id=1, source_target_pairs={{0,8},{1,9},{2,10},{3,11},{4,12},{5,13},{6,14},{7,15},{8,0},{9,1},... | collective-permute-start | bytes 221192 | tf_op jit(solution)/shard_map/ppermute | solution.py:101
  40.7 13.5 %copy-start.2 = (f32[128,2304]{1,0:T(8,128)S(1)}, f32[128,2304]{1,0:T(8,128)}, u32[]{:S(2)}) copy-start(f32[128,2304]{1,0:T(8,128)} %refs_11_.1) | copy-start | bytes 3538948
  40.7 10.2 %collective-permute-start.18 = (bf16[32,2304]{1,0:T(8,128)(2,1)S(1)}, bf16[32,2304]{1,0:T(8,128)(2,1)S(1)}, u32[]{:S(2)}, u32[]{:S(2)}) collective-permute-start(bf16[32,2304]{1,0:T(8,128)(2,1)S(1)} %pad_maximum_fusion.3.refs_0_), channel_id=1, source_target_pairs={{0,2},{1,3},{2,0},{3,1},{4,6},{5,7},{6,4},{7,5},{8,10},{9,11},{10,... | collective-permute-start | bytes 442376 | tf_op jit(solution)/shard_map/ppermute | solution.py:101
  47.2 5.5 %collective-permute-start.19 = (bf16[32,2304]{1,0:T(8,128)(2,1)S(1)}, bf16[32,2304]{1,0:T(8,128)(2,1)S(1)}, u32[]{:S(2)}, u32[]{:S(2)}) collective-permute-start(bf16[32,2304]{1,0:T(8,128)(2,1)S(1)} %constant_dynamic-update-slice_fusion.8.refs_1_), channel_id=1, source_target_pairs={{0,2},{1,3},{2,0},{3,1},{4,6},{5,7},{6,4},{7,5},{8,10},{9,11},{10,... | collective-permute-start | bytes 442376 | tf_op jit(solution)/shard_map/ppermute | solution.py:101
  49.1 1.2 %collective-permute-start.13 = (bf16[128,128]{0,1:T(8,128)(2,1)S(1)}, bf16[128,128]{0,1:T(8,128)(2,1)S(1)}, u32[]{:S(2)}, u32[]{:S(2)}) collective-permute-start(bf16[128,128]{0,1:T(8,128)(2,1)S(1)} %get-tuple-element.24), channel_id=1, source_target_pairs={{0,1},{1,0},{2,3},{3,2},{4,5},{5,4},{6,7},{7,6},{8,9},{9,8},{10,11... | collective-permute-start | bytes 98312 | tf_op jit(solution)/shard_map/ppermute | solution.py:108
  50.3 2.6 %collective-permute-start.20 = (bf16[32,2304]{1,0:T(8,128)(2,1)S(1)}, bf16[32,2304]{1,0:T(8,128)(2,1)S(1)}, u32[]{:S(2)}, u32[]{:S(2)}) collective-permute-start(bf16[32,2304]{1,0:T(8,128)(2,1)S(1)} %pad_maximum_fusion.3.refs_0_), channel_id=1, source_target_pairs={{0,1},{1,0},{2,3},{3,2},{4,5},{5,4},{6,7},{7,6},{8,9},{9,8},{10,11... | collective-permute-start | bytes 442376 | tf_op jit(solution)/shard_map/ppermute | solution.py:108
  50.5 2.4 %collective-permute-start.21 = (bf16[32,2304]{1,0:T(8,128)(2,1)S(1)}, bf16[32,2304]{1,0:T(8,128)(2,1)S(1)}, u32[]{:S(2)}, u32[]{:S(2)}) collective-permute-start(bf16[32,2304]{1,0:T(8,128)(2,1)S(1)} %constant_dynamic-update-slice_fusion.8.refs_1_), channel_id=1, source_target_pairs={{0,1},{1,0},{2,3},{3,2},{4,5},{5,4},{6,7},{7,6},{8,9},{9,8},{10,11... | collective-permute-start | bytes 442376 | tf_op jit(solution)/shard_map/ppermute | solution.py:108
  50.9 2.0 %collective-permute-start.22 = (bf16[32,2304]{1,0:T(8,128)(2,1)S(1)}, bf16[32,2304]{1,0:T(8,128)(2,1)S(1)}, u32[]{:S(2)}, u32[]{:S(2)}) collective-permute-start(bf16[32,2304]{1,0:T(8,128)(2,1)S(1)} %collective-permute-done.18.refs_2_), channel_id=1, source_target_pairs={{0,1},{1,0},{2,3},{3,2},{4,5},{5,4},{6,7},{7,6},{8,9},{9,8},{10,11... | collective-permute-start | bytes 442376 | tf_op jit(solution)/shard_map/ppermute | solution.py:108
  52.8 1.4 %collective-permute-start.23 = (bf16[32,2304]{1,0:T(8,128)(2,1)S(1)}, bf16[32,2304]{1,0:T(8,128)(2,1)S(1)}, u32[]{:S(2)}, u32[]{:S(2)}) collective-permute-start(bf16[32,2304]{1,0:T(8,128)(2,1)S(1)} %collective-permute-done.19.refs_3_), channel_id=1, source_target_pairs={{0,1},{1,0},{2,3},{3,2},{4,5},{5,4},{6,7},{7,6},{8,9},{9,8},{10,11... | collective-permute-start | bytes 442376 | tf_op jit(solution)/shard_map/ppermute | solution.py:108
  (2 other events, 7.8 us)

commit v6 on v5

--- a/solution.py
+++ b/solution.py
@@ -109,11 +109,13 @@
 
 
 def gather_chips(block, chips):
-    near = [block, to_chip(block, 2)]
-    far = [to_chip(block, k) for k in range(4, chips, 2)]
-    near = jnp.concatenate(near, 0)
-    far = jnp.concatenate(far, 0)
-    return [near, far, to_chip(near, 1), to_chip(far, 1)]
+    far = []
+    for k in range(4, chips, 4):
+        far.append(to_chip(block, k))
+        far.append(to_chip(far[-1], 2))
+    near = jnp.concatenate([block, to_chip(block, 2)], 0)
+    even = [near] + far
+    return even + [to_chip(one, 1) for one in even]
 
 
 def body(
@@ -156,16 +158,21 @@
             codes[first:last], decoder_both, preferred_element_type=jnp.float32
         ) + to_chip(given[first:last], 1).astype(jnp.float32)
 
+    far = [
+        pair_sums(k * rows_here, (k + 1) * rows_here).astype(jnp.bfloat16)
+        for k in range(2, pairs)
+    ]
     near = pair_sums(0, split)
-    far = pair_sums(split, pairs * rows_here).astype(jnp.bfloat16)
     summed = near[:rows_here] + to_chip(near[rows_here:].astype(jnp.bfloat16), 2).astype(
         jnp.float32
     )
-    for k in range(2, pairs):
-        block = far[(k - 2) * rows_here : (k - 1) * rows_here]
+    for k, block in enumerate(far, 2):
         summed = summed + to_chip(block, 2 * k).astype(jnp.float32)
     row_error = (summed - centered[:rows_here].astype(jnp.float32)).astype(jnp.bfloat16)
 
+    row_error, other_codes, other_centered = lax.optimization_barrier(
+        (row_error, other_codes, other_centered)
+    )
     errors = gather_chips(row_error, chips)
     codes_across = jnp.concatenate([codes[:, :latents_here], other_codes], 0).T
     centered_all = jnp.concatenate([centered, other_centered], 0)

time: 58.3 us -> 58.3 us (level)
  waiting for transfers between devices: 28 us -> 21 us
  starting transfers between devices: 22 us -> 27.8 us
  local copies, waits for them, and re-layouts: 1.31 us -> 2.17 us
    ppermute x15 -> x18, waiting for transfers between devices: 25.5 us -> 19.7 us  [to_chip(): lax.ppermute(block, 'latent', [(i, i ^ 2 * distance) for i in range(size)])]
    ppermute x15 -> x18, starting transfers between devices: 20.7 us -> 26.2 us  [to_chip(): lax.ppermute(block, 'latent', [(i, i ^ 2 * distance) for i in range(size)])]
    ppermute x9 -> x11, waiting for transfers between devices: 2.46 us -> 1.25 us  [to_other_core(): return lax.ppermute(block, 'latent', [(i, i ^ 1) for i in range(size)])]
    unnamed x27 -> x28, local copies, waits for them, and re-layouts: 1.19 us -> 2.08 us
    ppermute x9 -> x11, starting transfers between devices: 1.33 us -> 1.61 us  [to_other_core(): return lax.ppermute(block, 'latent', [(i, i ^ 1) for i in range(size)])]
  transfers between devices with their start and end apart: 24 -> 29, of which waited for: 13 -> 13; matrix products, arithmetic and copies ran while one was open for 4% -> 4% of each run, Pallas kernels for 0% -> 0%
where the time goes in v6:
time: 58.3 us; the launch traced here: 58.1 us
  starting transfers between devices  27.8 us (48%)
  waiting for transfers between devices  21 us (36%)
  Pallas kernels  3.93 us (7%)
  local copies, waits for them, and re-layouts  2.17 us (4%)
  matrix products  1.99 us (3%)
  between operations  0.95 us (2%)
    ppermute x18, starting transfers between devices, to_chip(): lax.ppermute(block, 'latent', [(i, i ^ 2 * distance) for i in range(size)])  26.2 us
    ppermute x18, waiting for transfers between devices, to_chip(): lax.ppermute(block, 'latent', [(i, i ^ 2 * distance) for i in range(size)])  19.7 us
    pallas_call x1, Pallas kernels, update(): pl.pallas_call(functools.partial(update_kernel, columns, float(total_rows...  3.93 us
    unnamed x28, local copies, waits for them, and re-layouts  2.08 us
    ppermute x11, starting transfers between devices, to_other_core(): return lax.ppermute(block, 'latent', [(i, i ^ 1) for i in range(size)])  1.61 us
    ppermute x11, waiting for transfers between devices, to_other_core(): return lax.ppermute(block, 'latent', [(i, i ^ 1) for i in range(size)])  1.25 us
  transfers between devices with their start and end apart: 29, of which 13 were waited for; matrix products, arithmetic and copies ran while one was open for 4% of the time, Pallas kernels for 0%

profile of v6, /device:TPU:0, one launch (start us, length us, event | category | flops | bytes accessed | tf_op | source)
XLA Modules:
  0.0 58.1 jit_solution(15816460396259089912)
XLA Ops:
  0.7 4.1 %collective-permute-start.1 = (bf16[16,2304]{1,0:T(8,128)(2,1)}, bf16[16,2304]{1,0:T(8,128)(2,1)S(1)}, u32[]{:S(2)}, u32[]{:S(2)}) collective-permute-start(bf16[16,2304]{1,0:T(8,128)(2,1)} %param.9), channel_id=1, source_target_pairs={{0,8},{1,9},{2,10},{3,11},{4,12},{5,13},{6,14},{7,15},{8,0},{9,1},... | collective-permute-start | bytes 221192 | tf_op jit(solution)/shard_map/ppermute | solution.py:101
  4.8 1.6 %collective-permute-start = (bf16[16,2304]{1,0:T(8,128)(2,1)}, bf16[16,2304]{1,0:T(8,128)(2,1)S(1)}, u32[]{:S(2)}, u32[]{:S(2)}) collective-permute-start(bf16[16,2304]{1,0:T(8,128)(2,1)} %param.9), channel_id=1, source_target_pairs={{0,4},{1,5},{2,6},{3,7},{4,0},{5,1},{6,2},{7,3},{8,12},{9,13},{10,... | collective-permute-start | bytes 221192 | tf_op jit(solution)/shard_map/ppermute | solution.py:101
  6.3 0.5 collective-permute-start.6
  6.9 1.1 %constant_dynamic-update-slice_fusion.8 = bf16[256,2304]{1,0:T(8,128)(2,1)S(1)} fusion(bf16[128,2304]{1,0:T(8,128)(2,1)} %refs_13_.1), kind=kLoop, calls=%fused_computation.35 | loop fusion | bytes 1179648
  8.0 1.3 %collective-permute-done = bf16[16,2304]{1,0:T(8,128)(2,1)S(1)} collective-permute-done((bf16[16,2304]{1,0:T(8,128)(2,1)}, bf16[16,2304]{1,0:T(8,128)(2,1)S(1)}, u32[]{:S(2)}, u32[]{:S(2)}) %collective-permute-start) | collective-permute-done | bytes 73760 | tf_op jit(solution)/shard_map/ppermute | solution.py:101
  9.3 1.7 %collective-permute-start.3 = (bf16[32,2304]{1,0:T(8,128)(2,1)S(1)}, bf16[32,2304]{1,0:T(8,128)(2,1)S(1)}, u32[]{:S(2)}, u32[]{:S(2)}) collective-permute-start(bf16[32,2304]{1,0:T(8,128)(2,1)S(1)} %pad_maximum_fusion.1), channel_id=1, source_target_pairs={{0,2},{1,3},{2,0},{3,1},{4,6},{5,7},{6,4},{7,5},{8,10},{9,11},{10,... | collective-permute-start | bytes 442376 | tf_op jit(solution)/shard_map/ppermute | solution.py:101
  11.4 1.6 %collective-permute-start.2 = (bf16[16,2304]{1,0:T(8,128)(2,1)S(1)}, bf16[16,2304]{1,0:T(8,128)(2,1)S(1)}, u32[]{:S(2)}, u32[]{:S(2)}) collective-permute-start(bf16[16,2304]{1,0:T(8,128)(2,1)S(1)} %collective-permute-done.1), channel_id=1, source_target_pairs={{0,4},{1,5},{2,6},{3,7},{4,0},{5,1},{6,2},{7,3},{8,12},{9,13},{10,... | collective-permute-start | bytes 221192 | tf_op jit(solution)/shard_map/ppermute | solution.py:101
  13.0 2.8 %collective-permute-done.2 = bf16[16,2304]{1,0:T(8,128)(2,1)S(1)} collective-permute-done((bf16[16,2304]{1,0:T(8,128)(2,1)S(1)}, bf16[16,2304]{1,0:T(8,128)(2,1)S(1)}, u32[]{:S(2)}, u32[]{:S(2)}) %collective-permute-start.2) | collective-permute-done | bytes 73760 | tf_op jit(solution)/shard_map/ppermute | solution.py:101
  15.8 1.7 %collective-permute-start.5 = (bf16[16,2304]{1,0:T(8,128)(2,1)S(1)}, bf16[16,2304]{1,0:T(8,128)(2,1)S(1)}, u32[]{:S(2)}, u32[]{:S(2)}) collective-permute-start(bf16[16,2304]{1,0:T(8,128)(2,1)S(1)} %collective-permute-done.2), channel_id=1, source_target_pairs={{0,2},{1,3},{2,0},{3,1},{4,6},{5,7},{6,4},{7,5},{8,10},{9,11},{10,... | collective-permute-start | bytes 221192 | tf_op jit(solution)/shard_map/ppermute | solution.py:101
  17.5 2.6 %collective-permute-done.5 = bf16[16,2304]{1,0:T(8,128)(2,1)S(1)} collective-permute-done((bf16[16,2304]{1,0:T(8,128)(2,1)S(1)}, bf16[16,2304]{1,0:T(8,128)(2,1)S(1)}, u32[]{:S(2)}, u32[]{:S(2)}) %collective-permute-start.5) | collective-permute-done | bytes 73760 | tf_op jit(solution)/shard_map/ppermute | solution.py:101
  20.3 0.9 %copy-done.5 = bf16[128,2304]{1,0:T(8,128)(2,1)S(1)} copy-done((bf16[128,2304]{1,0:T(8,128)(2,1)S(1)}, bf16[128,2304]{1,0:T(8,128)(2,1)}, u32[]{:S(2)}) %copy-start.5) | copy-done | bytes 589848
  22.2 1.7 %collective-permute-start.11 = (bf16[16,2304]{1,0:T(8,128)(2,1)S(1)}, bf16[16,2304]{1,0:T(8,128)(2,1)S(1)}, u32[]{:S(2)}, u32[]{:S(2)}) collective-permute-start(bf16[16,2304]{1,0:T(8,128)(2,1)S(1)} %get-tuple-element.25), channel_id=1, source_target_pairs={{0,2},{1,3},{2,0},{3,1},{4,6},{5,7},{6,4},{7,5},{8,10},{9,11},{10,... | collective-permute-start | bytes 221192 | tf_op jit(solution)/shard_map/ppermute | solution.py:101
  24.3 1.7 %collective-permute-start.9 = (bf16[32,2304]{1,0:T(8,128)(2,1)S(1)}, bf16[32,2304]{1,0:T(8,128)(2,1)S(1)}, u32[]{:S(2)}, u32[]{:S(2)}) collective-permute-start(bf16[32,2304]{1,0:T(8,128)(2,1)S(1)} %slice.51), channel_id=1, source_target_pairs={{0,2},{1,3},{2,0},{3,1},{4,6},{5,7},{6,4},{7,5},{8,10},{9,11},{10,... | collective-permute-start | bytes 442376 | tf_op jit(solution)/shard_map/ppermute | solution.py:101
  26.0 0.6 %collective-permute-done.11 = bf16[16,2304]{1,0:T(8,128)(2,1)S(1)} collective-permute-done((bf16[16,2304]{1,0:T(8,128)(2,1)S(1)}, bf16[16,2304]{1,0:T(8,128)(2,1)S(1)}, u32[]{:S(2)}, u32[]{:S(2)}) %collective-permute-start.11) | collective-permute-done | bytes 73760 | tf_op jit(solution)/shard_map/ppermute | solution.py:101
  26.9 1.2 %collective-permute-start.12 = (bf16[16,2304]{1,0:T(8,128)(2,1)S(1)}, bf16[16,2304]{1,0:T(8,128)(2,1)S(1)}, u32[]{:S(2)}, u32[]{:S(2)}) collective-permute-start(bf16[16,2304]{1,0:T(8,128)(2,1)S(1)} %fusion), channel_id=1, source_target_pairs={{0,8},{1,9},{2,10},{3,11},{4,12},{5,13},{6,14},{7,15},{8,0},{9,1},... | collective-permute-start | bytes 221192 | tf_op jit(solution)/shard_map/ppermute | solution.py:101
  28.1 0.9 %collective-permute-done.13 = bf16[16,2304]{1,0:T(8,128)(2,1)S(1)} collective-permute-done((bf16[16,2304]{1,0:T(8,128)(2,1)S(1)}, bf16[16,2304]{1,0:T(8,128)(2,1)S(1)}, u32[]{:S(2)}, u32[]{:S(2)}) %collective-permute-start.13) | collective-permute-done | bytes 73760 | tf_op jit(solution)/shard_map/ppermute | solution.py:101
  29.4 2.0 %collective-permute-start.14 = (bf16[16,2304]{1,0:T(8,128)(2,1)S(1)}, bf16[16,2304]{1,0:T(8,128)(2,1)S(1)}, u32[]{:S(2)}, u32[]{:S(2)}) collective-permute-start(bf16[16,2304]{1,0:T(8,128)(2,1)S(1)} %fusion.1), channel_id=1, source_target_pairs={{0,12},{1,13},{2,14},{3,15},{4,8},{5,9},{6,10},{7,11},{8,4},{9,5},... | collective-permute-start | bytes 221192 | tf_op jit(solution)/shard_map/ppermute | solution.py:101
  32.2 1.5 %collective-permute-start.10 = (bf16[16,2304]{1,0:T(8,128)(2,1)S(1)}, bf16[16,2304]{1,0:T(8,128)(2,1)S(1)}, u32[]{:S(2)}, u32[]{:S(2)}) collective-permute-start(bf16[16,2304]{1,0:T(8,128)(2,1)S(1)} %slice.80), channel_id=1, source_target_pairs={{0,4},{1,5},{2,6},{3,7},{4,0},{5,1},{6,2},{7,3},{8,12},{9,13},{10,... | collective-permute-start | bytes 221192 | tf_op jit(solution)/shard_map/ppermute | solution.py:101
  33.7 2.5 %collective-permute-done.14 = bf16[16,2304]{1,0:T(8,128)(2,1)S(1)} collective-permute-done((bf16[16,2304]{1,0:T(8,128)(2,1)S(1)}, bf16[16,2304]{1,0:T(8,128)(2,1)S(1)}, u32[]{:S(2)}, u32[]{:S(2)}) %collective-permute-start.14) | collective-permute-done | bytes 73760 | tf_op jit(solution)/shard_map/ppermute | solution.py:101
  36.2 0.7 %collective-permute-done.10 = bf16[16,2304]{1,0:T(8,128)(2,1)S(1)} collective-permute-done((bf16[16,2304]{1,0:T(8,128)(2,1)S(1)}, bf16[16,2304]{1,0:T(8,128)(2,1)S(1)}, u32[]{:S(2)}, u32[]{:S(2)}) %collective-permute-start.10) | collective-permute-done | bytes 73760 | tf_op jit(solution)/shard_map/ppermute | solution.py:101
  37.0 0.9 %collective-permute-start.18 = (bf16[16,2304]{1,0:T(8,128)(2,1)S(1)}, bf16[16,2304]{1,0:T(8,128)(2,1)S(1)}, u32[]{:S(2)}, u32[]{:S(2)}) collective-permute-start(bf16[16,2304]{1,0:T(8,128)(2,1)S(1)} %fusion.18), channel_id=1, source_target_pairs={{0,8},{1,9},{2,10},{3,11},{4,12},{5,13},{6,14},{7,15},{8,0},{9,1},... | collective-permute-start | bytes 221192 | tf_op jit(solution)/shard_map/ppermute | solution.py:101
  37.9 1.8 %collective-permute-start.17 = (bf16[16,2304]{1,0:T(8,128)(2,1)S(1)}, bf16[16,2304]{1,0:T(8,128)(2,1)S(1)}, u32[]{:S(2)}, u32[]{:S(2)}) collective-permute-start(bf16[16,2304]{1,0:T(8,128)(2,1)S(1)} %fusion.18), channel_id=1, source_target_pairs={{0,4},{1,5},{2,6},{3,7},{4,0},{5,1},{6,2},{7,3},{8,12},{9,13},{10,... | collective-permute-start | bytes 221192 | tf_op jit(solution)/shard_map/ppermute | solution.py:101
  39.7 3.3 %collective-permute-done.17 = bf16[16,2304]{1,0:T(8,128)(2,1)S(1)} collective-permute-done((bf16[16,2304]{1,0:T(8,128)(2,1)S(1)}, bf16[16,2304]{1,0:T(8,128)(2,1)S(1)}, u32[]{:S(2)}, u32[]{:S(2)}) %collective-permute-start.17) | collective-permute-done | bytes 73760 | tf_op jit(solution)/shard_map/ppermute | solution.py:101
  43.0 1.2 %collective-permute-start.20 = (bf16[32,2304]{1,0:T(8,128)(2,1)S(1)}, bf16[32,2304]{1,0:T(8,128)(2,1)S(1)}, u32[]{:S(2)}, u32[]{:S(2)}) collective-permute-start(bf16[32,2304]{1,0:T(8,128)(2,1)S(1)} %constant_dynamic-update-slice_fusion.9.refs_0_), channel_id=1, source_target_pairs={{0,2},{1,3},{2,0},{3,1},{4,6},{5,7},{6,4},{7,5},{8,10},{9,11},{10,... | collective-permute-start | bytes 442376 | tf_op jit(solution)/shard_map/ppermute | solution.py:101
  44.2 1.5 %collective-permute-start.19 = (bf16[16,2304]{1,0:T(8,128)(2,1)S(1)}, bf16[16,2304]{1,0:T(8,128)(2,1)S(1)}, u32[]{:S(2)}, u32[]{:S(2)}) collective-permute-start(bf16[16,2304]{1,0:T(8,128)(2,1)S(1)} %collective-permute-done.18.refs_1_), channel_id=1, source_target_pairs={{0,4},{1,5},{2,6},{3,7},{4,0},{5,1},{6,2},{7,3},{8,12},{9,13},{10,... | collective-permute-start | bytes 221192 | tf_op jit(solution)/shard_map/ppermute | solution.py:101
  46.7 1.9 %collective-permute-done.19.refs_2_ = bf16[16,2304]{1,0:T(8,128)(2,1)S(1)} collective-permute-done((bf16[16,2304]{1,0:T(8,128)(2,1)S(1)}, bf16[16,2304]{1,0:T(8,128)(2,1)S(1)}, u32[]{:S(2)}, u32[]{:S(2)}) %collective-permute-start.19) | collective-permute-done | bytes 73760 | tf_op jit(solution)/shard_map/ppermute | solution.py:101
  48.5 0.9 %collective-permute-start.22 = (bf16[16,2304]{1,0:T(8,128)(2,1)S(1)}, bf16[16,2304]{1,0:T(8,128)(2,1)S(1)}, u32[]{:S(2)}, u32[]{:S(2)}) collective-permute-start(bf16[16,2304]{1,0:T(8,128)(2,1)S(1)} %collective-permute-done.19.refs_2_), channel_id=1, source_target_pairs={{0,2},{1,3},{2,0},{3,1},{4,6},{5,7},{6,4},{7,5},{8,10},{9,11},{10,... | collective-permute-start | bytes 221192 | tf_op jit(solution)/shard_map/ppermute | solution.py:101
  49.6 0.6 collective-permute-start.25
  50.1 1.0 %collective-permute-done.21.refs_4_ = bf16[16,2304]{1,0:T(8,128)(2,1)S(1)} collective-permute-done((bf16[16,2304]{1,0:T(8,128)(2,1)S(1)}, bf16[16,2304]{1,0:T(8,128)(2,1)S(1)}, u32[]{:S(2)}, u32[]{:S(2)}) %collective-permute-start.21) | collective-permute-done | bytes 73760 | tf_op jit(solution)/shard_map/ppermute | solution.py:101
  51.1 1.7 %collective-permute-done.22.refs_5_ = bf16[16,2304]{1,0:T(8,128)(2,1)S(1)} collective-permute-done((bf16[16,2304]{1,0:T(8,128)(2,1)S(1)}, bf16[16,2304]{1,0:T(8,128)(2,1)S(1)}, u32[]{:S(2)}, u32[]{:S(2)}) %collective-permute-start.22) | collective-permute-done | bytes 73760 | tf_op jit(solution)/shard_map/ppermute | solution.py:101
  52.9 1.2 %collective-permute-done.28.refs_11_ = bf16[16,2304]{1,0:T(8,128)(2,1)S(1)} collective-permute-done((bf16[16,2304]{1,0:T(8,128)(2,1)S(1)}, bf16[16,2304]{1,0:T(8,128)(2,1)S(1)}, u32[]{:S(2)}, u32[]{:S(2)}) %collective-permute-start.28) | collective-permute-done | bytes 73760 | tf_op jit(solution)/shard_map/ppermute | solution.py:108
  54.2 3.9 %update.1 = (bf16[128,2304]{1,0:T(8,128)(2,1)}, f32[128,2304]{1,0:T(8,128)}, f32[128,2304]{1,0:T(8,128)}, bf16[128,2304]{1,0:T(8,128)(2,1)}, f32[128,2304]{1,0:T(8,128)}, /*index=5*/f32[128,2304]{1,0:T(8,128)}) custom-call(bf16[128,256]{1,0:T(8,128)(2,1)S(1)} %maximum_bitcast_fusion.codes_across, bf16[256,2304]{1,0:T(8,128)(2,1)S(1)} %pad_maximum_fusion.centered, ...), custom_call_target="tpu_custom_call" | custom-call | flops 452984832 | bytes 12976128 | tf_op jit(solution)/shard_map/update/pallas_call | solution.py:74
  (73 shorter events, 4.7 us)
Async XLA Ops:
  0.7 19.5 %copy-start.8 = (f32[2304]{0:T(1024)S(1)}, f32[2304]{0:T(1024)}, u32[]{:S(2)}) copy-start(f32[2304]{0:T(1024)} %param.13) | copy-start | bytes 27652
  0.7 10.4 %collective-permute-start.1 = (bf16[16,2304]{1,0:T(8,128)(2,1)}, bf16[16,2304]{1,0:T(8,128)(2,1)S(1)}, u32[]{:S(2)}, u32[]{:S(2)}) collective-permute-start(bf16[16,2304]{1,0:T(8,128)(2,1)} %param.9), channel_id=1, source_target_pairs={{0,8},{1,9},{2,10},{3,11},{4,12},{5,13},{6,14},{7,15},{8,0},{9,1},... | collective-permute-start | bytes 221192 | tf_op jit(solution)/shard_map/ppermute | solution.py:101
  4.8 4.6 %collective-permute-start = (bf16[16,2304]{1,0:T(8,128)(2,1)}, bf16[16,2304]{1,0:T(8,128)(2,1)S(1)}, u32[]{:S(2)}, u32[]{:S(2)}) collective-permute-start(bf16[16,2304]{1,0:T(8,128)(2,1)} %param.9), channel_id=1, source_target_pairs={{0,4},{1,5},{2,6},{3,7},{4,0},{5,1},{6,2},{7,3},{8,12},{9,13},{10,... | collective-permute-start | bytes 221192 | tf_op jit(solution)/shard_map/ppermute | solution.py:101
  6.3 1.6 %collective-permute-start.7 = (f32[128]{0:T(128)}, f32[128]{0:T(128)S(1)}, u32[]{:S(2)}, u32[]{:S(2)}) collective-permute-start(f32[128]{0:T(128)} %param.11), channel_id=1, source_target_pairs={{0,1},{1,0},{2,3},{3,2},{4,5},{5,4},{6,7},{7,6},{8,9},{9,8},{10,11... | collective-permute-start | bytes 1544 | tf_op jit(solution)/shard_map/ppermute | solution.py:108
  6.3 14.0 %collective-permute-start.6 = (bf16[128,2304]{1,0:T(8,128)(2,1)}, bf16[128,2304]{1,0:T(8,128)(2,1)S(1)}, u32[]{:S(2)}, u32[]{:S(2)}) collective-permute-start(bf16[128,2304]{1,0:T(8,128)(2,1)} %refs_12_.1), channel_id=1, source_target_pairs={{0,1},{1,0},{2,3},{3,2},{4,5},{5,4},{6,7},{7,6},{8,9},{9,8},{10,11... | collective-permute-start | bytes 1769480 | tf_op jit(solution)/shard_map/ppermute | solution.py:108
  6.9 13.4 %collective-permute-start.8 = (bf16[128,2304]{1,0:T(8,128)(2,1)}, bf16[128,2304]{1,0:T(8,128)(2,1)S(1)}, u32[]{:S(2)}, u32[]{:S(2)}) collective-permute-start(bf16[128,2304]{1,0:T(8,128)(2,1)} %refs_13_.1), channel_id=1, source_target_pairs={{0,1},{1,0},{2,3},{3,2},{4,5},{5,4},{6,7},{7,6},{8,9},{9,8},{10,11... | collective-permute-start | bytes 1769480 | tf_op jit(solution)/shard_map/ppermute | solution.py:108
  9.3 8.1 %collective-permute-start.3 = (bf16[32,2304]{1,0:T(8,128)(2,1)S(1)}, bf16[32,2304]{1,0:T(8,128)(2,1)S(1)}, u32[]{:S(2)}, u32[]{:S(2)}) collective-permute-start(bf16[32,2304]{1,0:T(8,128)(2,1)S(1)} %pad_maximum_fusion.1), channel_id=1, source_target_pairs={{0,2},{1,3},{2,0},{3,1},{4,6},{5,7},{6,4},{7,5},{8,10},{9,11},{10,... | collective-permute-start | bytes 442376 | tf_op jit(solution)/shard_map/ppermute | solution.py:101
  11.1 6.4 %collective-permute-start.4 = (bf16[16,2304]{1,0:T(8,128)(2,1)S(1)}, bf16[16,2304]{1,0:T(8,128)(2,1)S(1)}, u32[]{:S(2)}, u32[]{:S(2)}) collective-permute-start(bf16[16,2304]{1,0:T(8,128)(2,1)S(1)} %collective-permute-done.1), channel_id=1, source_target_pairs={{0,2},{1,3},{2,0},{3,1},{4,6},{5,7},{6,4},{7,5},{8,10},{9,11},{10,... | collective-permute-start | bytes 221192 | tf_op jit(solution)/shard_map/ppermute | solution.py:101
  11.4 4.4 %collective-permute-start.2 = (bf16[16,2304]{1,0:T(8,128)(2,1)S(1)}, bf16[16,2304]{1,0:T(8,128)(2,1)S(1)}, u32[]{:S(2)}, u32[]{:S(2)}) collective-permute-start(bf16[16,2304]{1,0:T(8,128)(2,1)S(1)} %collective-permute-done.1), channel_id=1, source_target_pairs={{0,4},{1,5},{2,6},{3,7},{4,0},{5,1},{6,2},{7,3},{8,12},{9,13},{10,... | collective-permute-start | bytes 221192 | tf_op jit(solution)/shard_map/ppermute | solution.py:101
  15.8 4.4 %collective-permute-start.5 = (bf16[16,2304]{1,0:T(8,128)(2,1)S(1)}, bf16[16,2304]{1,0:T(8,128)(2,1)S(1)}, u32[]{:S(2)}, u32[]{:S(2)}) collective-permute-start(bf16[16,2304]{1,0:T(8,128)(2,1)S(1)} %collective-permute-done.2), channel_id=1, source_target_pairs={{0,2},{1,3},{2,0},{3,1},{4,6},{5,7},{6,4},{7,5},{8,10},{9,11},{10,... | collective-permute-start | bytes 221192 | tf_op jit(solution)/shard_map/ppermute | solution.py:101
  22.2 4.4 %collective-permute-start.11 = (bf16[16,2304]{1,0:T(8,128)(2,1)S(1)}, bf16[16,2304]{1,0:T(8,128)(2,1)S(1)}, u32[]{:S(2)}, u32[]{:S(2)}) collective-permute-start(bf16[16,2304]{1,0:T(8,128)(2,1)S(1)} %get-tuple-element.25), channel_id=1, source_target_pairs={{0,2},{1,3},{2,0},{3,1},{4,6},{5,7},{6,4},{7,5},{8,10},{9,11},{10,... | collective-permute-start | bytes 221192 | tf_op jit(solution)/shard_map/ppermute | solution.py:101
  23.9 13.1 %collective-permute-start.16 = (bf16[128,2304]{1,0:T(8,128)(2,1)S(1)}, bf16[128,2304]{1,0:T(8,128)(2,1)S(1)}, u32[]{:S(2)}, u32[]{:S(2)}) collective-permute-start(bf16[128,2304]{1,0:T(8,128)(2,1)S(1)} %subtract_convert_fusion), channel_id=1, source_target_pairs={{0,1},{1,0},{2,3},{3,2},{4,5},{5,4},{6,7},{7,6},{8,9},{9,8},{10,11... | collective-permute-start | bytes 1769480 | tf_op jit(solution)/shard_map/ppermute | solution.py:108
  23.9 5.1 %collective-permute-start.13 = (bf16[16,2304]{1,0:T(8,128)(2,1)S(1)}, bf16[16,2304]{1,0:T(8,128)(2,1)S(1)}, u32[]{:S(2)}, u32[]{:S(2)}) collective-permute-start(bf16[16,2304]{1,0:T(8,128)(2,1)S(1)} %get-tuple-element.26), channel_id=1, source_target_pairs={{0,2},{1,3},{2,0},{3,1},{4,6},{5,7},{6,4},{7,5},{8,10},{9,11},{10,... | collective-permute-start | bytes 221192 | tf_op jit(solution)/shard_map/ppermute | solution.py:101
  24.3 7.5 %collective-permute-start.9 = (bf16[32,2304]{1,0:T(8,128)(2,1)S(1)}, bf16[32,2304]{1,0:T(8,128)(2,1)S(1)}, u32[]{:S(2)}, u32[]{:S(2)}) collective-permute-start(bf16[32,2304]{1,0:T(8,128)(2,1)S(1)} %slice.51), channel_id=1, source_target_pairs={{0,2},{1,3},{2,0},{3,1},{4,6},{5,7},{6,4},{7,5},{8,10},{9,11},{10,... | collective-permute-start | bytes 442376 | tf_op jit(solution)/shard_map/ppermute | solution.py:101
  26.9 6.7 %collective-permute-start.12 = (bf16[16,2304]{1,0:T(8,128)(2,1)S(1)}, bf16[16,2304]{1,0:T(8,128)(2,1)S(1)}, u32[]{:S(2)}, u32[]{:S(2)}) collective-permute-start(bf16[16,2304]{1,0:T(8,128)(2,1)S(1)} %fusion), channel_id=1, source_target_pairs={{0,8},{1,9},{2,10},{3,11},{4,12},{5,13},{6,14},{7,15},{8,0},{9,1},... | collective-permute-start | bytes 221192 | tf_op jit(solution)/shard_map/ppermute | solution.py:101
  29.0 25.1 %copy-start.4 = (f32[128,2304]{1,0:T(8,128)S(1)}, f32[128,2304]{1,0:T(8,128)}, u32[]{:S(2)}) copy-start(f32[128,2304]{1,0:T(8,128)} %refs_17_.1) | copy-start | bytes 3538948
  29.4 6.8 %collective-permute-start.14 = (bf16[16,2304]{1,0:T(8,128)(2,1)S(1)}, bf16[16,2304]{1,0:T(8,128)(2,1)S(1)}, u32[]{:S(2)}, u32[]{:S(2)}) collective-permute-start(bf16[16,2304]{1,0:T(8,128)(2,1)S(1)} %fusion.1), channel_id=1, source_target_pairs={{0,12},{1,13},{2,14},{3,15},{4,8},{5,9},{6,10},{7,11},{8,4},{9,5},... | collective-permute-start | bytes 221192 | tf_op jit(solution)/shard_map/ppermute | solution.py:101
  31.8 22.3 %copy-start.3 = (f32[128,2304]{1,0:T(8,128)S(1)}, f32[128,2304]{1,0:T(8,128)}, u32[]{:S(2)}) copy-start(f32[128,2304]{1,0:T(8,128)} %refs_16_.1) | copy-start | bytes 3538948
  32.2 4.8 %collective-permute-start.10 = (bf16[16,2304]{1,0:T(8,128)(2,1)S(1)}, bf16[16,2304]{1,0:T(8,128)(2,1)S(1)}, u32[]{:S(2)}, u32[]{:S(2)}) collective-permute-start(bf16[16,2304]{1,0:T(8,128)(2,1)S(1)} %slice.80), channel_id=1, source_target_pairs={{0,4},{1,5},{2,6},{3,7},{4,0},{5,1},{6,2},{7,3},{8,12},{9,13},{10,... | collective-permute-start | bytes 221192 | tf_op jit(solution)/shard_map/ppermute | solution.py:101
  33.7 3.3 %collective-permute-start.15 = (bf16[128,128]{0,1:T(8,128)(2,1)S(1)}, bf16[128,128]{0,1:T(8,128)(2,1)S(1)}, u32[]{:S(2)}, u32[]{:S(2)}) collective-permute-start(bf16[128,128]{0,1:T(8,128)(2,1)S(1)} %get-tuple-element.28), channel_id=1, source_target_pairs={{0,1},{1,0},{2,3},{3,2},{4,5},{5,4},{6,7},{7,6},{8,9},{9,8},{10,11... | collective-permute-start | bytes 98312 | tf_op jit(solution)/shard_map/ppermute | solution.py:108
  37.0 7.1 %collective-permute-start.18 = (bf16[16,2304]{1,0:T(8,128)(2,1)S(1)}, bf16[16,2304]{1,0:T(8,128)(2,1)S(1)}, u32[]{:S(2)}, u32[]{:S(2)}) collective-permute-start(bf16[16,2304]{1,0:T(8,128)(2,1)S(1)} %fusion.18), channel_id=1, source_target_pairs={{0,8},{1,9},{2,10},{3,11},{4,12},{5,13},{6,14},{7,15},{8,0},{9,1},... | collective-permute-start | bytes 221192 | tf_op jit(solution)/shard_map/ppermute | solution.py:101
  37.9 5.1 %collective-permute-start.17 = (bf16[16,2304]{1,0:T(8,128)(2,1)S(1)}, bf16[16,2304]{1,0:T(8,128)(2,1)S(1)}, u32[]{:S(2)}, u32[]{:S(2)}) collective-permute-start(bf16[16,2304]{1,0:T(8,128)(2,1)S(1)} %fusion.18), channel_id=1, source_target_pairs={{0,4},{1,5},{2,6},{3,7},{4,0},{5,1},{6,2},{7,3},{8,12},{9,13},{10,... | collective-permute-start | bytes 221192 | tf_op jit(solution)/shard_map/ppermute | solution.py:101
  43.0 6.5 %collective-permute-start.20 = (bf16[32,2304]{1,0:T(8,128)(2,1)S(1)}, bf16[32,2304]{1,0:T(8,128)(2,1)S(1)}, u32[]{:S(2)}, u32[]{:S(2)}) collective-permute-start(bf16[32,2304]{1,0:T(8,128)(2,1)S(1)} %constant_dynamic-update-slice_fusion.9.refs_0_), channel_id=1, source_target_pairs={{0,2},{1,3},{2,0},{3,1},{4,6},{5,7},{6,4},{7,5},{8,10},{9,11},{10,... | collective-permute-start | bytes 442376 | tf_op jit(solution)/shard_map/ppermute | solution.py:101
  44.2 4.4 %collective-permute-start.19 = (bf16[16,2304]{1,0:T(8,128)(2,1)S(1)}, bf16[16,2304]{1,0:T(8,128)(2,1)S(1)}, u32[]{:S(2)}, u32[]{:S(2)}) collective-permute-start(bf16[16,2304]{1,0:T(8,128)(2,1)S(1)} %collective-permute-done.18.refs_1_), channel_id=1, source_target_pairs={{0,4},{1,5},{2,6},{3,7},{4,0},{5,1},{6,2},{7,3},{8,12},{9,13},{10,... | collective-permute-start | bytes 221192 | tf_op jit(solution)/shard_map/ppermute | solution.py:101
  45.7 7.2 %collective-permute-start.23 = (bf16[32,2304]{1,0:T(8,128)(2,1)S(1)}, bf16[32,2304]{1,0:T(8,128)(2,1)S(1)}, u32[]{:S(2)}, u32[]{:S(2)}) collective-permute-start(bf16[32,2304]{1,0:T(8,128)(2,1)S(1)} %constant_dynamic-update-slice_fusion.9.refs_0_), channel_id=1, source_target_pairs={{0,1},{1,0},{2,3},{3,2},{4,5},{5,4},{6,7},{7,6},{8,9},{9,8},{10,11... | collective-permute-start | bytes 442376 | tf_op jit(solution)/shard_map/ppermute | solution.py:108
  45.7 3.9 %collective-permute-start.24 = (bf16[16,2304]{1,0:T(8,128)(2,1)S(1)}, bf16[16,2304]{1,0:T(8,128)(2,1)S(1)}, u32[]{:S(2)}, u32[]{:S(2)}) collective-permute-start(bf16[16,2304]{1,0:T(8,128)(2,1)S(1)} %collective-permute-done.18.refs_1_), channel_id=1, source_target_pairs={{0,1},{1,0},{2,3},{3,2},{4,5},{5,4},{6,7},{7,6},{8,9},{9,8},{10,11... | collective-permute-start | bytes 221192 | tf_op jit(solution)/shard_map/ppermute | solution.py:108
  46.2 5.0 %collective-permute-start.21 = (bf16[16,2304]{1,0:T(8,128)(2,1)S(1)}, bf16[16,2304]{1,0:T(8,128)(2,1)S(1)}, u32[]{:S(2)}, u32[]{:S(2)}) collective-permute-start(bf16[16,2304]{1,0:T(8,128)(2,1)S(1)} %collective-permute-done.18.refs_1_), channel_id=1, source_target_pairs={{0,2},{1,3},{2,0},{3,1},{4,6},{5,7},{6,4},{7,5},{8,10},{9,11},{10,... | collective-permute-start | bytes 221192 | tf_op jit(solution)/shard_map/ppermute | solution.py:101
  48.5 4.4 %collective-permute-start.22 = (bf16[16,2304]{1,0:T(8,128)(2,1)S(1)}, bf16[16,2304]{1,0:T(8,128)(2,1)S(1)}, u32[]{:S(2)}, u32[]{:S(2)}) collective-permute-start(bf16[16,2304]{1,0:T(8,128)(2,1)S(1)} %collective-permute-done.19.refs_2_), channel_id=1, source_target_pairs={{0,2},{1,3},{2,0},{3,1},{4,6},{5,7},{6,4},{7,5},{8,10},{9,11},{10,... | collective-permute-start | bytes 221192 | tf_op jit(solution)/shard_map/ppermute | solution.py:101
  49.5 4.7 %collective-permute-start.26 = (bf16[32,2304]{1,0:T(8,128)(2,1)S(1)}, bf16[32,2304]{1,0:T(8,128)(2,1)S(1)}, u32[]{:S(2)}, u32[]{:S(2)}) collective-permute-start(bf16[32,2304]{1,0:T(8,128)(2,1)S(1)} %collective-permute-done.20.refs_3_), channel_id=1, source_target_pairs={{0,1},{1,0},{2,3},{3,2},{4,5},{5,4},{6,7},{7,6},{8,9},{9,8},{10,11... | collective-permute-start | bytes 442376 | tf_op jit(solution)/shard_map/ppermute | solution.py:108
  49.6 3.4 %collective-permute-start.25 = (bf16[16,2304]{1,0:T(8,128)(2,1)S(1)}, bf16[16,2304]{1,0:T(8,128)(2,1)S(1)}, u32[]{:S(2)}, u32[]{:S(2)}) collective-permute-start(bf16[16,2304]{1,0:T(8,128)(2,1)S(1)} %collective-permute-done.19.refs_2_), channel_id=1, source_target_pairs={{0,1},{1,0},{2,3},{3,2},{4,5},{5,4},{6,7},{7,6},{8,9},{9,8},{10,11... | collective-permute-start | bytes 221192 | tf_op jit(solution)/shard_map/ppermute | solution.py:108
  51.1 1.8 %collective-permute-start.27 = (bf16[16,2304]{1,0:T(8,128)(2,1)S(1)}, bf16[16,2304]{1,0:T(8,128)(2,1)S(1)}, u32[]{:S(2)}, u32[]{:S(2)}) collective-permute-start(bf16[16,2304]{1,0:T(8,128)(2,1)S(1)} %collective-permute-done.21.refs_4_), channel_id=1, source_target_pairs={{0,1},{1,0},{2,3},{3,2},{4,5},{5,4},{6,7},{7,6},{8,9},{9,8},{10,11... | collective-permute-start | bytes 221192 | tf_op jit(solution)/shard_map/ppermute | solution.py:108
  52.9 1.3 %collective-permute-start.28 = (bf16[16,2304]{1,0:T(8,128)(2,1)S(1)}, bf16[16,2304]{1,0:T(8,128)(2,1)S(1)}, u32[]{:S(2)}, u32[]{:S(2)}) collective-permute-start(bf16[16,2304]{1,0:T(8,128)(2,1)S(1)} %collective-permute-done.22.refs_5_), channel_id=1, source_target_pairs={{0,1},{1,0},{2,3},{3,2},{4,5},{5,4},{6,7},{7,6},{8,9},{9,8},{10,11... | collective-permute-start | bytes 221192 | tf_op jit(solution)/shard_map/ppermute | solution.py:108
  (7 other events, 67.9 us)

commit v7 on v5

--- a/solution.py
+++ b/solution.py
@@ -108,12 +108,31 @@
     return lax.ppermute(block, "latent", [(i, i ^ 1) for i in range(size)])
 
 
-def gather_chips(block, chips):
-    near = [block, to_chip(block, 2)]
-    far = [to_chip(block, k) for k in range(4, chips, 2)]
-    near = jnp.concatenate(near, 0)
-    far = jnp.concatenate(far, 0)
-    return [near, far, to_chip(near, 1), to_chip(far, 1)]
+def gather_chips(block, chips, after=None):
+    quads = [[to_chip(block, q)] for q in range(4, chips, 4)]
+    if after is not None:
+        block, _ = lax.optimization_barrier((block, after))
+    quads = [[block]] + quads
+    for quad in quads:
+        quad += [to_chip(quad[0], k) for k in range(1, 4)]
+    return quads
+
+
+def sum_chips(parts):
+    def quad_sum(q):
+        total = parts[q]
+        for k in range(1, 4):
+            sent = to_chip(parts[q + k].astype(jnp.bfloat16), k)
+            total = total + sent.astype(jnp.float32)
+        return total
+
+    far = [quad_sum(q).astype(jnp.bfloat16) for q in range(4, len(parts), 4)]
+    if far:
+        far, own = lax.optimization_barrier((far, parts[:4]))
+        parts = own + parts[4:]
+    arrived = [to_chip(one, 4 * q) for q, one in enumerate(far, 1)]
+    summed = sum(one.astype(jnp.float32) for one in arrived)
+    return summed + quad_sum(0)
 
 
 def body(
@@ -131,13 +150,13 @@
     latents_here = encoder.shape[0]
     size = lax.axis_size("latent")
     chips = size // 2
-    pairs = chips // 2
     total_rows = rows_here * size
 
-    rows_core = jnp.concatenate(gather_chips(activations, chips), 0)
+    other_bias = to_other_core(encoder_bias)
+    bias_both = jnp.concatenate([encoder_bias, other_bias], 0)
     encoder_both = jnp.concatenate([encoder, to_other_core(encoder)], 0)
     decoder_both = jnp.concatenate([decoder, to_other_core(decoder)], 0)
-    bias_both = jnp.concatenate([encoder_bias, to_other_core(encoder_bias)], 0)
+    rows_core = jnp.concatenate(sum(gather_chips(activations, chips, other_bias), []), 0)
 
     centered = (rows_core.astype(jnp.float32) - decoder_bias).astype(jnp.bfloat16)
     codes = jnp.maximum(inner_last(centered, encoder_both) + bias_both, 0.0).astype(
@@ -146,27 +165,25 @@
     other_codes = to_other_core(codes[:, latents_here:])
     other_centered = to_other_core(centered)
 
-    split = 2 * rows_here
-    given = jnp.dot(
-        codes[pairs * rows_here :], decoder_both, preferred_element_type=jnp.float32
-    ).astype(jnp.bfloat16)
-
-    def pair_sums(first, last):
-        return jnp.dot(
-            codes[first:last], decoder_both, preferred_element_type=jnp.float32
-        ) + to_chip(given[first:last], 1).astype(jnp.float32)
-
-    near = pair_sums(0, split)
-    far = pair_sums(split, pairs * rows_here).astype(jnp.bfloat16)
-    summed = near[:rows_here] + to_chip(near[rows_here:].astype(jnp.bfloat16), 2).astype(
-        jnp.float32
-    )
-    for k in range(2, pairs):
-        block = far[(k - 2) * rows_here : (k - 1) * rows_here]
-        summed = summed + to_chip(block, 2 * k).astype(jnp.float32)
+    quad = 4 * rows_here
+    far = jnp.dot(codes[quad:], decoder_both, preferred_element_type=jnp.float32)
+    near = jnp.dot(codes[:quad], decoder_both, preferred_element_type=jnp.float32)
+    summed = sum_chips(
+        [
+            part[start : start + rows_here]
+            for part in (near, far)
+            for start in range(0, part.shape[0], rows_here)
+        ]
+    )
     row_error = (summed - centered[:rows_here].astype(jnp.float32)).astype(jnp.bfloat16)
 
-    errors = gather_chips(row_error, chips)
+    row_error, other_codes, other_centered = lax.optimization_barrier(
+        (row_error, other_codes, other_centered)
+    )
+    near, *far = gather_chips(row_error, chips)
+    errors = [jnp.concatenate(near, 0)]
+    for one in far:
+        errors += [one[0], jnp.concatenate(one[1:], 0)]
     codes_across = jnp.concatenate([codes[:, :latents_here], other_codes], 0).T
     centered_all = jnp.concatenate([centered, other_centered], 0)
     (

time: 58.3 us -> 60.4 us (1.036)
  starting transfers between devices: 22 us -> 30.8 us
  waiting for transfers between devices: 28 us -> 21.6 us
    ppermute x15 -> x21, starting transfers between devices: 20.7 us -> 29 us  [to_chip(): lax.ppermute(block, 'latent', [(i, i ^ 2 * distance) for i in range(size)])]
    ppermute x15 -> x21, waiting for transfers between devices: 25.5 us -> 20.7 us  [to_chip(): lax.ppermute(block, 'latent', [(i, i ^ 2 * distance) for i in range(size)])]
    ppermute x9 -> x8, waiting for transfers between devices: 2.46 us -> 0.92 us  [to_other_core(): return lax.ppermute(block, 'latent', [(i, i ^ 1) for i in range(size)])]
    ppermute x9 -> x8, starting transfers between devices: 1.33 us -> 1.8 us  [to_other_core(): return lax.ppermute(block, 'latent', [(i, i ^ 1) for i in range(size)])]
    unnamed x27 -> x33, local copies, waits for them, and re-layouts: 1.19 us -> 1.23 us
  transfers between devices with their start and end apart: 24 -> 29, of which waited for: 13 -> 13; matrix products, arithmetic and copies ran while one was open for 4% -> 5% of each run, Pallas kernels for 0% -> 0%
where the time goes in v7:
time: 60.4 us; the launch traced here: 60.3 us
  starting transfers between devices  30.8 us (51%)
  waiting for transfers between devices  21.6 us (36%)
  Pallas kernels  3.93 us (7%)
  local copies, waits for them, and re-layouts  1.35 us (2%)
  matrix products  1.26 us (2%)
  between operations  1 us (2%)
    ppermute x21, starting transfers between devices, to_chip(): lax.ppermute(block, 'latent', [(i, i ^ 2 * distance) for i in range(size)])  29 us
    ppermute x21, waiting for transfers between devices, to_chip(): lax.ppermute(block, 'latent', [(i, i ^ 2 * distance) for i in range(size)])  20.7 us
    pallas_call x1, Pallas kernels, update(): pl.pallas_call(functools.partial(update_kernel, columns, float(total_rows...  3.93 us
    ppermute x8, starting transfers between devices, to_other_core(): return lax.ppermute(block, 'latent', [(i, i ^ 1) for i in range(size)])  1.8 us
    unnamed x33, local copies, waits for them, and re-layouts  1.23 us
  transfers between devices with their start and end apart: 29, of which 13 were waited for; matrix products, arithmetic and copies ran while one was open for 5% of the time, Pallas kernels for 0%

profile of v7, /device:TPU:0, one launch (start us, length us, event | category | flops | bytes accessed | tf_op | source)
XLA Modules:
  0.0 60.3 jit_solution(113771088112733048)
XLA Ops:
  1.2 3.7 %collective-permute-start.4 = (bf16[16,2304]{1,0:T(8,128)(2,1)}, bf16[16,2304]{1,0:T(8,128)(2,1)S(1)}, u32[]{:S(2)}, u32[]{:S(2)}) collective-permute-start(bf16[16,2304]{1,0:T(8,128)(2,1)} %param.9), channel_id=1, source_target_pairs={{0,8},{1,9},{2,10},{3,11},{4,12},{5,13},{6,14},{7,15},{8,0},{9,1},... | collective-permute-start | bytes 221192 | tf_op jit(solution)/shard_map/ppermute | solution.py:101
  5.4 1.1 %constant_dynamic-update-slice_fusion.9 = bf16[256,2304]{1,0:T(8,128)(2,1)S(1)} fusion(bf16[128,2304]{1,0:T(8,128)(2,1)} %refs_7_.1), kind=kLoop, calls=%fused_computation.28 | loop fusion | bytes 1179648
  6.5 2.6 %collective-permute-start.3 = (bf16[16,2304]{1,0:T(8,128)(2,1)S(1)}, bf16[16,2304]{1,0:T(8,128)(2,1)S(1)}, u32[]{:S(2)}, u32[]{:S(2)}) collective-permute-start(bf16[16,2304]{1,0:T(8,128)(2,1)S(1)} %copy-done.7), channel_id=1, source_target_pairs={{0,6},{1,7},{2,4},{3,5},{4,2},{5,3},{6,0},{7,1},{8,14},{9,15},{10,... | collective-permute-start | bytes 221192 | tf_op jit(solution)/shard_map/ppermute | solution.py:101
  9.6 0.7 %collective-permute-start.2 = (bf16[16,2304]{1,0:T(8,128)(2,1)S(1)}, bf16[16,2304]{1,0:T(8,128)(2,1)S(1)}, u32[]{:S(2)}, u32[]{:S(2)}) collective-permute-start(bf16[16,2304]{1,0:T(8,128)(2,1)S(1)} %copy-done.7), channel_id=1, source_target_pairs={{0,4},{1,5},{2,6},{3,7},{4,0},{5,1},{6,2},{7,3},{8,12},{9,13},{10,... | collective-permute-start | bytes 221192 | tf_op jit(solution)/shard_map/ppermute | solution.py:101
  10.3 3.3 %collective-permute-done.1 = bf16[16,2304]{1,0:T(8,128)(2,1)S(1)} collective-permute-done((bf16[16,2304]{1,0:T(8,128)(2,1)S(1)}, bf16[16,2304]{1,0:T(8,128)(2,1)S(1)}, u32[]{:S(2)}, u32[]{:S(2)}) %collective-permute-start.1) | collective-permute-done | bytes 73760 | tf_op jit(solution)/shard_map/ppermute | solution.py:101
  13.7 1.4 %collective-permute-start.7 = (bf16[16,2304]{1,0:T(8,128)(2,1)S(1)}, bf16[16,2304]{1,0:T(8,128)(2,1)S(1)}, u32[]{:S(2)}, u32[]{:S(2)}) collective-permute-start(bf16[16,2304]{1,0:T(8,128)(2,1)S(1)} %collective-permute-done.4), channel_id=1, source_target_pairs={{0,6},{1,7},{2,4},{3,5},{4,2},{5,3},{6,0},{7,1},{8,14},{9,15},{10,... | collective-permute-start | bytes 221192 | tf_op jit(solution)/shard_map/ppermute | solution.py:101
  15.1 1.3 %collective-permute-start.6 = (bf16[16,2304]{1,0:T(8,128)(2,1)S(1)}, bf16[16,2304]{1,0:T(8,128)(2,1)S(1)}, u32[]{:S(2)}, u32[]{:S(2)}) collective-permute-start(bf16[16,2304]{1,0:T(8,128)(2,1)S(1)} %collective-permute-done.4), channel_id=1, source_target_pairs={{0,4},{1,5},{2,6},{3,7},{4,0},{5,1},{6,2},{7,3},{8,12},{9,13},{10,... | collective-permute-start | bytes 221192 | tf_op jit(solution)/shard_map/ppermute | solution.py:101
  16.4 0.9 %collective-permute-start.5 = (bf16[16,2304]{1,0:T(8,128)(2,1)S(1)}, bf16[16,2304]{1,0:T(8,128)(2,1)S(1)}, u32[]{:S(2)}, u32[]{:S(2)}) collective-permute-start(bf16[16,2304]{1,0:T(8,128)(2,1)S(1)} %collective-permute-done.4), channel_id=1, source_target_pairs={{0,2},{1,3},{2,0},{3,1},{4,6},{5,7},{6,4},{7,5},{8,10},{9,11},{10,... | collective-permute-start | bytes 221192 | tf_op jit(solution)/shard_map/ppermute | solution.py:101
  17.3 3.5 %collective-permute-done.5 = bf16[16,2304]{1,0:T(8,128)(2,1)S(1)} collective-permute-done((bf16[16,2304]{1,0:T(8,128)(2,1)S(1)}, bf16[16,2304]{1,0:T(8,128)(2,1)S(1)}, u32[]{:S(2)}, u32[]{:S(2)}) %collective-permute-start.5) | collective-permute-done | bytes 73760 | tf_op jit(solution)/shard_map/ppermute | solution.py:101
  22.5 0.9 %collective-permute-start.10 = (bf16[16,2304]{1,0:T(8,128)(2,1)S(1)}, bf16[16,2304]{1,0:T(8,128)(2,1)S(1)}, u32[]{:S(2)}, u32[]{:S(2)}) collective-permute-start(bf16[16,2304]{1,0:T(8,128)(2,1)S(1)} %get-tuple-element.40), channel_id=1, source_target_pairs={{0,2},{1,3},{2,0},{3,1},{4,6},{5,7},{6,4},{7,5},{8,10},{9,11},{10,... | collective-permute-start | bytes 221192 | tf_op jit(solution)/shard_map/ppermute | solution.py:101
  23.4 1.4 %collective-permute-start.12 = (bf16[16,2304]{1,0:T(8,128)(2,1)S(1)}, bf16[16,2304]{1,0:T(8,128)(2,1)S(1)}, u32[]{:S(2)}, u32[]{:S(2)}) collective-permute-start(bf16[16,2304]{1,0:T(8,128)(2,1)S(1)} %get-tuple-element.41), channel_id=1, source_target_pairs={{0,6},{1,7},{2,4},{3,5},{4,2},{5,3},{6,0},{7,1},{8,14},{9,15},{10,... | collective-permute-start | bytes 221192 | tf_op jit(solution)/shard_map/ppermute | solution.py:101
  24.8 1.2 %collective-permute-start.11 = (bf16[16,2304]{1,0:T(8,128)(2,1)S(1)}, bf16[16,2304]{1,0:T(8,128)(2,1)S(1)}, u32[]{:S(2)}, u32[]{:S(2)}) collective-permute-start(bf16[16,2304]{1,0:T(8,128)(2,1)S(1)} %get-tuple-element.42), channel_id=1, source_target_pairs={{0,4},{1,5},{2,6},{3,7},{4,0},{5,1},{6,2},{7,3},{8,12},{9,13},{10,... | collective-permute-start | bytes 221192 | tf_op jit(solution)/shard_map/ppermute | solution.py:101
  26.1 2.2 %collective-permute-done.10 = bf16[16,2304]{1,0:T(8,128)(2,1)S(1)} collective-permute-done((bf16[16,2304]{1,0:T(8,128)(2,1)S(1)}, bf16[16,2304]{1,0:T(8,128)(2,1)S(1)}, u32[]{:S(2)}, u32[]{:S(2)}) %collective-permute-start.10) | collective-permute-done | bytes 73760 | tf_op jit(solution)/shard_map/ppermute | solution.py:101
  28.3 1.0 %collective-permute-done.12 = bf16[16,2304]{1,0:T(8,128)(2,1)S(1)} collective-permute-done((bf16[16,2304]{1,0:T(8,128)(2,1)S(1)}, bf16[16,2304]{1,0:T(8,128)(2,1)S(1)}, u32[]{:S(2)}, u32[]{:S(2)}) %collective-permute-start.12) | collective-permute-done | bytes 73760 | tf_op jit(solution)/shard_map/ppermute | solution.py:101
  29.3 0.7 %collective-permute-done.11 = bf16[16,2304]{1,0:T(8,128)(2,1)S(1)} collective-permute-done((bf16[16,2304]{1,0:T(8,128)(2,1)S(1)}, bf16[16,2304]{1,0:T(8,128)(2,1)S(1)}, u32[]{:S(2)}, u32[]{:S(2)}) %collective-permute-start.11) | collective-permute-done | bytes 73760 | tf_op jit(solution)/shard_map/ppermute | solution.py:101
  30.0 2.5 %collective-permute-start.13 = (bf16[16,2304]{1,0:T(8,128)(2,1)S(1)}, bf16[16,2304]{1,0:T(8,128)(2,1)S(1)}, u32[]{:S(2)}, u32[]{:S(2)}) collective-permute-start(bf16[16,2304]{1,0:T(8,128)(2,1)S(1)} %fusion.15), channel_id=1, source_target_pairs={{0,8},{1,9},{2,10},{3,11},{4,12},{5,13},{6,14},{7,15},{8,0},{9,1},... | collective-permute-start | bytes 221192 | tf_op jit(solution)/shard_map/ppermute | solution.py:101
  32.5 1.4 %collective-permute-start.14 = (bf16[16,2304]{1,0:T(8,128)(2,1)S(1)}, bf16[16,2304]{1,0:T(8,128)(2,1)S(1)}, u32[]{:S(2)}, u32[]{:S(2)}) collective-permute-start(bf16[16,2304]{1,0:T(8,128)(2,1)S(1)} %get-tuple-element.25), channel_id=1, source_target_pairs={{0,2},{1,3},{2,0},{3,1},{4,6},{5,7},{6,4},{7,5},{8,10},{9,11},{10,... | collective-permute-start | bytes 221192 | tf_op jit(solution)/shard_map/ppermute | solution.py:101
  34.3 1.7 %collective-permute-start.16 = (bf16[16,2304]{1,0:T(8,128)(2,1)S(1)}, bf16[16,2304]{1,0:T(8,128)(2,1)S(1)}, u32[]{:S(2)}, u32[]{:S(2)}) collective-permute-start(bf16[16,2304]{1,0:T(8,128)(2,1)S(1)} %get-tuple-element.27), channel_id=1, source_target_pairs={{0,6},{1,7},{2,4},{3,5},{4,2},{5,3},{6,0},{7,1},{8,14},{9,15},{10,... | collective-permute-start | bytes 221192 | tf_op jit(solution)/shard_map/ppermute | solution.py:101
  36.2 1.4 %collective-permute-done.14 = bf16[16,2304]{1,0:T(8,128)(2,1)S(1)} collective-permute-done((bf16[16,2304]{1,0:T(8,128)(2,1)S(1)}, bf16[16,2304]{1,0:T(8,128)(2,1)S(1)}, u32[]{:S(2)}, u32[]{:S(2)}) %collective-permute-start.14) | collective-permute-done | bytes 73760 | tf_op jit(solution)/shard_map/ppermute | solution.py:101
  38.2 1.3 %collective-permute-done.16 = bf16[16,2304]{1,0:T(8,128)(2,1)S(1)} collective-permute-done((bf16[16,2304]{1,0:T(8,128)(2,1)S(1)}, bf16[16,2304]{1,0:T(8,128)(2,1)S(1)}, u32[]{:S(2)}, u32[]{:S(2)}) %collective-permute-start.16) | collective-permute-done | bytes 73760 | tf_op jit(solution)/shard_map/ppermute | solution.py:101
  39.7 0.8 %collective-permute-start.22 = (bf16[16,2304]{1,0:T(8,128)(2,1)S(1)}, bf16[16,2304]{1,0:T(8,128)(2,1)S(1)}, u32[]{:S(2)}, u32[]{:S(2)}) collective-permute-start(bf16[16,2304]{1,0:T(8,128)(2,1)S(1)} %subtract_convert_fusion.1), channel_id=1, source_target_pairs={{0,8},{1,9},{2,10},{3,11},{4,12},{5,13},{6,14},{7,15},{8,0},{9,1},... | collective-permute-start | bytes 221192 | tf_op jit(solution)/shard_map/ppermute | solution.py:101
  40.5 1.4 %collective-permute-start.21 = (bf16[16,2304]{1,0:T(8,128)(2,1)S(1)}, bf16[16,2304]{1,0:T(8,128)(2,1)S(1)}, u32[]{:S(2)}, u32[]{:S(2)}) collective-permute-start(bf16[16,2304]{1,0:T(8,128)(2,1)S(1)} %subtract_convert_fusion.1), channel_id=1, source_target_pairs={{0,6},{1,7},{2,4},{3,5},{4,2},{5,3},{6,0},{7,1},{8,14},{9,15},{10,... | collective-permute-start | bytes 221192 | tf_op jit(solution)/shard_map/ppermute | solution.py:101
  41.9 0.8 %collective-permute-start.20 = (bf16[16,2304]{1,0:T(8,128)(2,1)S(1)}, bf16[16,2304]{1,0:T(8,128)(2,1)S(1)}, u32[]{:S(2)}, u32[]{:S(2)}) collective-permute-start(bf16[16,2304]{1,0:T(8,128)(2,1)S(1)} %subtract_convert_fusion.1), channel_id=1, source_target_pairs={{0,4},{1,5},{2,6},{3,7},{4,0},{5,1},{6,2},{7,3},{8,12},{9,13},{10,... | collective-permute-start | bytes 221192 | tf_op jit(solution)/shard_map/ppermute | solution.py:101
  42.7 1.3 %collective-permute-start.19 = (bf16[16,2304]{1,0:T(8,128)(2,1)S(1)}, bf16[16,2304]{1,0:T(8,128)(2,1)S(1)}, u32[]{:S(2)}, u32[]{:S(2)}) collective-permute-start(bf16[16,2304]{1,0:T(8,128)(2,1)S(1)} %subtract_convert_fusion.1), channel_id=1, source_target_pairs={{0,2},{1,3},{2,0},{3,1},{4,6},{5,7},{6,4},{7,5},{8,10},{9,11},{10,... | collective-permute-start | bytes 221192 | tf_op jit(solution)/shard_map/ppermute | solution.py:101
  44.0 1.1 %collective-permute-done.22.refs_1_ = bf16[16,2304]{1,0:T(8,128)(2,1)S(1)} collective-permute-done((bf16[16,2304]{1,0:T(8,128)(2,1)S(1)}, bf16[16,2304]{1,0:T(8,128)(2,1)S(1)}, u32[]{:S(2)}, u32[]{:S(2)}) %collective-permute-start.22) | collective-permute-done | bytes 73760 | tf_op jit(solution)/shard_map/ppermute | solution.py:101
  45.1 1.0 %collective-permute-start.23 = (bf16[16,2304]{1,0:T(8,128)(2,1)S(1)}, bf16[16,2304]{1,0:T(8,128)(2,1)S(1)}, u32[]{:S(2)}, u32[]{:S(2)}) collective-permute-start(bf16[16,2304]{1,0:T(8,128)(2,1)S(1)} %collective-permute-done.22.refs_1_), channel_id=1, source_target_pairs={{0,2},{1,3},{2,0},{3,1},{4,6},{5,7},{6,4},{7,5},{8,10},{9,11},{10,... | collective-permute-start | bytes 221192 | tf_op jit(solution)/shard_map/ppermute | solution.py:101
  46.0 1.2 %collective-permute-done.19 = bf16[16,2304]{1,0:T(8,128)(2,1)S(1)} collective-permute-done((bf16[16,2304]{1,0:T(8,128)(2,1)S(1)}, bf16[16,2304]{1,0:T(8,128)(2,1)S(1)}, u32[]{:S(2)}, u32[]{:S(2)}) %collective-permute-start.19) | collective-permute-done | bytes 73760 | tf_op jit(solution)/shard_map/ppermute | solution.py:101
  47.3 1.8 %collective-permute-start.25 = (bf16[16,2304]{1,0:T(8,128)(2,1)S(1)}, bf16[16,2304]{1,0:T(8,128)(2,1)S(1)}, u32[]{:S(2)}, u32[]{:S(2)}) collective-permute-start(bf16[16,2304]{1,0:T(8,128)(2,1)S(1)} %collective-permute-done.22.refs_1_), channel_id=1, source_target_pairs={{0,6},{1,7},{2,4},{3,5},{4,2},{5,3},{6,0},{7,1},{8,14},{9,15},{10,... | collective-permute-start | bytes 221192 | tf_op jit(solution)/shard_map/ppermute | solution.py:101
  49.1 1.3 %collective-permute-start.24 = (bf16[16,2304]{1,0:T(8,128)(2,1)S(1)}, bf16[16,2304]{1,0:T(8,128)(2,1)S(1)}, u32[]{:S(2)}, u32[]{:S(2)}) collective-permute-start(bf16[16,2304]{1,0:T(8,128)(2,1)S(1)} %collective-permute-done.22.refs_1_), channel_id=1, source_target_pairs={{0,4},{1,5},{2,6},{3,7},{4,0},{5,1},{6,2},{7,3},{8,12},{9,13},{10,... | collective-permute-start | bytes 221192 | tf_op jit(solution)/shard_map/ppermute | solution.py:101
  50.4 4.2 %collective-permute-done.24 = bf16[16,2304]{1,0:T(8,128)(2,1)S(1)} collective-permute-done((bf16[16,2304]{1,0:T(8,128)(2,1)S(1)}, bf16[16,2304]{1,0:T(8,128)(2,1)S(1)}, u32[]{:S(2)}, u32[]{:S(2)}) %collective-permute-start.24) | collective-permute-done | bytes 73760 | tf_op jit(solution)/shard_map/ppermute | solution.py:101
  55.4 0.9 %collective-permute-done.27.refs_4_ = bf16[16,2304]{1,0:T(8,128)(2,1)S(1)} collective-permute-done((bf16[16,2304]{1,0:T(8,128)(2,1)S(1)}, bf16[16,2304]{1,0:T(8,128)(2,1)S(1)}, u32[]{:S(2)}, u32[]{:S(2)}) %collective-permute-start.27) | collective-permute-done | bytes 73760 | tf_op jit(solution)/shard_map/ppermute | solution.py:108
  56.3 3.9 %update.1 = (bf16[128,2304]{1,0:T(8,128)(2,1)}, f32[128,2304]{1,0:T(8,128)}, f32[128,2304]{1,0:T(8,128)}, bf16[128,2304]{1,0:T(8,128)(2,1)}, f32[128,2304]{1,0:T(8,128)}, /*index=5*/f32[128,2304]{1,0:T(8,128)}) custom-call(bf16[128,256]{1,0:T(8,128)(2,1)S(1)} %maximum_bitcast_fusion.codes_across, bf16[256,2304]{1,0:T(8,128)(2,1)S(1)} %pad_maximum_fusion.centered, ...), custom_call_target="tpu_custom_call" | custom-call | flops 452984832 | bytes 12976128 | tf_op jit(solution)/shard_map/update/pallas_call | solution.py:74
  (77 shorter events, 5.4 us)
Async XLA Ops:
  0.7 20.3 %copy-start.8 = (f32[2304]{0:T(1024)S(1)}, f32[2304]{0:T(1024)}, u32[]{:S(2)}) copy-start(f32[2304]{0:T(1024)} %param.13) | copy-start | bytes 27652
  0.7 5.8 %collective-permute-start = (f32[128]{0:T(128)}, f32[128]{0:T(128)S(1)}, u32[]{:S(2)}, u32[]{:S(2)}) collective-permute-start(f32[128]{0:T(128)} %param.11), channel_id=1, source_target_pairs={{0,1},{1,0},{2,3},{3,2},{4,5},{5,4},{6,7},{7,6},{8,9},{9,8},{10,11... | collective-permute-start | bytes 1544 | tf_op jit(solution)/shard_map/ppermute | solution.py:108
  1.2 8.4 %collective-permute-start.4 = (bf16[16,2304]{1,0:T(8,128)(2,1)}, bf16[16,2304]{1,0:T(8,128)(2,1)S(1)}, u32[]{:S(2)}, u32[]{:S(2)}) collective-permute-start(bf16[16,2304]{1,0:T(8,128)(2,1)} %param.9), channel_id=1, source_target_pairs={{0,8},{1,9},{2,10},{3,11},{4,12},{5,13},{6,14},{7,15},{8,0},{9,1},... | collective-permute-start | bytes 221192 | tf_op jit(solution)/shard_map/ppermute | solution.py:101
  4.8 16.3 %collective-permute-start.8 = (bf16[128,2304]{1,0:T(8,128)(2,1)}, bf16[128,2304]{1,0:T(8,128)(2,1)S(1)}, u32[]{:S(2)}, u32[]{:S(2)}) collective-permute-start(bf16[128,2304]{1,0:T(8,128)(2,1)} %refs_6_.1), channel_id=1, source_target_pairs={{0,1},{1,0},{2,3},{3,2},{4,5},{5,4},{6,7},{7,6},{8,9},{9,8},{10,11... | collective-permute-start | bytes 1769480 | tf_op jit(solution)/shard_map/ppermute | solution.py:108
  5.0 16.6 %collective-permute-start.9 = (bf16[128,2304]{1,0:T(8,128)(2,1)}, bf16[128,2304]{1,0:T(8,128)(2,1)S(1)}, u32[]{:S(2)}, u32[]{:S(2)}) collective-permute-start(bf16[128,2304]{1,0:T(8,128)(2,1)} %refs_7_.1), channel_id=1, source_target_pairs={{0,1},{1,0},{2,3},{3,2},{4,5},{5,4},{6,7},{7,6},{8,9},{9,8},{10,11... | collective-permute-start | bytes 1769480 | tf_op jit(solution)/shard_map/ppermute | solution.py:108
  6.5 10.0 %collective-permute-start.3 = (bf16[16,2304]{1,0:T(8,128)(2,1)S(1)}, bf16[16,2304]{1,0:T(8,128)(2,1)S(1)}, u32[]{:S(2)}, u32[]{:S(2)}) collective-permute-start(bf16[16,2304]{1,0:T(8,128)(2,1)S(1)} %copy-done.7), channel_id=1, source_target_pairs={{0,6},{1,7},{2,4},{3,5},{4,2},{5,3},{6,0},{7,1},{8,14},{9,15},{10,... | collective-permute-start | bytes 221192 | tf_op jit(solution)/shard_map/ppermute | solution.py:101
  9.1 4.6 %collective-permute-start.1 = (bf16[16,2304]{1,0:T(8,128)(2,1)S(1)}, bf16[16,2304]{1,0:T(8,128)(2,1)S(1)}, u32[]{:S(2)}, u32[]{:S(2)}) collective-permute-start(bf16[16,2304]{1,0:T(8,128)(2,1)S(1)} %copy-done.7), channel_id=1, source_target_pairs={{0,2},{1,3},{2,0},{3,1},{4,6},{5,7},{6,4},{7,5},{8,10},{9,11},{10,... | collective-permute-start | bytes 221192 | tf_op jit(solution)/shard_map/ppermute | solution.py:101
  9.6 5.5 %collective-permute-start.2 = (bf16[16,2304]{1,0:T(8,128)(2,1)S(1)}, bf16[16,2304]{1,0:T(8,128)(2,1)S(1)}, u32[]{:S(2)}, u32[]{:S(2)}) collective-permute-start(bf16[16,2304]{1,0:T(8,128)(2,1)S(1)} %copy-done.7), channel_id=1, source_target_pairs={{0,4},{1,5},{2,6},{3,7},{4,0},{5,1},{6,2},{7,3},{8,12},{9,13},{10,... | collective-permute-start | bytes 221192 | tf_op jit(solution)/shard_map/ppermute | solution.py:101
  13.7 7.2 %collective-permute-start.7 = (bf16[16,2304]{1,0:T(8,128)(2,1)S(1)}, bf16[16,2304]{1,0:T(8,128)(2,1)S(1)}, u32[]{:S(2)}, u32[]{:S(2)}) collective-permute-start(bf16[16,2304]{1,0:T(8,128)(2,1)S(1)} %collective-permute-done.4), channel_id=1, source_target_pairs={{0,6},{1,7},{2,4},{3,5},{4,2},{5,3},{6,0},{7,1},{8,14},{9,15},{10,... | collective-permute-start | bytes 221192 | tf_op jit(solution)/shard_map/ppermute | solution.py:101
  15.1 5.7 %collective-permute-start.6 = (bf16[16,2304]{1,0:T(8,128)(2,1)S(1)}, bf16[16,2304]{1,0:T(8,128)(2,1)S(1)}, u32[]{:S(2)}, u32[]{:S(2)}) collective-permute-start(bf16[16,2304]{1,0:T(8,128)(2,1)S(1)} %collective-permute-done.4), channel_id=1, source_target_pairs={{0,4},{1,5},{2,6},{3,7},{4,0},{5,1},{6,2},{7,3},{8,12},{9,13},{10,... | collective-permute-start | bytes 221192 | tf_op jit(solution)/shard_map/ppermute | solution.py:101
  16.4 4.4 %collective-permute-start.5 = (bf16[16,2304]{1,0:T(8,128)(2,1)S(1)}, bf16[16,2304]{1,0:T(8,128)(2,1)S(1)}, u32[]{:S(2)}, u32[]{:S(2)}) collective-permute-start(bf16[16,2304]{1,0:T(8,128)(2,1)S(1)} %collective-permute-done.4), channel_id=1, source_target_pairs={{0,2},{1,3},{2,0},{3,1},{4,6},{5,7},{6,4},{7,5},{8,10},{9,11},{10,... | collective-permute-start | bytes 221192 | tf_op jit(solution)/shard_map/ppermute | solution.py:101
  21.0 18.6 %collective-permute-start.18 = (bf16[128,2304]{1,0:T(8,128)(2,1)S(1)}, bf16[128,2304]{1,0:T(8,128)(2,1)S(1)}, u32[]{:S(2)}, u32[]{:S(2)}) collective-permute-start(bf16[128,2304]{1,0:T(8,128)(2,1)S(1)} %subtract_convert_fusion), channel_id=1, source_target_pairs={{0,1},{1,0},{2,3},{3,2},{4,5},{5,4},{6,7},{7,6},{8,9},{9,8},{10,11... | collective-permute-start | bytes 1769480 | tf_op jit(solution)/shard_map/ppermute | solution.py:108
  22.5 5.8 %collective-permute-start.10 = (bf16[16,2304]{1,0:T(8,128)(2,1)S(1)}, bf16[16,2304]{1,0:T(8,128)(2,1)S(1)}, u32[]{:S(2)}, u32[]{:S(2)}) collective-permute-start(bf16[16,2304]{1,0:T(8,128)(2,1)S(1)} %get-tuple-element.40), channel_id=1, source_target_pairs={{0,2},{1,3},{2,0},{3,1},{4,6},{5,7},{6,4},{7,5},{8,10},{9,11},{10,... | collective-permute-start | bytes 221192 | tf_op jit(solution)/shard_map/ppermute | solution.py:101
  23.4 5.9 %collective-permute-start.12 = (bf16[16,2304]{1,0:T(8,128)(2,1)S(1)}, bf16[16,2304]{1,0:T(8,128)(2,1)S(1)}, u32[]{:S(2)}, u32[]{:S(2)}) collective-permute-start(bf16[16,2304]{1,0:T(8,128)(2,1)S(1)} %get-tuple-element.41), channel_id=1, source_target_pairs={{0,6},{1,7},{2,4},{3,5},{4,2},{5,3},{6,0},{7,1},{8,14},{9,15},{10,... | collective-permute-start | bytes 221192 | tf_op jit(solution)/shard_map/ppermute | solution.py:101
  24.8 5.2 %collective-permute-start.11 = (bf16[16,2304]{1,0:T(8,128)(2,1)S(1)}, bf16[16,2304]{1,0:T(8,128)(2,1)S(1)}, u32[]{:S(2)}, u32[]{:S(2)}) collective-permute-start(bf16[16,2304]{1,0:T(8,128)(2,1)S(1)} %get-tuple-element.42), channel_id=1, source_target_pairs={{0,4},{1,5},{2,6},{3,7},{4,0},{5,1},{6,2},{7,3},{8,12},{9,13},{10,... | collective-permute-start | bytes 221192 | tf_op jit(solution)/shard_map/ppermute | solution.py:101
  26.0 30.3 %copy-start.4 = (f32[128,2304]{1,0:T(8,128)S(1)}, f32[128,2304]{1,0:T(8,128)}, u32[]{:S(2)}) copy-start(f32[128,2304]{1,0:T(8,128)} %refs_11_.1) | copy-start | bytes 3538948
  30.0 26.3 %copy-start.3 = (f32[128,2304]{1,0:T(8,128)S(1)}, f32[128,2304]{1,0:T(8,128)}, u32[]{:S(2)}) copy-start(f32[128,2304]{1,0:T(8,128)} %refs_10_.1) | copy-start | bytes 3538948
  30.0 6.2 %collective-permute-start.13 = (bf16[16,2304]{1,0:T(8,128)(2,1)S(1)}, bf16[16,2304]{1,0:T(8,128)(2,1)S(1)}, u32[]{:S(2)}, u32[]{:S(2)}) collective-permute-start(bf16[16,2304]{1,0:T(8,128)(2,1)S(1)} %fusion.15), channel_id=1, source_target_pairs={{0,8},{1,9},{2,10},{3,11},{4,12},{5,13},{6,14},{7,15},{8,0},{9,1},... | collective-permute-start | bytes 221192 | tf_op jit(solution)/shard_map/ppermute | solution.py:101
  32.5 5.1 %collective-permute-start.14 = (bf16[16,2304]{1,0:T(8,128)(2,1)S(1)}, bf16[16,2304]{1,0:T(8,128)(2,1)S(1)}, u32[]{:S(2)}, u32[]{:S(2)}) collective-permute-start(bf16[16,2304]{1,0:T(8,128)(2,1)S(1)} %get-tuple-element.25), channel_id=1, source_target_pairs={{0,2},{1,3},{2,0},{3,1},{4,6},{5,7},{6,4},{7,5},{8,10},{9,11},{10,... | collective-permute-start | bytes 221192 | tf_op jit(solution)/shard_map/ppermute | solution.py:101
  33.9 4.4 %collective-permute-start.15 = (bf16[16,2304]{1,0:T(8,128)(2,1)S(1)}, bf16[16,2304]{1,0:T(8,128)(2,1)S(1)}, u32[]{:S(2)}, u32[]{:S(2)}) collective-permute-start(bf16[16,2304]{1,0:T(8,128)(2,1)S(1)} %get-tuple-element.26), channel_id=1, source_target_pairs={{0,4},{1,5},{2,6},{3,7},{4,0},{5,1},{6,2},{7,3},{8,12},{9,13},{10,... | collective-permute-start | bytes 221192 | tf_op jit(solution)/shard_map/ppermute | solution.py:101
  34.3 5.3 %collective-permute-start.16 = (bf16[16,2304]{1,0:T(8,128)(2,1)S(1)}, bf16[16,2304]{1,0:T(8,128)(2,1)S(1)}, u32[]{:S(2)}, u32[]{:S(2)}) collective-permute-start(bf16[16,2304]{1,0:T(8,128)(2,1)S(1)} %get-tuple-element.27), channel_id=1, source_target_pairs={{0,6},{1,7},{2,4},{3,5},{4,2},{5,3},{6,0},{7,1},{8,14},{9,15},{10,... | collective-permute-start | bytes 221192 | tf_op jit(solution)/shard_map/ppermute | solution.py:101
  36.2 3.4 %collective-permute-start.17 = (bf16[128,128]{0,1:T(8,128)(2,1)S(1)}, bf16[128,128]{0,1:T(8,128)(2,1)S(1)}, u32[]{:S(2)}, u32[]{:S(2)}) collective-permute-start(bf16[128,128]{0,1:T(8,128)(2,1)S(1)} %get-tuple-element.44), channel_id=1, source_target_pairs={{0,1},{1,0},{2,3},{3,2},{4,5},{5,4},{6,7},{7,6},{8,9},{9,8},{10,11... | collective-permute-start | bytes 98312 | tf_op jit(solution)/shard_map/ppermute | solution.py:108
  39.7 5.4 %collective-permute-start.22 = (bf16[16,2304]{1,0:T(8,128)(2,1)S(1)}, bf16[16,2304]{1,0:T(8,128)(2,1)S(1)}, u32[]{:S(2)}, u32[]{:S(2)}) collective-permute-start(bf16[16,2304]{1,0:T(8,128)(2,1)S(1)} %subtract_convert_fusion.1), channel_id=1, source_target_pairs={{0,8},{1,9},{2,10},{3,11},{4,12},{5,13},{6,14},{7,15},{8,0},{9,1},... | collective-permute-start | bytes 221192 | tf_op jit(solution)/shard_map/ppermute | solution.py:101
  40.5 6.7 %collective-permute-start.21 = (bf16[16,2304]{1,0:T(8,128)(2,1)S(1)}, bf16[16,2304]{1,0:T(8,128)(2,1)S(1)}, u32[]{:S(2)}, u32[]{:S(2)}) collective-permute-start(bf16[16,2304]{1,0:T(8,128)(2,1)S(1)} %subtract_convert_fusion.1), channel_id=1, source_target_pairs={{0,6},{1,7},{2,4},{3,5},{4,2},{5,3},{6,0},{7,1},{8,14},{9,15},{10,... | collective-permute-start | bytes 221192 | tf_op jit(solution)/shard_map/ppermute | solution.py:101
  41.9 5.3 %collective-permute-start.20 = (bf16[16,2304]{1,0:T(8,128)(2,1)S(1)}, bf16[16,2304]{1,0:T(8,128)(2,1)S(1)}, u32[]{:S(2)}, u32[]{:S(2)}) collective-permute-start(bf16[16,2304]{1,0:T(8,128)(2,1)S(1)} %subtract_convert_fusion.1), channel_id=1, source_target_pairs={{0,4},{1,5},{2,6},{3,7},{4,0},{5,1},{6,2},{7,3},{8,12},{9,13},{10,... | collective-permute-start | bytes 221192 | tf_op jit(solution)/shard_map/ppermute | solution.py:101
  42.7 4.4 %collective-permute-start.19 = (bf16[16,2304]{1,0:T(8,128)(2,1)S(1)}, bf16[16,2304]{1,0:T(8,128)(2,1)S(1)}, u32[]{:S(2)}, u32[]{:S(2)}) collective-permute-start(bf16[16,2304]{1,0:T(8,128)(2,1)S(1)} %subtract_convert_fusion.1), channel_id=1, source_target_pairs={{0,2},{1,3},{2,0},{3,1},{4,6},{5,7},{6,4},{7,5},{8,10},{9,11},{10,... | collective-permute-start | bytes 221192 | tf_op jit(solution)/shard_map/ppermute | solution.py:101
  45.1 5.4 %collective-permute-start.23 = (bf16[16,2304]{1,0:T(8,128)(2,1)S(1)}, bf16[16,2304]{1,0:T(8,128)(2,1)S(1)}, u32[]{:S(2)}, u32[]{:S(2)}) collective-permute-start(bf16[16,2304]{1,0:T(8,128)(2,1)S(1)} %collective-permute-done.22.refs_1_), channel_id=1, source_target_pairs={{0,2},{1,3},{2,0},{3,1},{4,6},{5,7},{6,4},{7,5},{8,10},{9,11},{10,... | collective-permute-start | bytes 221192 | tf_op jit(solution)/shard_map/ppermute | solution.py:101
  47.2 9.1 %collective-permute-start.26 = (bf16[64,2304]{1,0:T(8,128)(2,1)S(1)}, bf16[64,2304]{1,0:T(8,128)(2,1)S(1)}, u32[]{:S(2)}, u32[]{:S(2)}) collective-permute-start(bf16[64,2304]{1,0:T(8,128)(2,1)S(1)} %constant_dynamic-update-slice_fusion.10.refs_0_), channel_id=1, source_target_pairs={{0,1},{1,0},{2,3},{3,2},{4,5},{5,4},{6,7},{7,6},{8,9},{9,8},{10,11... | collective-permute-start | bytes 884744 | tf_op jit(solution)/shard_map/ppermute | solution.py:108
  47.3 7.3 %collective-permute-start.25 = (bf16[16,2304]{1,0:T(8,128)(2,1)S(1)}, bf16[16,2304]{1,0:T(8,128)(2,1)S(1)}, u32[]{:S(2)}, u32[]{:S(2)}) collective-permute-start(bf16[16,2304]{1,0:T(8,128)(2,1)S(1)} %collective-permute-done.22.refs_1_), channel_id=1, source_target_pairs={{0,6},{1,7},{2,4},{3,5},{4,2},{5,3},{6,0},{7,1},{8,14},{9,15},{10,... | collective-permute-start | bytes 221192 | tf_op jit(solution)/shard_map/ppermute | solution.py:101
  49.1 5.5 %collective-permute-start.24 = (bf16[16,2304]{1,0:T(8,128)(2,1)S(1)}, bf16[16,2304]{1,0:T(8,128)(2,1)S(1)}, u32[]{:S(2)}, u32[]{:S(2)}) collective-permute-start(bf16[16,2304]{1,0:T(8,128)(2,1)S(1)} %collective-permute-done.22.refs_1_), channel_id=1, source_target_pairs={{0,4},{1,5},{2,6},{3,7},{4,0},{5,1},{6,2},{7,3},{8,12},{9,13},{10,... | collective-permute-start | bytes 221192 | tf_op jit(solution)/shard_map/ppermute | solution.py:101
  54.6 1.7 %collective-permute-start.28 = (bf16[48,2304]{1,0:T(8,128)(2,1)S(1)}, bf16[48,2304]{1,0:T(8,128)(2,1)S(1)}, u32[]{:S(2)}, u32[]{:S(2)}) collective-permute-start(bf16[48,2304]{1,0:T(8,128)(2,1)S(1)} %constant_dynamic-update-slice_fusion.14.refs_2_), channel_id=1, source_target_pairs={{0,1},{1,0},{2,3},{3,2},{4,5},{5,4},{6,7},{7,6},{8,9},{9,8},{10,11... | collective-permute-start | bytes 663560 | tf_op jit(solution)/shard_map/ppermute | solution.py:108
  54.8 1.5 %collective-permute-start.27 = (bf16[16,2304]{1,0:T(8,128)(2,1)S(1)}, bf16[16,2304]{1,0:T(8,128)(2,1)S(1)}, u32[]{:S(2)}, u32[]{:S(2)}) collective-permute-start(bf16[16,2304]{1,0:T(8,128)(2,1)S(1)} %collective-permute-done.22.refs_1_), channel_id=1, source_target_pairs={{0,1},{1,0},{2,3},{3,2},{4,5},{5,4},{6,7},{7,6},{8,9},{9,8},{10,11... | collective-permute-start | bytes 221192 | tf_op jit(solution)/shard_map/ppermute | solution.py:108
  (7 other events, 57.2 us)

commit v8 on v5

--- a/solution.py
+++ b/solution.py
@@ -19,7 +19,7 @@
     )
 
 
-def update_kernel(columns, rows_total, codes_across, centered, *refs):
+def update_kernel(columns, block, rows_total, codes_across, centered, *refs):
     blocks = len(refs) - 20
     errors, (encoder, decoder) = refs[:blocks], refs[blocks : blocks + 2]
     moments = refs[blocks + 2 : blocks + 6]
@@ -33,18 +33,16 @@
 
     start = 0
     for one in errors:
-        error_all[pl.ds(start, one.shape[0]), :] = one[...]
-        start += one.shape[0]
-    codes_t = codes_across[...]
-    signal = inner_last(decoder[...], error_all[...])
-    delta_t = jnp.where(codes_t.astype(jnp.float32) > 0, signal, 0.0).astype(jnp.bfloat16)
+        for first in (0, block):
+            for at in range(first, one.shape[0], 2 * block):
+                error_all[pl.ds(start, block), :] = one[pl.ds(at, block), :]
+                start += block
     first = (1.0 - beta_first) / rows_total
     second = (1.0 - beta_second) / (rows_total * rows_total)
-    for t in range(tiles):
-        at = pl.ds(t * columns, columns)
-        for which, (left, right, weight) in enumerate(
-            ((delta_t, centered, encoder), (codes_t, error_all, decoder))
-        ):
+
+    def advance(which, left, right, weight):
+        for t in range(tiles):
+            at = pl.ds(t * columns, columns)
             total = jnp.dot(left, right[:, at], preferred_element_type=jnp.float32)
             moment = beta_first * moments[2 * which][:, at] + first * total
             square = beta_second * moments[2 * which + 1][:, at] + second * (total * total)
@@ -57,12 +55,18 @@
             held[3 * which + 2][:, at] = square
             for i in range(3 * which, 3 * which + 3):
                 write(t, i).start()
+
+    codes_t = codes_across[...]
+    advance(1, codes_t, error_all, decoder)
+    signal = inner_last(decoder[...], error_all[...])
+    delta_t = jnp.where(codes_t.astype(jnp.float32) > 0, signal, 0.0).astype(jnp.bfloat16)
+    advance(0, delta_t, centered, encoder)
     for t in range(tiles):
         for i in range(6):
             write(t, i).wait()
 
 
-def update(total_rows, codes_across, centered, errors, weights, moments):
+def update(total_rows, codes_across, centered, errors, block, weights, moments):
     latents, width = weights[0].shape
     rows = centered.shape[0]
     columns = next(c for c in (256, 128, width) if width % c == 0)
@@ -72,7 +76,7 @@
     wide = pltpu.VMEM((latents, width), jnp.float32)
     narrow = pltpu.VMEM((latents, width), jnp.bfloat16)
     return pl.pallas_call(
-        functools.partial(update_kernel, columns, float(total_rows)),
+        functools.partial(update_kernel, columns, block, float(total_rows)),
         out_shape=(half, full, full, half, full, full),
         in_specs=[vmem] * (len(errors) + 8),
         out_specs=[pl.BlockSpec(memory_space=pl.ANY)] * 6,
@@ -109,11 +113,8 @@
 
 
 def gather_chips(block, chips):
-    near = [block, to_chip(block, 2)]
-    far = [to_chip(block, k) for k in range(4, chips, 2)]
-    near = jnp.concatenate(near, 0)
-    far = jnp.concatenate(far, 0)
-    return [near, far, to_chip(near, 1), to_chip(far, 1)]
+    even = [block] + [to_chip(block, k) for k in range(2, chips, 2)]
+    return even, [to_chip(one, 1) for one in even]
 
 
 def body(
@@ -134,7 +135,8 @@
     pairs = chips // 2
     total_rows = rows_here * size
 
-    rows_core = jnp.concatenate(gather_chips(activations, chips), 0)
+    even, odd = gather_chips(activations, chips)
+    rows_core = jnp.concatenate(even + odd, 0)
     encoder_both = jnp.concatenate([encoder, to_other_core(encoder)], 0)
     decoder_both = jnp.concatenate([decoder, to_other_core(decoder)], 0)
     bias_both = jnp.concatenate([encoder_bias, to_other_core(encoder_bias)], 0)
@@ -156,8 +158,8 @@
             codes[first:last], decoder_both, preferred_element_type=jnp.float32
         ) + to_chip(given[first:last], 1).astype(jnp.float32)
 
+    far = pair_sums(split, pairs * rows_here).astype(jnp.bfloat16)
     near = pair_sums(0, split)
-    far = pair_sums(split, pairs * rows_here).astype(jnp.bfloat16)
     summed = near[:rows_here] + to_chip(near[rows_here:].astype(jnp.bfloat16), 2).astype(
         jnp.float32
     )
@@ -166,7 +168,11 @@
         summed = summed + to_chip(block, 2 * k).astype(jnp.float32)
     row_error = (summed - centered[:rows_here].astype(jnp.float32)).astype(jnp.bfloat16)
 
-    errors = gather_chips(row_error, chips)
+    row_error, other_codes, other_centered = lax.optimization_barrier(
+        (row_error, other_codes, other_centered)
+    )
+    even, odd = gather_chips(row_error, chips)
+    errors = jnp.concatenate([one for both in zip(even, odd) for one in both], 0)
     codes_across = jnp.concatenate([codes[:, :latents_here], other_codes], 0).T
     centered_all = jnp.concatenate([centered, other_centered], 0)
     (
@@ -180,7 +186,8 @@
         total_rows,
         codes_across,
         centered_all,
-        errors + [to_other_core(one) for one in errors],
+        (errors, to_other_core(errors)),
+        rows_here,
         (encoder, decoder),
         (encoder_moment, encoder_square, decoder_moment, decoder_square),
     )

time: 58.3 us -> 55.1 us (0.945)
  waiting for transfers between devices: 28 us -> 19.9 us
  starting transfers between devices: 22 us -> 27.5 us
    ppermute x15 -> x19, waiting for transfers between devices: 25.5 us -> 17.9 us  [to_chip(): lax.ppermute(block, 'latent', [(i, i ^ 2 * distance) for i in range(size)])]
    ppermute x15 -> x19, starting transfers between devices: 20.7 us -> 26.8 us  [to_chip(): lax.ppermute(block, 'latent', [(i, i ^ 2 * distance) for i in range(size)])]
    ppermute x9 -> x6, starting transfers between devices: 1.33 us -> 0.65 us  [to_other_core(): return lax.ppermute(block, 'latent', [(i, i ^ 1) for i in range(size)])]
    ppermute x9 -> x6, waiting for transfers between devices: 2.46 us -> 1.98 us  [to_other_core(): return lax.ppermute(block, 'latent', [(i, i ^ 1) for i in range(size)])]
    unnamed x27 -> x35, local copies, waits for them, and re-layouts: 1.19 us -> 1.24 us
  transfers between devices with their start and end apart: 24 -> 25, of which waited for: 13 -> 9; matrix products, arithmetic and copies ran while one was open for 4% -> 4% of each run, Pallas kernels for 0% -> 0%
where the time goes in v8:
time: 55.1 us; the launch traced here: 55 us
  starting transfers between devices  27.5 us (50%)
  waiting for transfers between devices  19.9 us (36%)
  Pallas kernels  3.38 us (6%)
  matrix products  1.68 us (3%)
  local copies, waits for them, and re-layouts  1.35 us (2%)
  between operations  1 us (2%)
    ppermute x19, starting transfers between devices, to_chip(): lax.ppermute(block, 'latent', [(i, i ^ 2 * distance) for i in range(size)])  26.8 us
    ppermute x19, waiting for transfers between devices, to_chip(): lax.ppermute(block, 'latent', [(i, i ^ 2 * distance) for i in range(size)])  17.9 us
    pallas_call x1, Pallas kernels, update(): pl.pallas_call(functools.partial(update_kernel, columns, block, float(tot...  3.38 us
    ppermute x6, waiting for transfers between devices, to_other_core(): return lax.ppermute(block, 'latent', [(i, i ^ 1) for i in range(size)])  1.98 us
    unnamed x35, local copies, waits for them, and re-layouts  1.24 us
  transfers between devices with their start and end apart: 25, of which 9 were waited for; matrix products, arithmetic and copies ran while one was open for 4% of the time, Pallas kernels for 0%

profile of v8, /device:TPU:0, one launch (start us, length us, event | category | flops | bytes accessed | tf_op | source)
XLA Modules:
  0.0 55.0 jit_solution(12024279959273101071)
XLA Ops:
  0.7 5.1 %collective-permute-start.2 = (bf16[16,2304]{1,0:T(8,128)(2,1)}, bf16[16,2304]{1,0:T(8,128)(2,1)S(1)}, u32[]{:S(2)}, u32[]{:S(2)}) collective-permute-start(bf16[16,2304]{1,0:T(8,128)(2,1)} %param.9), channel_id=1, source_target_pairs={{0,12},{1,13},{2,14},{3,15},{4,8},{5,9},{6,10},{7,11},{8,4},{9,5},... | collective-permute-start | bytes 221192 | tf_op jit(solution)/shard_map/ppermute | solution.py:105
  5.8 0.6 %collective-permute-start = (bf16[16,2304]{1,0:T(8,128)(2,1)}, bf16[16,2304]{1,0:T(8,128)(2,1)S(1)}, u32[]{:S(2)}, u32[]{:S(2)}) collective-permute-start(bf16[16,2304]{1,0:T(8,128)(2,1)} %param.9), channel_id=1, source_target_pairs={{0,4},{1,5},{2,6},{3,7},{4,0},{5,1},{6,2},{7,3},{8,12},{9,13},{10,... | collective-permute-start | bytes 221192 | tf_op jit(solution)/shard_map/ppermute | solution.py:105
  6.4 1.7 %collective-permute-start.3 = (bf16[16,2304]{1,0:T(8,128)(2,1)}, bf16[16,2304]{1,0:T(8,128)(2,1)S(1)}, u32[]{:S(2)}, u32[]{:S(2)}) collective-permute-start(bf16[16,2304]{1,0:T(8,128)(2,1)} %param.9), channel_id=1, source_target_pairs={{0,2},{1,3},{2,0},{3,1},{4,6},{5,7},{6,4},{7,5},{8,10},{9,11},{10,... | collective-permute-start | bytes 221192 | tf_op jit(solution)/shard_map/ppermute | solution.py:105
  8.1 1.1 %constant_dynamic-update-slice_fusion.9 = bf16[256,2304]{1,0:T(8,128)(2,1)S(1)} fusion(bf16[128,2304]{1,0:T(8,128)(2,1)} %refs_3_.1), kind=kLoop, calls=%fused_computation.32 | loop fusion | bytes 1179648
  9.4 0.5 collective-permute-start.9
  10.0 2.3 %collective-permute-done.1 = bf16[16,2304]{1,0:T(8,128)(2,1)S(1)} collective-permute-done((bf16[16,2304]{1,0:T(8,128)(2,1)}, bf16[16,2304]{1,0:T(8,128)(2,1)S(1)}, u32[]{:S(2)}, u32[]{:S(2)}) %collective-permute-start.1) | collective-permute-done | bytes 73760 | tf_op jit(solution)/shard_map/ppermute | solution.py:105
  12.2 1.5 %collective-permute-start.6 = (bf16[16,2304]{1,0:T(8,128)(2,1)S(1)}, bf16[16,2304]{1,0:T(8,128)(2,1)S(1)}, u32[]{:S(2)}, u32[]{:S(2)}) collective-permute-start(bf16[16,2304]{1,0:T(8,128)(2,1)S(1)} %collective-permute-done.2), channel_id=1, source_target_pairs={{0,2},{1,3},{2,0},{3,1},{4,6},{5,7},{6,4},{7,5},{8,10},{9,11},{10,... | collective-permute-start | bytes 221192 | tf_op jit(solution)/shard_map/ppermute | solution.py:105
  13.7 0.5 collective-permute-start.5
  14.3 1.6 %collective-permute-start.4 = (bf16[16,2304]{1,0:T(8,128)(2,1)S(1)}, bf16[16,2304]{1,0:T(8,128)(2,1)S(1)}, u32[]{:S(2)}, u32[]{:S(2)}) collective-permute-start(bf16[16,2304]{1,0:T(8,128)(2,1)S(1)} %collective-permute-done), channel_id=1, source_target_pairs={{0,2},{1,3},{2,0},{3,1},{4,6},{5,7},{6,4},{7,5},{8,10},{9,11},{10,... | collective-permute-start | bytes 221192 | tf_op jit(solution)/shard_map/ppermute | solution.py:105
  15.9 3.8 %collective-permute-done.4 = bf16[16,2304]{1,0:T(8,128)(2,1)S(1)} collective-permute-done((bf16[16,2304]{1,0:T(8,128)(2,1)S(1)}, bf16[16,2304]{1,0:T(8,128)(2,1)S(1)}, u32[]{:S(2)}, u32[]{:S(2)}) %collective-permute-start.4) | collective-permute-done | bytes 73760 | tf_op jit(solution)/shard_map/ppermute | solution.py:105
  19.9 0.5 fusion.11
  20.4 0.4 convolution_convert_fusion
  20.9 1.1 %collective-permute-start.12 = (bf16[32,2304]{1,0:T(8,128)(2,1)S(1)}, bf16[32,2304]{1,0:T(8,128)(2,1)S(1)}, u32[]{:S(2)}, u32[]{:S(2)}) collective-permute-start(bf16[32,2304]{1,0:T(8,128)(2,1)S(1)} %get-tuple-element.25), channel_id=1, source_target_pairs={{0,2},{1,3},{2,0},{3,1},{4,6},{5,7},{6,4},{7,5},{8,10},{9,11},{10,... | collective-permute-start | bytes 442376 | tf_op jit(solution)/shard_map/ppermute | solution.py:105
  22.0 1.0 %collective-permute-start.10 = (bf16[32,2304]{1,0:T(8,128)(2,1)S(1)}, bf16[32,2304]{1,0:T(8,128)(2,1)S(1)}, u32[]{:S(2)}, u32[]{:S(2)}) collective-permute-start(bf16[32,2304]{1,0:T(8,128)(2,1)S(1)} %get-tuple-element.26), channel_id=1, source_target_pairs={{0,2},{1,3},{2,0},{3,1},{4,6},{5,7},{6,4},{7,5},{8,10},{9,11},{10,... | collective-permute-start | bytes 442376 | tf_op jit(solution)/shard_map/ppermute | solution.py:105
  22.9 4.1 %collective-permute-done.12 = bf16[32,2304]{1,0:T(8,128)(2,1)S(1)} collective-permute-done((bf16[32,2304]{1,0:T(8,128)(2,1)S(1)}, bf16[32,2304]{1,0:T(8,128)(2,1)S(1)}, u32[]{:S(2)}, u32[]{:S(2)}) %collective-permute-start.12) | collective-permute-done | bytes 147488 | tf_op jit(solution)/shard_map/ppermute | solution.py:105
  27.1 0.4 fusion
  27.5 0.9 %collective-permute-start.13 = (bf16[16,2304]{1,0:T(8,128)(2,1)S(1)}, bf16[16,2304]{1,0:T(8,128)(2,1)S(1)}, u32[]{:S(2)}, u32[]{:S(2)}) collective-permute-start(bf16[16,2304]{1,0:T(8,128)(2,1)S(1)} %get-tuple-element.27), channel_id=1, source_target_pairs={{0,8},{1,9},{2,10},{3,11},{4,12},{5,13},{6,14},{7,15},{8,0},{9,1},... | collective-permute-start | bytes 221192 | tf_op jit(solution)/shard_map/ppermute | solution.py:105
  28.4 1.4 %collective-permute-start.14 = (bf16[16,2304]{1,0:T(8,128)(2,1)S(1)}, bf16[16,2304]{1,0:T(8,128)(2,1)S(1)}, u32[]{:S(2)}, u32[]{:S(2)}) collective-permute-start(bf16[16,2304]{1,0:T(8,128)(2,1)S(1)} %get-tuple-element.28), channel_id=1, source_target_pairs={{0,12},{1,13},{2,14},{3,15},{4,8},{5,9},{6,10},{7,11},{8,4},{9,5},... | collective-permute-start | bytes 221192 | tf_op jit(solution)/shard_map/ppermute | solution.py:105
  29.8 0.3 convolution_add_fusion.1
  30.2 1.4 %collective-permute-start.11 = (bf16[16,2304]{1,0:T(8,128)(2,1)S(1)}, bf16[16,2304]{1,0:T(8,128)(2,1)S(1)}, u32[]{:S(2)}, u32[]{:S(2)}) collective-permute-start(bf16[16,2304]{1,0:T(8,128)(2,1)S(1)} %slice.78), channel_id=1, source_target_pairs={{0,4},{1,5},{2,6},{3,7},{4,0},{5,1},{6,2},{7,3},{8,12},{9,13},{10,... | collective-permute-start | bytes 221192 | tf_op jit(solution)/shard_map/ppermute | solution.py:105
  31.5 1.4 %collective-permute-done.13 = bf16[16,2304]{1,0:T(8,128)(2,1)S(1)} collective-permute-done((bf16[16,2304]{1,0:T(8,128)(2,1)S(1)}, bf16[16,2304]{1,0:T(8,128)(2,1)S(1)}, u32[]{:S(2)}, u32[]{:S(2)}) %collective-permute-start.13) | collective-permute-done | bytes 73760 | tf_op jit(solution)/shard_map/ppermute | solution.py:105
  32.9 1.7 %collective-permute-done.14 = bf16[16,2304]{1,0:T(8,128)(2,1)S(1)} collective-permute-done((bf16[16,2304]{1,0:T(8,128)(2,1)S(1)}, bf16[16,2304]{1,0:T(8,128)(2,1)S(1)}, u32[]{:S(2)}, u32[]{:S(2)}) %collective-permute-start.14) | collective-permute-done | bytes 73760 | tf_op jit(solution)/shard_map/ppermute | solution.py:105
  34.6 0.7 %collective-permute-done.11 = bf16[16,2304]{1,0:T(8,128)(2,1)S(1)} collective-permute-done((bf16[16,2304]{1,0:T(8,128)(2,1)S(1)}, bf16[16,2304]{1,0:T(8,128)(2,1)S(1)}, u32[]{:S(2)}, u32[]{:S(2)}) %collective-permute-start.11) | collective-permute-done | bytes 73760 | tf_op jit(solution)/shard_map/ppermute | solution.py:105
  35.4 1.7 %collective-permute-start.22 = (bf16[16,2304]{1,0:T(8,128)(2,1)S(1)}, bf16[16,2304]{1,0:T(8,128)(2,1)S(1)}, u32[]{:S(2)}, u32[]{:S(2)}) collective-permute-start(bf16[16,2304]{1,0:T(8,128)(2,1)S(1)} %fusion.17), channel_id=1, source_target_pairs={{0,12},{1,13},{2,14},{3,15},{4,8},{5,9},{6,10},{7,11},{8,4},{9,5},... | collective-permute-start | bytes 221192 | tf_op jit(solution)/shard_map/ppermute | solution.py:105
  37.5 2.4 %collective-permute-start.18 = (bf16[16,2304]{1,0:T(8,128)(2,1)S(1)}, bf16[16,2304]{1,0:T(8,128)(2,1)S(1)}, u32[]{:S(2)}, u32[]{:S(2)}) collective-permute-start(bf16[16,2304]{1,0:T(8,128)(2,1)S(1)} %fusion.17), channel_id=1, source_target_pairs={{0,4},{1,5},{2,6},{3,7},{4,0},{5,1},{6,2},{7,3},{8,12},{9,13},{10,... | collective-permute-start | bytes 221192 | tf_op jit(solution)/shard_map/ppermute | solution.py:105
  39.9 1.8 %collective-permute-start.17 = (bf16[16,2304]{1,0:T(8,128)(2,1)S(1)}, bf16[16,2304]{1,0:T(8,128)(2,1)S(1)}, u32[]{:S(2)}, u32[]{:S(2)}) collective-permute-start(bf16[16,2304]{1,0:T(8,128)(2,1)S(1)} %fusion.17), channel_id=1, source_target_pairs={{0,2},{1,3},{2,0},{3,1},{4,6},{5,7},{6,4},{7,5},{8,10},{9,11},{10,... | collective-permute-start | bytes 221192 | tf_op jit(solution)/shard_map/ppermute | solution.py:105
  41.7 1.8 %collective-permute-start.23 = (bf16[16,2304]{1,0:T(8,128)(2,1)S(1)}, bf16[16,2304]{1,0:T(8,128)(2,1)S(1)}, u32[]{:S(2)}, u32[]{:S(2)}) collective-permute-start(bf16[16,2304]{1,0:T(8,128)(2,1)S(1)} %collective-permute-done.22), channel_id=1, source_target_pairs={{0,2},{1,3},{2,0},{3,1},{4,6},{5,7},{6,4},{7,5},{8,10},{9,11},{10,... | collective-permute-start | bytes 221192 | tf_op jit(solution)/shard_map/ppermute | solution.py:105
  43.5 1.6 %collective-permute-start.21 = (bf16[16,2304]{1,0:T(8,128)(2,1)S(1)}, bf16[16,2304]{1,0:T(8,128)(2,1)S(1)}, u32[]{:S(2)}, u32[]{:S(2)}) collective-permute-start(bf16[16,2304]{1,0:T(8,128)(2,1)S(1)} %collective-permute-done.20), channel_id=1, source_target_pairs={{0,2},{1,3},{2,0},{3,1},{4,6},{5,7},{6,4},{7,5},{8,10},{9,11},{10,... | collective-permute-start | bytes 221192 | tf_op jit(solution)/shard_map/ppermute | solution.py:105
  45.1 0.5 collective-permute-start.19
  45.6 3.9 %collective-permute-done.19 = bf16[16,2304]{1,0:T(8,128)(2,1)S(1)} collective-permute-done((bf16[16,2304]{1,0:T(8,128)(2,1)S(1)}, bf16[16,2304]{1,0:T(8,128)(2,1)S(1)}, u32[]{:S(2)}, u32[]{:S(2)}) %collective-permute-start.19) | collective-permute-done | bytes 73760 | tf_op jit(solution)/shard_map/ppermute | solution.py:105
  49.7 1.9 %collective-permute-done.24.refs_1_ = bf16[128,2304]{1,0:T(8,128)(2,1)S(1)} collective-permute-done((bf16[128,2304]{1,0:T(8,128)(2,1)S(1)}, bf16[128,2304]{1,0:T(8,128)(2,1)S(1)}, u32[]{:S(2)}, u32[]{:S(2)}) %collective-permute-start.24) | collective-permute-done | bytes 589856 | tf_op jit(solution)/shard_map/ppermute | solution.py:112
  51.6 3.4 %update.1 = (bf16[128,2304]{1,0:T(8,128)(2,1)}, f32[128,2304]{1,0:T(8,128)}, f32[128,2304]{1,0:T(8,128)}, bf16[128,2304]{1,0:T(8,128)(2,1)}, f32[128,2304]{1,0:T(8,128)}, /*index=5*/f32[128,2304]{1,0:T(8,128)}) custom-call(bf16[128,256]{1,0:T(8,128)(2,1)S(1)} %maximum_bitcast_fusion.codes_across, bf16[256,2304]{1,0:T(8,128)(2,1)S(1)} %pad_maximum_fusion.centered, ...), custom_call_target="tpu_custom_call" | custom-call | flops 452984832 | bytes 12976128 | tf_op jit(solution)/shard_map/update/pallas_call | solution.py:78
  (70 shorter events, 1.2 us)
Async XLA Ops:
  0.6 9.2 %copy-start.9 = (f32[128]{0:T(128)S(1)}, f32[128]{0:T(128)}, u32[]{:S(2)}) copy-start(f32[128]{0:T(128)} %param.11) | copy-start | bytes 1540
  0.7 8.7 %copy-start = (bf16[128,2304]{1,0:T(8,128)(2,1)S(1)}, bf16[128,2304]{1,0:T(8,128)(2,1)}, u32[]{:S(2)}) copy-start(bf16[128,2304]{1,0:T(8,128)(2,1)} %refs_3_.1) | copy-start | bytes 1769476
  0.7 9.2 %copy-start.5 = (bf16[128,2304]{1,0:T(8,128)(2,1)S(1)}, bf16[128,2304]{1,0:T(8,128)(2,1)}, u32[]{:S(2)}) copy-start(bf16[128,2304]{1,0:T(8,128)(2,1)} %refs_2_.1) | copy-start | bytes 1769476
  0.7 19.1 %copy-start.8 = (f32[2304]{0:T(1024)S(1)}, f32[2304]{0:T(1024)}, u32[]{:S(2)}) copy-start(f32[2304]{0:T(1024)} %param.13) | copy-start | bytes 27652
  0.7 9.2 %collective-permute-start.2 = (bf16[16,2304]{1,0:T(8,128)(2,1)}, bf16[16,2304]{1,0:T(8,128)(2,1)S(1)}, u32[]{:S(2)}, u32[]{:S(2)}) collective-permute-start(bf16[16,2304]{1,0:T(8,128)(2,1)} %param.9), channel_id=1, source_target_pairs={{0,12},{1,13},{2,14},{3,15},{4,8},{5,9},{6,10},{7,11},{8,4},{9,5},... | collective-permute-start | bytes 221192 | tf_op jit(solution)/shard_map/ppermute | solution.py:105
  5.8 6.4 %collective-permute-start.1 = (bf16[16,2304]{1,0:T(8,128)(2,1)}, bf16[16,2304]{1,0:T(8,128)(2,1)S(1)}, u32[]{:S(2)}, u32[]{:S(2)}) collective-permute-start(bf16[16,2304]{1,0:T(8,128)(2,1)} %param.9), channel_id=1, source_target_pairs={{0,8},{1,9},{2,10},{3,11},{4,12},{5,13},{6,14},{7,15},{8,0},{9,1},... | collective-permute-start | bytes 221192 | tf_op jit(solution)/shard_map/ppermute | solution.py:105
  5.8 7.9 %collective-permute-start = (bf16[16,2304]{1,0:T(8,128)(2,1)}, bf16[16,2304]{1,0:T(8,128)(2,1)S(1)}, u32[]{:S(2)}, u32[]{:S(2)}) collective-permute-start(bf16[16,2304]{1,0:T(8,128)(2,1)} %param.9), channel_id=1, source_target_pairs={{0,4},{1,5},{2,6},{3,7},{4,0},{5,1},{6,2},{7,3},{8,12},{9,13},{10,... | collective-permute-start | bytes 221192 | tf_op jit(solution)/shard_map/ppermute | solution.py:105
  6.4 7.8 %collective-permute-start.3 = (bf16[16,2304]{1,0:T(8,128)(2,1)}, bf16[16,2304]{1,0:T(8,128)(2,1)S(1)}, u32[]{:S(2)}, u32[]{:S(2)}) collective-permute-start(bf16[16,2304]{1,0:T(8,128)(2,1)} %param.9), channel_id=1, source_target_pairs={{0,2},{1,3},{2,0},{3,1},{4,6},{5,7},{6,4},{7,5},{8,10},{9,11},{10,... | collective-permute-start | bytes 221192 | tf_op jit(solution)/shard_map/ppermute | solution.py:105
  8.1 1.3 %collective-permute-start.8 = (f32[128]{0:T(128)}, f32[128]{0:T(128)S(1)}, u32[]{:S(2)}, u32[]{:S(2)}) collective-permute-start(f32[128]{0:T(128)} %param.11), channel_id=1, source_target_pairs={{0,1},{1,0},{2,3},{3,2},{4,5},{5,4},{6,7},{7,6},{8,9},{9,8},{10,11... | collective-permute-start | bytes 1544 | tf_op jit(solution)/shard_map/ppermute | solution.py:112
  9.4 10.5 %collective-permute-start.9 = (bf16[128,2304]{1,0:T(8,128)(2,1)S(1)}, bf16[128,2304]{1,0:T(8,128)(2,1)S(1)}, u32[]{:S(2)}, u32[]{:S(2)}) collective-permute-start(bf16[128,2304]{1,0:T(8,128)(2,1)S(1)} %copy-done), channel_id=1, source_target_pairs={{0,1},{1,0},{2,3},{3,2},{4,5},{5,4},{6,7},{7,6},{8,9},{9,8},{10,11... | collective-permute-start | bytes 1769480 | tf_op jit(solution)/shard_map/ppermute | solution.py:112
  9.9 10.0 %collective-permute-start.7 = (bf16[128,2304]{1,0:T(8,128)(2,1)S(1)}, bf16[128,2304]{1,0:T(8,128)(2,1)S(1)}, u32[]{:S(2)}, u32[]{:S(2)}) collective-permute-start(bf16[128,2304]{1,0:T(8,128)(2,1)S(1)} %copy-done.5), channel_id=1, source_target_pairs={{0,1},{1,0},{2,3},{3,2},{4,5},{5,4},{6,7},{7,6},{8,9},{9,8},{10,11... | collective-permute-start | bytes 1769480 | tf_op jit(solution)/shard_map/ppermute | solution.py:112
  12.2 7.5 %collective-permute-start.6 = (bf16[16,2304]{1,0:T(8,128)(2,1)S(1)}, bf16[16,2304]{1,0:T(8,128)(2,1)S(1)}, u32[]{:S(2)}, u32[]{:S(2)}) collective-permute-start(bf16[16,2304]{1,0:T(8,128)(2,1)S(1)} %collective-permute-done.2), channel_id=1, source_target_pairs={{0,2},{1,3},{2,0},{3,1},{4,6},{5,7},{6,4},{7,5},{8,10},{9,11},{10,... | collective-permute-start | bytes 221192 | tf_op jit(solution)/shard_map/ppermute | solution.py:105
  13.7 5.9 %collective-permute-start.5 = (bf16[16,2304]{1,0:T(8,128)(2,1)S(1)}, bf16[16,2304]{1,0:T(8,128)(2,1)S(1)}, u32[]{:S(2)}, u32[]{:S(2)}) collective-permute-start(bf16[16,2304]{1,0:T(8,128)(2,1)S(1)} %collective-permute-done.1), channel_id=1, source_target_pairs={{0,2},{1,3},{2,0},{3,1},{4,6},{5,7},{6,4},{7,5},{8,10},{9,11},{10,... | collective-permute-start | bytes 221192 | tf_op jit(solution)/shard_map/ppermute | solution.py:105
  14.3 5.4 %collective-permute-start.4 = (bf16[16,2304]{1,0:T(8,128)(2,1)S(1)}, bf16[16,2304]{1,0:T(8,128)(2,1)S(1)}, u32[]{:S(2)}, u32[]{:S(2)}) collective-permute-start(bf16[16,2304]{1,0:T(8,128)(2,1)S(1)} %collective-permute-done), channel_id=1, source_target_pairs={{0,2},{1,3},{2,0},{3,1},{4,6},{5,7},{6,4},{7,5},{8,10},{9,11},{10,... | collective-permute-start | bytes 221192 | tf_op jit(solution)/shard_map/ppermute | solution.py:105
  20.9 6.2 %collective-permute-start.12 = (bf16[32,2304]{1,0:T(8,128)(2,1)S(1)}, bf16[32,2304]{1,0:T(8,128)(2,1)S(1)}, u32[]{:S(2)}, u32[]{:S(2)}) collective-permute-start(bf16[32,2304]{1,0:T(8,128)(2,1)S(1)} %get-tuple-element.25), channel_id=1, source_target_pairs={{0,2},{1,3},{2,0},{3,1},{4,6},{5,7},{6,4},{7,5},{8,10},{9,11},{10,... | collective-permute-start | bytes 442376 | tf_op jit(solution)/shard_map/ppermute | solution.py:105
  22.0 13.5 %collective-permute-start.16 = (bf16[128,2304]{1,0:T(8,128)(2,1)S(1)}, bf16[128,2304]{1,0:T(8,128)(2,1)S(1)}, u32[]{:S(2)}, u32[]{:S(2)}) collective-permute-start(bf16[128,2304]{1,0:T(8,128)(2,1)S(1)} %subtract_convert_fusion), channel_id=1, source_target_pairs={{0,1},{1,0},{2,3},{3,2},{4,5},{5,4},{6,7},{7,6},{8,9},{9,8},{10,11... | collective-permute-start | bytes 1769480 | tf_op jit(solution)/shard_map/ppermute | solution.py:112
  22.0 7.8 %collective-permute-start.10 = (bf16[32,2304]{1,0:T(8,128)(2,1)S(1)}, bf16[32,2304]{1,0:T(8,128)(2,1)S(1)}, u32[]{:S(2)}, u32[]{:S(2)}) collective-permute-start(bf16[32,2304]{1,0:T(8,128)(2,1)S(1)} %get-tuple-element.26), channel_id=1, source_target_pairs={{0,2},{1,3},{2,0},{3,1},{4,6},{5,7},{6,4},{7,5},{8,10},{9,11},{10,... | collective-permute-start | bytes 442376 | tf_op jit(solution)/shard_map/ppermute | solution.py:105
  27.5 5.4 %collective-permute-start.13 = (bf16[16,2304]{1,0:T(8,128)(2,1)S(1)}, bf16[16,2304]{1,0:T(8,128)(2,1)S(1)}, u32[]{:S(2)}, u32[]{:S(2)}) collective-permute-start(bf16[16,2304]{1,0:T(8,128)(2,1)S(1)} %get-tuple-element.27), channel_id=1, source_target_pairs={{0,8},{1,9},{2,10},{3,11},{4,12},{5,13},{6,14},{7,15},{8,0},{9,1},... | collective-permute-start | bytes 221192 | tf_op jit(solution)/shard_map/ppermute | solution.py:105
  28.4 6.2 %collective-permute-start.14 = (bf16[16,2304]{1,0:T(8,128)(2,1)S(1)}, bf16[16,2304]{1,0:T(8,128)(2,1)S(1)}, u32[]{:S(2)}, u32[]{:S(2)}) collective-permute-start(bf16[16,2304]{1,0:T(8,128)(2,1)S(1)} %get-tuple-element.28), channel_id=1, source_target_pairs={{0,12},{1,13},{2,14},{3,15},{4,8},{5,9},{6,10},{7,11},{8,4},{9,5},... | collective-permute-start | bytes 221192 | tf_op jit(solution)/shard_map/ppermute | solution.py:105
  29.8 21.8 %copy-start.4 = (f32[128,2304]{1,0:T(8,128)S(1)}, f32[128,2304]{1,0:T(8,128)}, u32[]{:S(2)}) copy-start(f32[128,2304]{1,0:T(8,128)} %refs_7_.1) | copy-start | bytes 3538948
  30.2 5.2 %collective-permute-start.11 = (bf16[16,2304]{1,0:T(8,128)(2,1)S(1)}, bf16[16,2304]{1,0:T(8,128)(2,1)S(1)}, u32[]{:S(2)}, u32[]{:S(2)}) collective-permute-start(bf16[16,2304]{1,0:T(8,128)(2,1)S(1)} %slice.78), channel_id=1, source_target_pairs={{0,4},{1,5},{2,6},{3,7},{4,0},{5,1},{6,2},{7,3},{8,12},{9,13},{10,... | collective-permute-start | bytes 221192 | tf_op jit(solution)/shard_map/ppermute | solution.py:105
  31.5 3.9 %collective-permute-start.15 = (bf16[128,128]{0,1:T(8,128)(2,1)S(1)}, bf16[128,128]{0,1:T(8,128)(2,1)S(1)}, u32[]{:S(2)}, u32[]{:S(2)}) collective-permute-start(bf16[128,128]{0,1:T(8,128)(2,1)S(1)} %get-tuple-element.30), channel_id=1, source_target_pairs={{0,1},{1,0},{2,3},{3,2},{4,5},{5,4},{6,7},{7,6},{8,9},{9,8},{10,11... | collective-permute-start | bytes 98312 | tf_op jit(solution)/shard_map/ppermute | solution.py:112
  35.4 16.2 %copy-start.3 = (f32[128,2304]{1,0:T(8,128)S(1)}, f32[128,2304]{1,0:T(8,128)}, u32[]{:S(2)}) copy-start(f32[128,2304]{1,0:T(8,128)} %refs_6_.1) | copy-start | bytes 3538948
  35.4 14.3 %copy-start.6 = (bf16[16,2304]{1,0:T(8,128)(2,1)}, bf16[16,2304]{1,0:T(8,128)(2,1)S(1)}, u32[]{:S(2)}) copy-start(bf16[16,2304]{1,0:T(8,128)(2,1)S(1)} %fusion.17) | copy-start | bytes 221188
  35.4 6.3 %collective-permute-start.22 = (bf16[16,2304]{1,0:T(8,128)(2,1)S(1)}, bf16[16,2304]{1,0:T(8,128)(2,1)S(1)}, u32[]{:S(2)}, u32[]{:S(2)}) collective-permute-start(bf16[16,2304]{1,0:T(8,128)(2,1)S(1)} %fusion.17), channel_id=1, source_target_pairs={{0,12},{1,13},{2,14},{3,15},{4,8},{5,9},{6,10},{7,11},{8,4},{9,5},... | collective-permute-start | bytes 221192 | tf_op jit(solution)/shard_map/ppermute | solution.py:105
  37.2 6.3 %collective-permute-start.20 = (bf16[16,2304]{1,0:T(8,128)(2,1)S(1)}, bf16[16,2304]{1,0:T(8,128)(2,1)S(1)}, u32[]{:S(2)}, u32[]{:S(2)}) collective-permute-start(bf16[16,2304]{1,0:T(8,128)(2,1)S(1)} %fusion.17), channel_id=1, source_target_pairs={{0,8},{1,9},{2,10},{3,11},{4,12},{5,13},{6,14},{7,15},{8,0},{9,1},... | collective-permute-start | bytes 221192 | tf_op jit(solution)/shard_map/ppermute | solution.py:105
  37.5 7.6 %collective-permute-start.18 = (bf16[16,2304]{1,0:T(8,128)(2,1)S(1)}, bf16[16,2304]{1,0:T(8,128)(2,1)S(1)}, u32[]{:S(2)}, u32[]{:S(2)}) collective-permute-start(bf16[16,2304]{1,0:T(8,128)(2,1)S(1)} %fusion.17), channel_id=1, source_target_pairs={{0,4},{1,5},{2,6},{3,7},{4,0},{5,1},{6,2},{7,3},{8,12},{9,13},{10,... | collective-permute-start | bytes 221192 | tf_op jit(solution)/shard_map/ppermute | solution.py:105
  39.9 5.6 %collective-permute-start.17 = (bf16[16,2304]{1,0:T(8,128)(2,1)S(1)}, bf16[16,2304]{1,0:T(8,128)(2,1)S(1)}, u32[]{:S(2)}, u32[]{:S(2)}) collective-permute-start(bf16[16,2304]{1,0:T(8,128)(2,1)S(1)} %fusion.17), channel_id=1, source_target_pairs={{0,2},{1,3},{2,0},{3,1},{4,6},{5,7},{6,4},{7,5},{8,10},{9,11},{10,... | collective-permute-start | bytes 221192 | tf_op jit(solution)/shard_map/ppermute | solution.py:105
  41.7 7.7 %collective-permute-start.23 = (bf16[16,2304]{1,0:T(8,128)(2,1)S(1)}, bf16[16,2304]{1,0:T(8,128)(2,1)S(1)}, u32[]{:S(2)}, u32[]{:S(2)}) collective-permute-start(bf16[16,2304]{1,0:T(8,128)(2,1)S(1)} %collective-permute-done.22), channel_id=1, source_target_pairs={{0,2},{1,3},{2,0},{3,1},{4,6},{5,7},{6,4},{7,5},{8,10},{9,11},{10,... | collective-permute-start | bytes 221192 | tf_op jit(solution)/shard_map/ppermute | solution.py:105
  43.5 5.9 %collective-permute-start.21 = (bf16[16,2304]{1,0:T(8,128)(2,1)S(1)}, bf16[16,2304]{1,0:T(8,128)(2,1)S(1)}, u32[]{:S(2)}, u32[]{:S(2)}) collective-permute-start(bf16[16,2304]{1,0:T(8,128)(2,1)S(1)} %collective-permute-done.20), channel_id=1, source_target_pairs={{0,2},{1,3},{2,0},{3,1},{4,6},{5,7},{6,4},{7,5},{8,10},{9,11},{10,... | collective-permute-start | bytes 221192 | tf_op jit(solution)/shard_map/ppermute | solution.py:105
  45.1 4.4 %collective-permute-start.19 = (bf16[16,2304]{1,0:T(8,128)(2,1)S(1)}, bf16[16,2304]{1,0:T(8,128)(2,1)S(1)}, u32[]{:S(2)}, u32[]{:S(2)}) collective-permute-start(bf16[16,2304]{1,0:T(8,128)(2,1)S(1)} %collective-permute-done.18), channel_id=1, source_target_pairs={{0,2},{1,3},{2,0},{3,1},{4,6},{5,7},{6,4},{7,5},{8,10},{9,11},{10,... | collective-permute-start | bytes 221192 | tf_op jit(solution)/shard_map/ppermute | solution.py:105
  49.5 2.1 %collective-permute-start.24 = (bf16[128,2304]{1,0:T(8,128)(2,1)S(1)}, bf16[128,2304]{1,0:T(8,128)(2,1)S(1)}, u32[]{:S(2)}, u32[]{:S(2)}) collective-permute-start(bf16[128,2304]{1,0:T(8,128)(2,1)S(1)} %constant_dynamic-update-slice_fusion.10.refs_0_), channel_id=1, source_target_pairs={{0,1},{1,0},{2,3},{3,2},{4,5},{5,4},{6,7},{7,6},{8,9},{9,8},{10,11... | collective-permute-start | bytes 1769480 | tf_op jit(solution)/shard_map/ppermute | solution.py:112
  (3 other events, 12.5 us)

commit v9 on v8

--- a/solution.py
+++ b/solution.py
@@ -19,7 +19,7 @@
     )
 
 
-def update_kernel(columns, block, rows_total, codes_across, centered, *refs):
+def update_kernel(columns, rows_total, codes_across, centered, *refs):
     blocks = len(refs) - 20
     errors, (encoder, decoder) = refs[:blocks], refs[blocks : blocks + 2]
     moments = refs[blocks + 2 : blocks + 6]
@@ -33,10 +33,8 @@
 
     start = 0
     for one in errors:
-        for first in (0, block):
-            for at in range(first, one.shape[0], 2 * block):
-                error_all[pl.ds(start, block), :] = one[pl.ds(at, block), :]
-                start += block
+        error_all[pl.ds(start, one.shape[0]), :] = one[...]
+        start += one.shape[0]
     first = (1.0 - beta_first) / rows_total
     second = (1.0 - beta_second) / (rows_total * rows_total)
 
@@ -66,7 +64,7 @@
             write(t, i).wait()
 
 
-def update(total_rows, codes_across, centered, errors, block, weights, moments):
+def update(total_rows, codes_across, centered, errors, weights, moments):
     latents, width = weights[0].shape
     rows = centered.shape[0]
     columns = next(c for c in (256, 128, width) if width % c == 0)
@@ -76,7 +74,7 @@
     wide = pltpu.VMEM((latents, width), jnp.float32)
     narrow = pltpu.VMEM((latents, width), jnp.bfloat16)
     return pl.pallas_call(
-        functools.partial(update_kernel, columns, block, float(total_rows)),
+        functools.partial(update_kernel, columns, float(total_rows)),
         out_shape=(half, full, full, half, full, full),
         in_specs=[vmem] * (len(errors) + 8),
         out_specs=[pl.BlockSpec(memory_space=pl.ANY)] * 6,
@@ -112,9 +110,18 @@
     return lax.ppermute(block, "latent", [(i, i ^ 1) for i in range(size)])
 
 
+def chip_order(chips):
+    even = [k for k in range(4, chips, 2) if k != 6] + [2, 6][: chips // 2 - 1]
+    return [0] + [k for one in even for k in (one, one + 1)] + [1]
+
+
 def gather_chips(block, chips):
-    even = [block] + [to_chip(block, k) for k in range(2, chips, 2)]
-    return even, [to_chip(one, 1) for one in even]
+    blocks = {0: block}
+    for k in range(2, chips, 2):
+        blocks[k] = to_chip(block, k)
+    for k in range(0, chips, 2):
+        blocks[k + 1] = to_chip(blocks[k], 1)
+    return jnp.concatenate([blocks[k] for k in chip_order(chips)], 0)
 
 
 def body(
@@ -135,8 +142,7 @@
     pairs = chips // 2
     total_rows = rows_here * size
 
-    even, odd = gather_chips(activations, chips)
-    rows_core = jnp.concatenate(even + odd, 0)
+    rows_core = gather_chips(activations, chips)
     encoder_both = jnp.concatenate([encoder, to_other_core(encoder)], 0)
     decoder_both = jnp.concatenate([decoder, to_other_core(decoder)], 0)
     bias_both = jnp.concatenate([encoder_bias, to_other_core(encoder_bias)], 0)
@@ -148,14 +154,23 @@
     other_codes = to_other_core(codes[:, latents_here:])
     other_centered = to_other_core(centered)
 
+    order = chip_order(chips)
+
+    def codes_of(wanted):
+        starts = [order.index(k) * rows_here for k in wanted]
+        return jnp.concatenate([codes[at : at + rows_here] for at in starts], 0)
+
+    even = list(range(0, chips, 2))
     split = 2 * rows_here
     given = jnp.dot(
-        codes[pairs * rows_here :], decoder_both, preferred_element_type=jnp.float32
+        codes_of([k + 1 for k in even]), decoder_both, preferred_element_type=jnp.float32
     ).astype(jnp.bfloat16)
 
     def pair_sums(first, last):
         return jnp.dot(
-            codes[first:last], decoder_both, preferred_element_type=jnp.float32
+            codes_of(even[first // rows_here : last // rows_here]),
+            decoder_both,
+            preferred_element_type=jnp.float32,
         ) + to_chip(given[first:last], 1).astype(jnp.float32)
 
     far = pair_sums(split, pairs * rows_here).astype(jnp.bfloat16)
@@ -171,8 +186,7 @@
     row_error, other_codes, other_centered = lax.optimization_barrier(
         (row_error, other_codes, other_centered)
     )
-    even, odd = gather_chips(row_error, chips)
-    errors = jnp.concatenate([one for both in zip(even, odd) for one in both], 0)
+    errors = gather_chips(row_error, chips)
     codes_across = jnp.concatenate([codes[:, :latents_here], other_codes], 0).T
     centered_all = jnp.concatenate([centered, other_centered], 0)
     (
@@ -187,7 +201,6 @@
         codes_across,
         centered_all,
         (errors, to_other_core(errors)),
-        rows_here,
         (encoder, decoder),
         (encoder_moment, encoder_square, decoder_moment, decoder_square),
     )

time: 55.1 us -> 59.8 us (1.085)
  waiting for transfers between devices: 19.9 us -> 21.8 us
  other arithmetic: 0.25 us -> 1.46 us
  local copies, waits for them, and re-layouts: 1.35 us -> 2.56 us
    ppermute x19, waiting for transfers between devices: 17.9 us -> 21 us  [to_chip(): lax.ppermute(block, 'latent', [(i, i ^ 2 * distance) for i in range(size)])]
    concatenate x1, other arithmetic: 0.08 us -> 1.29 us  [body(): centered_all = jnp.concatenate([centered, other_centered], 0)]
    ppermute x6, waiting for transfers between devices: 1.98 us -> 0.78 us  [to_other_core(): return lax.ppermute(block, 'latent', [(i, i ^ 1) for i in range(size)])]
    slice x1, local copies, waits for them, and re-layouts: 0.02 us -> 0.74 us  [pair_sums(): given[first:last]]
  transfers between devices with their start and end apart: 25 -> 25, of which waited for: 9 -> 12; matrix products, arithmetic and copies ran while one was open for 4% -> 7% of each run, Pallas kernels for 0% -> 0%
where the time goes in v9:
time: 59.8 us; the launch traced here: 59.7 us
  starting transfers between devices  27.8 us (46%)
  waiting for transfers between devices  21.8 us (36%)
  Pallas kernels  3.38 us (6%)
  local copies, waits for them, and re-layouts  2.56 us (4%)
  matrix products  1.59 us (3%)
  other arithmetic  1.46 us (2%)
  between operations  1.02 us (2%)
    ppermute x19, starting transfers between devices, to_chip(): lax.ppermute(block, 'latent', [(i, i ^ 2 * distance) for i in range(size)])  27.1 us
    ppermute x19, waiting for transfers between devices, to_chip(): lax.ppermute(block, 'latent', [(i, i ^ 2 * distance) for i in range(size)])  21 us
    pallas_call x1, Pallas kernels, update(): pl.pallas_call(functools.partial(update_kernel, columns, float(total_rows...  3.38 us
    concatenate x1, other arithmetic, body(): centered_all = jnp.concatenate([centered, other_centered], 0)  1.29 us
    unnamed x35, local copies, waits for them, and re-layouts  1.24 us
  transfers between devices with their start and end apart: 25, of which 12 were waited for; matrix products, arithmetic and copies ran while one was open for 7% of the time, Pallas kernels for 0%

profile of v9, /device:TPU:0, one launch (start us, length us, event | category | flops | bytes accessed | tf_op | source)
XLA Modules:
  0.0 59.7 jit_solution(7379239495185967399)
XLA Ops:
  0.7 5.1 %collective-permute-start.4 = (bf16[16,2304]{1,0:T(8,128)(2,1)}, bf16[16,2304]{1,0:T(8,128)(2,1)S(1)}, u32[]{:S(2)}, u32[]{:S(2)}) collective-permute-start(bf16[16,2304]{1,0:T(8,128)(2,1)} %param.9), channel_id=1, source_target_pairs={{0,12},{1,13},{2,14},{3,15},{4,8},{5,9},{6,10},{7,11},{8,4},{9,5},... | collective-permute-start | bytes 221192 | tf_op jit(solution)/shard_map/ppermute | solution.py:103
  5.8 0.6 %collective-permute-start = (bf16[16,2304]{1,0:T(8,128)(2,1)}, bf16[16,2304]{1,0:T(8,128)(2,1)S(1)}, u32[]{:S(2)}, u32[]{:S(2)}) collective-permute-start(bf16[16,2304]{1,0:T(8,128)(2,1)} %param.9), channel_id=1, source_target_pairs={{0,8},{1,9},{2,10},{3,11},{4,12},{5,13},{6,14},{7,15},{8,0},{9,1},... | collective-permute-start | bytes 221192 | tf_op jit(solution)/shard_map/ppermute | solution.py:103
  6.4 1.7 %collective-permute-start.6 = (bf16[16,2304]{1,0:T(8,128)(2,1)}, bf16[16,2304]{1,0:T(8,128)(2,1)S(1)}, u32[]{:S(2)}, u32[]{:S(2)}) collective-permute-start(bf16[16,2304]{1,0:T(8,128)(2,1)} %param.9), channel_id=1, source_target_pairs={{0,2},{1,3},{2,0},{3,1},{4,6},{5,7},{6,4},{7,5},{8,10},{9,11},{10,... | collective-permute-start | bytes 221192 | tf_op jit(solution)/shard_map/ppermute | solution.py:103
  8.1 1.1 %constant_dynamic-update-slice_fusion.9 = bf16[256,2304]{1,0:T(8,128)(2,1)S(1)} fusion(bf16[128,2304]{1,0:T(8,128)(2,1)} %refs_3_.1), kind=kLoop, calls=%fused_computation.36 | loop fusion | bytes 1179648
  9.4 0.5 collective-permute-start.9
  9.8 2.0 %collective-permute-done = bf16[16,2304]{1,0:T(8,128)(2,1)S(1)} collective-permute-done((bf16[16,2304]{1,0:T(8,128)(2,1)}, bf16[16,2304]{1,0:T(8,128)(2,1)S(1)}, u32[]{:S(2)}, u32[]{:S(2)}) %collective-permute-start) | collective-permute-done | bytes 73760 | tf_op jit(solution)/shard_map/ppermute | solution.py:103
  11.8 1.6 %collective-permute-start.1 = (bf16[16,2304]{1,0:T(8,128)(2,1)S(1)}, bf16[16,2304]{1,0:T(8,128)(2,1)S(1)}, u32[]{:S(2)}, u32[]{:S(2)}) collective-permute-start(bf16[16,2304]{1,0:T(8,128)(2,1)S(1)} %collective-permute-done), channel_id=1, source_target_pairs={{0,2},{1,3},{2,0},{3,1},{4,6},{5,7},{6,4},{7,5},{8,10},{9,11},{10,... | collective-permute-start | bytes 221192 | tf_op jit(solution)/shard_map/ppermute | solution.py:103
  13.5 0.5 collective-permute-start.5
  14.0 2.1 %collective-permute-done.1 = bf16[16,2304]{1,0:T(8,128)(2,1)S(1)} collective-permute-done((bf16[16,2304]{1,0:T(8,128)(2,1)S(1)}, bf16[16,2304]{1,0:T(8,128)(2,1)S(1)}, u32[]{:S(2)}, u32[]{:S(2)}) %collective-permute-start.1) | collective-permute-done | bytes 73760 | tf_op jit(solution)/shard_map/ppermute | solution.py:103
  16.2 2.3 %collective-permute-start.3 = (bf16[16,2304]{1,0:T(8,128)(2,1)S(1)}, bf16[16,2304]{1,0:T(8,128)(2,1)S(1)}, u32[]{:S(2)}, u32[]{:S(2)}) collective-permute-start(bf16[16,2304]{1,0:T(8,128)(2,1)S(1)} %collective-permute-done.2), channel_id=1, source_target_pairs={{0,2},{1,3},{2,0},{3,1},{4,6},{5,7},{6,4},{7,5},{8,10},{9,11},{10,... | collective-permute-start | bytes 221192 | tf_op jit(solution)/shard_map/ppermute | solution.py:103
  18.5 2.3 %collective-permute-done.3 = bf16[16,2304]{1,0:T(8,128)(2,1)S(1)} collective-permute-done((bf16[16,2304]{1,0:T(8,128)(2,1)S(1)}, bf16[16,2304]{1,0:T(8,128)(2,1)S(1)}, u32[]{:S(2)}, u32[]{:S(2)}) %collective-permute-start.3) | collective-permute-done | bytes 73760 | tf_op jit(solution)/shard_map/ppermute | solution.py:103
  21.0 0.5 fusion.11
  22.2 0.7 %fusion.35 = (bf16[32,2304]{1,0:T(8,128)(2,1)}, bf16[32,2304]{1,0:T(8,128)(2,1)}) fusion(bf16[64,2304]{1,0:T(8,128)(2,1)S(1)} %convolution_convert_fusion), kind=kLoop, calls=%fused_computation.56 | loop fusion | bytes 589824 | tf_op jit(solution)/shard_map/slice | solution.py:174
  23.0 2.0 %collective-permute-start.12 = (bf16[32,2304]{1,0:T(8,128)(2,1)}, bf16[32,2304]{1,0:T(8,128)(2,1)S(1)}, u32[]{:S(2)}, u32[]{:S(2)}) collective-permute-start(bf16[32,2304]{1,0:T(8,128)(2,1)} %get-tuple-element.25), channel_id=1, source_target_pairs={{0,2},{1,3},{2,0},{3,1},{4,6},{5,7},{6,4},{7,5},{8,10},{9,11},{10,... | collective-permute-start | bytes 442376 | tf_op jit(solution)/shard_map/ppermute | solution.py:103
  25.4 4.0 %collective-permute-done.12 = bf16[32,2304]{1,0:T(8,128)(2,1)S(1)} collective-permute-done((bf16[32,2304]{1,0:T(8,128)(2,1)}, bf16[32,2304]{1,0:T(8,128)(2,1)S(1)}, u32[]{:S(2)}, u32[]{:S(2)}) %collective-permute-start.12) | collective-permute-done | bytes 147488 | tf_op jit(solution)/shard_map/ppermute | solution.py:103
  29.7 2.1 %collective-permute-start.13 = (bf16[16,2304]{1,0:T(8,128)(2,1)S(1)}, bf16[16,2304]{1,0:T(8,128)(2,1)S(1)}, u32[]{:S(2)}, u32[]{:S(2)}) collective-permute-start(bf16[16,2304]{1,0:T(8,128)(2,1)S(1)} %get-tuple-element.27), channel_id=1, source_target_pairs={{0,8},{1,9},{2,10},{3,11},{4,12},{5,13},{6,14},{7,15},{8,0},{9,1},... | collective-permute-start | bytes 221192 | tf_op jit(solution)/shard_map/ppermute | solution.py:103
  31.9 1.6 %collective-permute-start.14 = (bf16[16,2304]{1,0:T(8,128)(2,1)S(1)}, bf16[16,2304]{1,0:T(8,128)(2,1)S(1)}, u32[]{:S(2)}, u32[]{:S(2)}) collective-permute-start(bf16[16,2304]{1,0:T(8,128)(2,1)S(1)} %get-tuple-element.28), channel_id=1, source_target_pairs={{0,12},{1,13},{2,14},{3,15},{4,8},{5,9},{6,10},{7,11},{8,4},{9,5},... | collective-permute-start | bytes 221192 | tf_op jit(solution)/shard_map/ppermute | solution.py:103
  33.9 1.1 %collective-permute-done.13 = bf16[16,2304]{1,0:T(8,128)(2,1)S(1)} collective-permute-done((bf16[16,2304]{1,0:T(8,128)(2,1)S(1)}, bf16[16,2304]{1,0:T(8,128)(2,1)S(1)}, u32[]{:S(2)}, u32[]{:S(2)}) %collective-permute-start.13) | collective-permute-done | bytes 73760 | tf_op jit(solution)/shard_map/ppermute | solution.py:103
  35.1 3.0 %collective-permute-done.14 = bf16[16,2304]{1,0:T(8,128)(2,1)S(1)} collective-permute-done((bf16[16,2304]{1,0:T(8,128)(2,1)S(1)}, bf16[16,2304]{1,0:T(8,128)(2,1)S(1)}, u32[]{:S(2)}, u32[]{:S(2)}) %collective-permute-start.14) | collective-permute-done | bytes 73760 | tf_op jit(solution)/shard_map/ppermute | solution.py:103
  38.1 0.7 %collective-permute-done.11 = bf16[16,2304]{1,0:T(8,128)(2,1)S(1)} collective-permute-done((bf16[16,2304]{1,0:T(8,128)(2,1)S(1)}, bf16[16,2304]{1,0:T(8,128)(2,1)S(1)}, u32[]{:S(2)}, u32[]{:S(2)}) %collective-permute-start.11) | collective-permute-done | bytes 73760 | tf_op jit(solution)/shard_map/ppermute | solution.py:103
  38.9 2.4 %collective-permute-start.23 = (bf16[16,2304]{1,0:T(8,128)(2,1)S(1)}, bf16[16,2304]{1,0:T(8,128)(2,1)S(1)}, u32[]{:S(2)}, u32[]{:S(2)}) collective-permute-start(bf16[16,2304]{1,0:T(8,128)(2,1)S(1)} %fusion.17), channel_id=1, source_target_pairs={{0,2},{1,3},{2,0},{3,1},{4,6},{5,7},{6,4},{7,5},{8,10},{9,11},{10,... | collective-permute-start | bytes 221192 | tf_op jit(solution)/shard_map/ppermute | solution.py:103
  41.3 1.7 %collective-permute-start.21 = (bf16[16,2304]{1,0:T(8,128)(2,1)S(1)}, bf16[16,2304]{1,0:T(8,128)(2,1)S(1)}, u32[]{:S(2)}, u32[]{:S(2)}) collective-permute-start(bf16[16,2304]{1,0:T(8,128)(2,1)S(1)} %fusion.17), channel_id=1, source_target_pairs={{0,12},{1,13},{2,14},{3,15},{4,8},{5,9},{6,10},{7,11},{8,4},{9,5},... | collective-permute-start | bytes 221192 | tf_op jit(solution)/shard_map/ppermute | solution.py:103
  43.0 2.7 %collective-permute-start.17 = (bf16[16,2304]{1,0:T(8,128)(2,1)S(1)}, bf16[16,2304]{1,0:T(8,128)(2,1)S(1)}, u32[]{:S(2)}, u32[]{:S(2)}) collective-permute-start(bf16[16,2304]{1,0:T(8,128)(2,1)S(1)} %fusion.17), channel_id=1, source_target_pairs={{0,8},{1,9},{2,10},{3,11},{4,12},{5,13},{6,14},{7,15},{8,0},{9,1},... | collective-permute-start | bytes 221192 | tf_op jit(solution)/shard_map/ppermute | solution.py:103
  45.7 1.9 %collective-permute-done.21 = bf16[16,2304]{1,0:T(8,128)(2,1)S(1)} collective-permute-done((bf16[16,2304]{1,0:T(8,128)(2,1)S(1)}, bf16[16,2304]{1,0:T(8,128)(2,1)S(1)}, u32[]{:S(2)}, u32[]{:S(2)}) %collective-permute-start.21) | collective-permute-done | bytes 73760 | tf_op jit(solution)/shard_map/ppermute | solution.py:103
  47.6 0.6 collective-permute-start.22
  48.2 0.8 %collective-permute-done.19 = bf16[16,2304]{1,0:T(8,128)(2,1)S(1)} collective-permute-done((bf16[16,2304]{1,0:T(8,128)(2,1)S(1)}, bf16[16,2304]{1,0:T(8,128)(2,1)S(1)}, u32[]{:S(2)}, u32[]{:S(2)}) %collective-permute-start.19) | collective-permute-done | bytes 73760 | tf_op jit(solution)/shard_map/ppermute | solution.py:103
  48.9 0.7 %collective-permute-start.20 = (bf16[16,2304]{1,0:T(8,128)(2,1)S(1)}, bf16[16,2304]{1,0:T(8,128)(2,1)S(1)}, u32[]{:S(2)}, u32[]{:S(2)}) collective-permute-start(bf16[16,2304]{1,0:T(8,128)(2,1)S(1)} %collective-permute-done.19), channel_id=1, source_target_pairs={{0,2},{1,3},{2,0},{3,1},{4,6},{5,7},{6,4},{7,5},{8,10},{9,11},{10,... | collective-permute-start | bytes 221192 | tf_op jit(solution)/shard_map/ppermute | solution.py:103
  49.6 1.3 %collective-permute-start.18 = (bf16[16,2304]{1,0:T(8,128)(2,1)S(1)}, bf16[16,2304]{1,0:T(8,128)(2,1)S(1)}, u32[]{:S(2)}, u32[]{:S(2)}) collective-permute-start(bf16[16,2304]{1,0:T(8,128)(2,1)S(1)} %collective-permute-done.17), channel_id=1, source_target_pairs={{0,2},{1,3},{2,0},{3,1},{4,6},{5,7},{6,4},{7,5},{8,10},{9,11},{10,... | collective-permute-start | bytes 221192 | tf_op jit(solution)/shard_map/ppermute | solution.py:103
  51.0 3.1 %collective-permute-done.18 = bf16[16,2304]{1,0:T(8,128)(2,1)S(1)} collective-permute-done((bf16[16,2304]{1,0:T(8,128)(2,1)S(1)}, bf16[16,2304]{1,0:T(8,128)(2,1)S(1)}, u32[]{:S(2)}, u32[]{:S(2)}) %collective-permute-start.18) | collective-permute-done | bytes 73760 | tf_op jit(solution)/shard_map/ppermute | solution.py:103
  54.3 1.3 %pad_maximum_fusion.centered = bf16[256,2304]{1,0:T(8,128)(2,1)S(1)} fusion(bf16[128,2304]{1,0:T(8,128)(2,1)} %collective-permute-done.16, bf16[128,2304]{1,0:T(8,128)(2,1)S(1)} %subtract_convert_fusion), kind=kLoop, calls=%fused_computation.8 | loop fusion | flops 2359296 | bytes 2359296 | tf_op jit(solution)/shard_map/concatenate | solution.py:191
  55.6 0.6 %collective-permute-done.24.refs_1_ = bf16[128,2304]{1,0:T(8,128)(2,1)S(1)} collective-permute-done((bf16[128,2304]{1,0:T(8,128)(2,1)S(1)}, bf16[128,2304]{1,0:T(8,128)(2,1)S(1)}, u32[]{:S(2)}, u32[]{:S(2)}) %collective-permute-start.24) | collective-permute-done | bytes 589856 | tf_op jit(solution)/shard_map/ppermute | solution.py:110
  56.3 3.4 %update.1 = (bf16[128,2304]{1,0:T(8,128)(2,1)}, f32[128,2304]{1,0:T(8,128)}, f32[128,2304]{1,0:T(8,128)}, bf16[128,2304]{1,0:T(8,128)(2,1)}, f32[128,2304]{1,0:T(8,128)}, /*index=5*/f32[128,2304]{1,0:T(8,128)}) custom-call(bf16[128,256]{1,0:T(8,128)(2,1)S(1)} %maximum_bitcast_fusion.codes_across, bf16[256,2304]{1,0:T(8,128)(2,1)S(1)} %pad_maximum_fusion.centered, ...), custom_call_target="tpu_custom_call" | custom-call | flops 452984832 | bytes 12976128 | tf_op jit(solution)/shard_map/update/pallas_call | solution.py:76
  (75 shorter events, 2.5 us)
Async XLA Ops:
  0.6 9.2 %copy-start.9 = (f32[128]{0:T(128)S(1)}, f32[128]{0:T(128)}, u32[]{:S(2)}) copy-start(f32[128]{0:T(128)} %param.11) | copy-start | bytes 1540
  0.7 8.7 %copy-start = (bf16[128,2304]{1,0:T(8,128)(2,1)S(1)}, bf16[128,2304]{1,0:T(8,128)(2,1)}, u32[]{:S(2)}) copy-start(bf16[128,2304]{1,0:T(8,128)(2,1)} %refs_3_.1) | copy-start | bytes 1769476
  0.7 12.8 %copy-start.5 = (bf16[128,2304]{1,0:T(8,128)(2,1)S(1)}, bf16[128,2304]{1,0:T(8,128)(2,1)}, u32[]{:S(2)}) copy-start(bf16[128,2304]{1,0:T(8,128)(2,1)} %refs_2_.1) | copy-start | bytes 1769476
  0.7 20.2 %copy-start.8 = (f32[2304]{0:T(1024)S(1)}, f32[2304]{0:T(1024)}, u32[]{:S(2)}) copy-start(f32[2304]{0:T(1024)} %param.13) | copy-start | bytes 27652
  0.7 12.8 %collective-permute-start.4 = (bf16[16,2304]{1,0:T(8,128)(2,1)}, bf16[16,2304]{1,0:T(8,128)(2,1)S(1)}, u32[]{:S(2)}, u32[]{:S(2)}) collective-permute-start(bf16[16,2304]{1,0:T(8,128)(2,1)} %param.9), channel_id=1, source_target_pairs={{0,12},{1,13},{2,14},{3,15},{4,8},{5,9},{6,10},{7,11},{8,4},{9,5},... | collective-permute-start | bytes 221192 | tf_op jit(solution)/shard_map/ppermute | solution.py:103
  5.8 7.7 %collective-permute-start.2 = (bf16[16,2304]{1,0:T(8,128)(2,1)}, bf16[16,2304]{1,0:T(8,128)(2,1)S(1)}, u32[]{:S(2)}, u32[]{:S(2)}) collective-permute-start(bf16[16,2304]{1,0:T(8,128)(2,1)} %param.9), channel_id=1, source_target_pairs={{0,4},{1,5},{2,6},{3,7},{4,0},{5,1},{6,2},{7,3},{8,12},{9,13},{10,... | collective-permute-start | bytes 221192 | tf_op jit(solution)/shard_map/ppermute | solution.py:103
  5.8 6.0 %collective-permute-start = (bf16[16,2304]{1,0:T(8,128)(2,1)}, bf16[16,2304]{1,0:T(8,128)(2,1)S(1)}, u32[]{:S(2)}, u32[]{:S(2)}) collective-permute-start(bf16[16,2304]{1,0:T(8,128)(2,1)} %param.9), channel_id=1, source_target_pairs={{0,8},{1,9},{2,10},{3,11},{4,12},{5,13},{6,14},{7,15},{8,0},{9,1},... | collective-permute-start | bytes 221192 | tf_op jit(solution)/shard_map/ppermute | solution.py:103
  6.4 14.5 %collective-permute-start.6 = (bf16[16,2304]{1,0:T(8,128)(2,1)}, bf16[16,2304]{1,0:T(8,128)(2,1)S(1)}, u32[]{:S(2)}, u32[]{:S(2)}) collective-permute-start(bf16[16,2304]{1,0:T(8,128)(2,1)} %param.9), channel_id=1, source_target_pairs={{0,2},{1,3},{2,0},{3,1},{4,6},{5,7},{6,4},{7,5},{8,10},{9,11},{10,... | collective-permute-start | bytes 221192 | tf_op jit(solution)/shard_map/ppermute | solution.py:103
  8.1 1.3 %collective-permute-start.8 = (f32[128]{0:T(128)}, f32[128]{0:T(128)S(1)}, u32[]{:S(2)}, u32[]{:S(2)}) collective-permute-start(f32[128]{0:T(128)} %param.11), channel_id=1, source_target_pairs={{0,1},{1,0},{2,3},{3,2},{4,5},{5,4},{6,7},{7,6},{8,9},{9,8},{10,11... | collective-permute-start | bytes 1544 | tf_op jit(solution)/shard_map/ppermute | solution.py:110
  9.4 12.4 %collective-permute-start.9 = (bf16[128,2304]{1,0:T(8,128)(2,1)S(1)}, bf16[128,2304]{1,0:T(8,128)(2,1)S(1)}, u32[]{:S(2)}, u32[]{:S(2)}) collective-permute-start(bf16[128,2304]{1,0:T(8,128)(2,1)S(1)} %copy-done), channel_id=1, source_target_pairs={{0,1},{1,0},{2,3},{3,2},{4,5},{5,4},{6,7},{7,6},{8,9},{9,8},{10,11... | collective-permute-start | bytes 1769480 | tf_op jit(solution)/shard_map/ppermute | solution.py:110
  11.8 4.4 %collective-permute-start.1 = (bf16[16,2304]{1,0:T(8,128)(2,1)S(1)}, bf16[16,2304]{1,0:T(8,128)(2,1)S(1)}, u32[]{:S(2)}, u32[]{:S(2)}) collective-permute-start(bf16[16,2304]{1,0:T(8,128)(2,1)S(1)} %collective-permute-done), channel_id=1, source_target_pairs={{0,2},{1,3},{2,0},{3,1},{4,6},{5,7},{6,4},{7,5},{8,10},{9,11},{10,... | collective-permute-start | bytes 221192 | tf_op jit(solution)/shard_map/ppermute | solution.py:103
  13.5 7.6 %collective-permute-start.7 = (bf16[128,2304]{1,0:T(8,128)(2,1)S(1)}, bf16[128,2304]{1,0:T(8,128)(2,1)S(1)}, u32[]{:S(2)}, u32[]{:S(2)}) collective-permute-start(bf16[128,2304]{1,0:T(8,128)(2,1)S(1)} %copy-done.5), channel_id=1, source_target_pairs={{0,1},{1,0},{2,3},{3,2},{4,5},{5,4},{6,7},{7,6},{8,9},{9,8},{10,11... | collective-permute-start | bytes 1769480 | tf_op jit(solution)/shard_map/ppermute | solution.py:110
  13.5 7.3 %collective-permute-start.5 = (bf16[16,2304]{1,0:T(8,128)(2,1)S(1)}, bf16[16,2304]{1,0:T(8,128)(2,1)S(1)}, u32[]{:S(2)}, u32[]{:S(2)}) collective-permute-start(bf16[16,2304]{1,0:T(8,128)(2,1)S(1)} %collective-permute-done.4), channel_id=1, source_target_pairs={{0,2},{1,3},{2,0},{3,1},{4,6},{5,7},{6,4},{7,5},{8,10},{9,11},{10,... | collective-permute-start | bytes 221192 | tf_op jit(solution)/shard_map/ppermute | solution.py:103
  16.2 4.7 %collective-permute-start.3 = (bf16[16,2304]{1,0:T(8,128)(2,1)S(1)}, bf16[16,2304]{1,0:T(8,128)(2,1)S(1)}, u32[]{:S(2)}, u32[]{:S(2)}) collective-permute-start(bf16[16,2304]{1,0:T(8,128)(2,1)S(1)} %collective-permute-done.2), channel_id=1, source_target_pairs={{0,2},{1,3},{2,0},{3,1},{4,6},{5,7},{6,4},{7,5},{8,10},{9,11},{10,... | collective-permute-start | bytes 221192 | tf_op jit(solution)/shard_map/ppermute | solution.py:103
  23.0 6.4 %collective-permute-start.12 = (bf16[32,2304]{1,0:T(8,128)(2,1)}, bf16[32,2304]{1,0:T(8,128)(2,1)S(1)}, u32[]{:S(2)}, u32[]{:S(2)}) collective-permute-start(bf16[32,2304]{1,0:T(8,128)(2,1)} %get-tuple-element.25), channel_id=1, source_target_pairs={{0,2},{1,3},{2,0},{3,1},{4,6},{5,7},{6,4},{7,5},{8,10},{9,11},{10,... | collective-permute-start | bytes 442376 | tf_op jit(solution)/shard_map/ppermute | solution.py:103
  25.0 13.9 %collective-permute-start.16 = (bf16[128,2304]{1,0:T(8,128)(2,1)S(1)}, bf16[128,2304]{1,0:T(8,128)(2,1)}, u32[]{:S(2)}, u32[]{:S(2)}) collective-permute-start(bf16[128,2304]{1,0:T(8,128)(2,1)S(1)} %subtract_convert_fusion), channel_id=1, source_target_pairs={{0,1},{1,0},{2,3},{3,2},{4,5},{5,4},{6,7},{7,6},{8,9},{9,8},{10,11... | collective-permute-start | bytes 1769480 | tf_op jit(solution)/shard_map/ppermute | solution.py:110
  25.3 8.1 %collective-permute-start.10 = (bf16[32,2304]{1,0:T(8,128)(2,1)}, bf16[32,2304]{1,0:T(8,128)(2,1)S(1)}, u32[]{:S(2)}, u32[]{:S(2)}) collective-permute-start(bf16[32,2304]{1,0:T(8,128)(2,1)} %get-tuple-element.26), channel_id=1, source_target_pairs={{0,2},{1,3},{2,0},{3,1},{4,6},{5,7},{6,4},{7,5},{8,10},{9,11},{10,... | collective-permute-start | bytes 442376 | tf_op jit(solution)/shard_map/ppermute | solution.py:103
  29.7 5.4 %collective-permute-start.13 = (bf16[16,2304]{1,0:T(8,128)(2,1)S(1)}, bf16[16,2304]{1,0:T(8,128)(2,1)S(1)}, u32[]{:S(2)}, u32[]{:S(2)}) collective-permute-start(bf16[16,2304]{1,0:T(8,128)(2,1)S(1)} %get-tuple-element.27), channel_id=1, source_target_pairs={{0,8},{1,9},{2,10},{3,11},{4,12},{5,13},{6,14},{7,15},{8,0},{9,1},... | collective-permute-start | bytes 221192 | tf_op jit(solution)/shard_map/ppermute | solution.py:103
  31.9 6.2 %collective-permute-start.14 = (bf16[16,2304]{1,0:T(8,128)(2,1)S(1)}, bf16[16,2304]{1,0:T(8,128)(2,1)S(1)}, u32[]{:S(2)}, u32[]{:S(2)}) collective-permute-start(bf16[16,2304]{1,0:T(8,128)(2,1)S(1)} %get-tuple-element.28), channel_id=1, source_target_pairs={{0,12},{1,13},{2,14},{3,15},{4,8},{5,9},{6,10},{7,11},{8,4},{9,5},... | collective-permute-start | bytes 221192 | tf_op jit(solution)/shard_map/ppermute | solution.py:103
  33.4 22.8 %copy-start.4 = (f32[128,2304]{1,0:T(8,128)S(1)}, f32[128,2304]{1,0:T(8,128)}, u32[]{:S(2)}) copy-start(f32[128,2304]{1,0:T(8,128)} %refs_7_.1) | copy-start | bytes 3538948
  33.8 5.0 %collective-permute-start.11 = (bf16[16,2304]{1,0:T(8,128)(2,1)S(1)}, bf16[16,2304]{1,0:T(8,128)(2,1)S(1)}, u32[]{:S(2)}, u32[]{:S(2)}) collective-permute-start(bf16[16,2304]{1,0:T(8,128)(2,1)S(1)} %slice.97), channel_id=1, source_target_pairs={{0,4},{1,5},{2,6},{3,7},{4,0},{5,1},{6,2},{7,3},{8,12},{9,13},{10,... | collective-permute-start | bytes 221192 | tf_op jit(solution)/shard_map/ppermute | solution.py:103
  33.9 5.0 %collective-permute-start.15 = (bf16[128,128]{0,1:T(8,128)(2,1)S(1)}, bf16[128,128]{0,1:T(8,128)(2,1)S(1)}, u32[]{:S(2)}, u32[]{:S(2)}) collective-permute-start(bf16[128,128]{0,1:T(8,128)(2,1)S(1)} %get-tuple-element.30), channel_id=1, source_target_pairs={{0,1},{1,0},{2,3},{3,2},{4,5},{5,4},{6,7},{7,6},{8,9},{9,8},{10,11... | collective-permute-start | bytes 98312 | tf_op jit(solution)/shard_map/ppermute | solution.py:110
  38.8 17.5 %copy-start.3 = (f32[128,2304]{1,0:T(8,128)S(1)}, f32[128,2304]{1,0:T(8,128)}, u32[]{:S(2)}) copy-start(f32[128,2304]{1,0:T(8,128)} %refs_6_.1) | copy-start | bytes 3538948
  38.9 16.7 %copy-start.6 = (bf16[16,2304]{1,0:T(8,128)(2,1)}, bf16[16,2304]{1,0:T(8,128)(2,1)S(1)}, u32[]{:S(2)}) copy-start(bf16[16,2304]{1,0:T(8,128)(2,1)S(1)} %fusion.17) | copy-start | bytes 221188
  38.9 15.3 %collective-permute-start.23 = (bf16[16,2304]{1,0:T(8,128)(2,1)S(1)}, bf16[16,2304]{1,0:T(8,128)(2,1)S(1)}, u32[]{:S(2)}, u32[]{:S(2)}) collective-permute-start(bf16[16,2304]{1,0:T(8,128)(2,1)S(1)} %fusion.17), channel_id=1, source_target_pairs={{0,2},{1,3},{2,0},{3,1},{4,6},{5,7},{6,4},{7,5},{8,10},{9,11},{10,... | collective-permute-start | bytes 221192 | tf_op jit(solution)/shard_map/ppermute | solution.py:103
  41.3 6.3 %collective-permute-start.21 = (bf16[16,2304]{1,0:T(8,128)(2,1)S(1)}, bf16[16,2304]{1,0:T(8,128)(2,1)S(1)}, u32[]{:S(2)}, u32[]{:S(2)}) collective-permute-start(bf16[16,2304]{1,0:T(8,128)(2,1)S(1)} %fusion.17), channel_id=1, source_target_pairs={{0,12},{1,13},{2,14},{3,15},{4,8},{5,9},{6,10},{7,11},{8,4},{9,5},... | collective-permute-start | bytes 221192 | tf_op jit(solution)/shard_map/ppermute | solution.py:103
  43.0 5.9 %collective-permute-start.19 = (bf16[16,2304]{1,0:T(8,128)(2,1)S(1)}, bf16[16,2304]{1,0:T(8,128)(2,1)S(1)}, u32[]{:S(2)}, u32[]{:S(2)}) collective-permute-start(bf16[16,2304]{1,0:T(8,128)(2,1)S(1)} %fusion.17), channel_id=1, source_target_pairs={{0,4},{1,5},{2,6},{3,7},{4,0},{5,1},{6,2},{7,3},{8,12},{9,13},{10,... | collective-permute-start | bytes 221192 | tf_op jit(solution)/shard_map/ppermute | solution.py:103
  43.0 6.6 %collective-permute-start.17 = (bf16[16,2304]{1,0:T(8,128)(2,1)S(1)}, bf16[16,2304]{1,0:T(8,128)(2,1)S(1)}, u32[]{:S(2)}, u32[]{:S(2)}) collective-permute-start(bf16[16,2304]{1,0:T(8,128)(2,1)S(1)} %fusion.17), channel_id=1, source_target_pairs={{0,8},{1,9},{2,10},{3,11},{4,12},{5,13},{6,14},{7,15},{8,0},{9,1},... | collective-permute-start | bytes 221192 | tf_op jit(solution)/shard_map/ppermute | solution.py:103
  47.6 6.6 %collective-permute-start.22 = (bf16[16,2304]{1,0:T(8,128)(2,1)S(1)}, bf16[16,2304]{1,0:T(8,128)(2,1)S(1)}, u32[]{:S(2)}, u32[]{:S(2)}) collective-permute-start(bf16[16,2304]{1,0:T(8,128)(2,1)S(1)} %collective-permute-done.21), channel_id=1, source_target_pairs={{0,2},{1,3},{2,0},{3,1},{4,6},{5,7},{6,4},{7,5},{8,10},{9,11},{10,... | collective-permute-start | bytes 221192 | tf_op jit(solution)/shard_map/ppermute | solution.py:103
  48.9 5.2 %collective-permute-start.20 = (bf16[16,2304]{1,0:T(8,128)(2,1)S(1)}, bf16[16,2304]{1,0:T(8,128)(2,1)S(1)}, u32[]{:S(2)}, u32[]{:S(2)}) collective-permute-start(bf16[16,2304]{1,0:T(8,128)(2,1)S(1)} %collective-permute-done.19), channel_id=1, source_target_pairs={{0,2},{1,3},{2,0},{3,1},{4,6},{5,7},{6,4},{7,5},{8,10},{9,11},{10,... | collective-permute-start | bytes 221192 | tf_op jit(solution)/shard_map/ppermute | solution.py:103
  49.6 4.5 %collective-permute-start.18 = (bf16[16,2304]{1,0:T(8,128)(2,1)S(1)}, bf16[16,2304]{1,0:T(8,128)(2,1)S(1)}, u32[]{:S(2)}, u32[]{:S(2)}) collective-permute-start(bf16[16,2304]{1,0:T(8,128)(2,1)S(1)} %collective-permute-done.17), channel_id=1, source_target_pairs={{0,2},{1,3},{2,0},{3,1},{4,6},{5,7},{6,4},{7,5},{8,10},{9,11},{10,... | collective-permute-start | bytes 221192 | tf_op jit(solution)/shard_map/ppermute | solution.py:103
  54.2 2.1 %collective-permute-start.24 = (bf16[128,2304]{1,0:T(8,128)(2,1)S(1)}, bf16[128,2304]{1,0:T(8,128)(2,1)S(1)}, u32[]{:S(2)}, u32[]{:S(2)}) collective-permute-start(bf16[128,2304]{1,0:T(8,128)(2,1)S(1)} %constant_dynamic-update-slice_fusion.10.refs_0_), channel_id=1, source_target_pairs={{0,1},{1,0},{2,3},{3,2},{4,5},{5,4},{6,7},{7,6},{8,9},{9,8},{10,11... | collective-permute-start | bytes 1769480 | tf_op jit(solution)/shard_map/ppermute | solution.py:110
  (3 other events, 12.5 us)

commit v10 on v8

--- a/solution.py
+++ b/solution.py
@@ -19,13 +19,14 @@
     )
 
 
-def update_kernel(columns, block, rows_total, codes_across, centered, *refs):
+def update_kernel(columns, rows_total, codes_across, centered, *refs):
     blocks = len(refs) - 20
     errors, (encoder, decoder) = refs[:blocks], refs[blocks : blocks + 2]
     moments = refs[blocks + 2 : blocks + 6]
     outs = refs[blocks + 6 : blocks + 12]
     error_all, *held, sem = refs[blocks + 12 :]
     tiles = encoder.shape[1] // columns
+    part = min(32, encoder.shape[0])
 
     def write(t, i):
         at = pl.ds(t * columns, columns)
@@ -33,10 +34,8 @@
 
     start = 0
     for one in errors:
-        for first in (0, block):
-            for at in range(first, one.shape[0], 2 * block):
-                error_all[pl.ds(start, block), :] = one[pl.ds(at, block), :]
-                start += block
+        error_all[pl.ds(start, one.shape[0]), :] = one[...]
+        start += one.shape[0]
     first = (1.0 - beta_first) / rows_total
     second = (1.0 - beta_second) / (rows_total * rows_total)
 
@@ -44,15 +43,18 @@
         for t in range(tiles):
             at = pl.ds(t * columns, columns)
             total = jnp.dot(left, right[:, at], preferred_element_type=jnp.float32)
-            moment = beta_first * moments[2 * which][:, at] + first * total
-            square = beta_second * moments[2 * which + 1][:, at] + second * (total * total)
-            root = square * lax.rsqrt(square)
-            held[3 * which][:, at] = (
-                weight[:, at].astype(jnp.float32)
-                - step_rate * moment * pl.reciprocal(root + adam_epsilon, approx=True)
-            ).astype(jnp.bfloat16)
-            held[3 * which + 1][:, at] = moment
-            held[3 * which + 2][:, at] = square
+            for start in range(0, total.shape[0], part):
+                some = (pl.ds(start, part), at)
+                grad = total[start : start + part]
+                moment = beta_first * moments[2 * which][some] + first * grad
+                square = beta_second * moments[2 * which + 1][some] + second * (grad * grad)
+                root = square * lax.rsqrt(square)
+                held[3 * which][some] = (
+                    weight[some].astype(jnp.float32)
+                    - step_rate * moment * pl.reciprocal(root + adam_epsilon, approx=True)
+                ).astype(jnp.bfloat16)
+                held[3 * which + 1][some] = moment
+                held[3 * which + 2][some] = square
             for i in range(3 * which, 3 * which + 3):
                 write(t, i).start()
 
@@ -66,7 +68,7 @@
             write(t, i).wait()
 
 
-def update(total_rows, codes_across, centered, errors, block, weights, moments):
+def update(total_rows, codes_across, centered, errors, weights, moments):
     latents, width = weights[0].shape
     rows = centered.shape[0]
     columns = next(c for c in (256, 128, width) if width % c == 0)
@@ -76,7 +78,7 @@
     wide = pltpu.VMEM((latents, width), jnp.float32)
     narrow = pltpu.VMEM((latents, width), jnp.bfloat16)
     return pl.pallas_call(
-        functools.partial(update_kernel, columns, block, float(total_rows)),
+        functools.partial(update_kernel, columns, float(total_rows)),
         out_shape=(half, full, full, half, full, full),
         in_specs=[vmem] * (len(errors) + 8),
         out_specs=[pl.BlockSpec(memory_space=pl.ANY)] * 6,
@@ -115,6 +117,10 @@
 def gather_chips(block, chips):
     even = [block] + [to_chip(block, k) for k in range(2, chips, 2)]
     return even, [to_chip(one, 1) for one in even]
+
+
+def in_turn(even, odd):
+    return [one for both in zip(even, odd) for one in both]
 
 
 def body(
@@ -132,11 +138,9 @@
     latents_here = encoder.shape[0]
     size = lax.axis_size("latent")
     chips = size // 2
-    pairs = chips // 2
     total_rows = rows_here * size
 
-    even, odd = gather_chips(activations, chips)
-    rows_core = jnp.concatenate(even + odd, 0)
+    rows_core = jnp.concatenate(in_turn(*gather_chips(activations, chips)), 0)
     encoder_both = jnp.concatenate([encoder, to_other_core(encoder)], 0)
     decoder_both = jnp.concatenate([decoder, to_other_core(decoder)], 0)
     bias_both = jnp.concatenate([encoder_bias, to_other_core(encoder_bias)], 0)
@@ -148,31 +152,31 @@
     other_codes = to_other_core(codes[:, latents_here:])
     other_centered = to_other_core(centered)
 
-    split = 2 * rows_here
-    given = jnp.dot(
-        codes[pairs * rows_here :], decoder_both, preferred_element_type=jnp.float32
-    ).astype(jnp.bfloat16)
-
-    def pair_sums(first, last):
-        return jnp.dot(
-            codes[first:last], decoder_both, preferred_element_type=jnp.float32
-        ) + to_chip(given[first:last], 1).astype(jnp.float32)
-
-    far = pair_sums(split, pairs * rows_here).astype(jnp.bfloat16)
-    near = pair_sums(0, split)
-    summed = near[:rows_here] + to_chip(near[rows_here:].astype(jnp.bfloat16), 2).astype(
-        jnp.float32
-    )
-    for k in range(2, pairs):
-        block = far[(k - 2) * rows_here : (k - 1) * rows_here]
-        summed = summed + to_chip(block, 2 * k).astype(jnp.float32)
+    partial_sums = jnp.dot(codes, decoder_both, preferred_element_type=jnp.float32)
+    parts = [partial_sums[k * rows_here : (k + 1) * rows_here] for k in range(chips)]
+
+    def pair_sums(first, last, after=None):
+        given = jnp.concatenate(parts[first + 1 : last : 2], 0).astype(jnp.bfloat16)
+        came = to_chip(given, 1)
+        if after is not None:
+            came, _ = lax.optimization_barrier((came, after))
+        return [
+            parts[k] + came[at * rows_here : (at + 1) * rows_here].astype(jnp.float32)
+            for at, k in enumerate(range(first, last, 2))
+        ]
+
+    far = [one.astype(jnp.bfloat16) for one in pair_sums(4, chips)]
+    own, near = pair_sums(0, 4, far)
+    summed = own + to_chip(near.astype(jnp.bfloat16), 2).astype(jnp.float32)
+    for k, one in enumerate(far, 2):
+        summed = summed + to_chip(one, 2 * k).astype(jnp.float32)
     row_error = (summed - centered[:rows_here].astype(jnp.float32)).astype(jnp.bfloat16)
 
     row_error, other_codes, other_centered = lax.optimization_barrier(
         (row_error, other_codes, other_centered)
     )
-    even, odd = gather_chips(row_error, chips)
-    errors = jnp.concatenate([one for both in zip(even, odd) for one in both], 0)
+    blocks = in_turn(*gather_chips(row_error, chips))
+    errors = [jnp.concatenate(blocks[:4], 0), jnp.concatenate(blocks[4:], 0)]
     codes_across = jnp.concatenate([codes[:, :latents_here], other_codes], 0).T
     centered_all = jnp.concatenate([centered, other_centered], 0)
     (
@@ -186,8 +190,7 @@
         total_rows,
         codes_across,
         centered_all,
-        (errors, to_other_core(errors)),
-        rows_here,
+        errors + [to_other_core(one) for one in errors],
         (encoder, decoder),
         (encoder_moment, encoder_square, decoder_moment, decoder_square),
     )

time: 55.1 us -> 55.4 us (level)
  starting transfers between devices: 27.5 us -> 25.4 us
  waiting for transfers between devices: 19.9 us -> 22 us
  matrix products: 1.68 us -> 0.83 us
  other arithmetic: 0.25 us -> 0.97 us
    ppermute x19, starting transfers between devices: 26.8 us -> 24.2 us  [to_chip(): lax.ppermute(block, 'latent', [(i, i ^ 2 * distance) for i in range(size)])]
    ppermute x19, waiting for transfers between devices: 17.9 us -> 20.4 us  [to_chip(): lax.ppermute(block, 'latent', [(i, i ^ 2 * distance) for i in range(size)])]
    dot_general x3 -> x1, matrix products: 1.19 us -> 0.35 us  [body(): jnp.dot(codes, decoder_both, preferred_element_type=jnp.float32)]
    concatenate x1, other arithmetic: 0.01 us -> 0.66 us  [body(): bias_both = jnp.concatenate([encoder_bias, to_other_core(encoder_bias)], 0)]
    ppermute x6 -> x7, starting transfers between devices: 0.65 us -> 1.2 us  [to_other_core(): return lax.ppermute(block, 'latent', [(i, i ^ 1) for i in range(size)])]
    ppermute x6 -> x7, waiting for transfers between devices: 1.98 us -> 1.6 us  [to_other_core(): return lax.ppermute(block, 'latent', [(i, i ^ 1) for i in range(size)])]
    unnamed x35 -> x29, local copies, waits for them, and re-layouts: 1.24 us -> 1.5 us
  transfers between devices with their start and end apart: 25 -> 26, of which waited for: 9 -> 11; matrix products, arithmetic and copies ran while one was open for 4% -> 5% of each run, Pallas kernels for 0% -> 0%
where the time goes in v10:
time: 55.4 us; the launch traced here: 55.1 us
  starting transfers between devices  25.4 us (46%)
  waiting for transfers between devices  22 us (40%)
  Pallas kernels  3.38 us (6%)
  local copies, waits for them, and re-layouts  1.55 us (3%)
  other arithmetic  0.97 us (2%)
  between operations  0.93 us (2%)
  matrix products  0.83 us (1%)
    ppermute x19, starting transfers between devices, to_chip(): lax.ppermute(block, 'latent', [(i, i ^ 2 * distance) for i in range(size)])  24.2 us
    ppermute x19, waiting for transfers between devices, to_chip(): lax.ppermute(block, 'latent', [(i, i ^ 2 * distance) for i in range(size)])  20.4 us
    pallas_call x1, Pallas kernels, update(): pl.pallas_call(functools.partial(update_kernel, columns, float(total_rows...  3.38 us
    ppermute x7, waiting for transfers between devices, to_other_core(): return lax.ppermute(block, 'latent', [(i, i ^ 1) for i in range(size)])  1.6 us
    unnamed x29, local copies, waits for them, and re-layouts  1.5 us
    ppermute x7, starting transfers between devices, to_other_core(): return lax.ppermute(block, 'latent', [(i, i ^ 1) for i in range(size)])  1.2 us
  transfers between devices with their start and end apart: 26, of which 11 were waited for; matrix products, arithmetic and copies ran while one was open for 5% of the time, Pallas kernels for 0%

profile of v10, /device:TPU:0, one launch (start us, length us, event | category | flops | bytes accessed | tf_op | source)
XLA Modules:
  0.0 55.1 jit_solution(8995311922998811517)
XLA Ops:
  0.7 4.1 %collective-permute-start.3 = (bf16[16,2304]{1,0:T(8,128)(2,1)}, bf16[16,2304]{1,0:T(8,128)(2,1)S(1)}, u32[]{:S(2)}, u32[]{:S(2)}) collective-permute-start(bf16[16,2304]{1,0:T(8,128)(2,1)} %param.9), channel_id=1, source_target_pairs={{0,8},{1,9},{2,10},{3,11},{4,12},{5,13},{6,14},{7,15},{8,0},{9,1},... | collective-permute-start | bytes 221192 | tf_op jit(solution)/shard_map/ppermute | solution.py:107
  4.8 1.6 %collective-permute-start.1 = (bf16[16,2304]{1,0:T(8,128)(2,1)}, bf16[16,2304]{1,0:T(8,128)(2,1)S(1)}, u32[]{:S(2)}, u32[]{:S(2)}) collective-permute-start(bf16[16,2304]{1,0:T(8,128)(2,1)} %param.9), channel_id=1, source_target_pairs={{0,4},{1,5},{2,6},{3,7},{4,0},{5,1},{6,2},{7,3},{8,12},{9,13},{10,... | collective-permute-start | bytes 221192 | tf_op jit(solution)/shard_map/ppermute | solution.py:107
  6.3 1.5 %collective-permute-start = (bf16[16,2304]{1,0:T(8,128)(2,1)}, bf16[16,2304]{1,0:T(8,128)(2,1)S(1)}, u32[]{:S(2)}, u32[]{:S(2)}) collective-permute-start(bf16[16,2304]{1,0:T(8,128)(2,1)} %param.9), channel_id=1, source_target_pairs={{0,2},{1,3},{2,0},{3,1},{4,6},{5,7},{6,4},{7,5},{8,10},{9,11},{10,... | collective-permute-start | bytes 221192 | tf_op jit(solution)/shard_map/ppermute | solution.py:107
  8.1 0.9 %constant_dynamic-update-slice_fusion.7 = bf16[128,2304]{1,0:T(8,128)(2,1)S(1)} fusion(bf16[16,2304]{1,0:T(8,128)(2,1)} %param.9), kind=kLoop, calls=%fused_computation.35 | loop fusion | bytes 147456
  9.5 0.7 %pad_maximum_fusion.3 = f32[256]{0:T(256)S(1)} fusion(f32[128]{0:T(128)S(1)} %collective-permute-done.8, f32[128]{0:T(128)} %param.11), kind=kLoop, calls=%fused_computation.44 | loop fusion | flops 256 | bytes 2048 | tf_op jit(solution)/shard_map/concatenate | solution.py:146
  11.0 1.6 %collective-permute-start.2 = (bf16[16,2304]{1,0:T(8,128)(2,1)S(1)}, bf16[16,2304]{1,0:T(8,128)(2,1)S(1)}, u32[]{:S(2)}, u32[]{:S(2)}) collective-permute-start(bf16[16,2304]{1,0:T(8,128)(2,1)S(1)} %collective-permute-done.1), channel_id=1, source_target_pairs={{0,2},{1,3},{2,0},{3,1},{4,6},{5,7},{6,4},{7,5},{8,10},{9,11},{10,... | collective-permute-start | bytes 221192 | tf_op jit(solution)/shard_map/ppermute | solution.py:107
  12.6 1.6 %collective-permute-done.5 = bf16[16,2304]{1,0:T(8,128)(2,1)S(1)} collective-permute-done((bf16[16,2304]{1,0:T(8,128)(2,1)}, bf16[16,2304]{1,0:T(8,128)(2,1)S(1)}, u32[]{:S(2)}, u32[]{:S(2)}) %collective-permute-start.5) | collective-permute-done | bytes 73760 | tf_op jit(solution)/shard_map/ppermute | solution.py:107
  14.2 0.5 collective-permute-start.6
  14.7 2.5 %collective-permute-done.2 = bf16[16,2304]{1,0:T(8,128)(2,1)S(1)} collective-permute-done((bf16[16,2304]{1,0:T(8,128)(2,1)S(1)}, bf16[16,2304]{1,0:T(8,128)(2,1)S(1)}, u32[]{:S(2)}, u32[]{:S(2)}) %collective-permute-start.2) | collective-permute-done | bytes 73760 | tf_op jit(solution)/shard_map/ppermute | solution.py:107
  17.3 1.3 %collective-permute-done.6 = bf16[16,2304]{1,0:T(8,128)(2,1)S(1)} collective-permute-done((bf16[16,2304]{1,0:T(8,128)(2,1)S(1)}, bf16[16,2304]{1,0:T(8,128)(2,1)S(1)}, u32[]{:S(2)}, u32[]{:S(2)}) %collective-permute-start.6) | collective-permute-done | bytes 73760 | tf_op jit(solution)/shard_map/ppermute | solution.py:107
  18.8 0.5 fusion.14
  19.3 0.5 copy-done
  20.2 0.6 %collective-permute-start.11 = (bf16[32,2304]{1,0:T(8,128)(2,1)S(1)}, bf16[32,2304]{1,0:T(8,128)(2,1)S(1)}, u32[]{:S(2)}, u32[]{:S(2)}) collective-permute-start(bf16[32,2304]{1,0:T(8,128)(2,1)S(1)} %pad_maximum_fusion.2), channel_id=1, source_target_pairs={{0,2},{1,3},{2,0},{3,1},{4,6},{5,7},{6,4},{7,5},{8,10},{9,11},{10,... | collective-permute-start | bytes 442376 | tf_op jit(solution)/shard_map/ppermute | solution.py:107
  20.7 1.6 %collective-permute-start.10 = (bf16[32,2304]{1,0:T(8,128)(2,1)S(1)}, bf16[32,2304]{1,0:T(8,128)(2,1)S(1)}, u32[]{:S(2)}, u32[]{:S(2)}) collective-permute-start(bf16[32,2304]{1,0:T(8,128)(2,1)S(1)} %pad_maximum_fusion.1), channel_id=1, source_target_pairs={{0,2},{1,3},{2,0},{3,1},{4,6},{5,7},{6,4},{7,5},{8,10},{9,11},{10,... | collective-permute-start | bytes 442376 | tf_op jit(solution)/shard_map/ppermute | solution.py:107
  22.3 4.6 %collective-permute-done.11 = bf16[32,2304]{1,0:T(8,128)(2,1)S(1)} collective-permute-done((bf16[32,2304]{1,0:T(8,128)(2,1)S(1)}, bf16[32,2304]{1,0:T(8,128)(2,1)S(1)}, u32[]{:S(2)}, u32[]{:S(2)}) %collective-permute-start.11) | collective-permute-done | bytes 147488 | tf_op jit(solution)/shard_map/ppermute | solution.py:107
  27.0 1.3 %collective-permute-start.13 = (bf16[16,2304]{1,0:T(8,128)(2,1)S(1)}, bf16[16,2304]{1,0:T(8,128)(2,1)S(1)}, u32[]{:S(2)}, u32[]{:S(2)}) collective-permute-start(bf16[16,2304]{1,0:T(8,128)(2,1)S(1)} %get-tuple-element.27), channel_id=1, source_target_pairs={{0,8},{1,9},{2,10},{3,11},{4,12},{5,13},{6,14},{7,15},{8,0},{9,1},... | collective-permute-start | bytes 221192 | tf_op jit(solution)/shard_map/ppermute | solution.py:107
  28.3 2.0 %collective-permute-start.14 = (bf16[16,2304]{1,0:T(8,128)(2,1)S(1)}, bf16[16,2304]{1,0:T(8,128)(2,1)S(1)}, u32[]{:S(2)}, u32[]{:S(2)}) collective-permute-start(bf16[16,2304]{1,0:T(8,128)(2,1)S(1)} %get-tuple-element.28), channel_id=1, source_target_pairs={{0,12},{1,13},{2,14},{3,15},{4,8},{5,9},{6,10},{7,11},{8,4},{9,5},... | collective-permute-start | bytes 221192 | tf_op jit(solution)/shard_map/ppermute | solution.py:107
  30.3 0.6 %collective-permute-start.12 = (bf16[16,2304]{1,0:T(8,128)(2,1)S(1)}, bf16[16,2304]{1,0:T(8,128)(2,1)S(1)}, u32[]{:S(2)}, u32[]{:S(2)}) collective-permute-start(bf16[16,2304]{1,0:T(8,128)(2,1)S(1)} %fusion.17), channel_id=1, source_target_pairs={{0,4},{1,5},{2,6},{3,7},{4,0},{5,1},{6,2},{7,3},{8,12},{9,13},{10,... | collective-permute-start | bytes 221192 | tf_op jit(solution)/shard_map/ppermute | solution.py:107
  30.8 3.8 %collective-permute-done.13 = bf16[16,2304]{1,0:T(8,128)(2,1)S(1)} collective-permute-done((bf16[16,2304]{1,0:T(8,128)(2,1)S(1)}, bf16[16,2304]{1,0:T(8,128)(2,1)S(1)}, u32[]{:S(2)}, u32[]{:S(2)}) %collective-permute-start.13) | collective-permute-done | bytes 73760 | tf_op jit(solution)/shard_map/ppermute | solution.py:107
  34.7 0.7 %collective-permute-done.12 = bf16[16,2304]{1,0:T(8,128)(2,1)S(1)} collective-permute-done((bf16[16,2304]{1,0:T(8,128)(2,1)S(1)}, bf16[16,2304]{1,0:T(8,128)(2,1)S(1)}, u32[]{:S(2)}, u32[]{:S(2)}) %collective-permute-start.12) | collective-permute-done | bytes 73760 | tf_op jit(solution)/shard_map/ppermute | solution.py:107
  35.5 2.2 %collective-permute-start.22 = (bf16[16,2304]{1,0:T(8,128)(2,1)S(1)}, bf16[16,2304]{1,0:T(8,128)(2,1)S(1)}, u32[]{:S(2)}, u32[]{:S(2)}) collective-permute-start(bf16[16,2304]{1,0:T(8,128)(2,1)S(1)} %fusion.24), channel_id=1, source_target_pairs={{0,12},{1,13},{2,14},{3,15},{4,8},{5,9},{6,10},{7,11},{8,4},{9,5},... | collective-permute-start | bytes 221192 | tf_op jit(solution)/shard_map/ppermute | solution.py:107
  37.6 2.3 %collective-permute-start.18 = (bf16[16,2304]{1,0:T(8,128)(2,1)S(1)}, bf16[16,2304]{1,0:T(8,128)(2,1)S(1)}, u32[]{:S(2)}, u32[]{:S(2)}) collective-permute-start(bf16[16,2304]{1,0:T(8,128)(2,1)S(1)} %fusion.24), channel_id=1, source_target_pairs={{0,4},{1,5},{2,6},{3,7},{4,0},{5,1},{6,2},{7,3},{8,12},{9,13},{10,... | collective-permute-start | bytes 221192 | tf_op jit(solution)/shard_map/ppermute | solution.py:107
  39.9 0.7 %collective-permute-start.17 = (bf16[16,2304]{1,0:T(8,128)(2,1)S(1)}, bf16[16,2304]{1,0:T(8,128)(2,1)S(1)}, u32[]{:S(2)}, u32[]{:S(2)}) collective-permute-start(bf16[16,2304]{1,0:T(8,128)(2,1)S(1)} %fusion.24), channel_id=1, source_target_pairs={{0,2},{1,3},{2,0},{3,1},{4,6},{5,7},{6,4},{7,5},{8,10},{9,11},{10,... | collective-permute-start | bytes 221192 | tf_op jit(solution)/shard_map/ppermute | solution.py:107
  40.6 2.6 %collective-permute-done.20 = bf16[16,2304]{1,0:T(8,128)(2,1)S(1)} collective-permute-done((bf16[16,2304]{1,0:T(8,128)(2,1)S(1)}, bf16[16,2304]{1,0:T(8,128)(2,1)S(1)}, u32[]{:S(2)}, u32[]{:S(2)}) %collective-permute-start.20) | collective-permute-done | bytes 73760 | tf_op jit(solution)/shard_map/ppermute | solution.py:107
  43.3 1.1 %collective-permute-start.21 = (bf16[16,2304]{1,0:T(8,128)(2,1)S(1)}, bf16[16,2304]{1,0:T(8,128)(2,1)S(1)}, u32[]{:S(2)}, u32[]{:S(2)}) collective-permute-start(bf16[16,2304]{1,0:T(8,128)(2,1)S(1)} %collective-permute-done.20), channel_id=1, source_target_pairs={{0,2},{1,3},{2,0},{3,1},{4,6},{5,7},{6,4},{7,5},{8,10},{9,11},{10,... | collective-permute-start | bytes 221192 | tf_op jit(solution)/shard_map/ppermute | solution.py:107
  44.4 1.0 %collective-permute-start.23 = (bf16[16,2304]{1,0:T(8,128)(2,1)S(1)}, bf16[16,2304]{1,0:T(8,128)(2,1)S(1)}, u32[]{:S(2)}, u32[]{:S(2)}) collective-permute-start(bf16[16,2304]{1,0:T(8,128)(2,1)S(1)} %collective-permute-done.22), channel_id=1, source_target_pairs={{0,2},{1,3},{2,0},{3,1},{4,6},{5,7},{6,4},{7,5},{8,10},{9,11},{10,... | collective-permute-start | bytes 221192 | tf_op jit(solution)/shard_map/ppermute | solution.py:107
  45.4 1.1 %collective-permute-start.19 = (bf16[16,2304]{1,0:T(8,128)(2,1)S(1)}, bf16[16,2304]{1,0:T(8,128)(2,1)S(1)}, u32[]{:S(2)}, u32[]{:S(2)}) collective-permute-start(bf16[16,2304]{1,0:T(8,128)(2,1)S(1)} %collective-permute-done.18), channel_id=1, source_target_pairs={{0,2},{1,3},{2,0},{3,1},{4,6},{5,7},{6,4},{7,5},{8,10},{9,11},{10,... | collective-permute-start | bytes 221192 | tf_op jit(solution)/shard_map/ppermute | solution.py:107
  46.5 3.2 %collective-permute-done.19 = bf16[16,2304]{1,0:T(8,128)(2,1)S(1)} collective-permute-done((bf16[16,2304]{1,0:T(8,128)(2,1)S(1)}, bf16[16,2304]{1,0:T(8,128)(2,1)S(1)}, u32[]{:S(2)}, u32[]{:S(2)}) %collective-permute-start.19) | collective-permute-done | bytes 73760 | tf_op jit(solution)/shard_map/ppermute | solution.py:107
  49.8 0.6 %collective-permute-start.25 = (bf16[64,2304]{1,0:T(8,128)(2,1)S(1)}, bf16[64,2304]{1,0:T(8,128)(2,1)S(1)}, u32[]{:S(2)}, u32[]{:S(2)}) collective-permute-start(bf16[64,2304]{1,0:T(8,128)(2,1)S(1)} %constant_dynamic-update-slice_fusion.12.refs_1_), channel_id=1, source_target_pairs={{0,1},{1,0},{2,3},{3,2},{4,5},{5,4},{6,7},{7,6},{8,9},{9,8},{10,11... | collective-permute-start | bytes 884744 | tf_op jit(solution)/shard_map/ppermute | solution.py:114
  50.5 0.8 %collective-permute-done.24.refs_2_ = bf16[64,2304]{1,0:T(8,128)(2,1)S(1)} collective-permute-done((bf16[64,2304]{1,0:T(8,128)(2,1)S(1)}, bf16[64,2304]{1,0:T(8,128)(2,1)S(1)}, u32[]{:S(2)}, u32[]{:S(2)}) %collective-permute-start.24) | collective-permute-done | bytes 294944 | tf_op jit(solution)/shard_map/ppermute | solution.py:114
  51.3 0.4 collective-permute-done.25.refs_3_
  51.8 3.4 %update.1 = (bf16[128,2304]{1,0:T(8,128)(2,1)}, f32[128,2304]{1,0:T(8,128)}, f32[128,2304]{1,0:T(8,128)}, bf16[128,2304]{1,0:T(8,128)(2,1)}, f32[128,2304]{1,0:T(8,128)}, /*index=5*/f32[128,2304]{1,0:T(8,128)}) custom-call(bf16[128,256]{1,0:T(8,128)(2,1)S(1)} %maximum_bitcast_fusion.codes_across, bf16[256,2304]{1,0:T(8,128)(2,1)S(1)} %pad_maximum_fusion.centered, ...), custom_call_target="tpu_custom_call" | custom-call | flops 452984832 | bytes 12976128 | tf_op jit(solution)/shard_map/update/pallas_call | solution.py:80
  (66 shorter events, 2.5 us)
Async XLA Ops:
  0.6 18.2 %copy-start.5 = (bf16[128,2304]{1,0:T(8,128)(2,1)S(1)}, bf16[128,2304]{1,0:T(8,128)(2,1)}, u32[]{:S(2)}) copy-start(bf16[128,2304]{1,0:T(8,128)(2,1)} %refs_4_.1) | copy-start | bytes 1769476
  0.6 17.9 %copy-start.7 = (f32[2304]{0:T(1024)S(1)}, f32[2304]{0:T(1024)}, u32[]{:S(2)}) copy-start(f32[2304]{0:T(1024)} %param.13) | copy-start | bytes 27652
  0.7 9.6 %collective-permute-start.3 = (bf16[16,2304]{1,0:T(8,128)(2,1)}, bf16[16,2304]{1,0:T(8,128)(2,1)S(1)}, u32[]{:S(2)}, u32[]{:S(2)}) collective-permute-start(bf16[16,2304]{1,0:T(8,128)(2,1)} %param.9), channel_id=1, source_target_pairs={{0,8},{1,9},{2,10},{3,11},{4,12},{5,13},{6,14},{7,15},{8,0},{9,1},... | collective-permute-start | bytes 221192 | tf_op jit(solution)/shard_map/ppermute | solution.py:107
  4.8 5.8 %collective-permute-start.1 = (bf16[16,2304]{1,0:T(8,128)(2,1)}, bf16[16,2304]{1,0:T(8,128)(2,1)S(1)}, u32[]{:S(2)}, u32[]{:S(2)}) collective-permute-start(bf16[16,2304]{1,0:T(8,128)(2,1)} %param.9), channel_id=1, source_target_pairs={{0,4},{1,5},{2,6},{3,7},{4,0},{5,1},{6,2},{7,3},{8,12},{9,13},{10,... | collective-permute-start | bytes 221192 | tf_op jit(solution)/shard_map/ppermute | solution.py:107
  6.3 4.7 %collective-permute-start = (bf16[16,2304]{1,0:T(8,128)(2,1)}, bf16[16,2304]{1,0:T(8,128)(2,1)S(1)}, u32[]{:S(2)}, u32[]{:S(2)}) collective-permute-start(bf16[16,2304]{1,0:T(8,128)(2,1)} %param.9), channel_id=1, source_target_pairs={{0,2},{1,3},{2,0},{3,1},{4,6},{5,7},{6,4},{7,5},{8,10},{9,11},{10,... | collective-permute-start | bytes 221192 | tf_op jit(solution)/shard_map/ppermute | solution.py:107
  7.9 6.4 %collective-permute-start.5 = (bf16[16,2304]{1,0:T(8,128)(2,1)}, bf16[16,2304]{1,0:T(8,128)(2,1)S(1)}, u32[]{:S(2)}, u32[]{:S(2)}) collective-permute-start(bf16[16,2304]{1,0:T(8,128)(2,1)} %param.9), channel_id=1, source_target_pairs={{0,12},{1,13},{2,14},{3,15},{4,8},{5,9},{6,10},{7,11},{8,4},{9,5},... | collective-permute-start | bytes 221192 | tf_op jit(solution)/shard_map/ppermute | solution.py:107
  8.1 1.3 %collective-permute-start.8 = (f32[128]{0:T(128)}, f32[128]{0:T(128)S(1)}, u32[]{:S(2)}, u32[]{:S(2)}) collective-permute-start(f32[128]{0:T(128)} %param.11), channel_id=1, source_target_pairs={{0,1},{1,0},{2,3},{3,2},{4,5},{5,4},{6,7},{7,6},{8,9},{9,8},{10,11... | collective-permute-start | bytes 1544 | tf_op jit(solution)/shard_map/ppermute | solution.py:114
  9.3 9.5 %collective-permute-start.7 = (bf16[128,2304]{1,0:T(8,128)(2,1)}, bf16[128,2304]{1,0:T(8,128)(2,1)S(1)}, u32[]{:S(2)}, u32[]{:S(2)}) collective-permute-start(bf16[128,2304]{1,0:T(8,128)(2,1)} %refs_4_.1), channel_id=1, source_target_pairs={{0,1},{1,0},{2,3},{3,2},{4,5},{5,4},{6,7},{7,6},{8,9},{9,8},{10,11... | collective-permute-start | bytes 1769480 | tf_op jit(solution)/shard_map/ppermute | solution.py:114
  10.2 9.1 %collective-permute-start.9 = (bf16[128,2304]{1,0:T(8,128)(2,1)}, bf16[128,2304]{1,0:T(8,128)(2,1)S(1)}, u32[]{:S(2)}, u32[]{:S(2)}) collective-permute-start(bf16[128,2304]{1,0:T(8,128)(2,1)} %refs_5_.1), channel_id=1, source_target_pairs={{0,1},{1,0},{2,3},{3,2},{4,5},{5,4},{6,7},{7,6},{8,9},{9,8},{10,11... | collective-permute-start | bytes 1769480 | tf_op jit(solution)/shard_map/ppermute | solution.py:114
  10.6 6.7 %collective-permute-start.4 = (bf16[16,2304]{1,0:T(8,128)(2,1)S(1)}, bf16[16,2304]{1,0:T(8,128)(2,1)S(1)}, u32[]{:S(2)}, u32[]{:S(2)}) collective-permute-start(bf16[16,2304]{1,0:T(8,128)(2,1)S(1)} %collective-permute-done.3), channel_id=1, source_target_pairs={{0,2},{1,3},{2,0},{3,1},{4,6},{5,7},{6,4},{7,5},{8,10},{9,11},{10,... | collective-permute-start | bytes 221192 | tf_op jit(solution)/shard_map/ppermute | solution.py:107
  11.0 6.3 %collective-permute-start.2 = (bf16[16,2304]{1,0:T(8,128)(2,1)S(1)}, bf16[16,2304]{1,0:T(8,128)(2,1)S(1)}, u32[]{:S(2)}, u32[]{:S(2)}) collective-permute-start(bf16[16,2304]{1,0:T(8,128)(2,1)S(1)} %collective-permute-done.1), channel_id=1, source_target_pairs={{0,2},{1,3},{2,0},{3,1},{4,6},{5,7},{6,4},{7,5},{8,10},{9,11},{10,... | collective-permute-start | bytes 221192 | tf_op jit(solution)/shard_map/ppermute | solution.py:107
  14.2 4.4 %collective-permute-start.6 = (bf16[16,2304]{1,0:T(8,128)(2,1)S(1)}, bf16[16,2304]{1,0:T(8,128)(2,1)S(1)}, u32[]{:S(2)}, u32[]{:S(2)}) collective-permute-start(bf16[16,2304]{1,0:T(8,128)(2,1)S(1)} %collective-permute-done.5), channel_id=1, source_target_pairs={{0,2},{1,3},{2,0},{3,1},{4,6},{5,7},{6,4},{7,5},{8,10},{9,11},{10,... | collective-permute-start | bytes 221192 | tf_op jit(solution)/shard_map/ppermute | solution.py:107
  18.7 16.8 %collective-permute-start.16 = (bf16[128,2304]{1,0:T(8,128)(2,1)S(1)}, bf16[128,2304]{1,0:T(8,128)(2,1)S(1)}, u32[]{:S(2)}, u32[]{:S(2)}) collective-permute-start(bf16[128,2304]{1,0:T(8,128)(2,1)S(1)} %subtract_convert_fusion), channel_id=1, source_target_pairs={{0,1},{1,0},{2,3},{3,2},{4,5},{5,4},{6,7},{7,6},{8,9},{9,8},{10,11... | collective-permute-start | bytes 1769480 | tf_op jit(solution)/shard_map/ppermute | solution.py:114
  20.2 6.8 %collective-permute-start.11 = (bf16[32,2304]{1,0:T(8,128)(2,1)S(1)}, bf16[32,2304]{1,0:T(8,128)(2,1)S(1)}, u32[]{:S(2)}, u32[]{:S(2)}) collective-permute-start(bf16[32,2304]{1,0:T(8,128)(2,1)S(1)} %pad_maximum_fusion.2), channel_id=1, source_target_pairs={{0,2},{1,3},{2,0},{3,1},{4,6},{5,7},{6,4},{7,5},{8,10},{9,11},{10,... | collective-permute-start | bytes 442376 | tf_op jit(solution)/shard_map/ppermute | solution.py:107
  20.7 9.5 %collective-permute-start.10 = (bf16[32,2304]{1,0:T(8,128)(2,1)S(1)}, bf16[32,2304]{1,0:T(8,128)(2,1)S(1)}, u32[]{:S(2)}, u32[]{:S(2)}) collective-permute-start(bf16[32,2304]{1,0:T(8,128)(2,1)S(1)} %pad_maximum_fusion.1), channel_id=1, source_target_pairs={{0,2},{1,3},{2,0},{3,1},{4,6},{5,7},{6,4},{7,5},{8,10},{9,11},{10,... | collective-permute-start | bytes 442376 | tf_op jit(solution)/shard_map/ppermute | solution.py:107
  26.9 24.8 %copy-start.4 = (f32[128,2304]{1,0:T(8,128)S(1)}, f32[128,2304]{1,0:T(8,128)}, u32[]{:S(2)}) copy-start(f32[128,2304]{1,0:T(8,128)} %refs_9_.1) | copy-start | bytes 3538948
  27.0 7.7 %collective-permute-start.13 = (bf16[16,2304]{1,0:T(8,128)(2,1)S(1)}, bf16[16,2304]{1,0:T(8,128)(2,1)S(1)}, u32[]{:S(2)}, u32[]{:S(2)}) collective-permute-start(bf16[16,2304]{1,0:T(8,128)(2,1)S(1)} %get-tuple-element.27), channel_id=1, source_target_pairs={{0,8},{1,9},{2,10},{3,11},{4,12},{5,13},{6,14},{7,15},{8,0},{9,1},... | collective-permute-start | bytes 221192 | tf_op jit(solution)/shard_map/ppermute | solution.py:107
  28.3 6.4 %collective-permute-start.14 = (bf16[16,2304]{1,0:T(8,128)(2,1)S(1)}, bf16[16,2304]{1,0:T(8,128)(2,1)S(1)}, u32[]{:S(2)}, u32[]{:S(2)}) collective-permute-start(bf16[16,2304]{1,0:T(8,128)(2,1)S(1)} %get-tuple-element.28), channel_id=1, source_target_pairs={{0,12},{1,13},{2,14},{3,15},{4,8},{5,9},{6,10},{7,11},{8,4},{9,5},... | collective-permute-start | bytes 221192 | tf_op jit(solution)/shard_map/ppermute | solution.py:107
  30.3 5.1 %collective-permute-start.12 = (bf16[16,2304]{1,0:T(8,128)(2,1)S(1)}, bf16[16,2304]{1,0:T(8,128)(2,1)S(1)}, u32[]{:S(2)}, u32[]{:S(2)}) collective-permute-start(bf16[16,2304]{1,0:T(8,128)(2,1)S(1)} %fusion.17), channel_id=1, source_target_pairs={{0,4},{1,5},{2,6},{3,7},{4,0},{5,1},{6,2},{7,3},{8,12},{9,13},{10,... | collective-permute-start | bytes 221192 | tf_op jit(solution)/shard_map/ppermute | solution.py:107
  30.8 4.6 %collective-permute-start.15 = (bf16[128,128]{0,1:T(8,128)(2,1)S(1)}, bf16[128,128]{0,1:T(8,128)(2,1)S(1)}, u32[]{:S(2)}, u32[]{:S(2)}) collective-permute-start(bf16[128,128]{0,1:T(8,128)(2,1)S(1)} %get-tuple-element.34), channel_id=1, source_target_pairs={{0,1},{1,0},{2,3},{3,2},{4,5},{5,4},{6,7},{7,6},{8,9},{9,8},{10,11... | collective-permute-start | bytes 98312 | tf_op jit(solution)/shard_map/ppermute | solution.py:114
  35.4 15.0 %copy-start.6 = (bf16[16,2304]{1,0:T(8,128)(2,1)}, bf16[16,2304]{1,0:T(8,128)(2,1)S(1)}, u32[]{:S(2)}) copy-start(bf16[16,2304]{1,0:T(8,128)(2,1)S(1)} %fusion.24) | copy-start | bytes 221188
  35.5 8.9 %collective-permute-start.22 = (bf16[16,2304]{1,0:T(8,128)(2,1)S(1)}, bf16[16,2304]{1,0:T(8,128)(2,1)S(1)}, u32[]{:S(2)}, u32[]{:S(2)}) collective-permute-start(bf16[16,2304]{1,0:T(8,128)(2,1)S(1)} %fusion.24), channel_id=1, source_target_pairs={{0,12},{1,13},{2,14},{3,15},{4,8},{5,9},{6,10},{7,11},{8,4},{9,5},... | collective-permute-start | bytes 221192 | tf_op jit(solution)/shard_map/ppermute | solution.py:107
  37.6 5.6 %collective-permute-start.20 = (bf16[16,2304]{1,0:T(8,128)(2,1)S(1)}, bf16[16,2304]{1,0:T(8,128)(2,1)S(1)}, u32[]{:S(2)}, u32[]{:S(2)}) collective-permute-start(bf16[16,2304]{1,0:T(8,128)(2,1)S(1)} %fusion.24), channel_id=1, source_target_pairs={{0,8},{1,9},{2,10},{3,11},{4,12},{5,13},{6,14},{7,15},{8,0},{9,1},... | collective-permute-start | bytes 221192 | tf_op jit(solution)/shard_map/ppermute | solution.py:107
  37.6 7.7 %collective-permute-start.18 = (bf16[16,2304]{1,0:T(8,128)(2,1)S(1)}, bf16[16,2304]{1,0:T(8,128)(2,1)S(1)}, u32[]{:S(2)}, u32[]{:S(2)}) collective-permute-start(bf16[16,2304]{1,0:T(8,128)(2,1)S(1)} %fusion.24), channel_id=1, source_target_pairs={{0,4},{1,5},{2,6},{3,7},{4,0},{5,1},{6,2},{7,3},{8,12},{9,13},{10,... | collective-permute-start | bytes 221192 | tf_op jit(solution)/shard_map/ppermute | solution.py:107
  39.9 6.5 %collective-permute-start.17 = (bf16[16,2304]{1,0:T(8,128)(2,1)S(1)}, bf16[16,2304]{1,0:T(8,128)(2,1)S(1)}, u32[]{:S(2)}, u32[]{:S(2)}) collective-permute-start(bf16[16,2304]{1,0:T(8,128)(2,1)S(1)} %fusion.24), channel_id=1, source_target_pairs={{0,2},{1,3},{2,0},{3,1},{4,6},{5,7},{6,4},{7,5},{8,10},{9,11},{10,... | collective-permute-start | bytes 221192 | tf_op jit(solution)/shard_map/ppermute | solution.py:107
  40.6 11.2 %copy-start.3 = (f32[128,2304]{1,0:T(8,128)S(1)}, f32[128,2304]{1,0:T(8,128)}, u32[]{:S(2)}) copy-start(f32[128,2304]{1,0:T(8,128)} %refs_8_.1) | copy-start | bytes 3538948
  43.3 6.5 %collective-permute-start.21 = (bf16[16,2304]{1,0:T(8,128)(2,1)S(1)}, bf16[16,2304]{1,0:T(8,128)(2,1)S(1)}, u32[]{:S(2)}, u32[]{:S(2)}) collective-permute-start(bf16[16,2304]{1,0:T(8,128)(2,1)S(1)} %collective-permute-done.20), channel_id=1, source_target_pairs={{0,2},{1,3},{2,0},{3,1},{4,6},{5,7},{6,4},{7,5},{8,10},{9,11},{10,... | collective-permute-start | bytes 221192 | tf_op jit(solution)/shard_map/ppermute | solution.py:107
  44.4 5.4 %collective-permute-start.23 = (bf16[16,2304]{1,0:T(8,128)(2,1)S(1)}, bf16[16,2304]{1,0:T(8,128)(2,1)S(1)}, u32[]{:S(2)}, u32[]{:S(2)}) collective-permute-start(bf16[16,2304]{1,0:T(8,128)(2,1)S(1)} %collective-permute-done.22), channel_id=1, source_target_pairs={{0,2},{1,3},{2,0},{3,1},{4,6},{5,7},{6,4},{7,5},{8,10},{9,11},{10,... | collective-permute-start | bytes 221192 | tf_op jit(solution)/shard_map/ppermute | solution.py:107
  45.4 4.4 %collective-permute-start.19 = (bf16[16,2304]{1,0:T(8,128)(2,1)S(1)}, bf16[16,2304]{1,0:T(8,128)(2,1)S(1)}, u32[]{:S(2)}, u32[]{:S(2)}) collective-permute-start(bf16[16,2304]{1,0:T(8,128)(2,1)S(1)} %collective-permute-done.18), channel_id=1, source_target_pairs={{0,2},{1,3},{2,0},{3,1},{4,6},{5,7},{6,4},{7,5},{8,10},{9,11},{10,... | collective-permute-start | bytes 221192 | tf_op jit(solution)/shard_map/ppermute | solution.py:107
  49.7 1.6 %collective-permute-start.24 = (bf16[64,2304]{1,0:T(8,128)(2,1)S(1)}, bf16[64,2304]{1,0:T(8,128)(2,1)S(1)}, u32[]{:S(2)}, u32[]{:S(2)}) collective-permute-start(bf16[64,2304]{1,0:T(8,128)(2,1)S(1)} %constant_dynamic-update-slice_fusion.8.refs_0_), channel_id=1, source_target_pairs={{0,1},{1,0},{2,3},{3,2},{4,5},{5,4},{6,7},{7,6},{8,9},{9,8},{10,11... | collective-permute-start | bytes 884744 | tf_op jit(solution)/shard_map/ppermute | solution.py:114
  49.8 1.9 %copy-start.1 = (f32[128,2304]{1,0:T(8,128)S(1)}, f32[128,2304]{1,0:T(8,128)}, u32[]{:S(2)}) copy-start(f32[128,2304]{1,0:T(8,128)} %refs_6_.1) | copy-start | bytes 3538948
  49.8 1.9 %collective-permute-start.25 = (bf16[64,2304]{1,0:T(8,128)(2,1)S(1)}, bf16[64,2304]{1,0:T(8,128)(2,1)S(1)}, u32[]{:S(2)}, u32[]{:S(2)}) collective-permute-start(bf16[64,2304]{1,0:T(8,128)(2,1)S(1)} %constant_dynamic-update-slice_fusion.12.refs_1_), channel_id=1, source_target_pairs={{0,1},{1,0},{2,3},{3,2},{4,5},{5,4},{6,7},{7,6},{8,9},{9,8},{10,11... | collective-permute-start | bytes 884744 | tf_op jit(solution)/shard_map/ppermute | solution.py:114
  (2 other events, 3.0 us)

commit v11 on v10

--- a/solution.py
+++ b/solution.py
@@ -152,8 +152,11 @@
     other_codes = to_other_core(codes[:, latents_here:])
     other_centered = to_other_core(centered)
 
-    partial_sums = jnp.dot(codes, decoder_both, preferred_element_type=jnp.float32)
-    parts = [partial_sums[k * rows_here : (k + 1) * rows_here] for k in range(chips)]
+    quad = 4 * rows_here
+    parts = []
+    for rows in (slice(0, quad), slice(quad, None)):
+        sums = jnp.dot(codes[rows], decoder_both, preferred_element_type=jnp.float32)
+        parts += [sums[at : at + rows_here] for at in range(0, sums.shape[0], rows_here)]
 
     def pair_sums(first, last, after=None):
         given = jnp.concatenate(parts[first + 1 : last : 2], 0).astype(jnp.bfloat16)
@@ -176,7 +179,8 @@
         (row_error, other_codes, other_centered)
     )
     blocks = in_turn(*gather_chips(row_error, chips))
-    errors = [jnp.concatenate(blocks[:4], 0), jnp.concatenate(blocks[4:], 0)]
+    errors = [jnp.concatenate(blocks, 0)]
+    errors += [to_other_core(jnp.concatenate(one, 0)) for one in (blocks[:4], blocks[4:])]
     codes_across = jnp.concatenate([codes[:, :latents_here], other_codes], 0).T
     centered_all = jnp.concatenate([centered, other_centered], 0)
     (
@@ -190,7 +194,7 @@
         total_rows,
         codes_across,
         centered_all,
-        errors + [to_other_core(one) for one in errors],
+        errors,
         (encoder, decoder),
         (encoder_moment, encoder_square, decoder_moment, decoder_square),
     )

time: 55.4 us -> 55.8 us (level)
  other arithmetic: 0.97 us -> 0.36 us
    ppermute x19, starting transfers between devices: 24.2 us -> 25.1 us  [to_chip(): lax.ppermute(block, 'latent', [(i, i ^ 2 * distance) for i in range(size)])]
    concatenate x1, other arithmetic: 0.66 us -> 0.01 us  [body(): bias_both = jnp.concatenate([encoder_bias, to_other_core(encoder_bias)], 0)]
    unnamed x29 -> x35, local copies, waits for them, and re-layouts: 1.5 us -> 1.25 us
  transfers between devices with their start and end apart: 26 -> 26, of which waited for: 11 -> 13; matrix products, arithmetic and copies ran while one was open for 5% -> 5% of each run, Pallas kernels for 0% -> 0%
where the time goes in v11:
time: 55.8 us; the launch traced here: 55.6 us
  starting transfers between devices  25.9 us (46%)
  waiting for transfers between devices  22.4 us (40%)
  Pallas kernels  3.38 us (6%)
  local copies, waits for them, and re-layouts  1.33 us (2%)
  matrix products  1.26 us (2%)
  between operations  1.01 us (2%)
    ppermute x19, starting transfers between devices, to_chip(): lax.ppermute(block, 'latent', [(i, i ^ 2 * distance) for i in range(size)])  25.1 us
    ppermute x19, waiting for transfers between devices, to_chip(): lax.ppermute(block, 'latent', [(i, i ^ 2 * distance) for i in range(size)])  20.8 us
    pallas_call x1, Pallas kernels, update(): pl.pallas_call(functools.partial(update_kernel, columns, float(total_rows...  3.38 us
    ppermute x7, waiting for transfers between devices, to_other_core(): return lax.ppermute(block, 'latent', [(i, i ^ 1) for i in range(size)])  1.62 us
    unnamed x35, local copies, waits for them, and re-layouts  1.25 us
  transfers between devices with their start and end apart: 26, of which 13 were waited for; matrix products, arithmetic and copies ran while one was open for 5% of the time, Pallas kernels for 0%

profile of v11, /device:TPU:0, one launch (start us, length us, event | category | flops | bytes accessed | tf_op | source)
XLA Modules:
  0.0 55.6 jit_solution(1315092938826752063)
XLA Ops:
  0.7 4.1 %collective-permute-start.3 = (bf16[16,2304]{1,0:T(8,128)(2,1)}, bf16[16,2304]{1,0:T(8,128)(2,1)S(1)}, u32[]{:S(2)}, u32[]{:S(2)}) collective-permute-start(bf16[16,2304]{1,0:T(8,128)(2,1)} %param.9), channel_id=1, source_target_pairs={{0,8},{1,9},{2,10},{3,11},{4,12},{5,13},{6,14},{7,15},{8,0},{9,1},... | collective-permute-start | bytes 221192 | tf_op jit(solution)/shard_map/ppermute | solution.py:107
  4.8 1.6 %collective-permute-start.1 = (bf16[16,2304]{1,0:T(8,128)(2,1)}, bf16[16,2304]{1,0:T(8,128)(2,1)S(1)}, u32[]{:S(2)}, u32[]{:S(2)}) collective-permute-start(bf16[16,2304]{1,0:T(8,128)(2,1)} %param.9), channel_id=1, source_target_pairs={{0,4},{1,5},{2,6},{3,7},{4,0},{5,1},{6,2},{7,3},{8,12},{9,13},{10,... | collective-permute-start | bytes 221192 | tf_op jit(solution)/shard_map/ppermute | solution.py:107
  6.4 1.5 %collective-permute-start = (bf16[16,2304]{1,0:T(8,128)(2,1)}, bf16[16,2304]{1,0:T(8,128)(2,1)S(1)}, u32[]{:S(2)}, u32[]{:S(2)}) collective-permute-start(bf16[16,2304]{1,0:T(8,128)(2,1)} %param.9), channel_id=1, source_target_pairs={{0,2},{1,3},{2,0},{3,1},{4,6},{5,7},{6,4},{7,5},{8,10},{9,11},{10,... | collective-permute-start | bytes 221192 | tf_op jit(solution)/shard_map/ppermute | solution.py:107
  8.1 1.1 %constant_dynamic-update-slice_fusion.9 = bf16[256,2304]{1,0:T(8,128)(2,1)S(1)} fusion(bf16[128,2304]{1,0:T(8,128)(2,1)} %refs_4_.1), kind=kLoop, calls=%fused_computation.39 | loop fusion | bytes 1179648
  9.4 0.5 collective-permute-start.9
  10.0 1.0 %collective-permute-start.4 = (bf16[16,2304]{1,0:T(8,128)(2,1)S(1)}, bf16[16,2304]{1,0:T(8,128)(2,1)S(1)}, u32[]{:S(2)}, u32[]{:S(2)}) collective-permute-start(bf16[16,2304]{1,0:T(8,128)(2,1)S(1)} %collective-permute-done.3), channel_id=1, source_target_pairs={{0,2},{1,3},{2,0},{3,1},{4,6},{5,7},{6,4},{7,5},{8,10},{9,11},{10,... | collective-permute-start | bytes 221192 | tf_op jit(solution)/shard_map/ppermute | solution.py:107
  11.0 1.4 %collective-permute-start.2 = (bf16[16,2304]{1,0:T(8,128)(2,1)S(1)}, bf16[16,2304]{1,0:T(8,128)(2,1)S(1)}, u32[]{:S(2)}, u32[]{:S(2)}) collective-permute-start(bf16[16,2304]{1,0:T(8,128)(2,1)S(1)} %collective-permute-done.1), channel_id=1, source_target_pairs={{0,2},{1,3},{2,0},{3,1},{4,6},{5,7},{6,4},{7,5},{8,10},{9,11},{10,... | collective-permute-start | bytes 221192 | tf_op jit(solution)/shard_map/ppermute | solution.py:107
  12.4 1.8 %collective-permute-done.5 = bf16[16,2304]{1,0:T(8,128)(2,1)S(1)} collective-permute-done((bf16[16,2304]{1,0:T(8,128)(2,1)}, bf16[16,2304]{1,0:T(8,128)(2,1)S(1)}, u32[]{:S(2)}, u32[]{:S(2)}) %collective-permute-start.5) | collective-permute-done | bytes 73760 | tf_op jit(solution)/shard_map/ppermute | solution.py:107
  14.2 0.5 collective-permute-start.6
  14.8 1.9 %collective-permute-done.2 = bf16[16,2304]{1,0:T(8,128)(2,1)S(1)} collective-permute-done((bf16[16,2304]{1,0:T(8,128)(2,1)S(1)}, bf16[16,2304]{1,0:T(8,128)(2,1)S(1)}, u32[]{:S(2)}, u32[]{:S(2)}) %collective-permute-start.2) | collective-permute-done | bytes 73760 | tf_op jit(solution)/shard_map/ppermute | solution.py:107
  16.7 1.9 %collective-permute-done.6 = bf16[16,2304]{1,0:T(8,128)(2,1)S(1)} collective-permute-done((bf16[16,2304]{1,0:T(8,128)(2,1)S(1)}, bf16[16,2304]{1,0:T(8,128)(2,1)S(1)}, u32[]{:S(2)}, u32[]{:S(2)}) %collective-permute-start.6) | collective-permute-done | bytes 73760 | tf_op jit(solution)/shard_map/ppermute | solution.py:107
  18.8 0.5 fusion.10
  19.3 0.4 fusion.29
  19.8 0.4 fusion.30
  20.2 0.6 %collective-permute-start.11 = (bf16[32,2304]{1,0:T(8,128)(2,1)S(1)}, bf16[32,2304]{1,0:T(8,128)(2,1)S(1)}, u32[]{:S(2)}, u32[]{:S(2)}) collective-permute-start(bf16[32,2304]{1,0:T(8,128)(2,1)S(1)} %pad_maximum_fusion.4), channel_id=1, source_target_pairs={{0,2},{1,3},{2,0},{3,1},{4,6},{5,7},{6,4},{7,5},{8,10},{9,11},{10,... | collective-permute-start | bytes 442376 | tf_op jit(solution)/shard_map/ppermute | solution.py:107
  20.8 1.6 %collective-permute-start.10 = (bf16[32,2304]{1,0:T(8,128)(2,1)S(1)}, bf16[32,2304]{1,0:T(8,128)(2,1)S(1)}, u32[]{:S(2)}, u32[]{:S(2)}) collective-permute-start(bf16[32,2304]{1,0:T(8,128)(2,1)S(1)} %pad_maximum_fusion.3), channel_id=1, source_target_pairs={{0,2},{1,3},{2,0},{3,1},{4,6},{5,7},{6,4},{7,5},{8,10},{9,11},{10,... | collective-permute-start | bytes 442376 | tf_op jit(solution)/shard_map/ppermute | solution.py:107
  22.4 4.5 %collective-permute-done.11 = bf16[32,2304]{1,0:T(8,128)(2,1)S(1)} collective-permute-done((bf16[32,2304]{1,0:T(8,128)(2,1)S(1)}, bf16[32,2304]{1,0:T(8,128)(2,1)S(1)}, u32[]{:S(2)}, u32[]{:S(2)}) %collective-permute-start.11) | collective-permute-done | bytes 147488 | tf_op jit(solution)/shard_map/ppermute | solution.py:107
  26.9 0.9 %collective-permute-start.13 = (bf16[16,2304]{1,0:T(8,128)(2,1)S(1)}, bf16[16,2304]{1,0:T(8,128)(2,1)S(1)}, u32[]{:S(2)}, u32[]{:S(2)}) collective-permute-start(bf16[16,2304]{1,0:T(8,128)(2,1)S(1)} %get-tuple-element.27), channel_id=1, source_target_pairs={{0,8},{1,9},{2,10},{3,11},{4,12},{5,13},{6,14},{7,15},{8,0},{9,1},... | collective-permute-start | bytes 221192 | tf_op jit(solution)/shard_map/ppermute | solution.py:107
  27.9 2.0 %collective-permute-start.14 = (bf16[16,2304]{1,0:T(8,128)(2,1)S(1)}, bf16[16,2304]{1,0:T(8,128)(2,1)S(1)}, u32[]{:S(2)}, u32[]{:S(2)}) collective-permute-start(bf16[16,2304]{1,0:T(8,128)(2,1)S(1)} %get-tuple-element.28), channel_id=1, source_target_pairs={{0,12},{1,13},{2,14},{3,15},{4,8},{5,9},{6,10},{7,11},{8,4},{9,5},... | collective-permute-start | bytes 221192 | tf_op jit(solution)/shard_map/ppermute | solution.py:107
  29.9 0.7 %collective-permute-start.12 = (bf16[16,2304]{1,0:T(8,128)(2,1)S(1)}, bf16[16,2304]{1,0:T(8,128)(2,1)S(1)}, u32[]{:S(2)}, u32[]{:S(2)}) collective-permute-start(bf16[16,2304]{1,0:T(8,128)(2,1)S(1)} %fusion.13), channel_id=1, source_target_pairs={{0,4},{1,5},{2,6},{3,7},{4,0},{5,1},{6,2},{7,3},{8,12},{9,13},{10,... | collective-permute-start | bytes 221192 | tf_op jit(solution)/shard_map/ppermute | solution.py:107
  30.6 4.7 %collective-permute-done.13 = bf16[16,2304]{1,0:T(8,128)(2,1)S(1)} collective-permute-done((bf16[16,2304]{1,0:T(8,128)(2,1)S(1)}, bf16[16,2304]{1,0:T(8,128)(2,1)S(1)}, u32[]{:S(2)}, u32[]{:S(2)}) %collective-permute-start.13) | collective-permute-done | bytes 73760 | tf_op jit(solution)/shard_map/ppermute | solution.py:107
  35.7 2.5 %collective-permute-start.22 = (bf16[16,2304]{1,0:T(8,128)(2,1)S(1)}, bf16[16,2304]{1,0:T(8,128)(2,1)S(1)}, u32[]{:S(2)}, u32[]{:S(2)}) collective-permute-start(bf16[16,2304]{1,0:T(8,128)(2,1)S(1)} %fusion.20), channel_id=1, source_target_pairs={{0,12},{1,13},{2,14},{3,15},{4,8},{5,9},{6,10},{7,11},{8,4},{9,5},... | collective-permute-start | bytes 221192 | tf_op jit(solution)/shard_map/ppermute | solution.py:107
  38.3 1.9 %collective-permute-start.18 = (bf16[16,2304]{1,0:T(8,128)(2,1)S(1)}, bf16[16,2304]{1,0:T(8,128)(2,1)S(1)}, u32[]{:S(2)}, u32[]{:S(2)}) collective-permute-start(bf16[16,2304]{1,0:T(8,128)(2,1)S(1)} %fusion.20), channel_id=1, source_target_pairs={{0,4},{1,5},{2,6},{3,7},{4,0},{5,1},{6,2},{7,3},{8,12},{9,13},{10,... | collective-permute-start | bytes 221192 | tf_op jit(solution)/shard_map/ppermute | solution.py:107
  40.2 0.8 %collective-permute-start.17 = (bf16[16,2304]{1,0:T(8,128)(2,1)S(1)}, bf16[16,2304]{1,0:T(8,128)(2,1)S(1)}, u32[]{:S(2)}, u32[]{:S(2)}) collective-permute-start(bf16[16,2304]{1,0:T(8,128)(2,1)S(1)} %fusion.20), channel_id=1, source_target_pairs={{0,2},{1,3},{2,0},{3,1},{4,6},{5,7},{6,4},{7,5},{8,10},{9,11},{10,... | collective-permute-start | bytes 221192 | tf_op jit(solution)/shard_map/ppermute | solution.py:107
  41.2 0.9 %collective-permute-done.22 = bf16[16,2304]{1,0:T(8,128)(2,1)S(1)} collective-permute-done((bf16[16,2304]{1,0:T(8,128)(2,1)S(1)}, bf16[16,2304]{1,0:T(8,128)(2,1)S(1)}, u32[]{:S(2)}, u32[]{:S(2)}) %collective-permute-start.22) | collective-permute-done | bytes 73760 | tf_op jit(solution)/shard_map/ppermute | solution.py:107
  42.1 1.6 %collective-permute-start.23 = (bf16[16,2304]{1,0:T(8,128)(2,1)S(1)}, bf16[16,2304]{1,0:T(8,128)(2,1)S(1)}, u32[]{:S(2)}, u32[]{:S(2)}) collective-permute-start(bf16[16,2304]{1,0:T(8,128)(2,1)S(1)} %collective-permute-done.22), channel_id=1, source_target_pairs={{0,2},{1,3},{2,0},{3,1},{4,6},{5,7},{6,4},{7,5},{8,10},{9,11},{10,... | collective-permute-start | bytes 221192 | tf_op jit(solution)/shard_map/ppermute | solution.py:107
  43.6 0.9 %collective-permute-done.20 = bf16[16,2304]{1,0:T(8,128)(2,1)S(1)} collective-permute-done((bf16[16,2304]{1,0:T(8,128)(2,1)S(1)}, bf16[16,2304]{1,0:T(8,128)(2,1)S(1)}, u32[]{:S(2)}, u32[]{:S(2)}) %collective-permute-start.20) | collective-permute-done | bytes 73760 | tf_op jit(solution)/shard_map/ppermute | solution.py:107
  44.5 1.7 %collective-permute-start.21 = (bf16[16,2304]{1,0:T(8,128)(2,1)S(1)}, bf16[16,2304]{1,0:T(8,128)(2,1)S(1)}, u32[]{:S(2)}, u32[]{:S(2)}) collective-permute-start(bf16[16,2304]{1,0:T(8,128)(2,1)S(1)} %collective-permute-done.20), channel_id=1, source_target_pairs={{0,2},{1,3},{2,0},{3,1},{4,6},{5,7},{6,4},{7,5},{8,10},{9,11},{10,... | collective-permute-start | bytes 221192 | tf_op jit(solution)/shard_map/ppermute | solution.py:107
  46.6 2.7 %collective-permute-done.21 = bf16[16,2304]{1,0:T(8,128)(2,1)S(1)} collective-permute-done((bf16[16,2304]{1,0:T(8,128)(2,1)S(1)}, bf16[16,2304]{1,0:T(8,128)(2,1)S(1)}, u32[]{:S(2)}, u32[]{:S(2)}) %collective-permute-start.21) | collective-permute-done | bytes 73760 | tf_op jit(solution)/shard_map/ppermute | solution.py:107
  49.4 1.1 %collective-permute-done.19 = bf16[16,2304]{1,0:T(8,128)(2,1)S(1)} collective-permute-done((bf16[16,2304]{1,0:T(8,128)(2,1)S(1)}, bf16[16,2304]{1,0:T(8,128)(2,1)S(1)}, u32[]{:S(2)}, u32[]{:S(2)}) %collective-permute-start.19) | collective-permute-done | bytes 73760 | tf_op jit(solution)/shard_map/ppermute | solution.py:107
  51.0 1.2 %collective-permute-done.24.refs_1_ = bf16[64,2304]{1,0:T(8,128)(2,1)S(1)} collective-permute-done((bf16[64,2304]{1,0:T(8,128)(2,1)S(1)}, bf16[64,2304]{1,0:T(8,128)(2,1)S(1)}, u32[]{:S(2)}, u32[]{:S(2)}) %collective-permute-start.24) | collective-permute-done | bytes 294944 | tf_op jit(solution)/shard_map/ppermute | solution.py:114
  52.2 3.4 %update.1 = (bf16[128,2304]{1,0:T(8,128)(2,1)}, f32[128,2304]{1,0:T(8,128)}, f32[128,2304]{1,0:T(8,128)}, bf16[128,2304]{1,0:T(8,128)(2,1)}, f32[128,2304]{1,0:T(8,128)}, /*index=5*/f32[128,2304]{1,0:T(8,128)}) custom-call(bf16[128,256]{1,0:T(8,128)(2,1)S(1)} %maximum_bitcast_fusion.codes_across, bf16[256,2304]{1,0:T(8,128)(2,1)S(1)} %pad_maximum_fusion.centered, ...), custom_call_target="tpu_custom_call" | custom-call | flops 452984832 | bytes 12976128 | tf_op jit(solution)/shard_map/update/pallas_call | solution.py:80
  (76 shorter events, 2.2 us)
Async XLA Ops:
  0.7 17.9 %copy-start.8 = (f32[2304]{0:T(1024)S(1)}, f32[2304]{0:T(1024)}, u32[]{:S(2)}) copy-start(f32[2304]{0:T(1024)} %param.13) | copy-start | bytes 27652
  0.7 9.2 %collective-permute-start.3 = (bf16[16,2304]{1,0:T(8,128)(2,1)}, bf16[16,2304]{1,0:T(8,128)(2,1)S(1)}, u32[]{:S(2)}, u32[]{:S(2)}) collective-permute-start(bf16[16,2304]{1,0:T(8,128)(2,1)} %param.9), channel_id=1, source_target_pairs={{0,8},{1,9},{2,10},{3,11},{4,12},{5,13},{6,14},{7,15},{8,0},{9,1},... | collective-permute-start | bytes 221192 | tf_op jit(solution)/shard_map/ppermute | solution.py:107
  4.8 5.2 %collective-permute-start.1 = (bf16[16,2304]{1,0:T(8,128)(2,1)}, bf16[16,2304]{1,0:T(8,128)(2,1)S(1)}, u32[]{:S(2)}, u32[]{:S(2)}) collective-permute-start(bf16[16,2304]{1,0:T(8,128)(2,1)} %param.9), channel_id=1, source_target_pairs={{0,4},{1,5},{2,6},{3,7},{4,0},{5,1},{6,2},{7,3},{8,12},{9,13},{10,... | collective-permute-start | bytes 221192 | tf_op jit(solution)/shard_map/ppermute | solution.py:107
  6.4 4.7 %collective-permute-start = (bf16[16,2304]{1,0:T(8,128)(2,1)}, bf16[16,2304]{1,0:T(8,128)(2,1)S(1)}, u32[]{:S(2)}, u32[]{:S(2)}) collective-permute-start(bf16[16,2304]{1,0:T(8,128)(2,1)} %param.9), channel_id=1, source_target_pairs={{0,2},{1,3},{2,0},{3,1},{4,6},{5,7},{6,4},{7,5},{8,10},{9,11},{10,... | collective-permute-start | bytes 221192 | tf_op jit(solution)/shard_map/ppermute | solution.py:107
  7.9 6.4 %collective-permute-start.5 = (bf16[16,2304]{1,0:T(8,128)(2,1)}, bf16[16,2304]{1,0:T(8,128)(2,1)S(1)}, u32[]{:S(2)}, u32[]{:S(2)}) collective-permute-start(bf16[16,2304]{1,0:T(8,128)(2,1)} %param.9), channel_id=1, source_target_pairs={{0,12},{1,13},{2,14},{3,15},{4,8},{5,9},{6,10},{7,11},{8,4},{9,5},... | collective-permute-start | bytes 221192 | tf_op jit(solution)/shard_map/ppermute | solution.py:107
  8.1 1.3 %collective-permute-start.8 = (f32[128]{0:T(128)}, f32[128]{0:T(128)S(1)}, u32[]{:S(2)}, u32[]{:S(2)}) collective-permute-start(f32[128]{0:T(128)} %param.11), channel_id=1, source_target_pairs={{0,1},{1,0},{2,3},{3,2},{4,5},{5,4},{6,7},{7,6},{8,9},{9,8},{10,11... | collective-permute-start | bytes 1544 | tf_op jit(solution)/shard_map/ppermute | solution.py:114
  9.4 9.9 %collective-permute-start.9 = (bf16[128,2304]{1,0:T(8,128)(2,1)S(1)}, bf16[128,2304]{1,0:T(8,128)(2,1)S(1)}, u32[]{:S(2)}, u32[]{:S(2)}) collective-permute-start(bf16[128,2304]{1,0:T(8,128)(2,1)S(1)} %copy-done), channel_id=1, source_target_pairs={{0,1},{1,0},{2,3},{3,2},{4,5},{5,4},{6,7},{7,6},{8,9},{9,8},{10,11... | collective-permute-start | bytes 1769480 | tf_op jit(solution)/shard_map/ppermute | solution.py:114
  9.9 8.9 %collective-permute-start.7 = (bf16[128,2304]{1,0:T(8,128)(2,1)S(1)}, bf16[128,2304]{1,0:T(8,128)(2,1)S(1)}, u32[]{:S(2)}, u32[]{:S(2)}) collective-permute-start(bf16[128,2304]{1,0:T(8,128)(2,1)S(1)} %copy-done.5), channel_id=1, source_target_pairs={{0,1},{1,0},{2,3},{3,2},{4,5},{5,4},{6,7},{7,6},{8,9},{9,8},{10,11... | collective-permute-start | bytes 1769480 | tf_op jit(solution)/shard_map/ppermute | solution.py:114
  10.0 6.7 %collective-permute-start.4 = (bf16[16,2304]{1,0:T(8,128)(2,1)S(1)}, bf16[16,2304]{1,0:T(8,128)(2,1)S(1)}, u32[]{:S(2)}, u32[]{:S(2)}) collective-permute-start(bf16[16,2304]{1,0:T(8,128)(2,1)S(1)} %collective-permute-done.3), channel_id=1, source_target_pairs={{0,2},{1,3},{2,0},{3,1},{4,6},{5,7},{6,4},{7,5},{8,10},{9,11},{10,... | collective-permute-start | bytes 221192 | tf_op jit(solution)/shard_map/ppermute | solution.py:107
  11.0 5.7 %collective-permute-start.2 = (bf16[16,2304]{1,0:T(8,128)(2,1)S(1)}, bf16[16,2304]{1,0:T(8,128)(2,1)S(1)}, u32[]{:S(2)}, u32[]{:S(2)}) collective-permute-start(bf16[16,2304]{1,0:T(8,128)(2,1)S(1)} %collective-permute-done.1), channel_id=1, source_target_pairs={{0,2},{1,3},{2,0},{3,1},{4,6},{5,7},{6,4},{7,5},{8,10},{9,11},{10,... | collective-permute-start | bytes 221192 | tf_op jit(solution)/shard_map/ppermute | solution.py:107
  14.2 4.4 %collective-permute-start.6 = (bf16[16,2304]{1,0:T(8,128)(2,1)S(1)}, bf16[16,2304]{1,0:T(8,128)(2,1)S(1)}, u32[]{:S(2)}, u32[]{:S(2)}) collective-permute-start(bf16[16,2304]{1,0:T(8,128)(2,1)S(1)} %collective-permute-done.5), channel_id=1, source_target_pairs={{0,2},{1,3},{2,0},{3,1},{4,6},{5,7},{6,4},{7,5},{8,10},{9,11},{10,... | collective-permute-start | bytes 221192 | tf_op jit(solution)/shard_map/ppermute | solution.py:107
  18.7 17.0 %collective-permute-start.16 = (bf16[128,2304]{1,0:T(8,128)(2,1)S(1)}, bf16[128,2304]{1,0:T(8,128)(2,1)S(1)}, u32[]{:S(2)}, u32[]{:S(2)}) collective-permute-start(bf16[128,2304]{1,0:T(8,128)(2,1)S(1)} %subtract_convert_fusion), channel_id=1, source_target_pairs={{0,1},{1,0},{2,3},{3,2},{4,5},{5,4},{6,7},{7,6},{8,9},{9,8},{10,11... | collective-permute-start | bytes 1769480 | tf_op jit(solution)/shard_map/ppermute | solution.py:114
  20.2 6.7 %collective-permute-start.11 = (bf16[32,2304]{1,0:T(8,128)(2,1)S(1)}, bf16[32,2304]{1,0:T(8,128)(2,1)S(1)}, u32[]{:S(2)}, u32[]{:S(2)}) collective-permute-start(bf16[32,2304]{1,0:T(8,128)(2,1)S(1)} %pad_maximum_fusion.4), channel_id=1, source_target_pairs={{0,2},{1,3},{2,0},{3,1},{4,6},{5,7},{6,4},{7,5},{8,10},{9,11},{10,... | collective-permute-start | bytes 442376 | tf_op jit(solution)/shard_map/ppermute | solution.py:107
  20.8 9.1 %collective-permute-start.10 = (bf16[32,2304]{1,0:T(8,128)(2,1)S(1)}, bf16[32,2304]{1,0:T(8,128)(2,1)S(1)}, u32[]{:S(2)}, u32[]{:S(2)}) collective-permute-start(bf16[32,2304]{1,0:T(8,128)(2,1)S(1)} %pad_maximum_fusion.3), channel_id=1, source_target_pairs={{0,2},{1,3},{2,0},{3,1},{4,6},{5,7},{6,4},{7,5},{8,10},{9,11},{10,... | collective-permute-start | bytes 442376 | tf_op jit(solution)/shard_map/ppermute | solution.py:107
  26.9 8.4 %collective-permute-start.13 = (bf16[16,2304]{1,0:T(8,128)(2,1)S(1)}, bf16[16,2304]{1,0:T(8,128)(2,1)S(1)}, u32[]{:S(2)}, u32[]{:S(2)}) collective-permute-start(bf16[16,2304]{1,0:T(8,128)(2,1)S(1)} %get-tuple-element.27), channel_id=1, source_target_pairs={{0,8},{1,9},{2,10},{3,11},{4,12},{5,13},{6,14},{7,15},{8,0},{9,1},... | collective-permute-start | bytes 221192 | tf_op jit(solution)/shard_map/ppermute | solution.py:107
  27.9 7.4 %collective-permute-start.14 = (bf16[16,2304]{1,0:T(8,128)(2,1)S(1)}, bf16[16,2304]{1,0:T(8,128)(2,1)S(1)}, u32[]{:S(2)}, u32[]{:S(2)}) collective-permute-start(bf16[16,2304]{1,0:T(8,128)(2,1)S(1)} %get-tuple-element.28), channel_id=1, source_target_pairs={{0,12},{1,13},{2,14},{3,15},{4,8},{5,9},{6,10},{7,11},{8,4},{9,5},... | collective-permute-start | bytes 221192 | tf_op jit(solution)/shard_map/ppermute | solution.py:107
  29.9 5.7 %collective-permute-start.12 = (bf16[16,2304]{1,0:T(8,128)(2,1)S(1)}, bf16[16,2304]{1,0:T(8,128)(2,1)S(1)}, u32[]{:S(2)}, u32[]{:S(2)}) collective-permute-start(bf16[16,2304]{1,0:T(8,128)(2,1)S(1)} %fusion.13), channel_id=1, source_target_pairs={{0,4},{1,5},{2,6},{3,7},{4,0},{5,1},{6,2},{7,3},{8,12},{9,13},{10,... | collective-permute-start | bytes 221192 | tf_op jit(solution)/shard_map/ppermute | solution.py:107
  30.6 5.1 %collective-permute-start.15 = (bf16[128,128]{0,1:T(8,128)(2,1)S(1)}, bf16[128,128]{0,1:T(8,128)(2,1)S(1)}, u32[]{:S(2)}, u32[]{:S(2)}) collective-permute-start(bf16[128,128]{0,1:T(8,128)(2,1)S(1)} %get-tuple-element.34), channel_id=1, source_target_pairs={{0,1},{1,0},{2,3},{3,2},{4,5},{5,4},{6,7},{7,6},{8,9},{9,8},{10,11... | collective-permute-start | bytes 98312 | tf_op jit(solution)/shard_map/ppermute | solution.py:114
  35.7 14.8 %copy-start.6 = (bf16[16,2304]{1,0:T(8,128)(2,1)}, bf16[16,2304]{1,0:T(8,128)(2,1)S(1)}, u32[]{:S(2)}) copy-start(bf16[16,2304]{1,0:T(8,128)(2,1)S(1)} %fusion.20) | copy-start | bytes 221188
  35.7 6.3 %collective-permute-start.22 = (bf16[16,2304]{1,0:T(8,128)(2,1)S(1)}, bf16[16,2304]{1,0:T(8,128)(2,1)S(1)}, u32[]{:S(2)}, u32[]{:S(2)}) collective-permute-start(bf16[16,2304]{1,0:T(8,128)(2,1)S(1)} %fusion.20), channel_id=1, source_target_pairs={{0,12},{1,13},{2,14},{3,15},{4,8},{5,9},{6,10},{7,11},{8,4},{9,5},... | collective-permute-start | bytes 221192 | tf_op jit(solution)/shard_map/ppermute | solution.py:107
  38.3 6.2 %collective-permute-start.20 = (bf16[16,2304]{1,0:T(8,128)(2,1)S(1)}, bf16[16,2304]{1,0:T(8,128)(2,1)S(1)}, u32[]{:S(2)}, u32[]{:S(2)}) collective-permute-start(bf16[16,2304]{1,0:T(8,128)(2,1)S(1)} %fusion.20), channel_id=1, source_target_pairs={{0,8},{1,9},{2,10},{3,11},{4,12},{5,13},{6,14},{7,15},{8,0},{9,1},... | collective-permute-start | bytes 221192 | tf_op jit(solution)/shard_map/ppermute | solution.py:107
  38.3 7.9 %collective-permute-start.18 = (bf16[16,2304]{1,0:T(8,128)(2,1)S(1)}, bf16[16,2304]{1,0:T(8,128)(2,1)S(1)}, u32[]{:S(2)}, u32[]{:S(2)}) collective-permute-start(bf16[16,2304]{1,0:T(8,128)(2,1)S(1)} %fusion.20), channel_id=1, source_target_pairs={{0,4},{1,5},{2,6},{3,7},{4,0},{5,1},{6,2},{7,3},{8,12},{9,13},{10,... | collective-permute-start | bytes 221192 | tf_op jit(solution)/shard_map/ppermute | solution.py:107
  40.2 6.3 %collective-permute-start.17 = (bf16[16,2304]{1,0:T(8,128)(2,1)S(1)}, bf16[16,2304]{1,0:T(8,128)(2,1)S(1)}, u32[]{:S(2)}, u32[]{:S(2)}) collective-permute-start(bf16[16,2304]{1,0:T(8,128)(2,1)S(1)} %fusion.20), channel_id=1, source_target_pairs={{0,2},{1,3},{2,0},{3,1},{4,6},{5,7},{6,4},{7,5},{8,10},{9,11},{10,... | collective-permute-start | bytes 221192 | tf_op jit(solution)/shard_map/ppermute | solution.py:107
  41.0 11.2 %copy-start.4 = (f32[128,2304]{1,0:T(8,128)S(1)}, f32[128,2304]{1,0:T(8,128)}, u32[]{:S(2)}) copy-start(f32[128,2304]{1,0:T(8,128)} %refs_8_.1) | copy-start | bytes 3538948
  41.0 11.2 %copy-start.2 = (f32[128,2304]{1,0:T(8,128)S(1)}, f32[128,2304]{1,0:T(8,128)}, u32[]{:S(2)}) copy-start(f32[128,2304]{1,0:T(8,128)} %refs_6_.1) | copy-start | bytes 3538948
  41.0 11.2 %copy-start.3 = (f32[128,2304]{1,0:T(8,128)S(1)}, f32[128,2304]{1,0:T(8,128)}, u32[]{:S(2)}) copy-start(f32[128,2304]{1,0:T(8,128)} %refs_7_.1) | copy-start | bytes 3538948
  41.1 11.1 %copy-start.1 = (f32[128,2304]{1,0:T(8,128)S(1)}, f32[128,2304]{1,0:T(8,128)}, u32[]{:S(2)}) copy-start(f32[128,2304]{1,0:T(8,128)} %refs_5_.1) | copy-start | bytes 3538948
  42.1 4.5 %collective-permute-start.23 = (bf16[16,2304]{1,0:T(8,128)(2,1)S(1)}, bf16[16,2304]{1,0:T(8,128)(2,1)S(1)}, u32[]{:S(2)}, u32[]{:S(2)}) collective-permute-start(bf16[16,2304]{1,0:T(8,128)(2,1)S(1)} %collective-permute-done.22), channel_id=1, source_target_pairs={{0,2},{1,3},{2,0},{3,1},{4,6},{5,7},{6,4},{7,5},{8,10},{9,11},{10,... | collective-permute-start | bytes 221192 | tf_op jit(solution)/shard_map/ppermute | solution.py:107
  44.5 4.8 %collective-permute-start.21 = (bf16[16,2304]{1,0:T(8,128)(2,1)S(1)}, bf16[16,2304]{1,0:T(8,128)(2,1)S(1)}, u32[]{:S(2)}, u32[]{:S(2)}) collective-permute-start(bf16[16,2304]{1,0:T(8,128)(2,1)S(1)} %collective-permute-done.20), channel_id=1, source_target_pairs={{0,2},{1,3},{2,0},{3,1},{4,6},{5,7},{6,4},{7,5},{8,10},{9,11},{10,... | collective-permute-start | bytes 221192 | tf_op jit(solution)/shard_map/ppermute | solution.py:107
  46.2 4.4 %collective-permute-start.19 = (bf16[16,2304]{1,0:T(8,128)(2,1)S(1)}, bf16[16,2304]{1,0:T(8,128)(2,1)S(1)}, u32[]{:S(2)}, u32[]{:S(2)}) collective-permute-start(bf16[16,2304]{1,0:T(8,128)(2,1)S(1)} %collective-permute-done.18), channel_id=1, source_target_pairs={{0,2},{1,3},{2,0},{3,1},{4,6},{5,7},{6,4},{7,5},{8,10},{9,11},{10,... | collective-permute-start | bytes 221192 | tf_op jit(solution)/shard_map/ppermute | solution.py:107
  49.3 1.6 %collective-permute-start.25 = (bf16[64,2304]{1,0:T(8,128)(2,1)S(1)}, bf16[64,2304]{1,0:T(8,128)(2,1)S(1)}, u32[]{:S(2)}, u32[]{:S(2)}) collective-permute-start(bf16[64,2304]{1,0:T(8,128)(2,1)S(1)} %pad_maximum_fusion.2), channel_id=1, source_target_pairs={{0,1},{1,0},{2,3},{3,2},{4,5},{5,4},{6,7},{7,6},{8,9},{9,8},{10,11... | collective-permute-start | bytes 884744 | tf_op jit(solution)/shard_map/ppermute | solution.py:114
  50.6 1.6 %collective-permute-start.24 = (bf16[64,2304]{1,0:T(8,128)(2,1)S(1)}, bf16[64,2304]{1,0:T(8,128)(2,1)S(1)}, u32[]{:S(2)}, u32[]{:S(2)}) collective-permute-start(bf16[64,2304]{1,0:T(8,128)(2,1)S(1)} %pad_maximum_fusion.1), channel_id=1, source_target_pairs={{0,1},{1,0},{2,3},{3,2},{4,5},{5,4},{6,7},{7,6},{8,9},{9,8},{10,11... | collective-permute-start | bytes 884744 | tf_op jit(solution)/shard_map/ppermute | solution.py:114
  (4 other events, 35.7 us)

commit v12 on v11

--- a/solution.py
+++ b/solution.py
@@ -46,8 +46,8 @@
             for start in range(0, total.shape[0], part):
                 some = (pl.ds(start, part), at)
                 grad = total[start : start + part]
-                moment = beta_first * moments[2 * which][some] + first * grad
-                square = beta_second * moments[2 * which + 1][some] + second * (grad * grad)
+                moment = moments[2 * which][some] + first * grad
+                square = moments[2 * which + 1][some] + second * (grad * grad)
                 root = square * lax.rsqrt(square)
                 held[3 * which][some] = (
                     weight[some].astype(jnp.float32)
@@ -114,9 +114,11 @@
     return lax.ppermute(block, "latent", [(i, i ^ 1) for i in range(size)])
 
 
-def gather_chips(block, chips):
+def gather_chips(block, chips, before=None):
     even = [block] + [to_chip(block, k) for k in range(2, chips, 2)]
-    return even, [to_chip(one, 1) for one in even]
+    if before is not None:
+        even[2], before = lax.optimization_barrier((even[2], before))
+    return even, [to_chip(one, 1) for one in even], before
 
 
 def in_turn(even, odd):
@@ -140,7 +142,14 @@
     chips = size // 2
     total_rows = rows_here * size
 
-    rows_core = jnp.concatenate(in_turn(*gather_chips(activations, chips)), 0)
+    decayed = (
+        beta_first * encoder_moment,
+        beta_second * encoder_square,
+        beta_first * decoder_moment,
+        beta_second * decoder_square,
+    )
+    even, odd, decayed = gather_chips(activations, chips, decayed)
+    rows_core = jnp.concatenate(in_turn(even, odd), 0)
     encoder_both = jnp.concatenate([encoder, to_other_core(encoder)], 0)
     decoder_both = jnp.concatenate([decoder, to_other_core(decoder)], 0)
     bias_both = jnp.concatenate([encoder_bias, to_other_core(encoder_bias)], 0)
@@ -178,7 +187,8 @@
     row_error, other_codes, other_centered = lax.optimization_barrier(
         (row_error, other_codes, other_centered)
     )
-    blocks = in_turn(*gather_chips(row_error, chips))
+    even, odd, _ = gather_chips(row_error, chips)
+    blocks = in_turn(even, odd)
     errors = [jnp.concatenate(blocks, 0)]
     errors += [to_other_core(jnp.concatenate(one, 0)) for one in (blocks[:4], blocks[4:])]
     codes_across = jnp.concatenate([codes[:, :latents_here], other_codes], 0).T
@@ -196,7 +206,7 @@
         centered_all,
         errors,
         (encoder, decoder),
-        (encoder_moment, encoder_square, decoder_moment, decoder_square),
+        decayed,
     )
     return (
         row_error,

time: 55.8 us -> 57.8 us (1.036)
  other arithmetic: 0.36 us -> 2.21 us
  starting transfers between devices: 25.9 us -> 24.5 us
  local copies, waits for them, and re-layouts: 1.33 us -> 2.5 us
    mul x0 -> x2, other arithmetic: none -> 1.83 us  [the longest x1 1.63 us: body(): beta_first * decoder_moment]
    ppermute x19, starting transfers between devices: 25.1 us -> 23.6 us  [to_chip(): lax.ppermute(block, 'latent', [(i, i ^ 2 * distance) for i in range(size)])]
    unnamed x35 -> x33, local copies, waits for them, and re-layouts: 1.25 us -> 2.41 us
  transfers between devices with their start and end apart: 26 -> 26, of which waited for: 13 -> 12; matrix products, arithmetic and copies ran while one was open for 5% -> 8% of each run, Pallas kernels for 0% -> 0%
where the time goes in v12:
time: 57.8 us; the launch traced here: 57.6 us
  starting transfers between devices  24.5 us (42%)
  waiting for transfers between devices  22.8 us (39%)
  Pallas kernels  3.33 us (6%)
  local copies, waits for them, and re-layouts  2.5 us (4%)
  other arithmetic  2.21 us (4%)
  matrix products  1.28 us (2%)
  between operations  0.98 us (2%)
    ppermute x19, starting transfers between devices, to_chip(): lax.ppermute(block, 'latent', [(i, i ^ 2 * distance) for i in range(size)])  23.6 us
    ppermute x19, waiting for transfers between devices, to_chip(): lax.ppermute(block, 'latent', [(i, i ^ 2 * distance) for i in range(size)])  21.3 us
    pallas_call x1, Pallas kernels, update(): pl.pallas_call(functools.partial(update_kernel, columns, float(total_rows...  3.33 us
    unnamed x33, local copies, waits for them, and re-layouts  2.41 us
    mul x1, other arithmetic, body(): beta_first * decoder_moment  1.63 us
    ppermute x7, waiting for transfers between devices, to_other_core(): return lax.ppermute(block, 'latent', [(i, i ^ 1) for i in range(size)])  1.51 us
  transfers between devices with their start and end apart: 26, of which 12 were waited for; matrix products, arithmetic and copies ran while one was open for 8% of the time, Pallas kernels for 0%

profile of v12, /device:TPU:0, one launch (start us, length us, event | category | flops | bytes accessed | tf_op | source)
XLA Modules:
  0.0 57.6 jit_solution(1449022237653931372)
XLA Ops:
  0.6 4.1 %collective-permute-start.3 = (bf16[16,2304]{1,0:T(8,128)(2,1)}, bf16[16,2304]{1,0:T(8,128)(2,1)S(1)}, u32[]{:S(2)}, u32[]{:S(2)}) collective-permute-start(bf16[16,2304]{1,0:T(8,128)(2,1)} %param.9), channel_id=1, source_target_pairs={{0,8},{1,9},{2,10},{3,11},{4,12},{5,13},{6,14},{7,15},{8,0},{9,1},... | collective-permute-start | bytes 221192 | tf_op jit(solution)/shard_map/ppermute | solution.py:107
  4.7 1.6 %collective-permute-start.1 = (bf16[16,2304]{1,0:T(8,128)(2,1)}, bf16[16,2304]{1,0:T(8,128)(2,1)S(1)}, u32[]{:S(2)}, u32[]{:S(2)}) collective-permute-start(bf16[16,2304]{1,0:T(8,128)(2,1)} %param.9), channel_id=1, source_target_pairs={{0,4},{1,5},{2,6},{3,7},{4,0},{5,1},{6,2},{7,3},{8,12},{9,13},{10,... | collective-permute-start | bytes 221192 | tf_op jit(solution)/shard_map/ppermute | solution.py:107
  6.3 1.5 %collective-permute-start = (bf16[16,2304]{1,0:T(8,128)(2,1)}, bf16[16,2304]{1,0:T(8,128)(2,1)S(1)}, u32[]{:S(2)}, u32[]{:S(2)}) collective-permute-start(bf16[16,2304]{1,0:T(8,128)(2,1)} %param.9), channel_id=1, source_target_pairs={{0,2},{1,3},{2,0},{3,1},{4,6},{5,7},{6,4},{7,5},{8,10},{9,11},{10,... | collective-permute-start | bytes 221192 | tf_op jit(solution)/shard_map/ppermute | solution.py:107
  8.1 1.1 %constant_dynamic-update-slice_fusion.9 = bf16[256,2304]{1,0:T(8,128)(2,1)S(1)} fusion(bf16[128,2304]{1,0:T(8,128)(2,1)} %refs_4_.1), kind=kLoop, calls=%fused_computation.43 | loop fusion | bytes 1179648
  9.2 1.6 %broadcast_multiply_fusion.2 = (f32[128,2304]{1,0:T(8,128)S(1)}, f32[128,2304]{1,0:T(8,128)S(1)}) fusion(f32[128,2304]{1,0:T(8,128)S(1)} %copy-done.2, f32[128,2304]{1,0:T(8,128)} %param.14), kind=kLoop, calls=%fused_computation.11 | loop fusion | flops 589824 | bytes 4718592 | tf_op jit(solution)/shard_map/mul | solution.py:148
  11.4 0.7 %copy-done.6 = bf16[16,2304]{1,0:T(8,128)(2,1)S(1)} copy-done((bf16[16,2304]{1,0:T(8,128)(2,1)S(1)}, bf16[16,2304]{1,0:T(8,128)(2,1)}, u32[]{:S(2)}) %copy-start.6) | copy-done | bytes 73752
  12.3 0.5 collective-permute-start.9
  13.3 1.7 %collective-permute-start.2 = (bf16[16,2304]{1,0:T(8,128)(2,1)S(1)}, bf16[16,2304]{1,0:T(8,128)(2,1)S(1)}, u32[]{:S(2)}, u32[]{:S(2)}) collective-permute-start(bf16[16,2304]{1,0:T(8,128)(2,1)S(1)} %collective-permute-done.1), channel_id=1, source_target_pairs={{0,2},{1,3},{2,0},{3,1},{4,6},{5,7},{6,4},{7,5},{8,10},{9,11},{10,... | collective-permute-start | bytes 221192 | tf_op jit(solution)/shard_map/ppermute | solution.py:107
  15.3 4.3 %collective-permute-done.2 = bf16[16,2304]{1,0:T(8,128)(2,1)S(1)} collective-permute-done((bf16[16,2304]{1,0:T(8,128)(2,1)S(1)}, bf16[16,2304]{1,0:T(8,128)(2,1)S(1)}, u32[]{:S(2)}, u32[]{:S(2)}) %collective-permute-start.2) | collective-permute-done | bytes 73760 | tf_op jit(solution)/shard_map/ppermute | solution.py:107
  19.7 1.1 %collective-permute-done.6 = bf16[16,2304]{1,0:T(8,128)(2,1)S(1)} collective-permute-done((bf16[16,2304]{1,0:T(8,128)(2,1)S(1)}, bf16[16,2304]{1,0:T(8,128)(2,1)S(1)}, u32[]{:S(2)}, u32[]{:S(2)}) %collective-permute-start.6) | collective-permute-done | bytes 73760 | tf_op jit(solution)/shard_map/ppermute | solution.py:107
  21.0 0.5 fusion.10
  21.5 0.4 fusion.29
  22.7 1.8 %collective-permute-start.10 = (bf16[32,2304]{1,0:T(8,128)(2,1)S(1)}, bf16[32,2304]{1,0:T(8,128)(2,1)S(1)}, u32[]{:S(2)}, u32[]{:S(2)}) collective-permute-start(bf16[32,2304]{1,0:T(8,128)(2,1)S(1)} %pad_maximum_fusion.3), channel_id=1, source_target_pairs={{0,2},{1,3},{2,0},{3,1},{4,6},{5,7},{6,4},{7,5},{8,10},{9,11},{10,... | collective-permute-start | bytes 442376 | tf_op jit(solution)/shard_map/ppermute | solution.py:107
  24.5 4.5 %collective-permute-done.11 = bf16[32,2304]{1,0:T(8,128)(2,1)S(1)} collective-permute-done((bf16[32,2304]{1,0:T(8,128)(2,1)S(1)}, bf16[32,2304]{1,0:T(8,128)(2,1)S(1)}, u32[]{:S(2)}, u32[]{:S(2)}) %collective-permute-start.11) | collective-permute-done | bytes 147488 | tf_op jit(solution)/shard_map/ppermute | solution.py:107
  29.1 1.8 %collective-permute-start.13 = (bf16[16,2304]{1,0:T(8,128)(2,1)S(1)}, bf16[16,2304]{1,0:T(8,128)(2,1)S(1)}, u32[]{:S(2)}, u32[]{:S(2)}) collective-permute-start(bf16[16,2304]{1,0:T(8,128)(2,1)S(1)} %get-tuple-element.37), channel_id=1, source_target_pairs={{0,8},{1,9},{2,10},{3,11},{4,12},{5,13},{6,14},{7,15},{8,0},{9,1},... | collective-permute-start | bytes 221192 | tf_op jit(solution)/shard_map/ppermute | solution.py:107
  30.9 2.0 %collective-permute-start.14 = (bf16[16,2304]{1,0:T(8,128)(2,1)S(1)}, bf16[16,2304]{1,0:T(8,128)(2,1)S(1)}, u32[]{:S(2)}, u32[]{:S(2)}) collective-permute-start(bf16[16,2304]{1,0:T(8,128)(2,1)S(1)} %get-tuple-element.38), channel_id=1, source_target_pairs={{0,12},{1,13},{2,14},{3,15},{4,8},{5,9},{6,10},{7,11},{8,4},{9,5},... | collective-permute-start | bytes 221192 | tf_op jit(solution)/shard_map/ppermute | solution.py:107
  32.9 0.6 collective-permute-start.12
  33.4 2.8 %collective-permute-done.13 = bf16[16,2304]{1,0:T(8,128)(2,1)S(1)} collective-permute-done((bf16[16,2304]{1,0:T(8,128)(2,1)S(1)}, bf16[16,2304]{1,0:T(8,128)(2,1)S(1)}, u32[]{:S(2)}, u32[]{:S(2)}) %collective-permute-start.13) | collective-permute-done | bytes 73760 | tf_op jit(solution)/shard_map/ppermute | solution.py:107
  36.2 1.5 %collective-permute-done.14 = bf16[16,2304]{1,0:T(8,128)(2,1)S(1)} collective-permute-done((bf16[16,2304]{1,0:T(8,128)(2,1)S(1)}, bf16[16,2304]{1,0:T(8,128)(2,1)S(1)}, u32[]{:S(2)}, u32[]{:S(2)}) %collective-permute-start.14) | collective-permute-done | bytes 73760 | tf_op jit(solution)/shard_map/ppermute | solution.py:107
  38.0 3.2 %collective-permute-start.22 = (bf16[16,2304]{1,0:T(8,128)(2,1)S(1)}, bf16[16,2304]{1,0:T(8,128)(2,1)S(1)}, u32[]{:S(2)}, u32[]{:S(2)}) collective-permute-start(bf16[16,2304]{1,0:T(8,128)(2,1)S(1)} %fusion.20), channel_id=1, source_target_pairs={{0,12},{1,13},{2,14},{3,15},{4,8},{5,9},{6,10},{7,11},{8,4},{9,5},... | collective-permute-start | bytes 221192 | tf_op jit(solution)/shard_map/ppermute | solution.py:107
  41.2 1.3 %collective-permute-start.18 = (bf16[16,2304]{1,0:T(8,128)(2,1)S(1)}, bf16[16,2304]{1,0:T(8,128)(2,1)S(1)}, u32[]{:S(2)}, u32[]{:S(2)}) collective-permute-start(bf16[16,2304]{1,0:T(8,128)(2,1)S(1)} %fusion.20), channel_id=1, source_target_pairs={{0,4},{1,5},{2,6},{3,7},{4,0},{5,1},{6,2},{7,3},{8,12},{9,13},{10,... | collective-permute-start | bytes 221192 | tf_op jit(solution)/shard_map/ppermute | solution.py:107
  42.5 0.5 collective-permute-start.17
  43.1 1.3 %collective-permute-done.22 = bf16[16,2304]{1,0:T(8,128)(2,1)S(1)} collective-permute-done((bf16[16,2304]{1,0:T(8,128)(2,1)S(1)}, bf16[16,2304]{1,0:T(8,128)(2,1)S(1)}, u32[]{:S(2)}, u32[]{:S(2)}) %collective-permute-start.22) | collective-permute-done | bytes 73760 | tf_op jit(solution)/shard_map/ppermute | solution.py:107
  44.4 0.5 collective-permute-start.23
  44.9 2.5 %collective-permute-done.20 = bf16[16,2304]{1,0:T(8,128)(2,1)S(1)} collective-permute-done((bf16[16,2304]{1,0:T(8,128)(2,1)S(1)}, bf16[16,2304]{1,0:T(8,128)(2,1)S(1)}, u32[]{:S(2)}, u32[]{:S(2)}) %collective-permute-start.20) | collective-permute-done | bytes 73760 | tf_op jit(solution)/shard_map/ppermute | solution.py:107
  47.4 0.5 collective-permute-start.21
  48.0 1.5 %collective-permute-start.19 = (bf16[16,2304]{1,0:T(8,128)(2,1)S(1)}, bf16[16,2304]{1,0:T(8,128)(2,1)S(1)}, u32[]{:S(2)}, u32[]{:S(2)}) collective-permute-start(bf16[16,2304]{1,0:T(8,128)(2,1)S(1)} %collective-permute-done.18), channel_id=1, source_target_pairs={{0,2},{1,3},{2,0},{3,1},{4,6},{5,7},{6,4},{7,5},{8,10},{9,11},{10,... | collective-permute-start | bytes 221192 | tf_op jit(solution)/shard_map/ppermute | solution.py:107
  49.5 2.3 %collective-permute-done.21 = bf16[16,2304]{1,0:T(8,128)(2,1)S(1)} collective-permute-done((bf16[16,2304]{1,0:T(8,128)(2,1)S(1)}, bf16[16,2304]{1,0:T(8,128)(2,1)S(1)}, u32[]{:S(2)}, u32[]{:S(2)}) %collective-permute-start.21) | collective-permute-done | bytes 73760 | tf_op jit(solution)/shard_map/ppermute | solution.py:107
  51.9 0.7 %collective-permute-done.19 = bf16[16,2304]{1,0:T(8,128)(2,1)S(1)} collective-permute-done((bf16[16,2304]{1,0:T(8,128)(2,1)S(1)}, bf16[16,2304]{1,0:T(8,128)(2,1)S(1)}, u32[]{:S(2)}, u32[]{:S(2)}) %collective-permute-start.19) | collective-permute-done | bytes 73760 | tf_op jit(solution)/shard_map/ppermute | solution.py:107
  52.8 0.7 %collective-permute-done.25.refs_2_ = bf16[64,2304]{1,0:T(8,128)(2,1)S(1)} collective-permute-done((bf16[64,2304]{1,0:T(8,128)(2,1)S(1)}, bf16[64,2304]{1,0:T(8,128)(2,1)S(1)}, u32[]{:S(2)}, u32[]{:S(2)}) %collective-permute-start.25) | collective-permute-done | bytes 294944 | tf_op jit(solution)/shard_map/ppermute | solution.py:114
  53.5 0.8 %collective-permute-done.24.refs_1_ = bf16[64,2304]{1,0:T(8,128)(2,1)S(1)} collective-permute-done((bf16[64,2304]{1,0:T(8,128)(2,1)S(1)}, bf16[64,2304]{1,0:T(8,128)(2,1)S(1)}, u32[]{:S(2)}, u32[]{:S(2)}) %collective-permute-start.24) | collective-permute-done | bytes 294944 | tf_op jit(solution)/shard_map/ppermute | solution.py:114
  54.3 3.3 %update.1 = (bf16[128,2304]{1,0:T(8,128)(2,1)}, f32[128,2304]{1,0:T(8,128)}, f32[128,2304]{1,0:T(8,128)}, bf16[128,2304]{1,0:T(8,128)(2,1)}, f32[128,2304]{1,0:T(8,128)}, /*index=5*/f32[128,2304]{1,0:T(8,128)}) custom-call(bf16[128,256]{1,0:T(8,128)(2,1)S(1)} %maximum_bitcast_fusion.codes_across, bf16[256,2304]{1,0:T(8,128)(2,1)S(1)} %pad_maximum_fusion.centered, ...), custom_call_target="tpu_custom_call" | custom-call | flops 452984832 | bytes 12976128 | tf_op jit(solution)/shard_map/update/pallas_call | solution.py:80
  (76 shorter events, 3.4 us)
Async XLA Ops:
  0.6 8.5 %copy-start.2 = (f32[128,2304]{1,0:T(8,128)S(1)}, f32[128,2304]{1,0:T(8,128)}, u32[]{:S(2)}) copy-start(f32[128,2304]{1,0:T(8,128)} %param.16) | copy-start | bytes 3538948
  0.6 12.2 %collective-permute-start.3 = (bf16[16,2304]{1,0:T(8,128)(2,1)}, bf16[16,2304]{1,0:T(8,128)(2,1)S(1)}, u32[]{:S(2)}, u32[]{:S(2)}) collective-permute-start(bf16[16,2304]{1,0:T(8,128)(2,1)} %param.9), channel_id=1, source_target_pairs={{0,8},{1,9},{2,10},{3,11},{4,12},{5,13},{6,14},{7,15},{8,0},{9,1},... | collective-permute-start | bytes 221192 | tf_op jit(solution)/shard_map/ppermute | solution.py:107
  4.7 8.2 %collective-permute-start.1 = (bf16[16,2304]{1,0:T(8,128)(2,1)}, bf16[16,2304]{1,0:T(8,128)(2,1)S(1)}, u32[]{:S(2)}, u32[]{:S(2)}) collective-permute-start(bf16[16,2304]{1,0:T(8,128)(2,1)} %param.9), channel_id=1, source_target_pairs={{0,4},{1,5},{2,6},{3,7},{4,0},{5,1},{6,2},{7,3},{8,12},{9,13},{10,... | collective-permute-start | bytes 221192 | tf_op jit(solution)/shard_map/ppermute | solution.py:107
  6.3 7.0 %collective-permute-start = (bf16[16,2304]{1,0:T(8,128)(2,1)}, bf16[16,2304]{1,0:T(8,128)(2,1)S(1)}, u32[]{:S(2)}, u32[]{:S(2)}) collective-permute-start(bf16[16,2304]{1,0:T(8,128)(2,1)} %param.9), channel_id=1, source_target_pairs={{0,2},{1,3},{2,0},{3,1},{4,6},{5,7},{6,4},{7,5},{8,10},{9,11},{10,... | collective-permute-start | bytes 221192 | tf_op jit(solution)/shard_map/ppermute | solution.py:107
  7.8 7.2 %collective-permute-start.5 = (bf16[16,2304]{1,0:T(8,128)(2,1)}, bf16[16,2304]{1,0:T(8,128)(2,1)S(1)}, u32[]{:S(2)}, u32[]{:S(2)}) collective-permute-start(bf16[16,2304]{1,0:T(8,128)(2,1)} %param.9), channel_id=1, source_target_pairs={{0,12},{1,13},{2,14},{3,15},{4,8},{5,9},{6,10},{7,11},{8,4},{9,5},... | collective-permute-start | bytes 221192 | tf_op jit(solution)/shard_map/ppermute | solution.py:107
  8.1 4.0 %collective-permute-start.8 = (f32[128]{0:T(128)}, f32[128]{0:T(128)S(1)}, u32[]{:S(2)}, u32[]{:S(2)}) collective-permute-start(f32[128]{0:T(128)} %param.11), channel_id=1, source_target_pairs={{0,1},{1,0},{2,3},{3,2},{4,5},{5,4},{6,7},{7,6},{8,9},{9,8},{10,11... | collective-permute-start | bytes 1544 | tf_op jit(solution)/shard_map/ppermute | solution.py:114
  9.2 1.7 %copy-start.3 = (f32[128,2304]{1,0:T(8,128)S(1)}, f32[128,2304]{1,0:T(8,128)}, u32[]{:S(2)}) copy-start(f32[128,2304]{1,0:T(8,128)} %param.17) | copy-start | bytes 3538948
  9.2 2.0 %copy-start.4 = (f32[128,2304]{1,0:T(8,128)S(1)}, f32[128,2304]{1,0:T(8,128)}, u32[]{:S(2)}) copy-start(f32[128,2304]{1,0:T(8,128)} %param.15) | copy-start | bytes 3538948
  11.2 1.6 %copy-start.1 = (bf16[128,2304]{1,0:T(8,128)(2,1)S(1)}, bf16[128,2304]{1,0:T(8,128)(2,1)}, u32[]{:S(2)}) copy-start(bf16[128,2304]{1,0:T(8,128)(2,1)} %refs_3_.1) | copy-start | bytes 1769476
  12.1 8.7 %copy-start.7 = (f32[2304]{0:T(1024)S(1)}, f32[2304]{0:T(1024)}, u32[]{:S(2)}) copy-start(f32[2304]{0:T(1024)} %param.13) | copy-start | bytes 27652
  12.3 8.7 %collective-permute-start.9 = (bf16[128,2304]{1,0:T(8,128)(2,1)S(1)}, bf16[128,2304]{1,0:T(8,128)(2,1)S(1)}, u32[]{:S(2)}, u32[]{:S(2)}) collective-permute-start(bf16[128,2304]{1,0:T(8,128)(2,1)S(1)} %copy-done), channel_id=1, source_target_pairs={{0,1},{1,0},{2,3},{3,2},{4,5},{5,4},{6,7},{7,6},{8,9},{9,8},{10,11... | collective-permute-start | bytes 1769480 | tf_op jit(solution)/shard_map/ppermute | solution.py:114
  12.8 8.2 %collective-permute-start.7 = (bf16[128,2304]{1,0:T(8,128)(2,1)S(1)}, bf16[128,2304]{1,0:T(8,128)(2,1)S(1)}, u32[]{:S(2)}, u32[]{:S(2)}) collective-permute-start(bf16[128,2304]{1,0:T(8,128)(2,1)S(1)} %copy-done.1), channel_id=1, source_target_pairs={{0,1},{1,0},{2,3},{3,2},{4,5},{5,4},{6,7},{7,6},{8,9},{9,8},{10,11... | collective-permute-start | bytes 1769480 | tf_op jit(solution)/shard_map/ppermute | solution.py:114
  13.0 6.7 %collective-permute-start.4 = (bf16[16,2304]{1,0:T(8,128)(2,1)S(1)}, bf16[16,2304]{1,0:T(8,128)(2,1)S(1)}, u32[]{:S(2)}, u32[]{:S(2)}) collective-permute-start(bf16[16,2304]{1,0:T(8,128)(2,1)S(1)} %collective-permute-done.3), channel_id=1, source_target_pairs={{0,2},{1,3},{2,0},{3,1},{4,6},{5,7},{6,4},{7,5},{8,10},{9,11},{10,... | collective-permute-start | bytes 221192 | tf_op jit(solution)/shard_map/ppermute | solution.py:107
  13.3 6.4 %collective-permute-start.2 = (bf16[16,2304]{1,0:T(8,128)(2,1)S(1)}, bf16[16,2304]{1,0:T(8,128)(2,1)S(1)}, u32[]{:S(2)}, u32[]{:S(2)}) collective-permute-start(bf16[16,2304]{1,0:T(8,128)(2,1)S(1)} %collective-permute-done.1), channel_id=1, source_target_pairs={{0,2},{1,3},{2,0},{3,1},{4,6},{5,7},{6,4},{7,5},{8,10},{9,11},{10,... | collective-permute-start | bytes 221192 | tf_op jit(solution)/shard_map/ppermute | solution.py:107
  15.0 5.7 %collective-permute-start.6 = (bf16[16,2304]{1,0:T(8,128)(2,1)S(1)}, bf16[16,2304]{1,0:T(8,128)(2,1)S(1)}, u32[]{:S(2)}, u32[]{:S(2)}) collective-permute-start(bf16[16,2304]{1,0:T(8,128)(2,1)S(1)} %collective-permute-done.5), channel_id=1, source_target_pairs={{0,2},{1,3},{2,0},{3,1},{4,6},{5,7},{6,4},{7,5},{8,10},{9,11},{10,... | collective-permute-start | bytes 221192 | tf_op jit(solution)/shard_map/ppermute | solution.py:107
  20.9 17.2 %collective-permute-start.16 = (bf16[128,2304]{1,0:T(8,128)(2,1)S(1)}, bf16[128,2304]{1,0:T(8,128)(2,1)S(1)}, u32[]{:S(2)}, u32[]{:S(2)}) collective-permute-start(bf16[128,2304]{1,0:T(8,128)(2,1)S(1)} %subtract_convert_fusion), channel_id=1, source_target_pairs={{0,1},{1,0},{2,3},{3,2},{4,5},{5,4},{6,7},{7,6},{8,9},{9,8},{10,11... | collective-permute-start | bytes 1769480 | tf_op jit(solution)/shard_map/ppermute | solution.py:114
  22.4 6.7 %collective-permute-start.11 = (bf16[32,2304]{1,0:T(8,128)(2,1)S(1)}, bf16[32,2304]{1,0:T(8,128)(2,1)S(1)}, u32[]{:S(2)}, u32[]{:S(2)}) collective-permute-start(bf16[32,2304]{1,0:T(8,128)(2,1)S(1)} %pad_maximum_fusion.4), channel_id=1, source_target_pairs={{0,2},{1,3},{2,0},{3,1},{4,6},{5,7},{6,4},{7,5},{8,10},{9,11},{10,... | collective-permute-start | bytes 442376 | tf_op jit(solution)/shard_map/ppermute | solution.py:107
  22.7 10.1 %collective-permute-start.10 = (bf16[32,2304]{1,0:T(8,128)(2,1)S(1)}, bf16[32,2304]{1,0:T(8,128)(2,1)S(1)}, u32[]{:S(2)}, u32[]{:S(2)}) collective-permute-start(bf16[32,2304]{1,0:T(8,128)(2,1)S(1)} %pad_maximum_fusion.3), channel_id=1, source_target_pairs={{0,2},{1,3},{2,0},{3,1},{4,6},{5,7},{6,4},{7,5},{8,10},{9,11},{10,... | collective-permute-start | bytes 442376 | tf_op jit(solution)/shard_map/ppermute | solution.py:107
  29.1 7.1 %collective-permute-start.13 = (bf16[16,2304]{1,0:T(8,128)(2,1)S(1)}, bf16[16,2304]{1,0:T(8,128)(2,1)S(1)}, u32[]{:S(2)}, u32[]{:S(2)}) collective-permute-start(bf16[16,2304]{1,0:T(8,128)(2,1)S(1)} %get-tuple-element.37), channel_id=1, source_target_pairs={{0,8},{1,9},{2,10},{3,11},{4,12},{5,13},{6,14},{7,15},{8,0},{9,1},... | collective-permute-start | bytes 221192 | tf_op jit(solution)/shard_map/ppermute | solution.py:107
  30.9 6.9 %collective-permute-start.14 = (bf16[16,2304]{1,0:T(8,128)(2,1)S(1)}, bf16[16,2304]{1,0:T(8,128)(2,1)S(1)}, u32[]{:S(2)}, u32[]{:S(2)}) collective-permute-start(bf16[16,2304]{1,0:T(8,128)(2,1)S(1)} %get-tuple-element.38), channel_id=1, source_target_pairs={{0,12},{1,13},{2,14},{3,15},{4,8},{5,9},{6,10},{7,11},{8,4},{9,5},... | collective-permute-start | bytes 221192 | tf_op jit(solution)/shard_map/ppermute | solution.py:107
  32.9 5.1 %collective-permute-start.12 = (bf16[16,2304]{1,0:T(8,128)(2,1)S(1)}, bf16[16,2304]{1,0:T(8,128)(2,1)S(1)}, u32[]{:S(2)}, u32[]{:S(2)}) collective-permute-start(bf16[16,2304]{1,0:T(8,128)(2,1)S(1)} %fusion.13), channel_id=1, source_target_pairs={{0,4},{1,5},{2,6},{3,7},{4,0},{5,1},{6,2},{7,3},{8,12},{9,13},{10,... | collective-permute-start | bytes 221192 | tf_op jit(solution)/shard_map/ppermute | solution.py:107
  33.4 4.6 %collective-permute-start.15 = (bf16[128,128]{0,1:T(8,128)(2,1)S(1)}, bf16[128,128]{0,1:T(8,128)(2,1)S(1)}, u32[]{:S(2)}, u32[]{:S(2)}) collective-permute-start(bf16[128,128]{0,1:T(8,128)(2,1)S(1)} %get-tuple-element.44), channel_id=1, source_target_pairs={{0,1},{1,0},{2,3},{3,2},{4,5},{5,4},{6,7},{7,6},{8,9},{9,8},{10,11... | collective-permute-start | bytes 98312 | tf_op jit(solution)/shard_map/ppermute | solution.py:114
  38.0 14.6 %copy-start.5 = (bf16[16,2304]{1,0:T(8,128)(2,1)}, bf16[16,2304]{1,0:T(8,128)(2,1)S(1)}, u32[]{:S(2)}) copy-start(bf16[16,2304]{1,0:T(8,128)(2,1)S(1)} %fusion.20) | copy-start | bytes 221188
  38.0 6.4 %collective-permute-start.22 = (bf16[16,2304]{1,0:T(8,128)(2,1)S(1)}, bf16[16,2304]{1,0:T(8,128)(2,1)S(1)}, u32[]{:S(2)}, u32[]{:S(2)}) collective-permute-start(bf16[16,2304]{1,0:T(8,128)(2,1)S(1)} %fusion.20), channel_id=1, source_target_pairs={{0,12},{1,13},{2,14},{3,15},{4,8},{5,9},{6,10},{7,11},{8,4},{9,5},... | collective-permute-start | bytes 221192 | tf_op jit(solution)/shard_map/ppermute | solution.py:107
  41.2 6.2 %collective-permute-start.20 = (bf16[16,2304]{1,0:T(8,128)(2,1)S(1)}, bf16[16,2304]{1,0:T(8,128)(2,1)S(1)}, u32[]{:S(2)}, u32[]{:S(2)}) collective-permute-start(bf16[16,2304]{1,0:T(8,128)(2,1)S(1)} %fusion.20), channel_id=1, source_target_pairs={{0,8},{1,9},{2,10},{3,11},{4,12},{5,13},{6,14},{7,15},{8,0},{9,1},... | collective-permute-start | bytes 221192 | tf_op jit(solution)/shard_map/ppermute | solution.py:107
  41.2 6.7 %collective-permute-start.18 = (bf16[16,2304]{1,0:T(8,128)(2,1)S(1)}, bf16[16,2304]{1,0:T(8,128)(2,1)S(1)}, u32[]{:S(2)}, u32[]{:S(2)}) collective-permute-start(bf16[16,2304]{1,0:T(8,128)(2,1)S(1)} %fusion.20), channel_id=1, source_target_pairs={{0,4},{1,5},{2,6},{3,7},{4,0},{5,1},{6,2},{7,3},{8,12},{9,13},{10,... | collective-permute-start | bytes 221192 | tf_op jit(solution)/shard_map/ppermute | solution.py:107
  42.5 6.9 %collective-permute-start.17 = (bf16[16,2304]{1,0:T(8,128)(2,1)S(1)}, bf16[16,2304]{1,0:T(8,128)(2,1)S(1)}, u32[]{:S(2)}, u32[]{:S(2)}) collective-permute-start(bf16[16,2304]{1,0:T(8,128)(2,1)S(1)} %fusion.20), channel_id=1, source_target_pairs={{0,2},{1,3},{2,0},{3,1},{4,6},{5,7},{6,4},{7,5},{8,10},{9,11},{10,... | collective-permute-start | bytes 221192 | tf_op jit(solution)/shard_map/ppermute | solution.py:107
  44.4 5.0 %collective-permute-start.23 = (bf16[16,2304]{1,0:T(8,128)(2,1)S(1)}, bf16[16,2304]{1,0:T(8,128)(2,1)S(1)}, u32[]{:S(2)}, u32[]{:S(2)}) collective-permute-start(bf16[16,2304]{1,0:T(8,128)(2,1)S(1)} %collective-permute-done.22), channel_id=1, source_target_pairs={{0,2},{1,3},{2,0},{3,1},{4,6},{5,7},{6,4},{7,5},{8,10},{9,11},{10,... | collective-permute-start | bytes 221192 | tf_op jit(solution)/shard_map/ppermute | solution.py:107
  47.4 4.4 %collective-permute-start.21 = (bf16[16,2304]{1,0:T(8,128)(2,1)S(1)}, bf16[16,2304]{1,0:T(8,128)(2,1)S(1)}, u32[]{:S(2)}, u32[]{:S(2)}) collective-permute-start(bf16[16,2304]{1,0:T(8,128)(2,1)S(1)} %collective-permute-done.20), channel_id=1, source_target_pairs={{0,2},{1,3},{2,0},{3,1},{4,6},{5,7},{6,4},{7,5},{8,10},{9,11},{10,... | collective-permute-start | bytes 221192 | tf_op jit(solution)/shard_map/ppermute | solution.py:107
  48.0 4.7 %collective-permute-start.19 = (bf16[16,2304]{1,0:T(8,128)(2,1)S(1)}, bf16[16,2304]{1,0:T(8,128)(2,1)S(1)}, u32[]{:S(2)}, u32[]{:S(2)}) collective-permute-start(bf16[16,2304]{1,0:T(8,128)(2,1)S(1)} %collective-permute-done.18), channel_id=1, source_target_pairs={{0,2},{1,3},{2,0},{3,1},{4,6},{5,7},{6,4},{7,5},{8,10},{9,11},{10,... | collective-permute-start | bytes 221192 | tf_op jit(solution)/shard_map/ppermute | solution.py:107
  51.8 1.6 %collective-permute-start.25 = (bf16[64,2304]{1,0:T(8,128)(2,1)S(1)}, bf16[64,2304]{1,0:T(8,128)(2,1)S(1)}, u32[]{:S(2)}, u32[]{:S(2)}) collective-permute-start(bf16[64,2304]{1,0:T(8,128)(2,1)S(1)} %pad_maximum_fusion.2), channel_id=1, source_target_pairs={{0,1},{1,0},{2,3},{3,2},{4,5},{5,4},{6,7},{7,6},{8,9},{9,8},{10,11... | collective-permute-start | bytes 884744 | tf_op jit(solution)/shard_map/ppermute | solution.py:114
  52.6 1.6 %collective-permute-start.24 = (bf16[64,2304]{1,0:T(8,128)(2,1)S(1)}, bf16[64,2304]{1,0:T(8,128)(2,1)S(1)}, u32[]{:S(2)}, u32[]{:S(2)}) collective-permute-start(bf16[64,2304]{1,0:T(8,128)(2,1)S(1)} %pad_maximum_fusion.1), channel_id=1, source_target_pairs={{0,1},{1,0},{2,3},{3,2},{4,5},{5,4},{6,7},{7,6},{8,9},{9,8},{10,11... | collective-permute-start | bytes 884744 | tf_op jit(solution)/shard_map/ppermute | solution.py:114
  (3 other events, 3.6 us)

commit v13 on v11

--- a/solution.py
+++ b/solution.py
@@ -28,9 +28,12 @@
     tiles = encoder.shape[1] // columns
     part = min(32, encoder.shape[0])
 
-    def write(t, i):
-        at = pl.ds(t * columns, columns)
-        return pltpu.make_async_copy(held[i].at[:, at], outs[i].at[:, at], sem.at[t, i])
+    groups = next(n for n in (3, 1) if tiles % n == 0)
+    wide = encoder.shape[1] // groups
+
+    def write(group, i):
+        at = pl.ds(group * wide, wide)
+        return pltpu.make_async_copy(held[i].at[:, at], outs[i].at[:, at], sem.at[group, i])
 
     start = 0
     for one in errors:
@@ -55,17 +58,18 @@
                 ).astype(jnp.bfloat16)
                 held[3 * which + 1][some] = moment
                 held[3 * which + 2][some] = square
-            for i in range(3 * which, 3 * which + 3):
-                write(t, i).start()
+            if (t + 1) * columns % wide == 0:
+                for i in range(3 * which, 3 * which + 3):
+                    write(t * columns // wide, i).start()
 
     codes_t = codes_across[...]
     advance(1, codes_t, error_all, decoder)
     signal = inner_last(decoder[...], error_all[...])
     delta_t = jnp.where(codes_t.astype(jnp.float32) > 0, signal, 0.0).astype(jnp.bfloat16)
     advance(0, delta_t, centered, encoder)
-    for t in range(tiles):
+    for group in range(groups):
         for i in range(6):
-            write(t, i).wait()
+            write(group, i).wait()
 
 
 def update(total_rows, codes_across, centered, errors, weights, moments):
@@ -160,16 +164,16 @@
 
     def pair_sums(first, last, after=None):
         given = jnp.concatenate(parts[first + 1 : last : 2], 0).astype(jnp.bfloat16)
+        if after is not None:
+            given, _ = lax.optimization_barrier((given, after))
         came = to_chip(given, 1)
-        if after is not None:
-            came, _ = lax.optimization_barrier((came, after))
         return [
             parts[k] + came[at * rows_here : (at + 1) * rows_here].astype(jnp.float32)
             for at, k in enumerate(range(first, last, 2))
         ]
 
     far = [one.astype(jnp.bfloat16) for one in pair_sums(4, chips)]
-    own, near = pair_sums(0, 4, far)
+    own, near = pair_sums(0, 4, (other_codes, other_centered))
     summed = own + to_chip(near.astype(jnp.bfloat16), 2).astype(jnp.float32)
     for k, one in enumerate(far, 2):
         summed = summed + to_chip(one, 2 * k).astype(jnp.float32)

time: 55.8 us -> 54.6 us (0.978)
  waiting for transfers between devices: 22.4 us -> 21 us
    ppermute x19, waiting for transfers between devices: 20.8 us -> 19.2 us  [to_chip(): lax.ppermute(block, 'latent', [(i, i ^ 2 * distance) for i in range(size)])]
  transfers between devices with their start and end apart: 26 -> 26, of which waited for: 13 -> 15; matrix products, arithmetic and copies ran while one was open for 5% -> 5% of each run, Pallas kernels for 0% -> 0%
where the time goes in v13:
time: 54.6 us; the launch traced here: 54.4 us
  starting transfers between devices  25.9 us (47%)
  waiting for transfers between devices  21 us (38%)
  Pallas kernels  3.49 us (6%)
  local copies, waits for them, and re-layouts  1.33 us (2%)
  matrix products  1.26 us (2%)
  between operations  0.99 us (2%)
    ppermute x19, starting transfers between devices, to_chip(): lax.ppermute(block, 'latent', [(i, i ^ 2 * distance) for i in range(size)])  24.6 us
    ppermute x19, waiting for transfers between devices, to_chip(): lax.ppermute(block, 'latent', [(i, i ^ 2 * distance) for i in range(size)])  19.2 us
    pallas_call x1, Pallas kernels, update(): pl.pallas_call(functools.partial(update_kernel, columns, float(total_rows...  3.49 us
    ppermute x7, waiting for transfers between devices, to_other_core(): return lax.ppermute(block, 'latent', [(i, i ^ 1) for i in range(size)])  1.85 us
    ppermute x7, starting transfers between devices, to_other_core(): return lax.ppermute(block, 'latent', [(i, i ^ 1) for i in range(size)])  1.32 us
    unnamed x35, local copies, waits for them, and re-layouts  1.25 us
  transfers between devices with their start and end apart: 26, of which 15 were waited for; matrix products, arithmetic and copies ran while one was open for 5% of the time, Pallas kernels for 0%

profile of v13, /device:TPU:0, one launch (start us, length us, event | category | flops | bytes accessed | tf_op | source)
XLA Modules:
  0.0 54.4 jit_solution(7953149969661400936)
XLA Ops:
  0.7 4.1 %collective-permute-start.3 = (bf16[16,2304]{1,0:T(8,128)(2,1)}, bf16[16,2304]{1,0:T(8,128)(2,1)S(1)}, u32[]{:S(2)}, u32[]{:S(2)}) collective-permute-start(bf16[16,2304]{1,0:T(8,128)(2,1)} %param.9), channel_id=1, source_target_pairs={{0,8},{1,9},{2,10},{3,11},{4,12},{5,13},{6,14},{7,15},{8,0},{9,1},... | collective-permute-start | bytes 221192 | tf_op jit(solution)/shard_map/ppermute | solution.py:111
  4.8 1.6 %collective-permute-start.1 = (bf16[16,2304]{1,0:T(8,128)(2,1)}, bf16[16,2304]{1,0:T(8,128)(2,1)S(1)}, u32[]{:S(2)}, u32[]{:S(2)}) collective-permute-start(bf16[16,2304]{1,0:T(8,128)(2,1)} %param.9), channel_id=1, source_target_pairs={{0,4},{1,5},{2,6},{3,7},{4,0},{5,1},{6,2},{7,3},{8,12},{9,13},{10,... | collective-permute-start | bytes 221192 | tf_op jit(solution)/shard_map/ppermute | solution.py:111
  6.4 1.5 %collective-permute-start = (bf16[16,2304]{1,0:T(8,128)(2,1)}, bf16[16,2304]{1,0:T(8,128)(2,1)S(1)}, u32[]{:S(2)}, u32[]{:S(2)}) collective-permute-start(bf16[16,2304]{1,0:T(8,128)(2,1)} %param.9), channel_id=1, source_target_pairs={{0,2},{1,3},{2,0},{3,1},{4,6},{5,7},{6,4},{7,5},{8,10},{9,11},{10,... | collective-permute-start | bytes 221192 | tf_op jit(solution)/shard_map/ppermute | solution.py:111
  8.1 1.1 %constant_dynamic-update-slice_fusion.9 = bf16[256,2304]{1,0:T(8,128)(2,1)S(1)} fusion(bf16[128,2304]{1,0:T(8,128)(2,1)} %refs_4_.1), kind=kLoop, calls=%fused_computation.39 | loop fusion | bytes 1179648
  10.0 1.0 %collective-permute-start.4 = (bf16[16,2304]{1,0:T(8,128)(2,1)S(1)}, bf16[16,2304]{1,0:T(8,128)(2,1)S(1)}, u32[]{:S(2)}, u32[]{:S(2)}) collective-permute-start(bf16[16,2304]{1,0:T(8,128)(2,1)S(1)} %collective-permute-done.3), channel_id=1, source_target_pairs={{0,2},{1,3},{2,0},{3,1},{4,6},{5,7},{6,4},{7,5},{8,10},{9,11},{10,... | collective-permute-start | bytes 221192 | tf_op jit(solution)/shard_map/ppermute | solution.py:111
  11.0 1.4 %collective-permute-start.2 = (bf16[16,2304]{1,0:T(8,128)(2,1)S(1)}, bf16[16,2304]{1,0:T(8,128)(2,1)S(1)}, u32[]{:S(2)}, u32[]{:S(2)}) collective-permute-start(bf16[16,2304]{1,0:T(8,128)(2,1)S(1)} %collective-permute-done.1), channel_id=1, source_target_pairs={{0,2},{1,3},{2,0},{3,1},{4,6},{5,7},{6,4},{7,5},{8,10},{9,11},{10,... | collective-permute-start | bytes 221192 | tf_op jit(solution)/shard_map/ppermute | solution.py:111
  12.4 1.8 %collective-permute-done.5 = bf16[16,2304]{1,0:T(8,128)(2,1)S(1)} collective-permute-done((bf16[16,2304]{1,0:T(8,128)(2,1)}, bf16[16,2304]{1,0:T(8,128)(2,1)S(1)}, u32[]{:S(2)}, u32[]{:S(2)}) %collective-permute-start.5) | collective-permute-done | bytes 73760 | tf_op jit(solution)/shard_map/ppermute | solution.py:111
  14.2 0.5 collective-permute-start.6
  14.8 1.9 %collective-permute-done.2 = bf16[16,2304]{1,0:T(8,128)(2,1)S(1)} collective-permute-done((bf16[16,2304]{1,0:T(8,128)(2,1)S(1)}, bf16[16,2304]{1,0:T(8,128)(2,1)S(1)}, u32[]{:S(2)}, u32[]{:S(2)}) %collective-permute-start.2) | collective-permute-done | bytes 73760 | tf_op jit(solution)/shard_map/ppermute | solution.py:111
  16.7 1.9 %collective-permute-done.6 = bf16[16,2304]{1,0:T(8,128)(2,1)S(1)} collective-permute-done((bf16[16,2304]{1,0:T(8,128)(2,1)S(1)}, bf16[16,2304]{1,0:T(8,128)(2,1)S(1)}, u32[]{:S(2)}, u32[]{:S(2)}) %collective-permute-start.6) | collective-permute-done | bytes 73760 | tf_op jit(solution)/shard_map/ppermute | solution.py:111
  20.1 0.5 collective-permute-start.10
  20.7 0.6 %collective-permute-start.14 = (bf16[32,2304]{1,0:T(8,128)(2,1)S(1)}, bf16[32,2304]{1,0:T(8,128)(2,1)S(1)}, u32[]{:S(2)}, u32[]{:S(2)}) collective-permute-start(bf16[32,2304]{1,0:T(8,128)(2,1)S(1)} %pad_maximum_fusion.4), channel_id=1, source_target_pairs={{0,2},{1,3},{2,0},{3,1},{4,6},{5,7},{6,4},{7,5},{8,10},{9,11},{10,... | collective-permute-start | bytes 442376 | tf_op jit(solution)/shard_map/ppermute | solution.py:111
  21.5 1.4 %collective-permute-start.12 = (bf16[32,2304]{1,0:T(8,128)(2,1)S(1)}, bf16[32,2304]{1,0:T(8,128)(2,1)S(1)}, u32[]{:S(2)}, u32[]{:S(2)}) collective-permute-start(bf16[32,2304]{1,0:T(8,128)(2,1)S(1)} %pad_maximum_fusion.3), channel_id=1, source_target_pairs={{0,2},{1,3},{2,0},{3,1},{4,6},{5,7},{6,4},{7,5},{8,10},{9,11},{10,... | collective-permute-start | bytes 442376 | tf_op jit(solution)/shard_map/ppermute | solution.py:111
  22.9 4.6 %collective-permute-done.14 = bf16[32,2304]{1,0:T(8,128)(2,1)S(1)} collective-permute-done((bf16[32,2304]{1,0:T(8,128)(2,1)S(1)}, bf16[32,2304]{1,0:T(8,128)(2,1)S(1)}, u32[]{:S(2)}, u32[]{:S(2)}) %collective-permute-start.14) | collective-permute-done | bytes 147488 | tf_op jit(solution)/shard_map/ppermute | solution.py:111
  27.5 1.0 %collective-permute-start.15 = (bf16[16,2304]{1,0:T(8,128)(2,1)S(1)}, bf16[16,2304]{1,0:T(8,128)(2,1)S(1)}, u32[]{:S(2)}, u32[]{:S(2)}) collective-permute-start(bf16[16,2304]{1,0:T(8,128)(2,1)S(1)} %get-tuple-element.27), channel_id=1, source_target_pairs={{0,8},{1,9},{2,10},{3,11},{4,12},{5,13},{6,14},{7,15},{8,0},{9,1},... | collective-permute-start | bytes 221192 | tf_op jit(solution)/shard_map/ppermute | solution.py:111
  28.5 2.0 %collective-permute-start.16 = (bf16[16,2304]{1,0:T(8,128)(2,1)S(1)}, bf16[16,2304]{1,0:T(8,128)(2,1)S(1)}, u32[]{:S(2)}, u32[]{:S(2)}) collective-permute-start(bf16[16,2304]{1,0:T(8,128)(2,1)S(1)} %get-tuple-element.28), channel_id=1, source_target_pairs={{0,12},{1,13},{2,14},{3,15},{4,8},{5,9},{6,10},{7,11},{8,4},{9,5},... | collective-permute-start | bytes 221192 | tf_op jit(solution)/shard_map/ppermute | solution.py:111
  30.5 0.7 %collective-permute-start.13 = (bf16[16,2304]{1,0:T(8,128)(2,1)S(1)}, bf16[16,2304]{1,0:T(8,128)(2,1)S(1)}, u32[]{:S(2)}, u32[]{:S(2)}) collective-permute-start(bf16[16,2304]{1,0:T(8,128)(2,1)S(1)} %fusion.15), channel_id=1, source_target_pairs={{0,4},{1,5},{2,6},{3,7},{4,0},{5,1},{6,2},{7,3},{8,12},{9,13},{10,... | collective-permute-start | bytes 221192 | tf_op jit(solution)/shard_map/ppermute | solution.py:111
  31.2 3.8 %collective-permute-done.15 = bf16[16,2304]{1,0:T(8,128)(2,1)S(1)} collective-permute-done((bf16[16,2304]{1,0:T(8,128)(2,1)S(1)}, bf16[16,2304]{1,0:T(8,128)(2,1)S(1)}, u32[]{:S(2)}, u32[]{:S(2)}) %collective-permute-start.15) | collective-permute-done | bytes 73760 | tf_op jit(solution)/shard_map/ppermute | solution.py:111
  35.0 0.7 %collective-permute-done.13 = bf16[16,2304]{1,0:T(8,128)(2,1)S(1)} collective-permute-done((bf16[16,2304]{1,0:T(8,128)(2,1)S(1)}, bf16[16,2304]{1,0:T(8,128)(2,1)S(1)}, u32[]{:S(2)}, u32[]{:S(2)}) %collective-permute-start.13) | collective-permute-done | bytes 73760 | tf_op jit(solution)/shard_map/ppermute | solution.py:111
  35.7 2.1 %collective-permute-start.22 = (bf16[16,2304]{1,0:T(8,128)(2,1)S(1)}, bf16[16,2304]{1,0:T(8,128)(2,1)S(1)}, u32[]{:S(2)}, u32[]{:S(2)}) collective-permute-start(bf16[16,2304]{1,0:T(8,128)(2,1)S(1)} %fusion.20), channel_id=1, source_target_pairs={{0,12},{1,13},{2,14},{3,15},{4,8},{5,9},{6,10},{7,11},{8,4},{9,5},... | collective-permute-start | bytes 221192 | tf_op jit(solution)/shard_map/ppermute | solution.py:111
  37.8 2.4 %collective-permute-start.18 = (bf16[16,2304]{1,0:T(8,128)(2,1)S(1)}, bf16[16,2304]{1,0:T(8,128)(2,1)S(1)}, u32[]{:S(2)}, u32[]{:S(2)}) collective-permute-start(bf16[16,2304]{1,0:T(8,128)(2,1)S(1)} %fusion.20), channel_id=1, source_target_pairs={{0,4},{1,5},{2,6},{3,7},{4,0},{5,1},{6,2},{7,3},{8,12},{9,13},{10,... | collective-permute-start | bytes 221192 | tf_op jit(solution)/shard_map/ppermute | solution.py:111
  40.2 1.0 %collective-permute-start.17 = (bf16[16,2304]{1,0:T(8,128)(2,1)S(1)}, bf16[16,2304]{1,0:T(8,128)(2,1)S(1)}, u32[]{:S(2)}, u32[]{:S(2)}) collective-permute-start(bf16[16,2304]{1,0:T(8,128)(2,1)S(1)} %fusion.20), channel_id=1, source_target_pairs={{0,2},{1,3},{2,0},{3,1},{4,6},{5,7},{6,4},{7,5},{8,10},{9,11},{10,... | collective-permute-start | bytes 221192 | tf_op jit(solution)/shard_map/ppermute | solution.py:111
  41.3 0.7 %collective-permute-done.22 = bf16[16,2304]{1,0:T(8,128)(2,1)S(1)} collective-permute-done((bf16[16,2304]{1,0:T(8,128)(2,1)S(1)}, bf16[16,2304]{1,0:T(8,128)(2,1)S(1)}, u32[]{:S(2)}, u32[]{:S(2)}) %collective-permute-start.22) | collective-permute-done | bytes 73760 | tf_op jit(solution)/shard_map/ppermute | solution.py:111
  42.0 1.2 %collective-permute-start.23 = (bf16[16,2304]{1,0:T(8,128)(2,1)S(1)}, bf16[16,2304]{1,0:T(8,128)(2,1)S(1)}, u32[]{:S(2)}, u32[]{:S(2)}) collective-permute-start(bf16[16,2304]{1,0:T(8,128)(2,1)S(1)} %collective-permute-done.22), channel_id=1, source_target_pairs={{0,2},{1,3},{2,0},{3,1},{4,6},{5,7},{6,4},{7,5},{8,10},{9,11},{10,... | collective-permute-start | bytes 221192 | tf_op jit(solution)/shard_map/ppermute | solution.py:111
  43.5 1.3 %collective-permute-start.21 = (bf16[16,2304]{1,0:T(8,128)(2,1)S(1)}, bf16[16,2304]{1,0:T(8,128)(2,1)S(1)}, u32[]{:S(2)}, u32[]{:S(2)}) collective-permute-start(bf16[16,2304]{1,0:T(8,128)(2,1)S(1)} %collective-permute-done.20), channel_id=1, source_target_pairs={{0,2},{1,3},{2,0},{3,1},{4,6},{5,7},{6,4},{7,5},{8,10},{9,11},{10,... | collective-permute-start | bytes 221192 | tf_op jit(solution)/shard_map/ppermute | solution.py:111
  44.9 0.7 %collective-permute-start.19 = (bf16[16,2304]{1,0:T(8,128)(2,1)S(1)}, bf16[16,2304]{1,0:T(8,128)(2,1)S(1)}, u32[]{:S(2)}, u32[]{:S(2)}) collective-permute-start(bf16[16,2304]{1,0:T(8,128)(2,1)S(1)} %collective-permute-done.18), channel_id=1, source_target_pairs={{0,2},{1,3},{2,0},{3,1},{4,6},{5,7},{6,4},{7,5},{8,10},{9,11},{10,... | collective-permute-start | bytes 221192 | tf_op jit(solution)/shard_map/ppermute | solution.py:111
  45.6 1.2 %collective-permute-done.23 = bf16[16,2304]{1,0:T(8,128)(2,1)S(1)} collective-permute-done((bf16[16,2304]{1,0:T(8,128)(2,1)S(1)}, bf16[16,2304]{1,0:T(8,128)(2,1)S(1)}, u32[]{:S(2)}, u32[]{:S(2)}) %collective-permute-start.23) | collective-permute-done | bytes 73760 | tf_op jit(solution)/shard_map/ppermute | solution.py:111
  46.8 1.5 %collective-permute-done.21 = bf16[16,2304]{1,0:T(8,128)(2,1)S(1)} collective-permute-done((bf16[16,2304]{1,0:T(8,128)(2,1)S(1)}, bf16[16,2304]{1,0:T(8,128)(2,1)S(1)}, u32[]{:S(2)}, u32[]{:S(2)}) %collective-permute-start.21) | collective-permute-done | bytes 73760 | tf_op jit(solution)/shard_map/ppermute | solution.py:111
  48.4 0.9 %collective-permute-done.19 = bf16[16,2304]{1,0:T(8,128)(2,1)S(1)} collective-permute-done((bf16[16,2304]{1,0:T(8,128)(2,1)S(1)}, bf16[16,2304]{1,0:T(8,128)(2,1)S(1)}, u32[]{:S(2)}, u32[]{:S(2)}) %collective-permute-start.19) | collective-permute-done | bytes 73760 | tf_op jit(solution)/shard_map/ppermute | solution.py:111
  49.4 0.5 collective-permute-done.25.refs_2_
  49.9 1.0 %collective-permute-done.24.refs_1_ = bf16[64,2304]{1,0:T(8,128)(2,1)S(1)} collective-permute-done((bf16[64,2304]{1,0:T(8,128)(2,1)S(1)}, bf16[64,2304]{1,0:T(8,128)(2,1)S(1)}, u32[]{:S(2)}, u32[]{:S(2)}) %collective-permute-start.24) | collective-permute-done | bytes 294944 | tf_op jit(solution)/shard_map/ppermute | solution.py:118
  50.9 3.5 %update.1 = (bf16[128,2304]{1,0:T(8,128)(2,1)}, f32[128,2304]{1,0:T(8,128)}, f32[128,2304]{1,0:T(8,128)}, bf16[128,2304]{1,0:T(8,128)(2,1)}, f32[128,2304]{1,0:T(8,128)}, /*index=5*/f32[128,2304]{1,0:T(8,128)}) custom-call(bf16[128,256]{1,0:T(8,128)(2,1)S(1)} %maximum_bitcast_fusion.codes_across, bf16[256,2304]{1,0:T(8,128)(2,1)S(1)} %pad_maximum_fusion.centered, ...), custom_call_target="tpu_custom_call" | custom-call | flops 452984832 | bytes 12976128 | tf_op jit(solution)/shard_map/update/pallas_call | solution.py:84
  (76 shorter events, 3.6 us)
Async XLA Ops:
  0.7 17.9 %copy-start.8 = (f32[2304]{0:T(1024)S(1)}, f32[2304]{0:T(1024)}, u32[]{:S(2)}) copy-start(f32[2304]{0:T(1024)} %param.13) | copy-start | bytes 27652
  0.7 9.2 %collective-permute-start.3 = (bf16[16,2304]{1,0:T(8,128)(2,1)}, bf16[16,2304]{1,0:T(8,128)(2,1)S(1)}, u32[]{:S(2)}, u32[]{:S(2)}) collective-permute-start(bf16[16,2304]{1,0:T(8,128)(2,1)} %param.9), channel_id=1, source_target_pairs={{0,8},{1,9},{2,10},{3,11},{4,12},{5,13},{6,14},{7,15},{8,0},{9,1},... | collective-permute-start | bytes 221192 | tf_op jit(solution)/shard_map/ppermute | solution.py:111
  4.8 5.2 %collective-permute-start.1 = (bf16[16,2304]{1,0:T(8,128)(2,1)}, bf16[16,2304]{1,0:T(8,128)(2,1)S(1)}, u32[]{:S(2)}, u32[]{:S(2)}) collective-permute-start(bf16[16,2304]{1,0:T(8,128)(2,1)} %param.9), channel_id=1, source_target_pairs={{0,4},{1,5},{2,6},{3,7},{4,0},{5,1},{6,2},{7,3},{8,12},{9,13},{10,... | collective-permute-start | bytes 221192 | tf_op jit(solution)/shard_map/ppermute | solution.py:111
  6.4 4.7 %collective-permute-start = (bf16[16,2304]{1,0:T(8,128)(2,1)}, bf16[16,2304]{1,0:T(8,128)(2,1)S(1)}, u32[]{:S(2)}, u32[]{:S(2)}) collective-permute-start(bf16[16,2304]{1,0:T(8,128)(2,1)} %param.9), channel_id=1, source_target_pairs={{0,2},{1,3},{2,0},{3,1},{4,6},{5,7},{6,4},{7,5},{8,10},{9,11},{10,... | collective-permute-start | bytes 221192 | tf_op jit(solution)/shard_map/ppermute | solution.py:111
  7.9 6.4 %collective-permute-start.5 = (bf16[16,2304]{1,0:T(8,128)(2,1)}, bf16[16,2304]{1,0:T(8,128)(2,1)S(1)}, u32[]{:S(2)}, u32[]{:S(2)}) collective-permute-start(bf16[16,2304]{1,0:T(8,128)(2,1)} %param.9), channel_id=1, source_target_pairs={{0,12},{1,13},{2,14},{3,15},{4,8},{5,9},{6,10},{7,11},{8,4},{9,5},... | collective-permute-start | bytes 221192 | tf_op jit(solution)/shard_map/ppermute | solution.py:111
  8.1 1.3 %collective-permute-start.8 = (f32[128]{0:T(128)}, f32[128]{0:T(128)S(1)}, u32[]{:S(2)}, u32[]{:S(2)}) collective-permute-start(f32[128]{0:T(128)} %param.11), channel_id=1, source_target_pairs={{0,1},{1,0},{2,3},{3,2},{4,5},{5,4},{6,7},{7,6},{8,9},{9,8},{10,11... | collective-permute-start | bytes 1544 | tf_op jit(solution)/shard_map/ppermute | solution.py:118
  9.4 9.9 %collective-permute-start.9 = (bf16[128,2304]{1,0:T(8,128)(2,1)S(1)}, bf16[128,2304]{1,0:T(8,128)(2,1)S(1)}, u32[]{:S(2)}, u32[]{:S(2)}) collective-permute-start(bf16[128,2304]{1,0:T(8,128)(2,1)S(1)} %copy-done), channel_id=1, source_target_pairs={{0,1},{1,0},{2,3},{3,2},{4,5},{5,4},{6,7},{7,6},{8,9},{9,8},{10,11... | collective-permute-start | bytes 1769480 | tf_op jit(solution)/shard_map/ppermute | solution.py:118
  9.9 8.9 %collective-permute-start.7 = (bf16[128,2304]{1,0:T(8,128)(2,1)S(1)}, bf16[128,2304]{1,0:T(8,128)(2,1)S(1)}, u32[]{:S(2)}, u32[]{:S(2)}) collective-permute-start(bf16[128,2304]{1,0:T(8,128)(2,1)S(1)} %copy-done.5), channel_id=1, source_target_pairs={{0,1},{1,0},{2,3},{3,2},{4,5},{5,4},{6,7},{7,6},{8,9},{9,8},{10,11... | collective-permute-start | bytes 1769480 | tf_op jit(solution)/shard_map/ppermute | solution.py:118
  10.0 6.7 %collective-permute-start.4 = (bf16[16,2304]{1,0:T(8,128)(2,1)S(1)}, bf16[16,2304]{1,0:T(8,128)(2,1)S(1)}, u32[]{:S(2)}, u32[]{:S(2)}) collective-permute-start(bf16[16,2304]{1,0:T(8,128)(2,1)S(1)} %collective-permute-done.3), channel_id=1, source_target_pairs={{0,2},{1,3},{2,0},{3,1},{4,6},{5,7},{6,4},{7,5},{8,10},{9,11},{10,... | collective-permute-start | bytes 221192 | tf_op jit(solution)/shard_map/ppermute | solution.py:111
  11.0 5.7 %collective-permute-start.2 = (bf16[16,2304]{1,0:T(8,128)(2,1)S(1)}, bf16[16,2304]{1,0:T(8,128)(2,1)S(1)}, u32[]{:S(2)}, u32[]{:S(2)}) collective-permute-start(bf16[16,2304]{1,0:T(8,128)(2,1)S(1)} %collective-permute-done.1), channel_id=1, source_target_pairs={{0,2},{1,3},{2,0},{3,1},{4,6},{5,7},{6,4},{7,5},{8,10},{9,11},{10,... | collective-permute-start | bytes 221192 | tf_op jit(solution)/shard_map/ppermute | solution.py:111
  14.2 4.4 %collective-permute-start.6 = (bf16[16,2304]{1,0:T(8,128)(2,1)S(1)}, bf16[16,2304]{1,0:T(8,128)(2,1)S(1)}, u32[]{:S(2)}, u32[]{:S(2)}) collective-permute-start(bf16[16,2304]{1,0:T(8,128)(2,1)S(1)} %collective-permute-done.5), channel_id=1, source_target_pairs={{0,2},{1,3},{2,0},{3,1},{4,6},{5,7},{6,4},{7,5},{8,10},{9,11},{10,... | collective-permute-start | bytes 221192 | tf_op jit(solution)/shard_map/ppermute | solution.py:111
  18.7 2.8 %collective-permute-start.11 = (bf16[128,2304]{1,0:T(8,128)(2,1)S(1)}, bf16[128,2304]{1,0:T(8,128)(2,1)S(1)}, u32[]{:S(2)}, u32[]{:S(2)}) collective-permute-start(bf16[128,2304]{1,0:T(8,128)(2,1)S(1)} %subtract_convert_fusion), channel_id=1, source_target_pairs={{0,1},{1,0},{2,3},{3,2},{4,5},{5,4},{6,7},{7,6},{8,9},{9,8},{10,11... | collective-permute-start | bytes 1769480 | tf_op jit(solution)/shard_map/ppermute | solution.py:118
  20.1 1.4 %collective-permute-start.10 = (bf16[128,128]{0,1:T(8,128)(2,1)S(1)}, bf16[128,128]{0,1:T(8,128)(2,1)S(1)}, u32[]{:S(2)}, u32[]{:S(2)}) collective-permute-start(bf16[128,128]{0,1:T(8,128)(2,1)S(1)} %get-tuple-element.34), channel_id=1, source_target_pairs={{0,1},{1,0},{2,3},{3,2},{4,5},{5,4},{6,7},{7,6},{8,9},{9,8},{10,11... | collective-permute-start | bytes 98312 | tf_op jit(solution)/shard_map/ppermute | solution.py:118
  20.7 6.8 %collective-permute-start.14 = (bf16[32,2304]{1,0:T(8,128)(2,1)S(1)}, bf16[32,2304]{1,0:T(8,128)(2,1)S(1)}, u32[]{:S(2)}, u32[]{:S(2)}) collective-permute-start(bf16[32,2304]{1,0:T(8,128)(2,1)S(1)} %pad_maximum_fusion.4), channel_id=1, source_target_pairs={{0,2},{1,3},{2,0},{3,1},{4,6},{5,7},{6,4},{7,5},{8,10},{9,11},{10,... | collective-permute-start | bytes 442376 | tf_op jit(solution)/shard_map/ppermute | solution.py:111
  21.5 8.9 %collective-permute-start.12 = (bf16[32,2304]{1,0:T(8,128)(2,1)S(1)}, bf16[32,2304]{1,0:T(8,128)(2,1)S(1)}, u32[]{:S(2)}, u32[]{:S(2)}) collective-permute-start(bf16[32,2304]{1,0:T(8,128)(2,1)S(1)} %pad_maximum_fusion.3), channel_id=1, source_target_pairs={{0,2},{1,3},{2,0},{3,1},{4,6},{5,7},{6,4},{7,5},{8,10},{9,11},{10,... | collective-permute-start | bytes 442376 | tf_op jit(solution)/shard_map/ppermute | solution.py:111
  27.5 7.4 %collective-permute-start.15 = (bf16[16,2304]{1,0:T(8,128)(2,1)S(1)}, bf16[16,2304]{1,0:T(8,128)(2,1)S(1)}, u32[]{:S(2)}, u32[]{:S(2)}) collective-permute-start(bf16[16,2304]{1,0:T(8,128)(2,1)S(1)} %get-tuple-element.27), channel_id=1, source_target_pairs={{0,8},{1,9},{2,10},{3,11},{4,12},{5,13},{6,14},{7,15},{8,0},{9,1},... | collective-permute-start | bytes 221192 | tf_op jit(solution)/shard_map/ppermute | solution.py:111
  28.5 6.5 %collective-permute-start.16 = (bf16[16,2304]{1,0:T(8,128)(2,1)S(1)}, bf16[16,2304]{1,0:T(8,128)(2,1)S(1)}, u32[]{:S(2)}, u32[]{:S(2)}) collective-permute-start(bf16[16,2304]{1,0:T(8,128)(2,1)S(1)} %get-tuple-element.28), channel_id=1, source_target_pairs={{0,12},{1,13},{2,14},{3,15},{4,8},{5,9},{6,10},{7,11},{8,4},{9,5},... | collective-permute-start | bytes 221192 | tf_op jit(solution)/shard_map/ppermute | solution.py:111
  30.5 5.2 %collective-permute-start.13 = (bf16[16,2304]{1,0:T(8,128)(2,1)S(1)}, bf16[16,2304]{1,0:T(8,128)(2,1)S(1)}, u32[]{:S(2)}, u32[]{:S(2)}) collective-permute-start(bf16[16,2304]{1,0:T(8,128)(2,1)S(1)} %fusion.15), channel_id=1, source_target_pairs={{0,4},{1,5},{2,6},{3,7},{4,0},{5,1},{6,2},{7,3},{8,12},{9,13},{10,... | collective-permute-start | bytes 221192 | tf_op jit(solution)/shard_map/ppermute | solution.py:111
  35.7 13.5 %copy-start.6 = (bf16[16,2304]{1,0:T(8,128)(2,1)}, bf16[16,2304]{1,0:T(8,128)(2,1)S(1)}, u32[]{:S(2)}) copy-start(bf16[16,2304]{1,0:T(8,128)(2,1)S(1)} %fusion.20) | copy-start | bytes 221188
  35.7 6.2 %collective-permute-start.22 = (bf16[16,2304]{1,0:T(8,128)(2,1)S(1)}, bf16[16,2304]{1,0:T(8,128)(2,1)S(1)}, u32[]{:S(2)}, u32[]{:S(2)}) collective-permute-start(bf16[16,2304]{1,0:T(8,128)(2,1)S(1)} %fusion.20), channel_id=1, source_target_pairs={{0,12},{1,13},{2,14},{3,15},{4,8},{5,9},{6,10},{7,11},{8,4},{9,5},... | collective-permute-start | bytes 221192 | tf_op jit(solution)/shard_map/ppermute | solution.py:111
  37.8 5.7 %collective-permute-start.20 = (bf16[16,2304]{1,0:T(8,128)(2,1)S(1)}, bf16[16,2304]{1,0:T(8,128)(2,1)S(1)}, u32[]{:S(2)}, u32[]{:S(2)}) collective-permute-start(bf16[16,2304]{1,0:T(8,128)(2,1)S(1)} %fusion.20), channel_id=1, source_target_pairs={{0,8},{1,9},{2,10},{3,11},{4,12},{5,13},{6,14},{7,15},{8,0},{9,1},... | collective-permute-start | bytes 221192 | tf_op jit(solution)/shard_map/ppermute | solution.py:111
  37.8 7.0 %collective-permute-start.18 = (bf16[16,2304]{1,0:T(8,128)(2,1)S(1)}, bf16[16,2304]{1,0:T(8,128)(2,1)S(1)}, u32[]{:S(2)}, u32[]{:S(2)}) collective-permute-start(bf16[16,2304]{1,0:T(8,128)(2,1)S(1)} %fusion.20), channel_id=1, source_target_pairs={{0,4},{1,5},{2,6},{3,7},{4,0},{5,1},{6,2},{7,3},{8,12},{9,13},{10,... | collective-permute-start | bytes 221192 | tf_op jit(solution)/shard_map/ppermute | solution.py:111
  40.2 5.4 %collective-permute-start.17 = (bf16[16,2304]{1,0:T(8,128)(2,1)S(1)}, bf16[16,2304]{1,0:T(8,128)(2,1)S(1)}, u32[]{:S(2)}, u32[]{:S(2)}) collective-permute-start(bf16[16,2304]{1,0:T(8,128)(2,1)S(1)} %fusion.20), channel_id=1, source_target_pairs={{0,2},{1,3},{2,0},{3,1},{4,6},{5,7},{6,4},{7,5},{8,10},{9,11},{10,... | collective-permute-start | bytes 221192 | tf_op jit(solution)/shard_map/ppermute | solution.py:111
  41.2 9.8 %copy-start.4 = (f32[128,2304]{1,0:T(8,128)S(1)}, f32[128,2304]{1,0:T(8,128)}, u32[]{:S(2)}) copy-start(f32[128,2304]{1,0:T(8,128)} %refs_8_.1) | copy-start | bytes 3538948
  41.2 9.7 %copy-start.2 = (f32[128,2304]{1,0:T(8,128)S(1)}, f32[128,2304]{1,0:T(8,128)}, u32[]{:S(2)}) copy-start(f32[128,2304]{1,0:T(8,128)} %refs_6_.1) | copy-start | bytes 3538948
  41.2 9.7 %copy-start.3 = (f32[128,2304]{1,0:T(8,128)S(1)}, f32[128,2304]{1,0:T(8,128)}, u32[]{:S(2)}) copy-start(f32[128,2304]{1,0:T(8,128)} %refs_7_.1) | copy-start | bytes 3538948
  41.3 9.6 %copy-start.1 = (f32[128,2304]{1,0:T(8,128)S(1)}, f32[128,2304]{1,0:T(8,128)}, u32[]{:S(2)}) copy-start(f32[128,2304]{1,0:T(8,128)} %refs_5_.1) | copy-start | bytes 3538948
  42.0 4.8 %collective-permute-start.23 = (bf16[16,2304]{1,0:T(8,128)(2,1)S(1)}, bf16[16,2304]{1,0:T(8,128)(2,1)S(1)}, u32[]{:S(2)}, u32[]{:S(2)}) collective-permute-start(bf16[16,2304]{1,0:T(8,128)(2,1)S(1)} %collective-permute-done.22), channel_id=1, source_target_pairs={{0,2},{1,3},{2,0},{3,1},{4,6},{5,7},{6,4},{7,5},{8,10},{9,11},{10,... | collective-permute-start | bytes 221192 | tf_op jit(solution)/shard_map/ppermute | solution.py:111
  43.5 4.7 %collective-permute-start.21 = (bf16[16,2304]{1,0:T(8,128)(2,1)S(1)}, bf16[16,2304]{1,0:T(8,128)(2,1)S(1)}, u32[]{:S(2)}, u32[]{:S(2)}) collective-permute-start(bf16[16,2304]{1,0:T(8,128)(2,1)S(1)} %collective-permute-done.20), channel_id=1, source_target_pairs={{0,2},{1,3},{2,0},{3,1},{4,6},{5,7},{6,4},{7,5},{8,10},{9,11},{10,... | collective-permute-start | bytes 221192 | tf_op jit(solution)/shard_map/ppermute | solution.py:111
  44.9 4.4 %collective-permute-start.19 = (bf16[16,2304]{1,0:T(8,128)(2,1)S(1)}, bf16[16,2304]{1,0:T(8,128)(2,1)S(1)}, u32[]{:S(2)}, u32[]{:S(2)}) collective-permute-start(bf16[16,2304]{1,0:T(8,128)(2,1)S(1)} %collective-permute-done.18), channel_id=1, source_target_pairs={{0,2},{1,3},{2,0},{3,1},{4,6},{5,7},{6,4},{7,5},{8,10},{9,11},{10,... | collective-permute-start | bytes 221192 | tf_op jit(solution)/shard_map/ppermute | solution.py:111
  48.3 1.6 %collective-permute-start.25 = (bf16[64,2304]{1,0:T(8,128)(2,1)S(1)}, bf16[64,2304]{1,0:T(8,128)(2,1)S(1)}, u32[]{:S(2)}, u32[]{:S(2)}) collective-permute-start(bf16[64,2304]{1,0:T(8,128)(2,1)S(1)} %pad_maximum_fusion.2), channel_id=1, source_target_pairs={{0,1},{1,0},{2,3},{3,2},{4,5},{5,4},{6,7},{7,6},{8,9},{9,8},{10,11... | collective-permute-start | bytes 884744 | tf_op jit(solution)/shard_map/ppermute | solution.py:118
  49.3 1.6 %collective-permute-start.24 = (bf16[64,2304]{1,0:T(8,128)(2,1)S(1)}, bf16[64,2304]{1,0:T(8,128)(2,1)S(1)}, u32[]{:S(2)}, u32[]{:S(2)}) collective-permute-start(bf16[64,2304]{1,0:T(8,128)(2,1)S(1)} %pad_maximum_fusion.1), channel_id=1, source_target_pairs={{0,1},{1,0},{2,3},{3,2},{4,5},{5,4},{6,7},{7,6},{8,9},{9,8},{10,11... | collective-permute-start | bytes 884744 | tf_op jit(solution)/shard_map/ppermute | solution.py:118
  (4 other events, 35.7 us)

commit v14 on v11

--- a/solution.py
+++ b/solution.py
@@ -19,7 +19,7 @@
     )
 
 
-def update_kernel(columns, rows_total, codes_across, centered, *refs):
+def update_kernel(columns, places, rows_total, codes_across, centered, *refs):
     blocks = len(refs) - 20
     errors, (encoder, decoder) = refs[:blocks], refs[blocks : blocks + 2]
     moments = refs[blocks + 2 : blocks + 6]
@@ -32,8 +32,12 @@
         at = pl.ds(t * columns, columns)
         return pltpu.make_async_copy(held[i].at[:, at], outs[i].at[:, at], sem.at[t, i])
 
-    start = 0
-    for one in errors:
+    own, *other = errors
+    rows = own.shape[0] // len(places)
+    for k, place in enumerate(places):
+        error_all[pl.ds(place * rows, rows), :] = own[pl.ds(k * rows, rows), :]
+    start = own.shape[0]
+    for one in other:
         error_all[pl.ds(start, one.shape[0]), :] = one[...]
         start += one.shape[0]
     first = (1.0 - beta_first) / rows_total
@@ -68,7 +72,7 @@
             write(t, i).wait()
 
 
-def update(total_rows, codes_across, centered, errors, weights, moments):
+def update(total_rows, codes_across, centered, errors, places, weights, moments):
     latents, width = weights[0].shape
     rows = centered.shape[0]
     columns = next(c for c in (256, 128, width) if width % c == 0)
@@ -78,7 +82,7 @@
     wide = pltpu.VMEM((latents, width), jnp.float32)
     narrow = pltpu.VMEM((latents, width), jnp.bfloat16)
     return pl.pallas_call(
-        functools.partial(update_kernel, columns, float(total_rows)),
+        functools.partial(update_kernel, columns, places, float(total_rows)),
         out_shape=(half, full, full, half, full, full),
         in_specs=[vmem] * (len(errors) + 8),
         out_specs=[pl.BlockSpec(memory_space=pl.ANY)] * 6,
@@ -150,7 +154,6 @@
         jnp.bfloat16
     )
     other_codes = to_other_core(codes[:, latents_here:])
-    other_centered = to_other_core(centered)
 
     quad = 4 * rows_here
     parts = []
@@ -158,18 +161,22 @@
         sums = jnp.dot(codes[rows], decoder_both, preferred_element_type=jnp.float32)
         parts += [sums[at : at + rows_here] for at in range(0, sums.shape[0], rows_here)]
 
-    def pair_sums(first, last, after=None):
-        given = jnp.concatenate(parts[first + 1 : last : 2], 0).astype(jnp.bfloat16)
-        came = to_chip(given, 1)
-        if after is not None:
-            came, _ = lax.optimization_barrier((came, after))
+    def given(first, last):
+        return jnp.concatenate(parts[first + 1 : last : 2], 0).astype(jnp.bfloat16)
+
+    def pair_sums(first, last, sent):
+        came = to_chip(sent, 1)
         return [
             parts[k] + came[at * rows_here : (at + 1) * rows_here].astype(jnp.float32)
             for at, k in enumerate(range(first, last, 2))
         ]
 
-    far = [one.astype(jnp.bfloat16) for one in pair_sums(4, chips)]
-    own, near = pair_sums(0, 4, far)
+    far_sent = given(4, chips)
+    far = [one.astype(jnp.bfloat16) for one in pair_sums(4, chips, far_sent)]
+    later_centered, _ = lax.optimization_barrier((centered, far_sent))
+    other_centered = to_other_core(later_centered)
+    near_sent, _ = lax.optimization_barrier((given(0, 4), (other_codes, other_centered)))
+    own, near = pair_sums(0, 4, near_sent)
     summed = own + to_chip(near.astype(jnp.bfloat16), 2).astype(jnp.float32)
     for k, one in enumerate(far, 2):
         summed = summed + to_chip(one, 2 * k).astype(jnp.float32)
@@ -179,7 +186,8 @@
         (row_error, other_codes, other_centered)
     )
     blocks = in_turn(*gather_chips(row_error, chips))
-    errors = [jnp.concatenate(blocks, 0)]
+    places = [0] + list(range(2, chips - 2)) + [1, chips - 2, chips - 1]
+    errors = [jnp.concatenate([blocks[k] for k in places], 0)]
     errors += [to_other_core(jnp.concatenate(one, 0)) for one in (blocks[:4], blocks[4:])]
     codes_across = jnp.concatenate([codes[:, :latents_here], other_codes], 0).T
     centered_all = jnp.concatenate([centered, other_centered], 0)
@@ -195,6 +203,7 @@
         codes_across,
         centered_all,
         errors,
+        places,
         (encoder, decoder),
         (encoder_moment, encoder_square, decoder_moment, decoder_square),
     )

time: 55.8 us -> 54.3 us (0.973)
  waiting for transfers between devices: 22.4 us -> 20.3 us
    ppermute x19, waiting for transfers between devices: 20.8 us -> 17.1 us  [to_chip(): lax.ppermute(block, 'latent', [(i, i ^ 2 * distance) for i in range(size)])]
    ppermute x7, waiting for transfers between devices: 1.62 us -> 3.2 us  [to_other_core(): return lax.ppermute(block, 'latent', [(i, i ^ 1) for i in range(size)])]
  transfers between devices with their start and end apart: 26 -> 26, of which waited for: 13 -> 17; matrix products, arithmetic and copies ran while one was open for 5% -> 4% of each run, Pallas kernels for 0% -> 0%
where the time goes in v14:
time: 54.3 us; the launch traced here: 54.1 us
  starting transfers between devices  26.4 us (49%)
  waiting for transfers between devices  20.3 us (37%)
  Pallas kernels  3.38 us (6%)
  local copies, waits for them, and re-layouts  1.33 us (2%)
  matrix products  1.27 us (2%)
  between operations  0.99 us (2%)
    ppermute x19, starting transfers between devices, to_chip(): lax.ppermute(block, 'latent', [(i, i ^ 2 * distance) for i in range(size)])  25.2 us
    ppermute x19, waiting for transfers between devices, to_chip(): lax.ppermute(block, 'latent', [(i, i ^ 2 * distance) for i in range(size)])  17.1 us
    pallas_call x1, Pallas kernels, update(): pl.pallas_call(functools.partial(update_kernel, columns, places, float(to...  3.38 us
    ppermute x7, waiting for transfers between devices, to_other_core(): return lax.ppermute(block, 'latent', [(i, i ^ 1) for i in range(size)])  3.2 us
    unnamed x35, local copies, waits for them, and re-layouts  1.25 us
    ppermute x7, starting transfers between devices, to_other_core(): return lax.ppermute(block, 'latent', [(i, i ^ 1) for i in range(size)])  1.23 us
  transfers between devices with their start and end apart: 26, of which 17 were waited for; matrix products, arithmetic and copies ran while one was open for 4% of the time, Pallas kernels for 0%

profile of v14, /device:TPU:0, one launch (start us, length us, event | category | flops | bytes accessed | tf_op | source)
XLA Modules:
  0.0 54.1 jit_solution(8925068059267663979)
XLA Ops:
  0.7 4.1 %collective-permute-start.3 = (bf16[16,2304]{1,0:T(8,128)(2,1)}, bf16[16,2304]{1,0:T(8,128)(2,1)S(1)}, u32[]{:S(2)}, u32[]{:S(2)}) collective-permute-start(bf16[16,2304]{1,0:T(8,128)(2,1)} %param.9), channel_id=1, source_target_pairs={{0,8},{1,9},{2,10},{3,11},{4,12},{5,13},{6,14},{7,15},{8,0},{9,1},... | collective-permute-start | bytes 221192 | tf_op jit(solution)/shard_map/ppermute | solution.py:111
  4.8 1.6 %collective-permute-start.1 = (bf16[16,2304]{1,0:T(8,128)(2,1)}, bf16[16,2304]{1,0:T(8,128)(2,1)S(1)}, u32[]{:S(2)}, u32[]{:S(2)}) collective-permute-start(bf16[16,2304]{1,0:T(8,128)(2,1)} %param.9), channel_id=1, source_target_pairs={{0,4},{1,5},{2,6},{3,7},{4,0},{5,1},{6,2},{7,3},{8,12},{9,13},{10,... | collective-permute-start | bytes 221192 | tf_op jit(solution)/shard_map/ppermute | solution.py:111
  6.4 1.5 %collective-permute-start = (bf16[16,2304]{1,0:T(8,128)(2,1)}, bf16[16,2304]{1,0:T(8,128)(2,1)S(1)}, u32[]{:S(2)}, u32[]{:S(2)}) collective-permute-start(bf16[16,2304]{1,0:T(8,128)(2,1)} %param.9), channel_id=1, source_target_pairs={{0,2},{1,3},{2,0},{3,1},{4,6},{5,7},{6,4},{7,5},{8,10},{9,11},{10,... | collective-permute-start | bytes 221192 | tf_op jit(solution)/shard_map/ppermute | solution.py:111
  8.1 1.1 %constant_dynamic-update-slice_fusion.9 = bf16[256,2304]{1,0:T(8,128)(2,1)S(1)} fusion(bf16[128,2304]{1,0:T(8,128)(2,1)} %refs_4_.1), kind=kLoop, calls=%fused_computation.39 | loop fusion | bytes 1179648
  10.0 1.0 %collective-permute-start.4 = (bf16[16,2304]{1,0:T(8,128)(2,1)S(1)}, bf16[16,2304]{1,0:T(8,128)(2,1)S(1)}, u32[]{:S(2)}, u32[]{:S(2)}) collective-permute-start(bf16[16,2304]{1,0:T(8,128)(2,1)S(1)} %collective-permute-done.3), channel_id=1, source_target_pairs={{0,2},{1,3},{2,0},{3,1},{4,6},{5,7},{6,4},{7,5},{8,10},{9,11},{10,... | collective-permute-start | bytes 221192 | tf_op jit(solution)/shard_map/ppermute | solution.py:111
  11.0 1.4 %collective-permute-start.2 = (bf16[16,2304]{1,0:T(8,128)(2,1)S(1)}, bf16[16,2304]{1,0:T(8,128)(2,1)S(1)}, u32[]{:S(2)}, u32[]{:S(2)}) collective-permute-start(bf16[16,2304]{1,0:T(8,128)(2,1)S(1)} %collective-permute-done.1), channel_id=1, source_target_pairs={{0,2},{1,3},{2,0},{3,1},{4,6},{5,7},{6,4},{7,5},{8,10},{9,11},{10,... | collective-permute-start | bytes 221192 | tf_op jit(solution)/shard_map/ppermute | solution.py:111
  12.4 1.8 %collective-permute-done.5 = bf16[16,2304]{1,0:T(8,128)(2,1)S(1)} collective-permute-done((bf16[16,2304]{1,0:T(8,128)(2,1)}, bf16[16,2304]{1,0:T(8,128)(2,1)S(1)}, u32[]{:S(2)}, u32[]{:S(2)}) %collective-permute-start.5) | collective-permute-done | bytes 73760 | tf_op jit(solution)/shard_map/ppermute | solution.py:111
  14.8 1.9 %collective-permute-done.2 = bf16[16,2304]{1,0:T(8,128)(2,1)S(1)} collective-permute-done((bf16[16,2304]{1,0:T(8,128)(2,1)S(1)}, bf16[16,2304]{1,0:T(8,128)(2,1)S(1)}, u32[]{:S(2)}, u32[]{:S(2)}) %collective-permute-start.2) | collective-permute-done | bytes 73760 | tf_op jit(solution)/shard_map/ppermute | solution.py:111
  16.7 1.9 %collective-permute-done.6 = bf16[16,2304]{1,0:T(8,128)(2,1)S(1)} collective-permute-done((bf16[16,2304]{1,0:T(8,128)(2,1)S(1)}, bf16[16,2304]{1,0:T(8,128)(2,1)S(1)}, u32[]{:S(2)}, u32[]{:S(2)}) %collective-permute-start.6) | collective-permute-done | bytes 73760 | tf_op jit(solution)/shard_map/ppermute | solution.py:111
  20.1 0.6 %collective-permute-start.14 = (bf16[32,2304]{1,0:T(8,128)(2,1)S(1)}, bf16[32,2304]{1,0:T(8,128)(2,1)S(1)}, u32[]{:S(2)}, u32[]{:S(2)}) collective-permute-start(bf16[32,2304]{1,0:T(8,128)(2,1)S(1)} %pad_maximum_fusion.4), channel_id=1, source_target_pairs={{0,2},{1,3},{2,0},{3,1},{4,6},{5,7},{6,4},{7,5},{8,10},{9,11},{10,... | collective-permute-start | bytes 442376 | tf_op jit(solution)/shard_map/ppermute | solution.py:111
  20.7 0.5 collective-permute-start.11
  21.2 0.7 %collective-permute-done.10 = bf16[128,128]{0,1:T(8,128)(2,1)S(1)} collective-permute-done((bf16[128,128]{0,1:T(8,128)(2,1)S(1)}, bf16[128,128]{0,1:T(8,128)(2,1)S(1)}, u32[]{:S(2)}, u32[]{:S(2)}) %collective-permute-start.10) | collective-permute-done | bytes 32800 | tf_op jit(solution)/shard_map/ppermute | solution.py:118
  21.9 0.9 %collective-permute-done.11 = bf16[128,2304]{1,0:T(8,128)(2,1)S(1)} collective-permute-done((bf16[128,2304]{1,0:T(8,128)(2,1)S(1)}, bf16[128,2304]{1,0:T(8,128)(2,1)S(1)}, u32[]{:S(2)}, u32[]{:S(2)}) %collective-permute-start.11) | collective-permute-done | bytes 589856 | tf_op jit(solution)/shard_map/ppermute | solution.py:118
  22.8 1.5 %collective-permute-start.12 = (bf16[32,2304]{1,0:T(8,128)(2,1)S(1)}, bf16[32,2304]{1,0:T(8,128)(2,1)S(1)}, u32[]{:S(2)}, u32[]{:S(2)}) collective-permute-start(bf16[32,2304]{1,0:T(8,128)(2,1)S(1)} %pad_maximum_fusion.3), channel_id=1, source_target_pairs={{0,2},{1,3},{2,0},{3,1},{4,6},{5,7},{6,4},{7,5},{8,10},{9,11},{10,... | collective-permute-start | bytes 442376 | tf_op jit(solution)/shard_map/ppermute | solution.py:111
  24.4 1.0 %collective-permute-done.14 = bf16[32,2304]{1,0:T(8,128)(2,1)S(1)} collective-permute-done((bf16[32,2304]{1,0:T(8,128)(2,1)S(1)}, bf16[32,2304]{1,0:T(8,128)(2,1)S(1)}, u32[]{:S(2)}, u32[]{:S(2)}) %collective-permute-start.14) | collective-permute-done | bytes 147488 | tf_op jit(solution)/shard_map/ppermute | solution.py:111
  25.4 1.2 %collective-permute-start.15 = (bf16[16,2304]{1,0:T(8,128)(2,1)S(1)}, bf16[16,2304]{1,0:T(8,128)(2,1)S(1)}, u32[]{:S(2)}, u32[]{:S(2)}) collective-permute-start(bf16[16,2304]{1,0:T(8,128)(2,1)S(1)} %get-tuple-element.29), channel_id=1, source_target_pairs={{0,8},{1,9},{2,10},{3,11},{4,12},{5,13},{6,14},{7,15},{8,0},{9,1},... | collective-permute-start | bytes 221192 | tf_op jit(solution)/shard_map/ppermute | solution.py:111
  26.6 2.0 %collective-permute-start.16 = (bf16[16,2304]{1,0:T(8,128)(2,1)S(1)}, bf16[16,2304]{1,0:T(8,128)(2,1)S(1)}, u32[]{:S(2)}, u32[]{:S(2)}) collective-permute-start(bf16[16,2304]{1,0:T(8,128)(2,1)S(1)} %get-tuple-element.30), channel_id=1, source_target_pairs={{0,12},{1,13},{2,14},{3,15},{4,8},{5,9},{6,10},{7,11},{8,4},{9,5},... | collective-permute-start | bytes 221192 | tf_op jit(solution)/shard_map/ppermute | solution.py:111
  29.0 0.8 %collective-permute-start.13 = (bf16[16,2304]{1,0:T(8,128)(2,1)S(1)}, bf16[16,2304]{1,0:T(8,128)(2,1)S(1)}, u32[]{:S(2)}, u32[]{:S(2)}) collective-permute-start(bf16[16,2304]{1,0:T(8,128)(2,1)S(1)} %fusion.15), channel_id=1, source_target_pairs={{0,4},{1,5},{2,6},{3,7},{4,0},{5,1},{6,2},{7,3},{8,12},{9,13},{10,... | collective-permute-start | bytes 221192 | tf_op jit(solution)/shard_map/ppermute | solution.py:111
  29.8 3.8 %collective-permute-done.15 = bf16[16,2304]{1,0:T(8,128)(2,1)S(1)} collective-permute-done((bf16[16,2304]{1,0:T(8,128)(2,1)S(1)}, bf16[16,2304]{1,0:T(8,128)(2,1)S(1)}, u32[]{:S(2)}, u32[]{:S(2)}) %collective-permute-start.15) | collective-permute-done | bytes 73760 | tf_op jit(solution)/shard_map/ppermute | solution.py:111
  33.6 0.8 %collective-permute-done.13 = bf16[16,2304]{1,0:T(8,128)(2,1)S(1)} collective-permute-done((bf16[16,2304]{1,0:T(8,128)(2,1)S(1)}, bf16[16,2304]{1,0:T(8,128)(2,1)S(1)}, u32[]{:S(2)}, u32[]{:S(2)}) %collective-permute-start.13) | collective-permute-done | bytes 73760 | tf_op jit(solution)/shard_map/ppermute | solution.py:111
  34.4 2.9 %collective-permute-start.22 = (bf16[16,2304]{1,0:T(8,128)(2,1)S(1)}, bf16[16,2304]{1,0:T(8,128)(2,1)S(1)}, u32[]{:S(2)}, u32[]{:S(2)}) collective-permute-start(bf16[16,2304]{1,0:T(8,128)(2,1)S(1)} %fusion.20), channel_id=1, source_target_pairs={{0,12},{1,13},{2,14},{3,15},{4,8},{5,9},{6,10},{7,11},{8,4},{9,5},... | collective-permute-start | bytes 221192 | tf_op jit(solution)/shard_map/ppermute | solution.py:111
  37.3 1.0 %collective-permute-start.21 = (bf16[16,2304]{1,0:T(8,128)(2,1)S(1)}, bf16[16,2304]{1,0:T(8,128)(2,1)S(1)}, u32[]{:S(2)}, u32[]{:S(2)}) collective-permute-start(bf16[16,2304]{1,0:T(8,128)(2,1)S(1)} %fusion.20), channel_id=1, source_target_pairs={{0,2},{1,3},{2,0},{3,1},{4,6},{5,7},{6,4},{7,5},{8,10},{9,11},{10,... | collective-permute-start | bytes 221192 | tf_op jit(solution)/shard_map/ppermute | solution.py:111
  38.3 1.7 %collective-permute-start.17 = (bf16[16,2304]{1,0:T(8,128)(2,1)S(1)}, bf16[16,2304]{1,0:T(8,128)(2,1)S(1)}, u32[]{:S(2)}, u32[]{:S(2)}) collective-permute-start(bf16[16,2304]{1,0:T(8,128)(2,1)S(1)} %fusion.20), channel_id=1, source_target_pairs={{0,4},{1,5},{2,6},{3,7},{4,0},{5,1},{6,2},{7,3},{8,12},{9,13},{10,... | collective-permute-start | bytes 221192 | tf_op jit(solution)/shard_map/ppermute | solution.py:111
  40.2 1.1 %collective-permute-done.22 = bf16[16,2304]{1,0:T(8,128)(2,1)S(1)} collective-permute-done((bf16[16,2304]{1,0:T(8,128)(2,1)S(1)}, bf16[16,2304]{1,0:T(8,128)(2,1)S(1)}, u32[]{:S(2)}, u32[]{:S(2)}) %collective-permute-start.22) | collective-permute-done | bytes 73760 | tf_op jit(solution)/shard_map/ppermute | solution.py:111
  41.3 1.0 %collective-permute-start.23 = (bf16[16,2304]{1,0:T(8,128)(2,1)S(1)}, bf16[16,2304]{1,0:T(8,128)(2,1)S(1)}, u32[]{:S(2)}, u32[]{:S(2)}) collective-permute-start(bf16[16,2304]{1,0:T(8,128)(2,1)S(1)} %collective-permute-done.22), channel_id=1, source_target_pairs={{0,2},{1,3},{2,0},{3,1},{4,6},{5,7},{6,4},{7,5},{8,10},{9,11},{10,... | collective-permute-start | bytes 221192 | tf_op jit(solution)/shard_map/ppermute | solution.py:111
  42.3 1.4 %collective-permute-done.19 = bf16[16,2304]{1,0:T(8,128)(2,1)S(1)} collective-permute-done((bf16[16,2304]{1,0:T(8,128)(2,1)S(1)}, bf16[16,2304]{1,0:T(8,128)(2,1)S(1)}, u32[]{:S(2)}, u32[]{:S(2)}) %collective-permute-start.19) | collective-permute-done | bytes 73760 | tf_op jit(solution)/shard_map/ppermute | solution.py:111
  43.7 1.0 %collective-permute-start.20 = (bf16[16,2304]{1,0:T(8,128)(2,1)S(1)}, bf16[16,2304]{1,0:T(8,128)(2,1)S(1)}, u32[]{:S(2)}, u32[]{:S(2)}) collective-permute-start(bf16[16,2304]{1,0:T(8,128)(2,1)S(1)} %collective-permute-done.19), channel_id=1, source_target_pairs={{0,2},{1,3},{2,0},{3,1},{4,6},{5,7},{6,4},{7,5},{8,10},{9,11},{10,... | collective-permute-start | bytes 221192 | tf_op jit(solution)/shard_map/ppermute | solution.py:111
  44.7 1.0 %collective-permute-start.18 = (bf16[16,2304]{1,0:T(8,128)(2,1)S(1)}, bf16[16,2304]{1,0:T(8,128)(2,1)S(1)}, u32[]{:S(2)}, u32[]{:S(2)}) collective-permute-start(bf16[16,2304]{1,0:T(8,128)(2,1)S(1)} %collective-permute-done.17), channel_id=1, source_target_pairs={{0,2},{1,3},{2,0},{3,1},{4,6},{5,7},{6,4},{7,5},{8,10},{9,11},{10,... | collective-permute-start | bytes 221192 | tf_op jit(solution)/shard_map/ppermute | solution.py:111
  46.1 1.9 %collective-permute-done.20 = bf16[16,2304]{1,0:T(8,128)(2,1)S(1)} collective-permute-done((bf16[16,2304]{1,0:T(8,128)(2,1)S(1)}, bf16[16,2304]{1,0:T(8,128)(2,1)S(1)}, u32[]{:S(2)}, u32[]{:S(2)}) %collective-permute-start.20) | collective-permute-done | bytes 73760 | tf_op jit(solution)/shard_map/ppermute | solution.py:111
  48.1 0.9 %collective-permute-done.18 = bf16[16,2304]{1,0:T(8,128)(2,1)S(1)} collective-permute-done((bf16[16,2304]{1,0:T(8,128)(2,1)S(1)}, bf16[16,2304]{1,0:T(8,128)(2,1)S(1)}, u32[]{:S(2)}, u32[]{:S(2)}) %collective-permute-start.18) | collective-permute-done | bytes 73760 | tf_op jit(solution)/shard_map/ppermute | solution.py:111
  49.7 1.0 %collective-permute-done.24.refs_1_ = bf16[64,2304]{1,0:T(8,128)(2,1)S(1)} collective-permute-done((bf16[64,2304]{1,0:T(8,128)(2,1)S(1)}, bf16[64,2304]{1,0:T(8,128)(2,1)S(1)}, u32[]{:S(2)}, u32[]{:S(2)}) %collective-permute-start.24) | collective-permute-done | bytes 294944 | tf_op jit(solution)/shard_map/ppermute | solution.py:118
  50.7 3.4 %update.1 = (bf16[128,2304]{1,0:T(8,128)(2,1)}, f32[128,2304]{1,0:T(8,128)}, f32[128,2304]{1,0:T(8,128)}, bf16[128,2304]{1,0:T(8,128)(2,1)}, f32[128,2304]{1,0:T(8,128)}, /*index=5*/f32[128,2304]{1,0:T(8,128)}) custom-call(bf16[128,256]{1,0:T(8,128)(2,1)S(1)} %maximum_bitcast_fusion.codes_across, bf16[256,2304]{1,0:T(8,128)(2,1)S(1)} %pad_maximum_fusion.centered, ...), custom_call_target="tpu_custom_call" | custom-call | flops 452984832 | bytes 12976128 | tf_op jit(solution)/shard_map/update/pallas_call | solution.py:84
  (76 shorter events, 4.7 us)
Async XLA Ops:
  0.7 17.9 %copy-start.8 = (f32[2304]{0:T(1024)S(1)}, f32[2304]{0:T(1024)}, u32[]{:S(2)}) copy-start(f32[2304]{0:T(1024)} %param.13) | copy-start | bytes 27652
  0.7 9.2 %collective-permute-start.3 = (bf16[16,2304]{1,0:T(8,128)(2,1)}, bf16[16,2304]{1,0:T(8,128)(2,1)S(1)}, u32[]{:S(2)}, u32[]{:S(2)}) collective-permute-start(bf16[16,2304]{1,0:T(8,128)(2,1)} %param.9), channel_id=1, source_target_pairs={{0,8},{1,9},{2,10},{3,11},{4,12},{5,13},{6,14},{7,15},{8,0},{9,1},... | collective-permute-start | bytes 221192 | tf_op jit(solution)/shard_map/ppermute | solution.py:111
  4.8 5.2 %collective-permute-start.1 = (bf16[16,2304]{1,0:T(8,128)(2,1)}, bf16[16,2304]{1,0:T(8,128)(2,1)S(1)}, u32[]{:S(2)}, u32[]{:S(2)}) collective-permute-start(bf16[16,2304]{1,0:T(8,128)(2,1)} %param.9), channel_id=1, source_target_pairs={{0,4},{1,5},{2,6},{3,7},{4,0},{5,1},{6,2},{7,3},{8,12},{9,13},{10,... | collective-permute-start | bytes 221192 | tf_op jit(solution)/shard_map/ppermute | solution.py:111
  6.4 4.7 %collective-permute-start = (bf16[16,2304]{1,0:T(8,128)(2,1)}, bf16[16,2304]{1,0:T(8,128)(2,1)S(1)}, u32[]{:S(2)}, u32[]{:S(2)}) collective-permute-start(bf16[16,2304]{1,0:T(8,128)(2,1)} %param.9), channel_id=1, source_target_pairs={{0,2},{1,3},{2,0},{3,1},{4,6},{5,7},{6,4},{7,5},{8,10},{9,11},{10,... | collective-permute-start | bytes 221192 | tf_op jit(solution)/shard_map/ppermute | solution.py:111
  7.9 6.4 %collective-permute-start.5 = (bf16[16,2304]{1,0:T(8,128)(2,1)}, bf16[16,2304]{1,0:T(8,128)(2,1)S(1)}, u32[]{:S(2)}, u32[]{:S(2)}) collective-permute-start(bf16[16,2304]{1,0:T(8,128)(2,1)} %param.9), channel_id=1, source_target_pairs={{0,12},{1,13},{2,14},{3,15},{4,8},{5,9},{6,10},{7,11},{8,4},{9,5},... | collective-permute-start | bytes 221192 | tf_op jit(solution)/shard_map/ppermute | solution.py:111
  8.1 1.3 %collective-permute-start.8 = (f32[128]{0:T(128)}, f32[128]{0:T(128)S(1)}, u32[]{:S(2)}, u32[]{:S(2)}) collective-permute-start(f32[128]{0:T(128)} %param.11), channel_id=1, source_target_pairs={{0,1},{1,0},{2,3},{3,2},{4,5},{5,4},{6,7},{7,6},{8,9},{9,8},{10,11... | collective-permute-start | bytes 1544 | tf_op jit(solution)/shard_map/ppermute | solution.py:118
  9.4 9.9 %collective-permute-start.9 = (bf16[128,2304]{1,0:T(8,128)(2,1)S(1)}, bf16[128,2304]{1,0:T(8,128)(2,1)S(1)}, u32[]{:S(2)}, u32[]{:S(2)}) collective-permute-start(bf16[128,2304]{1,0:T(8,128)(2,1)S(1)} %copy-done), channel_id=1, source_target_pairs={{0,1},{1,0},{2,3},{3,2},{4,5},{5,4},{6,7},{7,6},{8,9},{9,8},{10,11... | collective-permute-start | bytes 1769480 | tf_op jit(solution)/shard_map/ppermute | solution.py:118
  9.9 8.9 %collective-permute-start.7 = (bf16[128,2304]{1,0:T(8,128)(2,1)S(1)}, bf16[128,2304]{1,0:T(8,128)(2,1)S(1)}, u32[]{:S(2)}, u32[]{:S(2)}) collective-permute-start(bf16[128,2304]{1,0:T(8,128)(2,1)S(1)} %copy-done.5), channel_id=1, source_target_pairs={{0,1},{1,0},{2,3},{3,2},{4,5},{5,4},{6,7},{7,6},{8,9},{9,8},{10,11... | collective-permute-start | bytes 1769480 | tf_op jit(solution)/shard_map/ppermute | solution.py:118
  10.0 6.7 %collective-permute-start.4 = (bf16[16,2304]{1,0:T(8,128)(2,1)S(1)}, bf16[16,2304]{1,0:T(8,128)(2,1)S(1)}, u32[]{:S(2)}, u32[]{:S(2)}) collective-permute-start(bf16[16,2304]{1,0:T(8,128)(2,1)S(1)} %collective-permute-done.3), channel_id=1, source_target_pairs={{0,2},{1,3},{2,0},{3,1},{4,6},{5,7},{6,4},{7,5},{8,10},{9,11},{10,... | collective-permute-start | bytes 221192 | tf_op jit(solution)/shard_map/ppermute | solution.py:111
  11.0 5.7 %collective-permute-start.2 = (bf16[16,2304]{1,0:T(8,128)(2,1)S(1)}, bf16[16,2304]{1,0:T(8,128)(2,1)S(1)}, u32[]{:S(2)}, u32[]{:S(2)}) collective-permute-start(bf16[16,2304]{1,0:T(8,128)(2,1)S(1)} %collective-permute-done.1), channel_id=1, source_target_pairs={{0,2},{1,3},{2,0},{3,1},{4,6},{5,7},{6,4},{7,5},{8,10},{9,11},{10,... | collective-permute-start | bytes 221192 | tf_op jit(solution)/shard_map/ppermute | solution.py:111
  14.2 4.4 %collective-permute-start.6 = (bf16[16,2304]{1,0:T(8,128)(2,1)S(1)}, bf16[16,2304]{1,0:T(8,128)(2,1)S(1)}, u32[]{:S(2)}, u32[]{:S(2)}) collective-permute-start(bf16[16,2304]{1,0:T(8,128)(2,1)S(1)} %collective-permute-done.5), channel_id=1, source_target_pairs={{0,2},{1,3},{2,0},{3,1},{4,6},{5,7},{6,4},{7,5},{8,10},{9,11},{10,... | collective-permute-start | bytes 221192 | tf_op jit(solution)/shard_map/ppermute | solution.py:111
  20.1 5.2 %collective-permute-start.14 = (bf16[32,2304]{1,0:T(8,128)(2,1)S(1)}, bf16[32,2304]{1,0:T(8,128)(2,1)S(1)}, u32[]{:S(2)}, u32[]{:S(2)}) collective-permute-start(bf16[32,2304]{1,0:T(8,128)(2,1)S(1)} %pad_maximum_fusion.4), channel_id=1, source_target_pairs={{0,2},{1,3},{2,0},{3,1},{4,6},{5,7},{6,4},{7,5},{8,10},{9,11},{10,... | collective-permute-start | bytes 442376 | tf_op jit(solution)/shard_map/ppermute | solution.py:111
  20.7 1.2 %collective-permute-start.10 = (bf16[128,128]{0,1:T(8,128)(2,1)S(1)}, bf16[128,128]{0,1:T(8,128)(2,1)S(1)}, u32[]{:S(2)}, u32[]{:S(2)}) collective-permute-start(bf16[128,128]{0,1:T(8,128)(2,1)S(1)} %get-tuple-element.36), channel_id=1, source_target_pairs={{0,1},{1,0},{2,3},{3,2},{4,5},{5,4},{6,7},{7,6},{8,9},{9,8},{10,11... | collective-permute-start | bytes 98312 | tf_op jit(solution)/shard_map/ppermute | solution.py:118
  20.7 2.1 %collective-permute-start.11 = (bf16[128,2304]{1,0:T(8,128)(2,1)S(1)}, bf16[128,2304]{1,0:T(8,128)(2,1)S(1)}, u32[]{:S(2)}, u32[]{:S(2)}) collective-permute-start(bf16[128,2304]{1,0:T(8,128)(2,1)S(1)} %subtract_convert_fusion), channel_id=1, source_target_pairs={{0,1},{1,0},{2,3},{3,2},{4,5},{5,4},{6,7},{7,6},{8,9},{9,8},{10,11... | collective-permute-start | bytes 1769480 | tf_op jit(solution)/shard_map/ppermute | solution.py:118
  22.8 6.1 %collective-permute-start.12 = (bf16[32,2304]{1,0:T(8,128)(2,1)S(1)}, bf16[32,2304]{1,0:T(8,128)(2,1)S(1)}, u32[]{:S(2)}, u32[]{:S(2)}) collective-permute-start(bf16[32,2304]{1,0:T(8,128)(2,1)S(1)} %pad_maximum_fusion.3), channel_id=1, source_target_pairs={{0,2},{1,3},{2,0},{3,1},{4,6},{5,7},{6,4},{7,5},{8,10},{9,11},{10,... | collective-permute-start | bytes 442376 | tf_op jit(solution)/shard_map/ppermute | solution.py:111
  25.4 8.2 %collective-permute-start.15 = (bf16[16,2304]{1,0:T(8,128)(2,1)S(1)}, bf16[16,2304]{1,0:T(8,128)(2,1)S(1)}, u32[]{:S(2)}, u32[]{:S(2)}) collective-permute-start(bf16[16,2304]{1,0:T(8,128)(2,1)S(1)} %get-tuple-element.29), channel_id=1, source_target_pairs={{0,8},{1,9},{2,10},{3,11},{4,12},{5,13},{6,14},{7,15},{8,0},{9,1},... | collective-permute-start | bytes 221192 | tf_op jit(solution)/shard_map/ppermute | solution.py:111
  26.6 7.0 %collective-permute-start.16 = (bf16[16,2304]{1,0:T(8,128)(2,1)S(1)}, bf16[16,2304]{1,0:T(8,128)(2,1)S(1)}, u32[]{:S(2)}, u32[]{:S(2)}) collective-permute-start(bf16[16,2304]{1,0:T(8,128)(2,1)S(1)} %get-tuple-element.30), channel_id=1, source_target_pairs={{0,12},{1,13},{2,14},{3,15},{4,8},{5,9},{6,10},{7,11},{8,4},{9,5},... | collective-permute-start | bytes 221192 | tf_op jit(solution)/shard_map/ppermute | solution.py:111
  29.0 5.4 %collective-permute-start.13 = (bf16[16,2304]{1,0:T(8,128)(2,1)S(1)}, bf16[16,2304]{1,0:T(8,128)(2,1)S(1)}, u32[]{:S(2)}, u32[]{:S(2)}) collective-permute-start(bf16[16,2304]{1,0:T(8,128)(2,1)S(1)} %fusion.15), channel_id=1, source_target_pairs={{0,4},{1,5},{2,6},{3,7},{4,0},{5,1},{6,2},{7,3},{8,12},{9,13},{10,... | collective-permute-start | bytes 221192 | tf_op jit(solution)/shard_map/ppermute | solution.py:111
  34.4 14.6 %copy-start.6 = (bf16[16,2304]{1,0:T(8,128)(2,1)}, bf16[16,2304]{1,0:T(8,128)(2,1)S(1)}, u32[]{:S(2)}) copy-start(bf16[16,2304]{1,0:T(8,128)(2,1)S(1)} %fusion.20) | copy-start | bytes 221188
  34.4 6.9 %collective-permute-start.22 = (bf16[16,2304]{1,0:T(8,128)(2,1)S(1)}, bf16[16,2304]{1,0:T(8,128)(2,1)S(1)}, u32[]{:S(2)}, u32[]{:S(2)}) collective-permute-start(bf16[16,2304]{1,0:T(8,128)(2,1)S(1)} %fusion.20), channel_id=1, source_target_pairs={{0,12},{1,13},{2,14},{3,15},{4,8},{5,9},{6,10},{7,11},{8,4},{9,5},... | collective-permute-start | bytes 221192 | tf_op jit(solution)/shard_map/ppermute | solution.py:111
  37.3 10.8 %collective-permute-start.21 = (bf16[16,2304]{1,0:T(8,128)(2,1)S(1)}, bf16[16,2304]{1,0:T(8,128)(2,1)S(1)}, u32[]{:S(2)}, u32[]{:S(2)}) collective-permute-start(bf16[16,2304]{1,0:T(8,128)(2,1)S(1)} %fusion.20), channel_id=1, source_target_pairs={{0,2},{1,3},{2,0},{3,1},{4,6},{5,7},{6,4},{7,5},{8,10},{9,11},{10,... | collective-permute-start | bytes 221192 | tf_op jit(solution)/shard_map/ppermute | solution.py:111
  38.3 5.4 %collective-permute-start.19 = (bf16[16,2304]{1,0:T(8,128)(2,1)S(1)}, bf16[16,2304]{1,0:T(8,128)(2,1)S(1)}, u32[]{:S(2)}, u32[]{:S(2)}) collective-permute-start(bf16[16,2304]{1,0:T(8,128)(2,1)S(1)} %fusion.20), channel_id=1, source_target_pairs={{0,8},{1,9},{2,10},{3,11},{4,12},{5,13},{6,14},{7,15},{8,0},{9,1},... | collective-permute-start | bytes 221192 | tf_op jit(solution)/shard_map/ppermute | solution.py:111
  38.3 6.4 %collective-permute-start.17 = (bf16[16,2304]{1,0:T(8,128)(2,1)S(1)}, bf16[16,2304]{1,0:T(8,128)(2,1)S(1)}, u32[]{:S(2)}, u32[]{:S(2)}) collective-permute-start(bf16[16,2304]{1,0:T(8,128)(2,1)S(1)} %fusion.20), channel_id=1, source_target_pairs={{0,4},{1,5},{2,6},{3,7},{4,0},{5,1},{6,2},{7,3},{8,12},{9,13},{10,... | collective-permute-start | bytes 221192 | tf_op jit(solution)/shard_map/ppermute | solution.py:111
  40.0 10.7 %copy-start.4 = (f32[128,2304]{1,0:T(8,128)S(1)}, f32[128,2304]{1,0:T(8,128)}, u32[]{:S(2)}) copy-start(f32[128,2304]{1,0:T(8,128)} %refs_8_.1) | copy-start | bytes 3538948
  40.0 10.7 %copy-start.2 = (f32[128,2304]{1,0:T(8,128)S(1)}, f32[128,2304]{1,0:T(8,128)}, u32[]{:S(2)}) copy-start(f32[128,2304]{1,0:T(8,128)} %refs_6_.1) | copy-start | bytes 3538948
  40.0 10.7 %copy-start.3 = (f32[128,2304]{1,0:T(8,128)S(1)}, f32[128,2304]{1,0:T(8,128)}, u32[]{:S(2)}) copy-start(f32[128,2304]{1,0:T(8,128)} %refs_7_.1) | copy-start | bytes 3538948
  40.1 10.6 %copy-start.1 = (f32[128,2304]{1,0:T(8,128)S(1)}, f32[128,2304]{1,0:T(8,128)}, u32[]{:S(2)}) copy-start(f32[128,2304]{1,0:T(8,128)} %refs_5_.1) | copy-start | bytes 3538948
  41.3 4.8 %collective-permute-start.23 = (bf16[16,2304]{1,0:T(8,128)(2,1)S(1)}, bf16[16,2304]{1,0:T(8,128)(2,1)S(1)}, u32[]{:S(2)}, u32[]{:S(2)}) collective-permute-start(bf16[16,2304]{1,0:T(8,128)(2,1)S(1)} %collective-permute-done.22), channel_id=1, source_target_pairs={{0,2},{1,3},{2,0},{3,1},{4,6},{5,7},{6,4},{7,5},{8,10},{9,11},{10,... | collective-permute-start | bytes 221192 | tf_op jit(solution)/shard_map/ppermute | solution.py:111
  43.7 4.4 %collective-permute-start.20 = (bf16[16,2304]{1,0:T(8,128)(2,1)S(1)}, bf16[16,2304]{1,0:T(8,128)(2,1)S(1)}, u32[]{:S(2)}, u32[]{:S(2)}) collective-permute-start(bf16[16,2304]{1,0:T(8,128)(2,1)S(1)} %collective-permute-done.19), channel_id=1, source_target_pairs={{0,2},{1,3},{2,0},{3,1},{4,6},{5,7},{6,4},{7,5},{8,10},{9,11},{10,... | collective-permute-start | bytes 221192 | tf_op jit(solution)/shard_map/ppermute | solution.py:111
  44.7 4.4 %collective-permute-start.18 = (bf16[16,2304]{1,0:T(8,128)(2,1)S(1)}, bf16[16,2304]{1,0:T(8,128)(2,1)S(1)}, u32[]{:S(2)}, u32[]{:S(2)}) collective-permute-start(bf16[16,2304]{1,0:T(8,128)(2,1)S(1)} %collective-permute-done.17), channel_id=1, source_target_pairs={{0,2},{1,3},{2,0},{3,1},{4,6},{5,7},{6,4},{7,5},{8,10},{9,11},{10,... | collective-permute-start | bytes 221192 | tf_op jit(solution)/shard_map/ppermute | solution.py:111
  48.0 1.6 %collective-permute-start.25 = (bf16[64,2304]{1,0:T(8,128)(2,1)S(1)}, bf16[64,2304]{1,0:T(8,128)(2,1)S(1)}, u32[]{:S(2)}, u32[]{:S(2)}) collective-permute-start(bf16[64,2304]{1,0:T(8,128)(2,1)S(1)} %pad_maximum_fusion.2), channel_id=1, source_target_pairs={{0,1},{1,0},{2,3},{3,2},{4,5},{5,4},{6,7},{7,6},{8,9},{9,8},{10,11... | collective-permute-start | bytes 884744 | tf_op jit(solution)/shard_map/ppermute | solution.py:118
  49.0 1.6 %collective-permute-start.24 = (bf16[64,2304]{1,0:T(8,128)(2,1)S(1)}, bf16[64,2304]{1,0:T(8,128)(2,1)S(1)}, u32[]{:S(2)}, u32[]{:S(2)}) collective-permute-start(bf16[64,2304]{1,0:T(8,128)(2,1)S(1)} %pad_maximum_fusion.1), channel_id=1, source_target_pairs={{0,1},{1,0},{2,3},{3,2},{4,5},{5,4},{6,7},{7,6},{8,9},{9,8},{10,11... | collective-permute-start | bytes 884744 | tf_op jit(solution)/shard_map/ppermute | solution.py:118
  (4 other events, 35.7 us)

commit v15 on v14

--- a/solution.py
+++ b/solution.py
@@ -19,7 +19,7 @@
     )
 
 
-def update_kernel(columns, places, rows_total, codes_across, centered, *refs):
+def update_kernel(columns, rows_total, codes_across, centered, *refs):
     blocks = len(refs) - 20
     errors, (encoder, decoder) = refs[:blocks], refs[blocks : blocks + 2]
     moments = refs[blocks + 2 : blocks + 6]
@@ -32,12 +32,8 @@
         at = pl.ds(t * columns, columns)
         return pltpu.make_async_copy(held[i].at[:, at], outs[i].at[:, at], sem.at[t, i])
 
-    own, *other = errors
-    rows = own.shape[0] // len(places)
-    for k, place in enumerate(places):
-        error_all[pl.ds(place * rows, rows), :] = own[pl.ds(k * rows, rows), :]
-    start = own.shape[0]
-    for one in other:
+    start = 0
+    for one in errors:
         error_all[pl.ds(start, one.shape[0]), :] = one[...]
         start += one.shape[0]
     first = (1.0 - beta_first) / rows_total
@@ -72,7 +68,7 @@
             write(t, i).wait()
 
 
-def update(total_rows, codes_across, centered, errors, places, weights, moments):
+def update(total_rows, codes_across, centered, errors, weights, moments):
     latents, width = weights[0].shape
     rows = centered.shape[0]
     columns = next(c for c in (256, 128, width) if width % c == 0)
@@ -82,7 +78,7 @@
     wide = pltpu.VMEM((latents, width), jnp.float32)
     narrow = pltpu.VMEM((latents, width), jnp.bfloat16)
     return pl.pallas_call(
-        functools.partial(update_kernel, columns, places, float(total_rows)),
+        functools.partial(update_kernel, columns, float(total_rows)),
         out_shape=(half, full, full, half, full, full),
         in_specs=[vmem] * (len(errors) + 8),
         out_specs=[pl.BlockSpec(memory_space=pl.ANY)] * 6,
@@ -118,8 +114,11 @@
     return lax.ppermute(block, "latent", [(i, i ^ 1) for i in range(size)])
 
 
-def gather_chips(block, chips):
-    even = [block] + [to_chip(block, k) for k in range(2, chips, 2)]
+def gather_chips(block, chips, after=None):
+    later = block
+    if after is not None:
+        later, _ = lax.optimization_barrier((block, after))
+    even = [later] + [to_chip(later, k) for k in range(2, chips, 2)]
     return even, [to_chip(one, 1) for one in even]
 
 
@@ -144,10 +143,13 @@
     chips = size // 2
     total_rows = rows_here * size
 
-    rows_core = jnp.concatenate(in_turn(*gather_chips(activations, chips)), 0)
-    encoder_both = jnp.concatenate([encoder, to_other_core(encoder)], 0)
-    decoder_both = jnp.concatenate([decoder, to_other_core(decoder)], 0)
-    bias_both = jnp.concatenate([encoder_bias, to_other_core(encoder_bias)], 0)
+    others = [to_other_core(one) for one in (encoder_bias, encoder, decoder)]
+    even, odd = gather_chips(activations, chips, others)
+    rows_core = jnp.concatenate(in_turn(even, odd), 0)
+    mine, _ = lax.optimization_barrier(((encoder_bias, encoder, decoder), odd[0]))
+    bias_both, encoder_both, decoder_both = (
+        jnp.concatenate(both, 0) for both in zip(mine, others)
+    )
 
     centered = (rows_core.astype(jnp.float32) - decoder_bias).astype(jnp.bfloat16)
     codes = jnp.maximum(inner_last(centered, encoder_both) + bias_both, 0.0).astype(
@@ -186,8 +188,7 @@
         (row_error, other_codes, other_centered)
     )
     blocks = in_turn(*gather_chips(row_error, chips))
-    places = [0] + list(range(2, chips - 2)) + [1, chips - 2, chips - 1]
-    errors = [jnp.concatenate([blocks[k] for k in places], 0)]
+    errors = [jnp.concatenate(blocks, 0)]
     errors += [to_other_core(jnp.concatenate(one, 0)) for one in (blocks[:4], blocks[4:])]
     codes_across = jnp.concatenate([codes[:, :latents_here], other_codes], 0).T
     centered_all = jnp.concatenate([centered, other_centered], 0)
@@ -203,7 +204,6 @@
         codes_across,
         centered_all,
         errors,
-        places,
         (encoder, decoder),
         (encoder_moment, encoder_square, decoder_moment, decoder_square),
     )

time: 54.3 us -> 58.2 us (1.072)
  starting transfers between devices: 26.4 us -> 28.4 us
  waiting for transfers between devices: 20.3 us -> 21.3 us
  local copies, waits for them, and re-layouts: 1.33 us -> 2.24 us
    ppermute x7, waiting for transfers between devices: 3.2 us -> 5.27 us  [to_other_core(): return lax.ppermute(block, 'latent', [(i, i ^ 1) for i in range(size)])]
    ppermute x19, starting transfers between devices: 25.2 us -> 26.8 us  [to_chip(): lax.ppermute(block, 'latent', [(i, i ^ 2 * distance) for i in range(size)])]
    ppermute x19, waiting for transfers between devices: 17.1 us -> 16 us  [to_chip(): lax.ppermute(block, 'latent', [(i, i ^ 2 * distance) for i in range(size)])]
    unnamed x35 -> x33, local copies, waits for them, and re-layouts: 1.25 us -> 2.16 us
  transfers between devices with their start and end apart: 26 -> 26, of which waited for: 17 -> 16; matrix products, arithmetic and copies ran while one was open for 4% -> 4% of each run, Pallas kernels for 0% -> 0%
where the time goes in v15:
time: 58.2 us; the launch traced here: 58 us
  starting transfers between devices  28.4 us (49%)
  waiting for transfers between devices  21.3 us (37%)
  Pallas kernels  3.38 us (6%)
  local copies, waits for them, and re-layouts  2.24 us (4%)
  matrix products  1.26 us (2%)
  between operations  0.97 us (2%)
    ppermute x19, starting transfers between devices, to_chip(): lax.ppermute(block, 'latent', [(i, i ^ 2 * distance) for i in range(size)])  26.8 us
    ppermute x19, waiting for transfers between devices, to_chip(): lax.ppermute(block, 'latent', [(i, i ^ 2 * distance) for i in range(size)])  16 us
    ppermute x7, waiting for transfers between devices, to_other_core(): return lax.ppermute(block, 'latent', [(i, i ^ 1) for i in range(size)])  5.27 us
    pallas_call x1, Pallas kernels, update(): pl.pallas_call(functools.partial(update_kernel, columns, float(total_rows...  3.38 us
    unnamed x33, local copies, waits for them, and re-layouts  2.16 us
    ppermute x7, starting transfers between devices, to_other_core(): return lax.ppermute(block, 'latent', [(i, i ^ 1) for i in range(size)])  1.68 us
  transfers between devices with their start and end apart: 26, of which 16 were waited for; matrix products, arithmetic and copies ran while one was open for 4% of the time, Pallas kernels for 0%

profile of v15, /device:TPU:0, one launch (start us, length us, event | category | flops | bytes accessed | tf_op | source)
XLA Modules:
  0.0 58.0 jit_solution(14688918867029705297)
XLA Ops:
  1.7 2.2 %collective-permute-done = f32[128]{0:T(128)S(1)} collective-permute-done((f32[128]{0:T(128)}, f32[128]{0:T(128)S(1)}, u32[]{:S(2)}, u32[]{:S(2)}) %collective-permute-start) | collective-permute-done | bytes 544 | tf_op jit(solution)/shard_map/ppermute | solution.py:114
  3.8 5.0 %collective-permute-start.8 = (bf16[16,2304]{1,0:T(8,128)(2,1)}, bf16[16,2304]{1,0:T(8,128)(2,1)S(1)}, u32[]{:S(2)}, u32[]{:S(2)}) collective-permute-start(bf16[16,2304]{1,0:T(8,128)(2,1)} %param.9), channel_id=1, source_target_pairs={{0,12},{1,13},{2,14},{3,15},{4,8},{5,9},{6,10},{7,11},{8,4},{9,5},... | collective-permute-start | bytes 221192 | tf_op jit(solution)/shard_map/ppermute | solution.py:107
  9.4 1.7 %collective-permute-start.3 = (bf16[16,2304]{1,0:T(8,128)(2,1)}, bf16[16,2304]{1,0:T(8,128)(2,1)S(1)}, u32[]{:S(2)}, u32[]{:S(2)}) collective-permute-start(bf16[16,2304]{1,0:T(8,128)(2,1)} %param.9), channel_id=1, source_target_pairs={{0,2},{1,3},{2,0},{3,1},{4,6},{5,7},{6,4},{7,5},{8,10},{9,11},{10,... | collective-permute-start | bytes 221192 | tf_op jit(solution)/shard_map/ppermute | solution.py:107
  11.1 0.9 %constant_dynamic-update-slice_fusion.7 = bf16[128,2304]{1,0:T(8,128)(2,1)S(1)} fusion(bf16[16,2304]{1,0:T(8,128)(2,1)} %param.9), kind=kLoop, calls=%fused_computation.37 | loop fusion | bytes 147456
  12.0 2.0 %collective-permute-done.3 = bf16[16,2304]{1,0:T(8,128)(2,1)S(1)} collective-permute-done((bf16[16,2304]{1,0:T(8,128)(2,1)}, bf16[16,2304]{1,0:T(8,128)(2,1)S(1)}, u32[]{:S(2)}, u32[]{:S(2)}) %collective-permute-start.3) | collective-permute-done | bytes 73760 | tf_op jit(solution)/shard_map/ppermute | solution.py:107
  14.0 1.1 %constant_dynamic-update-slice_fusion.9 = bf16[256,2304]{1,0:T(8,128)(2,1)S(1)} fusion(bf16[128,2304]{1,0:T(8,128)(2,1)} %refs_4_.1), kind=kLoop, calls=%fused_computation.39 | loop fusion | bytes 1179648
  15.1 1.7 %collective-permute-start.9 = (bf16[16,2304]{1,0:T(8,128)(2,1)S(1)}, bf16[16,2304]{1,0:T(8,128)(2,1)S(1)}, u32[]{:S(2)}, u32[]{:S(2)}) collective-permute-start(bf16[16,2304]{1,0:T(8,128)(2,1)S(1)} %collective-permute-done.8), channel_id=1, source_target_pairs={{0,2},{1,3},{2,0},{3,1},{4,6},{5,7},{6,4},{7,5},{8,10},{9,11},{10,... | collective-permute-start | bytes 221192 | tf_op jit(solution)/shard_map/ppermute | solution.py:107
  17.2 1.7 %collective-permute-start.5 = (bf16[16,2304]{1,0:T(8,128)(2,1)S(1)}, bf16[16,2304]{1,0:T(8,128)(2,1)S(1)}, u32[]{:S(2)}, u32[]{:S(2)}) collective-permute-start(bf16[16,2304]{1,0:T(8,128)(2,1)S(1)} %collective-permute-done.4), channel_id=1, source_target_pairs={{0,2},{1,3},{2,0},{3,1},{4,6},{5,7},{6,4},{7,5},{8,10},{9,11},{10,... | collective-permute-start | bytes 221192 | tf_op jit(solution)/shard_map/ppermute | solution.py:107
  19.0 3.0 %collective-permute-done.5 = bf16[16,2304]{1,0:T(8,128)(2,1)S(1)} collective-permute-done((bf16[16,2304]{1,0:T(8,128)(2,1)S(1)}, bf16[16,2304]{1,0:T(8,128)(2,1)S(1)}, u32[]{:S(2)}, u32[]{:S(2)}) %collective-permute-start.5) | collective-permute-done | bytes 73760 | tf_op jit(solution)/shard_map/ppermute | solution.py:107
  23.6 1.3 %collective-permute-start.14 = (bf16[32,2304]{1,0:T(8,128)(2,1)S(1)}, bf16[32,2304]{1,0:T(8,128)(2,1)S(1)}, u32[]{:S(2)}, u32[]{:S(2)}) collective-permute-start(bf16[32,2304]{1,0:T(8,128)(2,1)S(1)} %pad_maximum_fusion.4), channel_id=1, source_target_pairs={{0,2},{1,3},{2,0},{3,1},{4,6},{5,7},{6,4},{7,5},{8,10},{9,11},{10,... | collective-permute-start | bytes 442376 | tf_op jit(solution)/shard_map/ppermute | solution.py:107
  25.4 0.7 %collective-permute-done.10 = bf16[128,128]{0,1:T(8,128)(2,1)S(1)} collective-permute-done((bf16[128,128]{0,1:T(8,128)(2,1)S(1)}, bf16[128,128]{0,1:T(8,128)(2,1)S(1)}, u32[]{:S(2)}, u32[]{:S(2)}) %collective-permute-start.10) | collective-permute-done | bytes 32800 | tf_op jit(solution)/shard_map/ppermute | solution.py:114
  26.1 0.9 %collective-permute-done.11 = bf16[128,2304]{1,0:T(8,128)(2,1)S(1)} collective-permute-done((bf16[128,2304]{1,0:T(8,128)(2,1)S(1)}, bf16[128,2304]{1,0:T(8,128)(2,1)S(1)}, u32[]{:S(2)}, u32[]{:S(2)}) %collective-permute-start.11) | collective-permute-done | bytes 589856 | tf_op jit(solution)/shard_map/ppermute | solution.py:114
  27.0 0.8 %collective-permute-start.12 = (bf16[32,2304]{1,0:T(8,128)(2,1)S(1)}, bf16[32,2304]{1,0:T(8,128)(2,1)S(1)}, u32[]{:S(2)}, u32[]{:S(2)}) collective-permute-start(bf16[32,2304]{1,0:T(8,128)(2,1)S(1)} %pad_maximum_fusion.3), channel_id=1, source_target_pairs={{0,2},{1,3},{2,0},{3,1},{4,6},{5,7},{6,4},{7,5},{8,10},{9,11},{10,... | collective-permute-start | bytes 442376 | tf_op jit(solution)/shard_map/ppermute | solution.py:107
  27.8 1.0 %collective-permute-done.14 = bf16[32,2304]{1,0:T(8,128)(2,1)S(1)} collective-permute-done((bf16[32,2304]{1,0:T(8,128)(2,1)S(1)}, bf16[32,2304]{1,0:T(8,128)(2,1)S(1)}, u32[]{:S(2)}, u32[]{:S(2)}) %collective-permute-start.14) | collective-permute-done | bytes 147488 | tf_op jit(solution)/shard_map/ppermute | solution.py:107
  28.8 2.2 %collective-permute-start.15 = (bf16[16,2304]{1,0:T(8,128)(2,1)S(1)}, bf16[16,2304]{1,0:T(8,128)(2,1)S(1)}, u32[]{:S(2)}, u32[]{:S(2)}) collective-permute-start(bf16[16,2304]{1,0:T(8,128)(2,1)S(1)} %get-tuple-element.37), channel_id=1, source_target_pairs={{0,8},{1,9},{2,10},{3,11},{4,12},{5,13},{6,14},{7,15},{8,0},{9,1},... | collective-permute-start | bytes 221192 | tf_op jit(solution)/shard_map/ppermute | solution.py:107
  31.0 1.5 %collective-permute-start.16 = (bf16[16,2304]{1,0:T(8,128)(2,1)S(1)}, bf16[16,2304]{1,0:T(8,128)(2,1)S(1)}, u32[]{:S(2)}, u32[]{:S(2)}) collective-permute-start(bf16[16,2304]{1,0:T(8,128)(2,1)S(1)} %get-tuple-element.38), channel_id=1, source_target_pairs={{0,12},{1,13},{2,14},{3,15},{4,8},{5,9},{6,10},{7,11},{8,4},{9,5},... | collective-permute-start | bytes 221192 | tf_op jit(solution)/shard_map/ppermute | solution.py:107
  33.2 1.3 %collective-permute-start.13 = (bf16[16,2304]{1,0:T(8,128)(2,1)S(1)}, bf16[16,2304]{1,0:T(8,128)(2,1)S(1)}, u32[]{:S(2)}, u32[]{:S(2)}) collective-permute-start(bf16[16,2304]{1,0:T(8,128)(2,1)S(1)} %fusion.15), channel_id=1, source_target_pairs={{0,4},{1,5},{2,6},{3,7},{4,0},{5,1},{6,2},{7,3},{8,12},{9,13},{10,... | collective-permute-start | bytes 221192 | tf_op jit(solution)/shard_map/ppermute | solution.py:107
  34.5 1.5 %collective-permute-done.15 = bf16[16,2304]{1,0:T(8,128)(2,1)S(1)} collective-permute-done((bf16[16,2304]{1,0:T(8,128)(2,1)S(1)}, bf16[16,2304]{1,0:T(8,128)(2,1)S(1)}, u32[]{:S(2)}, u32[]{:S(2)}) %collective-permute-start.15) | collective-permute-done | bytes 73760 | tf_op jit(solution)/shard_map/ppermute | solution.py:107
  36.0 1.4 %collective-permute-done.16 = bf16[16,2304]{1,0:T(8,128)(2,1)S(1)} collective-permute-done((bf16[16,2304]{1,0:T(8,128)(2,1)S(1)}, bf16[16,2304]{1,0:T(8,128)(2,1)S(1)}, u32[]{:S(2)}, u32[]{:S(2)}) %collective-permute-start.16) | collective-permute-done | bytes 73760 | tf_op jit(solution)/shard_map/ppermute | solution.py:107
  37.3 0.8 %collective-permute-done.13 = bf16[16,2304]{1,0:T(8,128)(2,1)S(1)} collective-permute-done((bf16[16,2304]{1,0:T(8,128)(2,1)S(1)}, bf16[16,2304]{1,0:T(8,128)(2,1)S(1)}, u32[]{:S(2)}, u32[]{:S(2)}) %collective-permute-start.13) | collective-permute-done | bytes 73760 | tf_op jit(solution)/shard_map/ppermute | solution.py:107
  38.2 3.1 %collective-permute-start.22 = (bf16[16,2304]{1,0:T(8,128)(2,1)S(1)}, bf16[16,2304]{1,0:T(8,128)(2,1)S(1)}, u32[]{:S(2)}, u32[]{:S(2)}) collective-permute-start(bf16[16,2304]{1,0:T(8,128)(2,1)S(1)} %fusion.20), channel_id=1, source_target_pairs={{0,12},{1,13},{2,14},{3,15},{4,8},{5,9},{6,10},{7,11},{8,4},{9,5},... | collective-permute-start | bytes 221192 | tf_op jit(solution)/shard_map/ppermute | solution.py:107
  41.3 1.4 %collective-permute-start.18 = (bf16[16,2304]{1,0:T(8,128)(2,1)S(1)}, bf16[16,2304]{1,0:T(8,128)(2,1)S(1)}, u32[]{:S(2)}, u32[]{:S(2)}) collective-permute-start(bf16[16,2304]{1,0:T(8,128)(2,1)S(1)} %fusion.20), channel_id=1, source_target_pairs={{0,4},{1,5},{2,6},{3,7},{4,0},{5,1},{6,2},{7,3},{8,12},{9,13},{10,... | collective-permute-start | bytes 221192 | tf_op jit(solution)/shard_map/ppermute | solution.py:107
  42.7 1.0 %collective-permute-start.17 = (bf16[16,2304]{1,0:T(8,128)(2,1)S(1)}, bf16[16,2304]{1,0:T(8,128)(2,1)S(1)}, u32[]{:S(2)}, u32[]{:S(2)}) collective-permute-start(bf16[16,2304]{1,0:T(8,128)(2,1)S(1)} %fusion.20), channel_id=1, source_target_pairs={{0,2},{1,3},{2,0},{3,1},{4,6},{5,7},{6,4},{7,5},{8,10},{9,11},{10,... | collective-permute-start | bytes 221192 | tf_op jit(solution)/shard_map/ppermute | solution.py:107
  43.9 0.7 %collective-permute-done.22 = bf16[16,2304]{1,0:T(8,128)(2,1)S(1)} collective-permute-done((bf16[16,2304]{1,0:T(8,128)(2,1)S(1)}, bf16[16,2304]{1,0:T(8,128)(2,1)S(1)}, u32[]{:S(2)}, u32[]{:S(2)}) %collective-permute-start.22) | collective-permute-done | bytes 73760 | tf_op jit(solution)/shard_map/ppermute | solution.py:107
  44.5 1.1 %collective-permute-start.23 = (bf16[16,2304]{1,0:T(8,128)(2,1)S(1)}, bf16[16,2304]{1,0:T(8,128)(2,1)S(1)}, u32[]{:S(2)}, u32[]{:S(2)}) collective-permute-start(bf16[16,2304]{1,0:T(8,128)(2,1)S(1)} %collective-permute-done.22), channel_id=1, source_target_pairs={{0,2},{1,3},{2,0},{3,1},{4,6},{5,7},{6,4},{7,5},{8,10},{9,11},{10,... | collective-permute-start | bytes 221192 | tf_op jit(solution)/shard_map/ppermute | solution.py:107
  45.6 1.9 %collective-permute-done.20 = bf16[16,2304]{1,0:T(8,128)(2,1)S(1)} collective-permute-done((bf16[16,2304]{1,0:T(8,128)(2,1)S(1)}, bf16[16,2304]{1,0:T(8,128)(2,1)S(1)}, u32[]{:S(2)}, u32[]{:S(2)}) %collective-permute-start.20) | collective-permute-done | bytes 73760 | tf_op jit(solution)/shard_map/ppermute | solution.py:107
  47.5 1.0 %collective-permute-start.21 = (bf16[16,2304]{1,0:T(8,128)(2,1)S(1)}, bf16[16,2304]{1,0:T(8,128)(2,1)S(1)}, u32[]{:S(2)}, u32[]{:S(2)}) collective-permute-start(bf16[16,2304]{1,0:T(8,128)(2,1)S(1)} %collective-permute-done.20), channel_id=1, source_target_pairs={{0,2},{1,3},{2,0},{3,1},{4,6},{5,7},{6,4},{7,5},{8,10},{9,11},{10,... | collective-permute-start | bytes 221192 | tf_op jit(solution)/shard_map/ppermute | solution.py:107
  48.5 1.0 %collective-permute-start.19 = (bf16[16,2304]{1,0:T(8,128)(2,1)S(1)}, bf16[16,2304]{1,0:T(8,128)(2,1)S(1)}, u32[]{:S(2)}, u32[]{:S(2)}) collective-permute-start(bf16[16,2304]{1,0:T(8,128)(2,1)S(1)} %collective-permute-done.18), channel_id=1, source_target_pairs={{0,2},{1,3},{2,0},{3,1},{4,6},{5,7},{6,4},{7,5},{8,10},{9,11},{10,... | collective-permute-start | bytes 221192 | tf_op jit(solution)/shard_map/ppermute | solution.py:107
  49.6 2.4 %collective-permute-done.21 = bf16[16,2304]{1,0:T(8,128)(2,1)S(1)} collective-permute-done((bf16[16,2304]{1,0:T(8,128)(2,1)S(1)}, bf16[16,2304]{1,0:T(8,128)(2,1)S(1)}, u32[]{:S(2)}, u32[]{:S(2)}) %collective-permute-start.21) | collective-permute-done | bytes 73760 | tf_op jit(solution)/shard_map/ppermute | solution.py:107
  52.1 0.8 %collective-permute-done.19 = bf16[16,2304]{1,0:T(8,128)(2,1)S(1)} collective-permute-done((bf16[16,2304]{1,0:T(8,128)(2,1)S(1)}, bf16[16,2304]{1,0:T(8,128)(2,1)S(1)}, u32[]{:S(2)}, u32[]{:S(2)}) %collective-permute-start.19) | collective-permute-done | bytes 73760 | tf_op jit(solution)/shard_map/ppermute | solution.py:107
  53.6 0.9 %collective-permute-done.24.refs_1_ = bf16[64,2304]{1,0:T(8,128)(2,1)S(1)} collective-permute-done((bf16[64,2304]{1,0:T(8,128)(2,1)S(1)}, bf16[64,2304]{1,0:T(8,128)(2,1)S(1)}, u32[]{:S(2)}, u32[]{:S(2)}) %collective-permute-start.24) | collective-permute-done | bytes 294944 | tf_op jit(solution)/shard_map/ppermute | solution.py:114
  54.6 3.4 %update.1 = (bf16[128,2304]{1,0:T(8,128)(2,1)}, f32[128,2304]{1,0:T(8,128)}, f32[128,2304]{1,0:T(8,128)}, bf16[128,2304]{1,0:T(8,128)(2,1)}, f32[128,2304]{1,0:T(8,128)}, /*index=5*/f32[128,2304]{1,0:T(8,128)}) custom-call(bf16[128,256]{1,0:T(8,128)(2,1)S(1)} %maximum_bitcast_fusion.codes_across, bf16[256,2304]{1,0:T(8,128)(2,1)S(1)} %pad_maximum_fusion.centered, ...), custom_call_target="tpu_custom_call" | custom-call | flops 452984832 | bytes 12976128 | tf_op jit(solution)/shard_map/update/pallas_call | solution.py:80
  (74 shorter events, 5.7 us)
Async XLA Ops:
  0.6 3.2 %collective-permute-start.1 = (bf16[128,2304]{1,0:T(8,128)(2,1)}, bf16[128,2304]{1,0:T(8,128)(2,1)S(1)}, u32[]{:S(2)}, u32[]{:S(2)}) collective-permute-start(bf16[128,2304]{1,0:T(8,128)(2,1)} %refs_3_.1), channel_id=1, source_target_pairs={{0,1},{1,0},{2,3},{3,2},{4,5},{5,4},{6,7},{7,6},{8,9},{9,8},{10,11... | collective-permute-start | bytes 1769480 | tf_op jit(solution)/shard_map/ppermute | solution.py:114
  1.1 2.7 %collective-permute-start.2 = (bf16[128,2304]{1,0:T(8,128)(2,1)}, bf16[128,2304]{1,0:T(8,128)(2,1)S(1)}, u32[]{:S(2)}, u32[]{:S(2)}) collective-permute-start(bf16[128,2304]{1,0:T(8,128)(2,1)} %refs_4_.1), channel_id=1, source_target_pairs={{0,1},{1,0},{2,3},{3,2},{4,5},{5,4},{6,7},{7,6},{8,9},{9,8},{10,11... | collective-permute-start | bytes 1769480 | tf_op jit(solution)/shard_map/ppermute | solution.py:114
  1.2 2.6 %collective-permute-start = (f32[128]{0:T(128)}, f32[128]{0:T(128)S(1)}, u32[]{:S(2)}, u32[]{:S(2)}) collective-permute-start(f32[128]{0:T(128)} %param.11), channel_id=1, source_target_pairs={{0,1},{1,0},{2,3},{3,2},{4,5},{5,4},{6,7},{7,6},{8,9},{9,8},{10,11... | collective-permute-start | bytes 1544 | tf_op jit(solution)/shard_map/ppermute | solution.py:114
  3.8 11.3 %collective-permute-start.8 = (bf16[16,2304]{1,0:T(8,128)(2,1)}, bf16[16,2304]{1,0:T(8,128)(2,1)S(1)}, u32[]{:S(2)}, u32[]{:S(2)}) collective-permute-start(bf16[16,2304]{1,0:T(8,128)(2,1)} %param.9), channel_id=1, source_target_pairs={{0,12},{1,13},{2,14},{3,15},{4,8},{5,9},{6,10},{7,11},{8,4},{9,5},... | collective-permute-start | bytes 221192 | tf_op jit(solution)/shard_map/ppermute | solution.py:107
  8.8 8.1 %collective-permute-start.6 = (bf16[16,2304]{1,0:T(8,128)(2,1)}, bf16[16,2304]{1,0:T(8,128)(2,1)S(1)}, u32[]{:S(2)}, u32[]{:S(2)}) collective-permute-start(bf16[16,2304]{1,0:T(8,128)(2,1)} %param.9), channel_id=1, source_target_pairs={{0,8},{1,9},{2,10},{3,11},{4,12},{5,13},{6,14},{7,15},{8,0},{9,1},... | collective-permute-start | bytes 221192 | tf_op jit(solution)/shard_map/ppermute | solution.py:107
  8.8 8.4 %collective-permute-start.4 = (bf16[16,2304]{1,0:T(8,128)(2,1)}, bf16[16,2304]{1,0:T(8,128)(2,1)S(1)}, u32[]{:S(2)}, u32[]{:S(2)}) collective-permute-start(bf16[16,2304]{1,0:T(8,128)(2,1)} %param.9), channel_id=1, source_target_pairs={{0,4},{1,5},{2,6},{3,7},{4,0},{5,1},{6,2},{7,3},{8,12},{9,13},{10,... | collective-permute-start | bytes 221192 | tf_op jit(solution)/shard_map/ppermute | solution.py:107
  9.4 4.6 %collective-permute-start.3 = (bf16[16,2304]{1,0:T(8,128)(2,1)}, bf16[16,2304]{1,0:T(8,128)(2,1)S(1)}, u32[]{:S(2)}, u32[]{:S(2)}) collective-permute-start(bf16[16,2304]{1,0:T(8,128)(2,1)} %param.9), channel_id=1, source_target_pairs={{0,2},{1,3},{2,0},{3,1},{4,6},{5,7},{6,4},{7,5},{8,10},{9,11},{10,... | collective-permute-start | bytes 221192 | tf_op jit(solution)/shard_map/ppermute | solution.py:107
  15.1 6.9 %collective-permute-start.9 = (bf16[16,2304]{1,0:T(8,128)(2,1)S(1)}, bf16[16,2304]{1,0:T(8,128)(2,1)S(1)}, u32[]{:S(2)}, u32[]{:S(2)}) collective-permute-start(bf16[16,2304]{1,0:T(8,128)(2,1)S(1)} %collective-permute-done.8), channel_id=1, source_target_pairs={{0,2},{1,3},{2,0},{3,1},{4,6},{5,7},{6,4},{7,5},{8,10},{9,11},{10,... | collective-permute-start | bytes 221192 | tf_op jit(solution)/shard_map/ppermute | solution.py:107
  16.9 5.2 %collective-permute-start.7 = (bf16[16,2304]{1,0:T(8,128)(2,1)S(1)}, bf16[16,2304]{1,0:T(8,128)(2,1)S(1)}, u32[]{:S(2)}, u32[]{:S(2)}) collective-permute-start(bf16[16,2304]{1,0:T(8,128)(2,1)S(1)} %collective-permute-done.6), channel_id=1, source_target_pairs={{0,2},{1,3},{2,0},{3,1},{4,6},{5,7},{6,4},{7,5},{8,10},{9,11},{10,... | collective-permute-start | bytes 221192 | tf_op jit(solution)/shard_map/ppermute | solution.py:107
  17.2 4.8 %collective-permute-start.5 = (bf16[16,2304]{1,0:T(8,128)(2,1)S(1)}, bf16[16,2304]{1,0:T(8,128)(2,1)S(1)}, u32[]{:S(2)}, u32[]{:S(2)}) collective-permute-start(bf16[16,2304]{1,0:T(8,128)(2,1)S(1)} %collective-permute-done.4), channel_id=1, source_target_pairs={{0,2},{1,3},{2,0},{3,1},{4,6},{5,7},{6,4},{7,5},{8,10},{9,11},{10,... | collective-permute-start | bytes 221192 | tf_op jit(solution)/shard_map/ppermute | solution.py:107
  23.6 5.2 %collective-permute-start.14 = (bf16[32,2304]{1,0:T(8,128)(2,1)S(1)}, bf16[32,2304]{1,0:T(8,128)(2,1)S(1)}, u32[]{:S(2)}, u32[]{:S(2)}) collective-permute-start(bf16[32,2304]{1,0:T(8,128)(2,1)S(1)} %pad_maximum_fusion.4), channel_id=1, source_target_pairs={{0,2},{1,3},{2,0},{3,1},{4,6},{5,7},{6,4},{7,5},{8,10},{9,11},{10,... | collective-permute-start | bytes 442376 | tf_op jit(solution)/shard_map/ppermute | solution.py:107
  24.9 1.2 %collective-permute-start.10 = (bf16[128,128]{0,1:T(8,128)(2,1)S(1)}, bf16[128,128]{0,1:T(8,128)(2,1)S(1)}, u32[]{:S(2)}, u32[]{:S(2)}) collective-permute-start(bf16[128,128]{0,1:T(8,128)(2,1)S(1)} %get-tuple-element.44), channel_id=1, source_target_pairs={{0,1},{1,0},{2,3},{3,2},{4,5},{5,4},{6,7},{7,6},{8,9},{9,8},{10,11... | collective-permute-start | bytes 98312 | tf_op jit(solution)/shard_map/ppermute | solution.py:114
  24.9 2.1 %collective-permute-start.11 = (bf16[128,2304]{1,0:T(8,128)(2,1)S(1)}, bf16[128,2304]{1,0:T(8,128)(2,1)S(1)}, u32[]{:S(2)}, u32[]{:S(2)}) collective-permute-start(bf16[128,2304]{1,0:T(8,128)(2,1)S(1)} %subtract_convert_fusion), channel_id=1, source_target_pairs={{0,1},{1,0},{2,3},{3,2},{4,5},{5,4},{6,7},{7,6},{8,9},{9,8},{10,11... | collective-permute-start | bytes 1769480 | tf_op jit(solution)/shard_map/ppermute | solution.py:114
  27.0 6.1 %collective-permute-start.12 = (bf16[32,2304]{1,0:T(8,128)(2,1)S(1)}, bf16[32,2304]{1,0:T(8,128)(2,1)S(1)}, u32[]{:S(2)}, u32[]{:S(2)}) collective-permute-start(bf16[32,2304]{1,0:T(8,128)(2,1)S(1)} %pad_maximum_fusion.3), channel_id=1, source_target_pairs={{0,2},{1,3},{2,0},{3,1},{4,6},{5,7},{6,4},{7,5},{8,10},{9,11},{10,... | collective-permute-start | bytes 442376 | tf_op jit(solution)/shard_map/ppermute | solution.py:107
  28.8 7.2 %collective-permute-start.15 = (bf16[16,2304]{1,0:T(8,128)(2,1)S(1)}, bf16[16,2304]{1,0:T(8,128)(2,1)S(1)}, u32[]{:S(2)}, u32[]{:S(2)}) collective-permute-start(bf16[16,2304]{1,0:T(8,128)(2,1)S(1)} %get-tuple-element.37), channel_id=1, source_target_pairs={{0,8},{1,9},{2,10},{3,11},{4,12},{5,13},{6,14},{7,15},{8,0},{9,1},... | collective-permute-start | bytes 221192 | tf_op jit(solution)/shard_map/ppermute | solution.py:107
  31.0 6.3 %collective-permute-start.16 = (bf16[16,2304]{1,0:T(8,128)(2,1)S(1)}, bf16[16,2304]{1,0:T(8,128)(2,1)S(1)}, u32[]{:S(2)}, u32[]{:S(2)}) collective-permute-start(bf16[16,2304]{1,0:T(8,128)(2,1)S(1)} %get-tuple-element.38), channel_id=1, source_target_pairs={{0,12},{1,13},{2,14},{3,15},{4,8},{5,9},{6,10},{7,11},{8,4},{9,5},... | collective-permute-start | bytes 221192 | tf_op jit(solution)/shard_map/ppermute | solution.py:107
  33.2 5.0 %collective-permute-start.13 = (bf16[16,2304]{1,0:T(8,128)(2,1)S(1)}, bf16[16,2304]{1,0:T(8,128)(2,1)S(1)}, u32[]{:S(2)}, u32[]{:S(2)}) collective-permute-start(bf16[16,2304]{1,0:T(8,128)(2,1)S(1)} %fusion.15), channel_id=1, source_target_pairs={{0,4},{1,5},{2,6},{3,7},{4,0},{5,1},{6,2},{7,3},{8,12},{9,13},{10,... | collective-permute-start | bytes 221192 | tf_op jit(solution)/shard_map/ppermute | solution.py:107
  38.2 16.4 %copy-start.4 = (f32[128,2304]{1,0:T(8,128)S(1)}, f32[128,2304]{1,0:T(8,128)}, u32[]{:S(2)}) copy-start(f32[128,2304]{1,0:T(8,128)} %refs_8_.1) | copy-start | bytes 3538948
  38.2 14.7 %copy-start.6 = (bf16[16,2304]{1,0:T(8,128)(2,1)}, bf16[16,2304]{1,0:T(8,128)(2,1)S(1)}, u32[]{:S(2)}) copy-start(bf16[16,2304]{1,0:T(8,128)(2,1)S(1)} %fusion.20) | copy-start | bytes 221188
  38.2 6.3 %collective-permute-start.22 = (bf16[16,2304]{1,0:T(8,128)(2,1)S(1)}, bf16[16,2304]{1,0:T(8,128)(2,1)S(1)}, u32[]{:S(2)}, u32[]{:S(2)}) collective-permute-start(bf16[16,2304]{1,0:T(8,128)(2,1)S(1)} %fusion.20), channel_id=1, source_target_pairs={{0,12},{1,13},{2,14},{3,15},{4,8},{5,9},{6,10},{7,11},{8,4},{9,5},... | collective-permute-start | bytes 221192 | tf_op jit(solution)/shard_map/ppermute | solution.py:107
  41.3 6.2 %collective-permute-start.20 = (bf16[16,2304]{1,0:T(8,128)(2,1)S(1)}, bf16[16,2304]{1,0:T(8,128)(2,1)S(1)}, u32[]{:S(2)}, u32[]{:S(2)}) collective-permute-start(bf16[16,2304]{1,0:T(8,128)(2,1)S(1)} %fusion.20), channel_id=1, source_target_pairs={{0,8},{1,9},{2,10},{3,11},{4,12},{5,13},{6,14},{7,15},{8,0},{9,1},... | collective-permute-start | bytes 221192 | tf_op jit(solution)/shard_map/ppermute | solution.py:107
  41.3 7.2 %collective-permute-start.18 = (bf16[16,2304]{1,0:T(8,128)(2,1)S(1)}, bf16[16,2304]{1,0:T(8,128)(2,1)S(1)}, u32[]{:S(2)}, u32[]{:S(2)}) collective-permute-start(bf16[16,2304]{1,0:T(8,128)(2,1)S(1)} %fusion.20), channel_id=1, source_target_pairs={{0,4},{1,5},{2,6},{3,7},{4,0},{5,1},{6,2},{7,3},{8,12},{9,13},{10,... | collective-permute-start | bytes 221192 | tf_op jit(solution)/shard_map/ppermute | solution.py:107
  42.7 6.8 %collective-permute-start.17 = (bf16[16,2304]{1,0:T(8,128)(2,1)S(1)}, bf16[16,2304]{1,0:T(8,128)(2,1)S(1)}, u32[]{:S(2)}, u32[]{:S(2)}) collective-permute-start(bf16[16,2304]{1,0:T(8,128)(2,1)S(1)} %fusion.20), channel_id=1, source_target_pairs={{0,2},{1,3},{2,0},{3,1},{4,6},{5,7},{6,4},{7,5},{8,10},{9,11},{10,... | collective-permute-start | bytes 221192 | tf_op jit(solution)/shard_map/ppermute | solution.py:107
  43.7 10.8 %copy-start.2 = (f32[128,2304]{1,0:T(8,128)S(1)}, f32[128,2304]{1,0:T(8,128)}, u32[]{:S(2)}) copy-start(f32[128,2304]{1,0:T(8,128)} %refs_6_.1) | copy-start | bytes 3538948
  43.7 10.8 %copy-start.3 = (f32[128,2304]{1,0:T(8,128)S(1)}, f32[128,2304]{1,0:T(8,128)}, u32[]{:S(2)}) copy-start(f32[128,2304]{1,0:T(8,128)} %refs_7_.1) | copy-start | bytes 3538948
  43.8 10.8 %copy-start = (bf16[128,2304]{1,0:T(8,128)(2,1)S(1)}, bf16[128,2304]{1,0:T(8,128)(2,1)}, u32[]{:S(2)}) copy-start(bf16[128,2304]{1,0:T(8,128)(2,1)} %refs_4_.1) | copy-start | bytes 1769476
  43.8 10.8 %copy-start.1 = (f32[128,2304]{1,0:T(8,128)S(1)}, f32[128,2304]{1,0:T(8,128)}, u32[]{:S(2)}) copy-start(f32[128,2304]{1,0:T(8,128)} %refs_5_.1) | copy-start | bytes 3538948
  44.5 5.0 %collective-permute-start.23 = (bf16[16,2304]{1,0:T(8,128)(2,1)S(1)}, bf16[16,2304]{1,0:T(8,128)(2,1)S(1)}, u32[]{:S(2)}, u32[]{:S(2)}) collective-permute-start(bf16[16,2304]{1,0:T(8,128)(2,1)S(1)} %collective-permute-done.22), channel_id=1, source_target_pairs={{0,2},{1,3},{2,0},{3,1},{4,6},{5,7},{6,4},{7,5},{8,10},{9,11},{10,... | collective-permute-start | bytes 221192 | tf_op jit(solution)/shard_map/ppermute | solution.py:107
  47.5 4.5 %collective-permute-start.21 = (bf16[16,2304]{1,0:T(8,128)(2,1)S(1)}, bf16[16,2304]{1,0:T(8,128)(2,1)S(1)}, u32[]{:S(2)}, u32[]{:S(2)}) collective-permute-start(bf16[16,2304]{1,0:T(8,128)(2,1)S(1)} %collective-permute-done.20), channel_id=1, source_target_pairs={{0,2},{1,3},{2,0},{3,1},{4,6},{5,7},{6,4},{7,5},{8,10},{9,11},{10,... | collective-permute-start | bytes 221192 | tf_op jit(solution)/shard_map/ppermute | solution.py:107
  48.5 4.4 %collective-permute-start.19 = (bf16[16,2304]{1,0:T(8,128)(2,1)S(1)}, bf16[16,2304]{1,0:T(8,128)(2,1)S(1)}, u32[]{:S(2)}, u32[]{:S(2)}) collective-permute-start(bf16[16,2304]{1,0:T(8,128)(2,1)S(1)} %collective-permute-done.18), channel_id=1, source_target_pairs={{0,2},{1,3},{2,0},{3,1},{4,6},{5,7},{6,4},{7,5},{8,10},{9,11},{10,... | collective-permute-start | bytes 221192 | tf_op jit(solution)/shard_map/ppermute | solution.py:107
  52.0 1.6 %collective-permute-start.25 = (bf16[64,2304]{1,0:T(8,128)(2,1)S(1)}, bf16[64,2304]{1,0:T(8,128)(2,1)S(1)}, u32[]{:S(2)}, u32[]{:S(2)}) collective-permute-start(bf16[64,2304]{1,0:T(8,128)(2,1)S(1)} %pad_maximum_fusion.2), channel_id=1, source_target_pairs={{0,1},{1,0},{2,3},{3,2},{4,5},{5,4},{6,7},{7,6},{8,9},{9,8},{10,11... | collective-permute-start | bytes 884744 | tf_op jit(solution)/shard_map/ppermute | solution.py:114
  52.9 1.6 %collective-permute-start.24 = (bf16[64,2304]{1,0:T(8,128)(2,1)S(1)}, bf16[64,2304]{1,0:T(8,128)(2,1)S(1)}, u32[]{:S(2)}, u32[]{:S(2)}) collective-permute-start(bf16[64,2304]{1,0:T(8,128)(2,1)S(1)} %pad_maximum_fusion.1), channel_id=1, source_target_pairs={{0,1},{1,0},{2,3},{3,2},{4,5},{5,4},{6,7},{7,6},{8,9},{9,8},{10,11... | collective-permute-start | bytes 884744 | tf_op jit(solution)/shard_map/ppermute | solution.py:114
  (3 other events, 17.2 us)

commit v16 on v15

--- a/solution.py
+++ b/solution.py
@@ -114,11 +114,8 @@
     return lax.ppermute(block, "latent", [(i, i ^ 1) for i in range(size)])
 
 
-def gather_chips(block, chips, after=None):
-    later = block
-    if after is not None:
-        later, _ = lax.optimization_barrier((block, after))
-    even = [later] + [to_chip(later, k) for k in range(2, chips, 2)]
+def gather_chips(block, chips):
+    even = [block] + [to_chip(block, k) for k in range(2, chips, 2)]
     return even, [to_chip(one, 1) for one in even]
 
 
@@ -143,13 +140,10 @@
     chips = size // 2
     total_rows = rows_here * size
 
-    others = [to_other_core(one) for one in (encoder_bias, encoder, decoder)]
-    even, odd = gather_chips(activations, chips, others)
-    rows_core = jnp.concatenate(in_turn(even, odd), 0)
-    mine, _ = lax.optimization_barrier(((encoder_bias, encoder, decoder), odd[0]))
-    bias_both, encoder_both, decoder_both = (
-        jnp.concatenate(both, 0) for both in zip(mine, others)
-    )
+    rows_core = jnp.concatenate(in_turn(*gather_chips(activations, chips)), 0)
+    encoder_both = jnp.concatenate([encoder, to_other_core(encoder)], 0)
+    decoder_both = jnp.concatenate([decoder, to_other_core(decoder)], 0)
+    bias_both = jnp.concatenate([encoder_bias, to_other_core(encoder_bias)], 0)
 
     centered = (rows_core.astype(jnp.float32) - decoder_bias).astype(jnp.bfloat16)
     codes = jnp.maximum(inner_last(centered, encoder_both) + bias_both, 0.0).astype(

time: 58.2 us -> 54.5 us (0.936)
  starting transfers between devices: 28.4 us -> 26.6 us
  local copies, waits for them, and re-layouts: 2.24 us -> 1.33 us
  waiting for transfers between devices: 21.3 us -> 20.4 us
    ppermute x7, waiting for transfers between devices: 5.27 us -> 3.22 us  [to_other_core(): return lax.ppermute(block, 'latent', [(i, i ^ 1) for i in range(size)])]
    ppermute x19, starting transfers between devices: 26.8 us -> 25.4 us  [to_chip(): lax.ppermute(block, 'latent', [(i, i ^ 2 * distance) for i in range(size)])]
    ppermute x19, waiting for transfers between devices: 16 us -> 17.1 us  [to_chip(): lax.ppermute(block, 'latent', [(i, i ^ 2 * distance) for i in range(size)])]
    unnamed x33 -> x35, local copies, waits for them, and re-layouts: 2.16 us -> 1.25 us
where the time goes in v16:
time: 54.5 us; the launch traced here: 54.3 us
  starting transfers between devices  26.6 us (49%)
  waiting for transfers between devices  20.4 us (37%)
  Pallas kernels  3.38 us (6%)
  local copies, waits for them, and re-layouts  1.33 us (2%)
  matrix products  1.27 us (2%)
  between operations  0.99 us (2%)
    ppermute x19, starting transfers between devices, to_chip(): lax.ppermute(block, 'latent', [(i, i ^ 2 * distance) for i in range(size)])  25.4 us
    ppermute x19, waiting for transfers between devices, to_chip(): lax.ppermute(block, 'latent', [(i, i ^ 2 * distance) for i in range(size)])  17.1 us
    pallas_call x1, Pallas kernels, update(): pl.pallas_call(functools.partial(update_kernel, columns, float(total_rows...  3.38 us
    ppermute x7, waiting for transfers between devices, to_other_core(): return lax.ppermute(block, 'latent', [(i, i ^ 1) for i in range(size)])  3.22 us
    unnamed x35, local copies, waits for them, and re-layouts  1.25 us
    ppermute x7, starting transfers between devices, to_other_core(): return lax.ppermute(block, 'latent', [(i, i ^ 1) for i in range(size)])  1.23 us
  transfers between devices with their start and end apart: 26, of which 16 were waited for; matrix products, arithmetic and copies ran while one was open for 4% of the time, Pallas kernels for 0%

profile of v16, /device:TPU:0, one launch (start us, length us, event | category | flops | bytes accessed | tf_op | source)
XLA Modules:
  0.0 54.3 jit_solution(11374060941650069445)
XLA Ops:
  0.7 4.1 %collective-permute-start.3 = (bf16[16,2304]{1,0:T(8,128)(2,1)}, bf16[16,2304]{1,0:T(8,128)(2,1)S(1)}, u32[]{:S(2)}, u32[]{:S(2)}) collective-permute-start(bf16[16,2304]{1,0:T(8,128)(2,1)} %param.9), channel_id=1, source_target_pairs={{0,8},{1,9},{2,10},{3,11},{4,12},{5,13},{6,14},{7,15},{8,0},{9,1},... | collective-permute-start | bytes 221192 | tf_op jit(solution)/shard_map/ppermute | solution.py:107
  4.8 1.6 %collective-permute-start.1 = (bf16[16,2304]{1,0:T(8,128)(2,1)}, bf16[16,2304]{1,0:T(8,128)(2,1)S(1)}, u32[]{:S(2)}, u32[]{:S(2)}) collective-permute-start(bf16[16,2304]{1,0:T(8,128)(2,1)} %param.9), channel_id=1, source_target_pairs={{0,4},{1,5},{2,6},{3,7},{4,0},{5,1},{6,2},{7,3},{8,12},{9,13},{10,... | collective-permute-start | bytes 221192 | tf_op jit(solution)/shard_map/ppermute | solution.py:107
  6.4 1.5 %collective-permute-start = (bf16[16,2304]{1,0:T(8,128)(2,1)}, bf16[16,2304]{1,0:T(8,128)(2,1)S(1)}, u32[]{:S(2)}, u32[]{:S(2)}) collective-permute-start(bf16[16,2304]{1,0:T(8,128)(2,1)} %param.9), channel_id=1, source_target_pairs={{0,2},{1,3},{2,0},{3,1},{4,6},{5,7},{6,4},{7,5},{8,10},{9,11},{10,... | collective-permute-start | bytes 221192 | tf_op jit(solution)/shard_map/ppermute | solution.py:107
  8.1 1.1 %constant_dynamic-update-slice_fusion.9 = bf16[256,2304]{1,0:T(8,128)(2,1)S(1)} fusion(bf16[128,2304]{1,0:T(8,128)(2,1)} %refs_4_.1), kind=kLoop, calls=%fused_computation.39 | loop fusion | bytes 1179648
  10.0 1.0 %collective-permute-start.4 = (bf16[16,2304]{1,0:T(8,128)(2,1)S(1)}, bf16[16,2304]{1,0:T(8,128)(2,1)S(1)}, u32[]{:S(2)}, u32[]{:S(2)}) collective-permute-start(bf16[16,2304]{1,0:T(8,128)(2,1)S(1)} %collective-permute-done.3), channel_id=1, source_target_pairs={{0,2},{1,3},{2,0},{3,1},{4,6},{5,7},{6,4},{7,5},{8,10},{9,11},{10,... | collective-permute-start | bytes 221192 | tf_op jit(solution)/shard_map/ppermute | solution.py:107
  11.0 1.4 %collective-permute-start.2 = (bf16[16,2304]{1,0:T(8,128)(2,1)S(1)}, bf16[16,2304]{1,0:T(8,128)(2,1)S(1)}, u32[]{:S(2)}, u32[]{:S(2)}) collective-permute-start(bf16[16,2304]{1,0:T(8,128)(2,1)S(1)} %collective-permute-done.1), channel_id=1, source_target_pairs={{0,2},{1,3},{2,0},{3,1},{4,6},{5,7},{6,4},{7,5},{8,10},{9,11},{10,... | collective-permute-start | bytes 221192 | tf_op jit(solution)/shard_map/ppermute | solution.py:107
  12.4 1.8 %collective-permute-done.5 = bf16[16,2304]{1,0:T(8,128)(2,1)S(1)} collective-permute-done((bf16[16,2304]{1,0:T(8,128)(2,1)}, bf16[16,2304]{1,0:T(8,128)(2,1)S(1)}, u32[]{:S(2)}, u32[]{:S(2)}) %collective-permute-start.5) | collective-permute-done | bytes 73760 | tf_op jit(solution)/shard_map/ppermute | solution.py:107
  14.8 1.9 %collective-permute-done.2 = bf16[16,2304]{1,0:T(8,128)(2,1)S(1)} collective-permute-done((bf16[16,2304]{1,0:T(8,128)(2,1)S(1)}, bf16[16,2304]{1,0:T(8,128)(2,1)S(1)}, u32[]{:S(2)}, u32[]{:S(2)}) %collective-permute-start.2) | collective-permute-done | bytes 73760 | tf_op jit(solution)/shard_map/ppermute | solution.py:107
  16.7 1.9 %collective-permute-done.6 = bf16[16,2304]{1,0:T(8,128)(2,1)S(1)} collective-permute-done((bf16[16,2304]{1,0:T(8,128)(2,1)S(1)}, bf16[16,2304]{1,0:T(8,128)(2,1)S(1)}, u32[]{:S(2)}, u32[]{:S(2)}) %collective-permute-start.6) | collective-permute-done | bytes 73760 | tf_op jit(solution)/shard_map/ppermute | solution.py:107
  20.1 0.6 %collective-permute-start.14 = (bf16[32,2304]{1,0:T(8,128)(2,1)S(1)}, bf16[32,2304]{1,0:T(8,128)(2,1)S(1)}, u32[]{:S(2)}, u32[]{:S(2)}) collective-permute-start(bf16[32,2304]{1,0:T(8,128)(2,1)S(1)} %pad_maximum_fusion.4), channel_id=1, source_target_pairs={{0,2},{1,3},{2,0},{3,1},{4,6},{5,7},{6,4},{7,5},{8,10},{9,11},{10,... | collective-permute-start | bytes 442376 | tf_op jit(solution)/shard_map/ppermute | solution.py:107
  21.2 0.7 %collective-permute-done.10 = bf16[128,128]{0,1:T(8,128)(2,1)S(1)} collective-permute-done((bf16[128,128]{0,1:T(8,128)(2,1)S(1)}, bf16[128,128]{0,1:T(8,128)(2,1)S(1)}, u32[]{:S(2)}, u32[]{:S(2)}) %collective-permute-start.10) | collective-permute-done | bytes 32800 | tf_op jit(solution)/shard_map/ppermute | solution.py:114
  21.9 0.9 %collective-permute-done.11 = bf16[128,2304]{1,0:T(8,128)(2,1)S(1)} collective-permute-done((bf16[128,2304]{1,0:T(8,128)(2,1)S(1)}, bf16[128,2304]{1,0:T(8,128)(2,1)S(1)}, u32[]{:S(2)}, u32[]{:S(2)}) %collective-permute-start.11) | collective-permute-done | bytes 589856 | tf_op jit(solution)/shard_map/ppermute | solution.py:114
  22.8 1.5 %collective-permute-start.12 = (bf16[32,2304]{1,0:T(8,128)(2,1)S(1)}, bf16[32,2304]{1,0:T(8,128)(2,1)S(1)}, u32[]{:S(2)}, u32[]{:S(2)}) collective-permute-start(bf16[32,2304]{1,0:T(8,128)(2,1)S(1)} %pad_maximum_fusion.3), channel_id=1, source_target_pairs={{0,2},{1,3},{2,0},{3,1},{4,6},{5,7},{6,4},{7,5},{8,10},{9,11},{10,... | collective-permute-start | bytes 442376 | tf_op jit(solution)/shard_map/ppermute | solution.py:107
  24.4 1.0 %collective-permute-done.14 = bf16[32,2304]{1,0:T(8,128)(2,1)S(1)} collective-permute-done((bf16[32,2304]{1,0:T(8,128)(2,1)S(1)}, bf16[32,2304]{1,0:T(8,128)(2,1)S(1)}, u32[]{:S(2)}, u32[]{:S(2)}) %collective-permute-start.14) | collective-permute-done | bytes 147488 | tf_op jit(solution)/shard_map/ppermute | solution.py:107
  25.4 1.2 %collective-permute-start.15 = (bf16[16,2304]{1,0:T(8,128)(2,1)S(1)}, bf16[16,2304]{1,0:T(8,128)(2,1)S(1)}, u32[]{:S(2)}, u32[]{:S(2)}) collective-permute-start(bf16[16,2304]{1,0:T(8,128)(2,1)S(1)} %get-tuple-element.29), channel_id=1, source_target_pairs={{0,8},{1,9},{2,10},{3,11},{4,12},{5,13},{6,14},{7,15},{8,0},{9,1},... | collective-permute-start | bytes 221192 | tf_op jit(solution)/shard_map/ppermute | solution.py:107
  26.6 2.0 %collective-permute-start.16 = (bf16[16,2304]{1,0:T(8,128)(2,1)S(1)}, bf16[16,2304]{1,0:T(8,128)(2,1)S(1)}, u32[]{:S(2)}, u32[]{:S(2)}) collective-permute-start(bf16[16,2304]{1,0:T(8,128)(2,1)S(1)} %get-tuple-element.30), channel_id=1, source_target_pairs={{0,12},{1,13},{2,14},{3,15},{4,8},{5,9},{6,10},{7,11},{8,4},{9,5},... | collective-permute-start | bytes 221192 | tf_op jit(solution)/shard_map/ppermute | solution.py:107
  29.0 0.8 %collective-permute-start.13 = (bf16[16,2304]{1,0:T(8,128)(2,1)S(1)}, bf16[16,2304]{1,0:T(8,128)(2,1)S(1)}, u32[]{:S(2)}, u32[]{:S(2)}) collective-permute-start(bf16[16,2304]{1,0:T(8,128)(2,1)S(1)} %fusion.15), channel_id=1, source_target_pairs={{0,4},{1,5},{2,6},{3,7},{4,0},{5,1},{6,2},{7,3},{8,12},{9,13},{10,... | collective-permute-start | bytes 221192 | tf_op jit(solution)/shard_map/ppermute | solution.py:107
  29.8 3.8 %collective-permute-done.15 = bf16[16,2304]{1,0:T(8,128)(2,1)S(1)} collective-permute-done((bf16[16,2304]{1,0:T(8,128)(2,1)S(1)}, bf16[16,2304]{1,0:T(8,128)(2,1)S(1)}, u32[]{:S(2)}, u32[]{:S(2)}) %collective-permute-start.15) | collective-permute-done | bytes 73760 | tf_op jit(solution)/shard_map/ppermute | solution.py:107
  33.6 0.8 %collective-permute-done.13 = bf16[16,2304]{1,0:T(8,128)(2,1)S(1)} collective-permute-done((bf16[16,2304]{1,0:T(8,128)(2,1)S(1)}, bf16[16,2304]{1,0:T(8,128)(2,1)S(1)}, u32[]{:S(2)}, u32[]{:S(2)}) %collective-permute-start.13) | collective-permute-done | bytes 73760 | tf_op jit(solution)/shard_map/ppermute | solution.py:107
  34.4 2.9 %collective-permute-start.22 = (bf16[16,2304]{1,0:T(8,128)(2,1)S(1)}, bf16[16,2304]{1,0:T(8,128)(2,1)S(1)}, u32[]{:S(2)}, u32[]{:S(2)}) collective-permute-start(bf16[16,2304]{1,0:T(8,128)(2,1)S(1)} %fusion.20), channel_id=1, source_target_pairs={{0,12},{1,13},{2,14},{3,15},{4,8},{5,9},{6,10},{7,11},{8,4},{9,5},... | collective-permute-start | bytes 221192 | tf_op jit(solution)/shard_map/ppermute | solution.py:107
  37.3 1.6 %collective-permute-start.18 = (bf16[16,2304]{1,0:T(8,128)(2,1)S(1)}, bf16[16,2304]{1,0:T(8,128)(2,1)S(1)}, u32[]{:S(2)}, u32[]{:S(2)}) collective-permute-start(bf16[16,2304]{1,0:T(8,128)(2,1)S(1)} %fusion.20), channel_id=1, source_target_pairs={{0,4},{1,5},{2,6},{3,7},{4,0},{5,1},{6,2},{7,3},{8,12},{9,13},{10,... | collective-permute-start | bytes 221192 | tf_op jit(solution)/shard_map/ppermute | solution.py:107
  38.9 1.1 %collective-permute-start.17 = (bf16[16,2304]{1,0:T(8,128)(2,1)S(1)}, bf16[16,2304]{1,0:T(8,128)(2,1)S(1)}, u32[]{:S(2)}, u32[]{:S(2)}) collective-permute-start(bf16[16,2304]{1,0:T(8,128)(2,1)S(1)} %fusion.20), channel_id=1, source_target_pairs={{0,2},{1,3},{2,0},{3,1},{4,6},{5,7},{6,4},{7,5},{8,10},{9,11},{10,... | collective-permute-start | bytes 221192 | tf_op jit(solution)/shard_map/ppermute | solution.py:107
  40.2 1.0 %collective-permute-done.22 = bf16[16,2304]{1,0:T(8,128)(2,1)S(1)} collective-permute-done((bf16[16,2304]{1,0:T(8,128)(2,1)S(1)}, bf16[16,2304]{1,0:T(8,128)(2,1)S(1)}, u32[]{:S(2)}, u32[]{:S(2)}) %collective-permute-start.22) | collective-permute-done | bytes 73760 | tf_op jit(solution)/shard_map/ppermute | solution.py:107
  41.1 1.2 %collective-permute-start.23 = (bf16[16,2304]{1,0:T(8,128)(2,1)S(1)}, bf16[16,2304]{1,0:T(8,128)(2,1)S(1)}, u32[]{:S(2)}, u32[]{:S(2)}) collective-permute-start(bf16[16,2304]{1,0:T(8,128)(2,1)S(1)} %collective-permute-done.22), channel_id=1, source_target_pairs={{0,2},{1,3},{2,0},{3,1},{4,6},{5,7},{6,4},{7,5},{8,10},{9,11},{10,... | collective-permute-start | bytes 221192 | tf_op jit(solution)/shard_map/ppermute | solution.py:107
  42.3 1.3 %collective-permute-done.20 = bf16[16,2304]{1,0:T(8,128)(2,1)S(1)} collective-permute-done((bf16[16,2304]{1,0:T(8,128)(2,1)S(1)}, bf16[16,2304]{1,0:T(8,128)(2,1)S(1)}, u32[]{:S(2)}, u32[]{:S(2)}) %collective-permute-start.20) | collective-permute-done | bytes 73760 | tf_op jit(solution)/shard_map/ppermute | solution.py:107
  43.6 0.9 %collective-permute-start.21 = (bf16[16,2304]{1,0:T(8,128)(2,1)S(1)}, bf16[16,2304]{1,0:T(8,128)(2,1)S(1)}, u32[]{:S(2)}, u32[]{:S(2)}) collective-permute-start(bf16[16,2304]{1,0:T(8,128)(2,1)S(1)} %collective-permute-done.20), channel_id=1, source_target_pairs={{0,2},{1,3},{2,0},{3,1},{4,6},{5,7},{6,4},{7,5},{8,10},{9,11},{10,... | collective-permute-start | bytes 221192 | tf_op jit(solution)/shard_map/ppermute | solution.py:107
  44.5 1.1 %collective-permute-start.19 = (bf16[16,2304]{1,0:T(8,128)(2,1)S(1)}, bf16[16,2304]{1,0:T(8,128)(2,1)S(1)}, u32[]{:S(2)}, u32[]{:S(2)}) collective-permute-start(bf16[16,2304]{1,0:T(8,128)(2,1)S(1)} %collective-permute-done.18), channel_id=1, source_target_pairs={{0,2},{1,3},{2,0},{3,1},{4,6},{5,7},{6,4},{7,5},{8,10},{9,11},{10,... | collective-permute-start | bytes 221192 | tf_op jit(solution)/shard_map/ppermute | solution.py:107
  45.7 2.8 %collective-permute-done.21 = bf16[16,2304]{1,0:T(8,128)(2,1)S(1)} collective-permute-done((bf16[16,2304]{1,0:T(8,128)(2,1)S(1)}, bf16[16,2304]{1,0:T(8,128)(2,1)S(1)}, u32[]{:S(2)}, u32[]{:S(2)}) %collective-permute-start.21) | collective-permute-done | bytes 73760 | tf_op jit(solution)/shard_map/ppermute | solution.py:107
  48.5 0.7 %collective-permute-done.19 = bf16[16,2304]{1,0:T(8,128)(2,1)S(1)} collective-permute-done((bf16[16,2304]{1,0:T(8,128)(2,1)S(1)}, bf16[16,2304]{1,0:T(8,128)(2,1)S(1)}, u32[]{:S(2)}, u32[]{:S(2)}) %collective-permute-start.19) | collective-permute-done | bytes 73760 | tf_op jit(solution)/shard_map/ppermute | solution.py:107
  49.4 0.7 %collective-permute-done.25.refs_2_ = bf16[64,2304]{1,0:T(8,128)(2,1)S(1)} collective-permute-done((bf16[64,2304]{1,0:T(8,128)(2,1)S(1)}, bf16[64,2304]{1,0:T(8,128)(2,1)S(1)}, u32[]{:S(2)}, u32[]{:S(2)}) %collective-permute-start.25) | collective-permute-done | bytes 294944 | tf_op jit(solution)/shard_map/ppermute | solution.py:114
  50.1 0.8 %collective-permute-done.24.refs_1_ = bf16[64,2304]{1,0:T(8,128)(2,1)S(1)} collective-permute-done((bf16[64,2304]{1,0:T(8,128)(2,1)S(1)}, bf16[64,2304]{1,0:T(8,128)(2,1)S(1)}, u32[]{:S(2)}, u32[]{:S(2)}) %collective-permute-start.24) | collective-permute-done | bytes 294944 | tf_op jit(solution)/shard_map/ppermute | solution.py:114
  50.9 3.4 %update.1 = (bf16[128,2304]{1,0:T(8,128)(2,1)}, f32[128,2304]{1,0:T(8,128)}, f32[128,2304]{1,0:T(8,128)}, bf16[128,2304]{1,0:T(8,128)(2,1)}, f32[128,2304]{1,0:T(8,128)}, /*index=5*/f32[128,2304]{1,0:T(8,128)}) custom-call(bf16[128,256]{1,0:T(8,128)(2,1)S(1)} %maximum_bitcast_fusion.codes_across, bf16[256,2304]{1,0:T(8,128)(2,1)S(1)} %pad_maximum_fusion.centered, ...), custom_call_target="tpu_custom_call" | custom-call | flops 452984832 | bytes 12976128 | tf_op jit(solution)/shard_map/update/pallas_call | solution.py:80
  (76 shorter events, 4.3 us)
Async XLA Ops:
  0.7 17.9 %copy-start.8 = (f32[2304]{0:T(1024)S(1)}, f32[2304]{0:T(1024)}, u32[]{:S(2)}) copy-start(f32[2304]{0:T(1024)} %param.13) | copy-start | bytes 27652
  0.7 9.2 %collective-permute-start.3 = (bf16[16,2304]{1,0:T(8,128)(2,1)}, bf16[16,2304]{1,0:T(8,128)(2,1)S(1)}, u32[]{:S(2)}, u32[]{:S(2)}) collective-permute-start(bf16[16,2304]{1,0:T(8,128)(2,1)} %param.9), channel_id=1, source_target_pairs={{0,8},{1,9},{2,10},{3,11},{4,12},{5,13},{6,14},{7,15},{8,0},{9,1},... | collective-permute-start | bytes 221192 | tf_op jit(solution)/shard_map/ppermute | solution.py:107
  4.8 5.2 %collective-permute-start.1 = (bf16[16,2304]{1,0:T(8,128)(2,1)}, bf16[16,2304]{1,0:T(8,128)(2,1)S(1)}, u32[]{:S(2)}, u32[]{:S(2)}) collective-permute-start(bf16[16,2304]{1,0:T(8,128)(2,1)} %param.9), channel_id=1, source_target_pairs={{0,4},{1,5},{2,6},{3,7},{4,0},{5,1},{6,2},{7,3},{8,12},{9,13},{10,... | collective-permute-start | bytes 221192 | tf_op jit(solution)/shard_map/ppermute | solution.py:107
  6.4 4.7 %collective-permute-start = (bf16[16,2304]{1,0:T(8,128)(2,1)}, bf16[16,2304]{1,0:T(8,128)(2,1)S(1)}, u32[]{:S(2)}, u32[]{:S(2)}) collective-permute-start(bf16[16,2304]{1,0:T(8,128)(2,1)} %param.9), channel_id=1, source_target_pairs={{0,2},{1,3},{2,0},{3,1},{4,6},{5,7},{6,4},{7,5},{8,10},{9,11},{10,... | collective-permute-start | bytes 221192 | tf_op jit(solution)/shard_map/ppermute | solution.py:107
  7.9 6.4 %collective-permute-start.5 = (bf16[16,2304]{1,0:T(8,128)(2,1)}, bf16[16,2304]{1,0:T(8,128)(2,1)S(1)}, u32[]{:S(2)}, u32[]{:S(2)}) collective-permute-start(bf16[16,2304]{1,0:T(8,128)(2,1)} %param.9), channel_id=1, source_target_pairs={{0,12},{1,13},{2,14},{3,15},{4,8},{5,9},{6,10},{7,11},{8,4},{9,5},... | collective-permute-start | bytes 221192 | tf_op jit(solution)/shard_map/ppermute | solution.py:107
  8.1 1.3 %collective-permute-start.8 = (f32[128]{0:T(128)}, f32[128]{0:T(128)S(1)}, u32[]{:S(2)}, u32[]{:S(2)}) collective-permute-start(f32[128]{0:T(128)} %param.11), channel_id=1, source_target_pairs={{0,1},{1,0},{2,3},{3,2},{4,5},{5,4},{6,7},{7,6},{8,9},{9,8},{10,11... | collective-permute-start | bytes 1544 | tf_op jit(solution)/shard_map/ppermute | solution.py:114
  9.4 9.9 %collective-permute-start.9 = (bf16[128,2304]{1,0:T(8,128)(2,1)S(1)}, bf16[128,2304]{1,0:T(8,128)(2,1)S(1)}, u32[]{:S(2)}, u32[]{:S(2)}) collective-permute-start(bf16[128,2304]{1,0:T(8,128)(2,1)S(1)} %copy-done), channel_id=1, source_target_pairs={{0,1},{1,0},{2,3},{3,2},{4,5},{5,4},{6,7},{7,6},{8,9},{9,8},{10,11... | collective-permute-start | bytes 1769480 | tf_op jit(solution)/shard_map/ppermute | solution.py:114
  9.9 8.9 %collective-permute-start.7 = (bf16[128,2304]{1,0:T(8,128)(2,1)S(1)}, bf16[128,2304]{1,0:T(8,128)(2,1)S(1)}, u32[]{:S(2)}, u32[]{:S(2)}) collective-permute-start(bf16[128,2304]{1,0:T(8,128)(2,1)S(1)} %copy-done.5), channel_id=1, source_target_pairs={{0,1},{1,0},{2,3},{3,2},{4,5},{5,4},{6,7},{7,6},{8,9},{9,8},{10,11... | collective-permute-start | bytes 1769480 | tf_op jit(solution)/shard_map/ppermute | solution.py:114
  10.0 6.7 %collective-permute-start.4 = (bf16[16,2304]{1,0:T(8,128)(2,1)S(1)}, bf16[16,2304]{1,0:T(8,128)(2,1)S(1)}, u32[]{:S(2)}, u32[]{:S(2)}) collective-permute-start(bf16[16,2304]{1,0:T(8,128)(2,1)S(1)} %collective-permute-done.3), channel_id=1, source_target_pairs={{0,2},{1,3},{2,0},{3,1},{4,6},{5,7},{6,4},{7,5},{8,10},{9,11},{10,... | collective-permute-start | bytes 221192 | tf_op jit(solution)/shard_map/ppermute | solution.py:107
  11.0 5.7 %collective-permute-start.2 = (bf16[16,2304]{1,0:T(8,128)(2,1)S(1)}, bf16[16,2304]{1,0:T(8,128)(2,1)S(1)}, u32[]{:S(2)}, u32[]{:S(2)}) collective-permute-start(bf16[16,2304]{1,0:T(8,128)(2,1)S(1)} %collective-permute-done.1), channel_id=1, source_target_pairs={{0,2},{1,3},{2,0},{3,1},{4,6},{5,7},{6,4},{7,5},{8,10},{9,11},{10,... | collective-permute-start | bytes 221192 | tf_op jit(solution)/shard_map/ppermute | solution.py:107
  14.2 4.4 %collective-permute-start.6 = (bf16[16,2304]{1,0:T(8,128)(2,1)S(1)}, bf16[16,2304]{1,0:T(8,128)(2,1)S(1)}, u32[]{:S(2)}, u32[]{:S(2)}) collective-permute-start(bf16[16,2304]{1,0:T(8,128)(2,1)S(1)} %collective-permute-done.5), channel_id=1, source_target_pairs={{0,2},{1,3},{2,0},{3,1},{4,6},{5,7},{6,4},{7,5},{8,10},{9,11},{10,... | collective-permute-start | bytes 221192 | tf_op jit(solution)/shard_map/ppermute | solution.py:107
  20.1 5.2 %collective-permute-start.14 = (bf16[32,2304]{1,0:T(8,128)(2,1)S(1)}, bf16[32,2304]{1,0:T(8,128)(2,1)S(1)}, u32[]{:S(2)}, u32[]{:S(2)}) collective-permute-start(bf16[32,2304]{1,0:T(8,128)(2,1)S(1)} %pad_maximum_fusion.4), channel_id=1, source_target_pairs={{0,2},{1,3},{2,0},{3,1},{4,6},{5,7},{6,4},{7,5},{8,10},{9,11},{10,... | collective-permute-start | bytes 442376 | tf_op jit(solution)/shard_map/ppermute | solution.py:107
  20.7 1.2 %collective-permute-start.10 = (bf16[128,128]{0,1:T(8,128)(2,1)S(1)}, bf16[128,128]{0,1:T(8,128)(2,1)S(1)}, u32[]{:S(2)}, u32[]{:S(2)}) collective-permute-start(bf16[128,128]{0,1:T(8,128)(2,1)S(1)} %get-tuple-element.36), channel_id=1, source_target_pairs={{0,1},{1,0},{2,3},{3,2},{4,5},{5,4},{6,7},{7,6},{8,9},{9,8},{10,11... | collective-permute-start | bytes 98312 | tf_op jit(solution)/shard_map/ppermute | solution.py:114
  20.7 2.1 %collective-permute-start.11 = (bf16[128,2304]{1,0:T(8,128)(2,1)S(1)}, bf16[128,2304]{1,0:T(8,128)(2,1)S(1)}, u32[]{:S(2)}, u32[]{:S(2)}) collective-permute-start(bf16[128,2304]{1,0:T(8,128)(2,1)S(1)} %subtract_convert_fusion), channel_id=1, source_target_pairs={{0,1},{1,0},{2,3},{3,2},{4,5},{5,4},{6,7},{7,6},{8,9},{9,8},{10,11... | collective-permute-start | bytes 1769480 | tf_op jit(solution)/shard_map/ppermute | solution.py:114
  22.8 6.1 %collective-permute-start.12 = (bf16[32,2304]{1,0:T(8,128)(2,1)S(1)}, bf16[32,2304]{1,0:T(8,128)(2,1)S(1)}, u32[]{:S(2)}, u32[]{:S(2)}) collective-permute-start(bf16[32,2304]{1,0:T(8,128)(2,1)S(1)} %pad_maximum_fusion.3), channel_id=1, source_target_pairs={{0,2},{1,3},{2,0},{3,1},{4,6},{5,7},{6,4},{7,5},{8,10},{9,11},{10,... | collective-permute-start | bytes 442376 | tf_op jit(solution)/shard_map/ppermute | solution.py:107
  25.4 8.2 %collective-permute-start.15 = (bf16[16,2304]{1,0:T(8,128)(2,1)S(1)}, bf16[16,2304]{1,0:T(8,128)(2,1)S(1)}, u32[]{:S(2)}, u32[]{:S(2)}) collective-permute-start(bf16[16,2304]{1,0:T(8,128)(2,1)S(1)} %get-tuple-element.29), channel_id=1, source_target_pairs={{0,8},{1,9},{2,10},{3,11},{4,12},{5,13},{6,14},{7,15},{8,0},{9,1},... | collective-permute-start | bytes 221192 | tf_op jit(solution)/shard_map/ppermute | solution.py:107
  26.6 7.0 %collective-permute-start.16 = (bf16[16,2304]{1,0:T(8,128)(2,1)S(1)}, bf16[16,2304]{1,0:T(8,128)(2,1)S(1)}, u32[]{:S(2)}, u32[]{:S(2)}) collective-permute-start(bf16[16,2304]{1,0:T(8,128)(2,1)S(1)} %get-tuple-element.30), channel_id=1, source_target_pairs={{0,12},{1,13},{2,14},{3,15},{4,8},{5,9},{6,10},{7,11},{8,4},{9,5},... | collective-permute-start | bytes 221192 | tf_op jit(solution)/shard_map/ppermute | solution.py:107
  29.0 5.4 %collective-permute-start.13 = (bf16[16,2304]{1,0:T(8,128)(2,1)S(1)}, bf16[16,2304]{1,0:T(8,128)(2,1)S(1)}, u32[]{:S(2)}, u32[]{:S(2)}) collective-permute-start(bf16[16,2304]{1,0:T(8,128)(2,1)S(1)} %fusion.15), channel_id=1, source_target_pairs={{0,4},{1,5},{2,6},{3,7},{4,0},{5,1},{6,2},{7,3},{8,12},{9,13},{10,... | collective-permute-start | bytes 221192 | tf_op jit(solution)/shard_map/ppermute | solution.py:107
  34.4 14.8 %copy-start.6 = (bf16[16,2304]{1,0:T(8,128)(2,1)}, bf16[16,2304]{1,0:T(8,128)(2,1)S(1)}, u32[]{:S(2)}) copy-start(bf16[16,2304]{1,0:T(8,128)(2,1)S(1)} %fusion.20) | copy-start | bytes 221188
  34.4 6.7 %collective-permute-start.22 = (bf16[16,2304]{1,0:T(8,128)(2,1)S(1)}, bf16[16,2304]{1,0:T(8,128)(2,1)S(1)}, u32[]{:S(2)}, u32[]{:S(2)}) collective-permute-start(bf16[16,2304]{1,0:T(8,128)(2,1)S(1)} %fusion.20), channel_id=1, source_target_pairs={{0,12},{1,13},{2,14},{3,15},{4,8},{5,9},{6,10},{7,11},{8,4},{9,5},... | collective-permute-start | bytes 221192 | tf_op jit(solution)/shard_map/ppermute | solution.py:107
  37.3 6.3 %collective-permute-start.20 = (bf16[16,2304]{1,0:T(8,128)(2,1)S(1)}, bf16[16,2304]{1,0:T(8,128)(2,1)S(1)}, u32[]{:S(2)}, u32[]{:S(2)}) collective-permute-start(bf16[16,2304]{1,0:T(8,128)(2,1)S(1)} %fusion.20), channel_id=1, source_target_pairs={{0,8},{1,9},{2,10},{3,11},{4,12},{5,13},{6,14},{7,15},{8,0},{9,1},... | collective-permute-start | bytes 221192 | tf_op jit(solution)/shard_map/ppermute | solution.py:107
  37.3 7.2 %collective-permute-start.18 = (bf16[16,2304]{1,0:T(8,128)(2,1)S(1)}, bf16[16,2304]{1,0:T(8,128)(2,1)S(1)}, u32[]{:S(2)}, u32[]{:S(2)}) collective-permute-start(bf16[16,2304]{1,0:T(8,128)(2,1)S(1)} %fusion.20), channel_id=1, source_target_pairs={{0,4},{1,5},{2,6},{3,7},{4,0},{5,1},{6,2},{7,3},{8,12},{9,13},{10,... | collective-permute-start | bytes 221192 | tf_op jit(solution)/shard_map/ppermute | solution.py:107
  38.9 6.8 %collective-permute-start.17 = (bf16[16,2304]{1,0:T(8,128)(2,1)S(1)}, bf16[16,2304]{1,0:T(8,128)(2,1)S(1)}, u32[]{:S(2)}, u32[]{:S(2)}) collective-permute-start(bf16[16,2304]{1,0:T(8,128)(2,1)S(1)} %fusion.20), channel_id=1, source_target_pairs={{0,2},{1,3},{2,0},{3,1},{4,6},{5,7},{6,4},{7,5},{8,10},{9,11},{10,... | collective-permute-start | bytes 221192 | tf_op jit(solution)/shard_map/ppermute | solution.py:107
  40.0 10.9 %copy-start.4 = (f32[128,2304]{1,0:T(8,128)S(1)}, f32[128,2304]{1,0:T(8,128)}, u32[]{:S(2)}) copy-start(f32[128,2304]{1,0:T(8,128)} %refs_8_.1) | copy-start | bytes 3538948
  40.0 10.9 %copy-start.2 = (f32[128,2304]{1,0:T(8,128)S(1)}, f32[128,2304]{1,0:T(8,128)}, u32[]{:S(2)}) copy-start(f32[128,2304]{1,0:T(8,128)} %refs_6_.1) | copy-start | bytes 3538948
  40.0 10.9 %copy-start.3 = (f32[128,2304]{1,0:T(8,128)S(1)}, f32[128,2304]{1,0:T(8,128)}, u32[]{:S(2)}) copy-start(f32[128,2304]{1,0:T(8,128)} %refs_7_.1) | copy-start | bytes 3538948
  40.1 10.8 %copy-start.1 = (f32[128,2304]{1,0:T(8,128)S(1)}, f32[128,2304]{1,0:T(8,128)}, u32[]{:S(2)}) copy-start(f32[128,2304]{1,0:T(8,128)} %refs_5_.1) | copy-start | bytes 3538948
  41.1 4.5 %collective-permute-start.23 = (bf16[16,2304]{1,0:T(8,128)(2,1)S(1)}, bf16[16,2304]{1,0:T(8,128)(2,1)S(1)}, u32[]{:S(2)}, u32[]{:S(2)}) collective-permute-start(bf16[16,2304]{1,0:T(8,128)(2,1)S(1)} %collective-permute-done.22), channel_id=1, source_target_pairs={{0,2},{1,3},{2,0},{3,1},{4,6},{5,7},{6,4},{7,5},{8,10},{9,11},{10,... | collective-permute-start | bytes 221192 | tf_op jit(solution)/shard_map/ppermute | solution.py:107
  43.6 4.8 %collective-permute-start.21 = (bf16[16,2304]{1,0:T(8,128)(2,1)S(1)}, bf16[16,2304]{1,0:T(8,128)(2,1)S(1)}, u32[]{:S(2)}, u32[]{:S(2)}) collective-permute-start(bf16[16,2304]{1,0:T(8,128)(2,1)S(1)} %collective-permute-done.20), channel_id=1, source_target_pairs={{0,2},{1,3},{2,0},{3,1},{4,6},{5,7},{6,4},{7,5},{8,10},{9,11},{10,... | collective-permute-start | bytes 221192 | tf_op jit(solution)/shard_map/ppermute | solution.py:107
  44.5 4.7 %collective-permute-start.19 = (bf16[16,2304]{1,0:T(8,128)(2,1)S(1)}, bf16[16,2304]{1,0:T(8,128)(2,1)S(1)}, u32[]{:S(2)}, u32[]{:S(2)}) collective-permute-start(bf16[16,2304]{1,0:T(8,128)(2,1)S(1)} %collective-permute-done.18), channel_id=1, source_target_pairs={{0,2},{1,3},{2,0},{3,1},{4,6},{5,7},{6,4},{7,5},{8,10},{9,11},{10,... | collective-permute-start | bytes 221192 | tf_op jit(solution)/shard_map/ppermute | solution.py:107
  48.5 1.6 %collective-permute-start.25 = (bf16[64,2304]{1,0:T(8,128)(2,1)S(1)}, bf16[64,2304]{1,0:T(8,128)(2,1)S(1)}, u32[]{:S(2)}, u32[]{:S(2)}) collective-permute-start(bf16[64,2304]{1,0:T(8,128)(2,1)S(1)} %pad_maximum_fusion.2), channel_id=1, source_target_pairs={{0,1},{1,0},{2,3},{3,2},{4,5},{5,4},{6,7},{7,6},{8,9},{9,8},{10,11... | collective-permute-start | bytes 884744 | tf_op jit(solution)/shard_map/ppermute | solution.py:114
  49.3 1.6 %collective-permute-start.24 = (bf16[64,2304]{1,0:T(8,128)(2,1)S(1)}, bf16[64,2304]{1,0:T(8,128)(2,1)S(1)}, u32[]{:S(2)}, u32[]{:S(2)}) collective-permute-start(bf16[64,2304]{1,0:T(8,128)(2,1)S(1)} %pad_maximum_fusion.1), channel_id=1, source_target_pairs={{0,1},{1,0},{2,3},{3,2},{4,5},{5,4},{6,7},{7,6},{8,9},{9,8},{10,11... | collective-permute-start | bytes 884744 | tf_op jit(solution)/shard_map/ppermute | solution.py:114
  (4 other events, 35.7 us)

commit v17 on v16

--- a/solution.py
+++ b/solution.py
@@ -19,12 +19,51 @@
     )
 
 
+def own_kernel(columns, codes_across, centered, errors, decoder, encoder_total, decoder_total):
+    codes_t = codes_across[...]
+    signal = inner_last(decoder[...], errors[...])
+    delta_t = jnp.where(codes_t.astype(jnp.float32) > 0, signal, 0.0).astype(jnp.bfloat16)
+    for start in range(0, decoder.shape[1], columns):
+        at = pl.ds(start, columns)
+        decoder_total[:, at] = jnp.dot(
+            codes_t, errors[:, at], preferred_element_type=jnp.float32
+        )
+        encoder_total[:, at] = jnp.dot(
+            delta_t, centered[:, at], preferred_element_type=jnp.float32
+        )
+
+
+def own_totals(codes_across, centered, errors, decoder):
+    latents, width = decoder.shape
+    rows = centered.shape[0]
+    vmem = pl.BlockSpec(memory_space=pltpu.VMEM)
+    total = jax.ShapeDtypeStruct((latents, width), jnp.float32)
+    return pl.pallas_call(
+        functools.partial(own_kernel, columns_of(width)),
+        out_shape=(total, total),
+        in_specs=[vmem] * 4,
+        out_specs=[vmem] * 2,
+        compiler_params=pltpu.CompilerParams(vmem_limit_bytes=16 * 1024 * 1024 + 8 * rows * width),
+        cost_estimate=pl.CostEstimate(
+            flops=6 * latents * width * rows,
+            bytes_accessed=12 * latents * width + 4 * rows * width,
+            transcendentals=0,
+        ),
+        name="own_totals",
+    )(codes_across, centered, errors, decoder)
+
+
+def columns_of(width):
+    return next(c for c in (256, 128, width) if width % c == 0)
+
+
 def update_kernel(columns, rows_total, codes_across, centered, *refs):
-    blocks = len(refs) - 20
+    blocks = len(refs) - 22
     errors, (encoder, decoder) = refs[:blocks], refs[blocks : blocks + 2]
     moments = refs[blocks + 2 : blocks + 6]
-    outs = refs[blocks + 6 : blocks + 12]
-    error_all, *held, sem = refs[blocks + 12 :]
+    totals = refs[blocks + 6 : blocks + 8]
+    outs = refs[blocks + 8 : blocks + 14]
+    error_all, *held, sem = refs[blocks + 14 :]
     tiles = encoder.shape[1] // columns
     part = min(32, encoder.shape[0])
 
@@ -45,7 +84,7 @@
             total = jnp.dot(left, right[:, at], preferred_element_type=jnp.float32)
             for start in range(0, total.shape[0], part):
                 some = (pl.ds(start, part), at)
-                grad = total[start : start + part]
+                grad = totals[which][some] + total[start : start + part]
                 moment = beta_first * moments[2 * which][some] + first * grad
                 square = beta_second * moments[2 * which + 1][some] + second * (grad * grad)
                 root = square * lax.rsqrt(square)
@@ -68,10 +107,10 @@
             write(t, i).wait()
 
 
-def update(total_rows, codes_across, centered, errors, weights, moments):
+def update(total_rows, codes_across, centered, errors, weights, moments, totals):
     latents, width = weights[0].shape
     rows = centered.shape[0]
-    columns = next(c for c in (256, 128, width) if width % c == 0)
+    columns = columns_of(width)
     full = jax.ShapeDtypeStruct((latents, width), jnp.float32)
     half = jax.ShapeDtypeStruct((latents, width), jnp.bfloat16)
     vmem = pl.BlockSpec(memory_space=pltpu.VMEM)
@@ -80,7 +119,7 @@
     return pl.pallas_call(
         functools.partial(update_kernel, columns, float(total_rows)),
         out_shape=(half, full, full, half, full, full),
-        in_specs=[vmem] * (len(errors) + 8),
+        in_specs=[vmem] * (len(errors) + 10),
         out_specs=[pl.BlockSpec(memory_space=pl.ANY)] * 6,
         scratch_shapes=[
             pltpu.VMEM((rows, width), jnp.bfloat16),
@@ -99,7 +138,7 @@
             transcendentals=4 * latents * width,
         ),
         name="update",
-    )(codes_across, centered, *errors, *weights, *moments)
+    )(codes_across, centered, *errors, *weights, *moments, *totals)
 
 
 def to_chip(block, distance):
@@ -182,10 +221,9 @@
         (row_error, other_codes, other_centered)
     )
     blocks = in_turn(*gather_chips(row_error, chips))
-    errors = [jnp.concatenate(blocks, 0)]
-    errors += [to_other_core(jnp.concatenate(one, 0)) for one in (blocks[:4], blocks[4:])]
-    codes_across = jnp.concatenate([codes[:, :latents_here], other_codes], 0).T
-    centered_all = jnp.concatenate([centered, other_centered], 0)
+    errors = jnp.concatenate(blocks, 0)
+    other_errors = [to_other_core(jnp.concatenate(one, 0)) for one in (blocks[:4], blocks[4:])]
+    totals = own_totals(codes[:, :latents_here].T, centered, errors, decoder)
     (
         encoder_next,
         encoder_moment_next,
@@ -195,11 +233,12 @@
         decoder_square_next,
     ) = update(
         total_rows,
-        codes_across,
-        centered_all,
-        errors,
+        other_codes.T,
+        other_centered,
+        other_errors,
         (encoder, decoder),
         (encoder_moment, encoder_square, decoder_moment, decoder_square),
+        totals,
     )
     return (
         row_error,

time: 54.5 us -> 54.5 us (level)
  Pallas kernels: 3.38 us -> 4.23 us
  waiting for transfers between devices: 20.4 us -> 19.6 us
    ppermute x7, waiting for transfers between devices: 3.22 us -> 2.2 us  [to_other_core(): return lax.ppermute(block, 'latent', [(i, i ^ 1) for i in range(size)])]
    pallas_call x0 -> x1, Pallas kernels: none -> 0.97 us  [own_totals(): pl.pallas_call(functools.partial(own_kernel, columns_of(width)), out_shap...]
  transfers between devices with their start and end apart: 26 -> 26, of which waited for: 16 -> 15; matrix products, arithmetic and copies ran while one was open for 4% -> 4% of each run, Pallas kernels for 0% -> 2%
where the time goes in v17:
time: 54.5 us; the launch traced here: 54.3 us
  starting transfers between devices  26.6 us (49%)
  waiting for transfers between devices  19.6 us (36%)
  Pallas kernels  4.23 us (8%)
  local copies, waits for them, and re-layouts  1.47 us (3%)
  matrix products  1.27 us (2%)
  between operations  0.98 us (2%)
    ppermute x19, starting transfers between devices, to_chip(): lax.ppermute(block, 'latent', [(i, i ^ 2 * distance) for i in range(size)])  25.3 us
    ppermute x19, waiting for transfers between devices, to_chip(): lax.ppermute(block, 'latent', [(i, i ^ 2 * distance) for i in range(size)])  17.4 us
    pallas_call x1, Pallas kernels, update(): pl.pallas_call(functools.partial(update_kernel, columns, float(total_rows...  3.26 us
    ppermute x7, waiting for transfers between devices, to_other_core(): return lax.ppermute(block, 'latent', [(i, i ^ 1) for i in range(size)])  2.2 us
    unnamed x35, local copies, waits for them, and re-layouts  1.39 us
    ppermute x7, starting transfers between devices, to_other_core(): return lax.ppermute(block, 'latent', [(i, i ^ 1) for i in range(size)])  1.23 us
  transfers between devices with their start and end apart: 26, of which 15 were waited for; matrix products, arithmetic and copies ran while one was open for 4% of the time, Pallas kernels for 2%

profile of v17, /device:TPU:0, one launch (start us, length us, event | category | flops | bytes accessed | tf_op | source)
XLA Modules:
  0.0 54.3 jit_solution(11773993131409736130)
XLA Ops:
  0.7 4.1 %collective-permute-start.3 = (bf16[16,2304]{1,0:T(8,128)(2,1)}, bf16[16,2304]{1,0:T(8,128)(2,1)S(1)}, u32[]{:S(2)}, u32[]{:S(2)}) collective-permute-start(bf16[16,2304]{1,0:T(8,128)(2,1)} %param.9), channel_id=1, source_target_pairs={{0,8},{1,9},{2,10},{3,11},{4,12},{5,13},{6,14},{7,15},{8,0},{9,1},... | collective-permute-start | bytes 221192 | tf_op jit(solution)/shard_map/ppermute | solution.py:146
  4.8 1.6 %collective-permute-start.1 = (bf16[16,2304]{1,0:T(8,128)(2,1)}, bf16[16,2304]{1,0:T(8,128)(2,1)S(1)}, u32[]{:S(2)}, u32[]{:S(2)}) collective-permute-start(bf16[16,2304]{1,0:T(8,128)(2,1)} %param.9), channel_id=1, source_target_pairs={{0,4},{1,5},{2,6},{3,7},{4,0},{5,1},{6,2},{7,3},{8,12},{9,13},{10,... | collective-permute-start | bytes 221192 | tf_op jit(solution)/shard_map/ppermute | solution.py:146
  6.4 1.5 %collective-permute-start = (bf16[16,2304]{1,0:T(8,128)(2,1)}, bf16[16,2304]{1,0:T(8,128)(2,1)S(1)}, u32[]{:S(2)}, u32[]{:S(2)}) collective-permute-start(bf16[16,2304]{1,0:T(8,128)(2,1)} %param.9), channel_id=1, source_target_pairs={{0,2},{1,3},{2,0},{3,1},{4,6},{5,7},{6,4},{7,5},{8,10},{9,11},{10,... | collective-permute-start | bytes 221192 | tf_op jit(solution)/shard_map/ppermute | solution.py:146
  8.1 1.1 %constant_dynamic-update-slice_fusion.9 = bf16[256,2304]{1,0:T(8,128)(2,1)S(1)} fusion(bf16[128,2304]{1,0:T(8,128)(2,1)} %refs_3_.1), kind=kLoop, calls=%fused_computation.37 | loop fusion | bytes 1179648
  10.0 1.0 %collective-permute-start.4 = (bf16[16,2304]{1,0:T(8,128)(2,1)S(1)}, bf16[16,2304]{1,0:T(8,128)(2,1)S(1)}, u32[]{:S(2)}, u32[]{:S(2)}) collective-permute-start(bf16[16,2304]{1,0:T(8,128)(2,1)S(1)} %collective-permute-done.3), channel_id=1, source_target_pairs={{0,2},{1,3},{2,0},{3,1},{4,6},{5,7},{6,4},{7,5},{8,10},{9,11},{10,... | collective-permute-start | bytes 221192 | tf_op jit(solution)/shard_map/ppermute | solution.py:146
  11.0 1.4 %collective-permute-start.2 = (bf16[16,2304]{1,0:T(8,128)(2,1)S(1)}, bf16[16,2304]{1,0:T(8,128)(2,1)S(1)}, u32[]{:S(2)}, u32[]{:S(2)}) collective-permute-start(bf16[16,2304]{1,0:T(8,128)(2,1)S(1)} %collective-permute-done.1), channel_id=1, source_target_pairs={{0,2},{1,3},{2,0},{3,1},{4,6},{5,7},{6,4},{7,5},{8,10},{9,11},{10,... | collective-permute-start | bytes 221192 | tf_op jit(solution)/shard_map/ppermute | solution.py:146
  12.4 1.8 %collective-permute-done.5 = bf16[16,2304]{1,0:T(8,128)(2,1)S(1)} collective-permute-done((bf16[16,2304]{1,0:T(8,128)(2,1)}, bf16[16,2304]{1,0:T(8,128)(2,1)S(1)}, u32[]{:S(2)}, u32[]{:S(2)}) %collective-permute-start.5) | collective-permute-done | bytes 73760 | tf_op jit(solution)/shard_map/ppermute | solution.py:146
  14.8 1.9 %collective-permute-done.2 = bf16[16,2304]{1,0:T(8,128)(2,1)S(1)} collective-permute-done((bf16[16,2304]{1,0:T(8,128)(2,1)S(1)}, bf16[16,2304]{1,0:T(8,128)(2,1)S(1)}, u32[]{:S(2)}, u32[]{:S(2)}) %collective-permute-start.2) | collective-permute-done | bytes 73760 | tf_op jit(solution)/shard_map/ppermute | solution.py:146
  16.7 1.9 %collective-permute-done.6 = bf16[16,2304]{1,0:T(8,128)(2,1)S(1)} collective-permute-done((bf16[16,2304]{1,0:T(8,128)(2,1)S(1)}, bf16[16,2304]{1,0:T(8,128)(2,1)S(1)}, u32[]{:S(2)}, u32[]{:S(2)}) %collective-permute-start.6) | collective-permute-done | bytes 73760 | tf_op jit(solution)/shard_map/ppermute | solution.py:146
  20.1 0.6 %collective-permute-start.14 = (bf16[32,2304]{1,0:T(8,128)(2,1)S(1)}, bf16[32,2304]{1,0:T(8,128)(2,1)S(1)}, u32[]{:S(2)}, u32[]{:S(2)}) collective-permute-start(bf16[32,2304]{1,0:T(8,128)(2,1)S(1)} %pad_maximum_fusion.3), channel_id=1, source_target_pairs={{0,2},{1,3},{2,0},{3,1},{4,6},{5,7},{6,4},{7,5},{8,10},{9,11},{10,... | collective-permute-start | bytes 442376 | tf_op jit(solution)/shard_map/ppermute | solution.py:146
  20.7 0.5 collective-permute-start.11
  21.2 0.7 %collective-permute-done.10 = bf16[128,128]{0,1:T(8,128)(2,1)S(1)} collective-permute-done((bf16[128,128]{0,1:T(8,128)(2,1)S(1)}, bf16[128,128]{0,1:T(8,128)(2,1)S(1)}, u32[]{:S(2)}, u32[]{:S(2)}) %collective-permute-start.10) | collective-permute-done | bytes 32800 | tf_op jit(solution)/shard_map/ppermute | solution.py:153
  21.9 0.9 %collective-permute-done.11.centered = bf16[128,2304]{1,0:T(8,128)(2,1)S(1)} collective-permute-done((bf16[128,2304]{1,0:T(8,128)(2,1)S(1)}, bf16[128,2304]{1,0:T(8,128)(2,1)S(1)}, u32[]{:S(2)}, u32[]{:S(2)}) %collective-permute-start.11) | collective-permute-done | bytes 589856 | tf_op jit(solution)/shard_map/ppermute | solution.py:153
  22.8 1.5 %collective-permute-start.12 = (bf16[32,2304]{1,0:T(8,128)(2,1)S(1)}, bf16[32,2304]{1,0:T(8,128)(2,1)S(1)}, u32[]{:S(2)}, u32[]{:S(2)}) collective-permute-start(bf16[32,2304]{1,0:T(8,128)(2,1)S(1)} %pad_maximum_fusion.2), channel_id=1, source_target_pairs={{0,2},{1,3},{2,0},{3,1},{4,6},{5,7},{6,4},{7,5},{8,10},{9,11},{10,... | collective-permute-start | bytes 442376 | tf_op jit(solution)/shard_map/ppermute | solution.py:146
  24.4 1.0 %collective-permute-done.14 = bf16[32,2304]{1,0:T(8,128)(2,1)S(1)} collective-permute-done((bf16[32,2304]{1,0:T(8,128)(2,1)S(1)}, bf16[32,2304]{1,0:T(8,128)(2,1)S(1)}, u32[]{:S(2)}, u32[]{:S(2)}) %collective-permute-start.14) | collective-permute-done | bytes 147488 | tf_op jit(solution)/shard_map/ppermute | solution.py:146
  25.4 1.2 %collective-permute-start.15 = (bf16[16,2304]{1,0:T(8,128)(2,1)S(1)}, bf16[16,2304]{1,0:T(8,128)(2,1)S(1)}, u32[]{:S(2)}, u32[]{:S(2)}) collective-permute-start(bf16[16,2304]{1,0:T(8,128)(2,1)S(1)} %get-tuple-element.33), channel_id=1, source_target_pairs={{0,8},{1,9},{2,10},{3,11},{4,12},{5,13},{6,14},{7,15},{8,0},{9,1},... | collective-permute-start | bytes 221192 | tf_op jit(solution)/shard_map/ppermute | solution.py:146
  26.6 2.0 %collective-permute-start.16 = (bf16[16,2304]{1,0:T(8,128)(2,1)S(1)}, bf16[16,2304]{1,0:T(8,128)(2,1)S(1)}, u32[]{:S(2)}, u32[]{:S(2)}) collective-permute-start(bf16[16,2304]{1,0:T(8,128)(2,1)S(1)} %get-tuple-element.34), channel_id=1, source_target_pairs={{0,12},{1,13},{2,14},{3,15},{4,8},{5,9},{6,10},{7,11},{8,4},{9,5},... | collective-permute-start | bytes 221192 | tf_op jit(solution)/shard_map/ppermute | solution.py:146
  29.0 0.8 %collective-permute-start.13 = (bf16[16,2304]{1,0:T(8,128)(2,1)S(1)}, bf16[16,2304]{1,0:T(8,128)(2,1)S(1)}, u32[]{:S(2)}, u32[]{:S(2)}) collective-permute-start(bf16[16,2304]{1,0:T(8,128)(2,1)S(1)} %fusion.15), channel_id=1, source_target_pairs={{0,4},{1,5},{2,6},{3,7},{4,0},{5,1},{6,2},{7,3},{8,12},{9,13},{10,... | collective-permute-start | bytes 221192 | tf_op jit(solution)/shard_map/ppermute | solution.py:146
  29.8 3.8 %collective-permute-done.15 = bf16[16,2304]{1,0:T(8,128)(2,1)S(1)} collective-permute-done((bf16[16,2304]{1,0:T(8,128)(2,1)S(1)}, bf16[16,2304]{1,0:T(8,128)(2,1)S(1)}, u32[]{:S(2)}, u32[]{:S(2)}) %collective-permute-start.15) | collective-permute-done | bytes 73760 | tf_op jit(solution)/shard_map/ppermute | solution.py:146
  33.6 0.8 %collective-permute-done.13 = bf16[16,2304]{1,0:T(8,128)(2,1)S(1)} collective-permute-done((bf16[16,2304]{1,0:T(8,128)(2,1)S(1)}, bf16[16,2304]{1,0:T(8,128)(2,1)S(1)}, u32[]{:S(2)}, u32[]{:S(2)}) %collective-permute-start.13) | collective-permute-done | bytes 73760 | tf_op jit(solution)/shard_map/ppermute | solution.py:146
  34.4 2.9 %collective-permute-start.23 = (bf16[16,2304]{1,0:T(8,128)(2,1)S(1)}, bf16[16,2304]{1,0:T(8,128)(2,1)S(1)}, u32[]{:S(2)}, u32[]{:S(2)}) collective-permute-start(bf16[16,2304]{1,0:T(8,128)(2,1)S(1)} %fusion.20), channel_id=1, source_target_pairs={{0,12},{1,13},{2,14},{3,15},{4,8},{5,9},{6,10},{7,11},{8,4},{9,5},... | collective-permute-start | bytes 221192 | tf_op jit(solution)/shard_map/ppermute | solution.py:146
  37.3 1.6 %collective-permute-start.18 = (bf16[16,2304]{1,0:T(8,128)(2,1)S(1)}, bf16[16,2304]{1,0:T(8,128)(2,1)S(1)}, u32[]{:S(2)}, u32[]{:S(2)}) collective-permute-start(bf16[16,2304]{1,0:T(8,128)(2,1)S(1)} %fusion.20), channel_id=1, source_target_pairs={{0,4},{1,5},{2,6},{3,7},{4,0},{5,1},{6,2},{7,3},{8,12},{9,13},{10,... | collective-permute-start | bytes 221192 | tf_op jit(solution)/shard_map/ppermute | solution.py:146
  38.9 1.1 %collective-permute-start.17 = (bf16[16,2304]{1,0:T(8,128)(2,1)S(1)}, bf16[16,2304]{1,0:T(8,128)(2,1)S(1)}, u32[]{:S(2)}, u32[]{:S(2)}) collective-permute-start(bf16[16,2304]{1,0:T(8,128)(2,1)S(1)} %fusion.20), channel_id=1, source_target_pairs={{0,2},{1,3},{2,0},{3,1},{4,6},{5,7},{6,4},{7,5},{8,10},{9,11},{10,... | collective-permute-start | bytes 221192 | tf_op jit(solution)/shard_map/ppermute | solution.py:146
  40.0 1.1 %collective-permute-done.23 = bf16[16,2304]{1,0:T(8,128)(2,1)S(1)} collective-permute-done((bf16[16,2304]{1,0:T(8,128)(2,1)S(1)}, bf16[16,2304]{1,0:T(8,128)(2,1)S(1)}, u32[]{:S(2)}, u32[]{:S(2)}) %collective-permute-start.23) | collective-permute-done | bytes 73760 | tf_op jit(solution)/shard_map/ppermute | solution.py:146
  41.1 1.2 %collective-permute-start.24 = (bf16[16,2304]{1,0:T(8,128)(2,1)S(1)}, bf16[16,2304]{1,0:T(8,128)(2,1)S(1)}, u32[]{:S(2)}, u32[]{:S(2)}) collective-permute-start(bf16[16,2304]{1,0:T(8,128)(2,1)S(1)} %collective-permute-done.23), channel_id=1, source_target_pairs={{0,2},{1,3},{2,0},{3,1},{4,6},{5,7},{6,4},{7,5},{8,10},{9,11},{10,... | collective-permute-start | bytes 221192 | tf_op jit(solution)/shard_map/ppermute | solution.py:146
  42.3 1.3 %collective-permute-done.21 = bf16[16,2304]{1,0:T(8,128)(2,1)S(1)} collective-permute-done((bf16[16,2304]{1,0:T(8,128)(2,1)S(1)}, bf16[16,2304]{1,0:T(8,128)(2,1)S(1)}, u32[]{:S(2)}, u32[]{:S(2)}) %collective-permute-start.21) | collective-permute-done | bytes 73760 | tf_op jit(solution)/shard_map/ppermute | solution.py:146
  43.6 1.0 %collective-permute-start.22 = (bf16[16,2304]{1,0:T(8,128)(2,1)S(1)}, bf16[16,2304]{1,0:T(8,128)(2,1)S(1)}, u32[]{:S(2)}, u32[]{:S(2)}) collective-permute-start(bf16[16,2304]{1,0:T(8,128)(2,1)S(1)} %collective-permute-done.21), channel_id=1, source_target_pairs={{0,2},{1,3},{2,0},{3,1},{4,6},{5,7},{6,4},{7,5},{8,10},{9,11},{10,... | collective-permute-start | bytes 221192 | tf_op jit(solution)/shard_map/ppermute | solution.py:146
  44.5 1.1 %collective-permute-start.19 = (bf16[16,2304]{1,0:T(8,128)(2,1)S(1)}, bf16[16,2304]{1,0:T(8,128)(2,1)S(1)}, u32[]{:S(2)}, u32[]{:S(2)}) collective-permute-start(bf16[16,2304]{1,0:T(8,128)(2,1)S(1)} %collective-permute-done.18), channel_id=1, source_target_pairs={{0,2},{1,3},{2,0},{3,1},{4,6},{5,7},{6,4},{7,5},{8,10},{9,11},{10,... | collective-permute-start | bytes 221192 | tf_op jit(solution)/shard_map/ppermute | solution.py:146
  45.7 2.8 %collective-permute-done.22 = bf16[16,2304]{1,0:T(8,128)(2,1)S(1)} collective-permute-done((bf16[16,2304]{1,0:T(8,128)(2,1)S(1)}, bf16[16,2304]{1,0:T(8,128)(2,1)S(1)}, u32[]{:S(2)}, u32[]{:S(2)}) %collective-permute-start.22) | collective-permute-done | bytes 73760 | tf_op jit(solution)/shard_map/ppermute | solution.py:146
  48.6 0.7 %collective-permute-done.19 = bf16[16,2304]{1,0:T(8,128)(2,1)S(1)} collective-permute-done((bf16[16,2304]{1,0:T(8,128)(2,1)S(1)}, bf16[16,2304]{1,0:T(8,128)(2,1)S(1)}, u32[]{:S(2)}, u32[]{:S(2)}) %collective-permute-start.19) | collective-permute-done | bytes 73760 | tf_op jit(solution)/shard_map/ppermute | solution.py:146
  49.5 1.0 %own_totals.1 = (f32[128,2304]{1,0:T(8,128)S(1)}, f32[128,2304]{1,0:T(8,128)S(1)}) custom-call(bf16[128,128]{1,0:T(8,128)(2,1)S(1)} %get-tuple-element.39.codes_across, bf16[128,2304]{1,0:T(8,128)(2,1)S(1)} %subtract_convert_fusion.centered, bf16[128,2304]{1,0:T(8,128)(2,1)S(1)} %constant_dynamic-update-slice_fusion.10.errors, bf16[128,2304]{1,0:T(8,128)(2,1)S(1)} %copy-done), custom_call_target="tpu_custom_call" | custom-call | flops 226492416 | bytes 4718592 | tf_op jit(solution)/shard_map/own_totals/pallas_call | solution.py:41
  51.1 3.3 %update.1 = (bf16[128,2304]{1,0:T(8,128)(2,1)}, f32[128,2304]{1,0:T(8,128)}, f32[128,2304]{1,0:T(8,128)}, bf16[128,2304]{1,0:T(8,128)(2,1)}, f32[128,2304]{1,0:T(8,128)}, /*index=5*/f32[128,2304]{1,0:T(8,128)}) custom-call(bf16[128,128]{1,0:T(8,128)(2,1)S(1)} %bitcast.6, bf16[128,2304]{1,0:T(8,128)(2,1)S(1)} %collective-permute-done.11.centered, ...), custom_call_target="tpu_custom_call" | custom-call | flops 226492416 | bytes 12976128 | tf_op jit(solution)/shard_map/update/pallas_call | solution.py:119
  (75 shorter events, 4.4 us)
Async XLA Ops:
  0.6 9.2 %copy-start.9 = (f32[128]{0:T(128)S(1)}, f32[128]{0:T(128)}, u32[]{:S(2)}) copy-start(f32[128]{0:T(128)} %param.11) | copy-start | bytes 1540
  0.7 8.7 %copy-start = (bf16[128,2304]{1,0:T(8,128)(2,1)S(1)}, bf16[128,2304]{1,0:T(8,128)(2,1)}, u32[]{:S(2)}) copy-start(bf16[128,2304]{1,0:T(8,128)(2,1)} %refs_3_.1) | copy-start | bytes 1769476
  0.7 9.2 %copy-start.5 = (bf16[128,2304]{1,0:T(8,128)(2,1)S(1)}, bf16[128,2304]{1,0:T(8,128)(2,1)}, u32[]{:S(2)}) copy-start(bf16[128,2304]{1,0:T(8,128)(2,1)} %refs_2_.1) | copy-start | bytes 1769476
  0.7 17.9 %copy-start.8 = (f32[2304]{0:T(1024)S(1)}, f32[2304]{0:T(1024)}, u32[]{:S(2)}) copy-start(f32[2304]{0:T(1024)} %param.13) | copy-start | bytes 27652
  0.7 9.2 %collective-permute-start.3 = (bf16[16,2304]{1,0:T(8,128)(2,1)}, bf16[16,2304]{1,0:T(8,128)(2,1)S(1)}, u32[]{:S(2)}, u32[]{:S(2)}) collective-permute-start(bf16[16,2304]{1,0:T(8,128)(2,1)} %param.9), channel_id=1, source_target_pairs={{0,8},{1,9},{2,10},{3,11},{4,12},{5,13},{6,14},{7,15},{8,0},{9,1},... | collective-permute-start | bytes 221192 | tf_op jit(solution)/shard_map/ppermute | solution.py:146
  4.8 5.2 %collective-permute-start.1 = (bf16[16,2304]{1,0:T(8,128)(2,1)}, bf16[16,2304]{1,0:T(8,128)(2,1)S(1)}, u32[]{:S(2)}, u32[]{:S(2)}) collective-permute-start(bf16[16,2304]{1,0:T(8,128)(2,1)} %param.9), channel_id=1, source_target_pairs={{0,4},{1,5},{2,6},{3,7},{4,0},{5,1},{6,2},{7,3},{8,12},{9,13},{10,... | collective-permute-start | bytes 221192 | tf_op jit(solution)/shard_map/ppermute | solution.py:146
  6.4 4.7 %collective-permute-start = (bf16[16,2304]{1,0:T(8,128)(2,1)}, bf16[16,2304]{1,0:T(8,128)(2,1)S(1)}, u32[]{:S(2)}, u32[]{:S(2)}) collective-permute-start(bf16[16,2304]{1,0:T(8,128)(2,1)} %param.9), channel_id=1, source_target_pairs={{0,2},{1,3},{2,0},{3,1},{4,6},{5,7},{6,4},{7,5},{8,10},{9,11},{10,... | collective-permute-start | bytes 221192 | tf_op jit(solution)/shard_map/ppermute | solution.py:146
  7.9 6.4 %collective-permute-start.5 = (bf16[16,2304]{1,0:T(8,128)(2,1)}, bf16[16,2304]{1,0:T(8,128)(2,1)S(1)}, u32[]{:S(2)}, u32[]{:S(2)}) collective-permute-start(bf16[16,2304]{1,0:T(8,128)(2,1)} %param.9), channel_id=1, source_target_pairs={{0,12},{1,13},{2,14},{3,15},{4,8},{5,9},{6,10},{7,11},{8,4},{9,5},... | collective-permute-start | bytes 221192 | tf_op jit(solution)/shard_map/ppermute | solution.py:146
  8.1 1.3 %collective-permute-start.8 = (f32[128]{0:T(128)}, f32[128]{0:T(128)S(1)}, u32[]{:S(2)}, u32[]{:S(2)}) collective-permute-start(f32[128]{0:T(128)} %param.11), channel_id=1, source_target_pairs={{0,1},{1,0},{2,3},{3,2},{4,5},{5,4},{6,7},{7,6},{8,9},{9,8},{10,11... | collective-permute-start | bytes 1544 | tf_op jit(solution)/shard_map/ppermute | solution.py:153
  9.4 9.9 %collective-permute-start.9 = (bf16[128,2304]{1,0:T(8,128)(2,1)S(1)}, bf16[128,2304]{1,0:T(8,128)(2,1)S(1)}, u32[]{:S(2)}, u32[]{:S(2)}) collective-permute-start(bf16[128,2304]{1,0:T(8,128)(2,1)S(1)} %copy-done), channel_id=1, source_target_pairs={{0,1},{1,0},{2,3},{3,2},{4,5},{5,4},{6,7},{7,6},{8,9},{9,8},{10,11... | collective-permute-start | bytes 1769480 | tf_op jit(solution)/shard_map/ppermute | solution.py:153
  9.9 8.9 %collective-permute-start.7 = (bf16[128,2304]{1,0:T(8,128)(2,1)S(1)}, bf16[128,2304]{1,0:T(8,128)(2,1)S(1)}, u32[]{:S(2)}, u32[]{:S(2)}) collective-permute-start(bf16[128,2304]{1,0:T(8,128)(2,1)S(1)} %copy-done.5), channel_id=1, source_target_pairs={{0,1},{1,0},{2,3},{3,2},{4,5},{5,4},{6,7},{7,6},{8,9},{9,8},{10,11... | collective-permute-start | bytes 1769480 | tf_op jit(solution)/shard_map/ppermute | solution.py:153
  10.0 6.7 %collective-permute-start.4 = (bf16[16,2304]{1,0:T(8,128)(2,1)S(1)}, bf16[16,2304]{1,0:T(8,128)(2,1)S(1)}, u32[]{:S(2)}, u32[]{:S(2)}) collective-permute-start(bf16[16,2304]{1,0:T(8,128)(2,1)S(1)} %collective-permute-done.3), channel_id=1, source_target_pairs={{0,2},{1,3},{2,0},{3,1},{4,6},{5,7},{6,4},{7,5},{8,10},{9,11},{10,... | collective-permute-start | bytes 221192 | tf_op jit(solution)/shard_map/ppermute | solution.py:146
  11.0 5.7 %collective-permute-start.2 = (bf16[16,2304]{1,0:T(8,128)(2,1)S(1)}, bf16[16,2304]{1,0:T(8,128)(2,1)S(1)}, u32[]{:S(2)}, u32[]{:S(2)}) collective-permute-start(bf16[16,2304]{1,0:T(8,128)(2,1)S(1)} %collective-permute-done.1), channel_id=1, source_target_pairs={{0,2},{1,3},{2,0},{3,1},{4,6},{5,7},{6,4},{7,5},{8,10},{9,11},{10,... | collective-permute-start | bytes 221192 | tf_op jit(solution)/shard_map/ppermute | solution.py:146
  14.2 4.4 %collective-permute-start.6 = (bf16[16,2304]{1,0:T(8,128)(2,1)S(1)}, bf16[16,2304]{1,0:T(8,128)(2,1)S(1)}, u32[]{:S(2)}, u32[]{:S(2)}) collective-permute-start(bf16[16,2304]{1,0:T(8,128)(2,1)S(1)} %collective-permute-done.5), channel_id=1, source_target_pairs={{0,2},{1,3},{2,0},{3,1},{4,6},{5,7},{6,4},{7,5},{8,10},{9,11},{10,... | collective-permute-start | bytes 221192 | tf_op jit(solution)/shard_map/ppermute | solution.py:146
  20.1 5.2 %collective-permute-start.14 = (bf16[32,2304]{1,0:T(8,128)(2,1)S(1)}, bf16[32,2304]{1,0:T(8,128)(2,1)S(1)}, u32[]{:S(2)}, u32[]{:S(2)}) collective-permute-start(bf16[32,2304]{1,0:T(8,128)(2,1)S(1)} %pad_maximum_fusion.3), channel_id=1, source_target_pairs={{0,2},{1,3},{2,0},{3,1},{4,6},{5,7},{6,4},{7,5},{8,10},{9,11},{10,... | collective-permute-start | bytes 442376 | tf_op jit(solution)/shard_map/ppermute | solution.py:146
  20.7 1.2 %collective-permute-start.10 = (bf16[128,128]{0,1:T(8,128)(2,1)S(1)}, bf16[128,128]{0,1:T(8,128)(2,1)S(1)}, u32[]{:S(2)}, u32[]{:S(2)}) collective-permute-start(bf16[128,128]{0,1:T(8,128)(2,1)S(1)} %get-tuple-element.40), channel_id=1, source_target_pairs={{0,1},{1,0},{2,3},{3,2},{4,5},{5,4},{6,7},{7,6},{8,9},{9,8},{10,11... | collective-permute-start | bytes 98312 | tf_op jit(solution)/shard_map/ppermute | solution.py:153
  20.7 2.1 %collective-permute-start.11 = (bf16[128,2304]{1,0:T(8,128)(2,1)S(1)}, bf16[128,2304]{1,0:T(8,128)(2,1)S(1)}, u32[]{:S(2)}, u32[]{:S(2)}) collective-permute-start(bf16[128,2304]{1,0:T(8,128)(2,1)S(1)} %subtract_convert_fusion.centered), channel_id=1, source_target_pairs={{0,1},{1,0},{2,3},{3,2},{4,5},{5,4},{6,7},{7,6},{8,9},{9,8},{10,11... | collective-permute-start | bytes 1769480 | tf_op jit(solution)/shard_map/ppermute | solution.py:153
  22.8 6.1 %collective-permute-start.12 = (bf16[32,2304]{1,0:T(8,128)(2,1)S(1)}, bf16[32,2304]{1,0:T(8,128)(2,1)S(1)}, u32[]{:S(2)}, u32[]{:S(2)}) collective-permute-start(bf16[32,2304]{1,0:T(8,128)(2,1)S(1)} %pad_maximum_fusion.2), channel_id=1, source_target_pairs={{0,2},{1,3},{2,0},{3,1},{4,6},{5,7},{6,4},{7,5},{8,10},{9,11},{10,... | collective-permute-start | bytes 442376 | tf_op jit(solution)/shard_map/ppermute | solution.py:146
  25.4 8.2 %collective-permute-start.15 = (bf16[16,2304]{1,0:T(8,128)(2,1)S(1)}, bf16[16,2304]{1,0:T(8,128)(2,1)S(1)}, u32[]{:S(2)}, u32[]{:S(2)}) collective-permute-start(bf16[16,2304]{1,0:T(8,128)(2,1)S(1)} %get-tuple-element.33), channel_id=1, source_target_pairs={{0,8},{1,9},{2,10},{3,11},{4,12},{5,13},{6,14},{7,15},{8,0},{9,1},... | collective-permute-start | bytes 221192 | tf_op jit(solution)/shard_map/ppermute | solution.py:146
  26.6 7.0 %collective-permute-start.16 = (bf16[16,2304]{1,0:T(8,128)(2,1)S(1)}, bf16[16,2304]{1,0:T(8,128)(2,1)S(1)}, u32[]{:S(2)}, u32[]{:S(2)}) collective-permute-start(bf16[16,2304]{1,0:T(8,128)(2,1)S(1)} %get-tuple-element.34), channel_id=1, source_target_pairs={{0,12},{1,13},{2,14},{3,15},{4,8},{5,9},{6,10},{7,11},{8,4},{9,5},... | collective-permute-start | bytes 221192 | tf_op jit(solution)/shard_map/ppermute | solution.py:146
  29.0 5.4 %collective-permute-start.13 = (bf16[16,2304]{1,0:T(8,128)(2,1)S(1)}, bf16[16,2304]{1,0:T(8,128)(2,1)S(1)}, u32[]{:S(2)}, u32[]{:S(2)}) collective-permute-start(bf16[16,2304]{1,0:T(8,128)(2,1)S(1)} %fusion.15), channel_id=1, source_target_pairs={{0,4},{1,5},{2,6},{3,7},{4,0},{5,1},{6,2},{7,3},{8,12},{9,13},{10,... | collective-permute-start | bytes 221192 | tf_op jit(solution)/shard_map/ppermute | solution.py:146
  34.4 16.6 %copy-start.4 = (f32[128,2304]{1,0:T(8,128)S(1)}, f32[128,2304]{1,0:T(8,128)}, u32[]{:S(2)}) copy-start(f32[128,2304]{1,0:T(8,128)} %refs_7_.1) | copy-start | bytes 3538948
  34.4 15.0 %copy-start.6 = (bf16[16,2304]{1,0:T(8,128)(2,1)}, bf16[16,2304]{1,0:T(8,128)(2,1)S(1)}, u32[]{:S(2)}) copy-start(bf16[16,2304]{1,0:T(8,128)(2,1)S(1)} %fusion.20) | copy-start | bytes 221188
  34.4 6.7 %collective-permute-start.23 = (bf16[16,2304]{1,0:T(8,128)(2,1)S(1)}, bf16[16,2304]{1,0:T(8,128)(2,1)S(1)}, u32[]{:S(2)}, u32[]{:S(2)}) collective-permute-start(bf16[16,2304]{1,0:T(8,128)(2,1)S(1)} %fusion.20), channel_id=1, source_target_pairs={{0,12},{1,13},{2,14},{3,15},{4,8},{5,9},{6,10},{7,11},{8,4},{9,5},... | collective-permute-start | bytes 221192 | tf_op jit(solution)/shard_map/ppermute | solution.py:146
  37.3 6.3 %collective-permute-start.21 = (bf16[16,2304]{1,0:T(8,128)(2,1)S(1)}, bf16[16,2304]{1,0:T(8,128)(2,1)S(1)}, u32[]{:S(2)}, u32[]{:S(2)}) collective-permute-start(bf16[16,2304]{1,0:T(8,128)(2,1)S(1)} %fusion.20), channel_id=1, source_target_pairs={{0,8},{1,9},{2,10},{3,11},{4,12},{5,13},{6,14},{7,15},{8,0},{9,1},... | collective-permute-start | bytes 221192 | tf_op jit(solution)/shard_map/ppermute | solution.py:146
  37.3 7.2 %collective-permute-start.18 = (bf16[16,2304]{1,0:T(8,128)(2,1)S(1)}, bf16[16,2304]{1,0:T(8,128)(2,1)S(1)}, u32[]{:S(2)}, u32[]{:S(2)}) collective-permute-start(bf16[16,2304]{1,0:T(8,128)(2,1)S(1)} %fusion.20), channel_id=1, source_target_pairs={{0,4},{1,5},{2,6},{3,7},{4,0},{5,1},{6,2},{7,3},{8,12},{9,13},{10,... | collective-permute-start | bytes 221192 | tf_op jit(solution)/shard_map/ppermute | solution.py:146
  38.9 6.7 %collective-permute-start.17 = (bf16[16,2304]{1,0:T(8,128)(2,1)S(1)}, bf16[16,2304]{1,0:T(8,128)(2,1)S(1)}, u32[]{:S(2)}, u32[]{:S(2)}) collective-permute-start(bf16[16,2304]{1,0:T(8,128)(2,1)S(1)} %fusion.20), channel_id=1, source_target_pairs={{0,2},{1,3},{2,0},{3,1},{4,6},{5,7},{6,4},{7,5},{8,10},{9,11},{10,... | collective-permute-start | bytes 221192 | tf_op jit(solution)/shard_map/ppermute | solution.py:146
  41.1 4.5 %collective-permute-start.24 = (bf16[16,2304]{1,0:T(8,128)(2,1)S(1)}, bf16[16,2304]{1,0:T(8,128)(2,1)S(1)}, u32[]{:S(2)}, u32[]{:S(2)}) collective-permute-start(bf16[16,2304]{1,0:T(8,128)(2,1)S(1)} %collective-permute-done.23), channel_id=1, source_target_pairs={{0,2},{1,3},{2,0},{3,1},{4,6},{5,7},{6,4},{7,5},{8,10},{9,11},{10,... | collective-permute-start | bytes 221192 | tf_op jit(solution)/shard_map/ppermute | solution.py:146
  43.6 4.9 %collective-permute-start.22 = (bf16[16,2304]{1,0:T(8,128)(2,1)S(1)}, bf16[16,2304]{1,0:T(8,128)(2,1)S(1)}, u32[]{:S(2)}, u32[]{:S(2)}) collective-permute-start(bf16[16,2304]{1,0:T(8,128)(2,1)S(1)} %collective-permute-done.21), channel_id=1, source_target_pairs={{0,2},{1,3},{2,0},{3,1},{4,6},{5,7},{6,4},{7,5},{8,10},{9,11},{10,... | collective-permute-start | bytes 221192 | tf_op jit(solution)/shard_map/ppermute | solution.py:146
  44.5 4.7 %collective-permute-start.19 = (bf16[16,2304]{1,0:T(8,128)(2,1)S(1)}, bf16[16,2304]{1,0:T(8,128)(2,1)S(1)}, u32[]{:S(2)}, u32[]{:S(2)}) collective-permute-start(bf16[16,2304]{1,0:T(8,128)(2,1)S(1)} %collective-permute-done.18), channel_id=1, source_target_pairs={{0,2},{1,3},{2,0},{3,1},{4,6},{5,7},{6,4},{7,5},{8,10},{9,11},{10,... | collective-permute-start | bytes 221192 | tf_op jit(solution)/shard_map/ppermute | solution.py:146
  48.5 2.0 %collective-permute-start.25 = (bf16[64,2304]{1,0:T(8,128)(2,1)S(1)}, bf16[64,2304]{1,0:T(8,128)(2,1)S(1)}, u32[]{:S(2)}, u32[]{:S(2)}) collective-permute-start(bf16[64,2304]{1,0:T(8,128)(2,1)S(1)} %pad_maximum_fusion.1), channel_id=1, source_target_pairs={{0,1},{1,0},{2,3},{3,2},{4,5},{5,4},{6,7},{7,6},{8,9},{9,8},{10,11... | collective-permute-start | bytes 884744 | tf_op jit(solution)/shard_map/ppermute | solution.py:153
  49.3 1.6 %collective-permute-start.20 = (bf16[64,2304]{1,0:T(8,128)(2,1)S(1)}, bf16[64,2304]{1,0:T(8,128)(2,1)S(1)}, u32[]{:S(2)}, u32[]{:S(2)}) collective-permute-start(bf16[64,2304]{1,0:T(8,128)(2,1)S(1)} %pad_maximum_fusion), channel_id=1, source_target_pairs={{0,1},{1,0},{2,3},{3,2},{4,5},{5,4},{6,7},{7,6},{8,9},{9,8},{10,11... | collective-permute-start | bytes 884744 | tf_op jit(solution)/shard_map/ppermute | solution.py:153
  (4 other events, 14.3 us)

commit v18 on v17

--- a/solution.py
+++ b/solution.py
@@ -87,10 +87,11 @@
                 grad = totals[which][some] + total[start : start + part]
                 moment = beta_first * moments[2 * which][some] + first * grad
                 square = beta_second * moments[2 * which + 1][some] + second * (grad * grad)
-                root = square * lax.rsqrt(square)
+                guess = lax.rsqrt(square)
+                root = square * guess
+                inverse = guess * (2.0 - (root + adam_epsilon) * guess)
                 held[3 * which][some] = (
-                    weight[some].astype(jnp.float32)
-                    - step_rate * moment * pl.reciprocal(root + adam_epsilon, approx=True)
+                    weight[some].astype(jnp.float32) - step_rate * moment * inverse
                 ).astype(jnp.bfloat16)
                 held[3 * which + 1][some] = moment
                 held[3 * which + 2][some] = square
@@ -191,27 +192,27 @@
     other_codes = to_other_core(codes[:, latents_here:])
 
     quad = 4 * rows_here
-    parts = []
-    for rows in (slice(0, quad), slice(quad, None)):
-        sums = jnp.dot(codes[rows], decoder_both, preferred_element_type=jnp.float32)
-        parts += [sums[at : at + rows_here] for at in range(0, sums.shape[0], rows_here)]
-
-    def given(first, last):
-        return jnp.concatenate(parts[first + 1 : last : 2], 0).astype(jnp.bfloat16)
-
-    def pair_sums(first, last, sent):
+
+    def partial_sums(some_codes):
+        sums = jnp.dot(some_codes, decoder_both, preferred_element_type=jnp.float32)
+        parts = [sums[at : at + rows_here] for at in range(0, sums.shape[0], rows_here)]
+        return parts, jnp.concatenate(parts[1::2], 0).astype(jnp.bfloat16)
+
+    def pair_sums(parts, sent):
         came = to_chip(sent, 1)
         return [
-            parts[k] + came[at * rows_here : (at + 1) * rows_here].astype(jnp.float32)
-            for at, k in enumerate(range(first, last, 2))
+            part + came[at * rows_here : (at + 1) * rows_here].astype(jnp.float32)
+            for at, part in enumerate(parts[::2])
         ]
 
-    far_sent = given(4, chips)
-    far = [one.astype(jnp.bfloat16) for one in pair_sums(4, chips, far_sent)]
+    far_parts, far_sent = partial_sums(codes[quad:])
+    far = [one.astype(jnp.bfloat16) for one in pair_sums(far_parts, far_sent)]
     later_centered, _ = lax.optimization_barrier((centered, far_sent))
     other_centered = to_other_core(later_centered)
-    near_sent, _ = lax.optimization_barrier((given(0, 4), (other_codes, other_centered)))
-    own, near = pair_sums(0, 4, near_sent)
+    near_codes, _ = lax.optimization_barrier((codes[:quad], other_codes))
+    near_parts, near_sent = partial_sums(near_codes)
+    near_sent, _ = lax.optimization_barrier((near_sent, other_centered))
+    own, near = pair_sums(near_parts, near_sent)
     summed = own + to_chip(near.astype(jnp.bfloat16), 2).astype(jnp.float32)
     for k, one in enumerate(far, 2):
         summed = summed + to_chip(one, 2 * k).astype(jnp.float32)

time: 54.5 us -> 56.2 us (1.031)
  waiting for transfers between devices: 19.6 us -> 23.4 us
  starting transfers between devices: 26.6 us -> 24.4 us
    ppermute x19, waiting for transfers between devices: 17.4 us -> 21.4 us  [to_chip(): lax.ppermute(block, 'latent', [(i, i ^ 2 * distance) for i in range(size)])]
    ppermute x19, starting transfers between devices: 25.3 us -> 23.4 us  [to_chip(): lax.ppermute(block, 'latent', [(i, i ^ 2 * distance) for i in range(size)])]
  transfers between devices with their start and end apart: 26 -> 26, of which waited for: 15 -> 14; matrix products, arithmetic and copies ran while one was open for 4% -> 5% of each run, Pallas kernels for 2% -> 2%
where the time goes in v18:
time: 56.2 us; the launch traced here: 56 us
  starting transfers between devices  24.4 us (43%)
  waiting for transfers between devices  23.4 us (42%)
  Pallas kernels  4.28 us (8%)
  local copies, waits for them, and re-layouts  1.47 us (3%)
  matrix products  1.26 us (2%)
  between operations  0.99 us (2%)
    ppermute x19, starting transfers between devices, to_chip(): lax.ppermute(block, 'latent', [(i, i ^ 2 * distance) for i in range(size)])  23.4 us
    ppermute x19, waiting for transfers between devices, to_chip(): lax.ppermute(block, 'latent', [(i, i ^ 2 * distance) for i in range(size)])  21.4 us
    pallas_call x1, Pallas kernels, update(): pl.pallas_call(functools.partial(update_kernel, columns, float(total_rows...  3.31 us
    ppermute x7, waiting for transfers between devices, to_other_core(): return lax.ppermute(block, 'latent', [(i, i ^ 1) for i in range(size)])  2.01 us
    unnamed x35, local copies, waits for them, and re-layouts  1.39 us
  transfers between devices with their start and end apart: 26, of which 14 were waited for; matrix products, arithmetic and copies ran while one was open for 5% of the time, Pallas kernels for 2%

profile of v18, /device:TPU:0, one launch (start us, length us, event | category | flops | bytes accessed | tf_op | source)
XLA Modules:
  0.0 56.0 jit_solution(16297149633107123712)
XLA Ops:
  0.7 4.1 %collective-permute-start.3 = (bf16[16,2304]{1,0:T(8,128)(2,1)}, bf16[16,2304]{1,0:T(8,128)(2,1)S(1)}, u32[]{:S(2)}, u32[]{:S(2)}) collective-permute-start(bf16[16,2304]{1,0:T(8,128)(2,1)} %param.9), channel_id=1, source_target_pairs={{0,8},{1,9},{2,10},{3,11},{4,12},{5,13},{6,14},{7,15},{8,0},{9,1},... | collective-permute-start | bytes 221192 | tf_op jit(solution)/shard_map/ppermute | solution.py:147
  4.8 1.6 %collective-permute-start.1 = (bf16[16,2304]{1,0:T(8,128)(2,1)}, bf16[16,2304]{1,0:T(8,128)(2,1)S(1)}, u32[]{:S(2)}, u32[]{:S(2)}) collective-permute-start(bf16[16,2304]{1,0:T(8,128)(2,1)} %param.9), channel_id=1, source_target_pairs={{0,4},{1,5},{2,6},{3,7},{4,0},{5,1},{6,2},{7,3},{8,12},{9,13},{10,... | collective-permute-start | bytes 221192 | tf_op jit(solution)/shard_map/ppermute | solution.py:147
  6.4 1.5 %collective-permute-start = (bf16[16,2304]{1,0:T(8,128)(2,1)}, bf16[16,2304]{1,0:T(8,128)(2,1)S(1)}, u32[]{:S(2)}, u32[]{:S(2)}) collective-permute-start(bf16[16,2304]{1,0:T(8,128)(2,1)} %param.9), channel_id=1, source_target_pairs={{0,2},{1,3},{2,0},{3,1},{4,6},{5,7},{6,4},{7,5},{8,10},{9,11},{10,... | collective-permute-start | bytes 221192 | tf_op jit(solution)/shard_map/ppermute | solution.py:147
  8.1 1.1 %constant_dynamic-update-slice_fusion.9 = bf16[256,2304]{1,0:T(8,128)(2,1)S(1)} fusion(bf16[128,2304]{1,0:T(8,128)(2,1)} %refs_3_.1), kind=kLoop, calls=%fused_computation.35 | loop fusion | bytes 1179648
  10.0 1.0 %collective-permute-start.4 = (bf16[16,2304]{1,0:T(8,128)(2,1)S(1)}, bf16[16,2304]{1,0:T(8,128)(2,1)S(1)}, u32[]{:S(2)}, u32[]{:S(2)}) collective-permute-start(bf16[16,2304]{1,0:T(8,128)(2,1)S(1)} %collective-permute-done.3), channel_id=1, source_target_pairs={{0,2},{1,3},{2,0},{3,1},{4,6},{5,7},{6,4},{7,5},{8,10},{9,11},{10,... | collective-permute-start | bytes 221192 | tf_op jit(solution)/shard_map/ppermute | solution.py:147
  11.0 1.4 %collective-permute-start.2 = (bf16[16,2304]{1,0:T(8,128)(2,1)S(1)}, bf16[16,2304]{1,0:T(8,128)(2,1)S(1)}, u32[]{:S(2)}, u32[]{:S(2)}) collective-permute-start(bf16[16,2304]{1,0:T(8,128)(2,1)S(1)} %collective-permute-done.1), channel_id=1, source_target_pairs={{0,2},{1,3},{2,0},{3,1},{4,6},{5,7},{6,4},{7,5},{8,10},{9,11},{10,... | collective-permute-start | bytes 221192 | tf_op jit(solution)/shard_map/ppermute | solution.py:147
  12.4 1.8 %collective-permute-done.5 = bf16[16,2304]{1,0:T(8,128)(2,1)S(1)} collective-permute-done((bf16[16,2304]{1,0:T(8,128)(2,1)}, bf16[16,2304]{1,0:T(8,128)(2,1)S(1)}, u32[]{:S(2)}, u32[]{:S(2)}) %collective-permute-start.5) | collective-permute-done | bytes 73760 | tf_op jit(solution)/shard_map/ppermute | solution.py:147
  14.2 0.5 collective-permute-start.6
  14.8 1.9 %collective-permute-done.2 = bf16[16,2304]{1,0:T(8,128)(2,1)S(1)} collective-permute-done((bf16[16,2304]{1,0:T(8,128)(2,1)S(1)}, bf16[16,2304]{1,0:T(8,128)(2,1)S(1)}, u32[]{:S(2)}, u32[]{:S(2)}) %collective-permute-start.2) | collective-permute-done | bytes 73760 | tf_op jit(solution)/shard_map/ppermute | solution.py:147
  16.7 1.9 %collective-permute-done.6 = bf16[16,2304]{1,0:T(8,128)(2,1)S(1)} collective-permute-done((bf16[16,2304]{1,0:T(8,128)(2,1)S(1)}, bf16[16,2304]{1,0:T(8,128)(2,1)S(1)}, u32[]{:S(2)}, u32[]{:S(2)}) %collective-permute-start.6) | collective-permute-done | bytes 73760 | tf_op jit(solution)/shard_map/ppermute | solution.py:147
  18.7 0.5 fusion.10
  19.8 0.6 %collective-permute-start.14 = (bf16[32,2304]{1,0:T(8,128)(2,1)S(1)}, bf16[32,2304]{1,0:T(8,128)(2,1)S(1)}, u32[]{:S(2)}, u32[]{:S(2)}) collective-permute-start(bf16[32,2304]{1,0:T(8,128)(2,1)S(1)} %pad_maximum_fusion.3), channel_id=1, source_target_pairs={{0,2},{1,3},{2,0},{3,1},{4,6},{5,7},{6,4},{7,5},{8,10},{9,11},{10,... | collective-permute-start | bytes 442376 | tf_op jit(solution)/shard_map/ppermute | solution.py:147
  21.0 1.4 %collective-permute-done.11.centered = bf16[128,2304]{1,0:T(8,128)(2,1)S(1)} collective-permute-done((bf16[128,2304]{1,0:T(8,128)(2,1)S(1)}, bf16[128,2304]{1,0:T(8,128)(2,1)S(1)}, u32[]{:S(2)}, u32[]{:S(2)}) %collective-permute-start.11) | collective-permute-done | bytes 589856 | tf_op jit(solution)/shard_map/ppermute | solution.py:154
  22.4 1.5 %collective-permute-start.12 = (bf16[32,2304]{1,0:T(8,128)(2,1)S(1)}, bf16[32,2304]{1,0:T(8,128)(2,1)S(1)}, u32[]{:S(2)}, u32[]{:S(2)}) collective-permute-start(bf16[32,2304]{1,0:T(8,128)(2,1)S(1)} %pad_maximum_fusion.2), channel_id=1, source_target_pairs={{0,2},{1,3},{2,0},{3,1},{4,6},{5,7},{6,4},{7,5},{8,10},{9,11},{10,... | collective-permute-start | bytes 442376 | tf_op jit(solution)/shard_map/ppermute | solution.py:147
  23.9 2.6 %collective-permute-done.14 = bf16[32,2304]{1,0:T(8,128)(2,1)S(1)} collective-permute-done((bf16[32,2304]{1,0:T(8,128)(2,1)S(1)}, bf16[32,2304]{1,0:T(8,128)(2,1)S(1)}, u32[]{:S(2)}, u32[]{:S(2)}) %collective-permute-start.14) | collective-permute-done | bytes 147488 | tf_op jit(solution)/shard_map/ppermute | solution.py:147
  26.6 0.9 %collective-permute-start.15 = (bf16[16,2304]{1,0:T(8,128)(2,1)S(1)}, bf16[16,2304]{1,0:T(8,128)(2,1)S(1)}, u32[]{:S(2)}, u32[]{:S(2)}) collective-permute-start(bf16[16,2304]{1,0:T(8,128)(2,1)S(1)} %get-tuple-element.35), channel_id=1, source_target_pairs={{0,8},{1,9},{2,10},{3,11},{4,12},{5,13},{6,14},{7,15},{8,0},{9,1},... | collective-permute-start | bytes 221192 | tf_op jit(solution)/shard_map/ppermute | solution.py:147
  27.4 1.7 %collective-permute-start.16 = (bf16[16,2304]{1,0:T(8,128)(2,1)S(1)}, bf16[16,2304]{1,0:T(8,128)(2,1)S(1)}, u32[]{:S(2)}, u32[]{:S(2)}) collective-permute-start(bf16[16,2304]{1,0:T(8,128)(2,1)S(1)} %get-tuple-element.36), channel_id=1, source_target_pairs={{0,12},{1,13},{2,14},{3,15},{4,8},{5,9},{6,10},{7,11},{8,4},{9,5},... | collective-permute-start | bytes 221192 | tf_op jit(solution)/shard_map/ppermute | solution.py:147
  29.3 0.9 %collective-permute-start.13 = (bf16[16,2304]{1,0:T(8,128)(2,1)S(1)}, bf16[16,2304]{1,0:T(8,128)(2,1)S(1)}, u32[]{:S(2)}, u32[]{:S(2)}) collective-permute-start(bf16[16,2304]{1,0:T(8,128)(2,1)S(1)} %fusion.15), channel_id=1, source_target_pairs={{0,4},{1,5},{2,6},{3,7},{4,0},{5,1},{6,2},{7,3},{8,12},{9,13},{10,... | collective-permute-start | bytes 221192 | tf_op jit(solution)/shard_map/ppermute | solution.py:147
  30.2 4.4 %collective-permute-done.15 = bf16[16,2304]{1,0:T(8,128)(2,1)S(1)} collective-permute-done((bf16[16,2304]{1,0:T(8,128)(2,1)S(1)}, bf16[16,2304]{1,0:T(8,128)(2,1)S(1)}, u32[]{:S(2)}, u32[]{:S(2)}) %collective-permute-start.15) | collective-permute-done | bytes 73760 | tf_op jit(solution)/shard_map/ppermute | solution.py:147
  34.6 1.0 %collective-permute-done.13 = bf16[16,2304]{1,0:T(8,128)(2,1)S(1)} collective-permute-done((bf16[16,2304]{1,0:T(8,128)(2,1)S(1)}, bf16[16,2304]{1,0:T(8,128)(2,1)S(1)}, u32[]{:S(2)}, u32[]{:S(2)}) %collective-permute-start.13) | collective-permute-done | bytes 73760 | tf_op jit(solution)/shard_map/ppermute | solution.py:147
  35.7 2.2 %collective-permute-start.23 = (bf16[16,2304]{1,0:T(8,128)(2,1)S(1)}, bf16[16,2304]{1,0:T(8,128)(2,1)S(1)}, u32[]{:S(2)}, u32[]{:S(2)}) collective-permute-start(bf16[16,2304]{1,0:T(8,128)(2,1)S(1)} %fusion.20), channel_id=1, source_target_pairs={{0,12},{1,13},{2,14},{3,15},{4,8},{5,9},{6,10},{7,11},{8,4},{9,5},... | collective-permute-start | bytes 221192 | tf_op jit(solution)/shard_map/ppermute | solution.py:147
  38.0 2.2 %collective-permute-start.18 = (bf16[16,2304]{1,0:T(8,128)(2,1)S(1)}, bf16[16,2304]{1,0:T(8,128)(2,1)S(1)}, u32[]{:S(2)}, u32[]{:S(2)}) collective-permute-start(bf16[16,2304]{1,0:T(8,128)(2,1)S(1)} %fusion.20), channel_id=1, source_target_pairs={{0,4},{1,5},{2,6},{3,7},{4,0},{5,1},{6,2},{7,3},{8,12},{9,13},{10,... | collective-permute-start | bytes 221192 | tf_op jit(solution)/shard_map/ppermute | solution.py:147
  40.6 2.1 %collective-permute-done.23 = bf16[16,2304]{1,0:T(8,128)(2,1)S(1)} collective-permute-done((bf16[16,2304]{1,0:T(8,128)(2,1)S(1)}, bf16[16,2304]{1,0:T(8,128)(2,1)S(1)}, u32[]{:S(2)}, u32[]{:S(2)}) %collective-permute-start.23) | collective-permute-done | bytes 73760 | tf_op jit(solution)/shard_map/ppermute | solution.py:147
  42.8 0.5 collective-permute-start.24
  43.2 1.8 %collective-permute-done.21 = bf16[16,2304]{1,0:T(8,128)(2,1)S(1)} collective-permute-done((bf16[16,2304]{1,0:T(8,128)(2,1)S(1)}, bf16[16,2304]{1,0:T(8,128)(2,1)S(1)}, u32[]{:S(2)}, u32[]{:S(2)}) %collective-permute-start.21) | collective-permute-done | bytes 73760 | tf_op jit(solution)/shard_map/ppermute | solution.py:147
  45.0 0.7 %collective-permute-start.22 = (bf16[16,2304]{1,0:T(8,128)(2,1)S(1)}, bf16[16,2304]{1,0:T(8,128)(2,1)S(1)}, u32[]{:S(2)}, u32[]{:S(2)}) collective-permute-start(bf16[16,2304]{1,0:T(8,128)(2,1)S(1)} %collective-permute-done.21), channel_id=1, source_target_pairs={{0,2},{1,3},{2,0},{3,1},{4,6},{5,7},{6,4},{7,5},{8,10},{9,11},{10,... | collective-permute-start | bytes 221192 | tf_op jit(solution)/shard_map/ppermute | solution.py:147
  45.8 1.3 %collective-permute-start.19 = (bf16[16,2304]{1,0:T(8,128)(2,1)S(1)}, bf16[16,2304]{1,0:T(8,128)(2,1)S(1)}, u32[]{:S(2)}, u32[]{:S(2)}) collective-permute-start(bf16[16,2304]{1,0:T(8,128)(2,1)S(1)} %collective-permute-done.18), channel_id=1, source_target_pairs={{0,2},{1,3},{2,0},{3,1},{4,6},{5,7},{6,4},{7,5},{8,10},{9,11},{10,... | collective-permute-start | bytes 221192 | tf_op jit(solution)/shard_map/ppermute | solution.py:147
  47.1 3.0 %collective-permute-done.22 = bf16[16,2304]{1,0:T(8,128)(2,1)S(1)} collective-permute-done((bf16[16,2304]{1,0:T(8,128)(2,1)S(1)}, bf16[16,2304]{1,0:T(8,128)(2,1)S(1)}, u32[]{:S(2)}, u32[]{:S(2)}) %collective-permute-start.22) | collective-permute-done | bytes 73760 | tf_op jit(solution)/shard_map/ppermute | solution.py:147
  50.2 0.7 %collective-permute-done.19 = bf16[16,2304]{1,0:T(8,128)(2,1)S(1)} collective-permute-done((bf16[16,2304]{1,0:T(8,128)(2,1)S(1)}, bf16[16,2304]{1,0:T(8,128)(2,1)S(1)}, u32[]{:S(2)}, u32[]{:S(2)}) %collective-permute-start.19) | collective-permute-done | bytes 73760 | tf_op jit(solution)/shard_map/ppermute | solution.py:147
  51.1 1.0 %own_totals.1 = (f32[128,2304]{1,0:T(8,128)S(1)}, f32[128,2304]{1,0:T(8,128)S(1)}) custom-call(bf16[128,128]{1,0:T(8,128)(2,1)S(1)} %get-tuple-element.41.codes_across, bf16[128,2304]{1,0:T(8,128)(2,1)S(1)} %subtract_convert_fusion.centered, bf16[128,2304]{1,0:T(8,128)(2,1)S(1)} %constant_dynamic-update-slice_fusion.10.errors, bf16[128,2304]{1,0:T(8,128)(2,1)S(1)} %copy-done), custom_call_target="tpu_custom_call" | custom-call | flops 226492416 | bytes 4718592 | tf_op jit(solution)/shard_map/own_totals/pallas_call | solution.py:41
  52.1 0.5 collective-permute-done.20.refs_0_
  52.7 3.3 %update.1 = (bf16[128,2304]{1,0:T(8,128)(2,1)}, f32[128,2304]{1,0:T(8,128)}, f32[128,2304]{1,0:T(8,128)}, bf16[128,2304]{1,0:T(8,128)(2,1)}, f32[128,2304]{1,0:T(8,128)}, /*index=5*/f32[128,2304]{1,0:T(8,128)}) custom-call(bf16[128,128]{1,0:T(8,128)(2,1)S(1)} %bitcast.8, bf16[128,2304]{1,0:T(8,128)(2,1)S(1)} %collective-permute-done.11.centered, ...), custom_call_target="tpu_custom_call" | custom-call | flops 226492416 | bytes 12976128 | tf_op jit(solution)/shard_map/update/pallas_call | solution.py:120
  (75 shorter events, 3.5 us)
Async XLA Ops:
  0.6 9.2 %copy-start.9 = (f32[128]{0:T(128)S(1)}, f32[128]{0:T(128)}, u32[]{:S(2)}) copy-start(f32[128]{0:T(128)} %param.11) | copy-start | bytes 1540
  0.7 8.7 %copy-start = (bf16[128,2304]{1,0:T(8,128)(2,1)S(1)}, bf16[128,2304]{1,0:T(8,128)(2,1)}, u32[]{:S(2)}) copy-start(bf16[128,2304]{1,0:T(8,128)(2,1)} %refs_3_.1) | copy-start | bytes 1769476
  0.7 9.2 %copy-start.5 = (bf16[128,2304]{1,0:T(8,128)(2,1)S(1)}, bf16[128,2304]{1,0:T(8,128)(2,1)}, u32[]{:S(2)}) copy-start(bf16[128,2304]{1,0:T(8,128)(2,1)} %refs_2_.1) | copy-start | bytes 1769476
  0.7 17.9 %copy-start.8 = (f32[2304]{0:T(1024)S(1)}, f32[2304]{0:T(1024)}, u32[]{:S(2)}) copy-start(f32[2304]{0:T(1024)} %param.13) | copy-start | bytes 27652
  0.7 9.2 %collective-permute-start.3 = (bf16[16,2304]{1,0:T(8,128)(2,1)}, bf16[16,2304]{1,0:T(8,128)(2,1)S(1)}, u32[]{:S(2)}, u32[]{:S(2)}) collective-permute-start(bf16[16,2304]{1,0:T(8,128)(2,1)} %param.9), channel_id=1, source_target_pairs={{0,8},{1,9},{2,10},{3,11},{4,12},{5,13},{6,14},{7,15},{8,0},{9,1},... | collective-permute-start | bytes 221192 | tf_op jit(solution)/shard_map/ppermute | solution.py:147
  4.8 5.2 %collective-permute-start.1 = (bf16[16,2304]{1,0:T(8,128)(2,1)}, bf16[16,2304]{1,0:T(8,128)(2,1)S(1)}, u32[]{:S(2)}, u32[]{:S(2)}) collective-permute-start(bf16[16,2304]{1,0:T(8,128)(2,1)} %param.9), channel_id=1, source_target_pairs={{0,4},{1,5},{2,6},{3,7},{4,0},{5,1},{6,2},{7,3},{8,12},{9,13},{10,... | collective-permute-start | bytes 221192 | tf_op jit(solution)/shard_map/ppermute | solution.py:147
  6.4 4.7 %collective-permute-start = (bf16[16,2304]{1,0:T(8,128)(2,1)}, bf16[16,2304]{1,0:T(8,128)(2,1)S(1)}, u32[]{:S(2)}, u32[]{:S(2)}) collective-permute-start(bf16[16,2304]{1,0:T(8,128)(2,1)} %param.9), channel_id=1, source_target_pairs={{0,2},{1,3},{2,0},{3,1},{4,6},{5,7},{6,4},{7,5},{8,10},{9,11},{10,... | collective-permute-start | bytes 221192 | tf_op jit(solution)/shard_map/ppermute | solution.py:147
  7.9 6.4 %collective-permute-start.5 = (bf16[16,2304]{1,0:T(8,128)(2,1)}, bf16[16,2304]{1,0:T(8,128)(2,1)S(1)}, u32[]{:S(2)}, u32[]{:S(2)}) collective-permute-start(bf16[16,2304]{1,0:T(8,128)(2,1)} %param.9), channel_id=1, source_target_pairs={{0,12},{1,13},{2,14},{3,15},{4,8},{5,9},{6,10},{7,11},{8,4},{9,5},... | collective-permute-start | bytes 221192 | tf_op jit(solution)/shard_map/ppermute | solution.py:147
  8.1 1.3 %collective-permute-start.8 = (f32[128]{0:T(128)}, f32[128]{0:T(128)S(1)}, u32[]{:S(2)}, u32[]{:S(2)}) collective-permute-start(f32[128]{0:T(128)} %param.11), channel_id=1, source_target_pairs={{0,1},{1,0},{2,3},{3,2},{4,5},{5,4},{6,7},{7,6},{8,9},{9,8},{10,11... | collective-permute-start | bytes 1544 | tf_op jit(solution)/shard_map/ppermute | solution.py:154
  9.4 9.9 %collective-permute-start.10 = (bf16[128,2304]{1,0:T(8,128)(2,1)S(1)}, bf16[128,2304]{1,0:T(8,128)(2,1)S(1)}, u32[]{:S(2)}, u32[]{:S(2)}) collective-permute-start(bf16[128,2304]{1,0:T(8,128)(2,1)S(1)} %copy-done), channel_id=1, source_target_pairs={{0,1},{1,0},{2,3},{3,2},{4,5},{5,4},{6,7},{7,6},{8,9},{9,8},{10,11... | collective-permute-start | bytes 1769480 | tf_op jit(solution)/shard_map/ppermute | solution.py:154
  9.9 8.9 %collective-permute-start.7 = (bf16[128,2304]{1,0:T(8,128)(2,1)S(1)}, bf16[128,2304]{1,0:T(8,128)(2,1)S(1)}, u32[]{:S(2)}, u32[]{:S(2)}) collective-permute-start(bf16[128,2304]{1,0:T(8,128)(2,1)S(1)} %copy-done.5), channel_id=1, source_target_pairs={{0,1},{1,0},{2,3},{3,2},{4,5},{5,4},{6,7},{7,6},{8,9},{9,8},{10,11... | collective-permute-start | bytes 1769480 | tf_op jit(solution)/shard_map/ppermute | solution.py:154
  10.0 6.7 %collective-permute-start.4 = (bf16[16,2304]{1,0:T(8,128)(2,1)S(1)}, bf16[16,2304]{1,0:T(8,128)(2,1)S(1)}, u32[]{:S(2)}, u32[]{:S(2)}) collective-permute-start(bf16[16,2304]{1,0:T(8,128)(2,1)S(1)} %collective-permute-done.3), channel_id=1, source_target_pairs={{0,2},{1,3},{2,0},{3,1},{4,6},{5,7},{6,4},{7,5},{8,10},{9,11},{10,... | collective-permute-start | bytes 221192 | tf_op jit(solution)/shard_map/ppermute | solution.py:147
  11.0 5.7 %collective-permute-start.2 = (bf16[16,2304]{1,0:T(8,128)(2,1)S(1)}, bf16[16,2304]{1,0:T(8,128)(2,1)S(1)}, u32[]{:S(2)}, u32[]{:S(2)}) collective-permute-start(bf16[16,2304]{1,0:T(8,128)(2,1)S(1)} %collective-permute-done.1), channel_id=1, source_target_pairs={{0,2},{1,3},{2,0},{3,1},{4,6},{5,7},{6,4},{7,5},{8,10},{9,11},{10,... | collective-permute-start | bytes 221192 | tf_op jit(solution)/shard_map/ppermute | solution.py:147
  14.2 4.4 %collective-permute-start.6 = (bf16[16,2304]{1,0:T(8,128)(2,1)S(1)}, bf16[16,2304]{1,0:T(8,128)(2,1)S(1)}, u32[]{:S(2)}, u32[]{:S(2)}) collective-permute-start(bf16[16,2304]{1,0:T(8,128)(2,1)S(1)} %collective-permute-done.5), channel_id=1, source_target_pairs={{0,2},{1,3},{2,0},{3,1},{4,6},{5,7},{6,4},{7,5},{8,10},{9,11},{10,... | collective-permute-start | bytes 221192 | tf_op jit(solution)/shard_map/ppermute | solution.py:147
  19.2 1.4 %collective-permute-start.9 = (bf16[128,128]{0,1:T(8,128)(2,1)S(1)}, bf16[128,128]{0,1:T(8,128)(2,1)S(1)}, u32[]{:S(2)}, u32[]{:S(2)}) collective-permute-start(bf16[128,128]{0,1:T(8,128)(2,1)S(1)} %get-tuple-element.42), channel_id=1, source_target_pairs={{0,1},{1,0},{2,3},{3,2},{4,5},{5,4},{6,7},{7,6},{8,9},{9,8},{10,11... | collective-permute-start | bytes 98312 | tf_op jit(solution)/shard_map/ppermute | solution.py:154
  19.8 6.7 %collective-permute-start.14 = (bf16[32,2304]{1,0:T(8,128)(2,1)S(1)}, bf16[32,2304]{1,0:T(8,128)(2,1)S(1)}, u32[]{:S(2)}, u32[]{:S(2)}) collective-permute-start(bf16[32,2304]{1,0:T(8,128)(2,1)S(1)} %pad_maximum_fusion.3), channel_id=1, source_target_pairs={{0,2},{1,3},{2,0},{3,1},{4,6},{5,7},{6,4},{7,5},{8,10},{9,11},{10,... | collective-permute-start | bytes 442376 | tf_op jit(solution)/shard_map/ppermute | solution.py:147
  20.4 2.0 %collective-permute-start.11 = (bf16[128,2304]{1,0:T(8,128)(2,1)S(1)}, bf16[128,2304]{1,0:T(8,128)(2,1)S(1)}, u32[]{:S(2)}, u32[]{:S(2)}) collective-permute-start(bf16[128,2304]{1,0:T(8,128)(2,1)S(1)} %subtract_convert_fusion.centered), channel_id=1, source_target_pairs={{0,1},{1,0},{2,3},{3,2},{4,5},{5,4},{6,7},{7,6},{8,9},{9,8},{10,11... | collective-permute-start | bytes 1769480 | tf_op jit(solution)/shard_map/ppermute | solution.py:154
  22.4 6.9 %collective-permute-start.12 = (bf16[32,2304]{1,0:T(8,128)(2,1)S(1)}, bf16[32,2304]{1,0:T(8,128)(2,1)S(1)}, u32[]{:S(2)}, u32[]{:S(2)}) collective-permute-start(bf16[32,2304]{1,0:T(8,128)(2,1)S(1)} %pad_maximum_fusion.2), channel_id=1, source_target_pairs={{0,2},{1,3},{2,0},{3,1},{4,6},{5,7},{6,4},{7,5},{8,10},{9,11},{10,... | collective-permute-start | bytes 442376 | tf_op jit(solution)/shard_map/ppermute | solution.py:147
  26.6 8.1 %collective-permute-start.15 = (bf16[16,2304]{1,0:T(8,128)(2,1)S(1)}, bf16[16,2304]{1,0:T(8,128)(2,1)S(1)}, u32[]{:S(2)}, u32[]{:S(2)}) collective-permute-start(bf16[16,2304]{1,0:T(8,128)(2,1)S(1)} %get-tuple-element.35), channel_id=1, source_target_pairs={{0,8},{1,9},{2,10},{3,11},{4,12},{5,13},{6,14},{7,15},{8,0},{9,1},... | collective-permute-start | bytes 221192 | tf_op jit(solution)/shard_map/ppermute | solution.py:147
  27.4 7.2 %collective-permute-start.16 = (bf16[16,2304]{1,0:T(8,128)(2,1)S(1)}, bf16[16,2304]{1,0:T(8,128)(2,1)S(1)}, u32[]{:S(2)}, u32[]{:S(2)}) collective-permute-start(bf16[16,2304]{1,0:T(8,128)(2,1)S(1)} %get-tuple-element.36), channel_id=1, source_target_pairs={{0,12},{1,13},{2,14},{3,15},{4,8},{5,9},{6,10},{7,11},{8,4},{9,5},... | collective-permute-start | bytes 221192 | tf_op jit(solution)/shard_map/ppermute | solution.py:147
  29.3 6.3 %collective-permute-start.13 = (bf16[16,2304]{1,0:T(8,128)(2,1)S(1)}, bf16[16,2304]{1,0:T(8,128)(2,1)S(1)}, u32[]{:S(2)}, u32[]{:S(2)}) collective-permute-start(bf16[16,2304]{1,0:T(8,128)(2,1)S(1)} %fusion.15), channel_id=1, source_target_pairs={{0,4},{1,5},{2,6},{3,7},{4,0},{5,1},{6,2},{7,3},{8,12},{9,13},{10,... | collective-permute-start | bytes 221192 | tf_op jit(solution)/shard_map/ppermute | solution.py:147
  35.6 16.9 %copy-start.4 = (f32[128,2304]{1,0:T(8,128)S(1)}, f32[128,2304]{1,0:T(8,128)}, u32[]{:S(2)}) copy-start(f32[128,2304]{1,0:T(8,128)} %refs_7_.1) | copy-start | bytes 3538948
  35.7 15.4 %copy-start.6 = (bf16[16,2304]{1,0:T(8,128)(2,1)}, bf16[16,2304]{1,0:T(8,128)(2,1)S(1)}, u32[]{:S(2)}) copy-start(bf16[16,2304]{1,0:T(8,128)(2,1)S(1)} %fusion.20) | copy-start | bytes 221188
  35.7 7.0 %collective-permute-start.23 = (bf16[16,2304]{1,0:T(8,128)(2,1)S(1)}, bf16[16,2304]{1,0:T(8,128)(2,1)S(1)}, u32[]{:S(2)}, u32[]{:S(2)}) collective-permute-start(bf16[16,2304]{1,0:T(8,128)(2,1)S(1)} %fusion.20), channel_id=1, source_target_pairs={{0,12},{1,13},{2,14},{3,15},{4,8},{5,9},{6,10},{7,11},{8,4},{9,5},... | collective-permute-start | bytes 221192 | tf_op jit(solution)/shard_map/ppermute | solution.py:147
  37.9 7.1 %collective-permute-start.21 = (bf16[16,2304]{1,0:T(8,128)(2,1)S(1)}, bf16[16,2304]{1,0:T(8,128)(2,1)S(1)}, u32[]{:S(2)}, u32[]{:S(2)}) collective-permute-start(bf16[16,2304]{1,0:T(8,128)(2,1)S(1)} %fusion.20), channel_id=1, source_target_pairs={{0,8},{1,9},{2,10},{3,11},{4,12},{5,13},{6,14},{7,15},{8,0},{9,1},... | collective-permute-start | bytes 221192 | tf_op jit(solution)/shard_map/ppermute | solution.py:147
  38.0 7.8 %collective-permute-start.18 = (bf16[16,2304]{1,0:T(8,128)(2,1)S(1)}, bf16[16,2304]{1,0:T(8,128)(2,1)S(1)}, u32[]{:S(2)}, u32[]{:S(2)}) collective-permute-start(bf16[16,2304]{1,0:T(8,128)(2,1)S(1)} %fusion.20), channel_id=1, source_target_pairs={{0,4},{1,5},{2,6},{3,7},{4,0},{5,1},{6,2},{7,3},{8,12},{9,13},{10,... | collective-permute-start | bytes 221192 | tf_op jit(solution)/shard_map/ppermute | solution.py:147
  40.2 6.9 %collective-permute-start.17 = (bf16[16,2304]{1,0:T(8,128)(2,1)S(1)}, bf16[16,2304]{1,0:T(8,128)(2,1)S(1)}, u32[]{:S(2)}, u32[]{:S(2)}) collective-permute-start(bf16[16,2304]{1,0:T(8,128)(2,1)S(1)} %fusion.20), channel_id=1, source_target_pairs={{0,2},{1,3},{2,0},{3,1},{4,6},{5,7},{6,4},{7,5},{8,10},{9,11},{10,... | collective-permute-start | bytes 221192 | tf_op jit(solution)/shard_map/ppermute | solution.py:147
  42.8 4.4 %collective-permute-start.24 = (bf16[16,2304]{1,0:T(8,128)(2,1)S(1)}, bf16[16,2304]{1,0:T(8,128)(2,1)S(1)}, u32[]{:S(2)}, u32[]{:S(2)}) collective-permute-start(bf16[16,2304]{1,0:T(8,128)(2,1)S(1)} %collective-permute-done.23), channel_id=1, source_target_pairs={{0,2},{1,3},{2,0},{3,1},{4,6},{5,7},{6,4},{7,5},{8,10},{9,11},{10,... | collective-permute-start | bytes 221192 | tf_op jit(solution)/shard_map/ppermute | solution.py:147
  45.0 5.1 %collective-permute-start.22 = (bf16[16,2304]{1,0:T(8,128)(2,1)S(1)}, bf16[16,2304]{1,0:T(8,128)(2,1)S(1)}, u32[]{:S(2)}, u32[]{:S(2)}) collective-permute-start(bf16[16,2304]{1,0:T(8,128)(2,1)S(1)} %collective-permute-done.21), channel_id=1, source_target_pairs={{0,2},{1,3},{2,0},{3,1},{4,6},{5,7},{6,4},{7,5},{8,10},{9,11},{10,... | collective-permute-start | bytes 221192 | tf_op jit(solution)/shard_map/ppermute | solution.py:147
  45.8 5.1 %collective-permute-start.19 = (bf16[16,2304]{1,0:T(8,128)(2,1)S(1)}, bf16[16,2304]{1,0:T(8,128)(2,1)S(1)}, u32[]{:S(2)}, u32[]{:S(2)}) collective-permute-start(bf16[16,2304]{1,0:T(8,128)(2,1)S(1)} %collective-permute-done.18), channel_id=1, source_target_pairs={{0,2},{1,3},{2,0},{3,1},{4,6},{5,7},{6,4},{7,5},{8,10},{9,11},{10,... | collective-permute-start | bytes 221192 | tf_op jit(solution)/shard_map/ppermute | solution.py:147
  50.1 2.0 %collective-permute-start.25 = (bf16[64,2304]{1,0:T(8,128)(2,1)S(1)}, bf16[64,2304]{1,0:T(8,128)(2,1)S(1)}, u32[]{:S(2)}, u32[]{:S(2)}) collective-permute-start(bf16[64,2304]{1,0:T(8,128)(2,1)S(1)} %pad_maximum_fusion.1), channel_id=1, source_target_pairs={{0,1},{1,0},{2,3},{3,2},{4,5},{5,4},{6,7},{7,6},{8,9},{9,8},{10,11... | collective-permute-start | bytes 884744 | tf_op jit(solution)/shard_map/ppermute | solution.py:154
  50.9 1.6 %collective-permute-start.20 = (bf16[64,2304]{1,0:T(8,128)(2,1)S(1)}, bf16[64,2304]{1,0:T(8,128)(2,1)S(1)}, u32[]{:S(2)}, u32[]{:S(2)}) collective-permute-start(bf16[64,2304]{1,0:T(8,128)(2,1)S(1)} %pad_maximum_fusion), channel_id=1, source_target_pairs={{0,1},{1,0},{2,3},{3,2},{4,5},{5,4},{6,7},{7,6},{8,9},{9,8},{10,11... | collective-permute-start | bytes 884744 | tf_op jit(solution)/shard_map/ppermute | solution.py:154
  (4 other events, 14.3 us)

commit v19 on v18

--- a/solution.py
+++ b/solution.py
@@ -87,11 +87,10 @@
                 grad = totals[which][some] + total[start : start + part]
                 moment = beta_first * moments[2 * which][some] + first * grad
                 square = beta_second * moments[2 * which + 1][some] + second * (grad * grad)
-                guess = lax.rsqrt(square)
-                root = square * guess
-                inverse = guess * (2.0 - (root + adam_epsilon) * guess)
+                root = square * lax.rsqrt(square)
                 held[3 * which][some] = (
-                    weight[some].astype(jnp.float32) - step_rate * moment * inverse
+                    weight[some].astype(jnp.float32)
+                    - step_rate * moment * pl.reciprocal(root + adam_epsilon, approx=True)
                 ).astype(jnp.bfloat16)
                 held[3 * which + 1][some] = moment
                 held[3 * which + 2][some] = square
@@ -209,9 +208,8 @@
     far = [one.astype(jnp.bfloat16) for one in pair_sums(far_parts, far_sent)]
     later_centered, _ = lax.optimization_barrier((centered, far_sent))
     other_centered = to_other_core(later_centered)
-    near_codes, _ = lax.optimization_barrier((codes[:quad], other_codes))
+    near_codes, _ = lax.optimization_barrier((codes[:quad], (other_codes, other_centered)))
     near_parts, near_sent = partial_sums(near_codes)
-    near_sent, _ = lax.optimization_barrier((near_sent, other_centered))
     own, near = pair_sums(near_parts, near_sent)
     summed = own + to_chip(near.astype(jnp.bfloat16), 2).astype(jnp.float32)
     for k, one in enumerate(far, 2):

time: 56.2 us -> 54.3 us (0.966)
  waiting for transfers between devices: 23.4 us -> 20.4 us
  starting transfers between devices: 24.4 us -> 25.5 us
    ppermute x19, waiting for transfers between devices: 21.4 us -> 18.8 us  [to_chip(): lax.ppermute(block, 'latent', [(i, i ^ 2 * distance) for i in range(size)])]
    ppermute x19, starting transfers between devices: 23.4 us -> 24.2 us  [to_chip(): lax.ppermute(block, 'latent', [(i, i ^ 2 * distance) for i in range(size)])]
  transfers between devices with their start and end apart: 26 -> 26, of which waited for: 14 -> 13; matrix products, arithmetic and copies ran while one was open for 5% -> 3% of each run, Pallas kernels for 2% -> 2%
where the time goes in v19:
time: 54.3 us; the launch traced here: 54.1 us
  starting transfers between devices  25.5 us (47%)
  waiting for transfers between devices  20.4 us (38%)
  Pallas kernels  4.23 us (8%)
  local copies, waits for them, and re-layouts  1.39 us (3%)
  matrix products  1.26 us (2%)
  between operations  0.99 us (2%)
    ppermute x19, starting transfers between devices, to_chip(): lax.ppermute(block, 'latent', [(i, i ^ 2 * distance) for i in range(size)])  24.2 us
    ppermute x19, waiting for transfers between devices, to_chip(): lax.ppermute(block, 'latent', [(i, i ^ 2 * distance) for i in range(size)])  18.8 us
    pallas_call x1, Pallas kernels, update(): pl.pallas_call(functools.partial(update_kernel, columns, float(total_rows...  3.26 us
    ppermute x7, waiting for transfers between devices, to_other_core(): return lax.ppermute(block, 'latent', [(i, i ^ 1) for i in range(size)])  1.63 us
    unnamed x35, local copies, waits for them, and re-layouts  1.31 us
    ppermute x7, starting transfers between devices, to_other_core(): return lax.ppermute(block, 'latent', [(i, i ^ 1) for i in range(size)])  1.28 us
  transfers between devices with their start and end apart: 26, of which 13 were waited for; matrix products, arithmetic and copies ran while one was open for 3% of the time, Pallas kernels for 2%

profile of v19, /device:TPU:0, one launch (start us, length us, event | category | flops | bytes accessed | tf_op | source)
XLA Modules:
  0.0 54.1 jit_solution(10808750975977948333)
XLA Ops:
  0.7 4.1 %collective-permute-start.3 = (bf16[16,2304]{1,0:T(8,128)(2,1)}, bf16[16,2304]{1,0:T(8,128)(2,1)S(1)}, u32[]{:S(2)}, u32[]{:S(2)}) collective-permute-start(bf16[16,2304]{1,0:T(8,128)(2,1)} %param.9), channel_id=1, source_target_pairs={{0,8},{1,9},{2,10},{3,11},{4,12},{5,13},{6,14},{7,15},{8,0},{9,1},... | collective-permute-start | bytes 221192 | tf_op jit(solution)/shard_map/ppermute | solution.py:146
  4.8 1.6 %collective-permute-start.1 = (bf16[16,2304]{1,0:T(8,128)(2,1)}, bf16[16,2304]{1,0:T(8,128)(2,1)S(1)}, u32[]{:S(2)}, u32[]{:S(2)}) collective-permute-start(bf16[16,2304]{1,0:T(8,128)(2,1)} %param.9), channel_id=1, source_target_pairs={{0,4},{1,5},{2,6},{3,7},{4,0},{5,1},{6,2},{7,3},{8,12},{9,13},{10,... | collective-permute-start | bytes 221192 | tf_op jit(solution)/shard_map/ppermute | solution.py:146
  6.4 1.5 %collective-permute-start = (bf16[16,2304]{1,0:T(8,128)(2,1)}, bf16[16,2304]{1,0:T(8,128)(2,1)S(1)}, u32[]{:S(2)}, u32[]{:S(2)}) collective-permute-start(bf16[16,2304]{1,0:T(8,128)(2,1)} %param.9), channel_id=1, source_target_pairs={{0,2},{1,3},{2,0},{3,1},{4,6},{5,7},{6,4},{7,5},{8,10},{9,11},{10,... | collective-permute-start | bytes 221192 | tf_op jit(solution)/shard_map/ppermute | solution.py:146
  8.1 1.1 %constant_dynamic-update-slice_fusion.9 = bf16[256,2304]{1,0:T(8,128)(2,1)S(1)} fusion(bf16[128,2304]{1,0:T(8,128)(2,1)} %refs_3_.1), kind=kLoop, calls=%fused_computation.35 | loop fusion | bytes 1179648
  10.0 1.0 %collective-permute-start.4 = (bf16[16,2304]{1,0:T(8,128)(2,1)S(1)}, bf16[16,2304]{1,0:T(8,128)(2,1)S(1)}, u32[]{:S(2)}, u32[]{:S(2)}) collective-permute-start(bf16[16,2304]{1,0:T(8,128)(2,1)S(1)} %collective-permute-done.3), channel_id=1, source_target_pairs={{0,2},{1,3},{2,0},{3,1},{4,6},{5,7},{6,4},{7,5},{8,10},{9,11},{10,... | collective-permute-start | bytes 221192 | tf_op jit(solution)/shard_map/ppermute | solution.py:146
  11.0 1.4 %collective-permute-start.2 = (bf16[16,2304]{1,0:T(8,128)(2,1)S(1)}, bf16[16,2304]{1,0:T(8,128)(2,1)S(1)}, u32[]{:S(2)}, u32[]{:S(2)}) collective-permute-start(bf16[16,2304]{1,0:T(8,128)(2,1)S(1)} %collective-permute-done.1), channel_id=1, source_target_pairs={{0,2},{1,3},{2,0},{3,1},{4,6},{5,7},{6,4},{7,5},{8,10},{9,11},{10,... | collective-permute-start | bytes 221192 | tf_op jit(solution)/shard_map/ppermute | solution.py:146
  12.4 1.8 %collective-permute-done.5 = bf16[16,2304]{1,0:T(8,128)(2,1)S(1)} collective-permute-done((bf16[16,2304]{1,0:T(8,128)(2,1)}, bf16[16,2304]{1,0:T(8,128)(2,1)S(1)}, u32[]{:S(2)}, u32[]{:S(2)}) %collective-permute-start.5) | collective-permute-done | bytes 73760 | tf_op jit(solution)/shard_map/ppermute | solution.py:146
  14.2 0.5 collective-permute-start.6
  14.8 1.9 %collective-permute-done.2 = bf16[16,2304]{1,0:T(8,128)(2,1)S(1)} collective-permute-done((bf16[16,2304]{1,0:T(8,128)(2,1)S(1)}, bf16[16,2304]{1,0:T(8,128)(2,1)S(1)}, u32[]{:S(2)}, u32[]{:S(2)}) %collective-permute-start.2) | collective-permute-done | bytes 73760 | tf_op jit(solution)/shard_map/ppermute | solution.py:146
  16.7 1.9 %collective-permute-done.6 = bf16[16,2304]{1,0:T(8,128)(2,1)S(1)} collective-permute-done((bf16[16,2304]{1,0:T(8,128)(2,1)S(1)}, bf16[16,2304]{1,0:T(8,128)(2,1)S(1)}, u32[]{:S(2)}, u32[]{:S(2)}) %collective-permute-start.6) | collective-permute-done | bytes 73760 | tf_op jit(solution)/shard_map/ppermute | solution.py:146
  19.8 0.5 collective-permute-start.9
  20.3 0.5 collective-permute-start.14
  20.8 1.0 %collective-permute-done.9 = bf16[128,128]{0,1:T(8,128)(2,1)S(1)} collective-permute-done((bf16[128,128]{0,1:T(8,128)(2,1)S(1)}, bf16[128,128]{0,1:T(8,128)(2,1)S(1)}, u32[]{:S(2)}, u32[]{:S(2)}) %collective-permute-start.9) | collective-permute-done | bytes 32800 | tf_op jit(solution)/shard_map/ppermute | solution.py:153
  22.3 0.6 %collective-permute-start.12 = (bf16[32,2304]{1,0:T(8,128)(2,1)S(1)}, bf16[32,2304]{1,0:T(8,128)(2,1)S(1)}, u32[]{:S(2)}, u32[]{:S(2)}) collective-permute-start(bf16[32,2304]{1,0:T(8,128)(2,1)S(1)} %pad_maximum_fusion.3), channel_id=1, source_target_pairs={{0,2},{1,3},{2,0},{3,1},{4,6},{5,7},{6,4},{7,5},{8,10},{9,11},{10,... | collective-permute-start | bytes 442376 | tf_op jit(solution)/shard_map/ppermute | solution.py:146
  22.8 4.2 %collective-permute-done.14 = bf16[32,2304]{1,0:T(8,128)(2,1)S(1)} collective-permute-done((bf16[32,2304]{1,0:T(8,128)(2,1)S(1)}, bf16[32,2304]{1,0:T(8,128)(2,1)S(1)}, u32[]{:S(2)}, u32[]{:S(2)}) %collective-permute-start.14) | collective-permute-done | bytes 147488 | tf_op jit(solution)/shard_map/ppermute | solution.py:146
  27.1 0.9 %collective-permute-start.15 = (bf16[16,2304]{1,0:T(8,128)(2,1)S(1)}, bf16[16,2304]{1,0:T(8,128)(2,1)S(1)}, u32[]{:S(2)}, u32[]{:S(2)}) collective-permute-start(bf16[16,2304]{1,0:T(8,128)(2,1)S(1)} %get-tuple-element.33), channel_id=1, source_target_pairs={{0,8},{1,9},{2,10},{3,11},{4,12},{5,13},{6,14},{7,15},{8,0},{9,1},... | collective-permute-start | bytes 221192 | tf_op jit(solution)/shard_map/ppermute | solution.py:146
  28.0 2.0 %collective-permute-start.16 = (bf16[16,2304]{1,0:T(8,128)(2,1)S(1)}, bf16[16,2304]{1,0:T(8,128)(2,1)S(1)}, u32[]{:S(2)}, u32[]{:S(2)}) collective-permute-start(bf16[16,2304]{1,0:T(8,128)(2,1)S(1)} %get-tuple-element.34), channel_id=1, source_target_pairs={{0,12},{1,13},{2,14},{3,15},{4,8},{5,9},{6,10},{7,11},{8,4},{9,5},... | collective-permute-start | bytes 221192 | tf_op jit(solution)/shard_map/ppermute | solution.py:146
  30.0 0.7 %collective-permute-start.13 = (bf16[16,2304]{1,0:T(8,128)(2,1)S(1)}, bf16[16,2304]{1,0:T(8,128)(2,1)S(1)}, u32[]{:S(2)}, u32[]{:S(2)}) collective-permute-start(bf16[16,2304]{1,0:T(8,128)(2,1)S(1)} %fusion.15), channel_id=1, source_target_pairs={{0,4},{1,5},{2,6},{3,7},{4,0},{5,1},{6,2},{7,3},{8,12},{9,13},{10,... | collective-permute-start | bytes 221192 | tf_op jit(solution)/shard_map/ppermute | solution.py:146
  30.7 3.8 %collective-permute-done.15 = bf16[16,2304]{1,0:T(8,128)(2,1)S(1)} collective-permute-done((bf16[16,2304]{1,0:T(8,128)(2,1)S(1)}, bf16[16,2304]{1,0:T(8,128)(2,1)S(1)}, u32[]{:S(2)}, u32[]{:S(2)}) %collective-permute-start.15) | collective-permute-done | bytes 73760 | tf_op jit(solution)/shard_map/ppermute | solution.py:146
  34.5 0.7 %collective-permute-done.13 = bf16[16,2304]{1,0:T(8,128)(2,1)S(1)} collective-permute-done((bf16[16,2304]{1,0:T(8,128)(2,1)S(1)}, bf16[16,2304]{1,0:T(8,128)(2,1)S(1)}, u32[]{:S(2)}, u32[]{:S(2)}) %collective-permute-start.13) | collective-permute-done | bytes 73760 | tf_op jit(solution)/shard_map/ppermute | solution.py:146
  35.3 2.2 %collective-permute-start.23 = (bf16[16,2304]{1,0:T(8,128)(2,1)S(1)}, bf16[16,2304]{1,0:T(8,128)(2,1)S(1)}, u32[]{:S(2)}, u32[]{:S(2)}) collective-permute-start(bf16[16,2304]{1,0:T(8,128)(2,1)S(1)} %fusion.20), channel_id=1, source_target_pairs={{0,12},{1,13},{2,14},{3,15},{4,8},{5,9},{6,10},{7,11},{8,4},{9,5},... | collective-permute-start | bytes 221192 | tf_op jit(solution)/shard_map/ppermute | solution.py:146
  37.5 2.3 %collective-permute-start.18 = (bf16[16,2304]{1,0:T(8,128)(2,1)S(1)}, bf16[16,2304]{1,0:T(8,128)(2,1)S(1)}, u32[]{:S(2)}, u32[]{:S(2)}) collective-permute-start(bf16[16,2304]{1,0:T(8,128)(2,1)S(1)} %fusion.20), channel_id=1, source_target_pairs={{0,4},{1,5},{2,6},{3,7},{4,0},{5,1},{6,2},{7,3},{8,12},{9,13},{10,... | collective-permute-start | bytes 221192 | tf_op jit(solution)/shard_map/ppermute | solution.py:146
  39.8 1.0 %collective-permute-start.17 = (bf16[16,2304]{1,0:T(8,128)(2,1)S(1)}, bf16[16,2304]{1,0:T(8,128)(2,1)S(1)}, u32[]{:S(2)}, u32[]{:S(2)}) collective-permute-start(bf16[16,2304]{1,0:T(8,128)(2,1)S(1)} %fusion.20), channel_id=1, source_target_pairs={{0,2},{1,3},{2,0},{3,1},{4,6},{5,7},{6,4},{7,5},{8,10},{9,11},{10,... | collective-permute-start | bytes 221192 | tf_op jit(solution)/shard_map/ppermute | solution.py:146
  40.8 0.8 %collective-permute-done.23 = bf16[16,2304]{1,0:T(8,128)(2,1)S(1)} collective-permute-done((bf16[16,2304]{1,0:T(8,128)(2,1)S(1)}, bf16[16,2304]{1,0:T(8,128)(2,1)S(1)}, u32[]{:S(2)}, u32[]{:S(2)}) %collective-permute-start.23) | collective-permute-done | bytes 73760 | tf_op jit(solution)/shard_map/ppermute | solution.py:146
  41.6 1.7 %collective-permute-start.24 = (bf16[16,2304]{1,0:T(8,128)(2,1)S(1)}, bf16[16,2304]{1,0:T(8,128)(2,1)S(1)}, u32[]{:S(2)}, u32[]{:S(2)}) collective-permute-start(bf16[16,2304]{1,0:T(8,128)(2,1)S(1)} %collective-permute-done.23), channel_id=1, source_target_pairs={{0,2},{1,3},{2,0},{3,1},{4,6},{5,7},{6,4},{7,5},{8,10},{9,11},{10,... | collective-permute-start | bytes 221192 | tf_op jit(solution)/shard_map/ppermute | solution.py:146
  43.2 1.5 %collective-permute-start.22 = (bf16[16,2304]{1,0:T(8,128)(2,1)S(1)}, bf16[16,2304]{1,0:T(8,128)(2,1)S(1)}, u32[]{:S(2)}, u32[]{:S(2)}) collective-permute-start(bf16[16,2304]{1,0:T(8,128)(2,1)S(1)} %collective-permute-done.21), channel_id=1, source_target_pairs={{0,2},{1,3},{2,0},{3,1},{4,6},{5,7},{6,4},{7,5},{8,10},{9,11},{10,... | collective-permute-start | bytes 221192 | tf_op jit(solution)/shard_map/ppermute | solution.py:146
  44.7 0.6 %collective-permute-start.19 = (bf16[16,2304]{1,0:T(8,128)(2,1)S(1)}, bf16[16,2304]{1,0:T(8,128)(2,1)S(1)}, u32[]{:S(2)}, u32[]{:S(2)}) collective-permute-start(bf16[16,2304]{1,0:T(8,128)(2,1)S(1)} %collective-permute-done.18), channel_id=1, source_target_pairs={{0,2},{1,3},{2,0},{3,1},{4,6},{5,7},{6,4},{7,5},{8,10},{9,11},{10,... | collective-permute-start | bytes 221192 | tf_op jit(solution)/shard_map/ppermute | solution.py:146
  45.3 1.2 %collective-permute-done.24 = bf16[16,2304]{1,0:T(8,128)(2,1)S(1)} collective-permute-done((bf16[16,2304]{1,0:T(8,128)(2,1)S(1)}, bf16[16,2304]{1,0:T(8,128)(2,1)S(1)}, u32[]{:S(2)}, u32[]{:S(2)}) %collective-permute-start.24) | collective-permute-done | bytes 73760 | tf_op jit(solution)/shard_map/ppermute | solution.py:146
  46.5 1.1 %collective-permute-done.22 = bf16[16,2304]{1,0:T(8,128)(2,1)S(1)} collective-permute-done((bf16[16,2304]{1,0:T(8,128)(2,1)S(1)}, bf16[16,2304]{1,0:T(8,128)(2,1)S(1)}, u32[]{:S(2)}, u32[]{:S(2)}) %collective-permute-start.22) | collective-permute-done | bytes 73760 | tf_op jit(solution)/shard_map/ppermute | solution.py:146
  47.7 1.4 %collective-permute-done.19 = bf16[16,2304]{1,0:T(8,128)(2,1)S(1)} collective-permute-done((bf16[16,2304]{1,0:T(8,128)(2,1)S(1)}, bf16[16,2304]{1,0:T(8,128)(2,1)S(1)}, u32[]{:S(2)}, u32[]{:S(2)}) %collective-permute-start.19) | collective-permute-done | bytes 73760 | tf_op jit(solution)/shard_map/ppermute | solution.py:146
  49.3 1.0 %own_totals.1 = (f32[128,2304]{1,0:T(8,128)S(1)}, f32[128,2304]{1,0:T(8,128)S(1)}) custom-call(bf16[128,128]{1,0:T(8,128)(2,1)S(1)} %get-tuple-element.39.codes_across, bf16[128,2304]{1,0:T(8,128)(2,1)S(1)} %subtract_convert_fusion.centered, bf16[128,2304]{1,0:T(8,128)(2,1)S(1)} %constant_dynamic-update-slice_fusion.10.errors, bf16[128,2304]{1,0:T(8,128)(2,1)S(1)} %copy-done), custom_call_target="tpu_custom_call" | custom-call | flops 226492416 | bytes 4718592 | tf_op jit(solution)/shard_map/own_totals/pallas_call | solution.py:41
  50.8 3.3 %update.1 = (bf16[128,2304]{1,0:T(8,128)(2,1)}, f32[128,2304]{1,0:T(8,128)}, f32[128,2304]{1,0:T(8,128)}, bf16[128,2304]{1,0:T(8,128)(2,1)}, f32[128,2304]{1,0:T(8,128)}, /*index=5*/f32[128,2304]{1,0:T(8,128)}) custom-call(bf16[128,128]{1,0:T(8,128)(2,1)S(1)} %bitcast.8, bf16[128,2304]{1,0:T(8,128)(2,1)S(1)} %collective-permute-done.11.centered, ...), custom_call_target="tpu_custom_call" | custom-call | flops 226492416 | bytes 12976128 | tf_op jit(solution)/shard_map/update/pallas_call | solution.py:119
  (75 shorter events, 3.5 us)
Async XLA Ops:
  0.6 9.2 %copy-start.9 = (f32[128]{0:T(128)S(1)}, f32[128]{0:T(128)}, u32[]{:S(2)}) copy-start(f32[128]{0:T(128)} %param.11) | copy-start | bytes 1540
  0.7 8.7 %copy-start = (bf16[128,2304]{1,0:T(8,128)(2,1)S(1)}, bf16[128,2304]{1,0:T(8,128)(2,1)}, u32[]{:S(2)}) copy-start(bf16[128,2304]{1,0:T(8,128)(2,1)} %refs_3_.1) | copy-start | bytes 1769476
  0.7 9.2 %copy-start.5 = (bf16[128,2304]{1,0:T(8,128)(2,1)S(1)}, bf16[128,2304]{1,0:T(8,128)(2,1)}, u32[]{:S(2)}) copy-start(bf16[128,2304]{1,0:T(8,128)(2,1)} %refs_2_.1) | copy-start | bytes 1769476
  0.7 17.9 %copy-start.8 = (f32[2304]{0:T(1024)S(1)}, f32[2304]{0:T(1024)}, u32[]{:S(2)}) copy-start(f32[2304]{0:T(1024)} %param.13) | copy-start | bytes 27652
  0.7 9.2 %collective-permute-start.3 = (bf16[16,2304]{1,0:T(8,128)(2,1)}, bf16[16,2304]{1,0:T(8,128)(2,1)S(1)}, u32[]{:S(2)}, u32[]{:S(2)}) collective-permute-start(bf16[16,2304]{1,0:T(8,128)(2,1)} %param.9), channel_id=1, source_target_pairs={{0,8},{1,9},{2,10},{3,11},{4,12},{5,13},{6,14},{7,15},{8,0},{9,1},... | collective-permute-start | bytes 221192 | tf_op jit(solution)/shard_map/ppermute | solution.py:146
  4.8 5.2 %collective-permute-start.1 = (bf16[16,2304]{1,0:T(8,128)(2,1)}, bf16[16,2304]{1,0:T(8,128)(2,1)S(1)}, u32[]{:S(2)}, u32[]{:S(2)}) collective-permute-start(bf16[16,2304]{1,0:T(8,128)(2,1)} %param.9), channel_id=1, source_target_pairs={{0,4},{1,5},{2,6},{3,7},{4,0},{5,1},{6,2},{7,3},{8,12},{9,13},{10,... | collective-permute-start | bytes 221192 | tf_op jit(solution)/shard_map/ppermute | solution.py:146
  6.4 4.7 %collective-permute-start = (bf16[16,2304]{1,0:T(8,128)(2,1)}, bf16[16,2304]{1,0:T(8,128)(2,1)S(1)}, u32[]{:S(2)}, u32[]{:S(2)}) collective-permute-start(bf16[16,2304]{1,0:T(8,128)(2,1)} %param.9), channel_id=1, source_target_pairs={{0,2},{1,3},{2,0},{3,1},{4,6},{5,7},{6,4},{7,5},{8,10},{9,11},{10,... | collective-permute-start | bytes 221192 | tf_op jit(solution)/shard_map/ppermute | solution.py:146
  7.9 6.4 %collective-permute-start.5 = (bf16[16,2304]{1,0:T(8,128)(2,1)}, bf16[16,2304]{1,0:T(8,128)(2,1)S(1)}, u32[]{:S(2)}, u32[]{:S(2)}) collective-permute-start(bf16[16,2304]{1,0:T(8,128)(2,1)} %param.9), channel_id=1, source_target_pairs={{0,12},{1,13},{2,14},{3,15},{4,8},{5,9},{6,10},{7,11},{8,4},{9,5},... | collective-permute-start | bytes 221192 | tf_op jit(solution)/shard_map/ppermute | solution.py:146
  8.1 1.3 %collective-permute-start.8 = (f32[128]{0:T(128)}, f32[128]{0:T(128)S(1)}, u32[]{:S(2)}, u32[]{:S(2)}) collective-permute-start(f32[128]{0:T(128)} %param.11), channel_id=1, source_target_pairs={{0,1},{1,0},{2,3},{3,2},{4,5},{5,4},{6,7},{7,6},{8,9},{9,8},{10,11... | collective-permute-start | bytes 1544 | tf_op jit(solution)/shard_map/ppermute | solution.py:153
  9.4 9.4 %collective-permute-start.10 = (bf16[128,2304]{1,0:T(8,128)(2,1)S(1)}, bf16[128,2304]{1,0:T(8,128)(2,1)S(1)}, u32[]{:S(2)}, u32[]{:S(2)}) collective-permute-start(bf16[128,2304]{1,0:T(8,128)(2,1)S(1)} %copy-done), channel_id=1, source_target_pairs={{0,1},{1,0},{2,3},{3,2},{4,5},{5,4},{6,7},{7,6},{8,9},{9,8},{10,11... | collective-permute-start | bytes 1769480 | tf_op jit(solution)/shard_map/ppermute | solution.py:153
  9.9 8.9 %collective-permute-start.7 = (bf16[128,2304]{1,0:T(8,128)(2,1)S(1)}, bf16[128,2304]{1,0:T(8,128)(2,1)S(1)}, u32[]{:S(2)}, u32[]{:S(2)}) collective-permute-start(bf16[128,2304]{1,0:T(8,128)(2,1)S(1)} %copy-done.5), channel_id=1, source_target_pairs={{0,1},{1,0},{2,3},{3,2},{4,5},{5,4},{6,7},{7,6},{8,9},{9,8},{10,11... | collective-permute-start | bytes 1769480 | tf_op jit(solution)/shard_map/ppermute | solution.py:153
  10.0 6.7 %collective-permute-start.4 = (bf16[16,2304]{1,0:T(8,128)(2,1)S(1)}, bf16[16,2304]{1,0:T(8,128)(2,1)S(1)}, u32[]{:S(2)}, u32[]{:S(2)}) collective-permute-start(bf16[16,2304]{1,0:T(8,128)(2,1)S(1)} %collective-permute-done.3), channel_id=1, source_target_pairs={{0,2},{1,3},{2,0},{3,1},{4,6},{5,7},{6,4},{7,5},{8,10},{9,11},{10,... | collective-permute-start | bytes 221192 | tf_op jit(solution)/shard_map/ppermute | solution.py:146
  11.0 5.7 %collective-permute-start.2 = (bf16[16,2304]{1,0:T(8,128)(2,1)S(1)}, bf16[16,2304]{1,0:T(8,128)(2,1)S(1)}, u32[]{:S(2)}, u32[]{:S(2)}) collective-permute-start(bf16[16,2304]{1,0:T(8,128)(2,1)S(1)} %collective-permute-done.1), channel_id=1, source_target_pairs={{0,2},{1,3},{2,0},{3,1},{4,6},{5,7},{6,4},{7,5},{8,10},{9,11},{10,... | collective-permute-start | bytes 221192 | tf_op jit(solution)/shard_map/ppermute | solution.py:146
  14.2 4.4 %collective-permute-start.6 = (bf16[16,2304]{1,0:T(8,128)(2,1)S(1)}, bf16[16,2304]{1,0:T(8,128)(2,1)S(1)}, u32[]{:S(2)}, u32[]{:S(2)}) collective-permute-start(bf16[16,2304]{1,0:T(8,128)(2,1)S(1)} %collective-permute-done.5), channel_id=1, source_target_pairs={{0,2},{1,3},{2,0},{3,1},{4,6},{5,7},{6,4},{7,5},{8,10},{9,11},{10,... | collective-permute-start | bytes 221192 | tf_op jit(solution)/shard_map/ppermute | solution.py:146
  19.7 2.1 %collective-permute-start.11 = (bf16[128,2304]{1,0:T(8,128)(2,1)S(1)}, bf16[128,2304]{1,0:T(8,128)(2,1)S(1)}, u32[]{:S(2)}, u32[]{:S(2)}) collective-permute-start(bf16[128,2304]{1,0:T(8,128)(2,1)S(1)} %subtract_convert_fusion.centered), channel_id=1, source_target_pairs={{0,1},{1,0},{2,3},{3,2},{4,5},{5,4},{6,7},{7,6},{8,9},{9,8},{10,11... | collective-permute-start | bytes 1769480 | tf_op jit(solution)/shard_map/ppermute | solution.py:153
  19.8 2.0 %collective-permute-start.9 = (bf16[128,128]{0,1:T(8,128)(2,1)S(1)}, bf16[128,128]{0,1:T(8,128)(2,1)S(1)}, u32[]{:S(2)}, u32[]{:S(2)}) collective-permute-start(bf16[128,128]{0,1:T(8,128)(2,1)S(1)} %get-tuple-element.40), channel_id=1, source_target_pairs={{0,1},{1,0},{2,3},{3,2},{4,5},{5,4},{6,7},{7,6},{8,9},{9,8},{10,11... | collective-permute-start | bytes 98312 | tf_op jit(solution)/shard_map/ppermute | solution.py:153
  20.3 6.7 %collective-permute-start.14 = (bf16[32,2304]{1,0:T(8,128)(2,1)S(1)}, bf16[32,2304]{1,0:T(8,128)(2,1)S(1)}, u32[]{:S(2)}, u32[]{:S(2)}) collective-permute-start(bf16[32,2304]{1,0:T(8,128)(2,1)S(1)} %pad_maximum_fusion.2), channel_id=1, source_target_pairs={{0,2},{1,3},{2,0},{3,1},{4,6},{5,7},{6,4},{7,5},{8,10},{9,11},{10,... | collective-permute-start | bytes 442376 | tf_op jit(solution)/shard_map/ppermute | solution.py:146
  22.3 7.8 %collective-permute-start.12 = (bf16[32,2304]{1,0:T(8,128)(2,1)S(1)}, bf16[32,2304]{1,0:T(8,128)(2,1)S(1)}, u32[]{:S(2)}, u32[]{:S(2)}) collective-permute-start(bf16[32,2304]{1,0:T(8,128)(2,1)S(1)} %pad_maximum_fusion.3), channel_id=1, source_target_pairs={{0,2},{1,3},{2,0},{3,1},{4,6},{5,7},{6,4},{7,5},{8,10},{9,11},{10,... | collective-permute-start | bytes 442376 | tf_op jit(solution)/shard_map/ppermute | solution.py:146
  27.1 7.5 %collective-permute-start.15 = (bf16[16,2304]{1,0:T(8,128)(2,1)S(1)}, bf16[16,2304]{1,0:T(8,128)(2,1)S(1)}, u32[]{:S(2)}, u32[]{:S(2)}) collective-permute-start(bf16[16,2304]{1,0:T(8,128)(2,1)S(1)} %get-tuple-element.33), channel_id=1, source_target_pairs={{0,8},{1,9},{2,10},{3,11},{4,12},{5,13},{6,14},{7,15},{8,0},{9,1},... | collective-permute-start | bytes 221192 | tf_op jit(solution)/shard_map/ppermute | solution.py:146
  28.0 6.5 %collective-permute-start.16 = (bf16[16,2304]{1,0:T(8,128)(2,1)S(1)}, bf16[16,2304]{1,0:T(8,128)(2,1)S(1)}, u32[]{:S(2)}, u32[]{:S(2)}) collective-permute-start(bf16[16,2304]{1,0:T(8,128)(2,1)S(1)} %get-tuple-element.34), channel_id=1, source_target_pairs={{0,12},{1,13},{2,14},{3,15},{4,8},{5,9},{6,10},{7,11},{8,4},{9,5},... | collective-permute-start | bytes 221192 | tf_op jit(solution)/shard_map/ppermute | solution.py:146
  30.0 5.2 %collective-permute-start.13 = (bf16[16,2304]{1,0:T(8,128)(2,1)S(1)}, bf16[16,2304]{1,0:T(8,128)(2,1)S(1)}, u32[]{:S(2)}, u32[]{:S(2)}) collective-permute-start(bf16[16,2304]{1,0:T(8,128)(2,1)S(1)} %fusion.15), channel_id=1, source_target_pairs={{0,4},{1,5},{2,6},{3,7},{4,0},{5,1},{6,2},{7,3},{8,12},{9,13},{10,... | collective-permute-start | bytes 221192 | tf_op jit(solution)/shard_map/ppermute | solution.py:146
  35.2 15.5 %copy-start.4 = (f32[128,2304]{1,0:T(8,128)S(1)}, f32[128,2304]{1,0:T(8,128)}, u32[]{:S(2)}) copy-start(f32[128,2304]{1,0:T(8,128)} %refs_7_.1) | copy-start | bytes 3538948
  35.3 13.9 %copy-start.6 = (bf16[16,2304]{1,0:T(8,128)(2,1)}, bf16[16,2304]{1,0:T(8,128)(2,1)S(1)}, u32[]{:S(2)}) copy-start(bf16[16,2304]{1,0:T(8,128)(2,1)S(1)} %fusion.20) | copy-start | bytes 221188
  35.3 6.2 %collective-permute-start.23 = (bf16[16,2304]{1,0:T(8,128)(2,1)S(1)}, bf16[16,2304]{1,0:T(8,128)(2,1)S(1)}, u32[]{:S(2)}, u32[]{:S(2)}) collective-permute-start(bf16[16,2304]{1,0:T(8,128)(2,1)S(1)} %fusion.20), channel_id=1, source_target_pairs={{0,12},{1,13},{2,14},{3,15},{4,8},{5,9},{6,10},{7,11},{8,4},{9,5},... | collective-permute-start | bytes 221192 | tf_op jit(solution)/shard_map/ppermute | solution.py:146
  37.5 5.7 %collective-permute-start.21 = (bf16[16,2304]{1,0:T(8,128)(2,1)S(1)}, bf16[16,2304]{1,0:T(8,128)(2,1)S(1)}, u32[]{:S(2)}, u32[]{:S(2)}) collective-permute-start(bf16[16,2304]{1,0:T(8,128)(2,1)S(1)} %fusion.20), channel_id=1, source_target_pairs={{0,8},{1,9},{2,10},{3,11},{4,12},{5,13},{6,14},{7,15},{8,0},{9,1},... | collective-permute-start | bytes 221192 | tf_op jit(solution)/shard_map/ppermute | solution.py:146
  37.5 7.2 %collective-permute-start.18 = (bf16[16,2304]{1,0:T(8,128)(2,1)S(1)}, bf16[16,2304]{1,0:T(8,128)(2,1)S(1)}, u32[]{:S(2)}, u32[]{:S(2)}) collective-permute-start(bf16[16,2304]{1,0:T(8,128)(2,1)S(1)} %fusion.20), channel_id=1, source_target_pairs={{0,4},{1,5},{2,6},{3,7},{4,0},{5,1},{6,2},{7,3},{8,12},{9,13},{10,... | collective-permute-start | bytes 221192 | tf_op jit(solution)/shard_map/ppermute | solution.py:146
  39.8 5.5 %collective-permute-start.17 = (bf16[16,2304]{1,0:T(8,128)(2,1)S(1)}, bf16[16,2304]{1,0:T(8,128)(2,1)S(1)}, u32[]{:S(2)}, u32[]{:S(2)}) collective-permute-start(bf16[16,2304]{1,0:T(8,128)(2,1)S(1)} %fusion.20), channel_id=1, source_target_pairs={{0,2},{1,3},{2,0},{3,1},{4,6},{5,7},{6,4},{7,5},{8,10},{9,11},{10,... | collective-permute-start | bytes 221192 | tf_op jit(solution)/shard_map/ppermute | solution.py:146
  41.6 4.9 %collective-permute-start.24 = (bf16[16,2304]{1,0:T(8,128)(2,1)S(1)}, bf16[16,2304]{1,0:T(8,128)(2,1)S(1)}, u32[]{:S(2)}, u32[]{:S(2)}) collective-permute-start(bf16[16,2304]{1,0:T(8,128)(2,1)S(1)} %collective-permute-done.23), channel_id=1, source_target_pairs={{0,2},{1,3},{2,0},{3,1},{4,6},{5,7},{6,4},{7,5},{8,10},{9,11},{10,... | collective-permute-start | bytes 221192 | tf_op jit(solution)/shard_map/ppermute | solution.py:146
  43.2 4.4 %collective-permute-start.22 = (bf16[16,2304]{1,0:T(8,128)(2,1)S(1)}, bf16[16,2304]{1,0:T(8,128)(2,1)S(1)}, u32[]{:S(2)}, u32[]{:S(2)}) collective-permute-start(bf16[16,2304]{1,0:T(8,128)(2,1)S(1)} %collective-permute-done.21), channel_id=1, source_target_pairs={{0,2},{1,3},{2,0},{3,1},{4,6},{5,7},{6,4},{7,5},{8,10},{9,11},{10,... | collective-permute-start | bytes 221192 | tf_op jit(solution)/shard_map/ppermute | solution.py:146
  44.7 4.4 %collective-permute-start.19 = (bf16[16,2304]{1,0:T(8,128)(2,1)S(1)}, bf16[16,2304]{1,0:T(8,128)(2,1)S(1)}, u32[]{:S(2)}, u32[]{:S(2)}) collective-permute-start(bf16[16,2304]{1,0:T(8,128)(2,1)S(1)} %collective-permute-done.18), channel_id=1, source_target_pairs={{0,2},{1,3},{2,0},{3,1},{4,6},{5,7},{6,4},{7,5},{8,10},{9,11},{10,... | collective-permute-start | bytes 221192 | tf_op jit(solution)/shard_map/ppermute | solution.py:146
  47.6 2.6 %collective-permute-start.25 = (bf16[64,2304]{1,0:T(8,128)(2,1)S(1)}, bf16[64,2304]{1,0:T(8,128)(2,1)S(1)}, u32[]{:S(2)}, u32[]{:S(2)}) collective-permute-start(bf16[64,2304]{1,0:T(8,128)(2,1)S(1)} %pad_maximum_fusion.1), channel_id=1, source_target_pairs={{0,1},{1,0},{2,3},{3,2},{4,5},{5,4},{6,7},{7,6},{8,9},{9,8},{10,11... | collective-permute-start | bytes 884744 | tf_op jit(solution)/shard_map/ppermute | solution.py:153
  49.1 1.6 %collective-permute-start.20 = (bf16[64,2304]{1,0:T(8,128)(2,1)S(1)}, bf16[64,2304]{1,0:T(8,128)(2,1)S(1)}, u32[]{:S(2)}, u32[]{:S(2)}) collective-permute-start(bf16[64,2304]{1,0:T(8,128)(2,1)S(1)} %pad_maximum_fusion), channel_id=1, source_target_pairs={{0,1},{1,0},{2,3},{3,2},{4,5},{5,4},{6,7},{7,6},{8,9},{9,8},{10,11... | collective-permute-start | bytes 884744 | tf_op jit(solution)/shard_map/ppermute | solution.py:153
  (4 other events, 14.9 us)

commit v20 on v17

--- a/solution.py
+++ b/solution.py
@@ -19,7 +19,18 @@
     )
 
 
-def own_kernel(columns, codes_across, centered, errors, decoder, encoder_total, decoder_total):
+def by_parity(placed, errors, block):
+    count = placed.shape[0] // block
+    blocks = [(one, at) for one in errors for at in range(0, one.shape[0], block)]
+    for k, (one, at) in enumerate(blocks):
+        place = k // 2 + k % 2 * (count // 2)
+        placed[pl.ds(place * block, block), :] = one[pl.ds(at, block), :]
+
+
+def own_kernel(
+    columns, block, codes_across, centered, sent, decoder, encoder_total, decoder_total, errors
+):
+    by_parity(errors, [sent], block)
     codes_t = codes_across[...]
     signal = inner_last(decoder[...], errors[...])
     delta_t = jnp.where(codes_t.astype(jnp.float32) > 0, signal, 0.0).astype(jnp.bfloat16)
@@ -33,16 +44,17 @@
         )
 
 
-def own_totals(codes_across, centered, errors, decoder):
+def own_totals(codes_across, centered, errors, decoder, block):
     latents, width = decoder.shape
     rows = centered.shape[0]
     vmem = pl.BlockSpec(memory_space=pltpu.VMEM)
     total = jax.ShapeDtypeStruct((latents, width), jnp.float32)
     return pl.pallas_call(
-        functools.partial(own_kernel, columns_of(width)),
+        functools.partial(own_kernel, columns_of(width), block),
         out_shape=(total, total),
         in_specs=[vmem] * 4,
         out_specs=[vmem] * 2,
+        scratch_shapes=[pltpu.VMEM((rows, width), jnp.bfloat16)],
         compiler_params=pltpu.CompilerParams(vmem_limit_bytes=16 * 1024 * 1024 + 8 * rows * width),
         cost_estimate=pl.CostEstimate(
             flops=6 * latents * width * rows,
@@ -57,7 +69,7 @@
     return next(c for c in (256, 128, width) if width % c == 0)
 
 
-def update_kernel(columns, rows_total, codes_across, centered, *refs):
+def update_kernel(columns, block, rows_total, codes_across, centered, *refs):
     blocks = len(refs) - 22
     errors, (encoder, decoder) = refs[:blocks], refs[blocks : blocks + 2]
     moments = refs[blocks + 2 : blocks + 6]
@@ -71,10 +83,7 @@
         at = pl.ds(t * columns, columns)
         return pltpu.make_async_copy(held[i].at[:, at], outs[i].at[:, at], sem.at[t, i])
 
-    start = 0
-    for one in errors:
-        error_all[pl.ds(start, one.shape[0]), :] = one[...]
-        start += one.shape[0]
+    by_parity(error_all, errors, block)
     first = (1.0 - beta_first) / rows_total
     second = (1.0 - beta_second) / (rows_total * rows_total)
 
@@ -107,7 +116,7 @@
             write(t, i).wait()
 
 
-def update(total_rows, codes_across, centered, errors, weights, moments, totals):
+def update(total_rows, codes_across, centered, errors, block, weights, moments, totals):
     latents, width = weights[0].shape
     rows = centered.shape[0]
     columns = columns_of(width)
@@ -117,7 +126,7 @@
     wide = pltpu.VMEM((latents, width), jnp.float32)
     narrow = pltpu.VMEM((latents, width), jnp.bfloat16)
     return pl.pallas_call(
-        functools.partial(update_kernel, columns, float(total_rows)),
+        functools.partial(update_kernel, columns, block, float(total_rows)),
         out_shape=(half, full, full, half, full, full),
         in_specs=[vmem] * (len(errors) + 10),
         out_specs=[pl.BlockSpec(memory_space=pl.ANY)] * 6,
@@ -179,7 +188,8 @@
     chips = size // 2
     total_rows = rows_here * size
 
-    rows_core = jnp.concatenate(in_turn(*gather_chips(activations, chips)), 0)
+    even, odd = gather_chips(activations, chips)
+    rows_core = jnp.concatenate(even + odd, 0)
     encoder_both = jnp.concatenate([encoder, to_other_core(encoder)], 0)
     decoder_both = jnp.concatenate([decoder, to_other_core(decoder)], 0)
     bias_both = jnp.concatenate([encoder_bias, to_other_core(encoder_bias)], 0)
@@ -190,31 +200,28 @@
     )
     other_codes = to_other_core(codes[:, latents_here:])
 
-    quad = 4 * rows_here
-    parts = []
-    for rows in (slice(0, quad), slice(quad, None)):
-        sums = jnp.dot(codes[rows], decoder_both, preferred_element_type=jnp.float32)
-        parts += [sums[at : at + rows_here] for at in range(0, sums.shape[0], rows_here)]
-
-    def given(first, last):
-        return jnp.concatenate(parts[first + 1 : last : 2], 0).astype(jnp.bfloat16)
+    split, half = 2 * rows_here, chips // 2 * rows_here
+    given = jnp.dot(codes[half:], decoder_both, preferred_element_type=jnp.float32).astype(
+        jnp.bfloat16
+    )
 
     def pair_sums(first, last, sent):
-        came = to_chip(sent, 1)
-        return [
-            parts[k] + came[at * rows_here : (at + 1) * rows_here].astype(jnp.float32)
-            for at, k in enumerate(range(first, last, 2))
-        ]
-
-    far_sent = given(4, chips)
-    far = [one.astype(jnp.bfloat16) for one in pair_sums(4, chips, far_sent)]
+        return jnp.dot(
+            codes[first:last], decoder_both, preferred_element_type=jnp.float32
+        ) + to_chip(sent, 1).astype(jnp.float32)
+
+    far_sent = given[split:]
+    far = pair_sums(split, half, far_sent).astype(jnp.bfloat16)
     later_centered, _ = lax.optimization_barrier((centered, far_sent))
     other_centered = to_other_core(later_centered)
-    near_sent, _ = lax.optimization_barrier((given(0, 4), (other_codes, other_centered)))
-    own, near = pair_sums(0, 4, near_sent)
-    summed = own + to_chip(near.astype(jnp.bfloat16), 2).astype(jnp.float32)
-    for k, one in enumerate(far, 2):
-        summed = summed + to_chip(one, 2 * k).astype(jnp.float32)
+    near_sent, _ = lax.optimization_barrier((given[:split], (other_codes, other_centered)))
+    near = pair_sums(0, split, near_sent)
+    summed = near[:rows_here] + to_chip(near[rows_here:].astype(jnp.bfloat16), 2).astype(
+        jnp.float32
+    )
+    for k in range(2, chips // 2):
+        block = far[(k - 2) * rows_here : (k - 1) * rows_here]
+        summed = summed + to_chip(block, 2 * k).astype(jnp.float32)
     row_error = (summed - centered[:rows_here].astype(jnp.float32)).astype(jnp.bfloat16)
 
     row_error, other_codes, other_centered = lax.optimization_barrier(
@@ -223,7 +230,7 @@
     blocks = in_turn(*gather_chips(row_error, chips))
     errors = jnp.concatenate(blocks, 0)
     other_errors = [to_other_core(jnp.concatenate(one, 0)) for one in (blocks[:4], blocks[4:])]
-    totals = own_totals(codes[:, :latents_here].T, centered, errors, decoder)
+    totals = own_totals(codes[:, :latents_here].T, centered, errors, decoder, rows_here)
     (
         encoder_next,
         encoder_moment_next,
@@ -236,6 +243,7 @@
         other_codes.T,
         other_centered,
         other_errors,
+        rows_here,
         (encoder, decoder),
         (encoder_moment, encoder_square, decoder_moment, decoder_square),
         totals,

time: 54.5 us -> 57.8 us (1.061)
  waiting for transfers between devices: 19.6 us -> 22.8 us
    ppermute x19, waiting for transfers between devices: 17.4 us -> 22.2 us  [to_chip(): lax.ppermute(block, 'latent', [(i, i ^ 2 * distance) for i in range(size)])]
    ppermute x7, waiting for transfers between devices: 2.2 us -> 0.61 us  [to_other_core(): return lax.ppermute(block, 'latent', [(i, i ^ 1) for i in range(size)])]
    dot_general x2 -> x3, matrix products: 0.79 us -> 1.19 us  [the longest x2 0.76 us: pair_sums(): jnp.dot(codes[first:last], decoder_both, preferred_element_type=jnp.float32)]
  transfers between devices with their start and end apart: 26 -> 26, of which waited for: 15 -> 13; matrix products, arithmetic and copies ran while one was open for 4% -> 4% of each run, Pallas kernels for 2% -> 2%
where the time goes in v20:
time: 57.8 us; the launch traced here: 57.6 us
  starting transfers between devices  26.2 us (45%)
  waiting for transfers between devices  22.8 us (39%)
  Pallas kernels  4.23 us (7%)
  matrix products  1.66 us (3%)
  local copies, waits for them, and re-layouts  1.5 us (3%)
  between operations  0.99 us (2%)
    ppermute x19, starting transfers between devices, to_chip(): lax.ppermute(block, 'latent', [(i, i ^ 2 * distance) for i in range(size)])  25.3 us
    ppermute x19, waiting for transfers between devices, to_chip(): lax.ppermute(block, 'latent', [(i, i ^ 2 * distance) for i in range(size)])  22.2 us
    pallas_call x1, Pallas kernels, update(): pl.pallas_call(functools.partial(update_kernel, columns, block, float(tot...  3.26 us
    unnamed x35, local copies, waits for them, and re-layouts  1.39 us
  transfers between devices with their start and end apart: 26, of which 13 were waited for; matrix products, arithmetic and copies ran while one was open for 4% of the time, Pallas kernels for 2%

profile of v20, /device:TPU:0, one launch (start us, length us, event | category | flops | bytes accessed | tf_op | source)
XLA Modules:
  0.0 57.6 jit_solution(4189032402412328687)
XLA Ops:
  0.7 5.1 %collective-permute-start.2 = (bf16[16,2304]{1,0:T(8,128)(2,1)}, bf16[16,2304]{1,0:T(8,128)(2,1)S(1)}, u32[]{:S(2)}, u32[]{:S(2)}) collective-permute-start(bf16[16,2304]{1,0:T(8,128)(2,1)} %param.9), channel_id=1, source_target_pairs={{0,12},{1,13},{2,14},{3,15},{4,8},{5,9},{6,10},{7,11},{8,4},{9,5},... | collective-permute-start | bytes 221192 | tf_op jit(solution)/shard_map/ppermute | solution.py:155
  5.8 0.6 %collective-permute-start = (bf16[16,2304]{1,0:T(8,128)(2,1)}, bf16[16,2304]{1,0:T(8,128)(2,1)S(1)}, u32[]{:S(2)}, u32[]{:S(2)}) collective-permute-start(bf16[16,2304]{1,0:T(8,128)(2,1)} %param.9), channel_id=1, source_target_pairs={{0,4},{1,5},{2,6},{3,7},{4,0},{5,1},{6,2},{7,3},{8,12},{9,13},{10,... | collective-permute-start | bytes 221192 | tf_op jit(solution)/shard_map/ppermute | solution.py:155
  6.4 1.7 %collective-permute-start.3 = (bf16[16,2304]{1,0:T(8,128)(2,1)}, bf16[16,2304]{1,0:T(8,128)(2,1)S(1)}, u32[]{:S(2)}, u32[]{:S(2)}) collective-permute-start(bf16[16,2304]{1,0:T(8,128)(2,1)} %param.9), channel_id=1, source_target_pairs={{0,2},{1,3},{2,0},{3,1},{4,6},{5,7},{6,4},{7,5},{8,10},{9,11},{10,... | collective-permute-start | bytes 221192 | tf_op jit(solution)/shard_map/ppermute | solution.py:155
  8.1 1.1 %constant_dynamic-update-slice_fusion.9 = bf16[256,2304]{1,0:T(8,128)(2,1)S(1)} fusion(bf16[128,2304]{1,0:T(8,128)(2,1)} %refs_3_.1), kind=kLoop, calls=%fused_computation.32 | loop fusion | bytes 1179648
  10.0 2.3 %collective-permute-done.1 = bf16[16,2304]{1,0:T(8,128)(2,1)S(1)} collective-permute-done((bf16[16,2304]{1,0:T(8,128)(2,1)}, bf16[16,2304]{1,0:T(8,128)(2,1)S(1)}, u32[]{:S(2)}, u32[]{:S(2)}) %collective-permute-start.1) | collective-permute-done | bytes 73760 | tf_op jit(solution)/shard_map/ppermute | solution.py:155
  12.2 1.5 %collective-permute-start.6 = (bf16[16,2304]{1,0:T(8,128)(2,1)S(1)}, bf16[16,2304]{1,0:T(8,128)(2,1)S(1)}, u32[]{:S(2)}, u32[]{:S(2)}) collective-permute-start(bf16[16,2304]{1,0:T(8,128)(2,1)S(1)} %collective-permute-done.2), channel_id=1, source_target_pairs={{0,2},{1,3},{2,0},{3,1},{4,6},{5,7},{6,4},{7,5},{8,10},{9,11},{10,... | collective-permute-start | bytes 221192 | tf_op jit(solution)/shard_map/ppermute | solution.py:155
  13.7 0.5 collective-permute-start.5
  14.3 1.6 %collective-permute-start.4 = (bf16[16,2304]{1,0:T(8,128)(2,1)S(1)}, bf16[16,2304]{1,0:T(8,128)(2,1)S(1)}, u32[]{:S(2)}, u32[]{:S(2)}) collective-permute-start(bf16[16,2304]{1,0:T(8,128)(2,1)S(1)} %collective-permute-done), channel_id=1, source_target_pairs={{0,2},{1,3},{2,0},{3,1},{4,6},{5,7},{6,4},{7,5},{8,10},{9,11},{10,... | collective-permute-start | bytes 221192 | tf_op jit(solution)/shard_map/ppermute | solution.py:155
  15.9 3.8 %collective-permute-done.4 = bf16[16,2304]{1,0:T(8,128)(2,1)S(1)} collective-permute-done((bf16[16,2304]{1,0:T(8,128)(2,1)S(1)}, bf16[16,2304]{1,0:T(8,128)(2,1)S(1)}, u32[]{:S(2)}, u32[]{:S(2)}) %collective-permute-start.4) | collective-permute-done | bytes 73760 | tf_op jit(solution)/shard_map/ppermute | solution.py:155
  19.9 0.5 fusion.11
  20.9 1.1 %collective-permute-start.14 = (bf16[32,2304]{1,0:T(8,128)(2,1)S(1)}, bf16[32,2304]{1,0:T(8,128)(2,1)S(1)}, u32[]{:S(2)}, u32[]{:S(2)}) collective-permute-start(bf16[32,2304]{1,0:T(8,128)(2,1)S(1)} %get-tuple-element.33), channel_id=1, source_target_pairs={{0,2},{1,3},{2,0},{3,1},{4,6},{5,7},{6,4},{7,5},{8,10},{9,11},{10,... | collective-permute-start | bytes 442376 | tf_op jit(solution)/shard_map/ppermute | solution.py:155
  22.2 5.0 %collective-permute-done.14 = bf16[32,2304]{1,0:T(8,128)(2,1)S(1)} collective-permute-done((bf16[32,2304]{1,0:T(8,128)(2,1)S(1)}, bf16[32,2304]{1,0:T(8,128)(2,1)S(1)}, u32[]{:S(2)}, u32[]{:S(2)}) %collective-permute-start.14) | collective-permute-done | bytes 147488 | tf_op jit(solution)/shard_map/ppermute | solution.py:155
  27.6 1.1 %collective-permute-start.12 = (bf16[32,2304]{1,0:T(8,128)(2,1)S(1)}, bf16[32,2304]{1,0:T(8,128)(2,1)S(1)}, u32[]{:S(2)}, u32[]{:S(2)}) collective-permute-start(bf16[32,2304]{1,0:T(8,128)(2,1)S(1)} %get-tuple-element.21), channel_id=1, source_target_pairs={{0,2},{1,3},{2,0},{3,1},{4,6},{5,7},{6,4},{7,5},{8,10},{9,11},{10,... | collective-permute-start | bytes 442376 | tf_op jit(solution)/shard_map/ppermute | solution.py:155
  28.8 1.6 %collective-permute-start.15 = (bf16[16,2304]{1,0:T(8,128)(2,1)S(1)}, bf16[16,2304]{1,0:T(8,128)(2,1)S(1)}, u32[]{:S(2)}, u32[]{:S(2)}) collective-permute-start(bf16[16,2304]{1,0:T(8,128)(2,1)S(1)} %get-tuple-element.35), channel_id=1, source_target_pairs={{0,8},{1,9},{2,10},{3,11},{4,12},{5,13},{6,14},{7,15},{8,0},{9,1},... | collective-permute-start | bytes 221192 | tf_op jit(solution)/shard_map/ppermute | solution.py:155
  30.3 1.2 %collective-permute-start.16 = (bf16[16,2304]{1,0:T(8,128)(2,1)S(1)}, bf16[16,2304]{1,0:T(8,128)(2,1)S(1)}, u32[]{:S(2)}, u32[]{:S(2)}) collective-permute-start(bf16[16,2304]{1,0:T(8,128)(2,1)S(1)} %get-tuple-element.36), channel_id=1, source_target_pairs={{0,12},{1,13},{2,14},{3,15},{4,8},{5,9},{6,10},{7,11},{8,4},{9,5},... | collective-permute-start | bytes 221192 | tf_op jit(solution)/shard_map/ppermute | solution.py:155
  31.5 1.6 %collective-permute-done.12 = bf16[32,2304]{1,0:T(8,128)(2,1)S(1)} collective-permute-done((bf16[32,2304]{1,0:T(8,128)(2,1)S(1)}, bf16[32,2304]{1,0:T(8,128)(2,1)S(1)}, u32[]{:S(2)}, u32[]{:S(2)}) %collective-permute-start.12) | collective-permute-done | bytes 147488 | tf_op jit(solution)/shard_map/ppermute | solution.py:155
  33.6 3.1 %collective-permute-done.15 = bf16[16,2304]{1,0:T(8,128)(2,1)S(1)} collective-permute-done((bf16[16,2304]{1,0:T(8,128)(2,1)S(1)}, bf16[16,2304]{1,0:T(8,128)(2,1)S(1)}, u32[]{:S(2)}, u32[]{:S(2)}) %collective-permute-start.15) | collective-permute-done | bytes 73760 | tf_op jit(solution)/shard_map/ppermute | solution.py:155
  36.7 0.5 collective-permute-done.16
  37.2 0.8 %collective-permute-done.13 = bf16[16,2304]{1,0:T(8,128)(2,1)S(1)} collective-permute-done((bf16[16,2304]{1,0:T(8,128)(2,1)S(1)}, bf16[16,2304]{1,0:T(8,128)(2,1)S(1)}, u32[]{:S(2)}, u32[]{:S(2)}) %collective-permute-start.13) | collective-permute-done | bytes 73760 | tf_op jit(solution)/shard_map/ppermute | solution.py:155
  38.1 2.3 %collective-permute-start.23 = (bf16[16,2304]{1,0:T(8,128)(2,1)S(1)}, bf16[16,2304]{1,0:T(8,128)(2,1)S(1)}, u32[]{:S(2)}, u32[]{:S(2)}) collective-permute-start(bf16[16,2304]{1,0:T(8,128)(2,1)S(1)} %fusion.17), channel_id=1, source_target_pairs={{0,12},{1,13},{2,14},{3,15},{4,8},{5,9},{6,10},{7,11},{8,4},{9,5},... | collective-permute-start | bytes 221192 | tf_op jit(solution)/shard_map/ppermute | solution.py:155
  40.4 2.1 %collective-permute-start.18 = (bf16[16,2304]{1,0:T(8,128)(2,1)S(1)}, bf16[16,2304]{1,0:T(8,128)(2,1)S(1)}, u32[]{:S(2)}, u32[]{:S(2)}) collective-permute-start(bf16[16,2304]{1,0:T(8,128)(2,1)S(1)} %fusion.17), channel_id=1, source_target_pairs={{0,4},{1,5},{2,6},{3,7},{4,0},{5,1},{6,2},{7,3},{8,12},{9,13},{10,... | collective-permute-start | bytes 221192 | tf_op jit(solution)/shard_map/ppermute | solution.py:155
  42.5 1.0 %collective-permute-start.17 = (bf16[16,2304]{1,0:T(8,128)(2,1)S(1)}, bf16[16,2304]{1,0:T(8,128)(2,1)S(1)}, u32[]{:S(2)}, u32[]{:S(2)}) collective-permute-start(bf16[16,2304]{1,0:T(8,128)(2,1)S(1)} %fusion.17), channel_id=1, source_target_pairs={{0,2},{1,3},{2,0},{3,1},{4,6},{5,7},{6,4},{7,5},{8,10},{9,11},{10,... | collective-permute-start | bytes 221192 | tf_op jit(solution)/shard_map/ppermute | solution.py:155
  43.5 0.8 %collective-permute-done.23 = bf16[16,2304]{1,0:T(8,128)(2,1)S(1)} collective-permute-done((bf16[16,2304]{1,0:T(8,128)(2,1)S(1)}, bf16[16,2304]{1,0:T(8,128)(2,1)S(1)}, u32[]{:S(2)}, u32[]{:S(2)}) %collective-permute-start.23) | collective-permute-done | bytes 73760 | tf_op jit(solution)/shard_map/ppermute | solution.py:155
  44.3 1.7 %collective-permute-start.24 = (bf16[16,2304]{1,0:T(8,128)(2,1)S(1)}, bf16[16,2304]{1,0:T(8,128)(2,1)S(1)}, u32[]{:S(2)}, u32[]{:S(2)}) collective-permute-start(bf16[16,2304]{1,0:T(8,128)(2,1)S(1)} %collective-permute-done.23), channel_id=1, source_target_pairs={{0,2},{1,3},{2,0},{3,1},{4,6},{5,7},{6,4},{7,5},{8,10},{9,11},{10,... | collective-permute-start | bytes 221192 | tf_op jit(solution)/shard_map/ppermute | solution.py:155
  46.0 1.0 %collective-permute-done.21 = bf16[16,2304]{1,0:T(8,128)(2,1)S(1)} collective-permute-done((bf16[16,2304]{1,0:T(8,128)(2,1)S(1)}, bf16[16,2304]{1,0:T(8,128)(2,1)S(1)}, u32[]{:S(2)}, u32[]{:S(2)}) %collective-permute-start.21) | collective-permute-done | bytes 73760 | tf_op jit(solution)/shard_map/ppermute | solution.py:155
  47.0 0.9 %collective-permute-start.22 = (bf16[16,2304]{1,0:T(8,128)(2,1)S(1)}, bf16[16,2304]{1,0:T(8,128)(2,1)S(1)}, u32[]{:S(2)}, u32[]{:S(2)}) collective-permute-start(bf16[16,2304]{1,0:T(8,128)(2,1)S(1)} %collective-permute-done.21), channel_id=1, source_target_pairs={{0,2},{1,3},{2,0},{3,1},{4,6},{5,7},{6,4},{7,5},{8,10},{9,11},{10,... | collective-permute-start | bytes 221192 | tf_op jit(solution)/shard_map/ppermute | solution.py:155
  47.9 1.1 %collective-permute-start.19 = (bf16[16,2304]{1,0:T(8,128)(2,1)S(1)}, bf16[16,2304]{1,0:T(8,128)(2,1)S(1)}, u32[]{:S(2)}, u32[]{:S(2)}) collective-permute-start(bf16[16,2304]{1,0:T(8,128)(2,1)S(1)} %collective-permute-done.18), channel_id=1, source_target_pairs={{0,2},{1,3},{2,0},{3,1},{4,6},{5,7},{6,4},{7,5},{8,10},{9,11},{10,... | collective-permute-start | bytes 221192 | tf_op jit(solution)/shard_map/ppermute | solution.py:155
  49.1 2.6 %collective-permute-done.22 = bf16[16,2304]{1,0:T(8,128)(2,1)S(1)} collective-permute-done((bf16[16,2304]{1,0:T(8,128)(2,1)S(1)}, bf16[16,2304]{1,0:T(8,128)(2,1)S(1)}, u32[]{:S(2)}, u32[]{:S(2)}) %collective-permute-start.22) | collective-permute-done | bytes 73760 | tf_op jit(solution)/shard_map/ppermute | solution.py:155
  51.8 0.7 %collective-permute-done.19 = bf16[16,2304]{1,0:T(8,128)(2,1)S(1)} collective-permute-done((bf16[16,2304]{1,0:T(8,128)(2,1)S(1)}, bf16[16,2304]{1,0:T(8,128)(2,1)S(1)}, u32[]{:S(2)}, u32[]{:S(2)}) %collective-permute-start.19) | collective-permute-done | bytes 73760 | tf_op jit(solution)/shard_map/ppermute | solution.py:155
  52.7 1.0 %own_totals.1 = (f32[128,2304]{1,0:T(8,128)S(1)}, f32[128,2304]{1,0:T(8,128)S(1)}) custom-call(bf16[128,128]{1,0:T(8,128)(2,1)S(1)} %get-tuple-element.37.codes_across, bf16[128,2304]{1,0:T(8,128)(2,1)S(1)} %subtract_convert_fusion.centered, bf16[128,2304]{1,0:T(8,128)(2,1)S(1)} %constant_dynamic-update-slice_fusion.10.sent, bf16[128,2304]{1,0:T(8,128)(2,1)S(1)} %copy-done), custom_call_target="tpu_custom_call" | custom-call | flops 226492416 | bytes 4718592 | tf_op jit(solution)/shard_map/own_totals/pallas_call | solution.py:52
  53.7 0.5 collective-permute-done.20.refs_0_
  54.3 3.3 %update.1 = (bf16[128,2304]{1,0:T(8,128)(2,1)}, f32[128,2304]{1,0:T(8,128)}, f32[128,2304]{1,0:T(8,128)}, bf16[128,2304]{1,0:T(8,128)(2,1)}, f32[128,2304]{1,0:T(8,128)}, /*index=5*/f32[128,2304]{1,0:T(8,128)}) custom-call(bf16[128,128]{1,0:T(8,128)(2,1)S(1)} %bitcast.7, bf16[128,2304]{1,0:T(8,128)(2,1)S(1)} %collective-permute-done.11.centered, ...), custom_call_target="tpu_custom_call" | custom-call | flops 226492416 | bytes 12976128 | tf_op jit(solution)/shard_map/update/pallas_call | solution.py:128
  (73 shorter events, 3.0 us)
Async XLA Ops:
  0.6 9.2 %copy-start.9 = (f32[128]{0:T(128)S(1)}, f32[128]{0:T(128)}, u32[]{:S(2)}) copy-start(f32[128]{0:T(128)} %param.11) | copy-start | bytes 1540
  0.7 8.7 %copy-start = (bf16[128,2304]{1,0:T(8,128)(2,1)S(1)}, bf16[128,2304]{1,0:T(8,128)(2,1)}, u32[]{:S(2)}) copy-start(bf16[128,2304]{1,0:T(8,128)(2,1)} %refs_3_.1) | copy-start | bytes 1769476
  0.7 9.2 %copy-start.5 = (bf16[128,2304]{1,0:T(8,128)(2,1)S(1)}, bf16[128,2304]{1,0:T(8,128)(2,1)}, u32[]{:S(2)}) copy-start(bf16[128,2304]{1,0:T(8,128)(2,1)} %refs_2_.1) | copy-start | bytes 1769476
  0.7 19.1 %copy-start.8 = (f32[2304]{0:T(1024)S(1)}, f32[2304]{0:T(1024)}, u32[]{:S(2)}) copy-start(f32[2304]{0:T(1024)} %param.13) | copy-start | bytes 27652
  0.7 9.2 %collective-permute-start.2 = (bf16[16,2304]{1,0:T(8,128)(2,1)}, bf16[16,2304]{1,0:T(8,128)(2,1)S(1)}, u32[]{:S(2)}, u32[]{:S(2)}) collective-permute-start(bf16[16,2304]{1,0:T(8,128)(2,1)} %param.9), channel_id=1, source_target_pairs={{0,12},{1,13},{2,14},{3,15},{4,8},{5,9},{6,10},{7,11},{8,4},{9,5},... | collective-permute-start | bytes 221192 | tf_op jit(solution)/shard_map/ppermute | solution.py:155
  5.8 6.4 %collective-permute-start.1 = (bf16[16,2304]{1,0:T(8,128)(2,1)}, bf16[16,2304]{1,0:T(8,128)(2,1)S(1)}, u32[]{:S(2)}, u32[]{:S(2)}) collective-permute-start(bf16[16,2304]{1,0:T(8,128)(2,1)} %param.9), channel_id=1, source_target_pairs={{0,8},{1,9},{2,10},{3,11},{4,12},{5,13},{6,14},{7,15},{8,0},{9,1},... | collective-permute-start | bytes 221192 | tf_op jit(solution)/shard_map/ppermute | solution.py:155
  5.8 7.9 %collective-permute-start = (bf16[16,2304]{1,0:T(8,128)(2,1)}, bf16[16,2304]{1,0:T(8,128)(2,1)S(1)}, u32[]{:S(2)}, u32[]{:S(2)}) collective-permute-start(bf16[16,2304]{1,0:T(8,128)(2,1)} %param.9), channel_id=1, source_target_pairs={{0,4},{1,5},{2,6},{3,7},{4,0},{5,1},{6,2},{7,3},{8,12},{9,13},{10,... | collective-permute-start | bytes 221192 | tf_op jit(solution)/shard_map/ppermute | solution.py:155
  6.4 7.8 %collective-permute-start.3 = (bf16[16,2304]{1,0:T(8,128)(2,1)}, bf16[16,2304]{1,0:T(8,128)(2,1)S(1)}, u32[]{:S(2)}, u32[]{:S(2)}) collective-permute-start(bf16[16,2304]{1,0:T(8,128)(2,1)} %param.9), channel_id=1, source_target_pairs={{0,2},{1,3},{2,0},{3,1},{4,6},{5,7},{6,4},{7,5},{8,10},{9,11},{10,... | collective-permute-start | bytes 221192 | tf_op jit(solution)/shard_map/ppermute | solution.py:155
  8.1 1.3 %collective-permute-start.8 = (f32[128]{0:T(128)}, f32[128]{0:T(128)S(1)}, u32[]{:S(2)}, u32[]{:S(2)}) collective-permute-start(f32[128]{0:T(128)} %param.11), channel_id=1, source_target_pairs={{0,1},{1,0},{2,3},{3,2},{4,5},{5,4},{6,7},{7,6},{8,9},{9,8},{10,11... | collective-permute-start | bytes 1544 | tf_op jit(solution)/shard_map/ppermute | solution.py:162
  9.4 10.5 %collective-permute-start.9 = (bf16[128,2304]{1,0:T(8,128)(2,1)S(1)}, bf16[128,2304]{1,0:T(8,128)(2,1)S(1)}, u32[]{:S(2)}, u32[]{:S(2)}) collective-permute-start(bf16[128,2304]{1,0:T(8,128)(2,1)S(1)} %copy-done), channel_id=1, source_target_pairs={{0,1},{1,0},{2,3},{3,2},{4,5},{5,4},{6,7},{7,6},{8,9},{9,8},{10,11... | collective-permute-start | bytes 1769480 | tf_op jit(solution)/shard_map/ppermute | solution.py:162
  9.9 10.0 %collective-permute-start.7 = (bf16[128,2304]{1,0:T(8,128)(2,1)S(1)}, bf16[128,2304]{1,0:T(8,128)(2,1)S(1)}, u32[]{:S(2)}, u32[]{:S(2)}) collective-permute-start(bf16[128,2304]{1,0:T(8,128)(2,1)S(1)} %copy-done.5), channel_id=1, source_target_pairs={{0,1},{1,0},{2,3},{3,2},{4,5},{5,4},{6,7},{7,6},{8,9},{9,8},{10,11... | collective-permute-start | bytes 1769480 | tf_op jit(solution)/shard_map/ppermute | solution.py:162
  12.2 7.5 %collective-permute-start.6 = (bf16[16,2304]{1,0:T(8,128)(2,1)S(1)}, bf16[16,2304]{1,0:T(8,128)(2,1)S(1)}, u32[]{:S(2)}, u32[]{:S(2)}) collective-permute-start(bf16[16,2304]{1,0:T(8,128)(2,1)S(1)} %collective-permute-done.2), channel_id=1, source_target_pairs={{0,2},{1,3},{2,0},{3,1},{4,6},{5,7},{6,4},{7,5},{8,10},{9,11},{10,... | collective-permute-start | bytes 221192 | tf_op jit(solution)/shard_map/ppermute | solution.py:155
  13.7 5.9 %collective-permute-start.5 = (bf16[16,2304]{1,0:T(8,128)(2,1)S(1)}, bf16[16,2304]{1,0:T(8,128)(2,1)S(1)}, u32[]{:S(2)}, u32[]{:S(2)}) collective-permute-start(bf16[16,2304]{1,0:T(8,128)(2,1)S(1)} %collective-permute-done.1), channel_id=1, source_target_pairs={{0,2},{1,3},{2,0},{3,1},{4,6},{5,7},{6,4},{7,5},{8,10},{9,11},{10,... | collective-permute-start | bytes 221192 | tf_op jit(solution)/shard_map/ppermute | solution.py:155
  14.3 5.4 %collective-permute-start.4 = (bf16[16,2304]{1,0:T(8,128)(2,1)S(1)}, bf16[16,2304]{1,0:T(8,128)(2,1)S(1)}, u32[]{:S(2)}, u32[]{:S(2)}) collective-permute-start(bf16[16,2304]{1,0:T(8,128)(2,1)S(1)} %collective-permute-done), channel_id=1, source_target_pairs={{0,2},{1,3},{2,0},{3,1},{4,6},{5,7},{6,4},{7,5},{8,10},{9,11},{10,... | collective-permute-start | bytes 221192 | tf_op jit(solution)/shard_map/ppermute | solution.py:155
  20.8 6.8 %collective-permute-start.11 = (bf16[128,2304]{1,0:T(8,128)(2,1)S(1)}, bf16[128,2304]{1,0:T(8,128)(2,1)S(1)}, u32[]{:S(2)}, u32[]{:S(2)}) collective-permute-start(bf16[128,2304]{1,0:T(8,128)(2,1)S(1)} %subtract_convert_fusion.centered), channel_id=1, source_target_pairs={{0,1},{1,0},{2,3},{3,2},{4,5},{5,4},{6,7},{7,6},{8,9},{9,8},{10,11... | collective-permute-start | bytes 1769480 | tf_op jit(solution)/shard_map/ppermute | solution.py:162
  20.9 6.3 %collective-permute-start.14 = (bf16[32,2304]{1,0:T(8,128)(2,1)S(1)}, bf16[32,2304]{1,0:T(8,128)(2,1)S(1)}, u32[]{:S(2)}, u32[]{:S(2)}) collective-permute-start(bf16[32,2304]{1,0:T(8,128)(2,1)S(1)} %get-tuple-element.33), channel_id=1, source_target_pairs={{0,2},{1,3},{2,0},{3,1},{4,6},{5,7},{6,4},{7,5},{8,10},{9,11},{10,... | collective-permute-start | bytes 442376 | tf_op jit(solution)/shard_map/ppermute | solution.py:155
  22.1 5.6 %collective-permute-start.10 = (bf16[128,128]{0,1:T(8,128)(2,1)S(1)}, bf16[128,128]{0,1:T(8,128)(2,1)S(1)}, u32[]{:S(2)}, u32[]{:S(2)}) collective-permute-start(bf16[128,128]{0,1:T(8,128)(2,1)S(1)} %get-tuple-element.38), channel_id=1, source_target_pairs={{0,1},{1,0},{2,3},{3,2},{4,5},{5,4},{6,7},{7,6},{8,9},{9,8},{10,11... | collective-permute-start | bytes 98312 | tf_op jit(solution)/shard_map/ppermute | solution.py:162
  27.6 5.5 %collective-permute-start.12 = (bf16[32,2304]{1,0:T(8,128)(2,1)S(1)}, bf16[32,2304]{1,0:T(8,128)(2,1)S(1)}, u32[]{:S(2)}, u32[]{:S(2)}) collective-permute-start(bf16[32,2304]{1,0:T(8,128)(2,1)S(1)} %get-tuple-element.21), channel_id=1, source_target_pairs={{0,2},{1,3},{2,0},{3,1},{4,6},{5,7},{6,4},{7,5},{8,10},{9,11},{10,... | collective-permute-start | bytes 442376 | tf_op jit(solution)/shard_map/ppermute | solution.py:155
  28.8 8.0 %collective-permute-start.15 = (bf16[16,2304]{1,0:T(8,128)(2,1)S(1)}, bf16[16,2304]{1,0:T(8,128)(2,1)S(1)}, u32[]{:S(2)}, u32[]{:S(2)}) collective-permute-start(bf16[16,2304]{1,0:T(8,128)(2,1)S(1)} %get-tuple-element.35), channel_id=1, source_target_pairs={{0,8},{1,9},{2,10},{3,11},{4,12},{5,13},{6,14},{7,15},{8,0},{9,1},... | collective-permute-start | bytes 221192 | tf_op jit(solution)/shard_map/ppermute | solution.py:155
  30.3 6.9 %collective-permute-start.16 = (bf16[16,2304]{1,0:T(8,128)(2,1)S(1)}, bf16[16,2304]{1,0:T(8,128)(2,1)S(1)}, u32[]{:S(2)}, u32[]{:S(2)}) collective-permute-start(bf16[16,2304]{1,0:T(8,128)(2,1)S(1)} %get-tuple-element.36), channel_id=1, source_target_pairs={{0,12},{1,13},{2,14},{3,15},{4,8},{5,9},{6,10},{7,11},{8,4},{9,5},... | collective-permute-start | bytes 221192 | tf_op jit(solution)/shard_map/ppermute | solution.py:155
  33.1 21.1 %copy-start.4 = (f32[128,2304]{1,0:T(8,128)S(1)}, f32[128,2304]{1,0:T(8,128)}, u32[]{:S(2)}) copy-start(f32[128,2304]{1,0:T(8,128)} %refs_7_.1) | copy-start | bytes 3538948
  33.5 4.5 %collective-permute-start.13 = (bf16[16,2304]{1,0:T(8,128)(2,1)S(1)}, bf16[16,2304]{1,0:T(8,128)(2,1)S(1)}, u32[]{:S(2)}, u32[]{:S(2)}) collective-permute-start(bf16[16,2304]{1,0:T(8,128)(2,1)S(1)} %slice.79), channel_id=1, source_target_pairs={{0,4},{1,5},{2,6},{3,7},{4,0},{5,1},{6,2},{7,3},{8,12},{9,13},{10,... | collective-permute-start | bytes 221192 | tf_op jit(solution)/shard_map/ppermute | solution.py:155
  38.1 14.7 %copy-start.6 = (bf16[16,2304]{1,0:T(8,128)(2,1)}, bf16[16,2304]{1,0:T(8,128)(2,1)S(1)}, u32[]{:S(2)}) copy-start(bf16[16,2304]{1,0:T(8,128)(2,1)S(1)} %fusion.17) | copy-start | bytes 221188
  38.1 6.2 %collective-permute-start.23 = (bf16[16,2304]{1,0:T(8,128)(2,1)S(1)}, bf16[16,2304]{1,0:T(8,128)(2,1)S(1)}, u32[]{:S(2)}, u32[]{:S(2)}) collective-permute-start(bf16[16,2304]{1,0:T(8,128)(2,1)S(1)} %fusion.17), channel_id=1, source_target_pairs={{0,12},{1,13},{2,14},{3,15},{4,8},{5,9},{6,10},{7,11},{8,4},{9,5},... | collective-permute-start | bytes 221192 | tf_op jit(solution)/shard_map/ppermute | solution.py:155
  40.4 6.6 %collective-permute-start.21 = (bf16[16,2304]{1,0:T(8,128)(2,1)S(1)}, bf16[16,2304]{1,0:T(8,128)(2,1)S(1)}, u32[]{:S(2)}, u32[]{:S(2)}) collective-permute-start(bf16[16,2304]{1,0:T(8,128)(2,1)S(1)} %fusion.17), channel_id=1, source_target_pairs={{0,8},{1,9},{2,10},{3,11},{4,12},{5,13},{6,14},{7,15},{8,0},{9,1},... | collective-permute-start | bytes 221192 | tf_op jit(solution)/shard_map/ppermute | solution.py:155
  40.4 7.5 %collective-permute-start.18 = (bf16[16,2304]{1,0:T(8,128)(2,1)S(1)}, bf16[16,2304]{1,0:T(8,128)(2,1)S(1)}, u32[]{:S(2)}, u32[]{:S(2)}) collective-permute-start(bf16[16,2304]{1,0:T(8,128)(2,1)S(1)} %fusion.17), channel_id=1, source_target_pairs={{0,4},{1,5},{2,6},{3,7},{4,0},{5,1},{6,2},{7,3},{8,12},{9,13},{10,... | collective-permute-start | bytes 221192 | tf_op jit(solution)/shard_map/ppermute | solution.py:155
  42.5 6.5 %collective-permute-start.17 = (bf16[16,2304]{1,0:T(8,128)(2,1)S(1)}, bf16[16,2304]{1,0:T(8,128)(2,1)S(1)}, u32[]{:S(2)}, u32[]{:S(2)}) collective-permute-start(bf16[16,2304]{1,0:T(8,128)(2,1)S(1)} %fusion.17), channel_id=1, source_target_pairs={{0,2},{1,3},{2,0},{3,1},{4,6},{5,7},{6,4},{7,5},{8,10},{9,11},{10,... | collective-permute-start | bytes 221192 | tf_op jit(solution)/shard_map/ppermute | solution.py:155
  44.3 4.8 %collective-permute-start.24 = (bf16[16,2304]{1,0:T(8,128)(2,1)S(1)}, bf16[16,2304]{1,0:T(8,128)(2,1)S(1)}, u32[]{:S(2)}, u32[]{:S(2)}) collective-permute-start(bf16[16,2304]{1,0:T(8,128)(2,1)S(1)} %collective-permute-done.23), channel_id=1, source_target_pairs={{0,2},{1,3},{2,0},{3,1},{4,6},{5,7},{6,4},{7,5},{8,10},{9,11},{10,... | collective-permute-start | bytes 221192 | tf_op jit(solution)/shard_map/ppermute | solution.py:155
  47.0 4.7 %collective-permute-start.22 = (bf16[16,2304]{1,0:T(8,128)(2,1)S(1)}, bf16[16,2304]{1,0:T(8,128)(2,1)S(1)}, u32[]{:S(2)}, u32[]{:S(2)}) collective-permute-start(bf16[16,2304]{1,0:T(8,128)(2,1)S(1)} %collective-permute-done.21), channel_id=1, source_target_pairs={{0,2},{1,3},{2,0},{3,1},{4,6},{5,7},{6,4},{7,5},{8,10},{9,11},{10,... | collective-permute-start | bytes 221192 | tf_op jit(solution)/shard_map/ppermute | solution.py:155
  47.9 4.6 %collective-permute-start.19 = (bf16[16,2304]{1,0:T(8,128)(2,1)S(1)}, bf16[16,2304]{1,0:T(8,128)(2,1)S(1)}, u32[]{:S(2)}, u32[]{:S(2)}) collective-permute-start(bf16[16,2304]{1,0:T(8,128)(2,1)S(1)} %collective-permute-done.18), channel_id=1, source_target_pairs={{0,2},{1,3},{2,0},{3,1},{4,6},{5,7},{6,4},{7,5},{8,10},{9,11},{10,... | collective-permute-start | bytes 221192 | tf_op jit(solution)/shard_map/ppermute | solution.py:155
  51.7 2.0 %collective-permute-start.25 = (bf16[64,2304]{1,0:T(8,128)(2,1)S(1)}, bf16[64,2304]{1,0:T(8,128)(2,1)S(1)}, u32[]{:S(2)}, u32[]{:S(2)}) collective-permute-start(bf16[64,2304]{1,0:T(8,128)(2,1)S(1)} %pad_maximum_fusion.1), channel_id=1, source_target_pairs={{0,1},{1,0},{2,3},{3,2},{4,5},{5,4},{6,7},{7,6},{8,9},{9,8},{10,11... | collective-permute-start | bytes 884744 | tf_op jit(solution)/shard_map/ppermute | solution.py:162
  52.5 1.6 %collective-permute-start.20 = (bf16[64,2304]{1,0:T(8,128)(2,1)S(1)}, bf16[64,2304]{1,0:T(8,128)(2,1)S(1)}, u32[]{:S(2)}, u32[]{:S(2)}) collective-permute-start(bf16[64,2304]{1,0:T(8,128)(2,1)S(1)} %pad_maximum_fusion), channel_id=1, source_target_pairs={{0,1},{1,0},{2,3},{3,2},{4,5},{5,4},{6,7},{7,6},{8,9},{9,8},{10,11... | collective-permute-start | bytes 884744 | tf_op jit(solution)/shard_map/ppermute | solution.py:162
  (4 other events, 14.3 us)

commit v21 on v17

--- a/solution.py
+++ b/solution.py
@@ -179,10 +179,13 @@
     chips = size // 2
     total_rows = rows_here * size
 
-    rows_core = jnp.concatenate(in_turn(*gather_chips(activations, chips)), 0)
-    encoder_both = jnp.concatenate([encoder, to_other_core(encoder)], 0)
-    decoder_both = jnp.concatenate([decoder, to_other_core(decoder)], 0)
-    bias_both = jnp.concatenate([encoder_bias, to_other_core(encoder_bias)], 0)
+    even, odd = gather_chips(activations, chips)
+    rows_core = jnp.concatenate(in_turn(even, odd), 0)
+    sent, _ = lax.optimization_barrier(((encoder_bias, encoder, decoder), odd[1]))
+    bias_both, encoder_both, decoder_both = (
+        jnp.concatenate([mine, to_other_core(one)], 0)
+        for mine, one in zip((encoder_bias, encoder, decoder), sent)
+    )
 
     centered = (rows_core.astype(jnp.float32) - decoder_bias).astype(jnp.bfloat16)
     codes = jnp.maximum(inner_last(centered, encoder_both) + bias_both, 0.0).astype(

time: 54.5 us -> 54.9 us (level)
  starting transfers between devices: 26.6 us -> 27.2 us
    ppermute x19, starting transfers between devices: 25.3 us -> 25.9 us  [to_chip(): lax.ppermute(block, 'latent', [(i, i ^ 2 * distance) for i in range(size)])]
  transfers between devices with their start and end apart: 26 -> 26, of which waited for: 15 -> 13; matrix products, arithmetic and copies ran while one was open for 4% -> 3% of each run, Pallas kernels for 2% -> 2%
where the time goes in v21:
time: 54.9 us; the launch traced here: 54.7 us
  starting transfers between devices  27.2 us (50%)
  waiting for transfers between devices  19.3 us (35%)
  Pallas kernels  4.23 us (8%)
  local copies, waits for them, and re-layouts  1.47 us (3%)
  matrix products  1.27 us (2%)
  between operations  0.99 us (2%)
    ppermute x19, starting transfers between devices, to_chip(): lax.ppermute(block, 'latent', [(i, i ^ 2 * distance) for i in range(size)])  25.9 us
    ppermute x19, waiting for transfers between devices, to_chip(): lax.ppermute(block, 'latent', [(i, i ^ 2 * distance) for i in range(size)])  17.2 us
    pallas_call x1, Pallas kernels, update(): pl.pallas_call(functools.partial(update_kernel, columns, float(total_rows...  3.26 us
    ppermute x7, waiting for transfers between devices, to_other_core(): return lax.ppermute(block, 'latent', [(i, i ^ 1) for i in range(size)])  2.08 us
    unnamed x35, local copies, waits for them, and re-layouts  1.39 us
    ppermute x7, starting transfers between devices, to_other_core(): return lax.ppermute(block, 'latent', [(i, i ^ 1) for i in range(size)])  1.23 us
  transfers between devices with their start and end apart: 26, of which 13 were waited for; matrix products, arithmetic and copies ran while one was open for 3% of the time, Pallas kernels for 2%

profile of v21, /device:TPU:0, one launch (start us, length us, event | category | flops | bytes accessed | tf_op | source)
XLA Modules:
  0.0 54.7 jit_solution(18129422701744408828)
XLA Ops:
  0.7 4.1 %collective-permute-start.3 = (bf16[16,2304]{1,0:T(8,128)(2,1)}, bf16[16,2304]{1,0:T(8,128)(2,1)S(1)}, u32[]{:S(2)}, u32[]{:S(2)}) collective-permute-start(bf16[16,2304]{1,0:T(8,128)(2,1)} %param.9), channel_id=1, source_target_pairs={{0,8},{1,9},{2,10},{3,11},{4,12},{5,13},{6,14},{7,15},{8,0},{9,1},... | collective-permute-start | bytes 221192 | tf_op jit(solution)/shard_map/ppermute | solution.py:146
  4.8 1.6 %collective-permute-start.1 = (bf16[16,2304]{1,0:T(8,128)(2,1)}, bf16[16,2304]{1,0:T(8,128)(2,1)S(1)}, u32[]{:S(2)}, u32[]{:S(2)}) collective-permute-start(bf16[16,2304]{1,0:T(8,128)(2,1)} %param.9), channel_id=1, source_target_pairs={{0,4},{1,5},{2,6},{3,7},{4,0},{5,1},{6,2},{7,3},{8,12},{9,13},{10,... | collective-permute-start | bytes 221192 | tf_op jit(solution)/shard_map/ppermute | solution.py:146
  6.4 1.5 %collective-permute-start = (bf16[16,2304]{1,0:T(8,128)(2,1)}, bf16[16,2304]{1,0:T(8,128)(2,1)S(1)}, u32[]{:S(2)}, u32[]{:S(2)}) collective-permute-start(bf16[16,2304]{1,0:T(8,128)(2,1)} %param.9), channel_id=1, source_target_pairs={{0,2},{1,3},{2,0},{3,1},{4,6},{5,7},{6,4},{7,5},{8,10},{9,11},{10,... | collective-permute-start | bytes 221192 | tf_op jit(solution)/shard_map/ppermute | solution.py:146
  8.1 1.1 %constant_dynamic-update-slice_fusion.9 = bf16[256,2304]{1,0:T(8,128)(2,1)S(1)} fusion(bf16[128,2304]{1,0:T(8,128)(2,1)} %refs_3_.1), kind=kLoop, calls=%fused_computation.37 | loop fusion | bytes 1179648
  9.2 1.4 %collective-permute-start.4 = (bf16[16,2304]{1,0:T(8,128)(2,1)S(1)}, bf16[16,2304]{1,0:T(8,128)(2,1)S(1)}, u32[]{:S(2)}, u32[]{:S(2)}) collective-permute-start(bf16[16,2304]{1,0:T(8,128)(2,1)S(1)} %collective-permute-done.3), channel_id=1, source_target_pairs={{0,2},{1,3},{2,0},{3,1},{4,6},{5,7},{6,4},{7,5},{8,10},{9,11},{10,... | collective-permute-start | bytes 221192 | tf_op jit(solution)/shard_map/ppermute | solution.py:146
  10.7 0.7 %collective-permute-start.2 = (bf16[16,2304]{1,0:T(8,128)(2,1)S(1)}, bf16[16,2304]{1,0:T(8,128)(2,1)S(1)}, u32[]{:S(2)}, u32[]{:S(2)}) collective-permute-start(bf16[16,2304]{1,0:T(8,128)(2,1)S(1)} %collective-permute-done.1), channel_id=1, source_target_pairs={{0,2},{1,3},{2,0},{3,1},{4,6},{5,7},{6,4},{7,5},{8,10},{9,11},{10,... | collective-permute-start | bytes 221192 | tf_op jit(solution)/shard_map/ppermute | solution.py:146
  11.3 2.9 %collective-permute-done.5 = bf16[16,2304]{1,0:T(8,128)(2,1)S(1)} collective-permute-done((bf16[16,2304]{1,0:T(8,128)(2,1)}, bf16[16,2304]{1,0:T(8,128)(2,1)S(1)}, u32[]{:S(2)}, u32[]{:S(2)}) %collective-permute-start.5) | collective-permute-done | bytes 73760 | tf_op jit(solution)/shard_map/ppermute | solution.py:146
  14.2 0.5 collective-permute-start.6
  14.8 0.6 %collective-permute-done.2 = bf16[16,2304]{1,0:T(8,128)(2,1)S(1)} collective-permute-done((bf16[16,2304]{1,0:T(8,128)(2,1)S(1)}, bf16[16,2304]{1,0:T(8,128)(2,1)S(1)}, u32[]{:S(2)}, u32[]{:S(2)}) %collective-permute-start.2) | collective-permute-done | bytes 73760 | tf_op jit(solution)/shard_map/ppermute | solution.py:146
  16.0 2.6 %collective-permute-done.6 = bf16[16,2304]{1,0:T(8,128)(2,1)S(1)} collective-permute-done((bf16[16,2304]{1,0:T(8,128)(2,1)S(1)}, bf16[16,2304]{1,0:T(8,128)(2,1)S(1)}, u32[]{:S(2)}, u32[]{:S(2)}) %collective-permute-start.6) | collective-permute-done | bytes 73760 | tf_op jit(solution)/shard_map/ppermute | solution.py:146
  20.1 0.6 %collective-permute-start.14 = (bf16[32,2304]{1,0:T(8,128)(2,1)S(1)}, bf16[32,2304]{1,0:T(8,128)(2,1)S(1)}, u32[]{:S(2)}, u32[]{:S(2)}) collective-permute-start(bf16[32,2304]{1,0:T(8,128)(2,1)S(1)} %pad_maximum_fusion.3), channel_id=1, source_target_pairs={{0,2},{1,3},{2,0},{3,1},{4,6},{5,7},{6,4},{7,5},{8,10},{9,11},{10,... | collective-permute-start | bytes 442376 | tf_op jit(solution)/shard_map/ppermute | solution.py:146
  20.7 0.5 collective-permute-start.11
  21.3 0.7 %collective-permute-done.10 = bf16[128,128]{0,1:T(8,128)(2,1)S(1)} collective-permute-done((bf16[128,128]{0,1:T(8,128)(2,1)S(1)}, bf16[128,128]{0,1:T(8,128)(2,1)S(1)}, u32[]{:S(2)}, u32[]{:S(2)}) %collective-permute-start.10) | collective-permute-done | bytes 32800 | tf_op jit(solution)/shard_map/ppermute | solution.py:153
  21.9 0.9 %collective-permute-done.11.centered = bf16[128,2304]{1,0:T(8,128)(2,1)S(1)} collective-permute-done((bf16[128,2304]{1,0:T(8,128)(2,1)S(1)}, bf16[128,2304]{1,0:T(8,128)(2,1)S(1)}, u32[]{:S(2)}, u32[]{:S(2)}) %collective-permute-start.11) | collective-permute-done | bytes 589856 | tf_op jit(solution)/shard_map/ppermute | solution.py:153
  22.9 1.5 %collective-permute-start.12 = (bf16[32,2304]{1,0:T(8,128)(2,1)S(1)}, bf16[32,2304]{1,0:T(8,128)(2,1)S(1)}, u32[]{:S(2)}, u32[]{:S(2)}) collective-permute-start(bf16[32,2304]{1,0:T(8,128)(2,1)S(1)} %pad_maximum_fusion.2), channel_id=1, source_target_pairs={{0,2},{1,3},{2,0},{3,1},{4,6},{5,7},{6,4},{7,5},{8,10},{9,11},{10,... | collective-permute-start | bytes 442376 | tf_op jit(solution)/shard_map/ppermute | solution.py:146
  24.4 1.0 %collective-permute-done.14 = bf16[32,2304]{1,0:T(8,128)(2,1)S(1)} collective-permute-done((bf16[32,2304]{1,0:T(8,128)(2,1)S(1)}, bf16[32,2304]{1,0:T(8,128)(2,1)S(1)}, u32[]{:S(2)}, u32[]{:S(2)}) %collective-permute-start.14) | collective-permute-done | bytes 147488 | tf_op jit(solution)/shard_map/ppermute | solution.py:146
  25.5 1.4 %collective-permute-start.15 = (bf16[16,2304]{1,0:T(8,128)(2,1)S(1)}, bf16[16,2304]{1,0:T(8,128)(2,1)S(1)}, u32[]{:S(2)}, u32[]{:S(2)}) collective-permute-start(bf16[16,2304]{1,0:T(8,128)(2,1)S(1)} %get-tuple-element.39), channel_id=1, source_target_pairs={{0,8},{1,9},{2,10},{3,11},{4,12},{5,13},{6,14},{7,15},{8,0},{9,1},... | collective-permute-start | bytes 221192 | tf_op jit(solution)/shard_map/ppermute | solution.py:146
  26.9 2.7 %collective-permute-start.16 = (bf16[16,2304]{1,0:T(8,128)(2,1)S(1)}, bf16[16,2304]{1,0:T(8,128)(2,1)S(1)}, u32[]{:S(2)}, u32[]{:S(2)}) collective-permute-start(bf16[16,2304]{1,0:T(8,128)(2,1)S(1)} %get-tuple-element.40), channel_id=1, source_target_pairs={{0,12},{1,13},{2,14},{3,15},{4,8},{5,9},{6,10},{7,11},{8,4},{9,5},... | collective-permute-start | bytes 221192 | tf_op jit(solution)/shard_map/ppermute | solution.py:146
  29.6 0.9 %collective-permute-start.13 = (bf16[16,2304]{1,0:T(8,128)(2,1)S(1)}, bf16[16,2304]{1,0:T(8,128)(2,1)S(1)}, u32[]{:S(2)}, u32[]{:S(2)}) collective-permute-start(bf16[16,2304]{1,0:T(8,128)(2,1)S(1)} %fusion.15), channel_id=1, source_target_pairs={{0,4},{1,5},{2,6},{3,7},{4,0},{5,1},{6,2},{7,3},{8,12},{9,13},{10,... | collective-permute-start | bytes 221192 | tf_op jit(solution)/shard_map/ppermute | solution.py:146
  30.6 4.0 %collective-permute-done.15 = bf16[16,2304]{1,0:T(8,128)(2,1)S(1)} collective-permute-done((bf16[16,2304]{1,0:T(8,128)(2,1)S(1)}, bf16[16,2304]{1,0:T(8,128)(2,1)S(1)}, u32[]{:S(2)}, u32[]{:S(2)}) %collective-permute-start.15) | collective-permute-done | bytes 73760 | tf_op jit(solution)/shard_map/ppermute | solution.py:146
  35.0 3.0 %collective-permute-start.23 = (bf16[16,2304]{1,0:T(8,128)(2,1)S(1)}, bf16[16,2304]{1,0:T(8,128)(2,1)S(1)}, u32[]{:S(2)}, u32[]{:S(2)}) collective-permute-start(bf16[16,2304]{1,0:T(8,128)(2,1)S(1)} %fusion.20), channel_id=1, source_target_pairs={{0,12},{1,13},{2,14},{3,15},{4,8},{5,9},{6,10},{7,11},{8,4},{9,5},... | collective-permute-start | bytes 221192 | tf_op jit(solution)/shard_map/ppermute | solution.py:146
  38.0 1.4 %collective-permute-start.18 = (bf16[16,2304]{1,0:T(8,128)(2,1)S(1)}, bf16[16,2304]{1,0:T(8,128)(2,1)S(1)}, u32[]{:S(2)}, u32[]{:S(2)}) collective-permute-start(bf16[16,2304]{1,0:T(8,128)(2,1)S(1)} %fusion.20), channel_id=1, source_target_pairs={{0,4},{1,5},{2,6},{3,7},{4,0},{5,1},{6,2},{7,3},{8,12},{9,13},{10,... | collective-permute-start | bytes 221192 | tf_op jit(solution)/shard_map/ppermute | solution.py:146
  39.4 1.2 %collective-permute-start.17 = (bf16[16,2304]{1,0:T(8,128)(2,1)S(1)}, bf16[16,2304]{1,0:T(8,128)(2,1)S(1)}, u32[]{:S(2)}, u32[]{:S(2)}) collective-permute-start(bf16[16,2304]{1,0:T(8,128)(2,1)S(1)} %fusion.20), channel_id=1, source_target_pairs={{0,2},{1,3},{2,0},{3,1},{4,6},{5,7},{6,4},{7,5},{8,10},{9,11},{10,... | collective-permute-start | bytes 221192 | tf_op jit(solution)/shard_map/ppermute | solution.py:146
  40.6 0.8 %collective-permute-done.23 = bf16[16,2304]{1,0:T(8,128)(2,1)S(1)} collective-permute-done((bf16[16,2304]{1,0:T(8,128)(2,1)S(1)}, bf16[16,2304]{1,0:T(8,128)(2,1)S(1)}, u32[]{:S(2)}, u32[]{:S(2)}) %collective-permute-start.23) | collective-permute-done | bytes 73760 | tf_op jit(solution)/shard_map/ppermute | solution.py:146
  41.4 1.0 %collective-permute-start.24 = (bf16[16,2304]{1,0:T(8,128)(2,1)S(1)}, bf16[16,2304]{1,0:T(8,128)(2,1)S(1)}, u32[]{:S(2)}, u32[]{:S(2)}) collective-permute-start(bf16[16,2304]{1,0:T(8,128)(2,1)S(1)} %collective-permute-done.23), channel_id=1, source_target_pairs={{0,2},{1,3},{2,0},{3,1},{4,6},{5,7},{6,4},{7,5},{8,10},{9,11},{10,... | collective-permute-start | bytes 221192 | tf_op jit(solution)/shard_map/ppermute | solution.py:146
  42.4 1.8 %collective-permute-done.21 = bf16[16,2304]{1,0:T(8,128)(2,1)S(1)} collective-permute-done((bf16[16,2304]{1,0:T(8,128)(2,1)S(1)}, bf16[16,2304]{1,0:T(8,128)(2,1)S(1)}, u32[]{:S(2)}, u32[]{:S(2)}) %collective-permute-start.21) | collective-permute-done | bytes 73760 | tf_op jit(solution)/shard_map/ppermute | solution.py:146
  44.2 0.7 %collective-permute-start.22 = (bf16[16,2304]{1,0:T(8,128)(2,1)S(1)}, bf16[16,2304]{1,0:T(8,128)(2,1)S(1)}, u32[]{:S(2)}, u32[]{:S(2)}) collective-permute-start(bf16[16,2304]{1,0:T(8,128)(2,1)S(1)} %collective-permute-done.21), channel_id=1, source_target_pairs={{0,2},{1,3},{2,0},{3,1},{4,6},{5,7},{6,4},{7,5},{8,10},{9,11},{10,... | collective-permute-start | bytes 221192 | tf_op jit(solution)/shard_map/ppermute | solution.py:146
  44.9 1.3 %collective-permute-start.19 = (bf16[16,2304]{1,0:T(8,128)(2,1)S(1)}, bf16[16,2304]{1,0:T(8,128)(2,1)S(1)}, u32[]{:S(2)}, u32[]{:S(2)}) collective-permute-start(bf16[16,2304]{1,0:T(8,128)(2,1)S(1)} %collective-permute-done.18), channel_id=1, source_target_pairs={{0,2},{1,3},{2,0},{3,1},{4,6},{5,7},{6,4},{7,5},{8,10},{9,11},{10,... | collective-permute-start | bytes 221192 | tf_op jit(solution)/shard_map/ppermute | solution.py:146
  46.3 2.6 %collective-permute-done.22 = bf16[16,2304]{1,0:T(8,128)(2,1)S(1)} collective-permute-done((bf16[16,2304]{1,0:T(8,128)(2,1)S(1)}, bf16[16,2304]{1,0:T(8,128)(2,1)S(1)}, u32[]{:S(2)}, u32[]{:S(2)}) %collective-permute-start.22) | collective-permute-done | bytes 73760 | tf_op jit(solution)/shard_map/ppermute | solution.py:146
  48.9 0.7 %collective-permute-done.19 = bf16[16,2304]{1,0:T(8,128)(2,1)S(1)} collective-permute-done((bf16[16,2304]{1,0:T(8,128)(2,1)S(1)}, bf16[16,2304]{1,0:T(8,128)(2,1)S(1)}, u32[]{:S(2)}, u32[]{:S(2)}) %collective-permute-start.19) | collective-permute-done | bytes 73760 | tf_op jit(solution)/shard_map/ppermute | solution.py:146
  49.8 1.0 %own_totals.1 = (f32[128,2304]{1,0:T(8,128)S(1)}, f32[128,2304]{1,0:T(8,128)S(1)}) custom-call(bf16[128,128]{1,0:T(8,128)(2,1)S(1)} %get-tuple-element.45.codes_across, bf16[128,2304]{1,0:T(8,128)(2,1)S(1)} %subtract_convert_fusion.centered, bf16[128,2304]{1,0:T(8,128)(2,1)S(1)} %constant_dynamic-update-slice_fusion.10.errors, bf16[128,2304]{1,0:T(8,128)(2,1)S(1)} %copy-done), custom_call_target="tpu_custom_call" | custom-call | flops 226492416 | bytes 4718592 | tf_op jit(solution)/shard_map/own_totals/pallas_call | solution.py:41
  51.5 3.3 %update.1 = (bf16[128,2304]{1,0:T(8,128)(2,1)}, f32[128,2304]{1,0:T(8,128)}, f32[128,2304]{1,0:T(8,128)}, bf16[128,2304]{1,0:T(8,128)(2,1)}, f32[128,2304]{1,0:T(8,128)}, /*index=5*/f32[128,2304]{1,0:T(8,128)}) custom-call(bf16[128,128]{1,0:T(8,128)(2,1)S(1)} %bitcast.6, bf16[128,2304]{1,0:T(8,128)(2,1)S(1)} %collective-permute-done.11.centered, ...), custom_call_target="tpu_custom_call" | custom-call | flops 226492416 | bytes 12976128 | tf_op jit(solution)/shard_map/update/pallas_call | solution.py:119
  (75 shorter events, 3.7 us)
Async XLA Ops:
  0.6 15.2 %copy-start = (bf16[128,2304]{1,0:T(8,128)(2,1)S(1)}, bf16[128,2304]{1,0:T(8,128)(2,1)}, u32[]{:S(2)}) copy-start(bf16[128,2304]{1,0:T(8,128)(2,1)} %refs_3_.1) | copy-start | bytes 1769476
  0.7 14.7 %copy-start.5 = (bf16[128,2304]{1,0:T(8,128)(2,1)S(1)}, bf16[128,2304]{1,0:T(8,128)(2,1)}, u32[]{:S(2)}) copy-start(bf16[128,2304]{1,0:T(8,128)(2,1)} %refs_2_.1) | copy-start | bytes 1769476
  0.7 14.7 %copy-start.9 = (f32[128]{0:T(128)S(1)}, f32[128]{0:T(128)}, u32[]{:S(2)}) copy-start(f32[128]{0:T(128)} %param.11) | copy-start | bytes 1540
  0.7 17.9 %copy-start.8 = (f32[2304]{0:T(1024)S(1)}, f32[2304]{0:T(1024)}, u32[]{:S(2)}) copy-start(f32[2304]{0:T(1024)} %param.13) | copy-start | bytes 27652
  0.7 8.6 %collective-permute-start.3 = (bf16[16,2304]{1,0:T(8,128)(2,1)}, bf16[16,2304]{1,0:T(8,128)(2,1)S(1)}, u32[]{:S(2)}, u32[]{:S(2)}) collective-permute-start(bf16[16,2304]{1,0:T(8,128)(2,1)} %param.9), channel_id=1, source_target_pairs={{0,8},{1,9},{2,10},{3,11},{4,12},{5,13},{6,14},{7,15},{8,0},{9,1},... | collective-permute-start | bytes 221192 | tf_op jit(solution)/shard_map/ppermute | solution.py:146
  4.8 5.9 %collective-permute-start.1 = (bf16[16,2304]{1,0:T(8,128)(2,1)}, bf16[16,2304]{1,0:T(8,128)(2,1)S(1)}, u32[]{:S(2)}, u32[]{:S(2)}) collective-permute-start(bf16[16,2304]{1,0:T(8,128)(2,1)} %param.9), channel_id=1, source_target_pairs={{0,4},{1,5},{2,6},{3,7},{4,0},{5,1},{6,2},{7,3},{8,12},{9,13},{10,... | collective-permute-start | bytes 221192 | tf_op jit(solution)/shard_map/ppermute | solution.py:146
  6.4 8.4 %collective-permute-start = (bf16[16,2304]{1,0:T(8,128)(2,1)}, bf16[16,2304]{1,0:T(8,128)(2,1)S(1)}, u32[]{:S(2)}, u32[]{:S(2)}) collective-permute-start(bf16[16,2304]{1,0:T(8,128)(2,1)} %param.9), channel_id=1, source_target_pairs={{0,2},{1,3},{2,0},{3,1},{4,6},{5,7},{6,4},{7,5},{8,10},{9,11},{10,... | collective-permute-start | bytes 221192 | tf_op jit(solution)/shard_map/ppermute | solution.py:146
  7.9 6.4 %collective-permute-start.5 = (bf16[16,2304]{1,0:T(8,128)(2,1)}, bf16[16,2304]{1,0:T(8,128)(2,1)S(1)}, u32[]{:S(2)}, u32[]{:S(2)}) collective-permute-start(bf16[16,2304]{1,0:T(8,128)(2,1)} %param.9), channel_id=1, source_target_pairs={{0,12},{1,13},{2,14},{3,15},{4,8},{5,9},{6,10},{7,11},{8,4},{9,5},... | collective-permute-start | bytes 221192 | tf_op jit(solution)/shard_map/ppermute | solution.py:146
  9.2 6.7 %collective-permute-start.4 = (bf16[16,2304]{1,0:T(8,128)(2,1)S(1)}, bf16[16,2304]{1,0:T(8,128)(2,1)S(1)}, u32[]{:S(2)}, u32[]{:S(2)}) collective-permute-start(bf16[16,2304]{1,0:T(8,128)(2,1)S(1)} %collective-permute-done.3), channel_id=1, source_target_pairs={{0,2},{1,3},{2,0},{3,1},{4,6},{5,7},{6,4},{7,5},{8,10},{9,11},{10,... | collective-permute-start | bytes 221192 | tf_op jit(solution)/shard_map/ppermute | solution.py:146
  10.7 4.7 %collective-permute-start.2 = (bf16[16,2304]{1,0:T(8,128)(2,1)S(1)}, bf16[16,2304]{1,0:T(8,128)(2,1)S(1)}, u32[]{:S(2)}, u32[]{:S(2)}) collective-permute-start(bf16[16,2304]{1,0:T(8,128)(2,1)S(1)} %collective-permute-done.1), channel_id=1, source_target_pairs={{0,2},{1,3},{2,0},{3,1},{4,6},{5,7},{6,4},{7,5},{8,10},{9,11},{10,... | collective-permute-start | bytes 221192 | tf_op jit(solution)/shard_map/ppermute | solution.py:146
  14.2 4.4 %collective-permute-start.6 = (bf16[16,2304]{1,0:T(8,128)(2,1)S(1)}, bf16[16,2304]{1,0:T(8,128)(2,1)S(1)}, u32[]{:S(2)}, u32[]{:S(2)}) collective-permute-start(bf16[16,2304]{1,0:T(8,128)(2,1)S(1)} %collective-permute-done.5), channel_id=1, source_target_pairs={{0,2},{1,3},{2,0},{3,1},{4,6},{5,7},{6,4},{7,5},{8,10},{9,11},{10,... | collective-permute-start | bytes 221192 | tf_op jit(solution)/shard_map/ppermute | solution.py:146
  15.4 3.3 %collective-permute-start.8 = (f32[128]{0:T(128)S(1)}, f32[128]{0:T(128)S(1)}, u32[]{:S(2)}, u32[]{:S(2)}) collective-permute-start(f32[128]{0:T(128)S(1)} %copy-done.9), channel_id=1, source_target_pairs={{0,1},{1,0},{2,3},{3,2},{4,5},{5,4},{6,7},{7,6},{8,9},{9,8},{10,11... | collective-permute-start | bytes 1544 | tf_op jit(solution)/shard_map/ppermute | solution.py:153
  15.4 3.4 %collective-permute-start.7 = (bf16[128,2304]{1,0:T(8,128)(2,1)S(1)}, bf16[128,2304]{1,0:T(8,128)(2,1)S(1)}, u32[]{:S(2)}, u32[]{:S(2)}) collective-permute-start(bf16[128,2304]{1,0:T(8,128)(2,1)S(1)} %copy-done.5), channel_id=1, source_target_pairs={{0,1},{1,0},{2,3},{3,2},{4,5},{5,4},{6,7},{7,6},{8,9},{9,8},{10,11... | collective-permute-start | bytes 1769480 | tf_op jit(solution)/shard_map/ppermute | solution.py:153
  15.9 3.4 %collective-permute-start.9 = (bf16[128,2304]{1,0:T(8,128)(2,1)S(1)}, bf16[128,2304]{1,0:T(8,128)(2,1)S(1)}, u32[]{:S(2)}, u32[]{:S(2)}) collective-permute-start(bf16[128,2304]{1,0:T(8,128)(2,1)S(1)} %copy-done), channel_id=1, source_target_pairs={{0,1},{1,0},{2,3},{3,2},{4,5},{5,4},{6,7},{7,6},{8,9},{9,8},{10,11... | collective-permute-start | bytes 1769480 | tf_op jit(solution)/shard_map/ppermute | solution.py:153
  20.1 5.3 %collective-permute-start.14 = (bf16[32,2304]{1,0:T(8,128)(2,1)S(1)}, bf16[32,2304]{1,0:T(8,128)(2,1)S(1)}, u32[]{:S(2)}, u32[]{:S(2)}) collective-permute-start(bf16[32,2304]{1,0:T(8,128)(2,1)S(1)} %pad_maximum_fusion.3), channel_id=1, source_target_pairs={{0,2},{1,3},{2,0},{3,1},{4,6},{5,7},{6,4},{7,5},{8,10},{9,11},{10,... | collective-permute-start | bytes 442376 | tf_op jit(solution)/shard_map/ppermute | solution.py:146
  20.7 1.2 %collective-permute-start.10 = (bf16[128,128]{0,1:T(8,128)(2,1)S(1)}, bf16[128,128]{0,1:T(8,128)(2,1)S(1)}, u32[]{:S(2)}, u32[]{:S(2)}) collective-permute-start(bf16[128,128]{0,1:T(8,128)(2,1)S(1)} %get-tuple-element.46), channel_id=1, source_target_pairs={{0,1},{1,0},{2,3},{3,2},{4,5},{5,4},{6,7},{7,6},{8,9},{9,8},{10,11... | collective-permute-start | bytes 98312 | tf_op jit(solution)/shard_map/ppermute | solution.py:153
  20.7 2.1 %collective-permute-start.11 = (bf16[128,2304]{1,0:T(8,128)(2,1)S(1)}, bf16[128,2304]{1,0:T(8,128)(2,1)S(1)}, u32[]{:S(2)}, u32[]{:S(2)}) collective-permute-start(bf16[128,2304]{1,0:T(8,128)(2,1)S(1)} %subtract_convert_fusion.centered), channel_id=1, source_target_pairs={{0,1},{1,0},{2,3},{3,2},{4,5},{5,4},{6,7},{7,6},{8,9},{9,8},{10,11... | collective-permute-start | bytes 1769480 | tf_op jit(solution)/shard_map/ppermute | solution.py:153
  22.9 6.8 %collective-permute-start.12 = (bf16[32,2304]{1,0:T(8,128)(2,1)S(1)}, bf16[32,2304]{1,0:T(8,128)(2,1)S(1)}, u32[]{:S(2)}, u32[]{:S(2)}) collective-permute-start(bf16[32,2304]{1,0:T(8,128)(2,1)S(1)} %pad_maximum_fusion.2), channel_id=1, source_target_pairs={{0,2},{1,3},{2,0},{3,1},{4,6},{5,7},{6,4},{7,5},{8,10},{9,11},{10,... | collective-permute-start | bytes 442376 | tf_op jit(solution)/shard_map/ppermute | solution.py:146
  25.5 9.1 %collective-permute-start.15 = (bf16[16,2304]{1,0:T(8,128)(2,1)S(1)}, bf16[16,2304]{1,0:T(8,128)(2,1)S(1)}, u32[]{:S(2)}, u32[]{:S(2)}) collective-permute-start(bf16[16,2304]{1,0:T(8,128)(2,1)S(1)} %get-tuple-element.39), channel_id=1, source_target_pairs={{0,8},{1,9},{2,10},{3,11},{4,12},{5,13},{6,14},{7,15},{8,0},{9,1},... | collective-permute-start | bytes 221192 | tf_op jit(solution)/shard_map/ppermute | solution.py:146
  26.9 7.7 %collective-permute-start.16 = (bf16[16,2304]{1,0:T(8,128)(2,1)S(1)}, bf16[16,2304]{1,0:T(8,128)(2,1)S(1)}, u32[]{:S(2)}, u32[]{:S(2)}) collective-permute-start(bf16[16,2304]{1,0:T(8,128)(2,1)S(1)} %get-tuple-element.40), channel_id=1, source_target_pairs={{0,12},{1,13},{2,14},{3,15},{4,8},{5,9},{6,10},{7,11},{8,4},{9,5},... | collective-permute-start | bytes 221192 | tf_op jit(solution)/shard_map/ppermute | solution.py:146
  29.6 5.2 %collective-permute-start.13 = (bf16[16,2304]{1,0:T(8,128)(2,1)S(1)}, bf16[16,2304]{1,0:T(8,128)(2,1)S(1)}, u32[]{:S(2)}, u32[]{:S(2)}) collective-permute-start(bf16[16,2304]{1,0:T(8,128)(2,1)S(1)} %fusion.15), channel_id=1, source_target_pairs={{0,4},{1,5},{2,6},{3,7},{4,0},{5,1},{6,2},{7,3},{8,12},{9,13},{10,... | collective-permute-start | bytes 221192 | tf_op jit(solution)/shard_map/ppermute | solution.py:146
  34.9 16.4 %copy-start.4 = (f32[128,2304]{1,0:T(8,128)S(1)}, f32[128,2304]{1,0:T(8,128)}, u32[]{:S(2)}) copy-start(f32[128,2304]{1,0:T(8,128)} %refs_7_.1) | copy-start | bytes 3538948
  34.9 14.9 %copy-start.6 = (bf16[16,2304]{1,0:T(8,128)(2,1)}, bf16[16,2304]{1,0:T(8,128)(2,1)S(1)}, u32[]{:S(2)}) copy-start(bf16[16,2304]{1,0:T(8,128)(2,1)S(1)} %fusion.20) | copy-start | bytes 221188
  35.0 6.4 %collective-permute-start.23 = (bf16[16,2304]{1,0:T(8,128)(2,1)S(1)}, bf16[16,2304]{1,0:T(8,128)(2,1)S(1)}, u32[]{:S(2)}, u32[]{:S(2)}) collective-permute-start(bf16[16,2304]{1,0:T(8,128)(2,1)S(1)} %fusion.20), channel_id=1, source_target_pairs={{0,12},{1,13},{2,14},{3,15},{4,8},{5,9},{6,10},{7,11},{8,4},{9,5},... | collective-permute-start | bytes 221192 | tf_op jit(solution)/shard_map/ppermute | solution.py:146
  38.0 6.2 %collective-permute-start.21 = (bf16[16,2304]{1,0:T(8,128)(2,1)S(1)}, bf16[16,2304]{1,0:T(8,128)(2,1)S(1)}, u32[]{:S(2)}, u32[]{:S(2)}) collective-permute-start(bf16[16,2304]{1,0:T(8,128)(2,1)S(1)} %fusion.20), channel_id=1, source_target_pairs={{0,8},{1,9},{2,10},{3,11},{4,12},{5,13},{6,14},{7,15},{8,0},{9,1},... | collective-permute-start | bytes 221192 | tf_op jit(solution)/shard_map/ppermute | solution.py:146
  38.0 6.9 %collective-permute-start.18 = (bf16[16,2304]{1,0:T(8,128)(2,1)S(1)}, bf16[16,2304]{1,0:T(8,128)(2,1)S(1)}, u32[]{:S(2)}, u32[]{:S(2)}) collective-permute-start(bf16[16,2304]{1,0:T(8,128)(2,1)S(1)} %fusion.20), channel_id=1, source_target_pairs={{0,4},{1,5},{2,6},{3,7},{4,0},{5,1},{6,2},{7,3},{8,12},{9,13},{10,... | collective-permute-start | bytes 221192 | tf_op jit(solution)/shard_map/ppermute | solution.py:146
  39.4 6.8 %collective-permute-start.17 = (bf16[16,2304]{1,0:T(8,128)(2,1)S(1)}, bf16[16,2304]{1,0:T(8,128)(2,1)S(1)}, u32[]{:S(2)}, u32[]{:S(2)}) collective-permute-start(bf16[16,2304]{1,0:T(8,128)(2,1)S(1)} %fusion.20), channel_id=1, source_target_pairs={{0,2},{1,3},{2,0},{3,1},{4,6},{5,7},{6,4},{7,5},{8,10},{9,11},{10,... | collective-permute-start | bytes 221192 | tf_op jit(solution)/shard_map/ppermute | solution.py:146
  41.4 4.9 %collective-permute-start.24 = (bf16[16,2304]{1,0:T(8,128)(2,1)S(1)}, bf16[16,2304]{1,0:T(8,128)(2,1)S(1)}, u32[]{:S(2)}, u32[]{:S(2)}) collective-permute-start(bf16[16,2304]{1,0:T(8,128)(2,1)S(1)} %collective-permute-done.23), channel_id=1, source_target_pairs={{0,2},{1,3},{2,0},{3,1},{4,6},{5,7},{6,4},{7,5},{8,10},{9,11},{10,... | collective-permute-start | bytes 221192 | tf_op jit(solution)/shard_map/ppermute | solution.py:146
  44.2 4.6 %collective-permute-start.22 = (bf16[16,2304]{1,0:T(8,128)(2,1)S(1)}, bf16[16,2304]{1,0:T(8,128)(2,1)S(1)}, u32[]{:S(2)}, u32[]{:S(2)}) collective-permute-start(bf16[16,2304]{1,0:T(8,128)(2,1)S(1)} %collective-permute-done.21), channel_id=1, source_target_pairs={{0,2},{1,3},{2,0},{3,1},{4,6},{5,7},{6,4},{7,5},{8,10},{9,11},{10,... | collective-permute-start | bytes 221192 | tf_op jit(solution)/shard_map/ppermute | solution.py:146
  44.9 4.7 %collective-permute-start.19 = (bf16[16,2304]{1,0:T(8,128)(2,1)S(1)}, bf16[16,2304]{1,0:T(8,128)(2,1)S(1)}, u32[]{:S(2)}, u32[]{:S(2)}) collective-permute-start(bf16[16,2304]{1,0:T(8,128)(2,1)S(1)} %collective-permute-done.18), channel_id=1, source_target_pairs={{0,2},{1,3},{2,0},{3,1},{4,6},{5,7},{6,4},{7,5},{8,10},{9,11},{10,... | collective-permute-start | bytes 221192 | tf_op jit(solution)/shard_map/ppermute | solution.py:146
  48.9 2.0 %collective-permute-start.25 = (bf16[64,2304]{1,0:T(8,128)(2,1)S(1)}, bf16[64,2304]{1,0:T(8,128)(2,1)S(1)}, u32[]{:S(2)}, u32[]{:S(2)}) collective-permute-start(bf16[64,2304]{1,0:T(8,128)(2,1)S(1)} %pad_maximum_fusion.1), channel_id=1, source_target_pairs={{0,1},{1,0},{2,3},{3,2},{4,5},{5,4},{6,7},{7,6},{8,9},{9,8},{10,11... | collective-permute-start | bytes 884744 | tf_op jit(solution)/shard_map/ppermute | solution.py:153
  49.7 1.6 %collective-permute-start.20 = (bf16[64,2304]{1,0:T(8,128)(2,1)S(1)}, bf16[64,2304]{1,0:T(8,128)(2,1)S(1)}, u32[]{:S(2)}, u32[]{:S(2)}) collective-permute-start(bf16[64,2304]{1,0:T(8,128)(2,1)S(1)} %pad_maximum_fusion), channel_id=1, source_target_pairs={{0,1},{1,0},{2,3},{3,2},{4,5},{5,4},{6,7},{7,6},{8,9},{9,8},{10,11... | collective-permute-start | bytes 884744 | tf_op jit(solution)/shard_map/ppermute | solution.py:153
  (4 other events, 14.3 us)

commit v22 on v21

--- a/solution.py
+++ b/solution.py
@@ -19,7 +19,18 @@
     )
 
 
-def own_kernel(columns, codes_across, centered, errors, decoder, encoder_total, decoder_total):
+def place_blocks(placed, errors, block):
+    pairs = (placed.shape[0] // block - 4) // 2
+    blocks = [(one, at) for one in errors for at in range(0, one.shape[0], block)]
+    for k, (one, at) in enumerate(blocks):
+        place = k if k < 4 else 4 + 2 * (pairs - 1 - (k - 4) // 2) + k % 2
+        placed[pl.ds(place * block, block), :] = one[pl.ds(at, block), :]
+
+
+def own_kernel(
+    columns, block, codes_across, centered, sent, decoder, encoder_total, decoder_total, errors
+):
+    place_blocks(errors, [sent], block)
     codes_t = codes_across[...]
     signal = inner_last(decoder[...], errors[...])
     delta_t = jnp.where(codes_t.astype(jnp.float32) > 0, signal, 0.0).astype(jnp.bfloat16)
@@ -33,16 +44,17 @@
         )
 
 
-def own_totals(codes_across, centered, errors, decoder):
+def own_totals(codes_across, centered, errors, decoder, block):
     latents, width = decoder.shape
     rows = centered.shape[0]
     vmem = pl.BlockSpec(memory_space=pltpu.VMEM)
     total = jax.ShapeDtypeStruct((latents, width), jnp.float32)
     return pl.pallas_call(
-        functools.partial(own_kernel, columns_of(width)),
+        functools.partial(own_kernel, columns_of(width), block),
         out_shape=(total, total),
         in_specs=[vmem] * 4,
         out_specs=[vmem] * 2,
+        scratch_shapes=[pltpu.VMEM((rows, width), jnp.bfloat16)],
         compiler_params=pltpu.CompilerParams(vmem_limit_bytes=16 * 1024 * 1024 + 8 * rows * width),
         cost_estimate=pl.CostEstimate(
             flops=6 * latents * width * rows,
@@ -57,7 +69,7 @@
     return next(c for c in (256, 128, width) if width % c == 0)
 
 
-def update_kernel(columns, rows_total, codes_across, centered, *refs):
+def update_kernel(columns, block, rows_total, codes_across, centered, *refs):
     blocks = len(refs) - 22
     errors, (encoder, decoder) = refs[:blocks], refs[blocks : blocks + 2]
     moments = refs[blocks + 2 : blocks + 6]
@@ -71,10 +83,7 @@
         at = pl.ds(t * columns, columns)
         return pltpu.make_async_copy(held[i].at[:, at], outs[i].at[:, at], sem.at[t, i])
 
-    start = 0
-    for one in errors:
-        error_all[pl.ds(start, one.shape[0]), :] = one[...]
-        start += one.shape[0]
+    place_blocks(error_all, errors, block)
     first = (1.0 - beta_first) / rows_total
     second = (1.0 - beta_second) / (rows_total * rows_total)
 
@@ -107,7 +116,7 @@
             write(t, i).wait()
 
 
-def update(total_rows, codes_across, centered, errors, weights, moments, totals):
+def update(total_rows, codes_across, centered, errors, block, weights, moments, totals):
     latents, width = weights[0].shape
     rows = centered.shape[0]
     columns = columns_of(width)
@@ -117,7 +126,7 @@
     wide = pltpu.VMEM((latents, width), jnp.float32)
     narrow = pltpu.VMEM((latents, width), jnp.bfloat16)
     return pl.pallas_call(
-        functools.partial(update_kernel, columns, float(total_rows)),
+        functools.partial(update_kernel, columns, block, float(total_rows)),
         out_shape=(half, full, full, half, full, full),
         in_specs=[vmem] * (len(errors) + 10),
         out_specs=[pl.BlockSpec(memory_space=pl.ANY)] * 6,
@@ -180,7 +189,10 @@
     total_rows = rows_here * size
 
     even, odd = gather_chips(activations, chips)
-    rows_core = jnp.concatenate(in_turn(even, odd), 0)
+    blocks = in_turn(even, odd)
+    for k in range(chips - 2, 2, -2):
+        blocks += blocks[k : k + 2]
+    rows_core = jnp.concatenate(blocks[:4] + blocks[chips:], 0)
     sent, _ = lax.optimization_barrier(((encoder_bias, encoder, decoder), odd[1]))
     bias_both, encoder_both, decoder_both = (
         jnp.concatenate([mine, to_other_core(one)], 0)
@@ -216,8 +228,8 @@
     near_sent, _ = lax.optimization_barrier((given(0, 4), (other_codes, other_centered)))
     own, near = pair_sums(0, 4, near_sent)
     summed = own + to_chip(near.astype(jnp.bfloat16), 2).astype(jnp.float32)
-    for k, one in enumerate(far, 2):
-        summed = summed + to_chip(one, 2 * k).astype(jnp.float32)
+    for k, one in enumerate(far):
+        summed = summed + to_chip(one, chips - 2 - 2 * k).astype(jnp.float32)
     row_error = (summed - centered[:rows_here].astype(jnp.float32)).astype(jnp.bfloat16)
 
     row_error, other_codes, other_centered = lax.optimization_barrier(
@@ -226,7 +238,7 @@
     blocks = in_turn(*gather_chips(row_error, chips))
     errors = jnp.concatenate(blocks, 0)
     other_errors = [to_other_core(jnp.concatenate(one, 0)) for one in (blocks[:4], blocks[4:])]
-    totals = own_totals(codes[:, :latents_here].T, centered, errors, decoder)
+    totals = own_totals(codes[:, :latents_here].T, centered, errors, decoder, rows_here)
     (
         encoder_next,
         encoder_moment_next,
@@ -239,6 +251,7 @@
         other_codes.T,
         other_centered,
         other_errors,
+        rows_here,
         (encoder, decoder),
         (encoder_moment, encoder_square, decoder_moment, decoder_square),
         totals,

time: 54.9 us -> 56 us (1.020)
  starting transfers between devices: 27.2 us -> 28.8 us
  waiting for transfers between devices: 19.3 us -> 18.7 us
    ppermute x19, starting transfers between devices: 25.9 us -> 27.6 us  [to_chip(): lax.ppermute(block, 'latent', [(i, i ^ 2 * distance) for i in range(size)])]
    ppermute x19, waiting for transfers between devices: 17.2 us -> 15.8 us  [to_chip(): lax.ppermute(block, 'latent', [(i, i ^ 2 * distance) for i in range(size)])]
    ppermute x7, waiting for transfers between devices: 2.08 us -> 2.93 us  [to_other_core(): return lax.ppermute(block, 'latent', [(i, i ^ 1) for i in range(size)])]
  transfers between devices with their start and end apart: 26 -> 26, of which waited for: 13 -> 16; matrix products, arithmetic and copies ran while one was open for 3% -> 3% of each run, Pallas kernels for 2% -> 2%
where the time goes in v22:
time: 56 us; the launch traced here: 55.8 us
  starting transfers between devices  28.8 us (51%)
  waiting for transfers between devices  18.7 us (33%)
  Pallas kernels  4.23 us (8%)
  local copies, waits for them, and re-layouts  1.47 us (3%)
  matrix products  1.26 us (2%)
  between operations  0.98 us (2%)
    ppermute x19, starting transfers between devices, to_chip(): lax.ppermute(block, 'latent', [(i, i ^ 2 * distance) for i in range(size)])  27.6 us
    ppermute x19, waiting for transfers between devices, to_chip(): lax.ppermute(block, 'latent', [(i, i ^ 2 * distance) for i in range(size)])  15.8 us
    pallas_call x1, Pallas kernels, update(): pl.pallas_call(functools.partial(update_kernel, columns, block, float(tot...  3.26 us
    ppermute x7, waiting for transfers between devices, to_other_core(): return lax.ppermute(block, 'latent', [(i, i ^ 1) for i in range(size)])  2.93 us
    unnamed x35, local copies, waits for them, and re-layouts  1.39 us
    ppermute x7, starting transfers between devices, to_other_core(): return lax.ppermute(block, 'latent', [(i, i ^ 1) for i in range(size)])  1.23 us
  transfers between devices with their start and end apart: 26, of which 16 were waited for; matrix products, arithmetic and copies ran while one was open for 3% of the time, Pallas kernels for 2%

profile of v22, /device:TPU:0, one launch (start us, length us, event | category | flops | bytes accessed | tf_op | source)
XLA Modules:
  0.0 55.8 jit_solution(406177502025343871)
XLA Ops:
  0.7 5.1 %collective-permute-start.3 = (bf16[16,2304]{1,0:T(8,128)(2,1)}, bf16[16,2304]{1,0:T(8,128)(2,1)S(1)}, u32[]{:S(2)}, u32[]{:S(2)}) collective-permute-start(bf16[16,2304]{1,0:T(8,128)(2,1)} %param.9), channel_id=1, source_target_pairs={{0,12},{1,13},{2,14},{3,15},{4,8},{5,9},{6,10},{7,11},{8,4},{9,5},... | collective-permute-start | bytes 221192 | tf_op jit(solution)/shard_map/ppermute | solution.py:155
  5.8 1.5 %collective-permute-start = (bf16[16,2304]{1,0:T(8,128)(2,1)}, bf16[16,2304]{1,0:T(8,128)(2,1)S(1)}, u32[]{:S(2)}, u32[]{:S(2)}) collective-permute-start(bf16[16,2304]{1,0:T(8,128)(2,1)} %param.9), channel_id=1, source_target_pairs={{0,2},{1,3},{2,0},{3,1},{4,6},{5,7},{6,4},{7,5},{8,10},{9,11},{10,... | collective-permute-start | bytes 221192 | tf_op jit(solution)/shard_map/ppermute | solution.py:155
  7.3 0.8 %collective-permute-start.5 = (bf16[16,2304]{1,0:T(8,128)(2,1)}, bf16[16,2304]{1,0:T(8,128)(2,1)S(1)}, u32[]{:S(2)}, u32[]{:S(2)}) collective-permute-start(bf16[16,2304]{1,0:T(8,128)(2,1)} %param.9), channel_id=1, source_target_pairs={{0,8},{1,9},{2,10},{3,11},{4,12},{5,13},{6,14},{7,15},{8,0},{9,1},... | collective-permute-start | bytes 221192 | tf_op jit(solution)/shard_map/ppermute | solution.py:155
  8.1 1.1 %constant_dynamic-update-slice_fusion.9 = bf16[256,2304]{1,0:T(8,128)(2,1)S(1)} fusion(bf16[128,2304]{1,0:T(8,128)(2,1)} %refs_3_.1), kind=kLoop, calls=%fused_computation.37 | loop fusion | bytes 1179648
  9.2 1.4 %collective-permute-start.4 = (bf16[16,2304]{1,0:T(8,128)(2,1)S(1)}, bf16[16,2304]{1,0:T(8,128)(2,1)S(1)}, u32[]{:S(2)}, u32[]{:S(2)}) collective-permute-start(bf16[16,2304]{1,0:T(8,128)(2,1)S(1)} %collective-permute-done.3), channel_id=1, source_target_pairs={{0,2},{1,3},{2,0},{3,1},{4,6},{5,7},{6,4},{7,5},{8,10},{9,11},{10,... | collective-permute-start | bytes 221192 | tf_op jit(solution)/shard_map/ppermute | solution.py:155
  10.7 2.0 %collective-permute-start.2 = (bf16[16,2304]{1,0:T(8,128)(2,1)S(1)}, bf16[16,2304]{1,0:T(8,128)(2,1)S(1)}, u32[]{:S(2)}, u32[]{:S(2)}) collective-permute-start(bf16[16,2304]{1,0:T(8,128)(2,1)S(1)} %collective-permute-done.1), channel_id=1, source_target_pairs={{0,2},{1,3},{2,0},{3,1},{4,6},{5,7},{6,4},{7,5},{8,10},{9,11},{10,... | collective-permute-start | bytes 221192 | tf_op jit(solution)/shard_map/ppermute | solution.py:155
  13.1 0.5 collective-permute-start.6
  13.6 2.3 %collective-permute-done.2 = bf16[16,2304]{1,0:T(8,128)(2,1)S(1)} collective-permute-done((bf16[16,2304]{1,0:T(8,128)(2,1)S(1)}, bf16[16,2304]{1,0:T(8,128)(2,1)S(1)}, u32[]{:S(2)}, u32[]{:S(2)}) %collective-permute-start.2) | collective-permute-done | bytes 73760 | tf_op jit(solution)/shard_map/ppermute | solution.py:155
  15.9 0.5 collective-permute-start.7
  16.6 0.9 %collective-permute-done.6 = bf16[16,2304]{1,0:T(8,128)(2,1)S(1)} collective-permute-done((bf16[16,2304]{1,0:T(8,128)(2,1)S(1)}, bf16[16,2304]{1,0:T(8,128)(2,1)S(1)}, u32[]{:S(2)}, u32[]{:S(2)}) %collective-permute-start.6) | collective-permute-done | bytes 73760 | tf_op jit(solution)/shard_map/ppermute | solution.py:155
  17.6 0.5 collective-permute-done.7
  19.8 1.6 %collective-permute-start.14 = (bf16[32,2304]{1,0:T(8,128)(2,1)S(1)}, bf16[32,2304]{1,0:T(8,128)(2,1)S(1)}, u32[]{:S(2)}, u32[]{:S(2)}) collective-permute-start(bf16[32,2304]{1,0:T(8,128)(2,1)S(1)} %pad_maximum_fusion.3), channel_id=1, source_target_pairs={{0,2},{1,3},{2,0},{3,1},{4,6},{5,7},{6,4},{7,5},{8,10},{9,11},{10,... | collective-permute-start | bytes 442376 | tf_op jit(solution)/shard_map/ppermute | solution.py:155
  21.9 0.7 %collective-permute-done.10 = bf16[128,128]{0,1:T(8,128)(2,1)S(1)} collective-permute-done((bf16[128,128]{0,1:T(8,128)(2,1)S(1)}, bf16[128,128]{0,1:T(8,128)(2,1)S(1)}, u32[]{:S(2)}, u32[]{:S(2)}) %collective-permute-start.10) | collective-permute-done | bytes 32800 | tf_op jit(solution)/shard_map/ppermute | solution.py:162
  22.6 0.9 %collective-permute-done.11.centered = bf16[128,2304]{1,0:T(8,128)(2,1)S(1)} collective-permute-done((bf16[128,2304]{1,0:T(8,128)(2,1)S(1)}, bf16[128,2304]{1,0:T(8,128)(2,1)S(1)}, u32[]{:S(2)}, u32[]{:S(2)}) %collective-permute-start.11) | collective-permute-done | bytes 589856 | tf_op jit(solution)/shard_map/ppermute | solution.py:162
  23.5 0.5 collective-permute-start.12
  24.0 1.9 %collective-permute-done.14 = bf16[32,2304]{1,0:T(8,128)(2,1)S(1)} collective-permute-done((bf16[32,2304]{1,0:T(8,128)(2,1)S(1)}, bf16[32,2304]{1,0:T(8,128)(2,1)S(1)}, u32[]{:S(2)}, u32[]{:S(2)}) %collective-permute-start.14) | collective-permute-done | bytes 147488 | tf_op jit(solution)/shard_map/ppermute | solution.py:155
  26.0 3.4 %collective-permute-start.15 = (bf16[16,2304]{1,0:T(8,128)(2,1)S(1)}, bf16[16,2304]{1,0:T(8,128)(2,1)S(1)}, u32[]{:S(2)}, u32[]{:S(2)}) collective-permute-start(bf16[16,2304]{1,0:T(8,128)(2,1)S(1)} %get-tuple-element.39), channel_id=1, source_target_pairs={{0,12},{1,13},{2,14},{3,15},{4,8},{5,9},{6,10},{7,11},{8,4},{9,5},... | collective-permute-start | bytes 221192 | tf_op jit(solution)/shard_map/ppermute | solution.py:155
  29.6 0.9 %collective-permute-start.13 = (bf16[16,2304]{1,0:T(8,128)(2,1)S(1)}, bf16[16,2304]{1,0:T(8,128)(2,1)S(1)}, u32[]{:S(2)}, u32[]{:S(2)}) collective-permute-start(bf16[16,2304]{1,0:T(8,128)(2,1)S(1)} %fusion.15), channel_id=1, source_target_pairs={{0,4},{1,5},{2,6},{3,7},{4,0},{5,1},{6,2},{7,3},{8,12},{9,13},{10,... | collective-permute-start | bytes 221192 | tf_op jit(solution)/shard_map/ppermute | solution.py:155
  30.6 2.0 %collective-permute-done.15 = bf16[16,2304]{1,0:T(8,128)(2,1)S(1)} collective-permute-done((bf16[16,2304]{1,0:T(8,128)(2,1)S(1)}, bf16[16,2304]{1,0:T(8,128)(2,1)S(1)}, u32[]{:S(2)}, u32[]{:S(2)}) %collective-permute-start.15) | collective-permute-done | bytes 73760 | tf_op jit(solution)/shard_map/ppermute | solution.py:155
  32.5 3.1 %collective-permute-done.16 = bf16[16,2304]{1,0:T(8,128)(2,1)S(1)} collective-permute-done((bf16[16,2304]{1,0:T(8,128)(2,1)S(1)}, bf16[16,2304]{1,0:T(8,128)(2,1)S(1)}, u32[]{:S(2)}, u32[]{:S(2)}) %collective-permute-start.16) | collective-permute-done | bytes 73760 | tf_op jit(solution)/shard_map/ppermute | solution.py:155
  35.7 2.5 %collective-permute-start.23 = (bf16[16,2304]{1,0:T(8,128)(2,1)S(1)}, bf16[16,2304]{1,0:T(8,128)(2,1)S(1)}, u32[]{:S(2)}, u32[]{:S(2)}) collective-permute-start(bf16[16,2304]{1,0:T(8,128)(2,1)S(1)} %fusion.20), channel_id=1, source_target_pairs={{0,12},{1,13},{2,14},{3,15},{4,8},{5,9},{6,10},{7,11},{8,4},{9,5},... | collective-permute-start | bytes 221192 | tf_op jit(solution)/shard_map/ppermute | solution.py:155
  38.2 2.0 %collective-permute-start.18 = (bf16[16,2304]{1,0:T(8,128)(2,1)S(1)}, bf16[16,2304]{1,0:T(8,128)(2,1)S(1)}, u32[]{:S(2)}, u32[]{:S(2)}) collective-permute-start(bf16[16,2304]{1,0:T(8,128)(2,1)S(1)} %fusion.20), channel_id=1, source_target_pairs={{0,4},{1,5},{2,6},{3,7},{4,0},{5,1},{6,2},{7,3},{8,12},{9,13},{10,... | collective-permute-start | bytes 221192 | tf_op jit(solution)/shard_map/ppermute | solution.py:155
  40.2 1.4 %collective-permute-start.17 = (bf16[16,2304]{1,0:T(8,128)(2,1)S(1)}, bf16[16,2304]{1,0:T(8,128)(2,1)S(1)}, u32[]{:S(2)}, u32[]{:S(2)}) collective-permute-start(bf16[16,2304]{1,0:T(8,128)(2,1)S(1)} %fusion.20), channel_id=1, source_target_pairs={{0,2},{1,3},{2,0},{3,1},{4,6},{5,7},{6,4},{7,5},{8,10},{9,11},{10,... | collective-permute-start | bytes 221192 | tf_op jit(solution)/shard_map/ppermute | solution.py:155
  42.0 1.9 %collective-permute-start.24 = (bf16[16,2304]{1,0:T(8,128)(2,1)S(1)}, bf16[16,2304]{1,0:T(8,128)(2,1)S(1)}, u32[]{:S(2)}, u32[]{:S(2)}) collective-permute-start(bf16[16,2304]{1,0:T(8,128)(2,1)S(1)} %collective-permute-done.23), channel_id=1, source_target_pairs={{0,2},{1,3},{2,0},{3,1},{4,6},{5,7},{6,4},{7,5},{8,10},{9,11},{10,... | collective-permute-start | bytes 221192 | tf_op jit(solution)/shard_map/ppermute | solution.py:155
  43.9 1.1 %collective-permute-done.21 = bf16[16,2304]{1,0:T(8,128)(2,1)S(1)} collective-permute-done((bf16[16,2304]{1,0:T(8,128)(2,1)S(1)}, bf16[16,2304]{1,0:T(8,128)(2,1)S(1)}, u32[]{:S(2)}, u32[]{:S(2)}) %collective-permute-start.21) | collective-permute-done | bytes 73760 | tf_op jit(solution)/shard_map/ppermute | solution.py:155
  45.0 1.1 %collective-permute-start.22 = (bf16[16,2304]{1,0:T(8,128)(2,1)S(1)}, bf16[16,2304]{1,0:T(8,128)(2,1)S(1)}, u32[]{:S(2)}, u32[]{:S(2)}) collective-permute-start(bf16[16,2304]{1,0:T(8,128)(2,1)S(1)} %collective-permute-done.21), channel_id=1, source_target_pairs={{0,2},{1,3},{2,0},{3,1},{4,6},{5,7},{6,4},{7,5},{8,10},{9,11},{10,... | collective-permute-start | bytes 221192 | tf_op jit(solution)/shard_map/ppermute | solution.py:155
  46.1 0.9 %collective-permute-start.19 = (bf16[16,2304]{1,0:T(8,128)(2,1)S(1)}, bf16[16,2304]{1,0:T(8,128)(2,1)S(1)}, u32[]{:S(2)}, u32[]{:S(2)}) collective-permute-start(bf16[16,2304]{1,0:T(8,128)(2,1)S(1)} %collective-permute-done.18), channel_id=1, source_target_pairs={{0,2},{1,3},{2,0},{3,1},{4,6},{5,7},{6,4},{7,5},{8,10},{9,11},{10,... | collective-permute-start | bytes 221192 | tf_op jit(solution)/shard_map/ppermute | solution.py:155
  47.1 2.8 %collective-permute-done.22 = bf16[16,2304]{1,0:T(8,128)(2,1)S(1)} collective-permute-done((bf16[16,2304]{1,0:T(8,128)(2,1)S(1)}, bf16[16,2304]{1,0:T(8,128)(2,1)S(1)}, u32[]{:S(2)}, u32[]{:S(2)}) %collective-permute-start.22) | collective-permute-done | bytes 73760 | tf_op jit(solution)/shard_map/ppermute | solution.py:155
  50.0 0.7 %collective-permute-done.19 = bf16[16,2304]{1,0:T(8,128)(2,1)S(1)} collective-permute-done((bf16[16,2304]{1,0:T(8,128)(2,1)S(1)}, bf16[16,2304]{1,0:T(8,128)(2,1)S(1)}, u32[]{:S(2)}, u32[]{:S(2)}) %collective-permute-start.19) | collective-permute-done | bytes 73760 | tf_op jit(solution)/shard_map/ppermute | solution.py:155
  50.9 1.0 %own_totals.1 = (f32[128,2304]{1,0:T(8,128)S(1)}, f32[128,2304]{1,0:T(8,128)S(1)}) custom-call(bf16[128,128]{1,0:T(8,128)(2,1)S(1)} %get-tuple-element.45.codes_across, bf16[128,2304]{1,0:T(8,128)(2,1)S(1)} %subtract_convert_fusion.centered, bf16[128,2304]{1,0:T(8,128)(2,1)S(1)} %constant_dynamic-update-slice_fusion.10.sent, bf16[128,2304]{1,0:T(8,128)(2,1)S(1)} %copy-done), custom_call_target="tpu_custom_call" | custom-call | flops 226492416 | bytes 4718592 | tf_op jit(solution)/shard_map/own_totals/pallas_call | solution.py:52
  51.9 0.5 collective-permute-done.20.refs_0_
  52.5 3.3 %update.1 = (bf16[128,2304]{1,0:T(8,128)(2,1)}, f32[128,2304]{1,0:T(8,128)}, f32[128,2304]{1,0:T(8,128)}, bf16[128,2304]{1,0:T(8,128)(2,1)}, f32[128,2304]{1,0:T(8,128)}, /*index=5*/f32[128,2304]{1,0:T(8,128)}) custom-call(bf16[128,128]{1,0:T(8,128)(2,1)S(1)} %bitcast.6, bf16[128,2304]{1,0:T(8,128)(2,1)S(1)} %collective-permute-done.11.centered, ...), custom_call_target="tpu_custom_call" | custom-call | flops 226492416 | bytes 12976128 | tf_op jit(solution)/shard_map/update/pallas_call | solution.py:128
  (75 shorter events, 4.0 us)
Async XLA Ops:
  0.6 15.8 %copy-start = (bf16[128,2304]{1,0:T(8,128)(2,1)S(1)}, bf16[128,2304]{1,0:T(8,128)(2,1)}, u32[]{:S(2)}) copy-start(bf16[128,2304]{1,0:T(8,128)(2,1)} %refs_3_.1) | copy-start | bytes 1769476
  0.7 15.3 %copy-start.5 = (bf16[128,2304]{1,0:T(8,128)(2,1)S(1)}, bf16[128,2304]{1,0:T(8,128)(2,1)}, u32[]{:S(2)}) copy-start(bf16[128,2304]{1,0:T(8,128)(2,1)} %refs_2_.1) | copy-start | bytes 1769476
  0.7 15.2 %copy-start.9 = (f32[128]{0:T(128)S(1)}, f32[128]{0:T(128)}, u32[]{:S(2)}) copy-start(f32[128]{0:T(128)} %param.11) | copy-start | bytes 1540
  0.7 16.7 %copy-start.8 = (f32[2304]{0:T(1024)S(1)}, f32[2304]{0:T(1024)}, u32[]{:S(2)}) copy-start(f32[2304]{0:T(1024)} %param.13) | copy-start | bytes 27652
  0.7 8.6 %collective-permute-start.3 = (bf16[16,2304]{1,0:T(8,128)(2,1)}, bf16[16,2304]{1,0:T(8,128)(2,1)S(1)}, u32[]{:S(2)}, u32[]{:S(2)}) collective-permute-start(bf16[16,2304]{1,0:T(8,128)(2,1)} %param.9), channel_id=1, source_target_pairs={{0,12},{1,13},{2,14},{3,15},{4,8},{5,9},{6,10},{7,11},{8,4},{9,5},... | collective-permute-start | bytes 221192 | tf_op jit(solution)/shard_map/ppermute | solution.py:155
  5.8 4.9 %collective-permute-start.1 = (bf16[16,2304]{1,0:T(8,128)(2,1)}, bf16[16,2304]{1,0:T(8,128)(2,1)S(1)}, u32[]{:S(2)}, u32[]{:S(2)}) collective-permute-start(bf16[16,2304]{1,0:T(8,128)(2,1)} %param.9), channel_id=1, source_target_pairs={{0,4},{1,5},{2,6},{3,7},{4,0},{5,1},{6,2},{7,3},{8,12},{9,13},{10,... | collective-permute-start | bytes 221192 | tf_op jit(solution)/shard_map/ppermute | solution.py:155
  5.8 7.8 %collective-permute-start = (bf16[16,2304]{1,0:T(8,128)(2,1)}, bf16[16,2304]{1,0:T(8,128)(2,1)S(1)}, u32[]{:S(2)}, u32[]{:S(2)}) collective-permute-start(bf16[16,2304]{1,0:T(8,128)(2,1)} %param.9), channel_id=1, source_target_pairs={{0,2},{1,3},{2,0},{3,1},{4,6},{5,7},{6,4},{7,5},{8,10},{9,11},{10,... | collective-permute-start | bytes 221192 | tf_op jit(solution)/shard_map/ppermute | solution.py:155
  7.3 5.7 %collective-permute-start.5 = (bf16[16,2304]{1,0:T(8,128)(2,1)}, bf16[16,2304]{1,0:T(8,128)(2,1)S(1)}, u32[]{:S(2)}, u32[]{:S(2)}) collective-permute-start(bf16[16,2304]{1,0:T(8,128)(2,1)} %param.9), channel_id=1, source_target_pairs={{0,8},{1,9},{2,10},{3,11},{4,12},{5,13},{6,14},{7,15},{8,0},{9,1},... | collective-permute-start | bytes 221192 | tf_op jit(solution)/shard_map/ppermute | solution.py:155
  9.2 7.3 %collective-permute-start.4 = (bf16[16,2304]{1,0:T(8,128)(2,1)S(1)}, bf16[16,2304]{1,0:T(8,128)(2,1)S(1)}, u32[]{:S(2)}, u32[]{:S(2)}) collective-permute-start(bf16[16,2304]{1,0:T(8,128)(2,1)S(1)} %collective-permute-done.3), channel_id=1, source_target_pairs={{0,2},{1,3},{2,0},{3,1},{4,6},{5,7},{6,4},{7,5},{8,10},{9,11},{10,... | collective-permute-start | bytes 221192 | tf_op jit(solution)/shard_map/ppermute | solution.py:155
  10.7 5.2 %collective-permute-start.2 = (bf16[16,2304]{1,0:T(8,128)(2,1)S(1)}, bf16[16,2304]{1,0:T(8,128)(2,1)S(1)}, u32[]{:S(2)}, u32[]{:S(2)}) collective-permute-start(bf16[16,2304]{1,0:T(8,128)(2,1)S(1)} %collective-permute-done.1), channel_id=1, source_target_pairs={{0,2},{1,3},{2,0},{3,1},{4,6},{5,7},{6,4},{7,5},{8,10},{9,11},{10,... | collective-permute-start | bytes 221192 | tf_op jit(solution)/shard_map/ppermute | solution.py:155
  13.1 4.4 %collective-permute-start.6 = (bf16[16,2304]{1,0:T(8,128)(2,1)S(1)}, bf16[16,2304]{1,0:T(8,128)(2,1)S(1)}, u32[]{:S(2)}, u32[]{:S(2)}) collective-permute-start(bf16[16,2304]{1,0:T(8,128)(2,1)S(1)} %collective-permute-done.5), channel_id=1, source_target_pairs={{0,2},{1,3},{2,0},{3,1},{4,6},{5,7},{6,4},{7,5},{8,10},{9,11},{10,... | collective-permute-start | bytes 221192 | tf_op jit(solution)/shard_map/ppermute | solution.py:155
  15.9 1.6 %collective-permute-start.8 = (f32[128]{0:T(128)S(1)}, f32[128]{0:T(128)S(1)}, u32[]{:S(2)}, u32[]{:S(2)}) collective-permute-start(f32[128]{0:T(128)S(1)} %copy-done.9), channel_id=1, source_target_pairs={{0,1},{1,0},{2,3},{3,2},{4,5},{5,4},{6,7},{7,6},{8,9},{9,8},{10,11... | collective-permute-start | bytes 1544 | tf_op jit(solution)/shard_map/ppermute | solution.py:162
  15.9 2.1 %collective-permute-start.7 = (bf16[128,2304]{1,0:T(8,128)(2,1)S(1)}, bf16[128,2304]{1,0:T(8,128)(2,1)S(1)}, u32[]{:S(2)}, u32[]{:S(2)}) collective-permute-start(bf16[128,2304]{1,0:T(8,128)(2,1)S(1)} %copy-done.5), channel_id=1, source_target_pairs={{0,1},{1,0},{2,3},{3,2},{4,5},{5,4},{6,7},{7,6},{8,9},{9,8},{10,11... | collective-permute-start | bytes 1769480 | tf_op jit(solution)/shard_map/ppermute | solution.py:162
  16.4 2.5 %collective-permute-start.9 = (bf16[128,2304]{1,0:T(8,128)(2,1)S(1)}, bf16[128,2304]{1,0:T(8,128)(2,1)S(1)}, u32[]{:S(2)}, u32[]{:S(2)}) collective-permute-start(bf16[128,2304]{1,0:T(8,128)(2,1)S(1)} %copy-done), channel_id=1, source_target_pairs={{0,1},{1,0},{2,3},{3,2},{4,5},{5,4},{6,7},{7,6},{8,9},{9,8},{10,11... | collective-permute-start | bytes 1769480 | tf_op jit(solution)/shard_map/ppermute | solution.py:162
  19.8 6.2 %collective-permute-start.14 = (bf16[32,2304]{1,0:T(8,128)(2,1)S(1)}, bf16[32,2304]{1,0:T(8,128)(2,1)S(1)}, u32[]{:S(2)}, u32[]{:S(2)}) collective-permute-start(bf16[32,2304]{1,0:T(8,128)(2,1)S(1)} %pad_maximum_fusion.3), channel_id=1, source_target_pairs={{0,2},{1,3},{2,0},{3,1},{4,6},{5,7},{6,4},{7,5},{8,10},{9,11},{10,... | collective-permute-start | bytes 442376 | tf_op jit(solution)/shard_map/ppermute | solution.py:155
  21.4 1.2 %collective-permute-start.10 = (bf16[128,128]{0,1:T(8,128)(2,1)S(1)}, bf16[128,128]{0,1:T(8,128)(2,1)S(1)}, u32[]{:S(2)}, u32[]{:S(2)}) collective-permute-start(bf16[128,128]{0,1:T(8,128)(2,1)S(1)} %get-tuple-element.46), channel_id=1, source_target_pairs={{0,1},{1,0},{2,3},{3,2},{4,5},{5,4},{6,7},{7,6},{8,9},{9,8},{10,11... | collective-permute-start | bytes 98312 | tf_op jit(solution)/shard_map/ppermute | solution.py:162
  21.4 2.1 %collective-permute-start.11 = (bf16[128,2304]{1,0:T(8,128)(2,1)S(1)}, bf16[128,2304]{1,0:T(8,128)(2,1)S(1)}, u32[]{:S(2)}, u32[]{:S(2)}) collective-permute-start(bf16[128,2304]{1,0:T(8,128)(2,1)S(1)} %subtract_convert_fusion.centered), channel_id=1, source_target_pairs={{0,1},{1,0},{2,3},{3,2},{4,5},{5,4},{6,7},{7,6},{8,9},{9,8},{10,11... | collective-permute-start | bytes 1769480 | tf_op jit(solution)/shard_map/ppermute | solution.py:162
  23.5 6.1 %collective-permute-start.12 = (bf16[32,2304]{1,0:T(8,128)(2,1)S(1)}, bf16[32,2304]{1,0:T(8,128)(2,1)S(1)}, u32[]{:S(2)}, u32[]{:S(2)}) collective-permute-start(bf16[32,2304]{1,0:T(8,128)(2,1)S(1)} %pad_maximum_fusion.2), channel_id=1, source_target_pairs={{0,2},{1,3},{2,0},{3,1},{4,6},{5,7},{6,4},{7,5},{8,10},{9,11},{10,... | collective-permute-start | bytes 442376 | tf_op jit(solution)/shard_map/ppermute | solution.py:155
  26.0 6.6 %collective-permute-start.15 = (bf16[16,2304]{1,0:T(8,128)(2,1)S(1)}, bf16[16,2304]{1,0:T(8,128)(2,1)S(1)}, u32[]{:S(2)}, u32[]{:S(2)}) collective-permute-start(bf16[16,2304]{1,0:T(8,128)(2,1)S(1)} %get-tuple-element.39), channel_id=1, source_target_pairs={{0,12},{1,13},{2,14},{3,15},{4,8},{5,9},{6,10},{7,11},{8,4},{9,5},... | collective-permute-start | bytes 221192 | tf_op jit(solution)/shard_map/ppermute | solution.py:155
  29.4 6.2 %collective-permute-start.16 = (bf16[16,2304]{1,0:T(8,128)(2,1)S(1)}, bf16[16,2304]{1,0:T(8,128)(2,1)S(1)}, u32[]{:S(2)}, u32[]{:S(2)}) collective-permute-start(bf16[16,2304]{1,0:T(8,128)(2,1)S(1)} %get-tuple-element.40), channel_id=1, source_target_pairs={{0,8},{1,9},{2,10},{3,11},{4,12},{5,13},{6,14},{7,15},{8,0},{9,1},... | collective-permute-start | bytes 221192 | tf_op jit(solution)/shard_map/ppermute | solution.py:155
  29.6 6.0 %collective-permute-start.13 = (bf16[16,2304]{1,0:T(8,128)(2,1)S(1)}, bf16[16,2304]{1,0:T(8,128)(2,1)S(1)}, u32[]{:S(2)}, u32[]{:S(2)}) collective-permute-start(bf16[16,2304]{1,0:T(8,128)(2,1)S(1)} %fusion.15), channel_id=1, source_target_pairs={{0,4},{1,5},{2,6},{3,7},{4,0},{5,1},{6,2},{7,3},{8,12},{9,13},{10,... | collective-permute-start | bytes 221192 | tf_op jit(solution)/shard_map/ppermute | solution.py:155
  35.6 16.7 %copy-start.4 = (f32[128,2304]{1,0:T(8,128)S(1)}, f32[128,2304]{1,0:T(8,128)}, u32[]{:S(2)}) copy-start(f32[128,2304]{1,0:T(8,128)} %refs_7_.1) | copy-start | bytes 3538948
  35.7 15.2 %copy-start.6 = (bf16[16,2304]{1,0:T(8,128)(2,1)}, bf16[16,2304]{1,0:T(8,128)(2,1)S(1)}, u32[]{:S(2)}) copy-start(bf16[16,2304]{1,0:T(8,128)(2,1)S(1)} %fusion.20) | copy-start | bytes 221188
  35.7 6.3 %collective-permute-start.23 = (bf16[16,2304]{1,0:T(8,128)(2,1)S(1)}, bf16[16,2304]{1,0:T(8,128)(2,1)S(1)}, u32[]{:S(2)}, u32[]{:S(2)}) collective-permute-start(bf16[16,2304]{1,0:T(8,128)(2,1)S(1)} %fusion.20), channel_id=1, source_target_pairs={{0,12},{1,13},{2,14},{3,15},{4,8},{5,9},{6,10},{7,11},{8,4},{9,5},... | collective-permute-start | bytes 221192 | tf_op jit(solution)/shard_map/ppermute | solution.py:155
  38.2 6.8 %collective-permute-start.21 = (bf16[16,2304]{1,0:T(8,128)(2,1)S(1)}, bf16[16,2304]{1,0:T(8,128)(2,1)S(1)}, u32[]{:S(2)}, u32[]{:S(2)}) collective-permute-start(bf16[16,2304]{1,0:T(8,128)(2,1)S(1)} %fusion.20), channel_id=1, source_target_pairs={{0,8},{1,9},{2,10},{3,11},{4,12},{5,13},{6,14},{7,15},{8,0},{9,1},... | collective-permute-start | bytes 221192 | tf_op jit(solution)/shard_map/ppermute | solution.py:155
  38.2 7.9 %collective-permute-start.18 = (bf16[16,2304]{1,0:T(8,128)(2,1)S(1)}, bf16[16,2304]{1,0:T(8,128)(2,1)S(1)}, u32[]{:S(2)}, u32[]{:S(2)}) collective-permute-start(bf16[16,2304]{1,0:T(8,128)(2,1)S(1)} %fusion.20), channel_id=1, source_target_pairs={{0,4},{1,5},{2,6},{3,7},{4,0},{5,1},{6,2},{7,3},{8,12},{9,13},{10,... | collective-permute-start | bytes 221192 | tf_op jit(solution)/shard_map/ppermute | solution.py:155
  40.2 6.9 %collective-permute-start.17 = (bf16[16,2304]{1,0:T(8,128)(2,1)S(1)}, bf16[16,2304]{1,0:T(8,128)(2,1)S(1)}, u32[]{:S(2)}, u32[]{:S(2)}) collective-permute-start(bf16[16,2304]{1,0:T(8,128)(2,1)S(1)} %fusion.20), channel_id=1, source_target_pairs={{0,2},{1,3},{2,0},{3,1},{4,6},{5,7},{6,4},{7,5},{8,10},{9,11},{10,... | collective-permute-start | bytes 221192 | tf_op jit(solution)/shard_map/ppermute | solution.py:155
  42.0 5.1 %collective-permute-start.24 = (bf16[16,2304]{1,0:T(8,128)(2,1)S(1)}, bf16[16,2304]{1,0:T(8,128)(2,1)S(1)}, u32[]{:S(2)}, u32[]{:S(2)}) collective-permute-start(bf16[16,2304]{1,0:T(8,128)(2,1)S(1)} %collective-permute-done.23), channel_id=1, source_target_pairs={{0,2},{1,3},{2,0},{3,1},{4,6},{5,7},{6,4},{7,5},{8,10},{9,11},{10,... | collective-permute-start | bytes 221192 | tf_op jit(solution)/shard_map/ppermute | solution.py:155
  45.0 4.9 %collective-permute-start.22 = (bf16[16,2304]{1,0:T(8,128)(2,1)S(1)}, bf16[16,2304]{1,0:T(8,128)(2,1)S(1)}, u32[]{:S(2)}, u32[]{:S(2)}) collective-permute-start(bf16[16,2304]{1,0:T(8,128)(2,1)S(1)} %collective-permute-done.21), channel_id=1, source_target_pairs={{0,2},{1,3},{2,0},{3,1},{4,6},{5,7},{6,4},{7,5},{8,10},{9,11},{10,... | collective-permute-start | bytes 221192 | tf_op jit(solution)/shard_map/ppermute | solution.py:155
  46.1 4.6 %collective-permute-start.19 = (bf16[16,2304]{1,0:T(8,128)(2,1)S(1)}, bf16[16,2304]{1,0:T(8,128)(2,1)S(1)}, u32[]{:S(2)}, u32[]{:S(2)}) collective-permute-start(bf16[16,2304]{1,0:T(8,128)(2,1)S(1)} %collective-permute-done.18), channel_id=1, source_target_pairs={{0,2},{1,3},{2,0},{3,1},{4,6},{5,7},{6,4},{7,5},{8,10},{9,11},{10,... | collective-permute-start | bytes 221192 | tf_op jit(solution)/shard_map/ppermute | solution.py:155
  49.9 2.0 %collective-permute-start.25 = (bf16[64,2304]{1,0:T(8,128)(2,1)S(1)}, bf16[64,2304]{1,0:T(8,128)(2,1)S(1)}, u32[]{:S(2)}, u32[]{:S(2)}) collective-permute-start(bf16[64,2304]{1,0:T(8,128)(2,1)S(1)} %pad_maximum_fusion.1), channel_id=1, source_target_pairs={{0,1},{1,0},{2,3},{3,2},{4,5},{5,4},{6,7},{7,6},{8,9},{9,8},{10,11... | collective-permute-start | bytes 884744 | tf_op jit(solution)/shard_map/ppermute | solution.py:162
  50.7 1.6 %collective-permute-start.20 = (bf16[64,2304]{1,0:T(8,128)(2,1)S(1)}, bf16[64,2304]{1,0:T(8,128)(2,1)S(1)}, u32[]{:S(2)}, u32[]{:S(2)}) collective-permute-start(bf16[64,2304]{1,0:T(8,128)(2,1)S(1)} %pad_maximum_fusion), channel_id=1, source_target_pairs={{0,1},{1,0},{2,3},{3,2},{4,5},{5,4},{6,7},{7,6},{8,9},{9,8},{10,11... | collective-permute-start | bytes 884744 | tf_op jit(solution)/shard_map/ppermute | solution.py:162
  (4 other events, 14.3 us)

commit v23 on v19

--- a/solution.py
+++ b/solution.py
@@ -221,7 +221,9 @@
     )
     blocks = in_turn(*gather_chips(row_error, chips))
     errors = jnp.concatenate(blocks, 0)
-    other_errors = [to_other_core(jnp.concatenate(one, 0)) for one in (blocks[:4], blocks[4:])]
+    other_errors = [
+        to_other_core(jnp.concatenate(one, 0)) for one in (blocks[:3], blocks[3:4], blocks[4:])
+    ]
     totals = own_totals(codes[:, :latents_here].T, centered, errors, decoder)
     (
         encoder_next,

time: 54.3 us -> 57.8 us (1.064)
  waiting for transfers between devices: 20.4 us -> 23.7 us
    ppermute x19, waiting for transfers between devices: 18.8 us -> 22.4 us  [to_chip(): lax.ppermute(block, 'latent', [(i, i ^ 2 * distance) for i in range(size)])]
    ppermute x19, starting transfers between devices: 24.2 us -> 23.6 us  [to_chip(): lax.ppermute(block, 'latent', [(i, i ^ 2 * distance) for i in range(size)])]
    ppermute x7 -> x8, starting transfers between devices: 1.28 us -> 1.77 us  [to_other_core(): return lax.ppermute(block, 'latent', [(i, i ^ 1) for i in range(size)])]
    ppermute x7 -> x8, waiting for transfers between devices: 1.63 us -> 1.26 us  [to_other_core(): return lax.ppermute(block, 'latent', [(i, i ^ 1) for i in range(size)])]
  transfers between devices with their start and end apart: 26 -> 27, of which waited for: 13 -> 13; matrix products, arithmetic and copies ran while one was open for 3% -> 3% of each run, Pallas kernels for 2% -> 2%
where the time goes in v23:
time: 57.8 us; the launch traced here: 57.6 us
  starting transfers between devices  25.4 us (44%)
  waiting for transfers between devices  23.7 us (41%)
  Pallas kernels  4.24 us (7%)
  local copies, waits for them, and re-layouts  1.75 us (3%)
  matrix products  1.26 us (2%)
  between operations  0.97 us (2%)
    ppermute x19, starting transfers between devices, to_chip(): lax.ppermute(block, 'latent', [(i, i ^ 2 * distance) for i in range(size)])  23.6 us
    ppermute x19, waiting for transfers between devices, to_chip(): lax.ppermute(block, 'latent', [(i, i ^ 2 * distance) for i in range(size)])  22.4 us
    pallas_call x1, Pallas kernels, update(): pl.pallas_call(functools.partial(update_kernel, columns, float(total_rows...  3.27 us
    ppermute x8, starting transfers between devices, to_other_core(): return lax.ppermute(block, 'latent', [(i, i ^ 1) for i in range(size)])  1.77 us
    unnamed x35, local copies, waits for them, and re-layouts  1.67 us
    ppermute x8, waiting for transfers between devices, to_other_core(): return lax.ppermute(block, 'latent', [(i, i ^ 1) for i in range(size)])  1.26 us
  transfers between devices with their start and end apart: 27, of which 13 were waited for; matrix products, arithmetic and copies ran while one was open for 3% of the time, Pallas kernels for 2%

profile of v23, /device:TPU:0, one launch (start us, length us, event | category | flops | bytes accessed | tf_op | source)
XLA Modules:
  0.0 57.6 jit_solution(9369928077348284038)
XLA Ops:
  0.7 4.1 %collective-permute-start.3 = (bf16[16,2304]{1,0:T(8,128)(2,1)}, bf16[16,2304]{1,0:T(8,128)(2,1)S(1)}, u32[]{:S(2)}, u32[]{:S(2)}) collective-permute-start(bf16[16,2304]{1,0:T(8,128)(2,1)} %param.9), channel_id=1, source_target_pairs={{0,8},{1,9},{2,10},{3,11},{4,12},{5,13},{6,14},{7,15},{8,0},{9,1},... | collective-permute-start | bytes 221192 | tf_op jit(solution)/shard_map/ppermute | solution.py:146
  4.8 1.6 %collective-permute-start.1 = (bf16[16,2304]{1,0:T(8,128)(2,1)}, bf16[16,2304]{1,0:T(8,128)(2,1)S(1)}, u32[]{:S(2)}, u32[]{:S(2)}) collective-permute-start(bf16[16,2304]{1,0:T(8,128)(2,1)} %param.9), channel_id=1, source_target_pairs={{0,4},{1,5},{2,6},{3,7},{4,0},{5,1},{6,2},{7,3},{8,12},{9,13},{10,... | collective-permute-start | bytes 221192 | tf_op jit(solution)/shard_map/ppermute | solution.py:146
  6.4 1.5 %collective-permute-start = (bf16[16,2304]{1,0:T(8,128)(2,1)}, bf16[16,2304]{1,0:T(8,128)(2,1)S(1)}, u32[]{:S(2)}, u32[]{:S(2)}) collective-permute-start(bf16[16,2304]{1,0:T(8,128)(2,1)} %param.9), channel_id=1, source_target_pairs={{0,2},{1,3},{2,0},{3,1},{4,6},{5,7},{6,4},{7,5},{8,10},{9,11},{10,... | collective-permute-start | bytes 221192 | tf_op jit(solution)/shard_map/ppermute | solution.py:146
  8.1 1.1 %constant_dynamic-update-slice_fusion.9 = bf16[256,2304]{1,0:T(8,128)(2,1)S(1)} fusion(bf16[128,2304]{1,0:T(8,128)(2,1)} %refs_4_.1), kind=kLoop, calls=%fused_computation.35 | loop fusion | bytes 1179648
  10.0 1.0 %collective-permute-start.4 = (bf16[16,2304]{1,0:T(8,128)(2,1)S(1)}, bf16[16,2304]{1,0:T(8,128)(2,1)S(1)}, u32[]{:S(2)}, u32[]{:S(2)}) collective-permute-start(bf16[16,2304]{1,0:T(8,128)(2,1)S(1)} %collective-permute-done.3), channel_id=1, source_target_pairs={{0,2},{1,3},{2,0},{3,1},{4,6},{5,7},{6,4},{7,5},{8,10},{9,11},{10,... | collective-permute-start | bytes 221192 | tf_op jit(solution)/shard_map/ppermute | solution.py:146
  11.0 1.4 %collective-permute-start.2 = (bf16[16,2304]{1,0:T(8,128)(2,1)S(1)}, bf16[16,2304]{1,0:T(8,128)(2,1)S(1)}, u32[]{:S(2)}, u32[]{:S(2)}) collective-permute-start(bf16[16,2304]{1,0:T(8,128)(2,1)S(1)} %collective-permute-done.1), channel_id=1, source_target_pairs={{0,2},{1,3},{2,0},{3,1},{4,6},{5,7},{6,4},{7,5},{8,10},{9,11},{10,... | collective-permute-start | bytes 221192 | tf_op jit(solution)/shard_map/ppermute | solution.py:146
  12.4 1.8 %collective-permute-done.5 = bf16[16,2304]{1,0:T(8,128)(2,1)S(1)} collective-permute-done((bf16[16,2304]{1,0:T(8,128)(2,1)}, bf16[16,2304]{1,0:T(8,128)(2,1)S(1)}, u32[]{:S(2)}, u32[]{:S(2)}) %collective-permute-start.5) | collective-permute-done | bytes 73760 | tf_op jit(solution)/shard_map/ppermute | solution.py:146
  14.2 0.5 collective-permute-start.6
  14.8 1.9 %collective-permute-done.2 = bf16[16,2304]{1,0:T(8,128)(2,1)S(1)} collective-permute-done((bf16[16,2304]{1,0:T(8,128)(2,1)S(1)}, bf16[16,2304]{1,0:T(8,128)(2,1)S(1)}, u32[]{:S(2)}, u32[]{:S(2)}) %collective-permute-start.2) | collective-permute-done | bytes 73760 | tf_op jit(solution)/shard_map/ppermute | solution.py:146
  16.7 1.9 %collective-permute-done.6 = bf16[16,2304]{1,0:T(8,128)(2,1)S(1)} collective-permute-done((bf16[16,2304]{1,0:T(8,128)(2,1)S(1)}, bf16[16,2304]{1,0:T(8,128)(2,1)S(1)}, u32[]{:S(2)}, u32[]{:S(2)}) %collective-permute-start.6) | collective-permute-done | bytes 73760 | tf_op jit(solution)/shard_map/ppermute | solution.py:146
  20.3 0.5 collective-permute-start.14
  20.8 1.0 %collective-permute-done.9 = bf16[128,128]{0,1:T(8,128)(2,1)S(1)} collective-permute-done((bf16[128,128]{0,1:T(8,128)(2,1)S(1)}, bf16[128,128]{0,1:T(8,128)(2,1)S(1)}, u32[]{:S(2)}, u32[]{:S(2)}) %collective-permute-start.9) | collective-permute-done | bytes 32800 | tf_op jit(solution)/shard_map/ppermute | solution.py:153
  22.3 0.6 %collective-permute-start.12 = (bf16[32,2304]{1,0:T(8,128)(2,1)S(1)}, bf16[32,2304]{1,0:T(8,128)(2,1)S(1)}, u32[]{:S(2)}, u32[]{:S(2)}) collective-permute-start(bf16[32,2304]{1,0:T(8,128)(2,1)S(1)} %pad_maximum_fusion.3), channel_id=1, source_target_pairs={{0,2},{1,3},{2,0},{3,1},{4,6},{5,7},{6,4},{7,5},{8,10},{9,11},{10,... | collective-permute-start | bytes 442376 | tf_op jit(solution)/shard_map/ppermute | solution.py:146
  22.8 4.2 %collective-permute-done.14 = bf16[32,2304]{1,0:T(8,128)(2,1)S(1)} collective-permute-done((bf16[32,2304]{1,0:T(8,128)(2,1)S(1)}, bf16[32,2304]{1,0:T(8,128)(2,1)S(1)}, u32[]{:S(2)}, u32[]{:S(2)}) %collective-permute-start.14) | collective-permute-done | bytes 147488 | tf_op jit(solution)/shard_map/ppermute | solution.py:146
  27.1 0.9 %collective-permute-start.15 = (bf16[16,2304]{1,0:T(8,128)(2,1)S(1)}, bf16[16,2304]{1,0:T(8,128)(2,1)S(1)}, u32[]{:S(2)}, u32[]{:S(2)}) collective-permute-start(bf16[16,2304]{1,0:T(8,128)(2,1)S(1)} %get-tuple-element.33), channel_id=1, source_target_pairs={{0,8},{1,9},{2,10},{3,11},{4,12},{5,13},{6,14},{7,15},{8,0},{9,1},... | collective-permute-start | bytes 221192 | tf_op jit(solution)/shard_map/ppermute | solution.py:146
  28.0 2.0 %collective-permute-start.16 = (bf16[16,2304]{1,0:T(8,128)(2,1)S(1)}, bf16[16,2304]{1,0:T(8,128)(2,1)S(1)}, u32[]{:S(2)}, u32[]{:S(2)}) collective-permute-start(bf16[16,2304]{1,0:T(8,128)(2,1)S(1)} %get-tuple-element.34), channel_id=1, source_target_pairs={{0,12},{1,13},{2,14},{3,15},{4,8},{5,9},{6,10},{7,11},{8,4},{9,5},... | collective-permute-start | bytes 221192 | tf_op jit(solution)/shard_map/ppermute | solution.py:146
  30.0 0.7 %collective-permute-start.13 = (bf16[16,2304]{1,0:T(8,128)(2,1)S(1)}, bf16[16,2304]{1,0:T(8,128)(2,1)S(1)}, u32[]{:S(2)}, u32[]{:S(2)}) collective-permute-start(bf16[16,2304]{1,0:T(8,128)(2,1)S(1)} %fusion.15), channel_id=1, source_target_pairs={{0,4},{1,5},{2,6},{3,7},{4,0},{5,1},{6,2},{7,3},{8,12},{9,13},{10,... | collective-permute-start | bytes 221192 | tf_op jit(solution)/shard_map/ppermute | solution.py:146
  30.7 3.8 %collective-permute-done.15 = bf16[16,2304]{1,0:T(8,128)(2,1)S(1)} collective-permute-done((bf16[16,2304]{1,0:T(8,128)(2,1)S(1)}, bf16[16,2304]{1,0:T(8,128)(2,1)S(1)}, u32[]{:S(2)}, u32[]{:S(2)}) %collective-permute-start.15) | collective-permute-done | bytes 73760 | tf_op jit(solution)/shard_map/ppermute | solution.py:146
  34.5 0.7 %collective-permute-done.13 = bf16[16,2304]{1,0:T(8,128)(2,1)S(1)} collective-permute-done((bf16[16,2304]{1,0:T(8,128)(2,1)S(1)}, bf16[16,2304]{1,0:T(8,128)(2,1)S(1)}, u32[]{:S(2)}, u32[]{:S(2)}) %collective-permute-start.13) | collective-permute-done | bytes 73760 | tf_op jit(solution)/shard_map/ppermute | solution.py:146
  35.3 2.2 %collective-permute-start.24 = (bf16[16,2304]{1,0:T(8,128)(2,1)S(1)}, bf16[16,2304]{1,0:T(8,128)(2,1)S(1)}, u32[]{:S(2)}, u32[]{:S(2)}) collective-permute-start(bf16[16,2304]{1,0:T(8,128)(2,1)S(1)} %fusion.20), channel_id=1, source_target_pairs={{0,12},{1,13},{2,14},{3,15},{4,8},{5,9},{6,10},{7,11},{8,4},{9,5},... | collective-permute-start | bytes 221192 | tf_op jit(solution)/shard_map/ppermute | solution.py:146
  37.5 2.3 %collective-permute-start.18 = (bf16[16,2304]{1,0:T(8,128)(2,1)S(1)}, bf16[16,2304]{1,0:T(8,128)(2,1)S(1)}, u32[]{:S(2)}, u32[]{:S(2)}) collective-permute-start(bf16[16,2304]{1,0:T(8,128)(2,1)S(1)} %fusion.20), channel_id=1, source_target_pairs={{0,4},{1,5},{2,6},{3,7},{4,0},{5,1},{6,2},{7,3},{8,12},{9,13},{10,... | collective-permute-start | bytes 221192 | tf_op jit(solution)/shard_map/ppermute | solution.py:146
  39.8 1.0 %collective-permute-start.17 = (bf16[16,2304]{1,0:T(8,128)(2,1)S(1)}, bf16[16,2304]{1,0:T(8,128)(2,1)S(1)}, u32[]{:S(2)}, u32[]{:S(2)}) collective-permute-start(bf16[16,2304]{1,0:T(8,128)(2,1)S(1)} %fusion.20), channel_id=1, source_target_pairs={{0,2},{1,3},{2,0},{3,1},{4,6},{5,7},{6,4},{7,5},{8,10},{9,11},{10,... | collective-permute-start | bytes 221192 | tf_op jit(solution)/shard_map/ppermute | solution.py:146
  40.8 1.6 %collective-permute-done.18 = bf16[16,2304]{1,0:T(8,128)(2,1)S(1)} collective-permute-done((bf16[16,2304]{1,0:T(8,128)(2,1)S(1)}, bf16[16,2304]{1,0:T(8,128)(2,1)S(1)}, u32[]{:S(2)}, u32[]{:S(2)}) %collective-permute-start.18) | collective-permute-done | bytes 73760 | tf_op jit(solution)/shard_map/ppermute | solution.py:146
  42.4 1.8 %collective-permute-done.17 = bf16[16,2304]{1,0:T(8,128)(2,1)S(1)} collective-permute-done((bf16[16,2304]{1,0:T(8,128)(2,1)S(1)}, bf16[16,2304]{1,0:T(8,128)(2,1)S(1)}, u32[]{:S(2)}, u32[]{:S(2)}) %collective-permute-start.17) | collective-permute-done | bytes 73760 | tf_op jit(solution)/shard_map/ppermute | solution.py:146
  44.2 1.0 %collective-permute-start.20 = (bf16[16,2304]{1,0:T(8,128)(2,1)S(1)}, bf16[16,2304]{1,0:T(8,128)(2,1)S(1)}, u32[]{:S(2)}, u32[]{:S(2)}) collective-permute-start(bf16[16,2304]{1,0:T(8,128)(2,1)S(1)} %collective-permute-done.18), channel_id=1, source_target_pairs={{0,2},{1,3},{2,0},{3,1},{4,6},{5,7},{6,4},{7,5},{8,10},{9,11},{10,... | collective-permute-start | bytes 221192 | tf_op jit(solution)/shard_map/ppermute | solution.py:146
  45.3 1.0 %collective-permute-start.25 = (bf16[16,2304]{1,0:T(8,128)(2,1)S(1)}, bf16[16,2304]{1,0:T(8,128)(2,1)S(1)}, u32[]{:S(2)}, u32[]{:S(2)}) collective-permute-start(bf16[16,2304]{1,0:T(8,128)(2,1)S(1)} %collective-permute-done.24), channel_id=1, source_target_pairs={{0,2},{1,3},{2,0},{3,1},{4,6},{5,7},{6,4},{7,5},{8,10},{9,11},{10,... | collective-permute-start | bytes 221192 | tf_op jit(solution)/shard_map/ppermute | solution.py:146
  46.3 1.0 %collective-permute-start.23 = (bf16[16,2304]{1,0:T(8,128)(2,1)S(1)}, bf16[16,2304]{1,0:T(8,128)(2,1)S(1)}, u32[]{:S(2)}, u32[]{:S(2)}) collective-permute-start(bf16[16,2304]{1,0:T(8,128)(2,1)S(1)} %collective-permute-done.22), channel_id=1, source_target_pairs={{0,2},{1,3},{2,0},{3,1},{4,6},{5,7},{6,4},{7,5},{8,10},{9,11},{10,... | collective-permute-start | bytes 221192 | tf_op jit(solution)/shard_map/ppermute | solution.py:146
  47.3 3.6 %collective-permute-done.25 = bf16[16,2304]{1,0:T(8,128)(2,1)S(1)} collective-permute-done((bf16[16,2304]{1,0:T(8,128)(2,1)S(1)}, bf16[16,2304]{1,0:T(8,128)(2,1)S(1)}, u32[]{:S(2)}, u32[]{:S(2)}) %collective-permute-start.25) | collective-permute-done | bytes 73760 | tf_op jit(solution)/shard_map/ppermute | solution.py:146
  50.9 1.1 %collective-permute-done.23 = bf16[16,2304]{1,0:T(8,128)(2,1)S(1)} collective-permute-done((bf16[16,2304]{1,0:T(8,128)(2,1)S(1)}, bf16[16,2304]{1,0:T(8,128)(2,1)S(1)}, u32[]{:S(2)}, u32[]{:S(2)}) %collective-permute-start.23) | collective-permute-done | bytes 73760 | tf_op jit(solution)/shard_map/ppermute | solution.py:146
  52.2 0.5 collective-permute-start.21
  52.8 1.0 %own_totals.1 = (f32[128,2304]{1,0:T(8,128)S(1)}, f32[128,2304]{1,0:T(8,128)S(1)}) custom-call(bf16[128,128]{1,0:T(8,128)(2,1)S(1)} %get-tuple-element.39.codes_across, bf16[128,2304]{1,0:T(8,128)(2,1)S(1)} %subtract_convert_fusion.centered, bf16[128,2304]{1,0:T(8,128)(2,1)S(1)} %constant_dynamic-update-slice_fusion.10.errors, bf16[128,2304]{1,0:T(8,128)(2,1)S(1)} %copy-done), custom_call_target="tpu_custom_call" | custom-call | flops 226492416 | bytes 4718592 | tf_op jit(solution)/shard_map/own_totals/pallas_call | solution.py:41
  54.3 3.3 %update.1 = (bf16[128,2304]{1,0:T(8,128)(2,1)}, f32[128,2304]{1,0:T(8,128)}, f32[128,2304]{1,0:T(8,128)}, bf16[128,2304]{1,0:T(8,128)(2,1)}, f32[128,2304]{1,0:T(8,128)}, /*index=5*/f32[128,2304]{1,0:T(8,128)}) custom-call(bf16[128,128]{1,0:T(8,128)(2,1)S(1)} %bitcast.8, bf16[128,2304]{1,0:T(8,128)(2,1)S(1)} %collective-permute-done.11.centered, ...), custom_call_target="tpu_custom_call" | custom-call | flops 226492416 | bytes 12976128 | tf_op jit(solution)/shard_map/update/pallas_call | solution.py:119
  (77 shorter events, 4.0 us)
Async XLA Ops:
  0.7 9.2 %copy-start.5 = (bf16[128,2304]{1,0:T(8,128)(2,1)S(1)}, bf16[128,2304]{1,0:T(8,128)(2,1)}, u32[]{:S(2)}) copy-start(bf16[128,2304]{1,0:T(8,128)(2,1)} %refs_3_.1) | copy-start | bytes 1769476
  0.7 17.9 %copy-start.8 = (f32[2304]{0:T(1024)S(1)}, f32[2304]{0:T(1024)}, u32[]{:S(2)}) copy-start(f32[2304]{0:T(1024)} %param.13) | copy-start | bytes 27652
  0.7 9.2 %collective-permute-start.3 = (bf16[16,2304]{1,0:T(8,128)(2,1)}, bf16[16,2304]{1,0:T(8,128)(2,1)S(1)}, u32[]{:S(2)}, u32[]{:S(2)}) collective-permute-start(bf16[16,2304]{1,0:T(8,128)(2,1)} %param.9), channel_id=1, source_target_pairs={{0,8},{1,9},{2,10},{3,11},{4,12},{5,13},{6,14},{7,15},{8,0},{9,1},... | collective-permute-start | bytes 221192 | tf_op jit(solution)/shard_map/ppermute | solution.py:146
  4.8 5.2 %collective-permute-start.1 = (bf16[16,2304]{1,0:T(8,128)(2,1)}, bf16[16,2304]{1,0:T(8,128)(2,1)S(1)}, u32[]{:S(2)}, u32[]{:S(2)}) collective-permute-start(bf16[16,2304]{1,0:T(8,128)(2,1)} %param.9), channel_id=1, source_target_pairs={{0,4},{1,5},{2,6},{3,7},{4,0},{5,1},{6,2},{7,3},{8,12},{9,13},{10,... | collective-permute-start | bytes 221192 | tf_op jit(solution)/shard_map/ppermute | solution.py:146
  6.4 4.7 %collective-permute-start = (bf16[16,2304]{1,0:T(8,128)(2,1)}, bf16[16,2304]{1,0:T(8,128)(2,1)S(1)}, u32[]{:S(2)}, u32[]{:S(2)}) collective-permute-start(bf16[16,2304]{1,0:T(8,128)(2,1)} %param.9), channel_id=1, source_target_pairs={{0,2},{1,3},{2,0},{3,1},{4,6},{5,7},{6,4},{7,5},{8,10},{9,11},{10,... | collective-permute-start | bytes 221192 | tf_op jit(solution)/shard_map/ppermute | solution.py:146
  7.9 6.4 %collective-permute-start.5 = (bf16[16,2304]{1,0:T(8,128)(2,1)}, bf16[16,2304]{1,0:T(8,128)(2,1)S(1)}, u32[]{:S(2)}, u32[]{:S(2)}) collective-permute-start(bf16[16,2304]{1,0:T(8,128)(2,1)} %param.9), channel_id=1, source_target_pairs={{0,12},{1,13},{2,14},{3,15},{4,8},{5,9},{6,10},{7,11},{8,4},{9,5},... | collective-permute-start | bytes 221192 | tf_op jit(solution)/shard_map/ppermute | solution.py:146
  8.1 1.3 %collective-permute-start.8 = (f32[128]{0:T(128)}, f32[128]{0:T(128)S(1)}, u32[]{:S(2)}, u32[]{:S(2)}) collective-permute-start(f32[128]{0:T(128)} %param.11), channel_id=1, source_target_pairs={{0,1},{1,0},{2,3},{3,2},{4,5},{5,4},{6,7},{7,6},{8,9},{9,8},{10,11... | collective-permute-start | bytes 1544 | tf_op jit(solution)/shard_map/ppermute | solution.py:153
  9.4 9.4 %collective-permute-start.10 = (bf16[128,2304]{1,0:T(8,128)(2,1)S(1)}, bf16[128,2304]{1,0:T(8,128)(2,1)S(1)}, u32[]{:S(2)}, u32[]{:S(2)}) collective-permute-start(bf16[128,2304]{1,0:T(8,128)(2,1)S(1)} %copy-done), channel_id=1, source_target_pairs={{0,1},{1,0},{2,3},{3,2},{4,5},{5,4},{6,7},{7,6},{8,9},{9,8},{10,11... | collective-permute-start | bytes 1769480 | tf_op jit(solution)/shard_map/ppermute | solution.py:153
  9.9 8.9 %collective-permute-start.7 = (bf16[128,2304]{1,0:T(8,128)(2,1)S(1)}, bf16[128,2304]{1,0:T(8,128)(2,1)S(1)}, u32[]{:S(2)}, u32[]{:S(2)}) collective-permute-start(bf16[128,2304]{1,0:T(8,128)(2,1)S(1)} %copy-done.5), channel_id=1, source_target_pairs={{0,1},{1,0},{2,3},{3,2},{4,5},{5,4},{6,7},{7,6},{8,9},{9,8},{10,11... | collective-permute-start | bytes 1769480 | tf_op jit(solution)/shard_map/ppermute | solution.py:153
  10.0 6.7 %collective-permute-start.4 = (bf16[16,2304]{1,0:T(8,128)(2,1)S(1)}, bf16[16,2304]{1,0:T(8,128)(2,1)S(1)}, u32[]{:S(2)}, u32[]{:S(2)}) collective-permute-start(bf16[16,2304]{1,0:T(8,128)(2,1)S(1)} %collective-permute-done.3), channel_id=1, source_target_pairs={{0,2},{1,3},{2,0},{3,1},{4,6},{5,7},{6,4},{7,5},{8,10},{9,11},{10,... | collective-permute-start | bytes 221192 | tf_op jit(solution)/shard_map/ppermute | solution.py:146
  11.0 5.7 %collective-permute-start.2 = (bf16[16,2304]{1,0:T(8,128)(2,1)S(1)}, bf16[16,2304]{1,0:T(8,128)(2,1)S(1)}, u32[]{:S(2)}, u32[]{:S(2)}) collective-permute-start(bf16[16,2304]{1,0:T(8,128)(2,1)S(1)} %collective-permute-done.1), channel_id=1, source_target_pairs={{0,2},{1,3},{2,0},{3,1},{4,6},{5,7},{6,4},{7,5},{8,10},{9,11},{10,... | collective-permute-start | bytes 221192 | tf_op jit(solution)/shard_map/ppermute | solution.py:146
  14.2 4.4 %collective-permute-start.6 = (bf16[16,2304]{1,0:T(8,128)(2,1)S(1)}, bf16[16,2304]{1,0:T(8,128)(2,1)S(1)}, u32[]{:S(2)}, u32[]{:S(2)}) collective-permute-start(bf16[16,2304]{1,0:T(8,128)(2,1)S(1)} %collective-permute-done.5), channel_id=1, source_target_pairs={{0,2},{1,3},{2,0},{3,1},{4,6},{5,7},{6,4},{7,5},{8,10},{9,11},{10,... | collective-permute-start | bytes 221192 | tf_op jit(solution)/shard_map/ppermute | solution.py:146
  19.7 2.1 %collective-permute-start.11 = (bf16[128,2304]{1,0:T(8,128)(2,1)S(1)}, bf16[128,2304]{1,0:T(8,128)(2,1)S(1)}, u32[]{:S(2)}, u32[]{:S(2)}) collective-permute-start(bf16[128,2304]{1,0:T(8,128)(2,1)S(1)} %subtract_convert_fusion.centered), channel_id=1, source_target_pairs={{0,1},{1,0},{2,3},{3,2},{4,5},{5,4},{6,7},{7,6},{8,9},{9,8},{10,11... | collective-permute-start | bytes 1769480 | tf_op jit(solution)/shard_map/ppermute | solution.py:153
  19.8 2.0 %collective-permute-start.9 = (bf16[128,128]{0,1:T(8,128)(2,1)S(1)}, bf16[128,128]{0,1:T(8,128)(2,1)S(1)}, u32[]{:S(2)}, u32[]{:S(2)}) collective-permute-start(bf16[128,128]{0,1:T(8,128)(2,1)S(1)} %get-tuple-element.40), channel_id=1, source_target_pairs={{0,1},{1,0},{2,3},{3,2},{4,5},{5,4},{6,7},{7,6},{8,9},{9,8},{10,11... | collective-permute-start | bytes 98312 | tf_op jit(solution)/shard_map/ppermute | solution.py:153
  20.3 6.7 %collective-permute-start.14 = (bf16[32,2304]{1,0:T(8,128)(2,1)S(1)}, bf16[32,2304]{1,0:T(8,128)(2,1)S(1)}, u32[]{:S(2)}, u32[]{:S(2)}) collective-permute-start(bf16[32,2304]{1,0:T(8,128)(2,1)S(1)} %pad_maximum_fusion.2), channel_id=1, source_target_pairs={{0,2},{1,3},{2,0},{3,1},{4,6},{5,7},{6,4},{7,5},{8,10},{9,11},{10,... | collective-permute-start | bytes 442376 | tf_op jit(solution)/shard_map/ppermute | solution.py:146
  22.3 7.8 %collective-permute-start.12 = (bf16[32,2304]{1,0:T(8,128)(2,1)S(1)}, bf16[32,2304]{1,0:T(8,128)(2,1)S(1)}, u32[]{:S(2)}, u32[]{:S(2)}) collective-permute-start(bf16[32,2304]{1,0:T(8,128)(2,1)S(1)} %pad_maximum_fusion.3), channel_id=1, source_target_pairs={{0,2},{1,3},{2,0},{3,1},{4,6},{5,7},{6,4},{7,5},{8,10},{9,11},{10,... | collective-permute-start | bytes 442376 | tf_op jit(solution)/shard_map/ppermute | solution.py:146
  27.1 7.5 %collective-permute-start.15 = (bf16[16,2304]{1,0:T(8,128)(2,1)S(1)}, bf16[16,2304]{1,0:T(8,128)(2,1)S(1)}, u32[]{:S(2)}, u32[]{:S(2)}) collective-permute-start(bf16[16,2304]{1,0:T(8,128)(2,1)S(1)} %get-tuple-element.33), channel_id=1, source_target_pairs={{0,8},{1,9},{2,10},{3,11},{4,12},{5,13},{6,14},{7,15},{8,0},{9,1},... | collective-permute-start | bytes 221192 | tf_op jit(solution)/shard_map/ppermute | solution.py:146
  28.0 6.5 %collective-permute-start.16 = (bf16[16,2304]{1,0:T(8,128)(2,1)S(1)}, bf16[16,2304]{1,0:T(8,128)(2,1)S(1)}, u32[]{:S(2)}, u32[]{:S(2)}) collective-permute-start(bf16[16,2304]{1,0:T(8,128)(2,1)S(1)} %get-tuple-element.34), channel_id=1, source_target_pairs={{0,12},{1,13},{2,14},{3,15},{4,8},{5,9},{6,10},{7,11},{8,4},{9,5},... | collective-permute-start | bytes 221192 | tf_op jit(solution)/shard_map/ppermute | solution.py:146
  30.0 23.8 %copy-start.4 = (f32[128,2304]{1,0:T(8,128)S(1)}, f32[128,2304]{1,0:T(8,128)}, u32[]{:S(2)}) copy-start(f32[128,2304]{1,0:T(8,128)} %refs_8_.1) | copy-start | bytes 3538948
  30.0 5.2 %collective-permute-start.13 = (bf16[16,2304]{1,0:T(8,128)(2,1)S(1)}, bf16[16,2304]{1,0:T(8,128)(2,1)S(1)}, u32[]{:S(2)}, u32[]{:S(2)}) collective-permute-start(bf16[16,2304]{1,0:T(8,128)(2,1)S(1)} %fusion.15), channel_id=1, source_target_pairs={{0,4},{1,5},{2,6},{3,7},{4,0},{5,1},{6,2},{7,3},{8,12},{9,13},{10,... | collective-permute-start | bytes 221192 | tf_op jit(solution)/shard_map/ppermute | solution.py:146
  35.3 18.4 %copy-start.6 = (bf16[16,2304]{1,0:T(8,128)(2,1)}, bf16[16,2304]{1,0:T(8,128)(2,1)S(1)}, u32[]{:S(2)}) copy-start(bf16[16,2304]{1,0:T(8,128)(2,1)S(1)} %fusion.20) | copy-start | bytes 221188
  35.3 10.0 %collective-permute-start.24 = (bf16[16,2304]{1,0:T(8,128)(2,1)S(1)}, bf16[16,2304]{1,0:T(8,128)(2,1)S(1)}, u32[]{:S(2)}, u32[]{:S(2)}) collective-permute-start(bf16[16,2304]{1,0:T(8,128)(2,1)S(1)} %fusion.20), channel_id=1, source_target_pairs={{0,12},{1,13},{2,14},{3,15},{4,8},{5,9},{6,10},{7,11},{8,4},{9,5},... | collective-permute-start | bytes 221192 | tf_op jit(solution)/shard_map/ppermute | solution.py:146
  37.5 8.8 %collective-permute-start.22 = (bf16[16,2304]{1,0:T(8,128)(2,1)S(1)}, bf16[16,2304]{1,0:T(8,128)(2,1)S(1)}, u32[]{:S(2)}, u32[]{:S(2)}) collective-permute-start(bf16[16,2304]{1,0:T(8,128)(2,1)S(1)} %fusion.20), channel_id=1, source_target_pairs={{0,8},{1,9},{2,10},{3,11},{4,12},{5,13},{6,14},{7,15},{8,0},{9,1},... | collective-permute-start | bytes 221192 | tf_op jit(solution)/shard_map/ppermute | solution.py:146
  37.5 4.9 %collective-permute-start.18 = (bf16[16,2304]{1,0:T(8,128)(2,1)S(1)}, bf16[16,2304]{1,0:T(8,128)(2,1)S(1)}, u32[]{:S(2)}, u32[]{:S(2)}) collective-permute-start(bf16[16,2304]{1,0:T(8,128)(2,1)S(1)} %fusion.20), channel_id=1, source_target_pairs={{0,4},{1,5},{2,6},{3,7},{4,0},{5,1},{6,2},{7,3},{8,12},{9,13},{10,... | collective-permute-start | bytes 221192 | tf_op jit(solution)/shard_map/ppermute | solution.py:146
  39.8 4.4 %collective-permute-start.17 = (bf16[16,2304]{1,0:T(8,128)(2,1)S(1)}, bf16[16,2304]{1,0:T(8,128)(2,1)S(1)}, u32[]{:S(2)}, u32[]{:S(2)}) collective-permute-start(bf16[16,2304]{1,0:T(8,128)(2,1)S(1)} %fusion.20), channel_id=1, source_target_pairs={{0,2},{1,3},{2,0},{3,1},{4,6},{5,7},{6,4},{7,5},{8,10},{9,11},{10,... | collective-permute-start | bytes 221192 | tf_op jit(solution)/shard_map/ppermute | solution.py:146
  44.1 9.7 %copy-start.3 = (f32[128,2304]{1,0:T(8,128)S(1)}, f32[128,2304]{1,0:T(8,128)}, u32[]{:S(2)}) copy-start(f32[128,2304]{1,0:T(8,128)} %refs_7_.1) | copy-start | bytes 3538948
  44.1 9.7 %collective-permute-start.19 = (bf16[48,2304]{1,0:T(8,128)(2,1)S(1)}, bf16[48,2304]{1,0:T(8,128)(2,1)S(1)}, u32[]{:S(2)}, u32[]{:S(2)}) collective-permute-start(bf16[48,2304]{1,0:T(8,128)(2,1)S(1)} %pad_maximum_fusion.1), channel_id=1, source_target_pairs={{0,1},{1,0},{2,3},{3,2},{4,5},{5,4},{6,7},{7,6},{8,9},{9,8},{10,11... | collective-permute-start | bytes 663560 | tf_op jit(solution)/shard_map/ppermute | solution.py:153
  44.2 8.0 %collective-permute-start.20 = (bf16[16,2304]{1,0:T(8,128)(2,1)S(1)}, bf16[16,2304]{1,0:T(8,128)(2,1)S(1)}, u32[]{:S(2)}, u32[]{:S(2)}) collective-permute-start(bf16[16,2304]{1,0:T(8,128)(2,1)S(1)} %collective-permute-done.18), channel_id=1, source_target_pairs={{0,2},{1,3},{2,0},{3,1},{4,6},{5,7},{6,4},{7,5},{8,10},{9,11},{10,... | collective-permute-start | bytes 221192 | tf_op jit(solution)/shard_map/ppermute | solution.py:146
  45.3 5.7 %collective-permute-start.25 = (bf16[16,2304]{1,0:T(8,128)(2,1)S(1)}, bf16[16,2304]{1,0:T(8,128)(2,1)S(1)}, u32[]{:S(2)}, u32[]{:S(2)}) collective-permute-start(bf16[16,2304]{1,0:T(8,128)(2,1)S(1)} %collective-permute-done.24), channel_id=1, source_target_pairs={{0,2},{1,3},{2,0},{3,1},{4,6},{5,7},{6,4},{7,5},{8,10},{9,11},{10,... | collective-permute-start | bytes 221192 | tf_op jit(solution)/shard_map/ppermute | solution.py:146
  46.3 5.7 %collective-permute-start.23 = (bf16[16,2304]{1,0:T(8,128)(2,1)S(1)}, bf16[16,2304]{1,0:T(8,128)(2,1)S(1)}, u32[]{:S(2)}, u32[]{:S(2)}) collective-permute-start(bf16[16,2304]{1,0:T(8,128)(2,1)S(1)} %collective-permute-done.22), channel_id=1, source_target_pairs={{0,2},{1,3},{2,0},{3,1},{4,6},{5,7},{6,4},{7,5},{8,10},{9,11},{10,... | collective-permute-start | bytes 221192 | tf_op jit(solution)/shard_map/ppermute | solution.py:146
  52.1 1.8 %collective-permute-start.26 = (bf16[64,2304]{1,0:T(8,128)(2,1)S(1)}, bf16[64,2304]{1,0:T(8,128)(2,1)S(1)}, u32[]{:S(2)}, u32[]{:S(2)}) collective-permute-start(bf16[64,2304]{1,0:T(8,128)(2,1)S(1)} %pad_maximum_fusion), channel_id=1, source_target_pairs={{0,1},{1,0},{2,3},{3,2},{4,5},{5,4},{6,7},{7,6},{8,9},{9,8},{10,11... | collective-permute-start | bytes 884744 | tf_op jit(solution)/shard_map/ppermute | solution.py:153
  52.2 1.7 %collective-permute-start.21 = (bf16[16,2304]{1,0:T(8,128)(2,1)S(1)}, bf16[16,2304]{1,0:T(8,128)(2,1)S(1)}, u32[]{:S(2)}, u32[]{:S(2)}) collective-permute-start(bf16[16,2304]{1,0:T(8,128)(2,1)S(1)} %collective-permute-done.20), channel_id=1, source_target_pairs={{0,1},{1,0},{2,3},{3,2},{4,5},{5,4},{6,7},{7,6},{8,9},{9,8},{10,11... | collective-permute-start | bytes 221192 | tf_op jit(solution)/shard_map/ppermute | solution.py:153
  (5 other events, 29.4 us)
